TPU v7x, 32 devices: a whole 2x2x4 slice. The times are simulated.
32 devices in a mesh: rows: 8 (over y, x, core), cols: 4 (over z).
Axes of the slice: x: 2, y: 2, z: 4, core: 2. Of those that a mesh axis runs over, the one named last changes fastest.
Arguments:
- tokens: bfloat16 [16384, 1536], P(('rows', 'cols')), may hold values from -6 to 6
- query_weight: bfloat16 [1536, 1536], P('rows', 'cols'), may hold values from -0.15625 to 0.15625
- key_weight: bfloat16 [1536, 256], P('rows', 'cols'), may hold values from -0.15625 to 0.15625
- value_weight: bfloat16 [1536, 256], P('rows', 'cols'), may hold values from -0.15625 to 0.15625
- out_weight: bfloat16 [1536, 1536], P('rows', 'cols'), may hold values from -1.25 to 1.25
- router_weight: bfloat16 [1536, 16], P('rows', 'cols'), may hold values from -0.078125 to 0.078125
- attention_gain: bfloat16 [1536], P(('rows', 'cols')), may hold values from 0.5 to 1.5
- experts_gain: bfloat16 [1536], P(('rows', 'cols')), may hold values from 0.5 to 1.5
- gate_weight: bfloat16 [16, 1536, 768], P('rows', None, 'cols'), may hold values from -0.15625 to 0.15625
- upward_weight: bfloat16 [16, 1536, 768], P('rows', None, 'cols'), may hold values from -0.15625 to 0.15625
- down_weight: bfloat16 [16, 768, 1536], P('rows', 'cols'), may hold values from -0.4375 to 0.4375
- routes: int32 [16384, 4], P(('rows', 'cols')), may hold values from 0 to 15, all different within a row; in each aligned block of 512 rows (0 to 511, 512 to 1023, ...) at most 160 rows name the same one
- leaf_parent: int32 [16, 8], replicated, may hold values from 0 to 3
- cotangent: bfloat16 [16384, 1536], P(('rows', 'cols')), may hold values from -6 to 6
Outputs:
- layer_output: bfloat16 [16384, 1536], P(('rows', 'cols'))
- tokens_grad: bfloat16 [16384, 1536], P(('rows', 'cols'))
- query_grad: float32 [1536, 1536], P('rows', 'cols')
- key_grad: float32 [1536, 256], P('rows', 'cols')
- value_grad: float32 [1536, 256], P('rows', 'cols')
- out_grad: float32 [1536, 1536], P('rows', 'cols')
- router_grad: float32 [1536, 16], P('rows', 'cols')
- attention_gain_grad: float32 [1536], P(('rows', 'cols'))
- experts_gain_grad: float32 [1536], P(('rows', 'cols'))
- gate_grad: float32 [16, 1536, 768], P('rows', None, 'cols')
- upward_grad: float32 [16, 1536, 768], P('rows', None, 'cols')
- down_grad: float32 [16, 768, 1536], P('rows', 'cols')
Inputs may be any that keep to these rules, and one draw needn't show every extreme that they name: `routes`: each row names 4 different experts. Within the 512 rows of one device no expert is named more than 160 times; on some device some expert is named exactly 160 times. `leaf_parent`: entry [j, l] is the branch (counted from 0) under which leaf l of tree j hangs.
All inputs are finite; a program needn't handle non-finite values.
Results may differ from a plain program's by a relative error of at most 0.022.
Values may be sent and summed in bfloat16 or wider, within the bound.
No kernel may reach another device: no remote copies, remote signals or barrier semaphores. Data moves between devices by JAX's collectives and lax.ppermute only.
A program may use at most 256 MiB of HBM per device.

v0:
```python
import jax
import jax.numpy as jnp
from jax import lax
from jax.sharding import PartitionSpec as P

D = 1536
HEADS = 12
KV_HEADS = 2
HEAD_DIM = 128
TOP = 4
TOK_DEV = 512
BRANCHES = 4
LEAVES = 8
TRUNK = 256
BRANCH = 64


EPSILON = 1e-06
ROPE_BASE = 10000.0
MASKED = -1e30
HIGHEST = lax.Precision.HIGHEST


def from_behind(block, axis, distance):
    devices = range(lax.axis_size(axis))
    route = [(i - distance, i) for i in devices if i - distance in devices]
    return lax.ppermute(block, axis, route)


def rms_norm(values, norm_gain):
    factor = lax.rsqrt(jnp.mean(values * values, axis=-1, keepdims=True) + EPSILON)
    return values * factor * norm_gain


def segment_of(token_index):
    branch_part = 1 + (token_index - TRUNK) // BRANCH
    leaf_part = 1 + BRANCHES + (token_index - TOK_DEV) // BRANCH
    return jnp.where(
        token_index < TRUNK, 0, jnp.where(token_index < TOK_DEV, branch_part, leaf_part)
    )


def position_of(token_index):
    branch_place = TRUNK + (token_index - TRUNK) % BRANCH
    leaf_place = TRUNK + BRANCH + (token_index - TOK_DEV) % BRANCH
    return jnp.where(
        token_index < TRUNK, token_index, jnp.where(token_index < TOK_DEV, branch_place, leaf_place)
    )


def path_mask(query_index, key_index, parent_row):
    query_part = segment_of(query_index)
    key_part = segment_of(key_index)
    leaf_slot = query_part - 1 - BRANCHES
    leaf_match = leaf_slot[:, None] == jnp.arange(LEAVES, dtype=jnp.int32)[None, :]
    ancestor = jnp.where(
        query_part > BRANCHES, 1 + jnp.sum(jnp.where(leaf_match, parent_row[None, :], 0), axis=1), 0
    )
    reachable = (
        (key_part[None, :] == query_part[:, None])
        | (key_part[None, :] == 0)
        | (key_part[None, :] == ancestor[:, None])
    )
    return reachable & (key_index[None, :] <= query_index[:, None])


def rotary_tables(positions):
    half_dim = HEAD_DIM // 2
    frequency = ROPE_BASE ** (-jnp.arange(half_dim, dtype=jnp.float32) / half_dim)
    angles = positions.astype(jnp.float32)[:, None] * frequency[None, :]
    return (jnp.cos(angles)[:, None, :], jnp.sin(angles)[:, None, :])


def rotate(values, cosine, sine_table):
    half_dim = HEAD_DIM // 2
    first_half = values[..., :half_dim]
    second_half = values[..., half_dim:]
    return jnp.concatenate(
        [
            first_half * cosine - second_half * sine_table,
            second_half * cosine + first_half * sine_table,
        ],
        axis=-1,
    )


def on_device(
    tokens,
    query_weight,
    key_weight,
    value_weight,
    out_weight,
    router_weight,
    attention_gain,
    experts_gain,
    gate_weight,
    upward_weight,
    down_weight,
    routes,
    leaf_parent,
    cotangent,
):
    row_count = lax.axis_size("rows")
    col_count = lax.axis_size("cols")
    parity = lax.axis_index("cols") % 2
    tree_id = (lax.axis_index("rows") * col_count + lax.axis_index("cols")) // 2
    parent_row = lax.dynamic_slice_in_dim(leaf_parent, tree_id, 1, 0)[0]
    key_width = KV_HEADS * HEAD_DIM
    query_width = HEADS * HEAD_DIM
    group_size = HEADS // KV_HEADS
    (
        query_cols,
        key_cols,
        value_cols,
        out_cols,
        router_cols,
        attention_cols,
        experts_cols,
        gate_full,
        upward_full,
        down_full,
    ) = (
        lax.all_gather(query_weight, "cols", axis=1, tiled=True),
        lax.all_gather(key_weight, "cols", axis=1, tiled=True),
        lax.all_gather(value_weight, "cols", axis=1, tiled=True),
        lax.all_gather(out_weight, "cols", axis=1, tiled=True),
        lax.all_gather(router_weight, "cols", axis=1, tiled=True),
        lax.all_gather(attention_gain, "cols", axis=0, tiled=True),
        lax.all_gather(experts_gain, "cols", axis=0, tiled=True),
        lax.all_gather(gate_weight, "cols", axis=2, tiled=True),
        lax.all_gather(upward_weight, "cols", axis=2, tiled=True),
        lax.all_gather(down_weight, "cols", axis=1, tiled=True),
    )
    query_full, key_full, value_full, out_full, router_full, attention_full, experts_full = (
        lax.all_gather(query_cols, "rows", axis=0, tiled=True),
        lax.all_gather(key_cols, "rows", axis=0, tiled=True),
        lax.all_gather(value_cols, "rows", axis=0, tiled=True),
        lax.all_gather(out_cols, "rows", axis=0, tiled=True),
        lax.all_gather(router_cols, "rows", axis=0, tiled=True),
        lax.all_gather(attention_cols, "rows", axis=0, tiled=True),
        lax.all_gather(experts_cols, "rows", axis=0, tiled=True),
    )
    token_float = tokens.astype(jnp.float32)
    attention_scale = attention_full.astype(jnp.float32)
    normed = rms_norm(token_float, attention_scale)
    normed_low = normed.astype(jnp.bfloat16)
    query_lin = jnp.dot(normed_low, query_full, preferred_element_type=jnp.float32)
    key_lin = jnp.dot(normed_low, key_full, preferred_element_type=jnp.float32)
    value_low = jnp.dot(normed_low, value_full, preferred_element_type=jnp.float32).astype(
        jnp.bfloat16
    )
    holds_leaves = parity == 0
    local_index = (1 - parity) * TOK_DEV + jnp.arange(TOK_DEV, dtype=jnp.int32)
    cosine, sine_table = rotary_tables(position_of(local_index))
    query_low = rotate(query_lin.reshape(TOK_DEV, HEADS, HEAD_DIM), cosine, sine_table).astype(
        jnp.bfloat16
    )
    key_low = (
        rotate(key_lin.reshape(TOK_DEV, KV_HEADS, HEAD_DIM), cosine, sine_table)
        .astype(jnp.bfloat16)
        .reshape(TOK_DEV, key_width)
    )
    partner_key, partner_value = from_behind((key_low, value_low), "cols", -1)
    zero_rows = jnp.zeros_like(key_low)
    key_tree = jnp.concatenate(
        [
            jnp.where(holds_leaves, partner_key, key_low),
            jnp.where(holds_leaves, key_low, zero_rows),
        ],
        axis=0,
    ).reshape(2 * TOK_DEV, KV_HEADS, HEAD_DIM)
    value_tree = jnp.concatenate(
        [
            jnp.where(holds_leaves, partner_value, value_low),
            jnp.where(holds_leaves, value_low, zero_rows),
        ],
        axis=0,
    ).reshape(2 * TOK_DEV, KV_HEADS, HEAD_DIM)
    key_index = jnp.arange(2 * TOK_DEV, dtype=jnp.int32)
    factor = HEAD_DIM ** (-0.5)
    block_rows = min(512, TOK_DEV)
    block_count = TOK_DEV // block_rows
    query_blocks = query_low.reshape(block_count, block_rows, KV_HEADS, group_size, HEAD_DIM)
    index_blocks = local_index.reshape(block_count, block_rows)

    def block_scores(query_block, query_index):
        scores = (
            jnp.einsum("qkgd,skd->kgqs", query_block, key_tree, preferred_element_type=jnp.float32)
            * factor
        )
        allowed = path_mask(query_index, key_index, parent_row)
        return jnp.where(allowed[None, None], scores, MASKED)

    def attend_block(inputs):
        query_block, query_index = inputs
        scores = block_scores(query_block, query_index)
        highest = jnp.max(scores, axis=-1, keepdims=True)
        weights = jnp.exp(scores - highest)
        totals = jnp.sum(weights, axis=-1, keepdims=True)
        attention = (weights / totals).astype(jnp.bfloat16)
        mixed_heads = jnp.einsum(
            "kgqs,skd->qkgd", attention, value_tree, preferred_element_type=jnp.float32
        )
        return (mixed_heads, (highest + jnp.log(totals))[..., 0])

    mixed_blocks, log_totals = lax.map(attend_block, (query_blocks, index_blocks))
    heads_low = mixed_blocks.reshape(TOK_DEV, query_width).astype(jnp.bfloat16)
    residual = token_float + jnp.dot(heads_low, out_full, preferred_element_type=jnp.float32)
    experts_scale = experts_full.astype(jnp.float32)
    normed_two = rms_norm(residual, experts_scale)
    normed_two_low = normed_two.astype(jnp.bfloat16)
    logits = jnp.dot(normed_two_low, router_full, preferred_element_type=jnp.float32)
    expert_total = router_full.shape[1]
    expert_ids = jnp.arange(expert_total, dtype=jnp.int32)
    route_match = routes[:, :, None] == expert_ids[None, None, :]

    def router_terms(logit_rows):
        softmax_out = jax.nn.softmax(logit_rows, axis=-1)
        chosen = jnp.sum(jnp.where(route_match, softmax_out[:, None, :], 0.0), axis=2)
        return chosen / jnp.sum(chosen, axis=1, keepdims=True)

    gate_share, router_pullback = jax.vjp(router_terms, logits)
    local_experts = gate_full.shape[0]
    capacity = TOK_DEV * TOP // expert_total * 5 // 4
    flat_routes = routes.reshape(-1)
    onehot = (flat_routes[:, None] == expert_ids[None, :]).astype(jnp.int32)
    earlier = jnp.cumsum(onehot, axis=0) - onehot
    slot_rank = jnp.sum(earlier * onehot, axis=1)
    send_place = (
        flat_routes % local_experts * row_count + flat_routes // local_experts
    ) * capacity + slot_rank
    route_ids = jnp.arange(TOK_DEV * TOP, dtype=jnp.int32)
    source = (
        jnp.zeros((local_experts * row_count * capacity,), jnp.int32)
        .at[send_place]
        .set(route_ids + 1)
    )
    filled = source > 0
    source_route = jnp.maximum(source - 1, 0)
    send_rows = jnp.where(
        filled[:, None], normed_two_low[source_route // TOP], jnp.zeros((), jnp.bfloat16)
    )
    arrived_rows = lax.all_to_all(
        send_rows.reshape(local_experts, row_count, capacity, D),
        "rows",
        split_axis=1,
        concat_axis=1,
        tiled=True,
    )
    expert_in = arrived_rows.reshape(local_experts, row_count * capacity, D)
    gate_act = jnp.einsum("erd,edf->erf", expert_in, gate_full, preferred_element_type=jnp.float32)
    upward = jnp.einsum("erd,edf->erf", expert_in, upward_full, preferred_element_type=jnp.float32)
    silu_gate = jax.nn.silu(gate_act)
    hidden_low = (silu_gate * upward).astype(jnp.bfloat16)
    expert_out = jnp.einsum(
        "erf,efd->erd", hidden_low, down_full, preferred_element_type=jnp.float32
    ).astype(jnp.bfloat16)
    back_rows = lax.all_to_all(
        expert_out.reshape(local_experts, row_count, capacity, D),
        "rows",
        split_axis=1,
        concat_axis=1,
        tiled=True,
    )
    picked = back_rows.reshape(-1, D)[send_place].reshape(TOK_DEV, TOP, D)
    mixture = jnp.sum(gate_share[:, :, None] * picked.astype(jnp.float32), axis=1)
    layer_output = (residual + mixture).astype(jnp.bfloat16)
    grad_out = cotangent.astype(jnp.float32)
    grad_send = jnp.where(
        filled[:, None],
        gate_share.reshape(-1)[source_route][:, None] * grad_out[source_route // TOP],
        0.0,
    ).astype(jnp.bfloat16)
    arrived_grads = lax.all_to_all(
        grad_send.reshape(local_experts, row_count, capacity, D),
        "rows",
        split_axis=1,
        concat_axis=1,
        tiled=True,
    )
    grad_expert = arrived_grads.reshape(local_experts, row_count * capacity, D)
    grad_hidden = jnp.einsum(
        "erd,efd->erf", grad_expert, down_full, preferred_element_type=jnp.float32
    )
    down_grad = jnp.einsum(
        "erf,erd->efd", hidden_low, grad_expert, preferred_element_type=jnp.float32
    )
    sigmoid_gate = jax.nn.sigmoid(gate_act)
    grad_gate_act = (
        grad_hidden * upward * sigmoid_gate * (1.0 + gate_act * (1.0 - sigmoid_gate))
    ).astype(jnp.bfloat16)
    grad_upward = (grad_hidden * silu_gate).astype(jnp.bfloat16)
    gate_grad = jnp.einsum(
        "erd,erf->edf", expert_in, grad_gate_act, preferred_element_type=jnp.float32
    )
    upward_grad = jnp.einsum(
        "erd,erf->edf", expert_in, grad_upward, preferred_element_type=jnp.float32
    )
    grad_route_in = (
        jnp.einsum("erf,edf->erd", grad_gate_act, gate_full, preferred_element_type=jnp.float32)
        + jnp.einsum("erf,edf->erd", grad_upward, upward_full, preferred_element_type=jnp.float32)
    ).astype(jnp.bfloat16)
    grad_back = lax.all_to_all(
        grad_route_in.reshape(local_experts, row_count, capacity, D),
        "rows",
        split_axis=1,
        concat_axis=1,
        tiled=True,
    )
    grad_normed_two = jnp.sum(
        grad_back.reshape(-1, D)[send_place].reshape(TOK_DEV, TOP, D).astype(jnp.float32), axis=1
    )
    grad_gates = jnp.sum(picked.astype(jnp.float32) * grad_out[:, None, :], axis=2)
    (grad_logits,) = router_pullback(grad_gates)
    router_float = router_full.astype(jnp.float32)
    grad_normed_two = grad_normed_two + jnp.dot(grad_logits, router_float.T, precision=HIGHEST)
    router_grad = jnp.dot(normed_two_low.astype(jnp.float32).T, grad_logits, precision=HIGHEST)
    second_norm, second_pullback = jax.vjp(rms_norm, residual, experts_scale)
    grad_residual_norm, experts_gain_grad = second_pullback(grad_normed_two)
    grad_residual = grad_out + grad_residual_norm
    grad_branch_low = grad_residual.astype(jnp.bfloat16)
    out_grad = jnp.einsum(
        "tq,td->qd", heads_low, grad_branch_low, preferred_element_type=jnp.float32
    )
    grad_heads_low = jnp.einsum(
        "td,qd->tq", grad_branch_low, out_full, preferred_element_type=jnp.float32
    ).astype(jnp.bfloat16)
    grad_blocks = grad_heads_low.reshape(block_count, block_rows, KV_HEADS, group_size, HEAD_DIM)

    def attend_back(accumulated, inputs):
        key_total, value_total = accumulated
        query_block, query_index, log_total, grad_block = inputs
        scores = block_scores(query_block, query_index)
        attention = jnp.exp(scores - log_total[..., None])
        attention_low = attention.astype(jnp.bfloat16)
        grad_attention = jnp.einsum(
            "qkgd,skd->kgqs", grad_block, value_tree, preferred_element_type=jnp.float32
        )
        grad_scores = (
            attention
            * (grad_attention - jnp.sum(attention * grad_attention, axis=-1, keepdims=True))
        ).astype(jnp.bfloat16)
        grad_query = (
            jnp.einsum("kgqs,skd->qkgd", grad_scores, key_tree, preferred_element_type=jnp.float32)
            * factor
        )
        key_total = (
            key_total
            + jnp.einsum(
                "kgqs,qkgd->skd", grad_scores, query_block, preferred_element_type=jnp.float32
            )
            * factor
        )
        value_total = value_total + jnp.einsum(
            "kgqs,qkgd->skd", attention_low, grad_block, preferred_element_type=jnp.float32
        )
        return ((key_total, value_total), grad_query)

    empty_tree = jnp.zeros((2 * TOK_DEV, KV_HEADS, HEAD_DIM), jnp.float32)
    (key_tree_grad, value_tree_grad), grad_query_blocks = lax.scan(
        attend_back, (empty_tree, empty_tree), (query_blocks, index_blocks, log_totals, grad_blocks)
    )
    key_tree_grad = key_tree_grad.reshape(2 * TOK_DEV, key_width)
    value_tree_grad = value_tree_grad.reshape(2 * TOK_DEV, key_width)
    keep_key = jnp.where(holds_leaves, key_tree_grad[TOK_DEV:], key_tree_grad[:TOK_DEV])
    keep_value = jnp.where(holds_leaves, value_tree_grad[TOK_DEV:], value_tree_grad[:TOK_DEV])
    arrived_key, arrived_value = (
        from_behind(key_tree_grad[:TOK_DEV].astype(jnp.bfloat16), "cols", 1).astype(jnp.float32),
        from_behind(value_tree_grad[:TOK_DEV].astype(jnp.bfloat16), "cols", 1).astype(jnp.float32),
    )
    arrived_key = jnp.where(holds_leaves, 0.0, arrived_key)
    arrived_value = jnp.where(holds_leaves, 0.0, arrived_value)
    grad_key_rot = (keep_key + arrived_key).reshape(TOK_DEV, KV_HEADS, HEAD_DIM)
    grad_key_low = (
        rotate(grad_key_rot, cosine, -sine_table).reshape(TOK_DEV, key_width).astype(jnp.bfloat16)
    )
    grad_value_low = (keep_value + arrived_value).astype(jnp.bfloat16)
    grad_query_low = (
        rotate(grad_query_blocks.reshape(TOK_DEV, HEADS, HEAD_DIM), cosine, -sine_table)
        .reshape(TOK_DEV, query_width)
        .astype(jnp.bfloat16)
    )
    query_grad = jnp.einsum(
        "td,tq->dq", normed_low, grad_query_low, preferred_element_type=jnp.float32
    )
    key_grad = jnp.einsum("td,tq->dq", normed_low, grad_key_low, preferred_element_type=jnp.float32)
    value_grad = jnp.einsum(
        "td,tq->dq", normed_low, grad_value_low, preferred_element_type=jnp.float32
    )
    grad_normed = (
        jnp.einsum("tq,dq->td", grad_query_low, query_full, preferred_element_type=jnp.float32)
        + jnp.einsum("tq,dq->td", grad_key_low, key_full, preferred_element_type=jnp.float32)
        + jnp.einsum("tq,dq->td", grad_value_low, value_full, preferred_element_type=jnp.float32)
    )
    first_norm, first_pullback = jax.vjp(rms_norm, token_float, attention_scale)
    grad_tokens_norm, attention_gain_grad = first_pullback(grad_normed)
    tokens_grad = (grad_residual + grad_tokens_norm).astype(jnp.bfloat16)
    query_part, key_part, value_part, out_part, router_part, attention_part, experts_part = (
        lax.psum_scatter(
            query_grad.astype(jnp.bfloat16), "rows", scatter_dimension=0, tiled=True
        ).astype(jnp.float32),
        lax.psum_scatter(
            key_grad.astype(jnp.bfloat16), "rows", scatter_dimension=0, tiled=True
        ).astype(jnp.float32),
        lax.psum_scatter(
            value_grad.astype(jnp.bfloat16), "rows", scatter_dimension=0, tiled=True
        ).astype(jnp.float32),
        lax.psum_scatter(
            out_grad.astype(jnp.bfloat16), "rows", scatter_dimension=0, tiled=True
        ).astype(jnp.float32),
        lax.psum_scatter(
            router_grad.astype(jnp.bfloat16), "rows", scatter_dimension=0, tiled=True
        ).astype(jnp.float32),
        lax.psum_scatter(
            attention_gain_grad.astype(jnp.bfloat16), "rows", scatter_dimension=0, tiled=True
        ).astype(jnp.float32),
        lax.psum_scatter(
            experts_gain_grad.astype(jnp.bfloat16), "rows", scatter_dimension=0, tiled=True
        ).astype(jnp.float32),
    )
    (
        query_final,
        key_final,
        value_final,
        out_final,
        router_final,
        attention_final,
        experts_final,
        gate_final,
        upward_final,
        down_final,
    ) = (
        lax.psum_scatter(
            query_part.astype(jnp.bfloat16), "cols", scatter_dimension=1, tiled=True
        ).astype(jnp.float32),
        lax.psum_scatter(
            key_part.astype(jnp.bfloat16), "cols", scatter_dimension=1, tiled=True
        ).astype(jnp.float32),
        lax.psum_scatter(
            value_part.astype(jnp.bfloat16), "cols", scatter_dimension=1, tiled=True
        ).astype(jnp.float32),
        lax.psum_scatter(
            out_part.astype(jnp.bfloat16), "cols", scatter_dimension=1, tiled=True
        ).astype(jnp.float32),
        lax.psum_scatter(
            router_part.astype(jnp.bfloat16), "cols", scatter_dimension=1, tiled=True
        ).astype(jnp.float32),
        lax.psum_scatter(
            attention_part.astype(jnp.bfloat16), "cols", scatter_dimension=0, tiled=True
        ).astype(jnp.float32),
        lax.psum_scatter(
            experts_part.astype(jnp.bfloat16), "cols", scatter_dimension=0, tiled=True
        ).astype(jnp.float32),
        lax.psum_scatter(
            gate_grad.astype(jnp.bfloat16), "cols", scatter_dimension=2, tiled=True
        ).astype(jnp.float32),
        lax.psum_scatter(
            upward_grad.astype(jnp.bfloat16), "cols", scatter_dimension=2, tiled=True
        ).astype(jnp.float32),
        lax.psum_scatter(
            down_grad.astype(jnp.bfloat16), "cols", scatter_dimension=1, tiled=True
        ).astype(jnp.float32),
    )
    return (
        layer_output,
        tokens_grad,
        query_final,
        key_final,
        value_final,
        out_final,
        router_final,
        attention_final,
        experts_final,
        gate_final,
        upward_final,
        down_final,
    )


def solution(mesh):
    in_specs = (
        P(("rows", "cols"), None),
        P("rows", "cols"),
        P("rows", "cols"),
        P("rows", "cols"),
        P("rows", "cols"),
        P("rows", "cols"),
        P(("rows", "cols")),
        P(("rows", "cols")),
        P("rows", None, "cols"),
        P("rows", None, "cols"),
        P("rows", "cols", None),
        P(("rows", "cols"), None),
        P(),
        P(("rows", "cols"), None),
    )
    out_specs = (
        P(("rows", "cols"), None),
        P(("rows", "cols"), None),
        P("rows", "cols"),
        P("rows", "cols"),
        P("rows", "cols"),
        P("rows", "cols"),
        P("rows", "cols"),
        P(("rows", "cols")),
        P(("rows", "cols")),
        P("rows", None, "cols"),
        P("rows", None, "cols"),
        P("rows", "cols", None),
    )
    return jax.shard_map(
        on_device, mesh=mesh, in_specs=in_specs, out_specs=out_specs, check_vma=False
    )
```

profile of v0, /device:TPU:0, one launch (start us, length us, event | category | flops | bytes accessed | tf_op | source)
XLA Modules:
  0.0 1441.6 jit_solution(3098540095099376685)
XLA Ops:
  7.3 20.3 %all_gather.57 = bf16[192,1536]{1,0:T(8,128)(2,1)} all-gather(bf16[192,384]{1,0:T(8,128)(2,1)} %param.15), channel_id=1, replica_groups=mesh['rows'=8,'cols'=4] {'cols'}, dimensions={1}, use_global_device_ids=true | all-gather | bytes 737280 | tf_op jit(solution)/shard_map/all_gather | solution.py:123
  27.6 17.2 %all_gather.59 = bf16[192,1536]{1,0:T(8,128)(2,1)} all-gather(bf16[192,384]{1,0:T(8,128)(2,1)} %param.18), channel_id=1, replica_groups=mesh['rows'=8,'cols'=4] {'cols'}, dimensions={1}, use_global_device_ids=true | all-gather | bytes 737280 | tf_op jit(solution)/shard_map/all_gather | solution.py:126
  49.3 10.3 all-reduce.12
  60.0 12.2 all-reduce.10
  72.2 13.8 all_gather.53
  86.2 12.4 all_gather.54
  102.1 17.7 %all_gather.55 = bf16[192,256]{0,1:T(8,128)(2,1)S(1)} all-gather(bf16[192,64]{0,1:T(8,128)(2,1)S(1)} %copy-done.69), channel_id=1, replica_groups=mesh['rows'=8,'cols'=4] {'cols'}, dimensions={1}, use_global_device_ids=true | all-gather | bytes 122880 | tf_op jit(solution)/shard_map/all_gather | solution.py:124
  121.9 10.0 all_gather.56
  153.6 12.2 all-gather
  179.1 11.0 gather_fusion.3
  205.9 12.9 fusion.11
  218.9 11.2 fusion.3
  230.2 13.7 fusion.23
  252.7 13.6 gather_fusion.2
  297.9 71.0 %all-to-all-done.2 = bf16[2,8,160,1536]{3,2,0,1:T(8,128)(2,1)} async-done(((bf16[2,8,160,1536]{3,2,0,1:T(8,128)(2,1)}), bf16[2,8,160,1536]{3,2,0,1:T(8,128)(2,1)}, u32[]{:S(2)}, u32[]{:S(2)}) %all-to-all-start.2) | async-done | bytes 7864352 | tf_op jit(solution)/shard_map/all_to_all | solution.py:274
  381.4 80.8 %all-to-all-done = bf16[2,8,160,1536]{3,2,0,1:T(8,128)(2,1)} async-done(((bf16[2,8,160,1536]{3,2,0,1:T(8,128)(2,1)}), bf16[2,8,160,1536]{3,2,0,1:T(8,128)(2,1)}, u32[]{:S(2)}, u32[]{:S(2)}) %all-to-all-start) | async-done | bytes 7864352 | tf_op jit(solution)/shard_map/all_to_all | solution.py:243
  469.3 11.9 fusion.110
  481.2 11.9 fusion.109
  493.1 17.4 %multiply_convert_fusion = (bf16[2,1280,768]{2,1,0:T(8,128)(2,1)}, bf16[2,1280,768]{2,1,0:T(8,128)(2,1)}, bf16[2,1280,768]{2,1,0:T(8,128)(2,1)}) fusion(f32[2,1280,768]{2,1,0:T(8,128)} %fusion.109, f32[2,1280,768]{2,1,0:T(8,128)} %fusion.110, bf16[2,1280,1536]{2,1,0:T(8,128)(2,1)} %bitcast.182, bf16[2,768,1536]{2,1,0:T(8,128)(2,1)} %all-gather.16.cloned.1.call-done), kind=kOutput, calls=%fused_computation.29 | convolution fusion | flops 6069288960 | bytes 40108032 | tf_op jit(solution)/shard_map/erd,efd->erf/dot_general | solution.py:282
  528.8 12.7 fusion.111
  541.5 11.1 add_convert_fusion
  556.3 60.9 %all-to-all-done.1 = bf16[2,8,160,1536]{3,2,0,1:T(8,128)(2,1)} async-done(((bf16[2,8,160,1536]{3,2,0,1:T(8,128)(2,1)}), bf16[2,8,160,1536]{3,2,0,1:T(8,128)(2,1)}, u32[]{:S(2)}, u32[]{:S(2)}) %all-to-all-start.1) | async-done | bytes 7864352 | tf_op jit(solution)/shard_map/all_to_all | solution.py:258
  630.3 18.0 %gather_fusion.1 = bf16[2048,1536]{1,0:T(8,128)(2,1)} fusion(bf16[2560,1536]{1,0:T(8,128)(2,1)} %bitcast.170, s32[2048]{0:T(1024)S(1)} %broadcast_clamp_fusion), kind=kCustom, calls=%fused_computation.1 | custom fusion | bytes 12591104 | tf_op jit(solution)/shard_map/gather | solution.py:265
  648.2 12.3 reshape.687
  660.6 18.0 %multiply_reduce_fusion = (f32[512,4]{1,0:T(8,128)}, f32[512,1536]{1,0:T(8,128)}) fusion(f32[512,4,1536]{2,1,0:T(4,128)} %reshape.687, f32[512,1536]{1,0:T(8,128)S(1)} %copy-done.3, f32[512,4]{1,0:T(8,128)S(1)} %copy-done.26), kind=kLoop, calls=%fused_computation.23 | loop fusion | flops 11794432 | bytes 18890752 | tf_op jit(solution)/shard_map/reduce_sum | solution.py:313
  679.8 30.8 %all-to-all-done.3 = bf16[2,8,160,1536]{3,2,0,1:T(8,128)(2,1)} async-done(((bf16[2,8,160,1536]{3,2,0,1:T(8,128)(2,1)}), bf16[2,8,160,1536]{3,2,0,1:T(8,128)(2,1)}, u32[]{:S(2)}, u32[]{:S(2)}) %all-to-all-start.3) | async-done | bytes 7864352 | tf_op jit(solution)/shard_map/all_to_all | solution.py:303
  717.7 17.5 %gather_fusion.4 = bf16[2048,1536]{1,0:T(8,128)(2,1)} fusion(bf16[2560,1536]{1,0:T(8,128)(2,1)} %bitcast.169, s32[2048]{0:T(1024)S(1)} %broadcast_clamp_fusion), kind=kCustom, calls=%fused_computation.4 | custom fusion | bytes 12591104 | tf_op jit(solution)/shard_map/gather | solution.py:311
  735.2 12.2 reshape.688
  747.4 13.1 reduce_sum.201
  775.0 12.6 fusion.24
  787.5 21.2 %fusion = (f32[2,6,512]{2,1,0:T(8,128)S(1)}, f32[2,1024,512,6]{2,1,3,0:T(8,128)}) fusion(f32[2,6,512]{2,1,0:T(8,128)S(1)} %log_add_fusion, f32[2,1024,512,6]{2,1,3,0:T(8,128)} %get-tuple-element.217, pred[512,1024]{0,1:T(8,128)(4,1)S(1)} %copy-done.7, bf16[512,2,6,128]{0,3,2,1:T(8,128)(2,1)S(1)} %bitcast.187, bf16[1024,2,128,1]{2,1,0,3:T(2,128)(2,1)S(1)} %bitcast.194), kind=kOutput, calls=%fused_computation.8 | convolution fusion | flops 1642063872 | bytes 53002240 | tf_op jit(solution)/shard_map/while/body/eval_jaxpr/qkgd,skd->kgqs/dot_general | solution.py:336
  814.4 22.4 %fusion.2 = bf16[2,6,512,1024]{2,3,1,0:T(8,128)(2,1)} fusion(f32[2,1024,512,6]{2,1,3,0:T(8,128)} %get-tuple-element.224, f32[2,6,512]{2,1,0:T(8,128)S(1)} %get-tuple-element.223, f32[2,6,512]{2,1,0:T(8,128)S(1)} %log_add_fusion, f32[2,1024,512,6]{2,1,3,0:T(8,128)} %get-tuple-element.217, pred[512,1024]{0,1:T(8,128)(4,1)S(1)} %copy-done.7), kind=kLoop, calls=%fused_computation.10 | loop fusion | flops 37748736 | bytes 63488000 | tf_op jit(solution)/shard_map/while/body/eval_jaxpr/convert_element_type | solution.py:342
  888.6 37.0 %reduce-scatter.25.cloned.1.call-done = bf16[192,256]{1,0:T(8,128)(2,1)} async-done(((bf16[1536,256]{1,0:T(8,128)(2,1)}), bf16[192,256]{1,0:T(8,128)(2,1)}) %reduce-scatter.25.cloned.1.call-update) | async-done | bytes 98320 | tf_op jit(solution)/shard_map/reduce_scatter | solution.py:402
  927.4 11.6 convolution_convert_fusion.3
  939.0 12.4 convolution_convert_fusion.4
  951.7 11.8 convolution_convert_fusion.5
  965.4 17.6 %reduce-scatter.29.cloned.1.call-done = bf16[192,1536]{1,0:T(8,128)(2,1)} async-done(((bf16[1536,1536]{1,0:T(8,128)(2,1)}), bf16[192,1536]{1,0:T(8,128)(2,1)}) %reduce-scatter.29.cloned.1.call-update) | async-done | bytes 589840 | tf_op jit(solution)/shard_map/reduce_scatter | solution.py:408
  992.5 28.3 %reduce-scatter.45.cloned.1.call-done = bf16[192,16]{1,0:T(8,128)(2,1)} async-done(((bf16[1536,16]{1,0:T(8,128)(2,1)}), bf16[192,16]{1,0:T(8,128)(2,1)}) %reduce-scatter.45.cloned.1.call-update) | async-done | bytes 6160
  1027.2 12.5 all-reduce.9
  1039.8 12.0 all-reduce.11
  1052.4 26.0 %reduce-scatter.23.cloned.1.call-done = bf16[192,1536]{1,0:T(8,128)(2,1)} async-done(((bf16[1536,1536]{1,0:T(8,128)(2,1)}), bf16[192,1536]{1,0:T(8,128)(2,1)}) %reduce-scatter.23.cloned.1.call-update) | async-done | bytes 589840 | tf_op jit(solution)/shard_map/reduce_scatter | solution.py:399
  1086.8 13.7 reduce-scatter.41.cloned.1.call-done
  1102.1 18.5 %reduce-scatter.39.cloned.1.call-done = bf16[64,192]{1,0:T(8,128)(2,1)} async-done(((bf16[256,192]{1,0:T(8,128)(2,1)}), bf16[64,192]{1,0:T(8,128)(2,1)}) %reduce-scatter.39.cloned.1.call-update) | async-done | bytes 24592
  1122.2 84.2 %reduce-scatter.35.cloned.1.call-done = bf16[2,192,1536]{2,1,0:T(8,128)(2,1)} async-done(((bf16[2,768,1536]{2,1,0:T(8,128)(2,1)}), bf16[2,192,1536]{2,1,0:T(8,128)(2,1)}) %reduce-scatter.35.cloned.1.call-update) | async-done | bytes 1179664 | tf_op jit(solution)/shard_map/reduce_scatter | solution.py:460
  1209.4 85.0 %reduce-scatter.33.cloned.1.call-done = bf16[2,1536,192]{1,2,0:T(8,128)(2,1)} async-done(((bf16[2,1536,768]{1,2,0:T(8,128)(2,1)}), bf16[2,1536,192]{1,2,0:T(8,128)(2,1)}) %reduce-scatter.33.cloned.1.call-update) | async-done | bytes 1179664 | tf_op jit(solution)/shard_map/reduce_scatter | solution.py:457
  1297.3 85.0 %reduce-scatter.31.cloned.1.call-done = bf16[2,1536,192]{1,2,0:T(8,128)(2,1)} async-done(((bf16[2,1536,768]{1,2,0:T(8,128)(2,1)}), bf16[2,1536,192]{1,2,0:T(8,128)(2,1)}) %reduce-scatter.31.cloned.1.call-update) | async-done | bytes 1179664 | tf_op jit(solution)/shard_map/reduce_scatter | solution.py:454
  1385.3 23.1 %reduce-scatter.43.cloned.1.call-done = bf16[384,192]{1,0:T(8,128)(2,1)} async-done(((bf16[1536,192]{1,0:T(8,128)(2,1)}), bf16[384,192]{1,0:T(8,128)(2,1)}) %reduce-scatter.43.cloned.1.call-update) | async-done | bytes 147472
  1410.1 22.9 %reduce-scatter.37.cloned.1.call-done = bf16[384,192]{1,0:T(8,128)(2,1)} async-done(((bf16[1536,192]{1,0:T(8,128)(2,1)}), bf16[384,192]{1,0:T(8,128)(2,1)}) %reduce-scatter.37.cloned.1.call-update) | async-done | bytes 147472
  (384 shorter events, 277.0 us)
Async XLA Ops:
  7.2 145.5 %copy-start = (s32[16,8]{0,1:T(8,128)S(1)}, s32[16,8]{0,1:T(8,128)}, u32[]{:S(2)}) copy-start(s32[16,8]{0,1:T(8,128)} %param.26) | copy-start | bytes 1540
  7.2 91.3 %copy-start.13 = (bf16[512,1536]{1,0:T(8,128)(2,1)S(1)}, bf16[512,1536]{1,0:T(8,128)(2,1)}, u32[]{:S(2)}) copy-start(bf16[512,1536]{1,0:T(8,128)(2,1)} %param.14) | copy-start | bytes 4718596
  7.2 188.7 %all-gather.8.cloned.1.call-start = ((), (), s32[]{:S(2)}) async-start(), calls=%async_computation.16 | async-start | bytes 5308416 | tf_op jit(solution)/shard_map/all_gather | solution.py:135
  27.5 216.4 %all-gather.10.cloned.1.call-start = ((), (), s32[]{:S(2)}) async-start(), calls=%async_computation.17 | async-start | bytes 5308416 | tf_op jit(solution)/shard_map/all_gather | solution.py:138
  44.8 424.4 %all-gather.14.cloned.1.call-start = ((), (), s32[]{:S(2)}) async-start(), calls=%async_computation.19 | async-start | bytes 5898240 | tf_op jit(solution)/shard_map/all_gather | solution.py:131
  72.2 59.7 %copy-start.60 = (f32[1536]{0:T(1024)}, f32[1536]{0:T(1024)S(1)}, u32[]{:S(2)}) copy-start(f32[1536]{0:T(1024)S(1)} %convert_element_type.217) | copy-start | bytes 18436
  99.4 96.5 %copy-start.74 = (f32[512]{0:T(512)}, f32[512]{0:T(512)S(1)}, u32[]{:S(2)}) copy-start(f32[512]{0:T(512)S(1)} %fusion.87) | copy-start | bytes 6148
  100.8 91.3 %collective-permute-start = (bf16[512,256]{1,0:T(8,128)(2,1)}, bf16[512,256]{1,0:T(8,128)(2,1)}, u32[]{:S(2)}, u32[]{:S(2)}) collective-permute-start(bf16[512,256]{1,0:T(8,128)(2,1)} %convolution_convert_fusion.10), channel_id=1, source_target_pairs={{1,0},{2,1},{3,2},{5,4},{6,5},{7,6},{9,8},{10,9},{11,10},{13,12},{... | collective-permute-start | bytes 786440 | tf_op jit(solution)/shard_map/ppermute | solution.py:27
  121.7 79.4 %copy-start.31 = (f32[512,64]{0,1:T(8,128)}, f32[512,64]{0,1:T(8,128)S(1)}, u32[]{:S(2)}) copy-start(f32[512,64]{0,1:T(8,128)S(1)} %get-tuple-element.211) | copy-start | bytes 393220
  133.3 20.3 %copy-start.82 = (bf16[192,4]{0,1:T(4,128)(2,1)S(1)}, bf16[192,4]{0,1:T(4,128)(2,1)}, u32[]{:S(2)}) copy-start(bf16[192,4]{0,1:T(4,128)(2,1)} %param.19) | copy-start | bytes 4612
  135.4 58.9 %collective-permute-start.1 = (bf16[512,256]{1,0:T(8,128)(2,1)}, bf16[512,256]{1,0:T(8,128)(2,1)}, u32[]{:S(2)}, u32[]{:S(2)}) collective-permute-start(bf16[512,256]{1,0:T(8,128)(2,1)} %bitcast.166), channel_id=1, source_target_pairs={{1,0},{2,1},{3,2},{5,4},{6,5},{7,6},{9,8},{10,9},{11,10},{13,12},{... | collective-permute-start | bytes 786440 | tf_op jit(solution)/shard_map/ppermute | solution.py:27
  144.0 31.9 %copy-start.72 = (s32[2048,1]{0,1:T(1,128)}, s32[2048,1]{0,1:T(1,128)S(1)}, u32[]{:S(2)}) copy-start(s32[2048,1]{0,1:T(1,128)S(1)} %compare_select_fusion) | copy-start | bytes 24580
  153.6 95.8 %copy-start.47 = (f32[1536]{0:T(1024)}, f32[1536]{0:T(1024)S(1)}, u32[]{:S(2)}) copy-start(f32[1536]{0:T(1024)S(1)} %convert_element_type.226) | copy-start | bytes 18436
  192.1 38.1 %copy-start.6 = (pred[512,1024]{0,1:T(8,128)(4,1)}, pred[512,1024]{0,1:T(8,128)(4,1)S(1)}, u32[]{:S(2)}) copy-start(pred[512,1024]{0,1:T(8,128)(4,1)S(1)} %fusion.22) | copy-start | bytes 1572868
  250.3 30.7 %copy-start.4 = (bf16[512,1536]{1,0:T(8,128)(2,1)}, bf16[512,1536]{1,0:T(8,128)(2,1)S(1)}, u32[]{:S(2)}) copy-start(bf16[512,1536]{1,0:T(8,128)(2,1)S(1)} %multiply_convert_fusion.3) | copy-start | bytes 4718596
  275.4 93.5 %all-to-all-start.2 = ((bf16[2,8,160,1536]{3,2,0,1:T(8,128)(2,1)}), bf16[2,8,160,1536]{3,2,0,1:T(8,128)(2,1)}, u32[]{:S(2)}, u32[]{:S(2)}) async-start(bf16[2,8,160,1536]{3,2,0,1:T(8,128)(2,1)} %fusion.6), calls=%async_computation.2 | async-start | bytes 15728640 | tf_op jit(solution)/shard_map/all_to_all | solution.py:274
  280.4 200.8 %all-gather.12.cloned.1.call-start = ((), (), s32[]{:S(2)}) async-start(), calls=%async_computation.18 | async-start | bytes 5898240 | tf_op jit(solution)/shard_map/all_gather | solution.py:130
  368.9 93.4 %all-to-all-start = ((bf16[2,8,160,1536]{3,2,0,1:T(8,128)(2,1)}), bf16[2,8,160,1536]{3,2,0,1:T(8,128)(2,1)}, u32[]{:S(2)}, u32[]{:S(2)}) async-start(bf16[2,8,160,1536]{3,2,0,1:T(8,128)(2,1)} %copy_select_fusion), calls=%async_computation | async-start | bytes 15728640 | tf_op jit(solution)/shard_map/all_to_all | solution.py:243
  373.8 119.4 %all-gather.16.cloned.1.call-start = ((), (), s32[]{:S(2)}) async-start(), calls=%async_computation.20 | async-start | bytes 5898240 | tf_op jit(solution)/shard_map/all_gather | solution.py:132
  523.6 93.6 %all-to-all-start.1 = ((bf16[2,8,160,1536]{3,2,0,1:T(8,128)(2,1)}), bf16[2,8,160,1536]{3,2,0,1:T(8,128)(2,1)}, u32[]{:S(2)}, u32[]{:S(2)}) async-start(bf16[2,8,160,1536]{3,2,0,1:T(8,128)(2,1)} %copy.323), calls=%async_computation.1 | async-start | bytes 15728640 | tf_op jit(solution)/shard_map/all_to_all | solution.py:258
  556.2 66.0 %copy-start.37 = (f32[512,64]{0,1:T(8,128)S(1)}, f32[512,64]{0,1:T(8,128)}, u32[]{:S(2)}) copy-start(f32[512,64]{0,1:T(8,128)} %get-tuple-element.209) | copy-start | bytes 393220
  556.2 66.8 %copy-start.73 = (s32[2048,1]{0,1:T(1,128)S(1)}, s32[2048,1]{0,1:T(1,128)}, u32[]{:S(2)}) copy-start(s32[2048,1]{0,1:T(1,128)} %copy-done.72) | copy-start | bytes 24580
  556.2 66.8 %copy-start.63 = (f32[512]{0:T(512)S(1)}, f32[512]{0:T(512)}, u32[]{:S(2)}) copy-start(f32[512]{0:T(512)} %copy-done.62) | copy-start | bytes 6148
  556.3 66.8 %copy-start.71 = (f32[512]{0:T(512)S(1)}, f32[512]{0:T(512)}, u32[]{:S(2)}) copy-start(f32[512]{0:T(512)} %copy-done.70) | copy-start | bytes 6148
  556.3 66.8 %copy-start.46 = (f32[2,6,512]{2,1,0:T(8,128)S(1)}, f32[2,6,512]{2,1,0:T(8,128)}, u32[]{:S(2)}) copy-start(f32[2,6,512]{2,1,0:T(8,128)} %copy-done.45) | copy-start | bytes 73732
  556.3 66.8 %copy-start.50 = (f32[2,6,512]{2,1,0:T(8,128)S(1)}, f32[2,6,512]{2,1,0:T(8,128)}, u32[]{:S(2)}) copy-start(f32[2,6,512]{2,1,0:T(8,128)} %copy-done.49) | copy-start | bytes 73732
  617.2 93.4 %all-to-all-start.3 = ((bf16[2,8,160,1536]{3,2,0,1:T(8,128)(2,1)}), bf16[2,8,160,1536]{3,2,0,1:T(8,128)(2,1)}, u32[]{:S(2)}, u32[]{:S(2)}) async-start(bf16[2,8,160,1536]{3,2,0,1:T(8,128)(2,1)} %copy.329), calls=%async_computation.3 | async-start | bytes 15728640 | tf_op jit(solution)/shard_map/all_to_all | solution.py:303
  622.2 264.8 %reduce-scatter.27.cloned.1.call-start = ((), (), s32[]{:S(2)}) async-start(), calls=%async_computation.23 | async-start | bytes 884736 | tf_op jit(solution)/shard_map/reduce_scatter | solution.py:405
  660.6 19.2 %copy-start.36 = (f32[512,16]{0,1:T(8,128)S(1)}, f32[512,16]{0,1:T(8,128)}, u32[]{:S(2)}) copy-start(f32[512,16]{0,1:T(8,128)} %copy-done.35) | copy-start | bytes 98308
  660.6 19.2 %copy-start.54 = (f32[512]{0:T(512)S(1)}, f32[512]{0:T(512)}, u32[]{:S(2)}) copy-start(f32[512]{0:T(512)} %copy-done.53) | copy-start | bytes 6148
  810.6 40.9 %collective-permute-start.3 = (bf16[512,256]{1,0:T(8,128)(2,1)}, bf16[512,256]{1,0:T(8,128)(2,1)}, u32[]{:S(2)}, u32[]{:S(2)}) collective-permute-start(bf16[512,256]{1,0:T(8,128)(2,1)} %copy.378), channel_id=1, source_target_pairs={{0,1},{1,2},{2,3},{4,5},{5,6},{6,7},{8,9},{9,10},{10,11},{12,13},{... | collective-permute-start | bytes 786440 | tf_op jit(solution)/shard_map/ppermute | solution.py:27
  814.4 22.4 %copy-start.11 = (bf16[512,12,64]{2,0,1:T(8,128)(2,1)S(1)}, bf16[512,12,64]{2,0,1:T(8,128)(2,1)}, u32[]{:S(2)}) copy-start(bf16[512,12,64]{2,0,1:T(8,128)(2,1)} %copy-done.10) | copy-start | bytes 2359300
  814.4 22.4 %copy-start.12 = (bf16[512,12,64]{2,0,1:T(8,128)(2,1)S(1)}, bf16[512,12,64]{2,0,1:T(8,128)(2,1)}, u32[]{:S(2)}) copy-start(bf16[512,12,64]{2,0,1:T(8,128)(2,1)} %copy.311) | copy-start | bytes 2359300
  849.3 7.2 collective-permute-start.2
  854.4 71.3 %reduce-scatter.25.cloned.1.call-start = ((), (), s32[]{:S(2)}) async-start(), calls=%async_computation.22 | async-start | bytes 884736 | tf_op jit(solution)/shard_map/reduce_scatter | solution.py:402
  862.2 120.8 %reduce-scatter.29.cloned.1.call-start = ((), (), s32[]{:S(2)}) async-start(), calls=%async_computation.24 | async-start | bytes 5308416 | tf_op jit(solution)/shard_map/reduce_scatter | solution.py:408
  868.5 152.4 %reduce-scatter.45.cloned.1.call-start = ((), (), s32[]{:S(2)}) async-start(), calls=%async_computation.32 | async-start | bytes 442368
  878.8 199.7 %reduce-scatter.23.cloned.1.call-start = ((), (), s32[]{:S(2)}) async-start(), calls=%async_computation.21 | async-start | bytes 5308416 | tf_op jit(solution)/shard_map/reduce_scatter | solution.py:399
  884.9 215.6 %reduce-scatter.41.cloned.1.call-start = ((), (), s32[]{:S(2)}) async-start(), calls=%async_computation.30 | async-start | bytes 163840
  888.6 232.0 %reduce-scatter.39.cloned.1.call-start = ((), (), s32[]{:S(2)}) async-start(), calls=%async_computation.29 | async-start | bytes 163840
  927.3 279.1 %reduce-scatter.35.cloned.1.call-start = ((), (), s32[]{:S(2)}) async-start(), calls=%async_computation.27 | async-start | bytes 5898240 | tf_op jit(solution)/shard_map/reduce_scatter | solution.py:460
  939.0 355.4 %reduce-scatter.33.cloned.1.call-start = ((), (), s32[]{:S(2)}) async-start(), calls=%async_computation.26 | async-start | bytes 5898240 | tf_op jit(solution)/shard_map/reduce_scatter | solution.py:457
  951.5 430.9 %reduce-scatter.31.cloned.1.call-start = ((), (), s32[]{:S(2)}) async-start(), calls=%async_computation.25 | async-start | bytes 5898240 | tf_op jit(solution)/shard_map/reduce_scatter | solution.py:454
  963.5 444.8 %reduce-scatter.43.cloned.1.call-start = ((), (), s32[]{:S(2)}) async-start(), calls=%async_computation.31 | async-start | bytes 983040
  985.3 36.4 %copy-start.24 = (bf16[1536,256]{1,0:T(8,128)(2,1)S(1)}, bf16[1536,256]{1,0:T(8,128)(2,1)}, u32[]{:S(2)}) copy-start(bf16[1536,256]{1,0:T(8,128)(2,1)} %copy-done.23) | copy-start | bytes 2359300
  985.3 447.8 %reduce-scatter.37.cloned.1.call-start = ((), (), s32[]{:S(2)}) async-start(), calls=%async_computation.28 | async-start | bytes 983040
  1024.3 57.6 %copy-start.77 = (f32[512]{0:T(512)S(1)}, f32[512]{0:T(512)}, u32[]{:S(2)}) copy-start(f32[512]{0:T(512)} %copy-done.76) | copy-start | bytes 6148
  1294.4 140.5 %copy-start.1 = (s32[16,8]{0,1:T(8,128)S(1)}, s32[16,8]{0,1:T(8,128)}, u32[]{:S(2)}) copy-start(s32[16,8]{0,1:T(8,128)} %param.26) | copy-start | bytes 1540
  (64 other events, 454.2 us)
Sparse Core Ops, SparseCore 0:
  27.7 38.7 all-gather.7
  68.4 40.1 all-gather.9
  136.8 89.5 all-gather.13
  282.5 90.0 all-gather.11
  375.9 90.0 all-gather.15
  854.5 32.3 reduce-scatter.26
  890.6 34.9 reduce-scatter.24
  929.1 53.8 reduce-scatter.28
  987.0 33.8 reduce-scatter.44
  1024.5 53.8 reduce-scatter.22
  1081.3 19.1 reduce-scatter.40
  1103.2 17.3 reduce-scatter.38
  1122.9 83.4 reduce-scatter.34
  1208.5 85.7 reduce-scatter.32
  1296.5 85.7 reduce-scatter.30
  1384.5 23.8 reduce-scatter.42
  1410.5 22.5 reduce-scatter.36
where the time goes:
time: 1450 us; the launch traced here: 1440 us
  waiting for transfers between devices  688 us (47%)
  matrix products  236 us (16%)
  local copies, waits for them, and re-layouts  182 us (13%)
  blocking collectives  160 us (11%)
  other arithmetic  127 us (9%)
  starting transfers between devices  29.8 us (2%)
  between operations  18.8 us (1%)
    unnamed x22, waiting for transfers between devices  108 us
    reduce_scatter x1, waiting for transfers between devices, on_device(): lax.psum_scatter(upward_grad.astype(jnp.bfloat16), 'cols', scatter_dimens...  85 us
    reduce_scatter x1, waiting for transfers between devices, on_device(): lax.psum_scatter(gate_grad.astype(jnp.bfloat16), 'cols', scatter_dimensio...  85 us
    reduce_scatter x1, waiting for transfers between devices, on_device(): lax.psum_scatter(down_grad.astype(jnp.bfloat16), 'cols', scatter_dimensio...  84.2 us
    all_to_all x1, waiting for transfers between devices, on_device(): lax.all_to_all(send_rows.reshape(local_experts, row_count, capacity, D),...  80.8 us
    all_to_all x1, waiting for transfers between devices, on_device(): lax.all_to_all(grad_send.reshape(local_experts, row_count, capacity, D),...  71 us
    all_to_all x1, waiting for transfers between devices, on_device(): lax.all_to_all(expert_out.reshape(local_experts, row_count, capacity, D),...  60.9 us
    unnamed x4, blocking collectives  46.9 us
  transfers between devices with their start and end apart: 25, of which 16 were waited for; matrix products, arithmetic and copies ran while one was open for 28% of the time, Pallas kernels for 0%

commit v1 on v0

v1 whole, which is shorter than its diff:
```python
import jax
import jax.numpy as jnp
from jax import lax
from jax.sharding import PartitionSpec as P

D = 1536
HEADS = 12
KV_HEADS = 2
HEAD_DIM = 128
TOP = 4
TOK_DEV = 512
BRANCHES = 4
LEAVES = 8
TRUNK = 256
BRANCH = 64


EPSILON = 1e-06
ROPE_BASE = 10000.0
MASKED = -1e30
HIGHEST = lax.Precision.HIGHEST


def rms_norm(values, norm_gain):
    factor = lax.rsqrt(jnp.mean(values * values, axis=-1, keepdims=True) + EPSILON)
    return values * factor * norm_gain


def segment_of(token_index):
    branch_part = 1 + (token_index - TRUNK) // BRANCH
    leaf_part = 1 + BRANCHES + (token_index - TOK_DEV) // BRANCH
    return jnp.where(
        token_index < TRUNK, 0, jnp.where(token_index < TOK_DEV, branch_part, leaf_part)
    )


def position_of(token_index):
    branch_place = TRUNK + (token_index - TRUNK) % BRANCH
    leaf_place = TRUNK + BRANCH + (token_index - TOK_DEV) % BRANCH
    return jnp.where(
        token_index < TRUNK, token_index, jnp.where(token_index < TOK_DEV, branch_place, leaf_place)
    )


def path_mask(query_index, key_index, parent_row):
    query_part = segment_of(query_index)
    key_part = segment_of(key_index)
    leaf_slot = query_part - 1 - BRANCHES
    leaf_match = leaf_slot[:, None] == jnp.arange(LEAVES, dtype=jnp.int32)[None, :]
    ancestor = jnp.where(
        query_part > BRANCHES, 1 + jnp.sum(jnp.where(leaf_match, parent_row[None, :], 0), axis=1), 0
    )
    reachable = (
        (key_part[None, :] == query_part[:, None])
        | (key_part[None, :] == 0)
        | (key_part[None, :] == ancestor[:, None])
    )
    return reachable & (key_index[None, :] <= query_index[:, None])


def rotary_tables(positions):
    half_dim = HEAD_DIM // 2
    frequency = ROPE_BASE ** (-jnp.arange(half_dim, dtype=jnp.float32) / half_dim)
    angles = positions.astype(jnp.float32)[:, None] * frequency[None, :]
    return (jnp.cos(angles)[:, None, :], jnp.sin(angles)[:, None, :])


def rotate(values, cosine, sine_table):
    half_dim = HEAD_DIM // 2
    first_half = values[..., :half_dim]
    second_half = values[..., half_dim:]
    return jnp.concatenate(
        [
            first_half * cosine - second_half * sine_table,
            second_half * cosine + first_half * sine_table,
        ],
        axis=-1,
    )


def take(block, index):
    return lax.dynamic_index_in_dim(block, index, 0, keepdims=False)


def pick(table, place):
    return jnp.asarray(table, jnp.int32)[place]


SLOT_SHARD = ((0, 2, 1, 3), (1, 3, 0, 2), (2, 0, 1, 3), (3, 1, 2, 0))


def slot_shards():
    count = lax.axis_size("cols")
    if count == 4:
        return pick(SLOT_SHARD, lax.axis_index("cols"))
    return jnp.arange(count, dtype=jnp.int32)


def gather_slots(block):
    count = lax.axis_size("cols")
    if count != 4:
        whole = lax.all_gather(block, "cols", axis=0)
        return [whole[i] for i in range(count)]
    place = lax.axis_index("cols")
    above = lax.ppermute(block, "cols", [(1, 0), (2, 1), (3, 2)])
    below = lax.ppermute(block, "cols", [(0, 1), (1, 2), (2, 3)])
    far = lax.ppermute(block, "cols", [(0, 3), (3, 0)])
    payload = jnp.where(place == 1, above, jnp.where(place == 2, below, block))
    second = lax.ppermute(payload, "cols", [(3, 1), (1, 0), (0, 2), (2, 3)])
    end = (place == 0) | (place == 3)
    return [
        block,
        second,
        jnp.where(place == 0, above, below),
        jnp.where(end, far, above),
    ]


def reduce_slots(slots):
    count = lax.axis_size("cols")
    if count != 4:
        whole = jnp.stack(slots).astype(jnp.bfloat16)
        return lax.psum_scatter(whole, "cols", scatter_dimension=0).astype(jnp.float32)
    place = lax.axis_index("cols")
    own, second, third, fourth = slots
    end = (place == 0) | (place == 3)
    relay = lax.ppermute(second, "cols", [(1, 3), (0, 1), (2, 0), (3, 2)])
    far = lax.ppermute(fourth, "cols", [(0, 3), (3, 0)])
    relayed = relay.astype(jnp.float32)
    upward_load = (
        jnp.where(place == 0, third, fourth).astype(jnp.float32)
        + jnp.where(place == 1, relayed, 0.0)
    ).astype(jnp.bfloat16)
    downward_load = (third.astype(jnp.float32) + jnp.where(place == 2, relayed, 0.0)).astype(
        jnp.bfloat16
    )
    below = lax.ppermute(upward_load, "cols", [(0, 1), (1, 2), (2, 3)])
    above = lax.ppermute(downward_load, "cols", [(1, 0), (2, 1), (3, 2)])
    return (
        own.astype(jnp.float32)
        + below.astype(jnp.float32)
        + above.astype(jnp.float32)
        + jnp.where(end, relayed + far.astype(jnp.float32), 0.0)
    )


def flip(block, bit):
    count = lax.axis_size("rows")
    return lax.ppermute(block, "rows", [(i, i ^ bit) for i in range(count)])


def gather_rows(block):
    count = lax.axis_size("rows")
    if count != 8:
        return lax.all_gather(block, "rows", axis=0)
    place = lax.axis_index("rows")
    core, side, level = place % 2, place // 2 % 2, place // 4
    half = block.shape[0] // 2
    beside = flip(block, 2)
    across = flip(block, 4)
    corner = jnp.concatenate([flip(beside[:half], 4), flip(across[half:], 2)], axis=0)
    near = [jnp.where(side == 0, block, beside), jnp.where(side == 0, beside, block)]
    away = [jnp.where(side == 0, across, corner), jnp.where(side == 0, corner, across)]
    same = jnp.stack(
        [jnp.where(level == 0, near[i], away[i]) for i in range(2)]
        + [jnp.where(level == 0, away[i], near[i]) for i in range(2)]
    )
    other = flip(same, 1)
    both = jnp.stack([jnp.where(core == 0, same, other), jnp.where(core == 0, other, same)], axis=1)
    return both.reshape((count,) + block.shape)


def reduce_rows(blocks):
    count = lax.axis_size("rows")
    if count != 8:
        return lax.psum_scatter(blocks, "rows", scatter_dimension=0).astype(jnp.float32)
    place = lax.axis_index("rows")
    core, side, level = place % 2, place // 2 % 2, place // 4
    half = blocks.shape[1] // 2
    rest = blocks.shape[1:]

    def own_of(array, axis, index):
        return lax.dynamic_index_in_dim(array, index, axis, keepdims=False)

    def add(array, axis, index, bit):
        arrived = flip(own_of(array, axis, 1 - index), bit)
        return own_of(array, axis, index).astype(jnp.float32) + arrived.astype(jnp.float32)

    chips = add(blocks.reshape((2, 2, 2) + rest), 2, core, 1).astype(jnp.bfloat16)
    first = add(chips[:, :, :half], 1, side, 2).astype(jnp.bfloat16)
    second = add(chips[:, :, half:], 0, level, 4).astype(jnp.bfloat16)
    return jnp.concatenate([add(first, 0, level, 4), add(second, 0, side, 2)], axis=0)


def on_device(
    tokens,
    query_weight,
    key_weight,
    value_weight,
    out_weight,
    router_weight,
    attention_gain,
    experts_gain,
    gate_weight,
    upward_weight,
    down_weight,
    routes,
    leaf_parent,
    cotangent,
):
    row_count = lax.axis_size("rows")
    col_count = lax.axis_size("cols")
    row_place = lax.axis_index("rows")
    col_place = lax.axis_index("cols")
    parity = col_place % 2
    tree_id = (row_place * col_count + col_place) // 2
    parent_row = lax.dynamic_slice_in_dim(leaf_parent, tree_id, 1, 0)[0]
    key_width = KV_HEADS * HEAD_DIM
    query_width = HEADS * HEAD_DIM
    group_size = HEADS // KV_HEADS
    depth, query_part = query_weight.shape
    key_part = key_weight.shape[1]
    router_part = router_weight.shape[1]
    gain_part = attention_gain.shape[0]
    expert_total = router_part * col_count
    local_experts = gate_weight.shape[0]
    capacity = TOK_DEV * TOP // expert_total * 5 // 4
    spare = 128

    extras = jnp.concatenate(
        [
            router_weight,
            jnp.pad(attention_gain, (0, depth - gain_part))[:, None],
            jnp.pad(experts_gain, (0, depth - gain_part))[:, None],
            jnp.zeros((depth, spare - router_part - 2), jnp.bfloat16),
        ],
        axis=1,
    )
    packed = jnp.concatenate([query_weight, key_weight, value_weight, out_weight, extras], axis=1)
    packed_width = packed.shape[1]
    packed_slots = jnp.stack(gather_slots(packed))
    shards = slot_shards()
    slot_of_shard = jnp.argsort(shards)
    packed_cols = jnp.take(packed_slots, slot_of_shard, axis=0)
    packed_all = gather_rows(packed_cols.reshape(col_count * depth, packed_width)).reshape(
        row_count, col_count, depth, packed_width
    )

    def unpack(start, width):
        part = packed_all[..., start : start + width]
        return jnp.swapaxes(part, 1, 2).reshape(row_count * depth, col_count * width)

    key_at = query_part
    value_at = key_at + key_part
    out_at = value_at + key_part
    extra_at = out_at + query_part
    query_full = unpack(0, query_part)
    key_full = unpack(key_at, key_part)
    value_full = unpack(value_at, key_part)
    out_full = unpack(out_at, query_part)
    router_full = unpack(extra_at, router_part)
    gain_at = extra_at + router_part
    attention_full = packed_all[:, :, :gain_part, gain_at].reshape(-1)
    experts_full = packed_all[:, :, :gain_part, gain_at + 1].reshape(-1)

    expert_weights = []
    ahead = packed_slots
    for expert in range(local_experts):
        block = jnp.stack(
            [gate_weight[expert].T, upward_weight[expert].T, down_weight[expert]], axis=0
        )
        block, ahead = lax.optimization_barrier((block, ahead))
        slots = gather_slots(block)
        ahead = slots[1]
        expert_weights.append(jnp.stack(slots, axis=1))

    routes_all = lax.all_gather(routes, "rows", axis=0)
    grad_all = lax.all_gather(cotangent, "rows", axis=0)

    token_float = tokens.astype(jnp.float32)
    attention_scale = attention_full.astype(jnp.float32)
    normed = rms_norm(token_float, attention_scale)
    normed_low = normed.astype(jnp.bfloat16)
    query_lin = jnp.dot(normed_low, query_full, preferred_element_type=jnp.float32)
    key_lin = jnp.dot(normed_low, key_full, preferred_element_type=jnp.float32)
    value_low = jnp.dot(normed_low, value_full, preferred_element_type=jnp.float32).astype(
        jnp.bfloat16
    )
    holds_leaves = parity == 0
    local_index = (1 - parity) * TOK_DEV + jnp.arange(TOK_DEV, dtype=jnp.int32)
    cosine, sine_table = rotary_tables(position_of(local_index))
    query_low = rotate(query_lin.reshape(TOK_DEV, HEADS, HEAD_DIM), cosine, sine_table).astype(
        jnp.bfloat16
    )
    key_low = (
        rotate(key_lin.reshape(TOK_DEV, KV_HEADS, HEAD_DIM), cosine, sine_table)
        .astype(jnp.bfloat16)
        .reshape(TOK_DEV, key_width)
    )
    pairs = [(i + 1, i) for i in range(0, col_count, 2)]
    own_pair = jnp.concatenate([key_low, value_low], axis=1)
    partner = lax.ppermute(own_pair, "cols", pairs)
    tree_rows = jnp.concatenate(
        [
            jnp.where(holds_leaves, partner, own_pair),
            jnp.where(holds_leaves, own_pair, jnp.zeros_like(own_pair)),
        ],
        axis=0,
    )
    key_tree = tree_rows[:, :key_width].reshape(2 * TOK_DEV, KV_HEADS, HEAD_DIM)
    value_tree = tree_rows[:, key_width:].reshape(2 * TOK_DEV, KV_HEADS, HEAD_DIM)
    key_index = jnp.arange(2 * TOK_DEV, dtype=jnp.int32)
    factor = HEAD_DIM ** (-0.5)
    query_group = query_low.reshape(TOK_DEV, KV_HEADS, group_size, HEAD_DIM)
    allowed = path_mask(local_index, key_index, parent_row)

    def block_scores():
        scores = (
            jnp.einsum("qkgd,skd->kgqs", query_group, key_tree, preferred_element_type=jnp.float32)
            * factor
        )
        return jnp.where(allowed[None, None], scores, MASKED)

    scores = block_scores()
    highest = jnp.max(scores, axis=-1, keepdims=True)
    weights = jnp.exp(scores - highest)
    totals = jnp.sum(weights, axis=-1, keepdims=True)
    attention = (weights / totals).astype(jnp.bfloat16)
    mixed_heads = jnp.einsum(
        "kgqs,skd->qkgd", attention, value_tree, preferred_element_type=jnp.float32
    )
    log_total = highest + jnp.log(totals)
    heads_low = mixed_heads.reshape(TOK_DEV, query_width).astype(jnp.bfloat16)
    residual = token_float + jnp.dot(heads_low, out_full, preferred_element_type=jnp.float32)
    experts_scale = experts_full.astype(jnp.float32)
    normed_two = rms_norm(residual, experts_scale)
    normed_two_low = normed_two.astype(jnp.bfloat16)
    normed_all = lax.all_gather(normed_two_low, "rows", axis=0)

    expert_ids = jnp.arange(expert_total, dtype=jnp.int32)

    def shares(chosen_of, logit_cols):
        softmax_out = jax.nn.softmax(logit_cols, axis=-2)
        return softmax_out / jnp.sum(
            jnp.where(chosen_of, softmax_out, 0.0), axis=-2, keepdims=True
        )

    own_ids = row_place * local_experts + jnp.arange(local_experts, dtype=jnp.int32)
    named = routes_all[:, :, :, None] == expert_ids[None, None, None, :]
    named = jnp.swapaxes(jnp.any(named, axis=2), 1, 2)
    logits_all = jnp.einsum(
        "de,rtd->ret", router_full, normed_all, preferred_element_type=jnp.float32
    )
    share_all = shares(named, logits_all)
    own_at = row_place * local_experts
    hit = lax.dynamic_slice_in_dim(named, own_at, local_experts, 1)
    share = lax.dynamic_slice_in_dim(share_all, own_at, local_experts, 1)
    earlier = jnp.arange(TOK_DEV)[:, None] < jnp.arange(TOK_DEV)[None, :]
    rank = jnp.einsum(
        "rlt,tu->rlu",
        hit.astype(jnp.bfloat16),
        earlier.astype(jnp.bfloat16),
        preferred_element_type=jnp.float32,
    ).astype(jnp.int32)
    place_ids = jnp.arange(capacity, dtype=jnp.int32)
    onehot = (hit[:, :, None, :] & (rank[:, :, None, :] == place_ids[None, None, :, None])).astype(
        jnp.bfloat16
    )
    share_rows = jnp.sum(
        onehot.astype(jnp.float32) * jnp.where(hit, share, 0.0)[:, :, None, :], axis=-1
    )
    token_rows = jnp.einsum("rlct,rtd->lrcd", onehot, normed_all).reshape(
        local_experts, row_count * capacity, D
    )
    grad_rows = jnp.einsum("rlct,rtd->lrcd", onehot, grad_all).reshape(
        local_experts, row_count * capacity, D
    )
    share_rows = jnp.swapaxes(share_rows, 0, 1).reshape(local_experts, row_count * capacity, 1)

    out_rows, back_rows, gate_dots, reduced = ([], [], [], [])
    for expert in range(local_experts):
        gate_full, upward_full, down_full = expert_weights[expert].reshape(3, -1, D)
        row_block = token_rows[expert]
        grad_block = grad_rows[expert].astype(jnp.float32)
        grad_expert = (share_rows[expert] * grad_block).astype(jnp.bfloat16)

        def dot(one, two, dims):
            return lax.dot_general(
                one, two, (dims, ((), ())), preferred_element_type=jnp.float32
            )

        gate_act = dot(row_block, gate_full, ((1,), (1,)))
        upward = dot(row_block, upward_full, ((1,), (1,)))
        silu_gate = jax.nn.silu(gate_act)
        hidden_low = (silu_gate * upward).astype(jnp.bfloat16)
        expert_out = dot(hidden_low, down_full, ((1,), (0,))).astype(jnp.bfloat16)
        grad_hidden = dot(grad_expert, down_full, ((1,), (1,)))
        sigmoid_gate = jax.nn.sigmoid(gate_act)
        grad_gate_act = (
            grad_hidden * upward * sigmoid_gate * (1.0 + gate_act * (1.0 - sigmoid_gate))
        ).astype(jnp.bfloat16)
        grad_upward = (grad_hidden * silu_gate).astype(jnp.bfloat16)
        down_grad = dot(hidden_low, grad_expert, ((0,), (0,)))
        gate_grad = dot(grad_gate_act, row_block, ((0,), (0,)))
        upward_grad = dot(grad_upward, row_block, ((0,), (0,)))
        slots = [
            jnp.stack(
                [
                    grad.astype(jnp.bfloat16).reshape(col_count, -1, D)[i]
                    for grad in (gate_grad, upward_grad, down_grad)
                ]
            )
            for i in range(col_count)
        ]
        reduced.append(reduce_slots(slots))
        grad_route_in = (
            dot(grad_gate_act, gate_full, ((1,), (0,)))
            + dot(grad_upward, upward_full, ((1,), (0,)))
        ).astype(jnp.bfloat16)
        out_float = expert_out.astype(jnp.float32)
        out_rows.append((share_rows[expert] * out_float).astype(jnp.bfloat16))
        back_rows.append(grad_route_in)
        gate_dots.append(jnp.sum(grad_block * out_float, axis=-1))

    out_rows = jnp.stack(out_rows).reshape(local_experts, row_count, capacity, D)
    back_rows = jnp.stack(back_rows).reshape(local_experts, row_count, capacity, D)
    gate_dots = jnp.stack(gate_dots).reshape(local_experts, row_count, capacity)
    grad_share = jnp.einsum(
        "rlct,lrc->rlt", onehot.astype(jnp.float32), gate_dots, precision=HIGHEST
    )
    back_part = jnp.einsum(
        "rlct,lrcd->rtd", onehot, back_rows, preferred_element_type=jnp.float32
    ).astype(jnp.bfloat16)
    out_part = jnp.einsum(
        "rlct,lrcd->rtd", onehot, out_rows, preferred_element_type=jnp.float32
    ).astype(jnp.bfloat16)
    grad_share_all = lax.all_gather(grad_share, "rows", axis=1, tiled=True)
    grad_shares = take(grad_share_all, row_place)
    back_sum = reduce_rows(back_part)
    mixture = reduce_rows(out_part)
    layer_output = (residual + mixture).astype(jnp.bfloat16)
    grad_out = cotangent.astype(jnp.float32)

    chosen_of = take(named, row_place)
    logits = take(logits_all, row_place)

    def shares_out(logit_cols):
        return jnp.where(chosen_of, shares(chosen_of, logit_cols), 0.0)

    _, router_pullback = jax.vjp(shares_out, logits)
    (grad_logits,) = router_pullback(grad_shares)
    router_float = router_full.astype(jnp.float32)
    grad_normed_two = back_sum + jnp.einsum(
        "et,de->td", grad_logits, router_float, precision=HIGHEST
    )
    router_grad = jnp.einsum(
        "td,et->de", normed_two_low.astype(jnp.float32), grad_logits, precision=HIGHEST
    )
    second_norm, second_pullback = jax.vjp(rms_norm, residual, experts_scale)
    grad_residual_norm, experts_gain_grad = second_pullback(grad_normed_two)
    grad_residual = grad_out + grad_residual_norm
    grad_branch_low = grad_residual.astype(jnp.bfloat16)
    out_grad = jnp.einsum(
        "tq,td->qd", heads_low, grad_branch_low, preferred_element_type=jnp.float32
    )
    grad_heads_low = jnp.einsum(
        "td,qd->tq", grad_branch_low, out_full, preferred_element_type=jnp.float32
    ).astype(jnp.bfloat16)
    grad_block = grad_heads_low.reshape(TOK_DEV, KV_HEADS, group_size, HEAD_DIM)

    attention = jnp.exp(block_scores() - log_total)
    attention_low = attention.astype(jnp.bfloat16)
    grad_attention = jnp.einsum(
        "qkgd,skd->kgqs", grad_block, value_tree, preferred_element_type=jnp.float32
    )
    grad_scores = (
        attention
        * (grad_attention - jnp.sum(attention * grad_attention, axis=-1, keepdims=True))
    ).astype(jnp.bfloat16)
    grad_query = (
        jnp.einsum("kgqs,skd->qkgd", grad_scores, key_tree, preferred_element_type=jnp.float32)
        * factor
    )
    key_tree_grad = (
        jnp.einsum("kgqs,qkgd->skd", grad_scores, query_group, preferred_element_type=jnp.float32)
        * factor
    ).reshape(2 * TOK_DEV, key_width)
    value_tree_grad = jnp.einsum(
        "kgqs,qkgd->skd", attention_low, grad_block, preferred_element_type=jnp.float32
    ).reshape(2 * TOK_DEV, key_width)
    tree_grads = jnp.concatenate([key_tree_grad, value_tree_grad], axis=1)
    arrived = lax.ppermute(
        tree_grads[:TOK_DEV].astype(jnp.bfloat16), "cols", [(j, i) for i, j in pairs]
    ).astype(jnp.float32)
    own_grads = jnp.where(holds_leaves, tree_grads[TOK_DEV:], tree_grads[:TOK_DEV] + arrived)
    grad_key_rot = own_grads[:, :key_width].reshape(TOK_DEV, KV_HEADS, HEAD_DIM)
    grad_key_low = (
        rotate(grad_key_rot, cosine, -sine_table).reshape(TOK_DEV, key_width).astype(jnp.bfloat16)
    )
    grad_value_low = own_grads[:, key_width:].astype(jnp.bfloat16)
    grad_query_low = (
        rotate(grad_query.reshape(TOK_DEV, HEADS, HEAD_DIM), cosine, -sine_table)
        .reshape(TOK_DEV, query_width)
        .astype(jnp.bfloat16)
    )
    query_grad = jnp.einsum(
        "td,tq->dq", normed_low, grad_query_low, preferred_element_type=jnp.float32
    )
    key_grad = jnp.einsum("td,tq->dq", normed_low, grad_key_low, preferred_element_type=jnp.float32)
    value_grad = jnp.einsum(
        "td,tq->dq", normed_low, grad_value_low, preferred_element_type=jnp.float32
    )
    grad_normed = (
        jnp.einsum("tq,dq->td", grad_query_low, query_full, preferred_element_type=jnp.float32)
        + jnp.einsum("tq,dq->td", grad_key_low, key_full, preferred_element_type=jnp.float32)
        + jnp.einsum("tq,dq->td", grad_value_low, value_full, preferred_element_type=jnp.float32)
    )
    first_norm, first_pullback = jax.vjp(rms_norm, token_float, attention_scale)
    grad_tokens_norm, attention_gain_grad = first_pullback(grad_normed)
    tokens_grad = (grad_residual + grad_tokens_norm).astype(jnp.bfloat16)

    def by_shard(grad, width):
        parts = grad.astype(jnp.bfloat16).reshape(row_count, depth, col_count, width)
        return jnp.swapaxes(parts, 1, 2)

    def gain_shard(grad):
        parts = grad.astype(jnp.bfloat16).reshape(row_count, col_count, gain_part)
        return jnp.pad(parts, ((0, 0), (0, 0), (0, depth - gain_part)))[..., None]

    packed_grad = jnp.concatenate(
        [
            by_shard(query_grad, query_part),
            by_shard(key_grad, key_part),
            by_shard(value_grad, key_part),
            by_shard(out_grad, query_part),
            by_shard(router_grad, router_part),
            gain_shard(attention_gain_grad),
            gain_shard(experts_gain_grad),
            jnp.zeros((row_count, col_count, depth, spare - router_part - 2), jnp.bfloat16),
        ],
        axis=-1,
    )
    row_sums = reduce_rows(packed_grad.reshape(row_count, col_count * depth, packed_width))
    row_sums = row_sums.astype(jnp.bfloat16).reshape(col_count, depth, packed_width)
    row_slots = jnp.take(row_sums, shards, axis=0)
    sums = reduce_slots([row_slots[i] for i in range(col_count)])

    def final(which):
        return jnp.stack([reduced[expert][which] for expert in range(local_experts)])

    return (
        layer_output,
        tokens_grad,
        sums[:, :key_at],
        sums[:, key_at:value_at],
        sums[:, value_at:out_at],
        sums[:, out_at:extra_at],
        sums[:, extra_at:gain_at],
        sums[:gain_part, gain_at],
        sums[:gain_part, gain_at + 1],
        jnp.swapaxes(final(0), 1, 2),
        jnp.swapaxes(final(1), 1, 2),
        final(2),
    )


def solution(mesh):
    in_specs = (
        P(("rows", "cols"), None),
        P("rows", "cols"),
        P("rows", "cols"),
        P("rows", "cols"),
        P("rows", "cols"),
        P("rows", "cols"),
        P(("rows", "cols")),
        P(("rows", "cols")),
        P("rows", None, "cols"),
        P("rows", None, "cols"),
        P("rows", "cols", None),
        P(("rows", "cols"), None),
        P(),
        P(("rows", "cols"), None),
    )
    out_specs = (
        P(("rows", "cols"), None),
        P(("rows", "cols"), None),
        P("rows", "cols"),
        P("rows", "cols"),
        P("rows", "cols"),
        P("rows", "cols"),
        P("rows", "cols"),
        P(("rows", "cols")),
        P(("rows", "cols")),
        P("rows", None, "cols"),
        P("rows", None, "cols"),
        P("rows", "cols", None),
    )
    return jax.shard_map(
        on_device, mesh=mesh, in_specs=in_specs, out_specs=out_specs, check_vma=False
    )
```

time: 1450 us -> 1320 us (0.910)
  blocking collectives: 160 us -> 18.4 us
  waiting for transfers between devices: 688 us -> 589 us
  starting transfers between devices: 29.8 us -> 82.5 us
  local copies, waits for them, and re-layouts: 182 us -> 222 us
  matrix products: 236 us -> 256 us
    ppermute x4 -> x46, waiting for transfers between devices: 0.01 us -> 589 us  [the longest x20 190 us: flip(): return lax.ppermute(block, 'rows', [(i, i ^ bit) for i in range(count)])]
    reduce_scatter x7 -> x0, waiting for transfers between devices: 337 us -> none  [the longest x1 85 us: on_device(): lax.psum_scatter(upward_grad.astype(jnp.bfloat16), 'cols', scatter_dimens...]
    all_to_all x4 -> x0, waiting for transfers between devices: 243 us -> none  [the longest x1 80.8 us: on_device(): lax.all_to_all(send_rows.reshape(local_experts, row_count, capacity, D),...]
    unnamed x22 -> x2, waiting for transfers between devices: 108 us -> 0.71 us
    all_gather x8 -> x2, blocking collectives: 113 us -> 18.4 us  [the longest x1 9.26 us: on_device(): grad_share_all = lax.all_gather(grad_share, 'rows', axis=1, tiled=True)]
    ppermute x4 -> x46, starting transfers between devices: 8.54 us -> 82.4 us  [the longest x20 18.5 us: flip(): return lax.ppermute(block, 'rows', [(i, i ^ bit) for i in range(count)])]
    gather x5 -> x2, local copies, waits for them, and re-layouts: 69.8 us -> 1.3 us  [the longest x1 0.65 us: on_device(): packed_cols = jnp.take(packed_slots, slot_of_shard, axis=0)]
    unnamed x4 -> x0, blocking collectives: 46.9 us -> none
  transfers between devices with their start and end apart: 25 -> 48, of which waited for: 16 -> 31; matrix products, arithmetic and copies ran while one was open for 28% -> 30% of each run, Pallas kernels for 0% -> 0%
where the time goes in v1:
time: 1320 us; the launch traced here: 1310 us
  waiting for transfers between devices  589 us (45%)
  matrix products  256 us (19%)
  local copies, waits for them, and re-layouts  222 us (17%)
  other arithmetic  130 us (10%)
  starting transfers between devices  82.5 us (6%)
  blocking collectives  18.4 us (1%)
  between operations  16.6 us (1%)
    ppermute x20, waiting for transfers between devices, flip(): return lax.ppermute(block, 'rows', [(i, i ^ bit) for i in range(count)])  190 us
    ppermute x3, waiting for transfers between devices, gather_slots(): above = lax.ppermute(block, 'cols', [(1, 0), (2, 1), (3, 2)])  110 us
    dot_general x18, matrix products, dot(): lax.dot_general(one, two, (dims, ((), ())), preferred_element_type=jnp.fl...  94.8 us
    ppermute x3, waiting for transfers between devices, reduce_slots(): relay = lax.ppermute(second, 'cols', [(1, 3), (0, 1), (2, 0), (3, 2)])  84.8 us
    ppermute x3, waiting for transfers between devices, gather_slots(): second = lax.ppermute(payload, 'cols', [(3, 1), (1, 0), (0, 2), (2, 3)])  59.6 us
    ppermute x3, waiting for transfers between devices, reduce_slots(): below = lax.ppermute(upward_load, 'cols', [(0, 1), (1, 2), (2, 3)])  49.8 us
    ppermute x3, waiting for transfers between devices, reduce_slots(): above = lax.ppermute(downward_load, 'cols', [(1, 0), (2, 1), (3, 2)])  46 us
    ppermute x3, waiting for transfers between devices, gather_slots(): far = lax.ppermute(block, 'cols', [(0, 3), (3, 0)])  44.7 us
  transfers between devices with their start and end apart: 48, of which 31 were waited for; matrix products, arithmetic and copies ran while one was open for 30% of the time, Pallas kernels for 0%

profile of v1, /device:TPU:0, one launch (start us, length us, event | category | flops | bytes accessed | tf_op | source)
XLA Modules:
  0.0 1314.6 jit_solution(17651322029654340745)
XLA Ops:
  28.9 8.3 collective-permute-done.3
  40.0 7.3 collective-permute-done.2
  51.4 31.3 %collective-permute-done.4 = bf16[768,1024]{1,0:T(8,128)(2,1)S(1)} collective-permute-done((bf16[768,1024]{1,0:T(8,128)(2,1)S(1)}, bf16[768,1024]{1,0:T(8,128)(2,1)S(1)}, u32[]{:S(2)}, u32[]{:S(2)}) %collective-permute-start.4) | collective-permute-done | bytes 1572896 | tf_op jit(solution)/shard_map/ppermute | solution.py:149
  88.8 12.1 collective-permute-done.6
  113.5 7.5 collective-permute-done.8
  132.5 7.1 slice_bitcast_fusion
  152.9 6.7 copy.211
  191.6 11.3 fusion.12
  202.9 11.5 fusion.3
  214.5 12.0 fusion.86
  244.2 72.6 %collective-permute-done.10 = bf16[3,192,1536]{2,1,0:T(8,128)(2,1)S(1)} collective-permute-done((bf16[3,192,1536]{2,1,0:T(8,128)(2,1)S(1)}, bf16[3,192,1536]{2,1,0:T(8,128)(2,1)S(1)}, u32[]{:S(2)}, u32[]{:S(2)}) %collective-permute-start.10) | collective-permute-done | bytes 1769504 | tf_op jit(solution)/shard_map/ppermute | solution.py:105
  324.1 35.7 %collective-permute-done.12 = bf16[3,192,1536]{2,1,0:T(8,128)(2,1)S(1)} collective-permute-done((bf16[3,192,1536]{2,1,0:T(8,128)(2,1)S(1)}, bf16[3,192,1536]{2,1,0:T(8,128)(2,1)S(1)}, u32[]{:S(2)}, u32[]{:S(2)}) %collective-permute-start.12) | collective-permute-done | bytes 1769504 | tf_op jit(solution)/shard_map/ppermute | solution.py:109
  368.8 35.4 %collective-permute-done.14 = bf16[3,192,1536]{2,1,0:T(8,128)(2,1)S(1)} collective-permute-done((bf16[3,192,1536]{2,1,0:T(8,128)(2,1)S(1)}, bf16[3,192,1536]{2,1,0:T(8,128)(2,1)S(1)}, u32[]{:S(2)}, u32[]{:S(2)}) %collective-permute-start.14) | collective-permute-done | bytes 1769504 | tf_op jit(solution)/shard_map/ppermute | solution.py:105
  405.8 35.2 %collective-permute-done.17 = bf16[3,192,1536]{2,1,0:T(8,128)(2,1)S(1)} collective-permute-done((bf16[3,192,1536]{2,1,0:T(8,128)(2,1)S(1)}, bf16[3,192,1536]{2,1,0:T(8,128)(2,1)S(1)}, u32[]{:S(2)}, u32[]{:S(2)}) %collective-permute-start.17) | collective-permute-done | bytes 1769504 | tf_op jit(solution)/shard_map/ppermute | solution.py:107
  447.2 9.2 all-gather
  465.1 16.6 %collective-permute-done.16 = bf16[3,192,1536]{2,1,0:T(8,128)(2,1)} collective-permute-done((bf16[3,192,1536]{2,1,0:T(8,128)(2,1)}, bf16[3,192,1536]{2,1,0:T(8,128)(2,1)}, u32[]{:S(2)}, u32[]{:S(2)}) %collective-permute-start.16) | collective-permute-done | bytes 1769504 | tf_op jit(solution)/shard_map/ppermute | solution.py:109
  491.6 8.1 fusion.216
  503.0 6.4 fusion.39
  524.6 9.4 fusion.42
  539.7 7.5 multiply_convert_fusion.2
  575.0 12.3 fusion.14
  587.2 10.3 bitcast_convert_fusion.1
  608.5 7.3 fusion.27
  620.9 10.3 bitcast_convert_fusion
  660.0 9.3 all_gather.27
  678.7 6.5 fusion.9
  689.8 6.5 fusion.8
  712.6 13.9 %collective-permute-done.19 = bf16[2,256,1536]{2,1,0:T(8,128)(2,1)} collective-permute-done((bf16[2,256,1536]{2,1,0:T(8,128)(2,1)}, bf16[2,256,1536]{2,1,0:T(8,128)(2,1)}, u32[]{:S(2)}, u32[]{:S(2)}) %collective-permute-start.19) | collective-permute-done | bytes 1572896 | tf_op jit(solution)/shard_map/ppermute | solution.py:149
  729.1 30.5 %collective-permute-done.24 = bf16[2,256,1536]{2,1,0:T(8,128)(2,1)} collective-permute-done((bf16[2,256,1536]{2,1,0:T(8,128)(2,1)}, bf16[2,256,1536]{2,1,0:T(8,128)(2,1)}, u32[]{:S(2)}, u32[]{:S(2)}) %collective-permute-start.24) | collective-permute-done | bytes 1572896 | tf_op jit(solution)/shard_map/ppermute | solution.py:149
  762.3 18.6 %collective-permute-done.26 = bf16[2,256,1536]{2,1,0:T(8,128)(2,1)S(1)} collective-permute-done((bf16[2,256,1536]{2,1,0:T(8,128)(2,1)S(1)}, bf16[2,256,1536]{2,1,0:T(8,128)(2,1)S(1)}, u32[]{:S(2)}, u32[]{:S(2)}) %collective-permute-start.26) | collective-permute-done | bytes 1572896 | tf_op jit(solution)/shard_map/ppermute | solution.py:149
  784.1 29.3 %collective-permute-done.25 = bf16[256,1536]{1,0:T(8,128)(2,1)S(1)} collective-permute-done((bf16[256,1536]{1,0:T(8,128)(2,1)S(1)}, bf16[256,1536]{1,0:T(8,128)(2,1)S(1)}, u32[]{:S(2)}, u32[]{:S(2)}) %collective-permute-start.25) | collective-permute-done | bytes 786464 | tf_op jit(solution)/shard_map/ppermute | solution.py:149
  830.3 11.6 fusion.5
  841.9 21.8 %fusion = (f32[2,6,512]{2,1,0:T(8,128)S(1)}, f32[2,1024,512,6]{2,1,3,0:T(8,128)}) fusion(f32[2,6,512]{2,1,0:T(8,128)S(1)} %copy-done.103, f32[2,1024,512,6]{2,1,3,0:T(8,128)} %get-tuple-element.210, pred[512,1024]{0,1:T(8,128)(4,1)S(1)} %copy-done.3, bf16[1024,2,128,1]{0,2,3,1:T(8,128)(2,1)} %bitcast.637, bf16[512,2,6,128]{0,3,2,1:T(8,128)(2,1)S(1)} %bitcast.585), kind=kOutput, calls=%fused_computation.4 | convolution fusion | flops 1642063872 | bytes 53002240 | tf_op jit(solution)/shard_map/qkgd,skd->kgqs/dot_general | solution.py:473
  863.8 22.4 %fusion.2 = bf16[2,6,512,1024]{2,3,1,0:T(8,128)(2,1)} fusion(f32[2,1024,512,6]{2,1,3,0:T(8,128)} %get-tuple-element.215, f32[2,6,512]{2,1,0:T(8,128)S(1)} %get-tuple-element.214, f32[2,6,512]{2,1,0:T(8,128)S(1)} %copy-done.103, f32[2,1024,512,6]{2,1,3,0:T(8,128)} %get-tuple-element.210, pred[512,1024]{0,1:T(8,128)(4,1)S(1)} %copy-done.3), kind=kLoop, calls=%fused_computation.6 | loop fusion | flops 37748736 | bytes 63488000 | tf_op jit(solution)/shard_map/convert_element_type | solution.py:479
  886.2 9.4 fusion.93
  895.7 8.1 convolution_multiply_fusion
  903.8 9.0 reshape.721
  930.2 9.1 reshape.718
  949.2 7.2 fusion.223
  981.3 22.9 %concatenate.85 = bf16[2,2,2,768,1024]{4,3,2,1,0:T(8,128)(2,1)} concatenate(bf16[2,2,2,768,384]{4,3,2,1,0:T(8,128)(2,1)} %bitcast.572, bf16[2,2,2,768,64]{4,3,2,1,0:T(8,128)(2,1)} %bitcast.591, bf16[2,2,2,768,64]{4,3,2,1,0:T(8,128)(2,1)} %bitcast.590, bf16[2,2,2,768,384]{4,3,2,1,0:T(8,128)(2,1)} %bitcast.571, bf16[2,2,2,768,4]{4,3,2,1,0:T(8,128)(2,1)S(1)} %bitcast.589, ...), dimensions={4} | concatenate | bytes 25165824 | tf_op jit(solution)/shard_map/concatenate | solution.py:530
  1028.2 69.5 %collective-permute-done.42 = bf16[3,192,1536]{2,1,0:T(8,128)(2,1)S(1)} collective-permute-done((bf16[3,192,1536]{2,1,0:T(8,128)(2,1)S(1)}, bf16[3,192,1536]{2,1,0:T(8,128)(2,1)S(1)}, u32[]{:S(2)}, u32[]{:S(2)}) %collective-permute-start.42) | collective-permute-done | bytes 1769504 | tf_op jit(solution)/shard_map/ppermute | solution.py:127
  1104.7 27.6 %collective-permute-done.39 = bf16[3,192,1536]{2,1,0:T(8,128)(2,1)S(1)} collective-permute-done((bf16[3,192,1536]{2,1,0:T(8,128)(2,1)S(1)}, bf16[3,192,1536]{2,1,0:T(8,128)(2,1)S(1)}, u32[]{:S(2)}, u32[]{:S(2)}) %collective-permute-start.39) | collective-permute-done | bytes 1769504 | tf_op jit(solution)/shard_map/ppermute | solution.py:137
  1133.7 38.6 %collective-permute-done.40 = bf16[3,192,1536]{2,1,0:T(8,128)(2,1)S(1)} collective-permute-done((bf16[3,192,1536]{2,1,0:T(8,128)(2,1)S(1)}, bf16[3,192,1536]{2,1,0:T(8,128)(2,1)S(1)}, u32[]{:S(2)}, u32[]{:S(2)}) %collective-permute-start.40) | collective-permute-done | bytes 1769504 | tf_op jit(solution)/shard_map/ppermute | solution.py:138
  1177.0 7.8 fusion.7
  1186.9 20.4 %collective-permute-done.43 = bf16[3,192,1536]{2,1,0:T(8,128)(2,1)} collective-permute-done((bf16[3,192,1536]{2,1,0:T(8,128)(2,1)}, bf16[3,192,1536]{2,1,0:T(8,128)(2,1)}, u32[]{:S(2)}, u32[]{:S(2)}) %collective-permute-start.43) | collective-permute-done | bytes 1769504 | tf_op jit(solution)/shard_map/ppermute | solution.py:137
  1224.1 27.9 %collective-permute-done.32 = bf16[2,384,1024]{2,1,0:T(8,128)(2,1)S(1)} collective-permute-done((bf16[2,384,1024]{2,1,0:T(8,128)(2,1)S(1)}, bf16[2,384,1024]{2,1,0:T(8,128)(2,1)S(1)}, u32[]{:S(2)}, u32[]{:S(2)}) %collective-permute-start.32) | collective-permute-done | bytes 1572896 | tf_op jit(solution)/shard_map/ppermute | solution.py:149
  1257.1 10.8 collective-permute-done.31
  1276.9 15.3 %collective-permute-done.34 = bf16[192,1024]{1,0:T(8,128)(2,1)S(1)} collective-permute-done((bf16[192,1024]{1,0:T(8,128)(2,1)S(1)}, bf16[192,1024]{1,0:T(8,128)(2,1)S(1)}, u32[]{:S(2)}, u32[]{:S(2)}) %collective-permute-start.34) | collective-permute-done | bytes 393248 | tf_op jit(solution)/shard_map/ppermute | solution.py:127
  (596 shorter events, 452.5 us)
Async XLA Ops:
  7.2 484.4 %all-gather.6.cloned.1.call-start = ((), (), s32[]{:S(2)}) async-start(), calls=%async_computation | async-start | bytes 14155776 | tf_op jit(solution)/shard_map/all_gather | solution.py:338
  12.5 14.0 %collective-permute-start = (bf16[192,1024]{1,0:T(8,128)(2,1)S(1)}, bf16[192,1024]{1,0:T(8,128)(2,1)S(1)}, u32[]{:S(2)}, u32[]{:S(2)}) collective-permute-start(bf16[192,1024]{1,0:T(8,128)(2,1)S(1)} %concatenate.65), channel_id=1, source_target_pairs={{1,0},{2,1},{3,2},{5,4},{6,5},{7,6},{9,8},{10,9},{11,10},{13,12},{... | collective-permute-start | bytes 1179656 | tf_op jit(solution)/shard_map/ppermute | solution.py:105
  13.8 15.1 %collective-permute-start.1 = (bf16[192,1024]{1,0:T(8,128)(2,1)S(1)}, bf16[192,1024]{1,0:T(8,128)(2,1)S(1)}, u32[]{:S(2)}, u32[]{:S(2)}) collective-permute-start(bf16[192,1024]{1,0:T(8,128)(2,1)S(1)} %concatenate.65), channel_id=1, source_target_pairs={{0,1},{1,2},{2,3},{4,5},{5,6},{6,7},{8,9},{9,10},{10,11},{12,13},{... | collective-permute-start | bytes 1179656 | tf_op jit(solution)/shard_map/ppermute | solution.py:106
  19.4 17.8 %collective-permute-start.3 = (bf16[192,1024]{1,0:T(8,128)(2,1)S(1)}, bf16[192,1024]{1,0:T(8,128)(2,1)S(1)}, u32[]{:S(2)}, u32[]{:S(2)}) collective-permute-start(bf16[192,1024]{1,0:T(8,128)(2,1)S(1)} %concatenate.65), channel_id=1, source_target_pairs={{0,3},{3,0},{4,7},{7,4},{8,11},{11,8},{12,15},{15,12},{16,19},{19,... | collective-permute-start | bytes 1179656 | tf_op jit(solution)/shard_map/ppermute | solution.py:107
  37.2 10.0 collective-permute-start.2
  48.4 34.4 %collective-permute-start.4 = (bf16[768,1024]{1,0:T(8,128)(2,1)S(1)}, bf16[768,1024]{1,0:T(8,128)(2,1)S(1)}, u32[]{:S(2)}, u32[]{:S(2)}) collective-permute-start(bf16[768,1024]{1,0:T(8,128)(2,1)S(1)} %bitcast.586), channel_id=1, source_target_pairs={{0,8},{4,12},{8,0},{12,4},{16,24},{20,28},{24,16},{28,20},{1,9},{5... | collective-permute-start | bytes 4718600 | tf_op jit(solution)/shard_map/ppermute | solution.py:149
  49.9 35.3 %collective-permute-start.5 = (bf16[768,1024]{1,0:T(8,128)(2,1)S(1)}, bf16[768,1024]{1,0:T(8,128)(2,1)S(1)}, u32[]{:S(2)}, u32[]{:S(2)}) collective-permute-start(bf16[768,1024]{1,0:T(8,128)(2,1)S(1)} %bitcast.587), channel_id=1, source_target_pairs={{0,16},{4,20},{8,24},{12,28},{16,0},{20,4},{24,8},{28,12},{1,17},{... | collective-permute-start | bytes 4718600 | tf_op jit(solution)/shard_map/ppermute | solution.py:149
  83.7 17.2 %collective-permute-start.6 = (bf16[384,1024]{1,0:T(8,128)(2,1)}, bf16[384,1024]{1,0:T(8,128)(2,1)}, u32[]{:S(2)}, u32[]{:S(2)}) collective-permute-start(bf16[384,1024]{1,0:T(8,128)(2,1)} %slice.450), channel_id=1, source_target_pairs={{0,16},{4,20},{8,24},{12,28},{16,0},{20,4},{24,8},{28,12},{1,17},{... | collective-permute-start | bytes 2359304 | tf_op jit(solution)/shard_map/ppermute | solution.py:149
  87.3 16.6 %collective-permute-start.7 = (bf16[384,1024]{1,0:T(8,128)(2,1)}, bf16[384,1024]{1,0:T(8,128)(2,1)}, u32[]{:S(2)}, u32[]{:S(2)}) collective-permute-start(bf16[384,1024]{1,0:T(8,128)(2,1)} %slice.451), channel_id=1, source_target_pairs={{0,8},{4,12},{8,0},{12,4},{16,24},{20,28},{24,16},{28,20},{1,9},{5... | collective-permute-start | bytes 2359304 | tf_op jit(solution)/shard_map/ppermute | solution.py:149
  110.5 10.5 collective-permute-start.8
  171.8 18.1 %collective-permute-start.9 = (bf16[512,512]{0,1:T(8,128)(2,1)}, bf16[512,512]{0,1:T(8,128)(2,1)}, u32[]{:S(2)}, u32[]{:S(2)}) collective-permute-start(bf16[512,512]{0,1:T(8,128)(2,1)} %get-tuple-element.202), channel_id=1, source_target_pairs={{1,0},{3,2},{5,4},{7,6},{9,8},{11,10},{13,12},{15,14},{17,16},{19,... | collective-permute-start | bytes 1572872 | tf_op jit(solution)/shard_map/ppermute | solution.py:302
  232.7 291.9 %all-gather.8.cloned.1.call-start = ((), (), s32[]{:S(2)}) async-start(), calls=%async_computation.1 | async-start | bytes 14155776 | tf_op jit(solution)/shard_map/all_gather | solution.py:278
  234.7 82.1 %collective-permute-start.10 = (bf16[3,192,1536]{2,1,0:T(8,128)(2,1)S(1)}, bf16[3,192,1536]{2,1,0:T(8,128)(2,1)S(1)}, u32[]{:S(2)}, u32[]{:S(2)}) collective-permute-start(bf16[3,192,1536]{2,1,0:T(8,128)(2,1)S(1)} %pad_maximum_fusion.5), channel_id=1, source_target_pairs={{1,0},{2,1},{3,2},{5,4},{6,5},{7,6},{9,8},{10,9},{11,10},{13,12},{... | collective-permute-start | bytes 5308424 | tf_op jit(solution)/shard_map/ppermute | solution.py:105
  236.0 80.8 %collective-permute-start.11 = (bf16[3,192,1536]{2,1,0:T(8,128)(2,1)S(1)}, bf16[3,192,1536]{2,1,0:T(8,128)(2,1)S(1)}, u32[]{:S(2)}, u32[]{:S(2)}) collective-permute-start(bf16[3,192,1536]{2,1,0:T(8,128)(2,1)S(1)} %pad_maximum_fusion.5), channel_id=1, source_target_pairs={{0,1},{1,2},{2,3},{4,5},{5,6},{6,7},{8,9},{9,10},{10,11},{12,13},{... | collective-permute-start | bytes 5308424 | tf_op jit(solution)/shard_map/ppermute | solution.py:106
  242.3 75.7 %collective-permute-start.13 = (bf16[3,192,1536]{2,1,0:T(8,128)(2,1)S(1)}, bf16[3,192,1536]{2,1,0:T(8,128)(2,1)S(1)}, u32[]{:S(2)}, u32[]{:S(2)}) collective-permute-start(bf16[3,192,1536]{2,1,0:T(8,128)(2,1)S(1)} %pad_maximum_fusion.5), channel_id=1, source_target_pairs={{0,3},{3,0},{4,7},{7,4},{8,11},{11,8},{12,15},{15,12},{16,19},{19,... | collective-permute-start | bytes 5308424 | tf_op jit(solution)/shard_map/ppermute | solution.py:107
  320.3 39.5 %collective-permute-start.12 = (bf16[3,192,1536]{2,1,0:T(8,128)(2,1)S(1)}, bf16[3,192,1536]{2,1,0:T(8,128)(2,1)S(1)}, u32[]{:S(2)}, u32[]{:S(2)}) collective-permute-start(bf16[3,192,1536]{2,1,0:T(8,128)(2,1)S(1)} %get-tuple-element.144), channel_id=1, source_target_pairs={{3,1},{1,0},{0,2},{2,3},{7,5},{5,4},{4,6},{6,7},{11,9},{9,8},{8,10... | collective-permute-start | bytes 5308424 | tf_op jit(solution)/shard_map/ppermute | solution.py:109
  359.8 44.4 %collective-permute-start.14 = (bf16[3,192,1536]{2,1,0:T(8,128)(2,1)S(1)}, bf16[3,192,1536]{2,1,0:T(8,128)(2,1)S(1)}, u32[]{:S(2)}, u32[]{:S(2)}) collective-permute-start(bf16[3,192,1536]{2,1,0:T(8,128)(2,1)S(1)} %pad_maximum_fusion.6), channel_id=1, source_target_pairs={{1,0},{2,1},{3,2},{5,4},{6,5},{7,6},{9,8},{10,9},{11,10},{13,12},{... | collective-permute-start | bytes 5308424 | tf_op jit(solution)/shard_map/ppermute | solution.py:105
  361.1 44.7 %collective-permute-start.15 = (bf16[3,192,1536]{2,1,0:T(8,128)(2,1)S(1)}, bf16[3,192,1536]{2,1,0:T(8,128)(2,1)S(1)}, u32[]{:S(2)}, u32[]{:S(2)}) collective-permute-start(bf16[3,192,1536]{2,1,0:T(8,128)(2,1)S(1)} %pad_maximum_fusion.6), channel_id=1, source_target_pairs={{0,1},{1,2},{2,3},{4,5},{5,6},{6,7},{8,9},{9,10},{10,11},{12,13},{... | collective-permute-start | bytes 5308424 | tf_op jit(solution)/shard_map/ppermute | solution.py:106
  366.8 74.2 %collective-permute-start.17 = (bf16[3,192,1536]{2,1,0:T(8,128)(2,1)S(1)}, bf16[3,192,1536]{2,1,0:T(8,128)(2,1)S(1)}, u32[]{:S(2)}, u32[]{:S(2)}) collective-permute-start(bf16[3,192,1536]{2,1,0:T(8,128)(2,1)S(1)} %pad_maximum_fusion.6), channel_id=1, source_target_pairs={{0,3},{3,0},{4,7},{7,4},{8,11},{11,8},{12,15},{15,12},{16,19},{19,... | collective-permute-start | bytes 5308424 | tf_op jit(solution)/shard_map/ppermute | solution.py:107
  443.5 38.2 %collective-permute-start.16 = (bf16[3,192,1536]{2,1,0:T(8,128)(2,1)}, bf16[3,192,1536]{2,1,0:T(8,128)(2,1)}, u32[]{:S(2)}, u32[]{:S(2)}) collective-permute-start(bf16[3,192,1536]{2,1,0:T(8,128)(2,1)} %get-tuple-element.145), channel_id=1, source_target_pairs={{3,1},{1,0},{0,2},{2,3},{7,5},{5,4},{4,6},{6,7},{11,9},{9,8},{8,10... | collective-permute-start | bytes 5308424 | tf_op jit(solution)/shard_map/ppermute | solution.py:109
  605.2 73.5 %collective-permute-start.18 = (bf16[2,2,512,1536]{3,2,1,0:T(8,128)(2,1)}, bf16[2,2,512,1536]{3,2,1,0:T(8,128)(2,1)}, u32[]{:S(2)}, u32[]{:S(2)}) collective-permute-start(bf16[2,2,512,1536]{3,2,1,0:T(8,128)(2,1)} %dynamic-slice_bitcast_fusion.2), channel_id=1, source_target_pairs={{0,4},{4,0},{8,12},{12,8},{16,20},{20,16},{24,28},{28,24},{1,5},{5... | collective-permute-start | bytes 18874376 | tf_op jit(solution)/shard_map/ppermute | solution.py:149
  638.7 51.0 %collective-permute-start.23 = (bf16[2,2,512,1536]{3,2,1,0:T(8,128)(2,1)}, bf16[2,2,512,1536]{3,2,1,0:T(8,128)(2,1)}, u32[]{:S(2)}, u32[]{:S(2)}) collective-permute-start(bf16[2,2,512,1536]{3,2,1,0:T(8,128)(2,1)} %dynamic-slice_bitcast_fusion.1), channel_id=1, source_target_pairs={{0,4},{4,0},{8,12},{12,8},{16,20},{20,16},{24,28},{28,24},{1,5},{5... | collective-permute-start | bytes 18874376 | tf_op jit(solution)/shard_map/ppermute | solution.py:149
  654.4 366.6 %collective-permute-start.38 = (bf16[3,192,1536]{2,1,0:T(8,128)(2,1)}, bf16[3,192,1536]{2,1,0:T(8,128)(2,1)}, u32[]{:S(2)}, u32[]{:S(2)}) collective-permute-start(bf16[3,192,1536]{2,1,0:T(8,128)(2,1)} %pad_maximum_fusion.9), channel_id=1, source_target_pairs={{1,3},{0,1},{2,0},{3,2},{5,7},{4,5},{6,4},{7,6},{9,11},{8,9},{10,8... | collective-permute-start | bytes 5308424 | tf_op jit(solution)/shard_map/ppermute | solution.py:127
  688.9 37.5 %collective-permute-start.19 = (bf16[2,256,1536]{2,1,0:T(8,128)(2,1)}, bf16[2,256,1536]{2,1,0:T(8,128)(2,1)}, u32[]{:S(2)}, u32[]{:S(2)}) collective-permute-start(bf16[2,256,1536]{2,1,0:T(8,128)(2,1)} %dynamic-slice_bitcast_fusion.8), channel_id=1, source_target_pairs={{0,8},{4,12},{8,0},{12,4},{16,24},{20,28},{24,16},{28,20},{1,9},{5... | collective-permute-start | bytes 4718600 | tf_op jit(solution)/shard_map/ppermute | solution.py:149
  701.5 58.1 %collective-permute-start.24 = (bf16[2,256,1536]{2,1,0:T(8,128)(2,1)}, bf16[2,256,1536]{2,1,0:T(8,128)(2,1)}, u32[]{:S(2)}, u32[]{:S(2)}) collective-permute-start(bf16[2,256,1536]{2,1,0:T(8,128)(2,1)} %dynamic-slice_bitcast_fusion.6), channel_id=1, source_target_pairs={{0,8},{4,12},{8,0},{12,4},{16,24},{20,28},{24,16},{28,20},{1,9},{5... | collective-permute-start | bytes 4718600 | tf_op jit(solution)/shard_map/ppermute | solution.py:149
  709.8 72.4 %collective-permute-start.21 = (bf16[2,256,1536]{2,1,0:T(8,128)(2,1)S(1)}, bf16[2,256,1536]{2,1,0:T(8,128)(2,1)S(1)}, u32[]{:S(2)}, u32[]{:S(2)}) collective-permute-start(bf16[2,256,1536]{2,1,0:T(8,128)(2,1)S(1)} %dynamic-slice_bitcast_fusion.7), channel_id=1, source_target_pairs={{0,16},{4,20},{8,24},{12,28},{16,0},{20,4},{24,8},{28,12},{1,17},{... | collective-permute-start | bytes 4718600 | tf_op jit(solution)/shard_map/ppermute | solution.py:149
  711.7 69.2 %collective-permute-start.26 = (bf16[2,256,1536]{2,1,0:T(8,128)(2,1)S(1)}, bf16[2,256,1536]{2,1,0:T(8,128)(2,1)S(1)}, u32[]{:S(2)}, u32[]{:S(2)}) collective-permute-start(bf16[2,256,1536]{2,1,0:T(8,128)(2,1)S(1)} %dynamic-slice_bitcast_fusion.5), channel_id=1, source_target_pairs={{0,16},{4,20},{8,24},{12,28},{16,0},{20,4},{24,8},{28,12},{1,17},{... | collective-permute-start | bytes 4718600 | tf_op jit(solution)/shard_map/ppermute | solution.py:149
  728.4 87.9 %collective-permute-start.20 = (bf16[256,1536]{1,0:T(8,128)(2,1)S(1)}, bf16[256,1536]{1,0:T(8,128)(2,1)S(1)}, u32[]{:S(2)}, u32[]{:S(2)}) collective-permute-start(bf16[256,1536]{1,0:T(8,128)(2,1)S(1)} %dynamic-slice_bitcast_fusion.14), channel_id=1, source_target_pairs={{0,16},{4,20},{8,24},{12,28},{16,0},{20,4},{24,8},{28,12},{1,17},{... | collective-permute-start | bytes 2359304 | tf_op jit(solution)/shard_map/ppermute | solution.py:149
  761.6 51.8 %collective-permute-start.25 = (bf16[256,1536]{1,0:T(8,128)(2,1)S(1)}, bf16[256,1536]{1,0:T(8,128)(2,1)S(1)}, u32[]{:S(2)}, u32[]{:S(2)}) collective-permute-start(bf16[256,1536]{1,0:T(8,128)(2,1)S(1)} %dynamic-slice_bitcast_fusion.12), channel_id=1, source_target_pairs={{0,16},{4,20},{8,24},{12,28},{16,0},{20,4},{24,8},{28,12},{1,17},{... | collective-permute-start | bytes 2359304 | tf_op jit(solution)/shard_map/ppermute | solution.py:149
  781.4 32.2 %collective-permute-start.27 = (bf16[256,1536]{1,0:T(8,128)(2,1)S(1)}, bf16[256,1536]{1,0:T(8,128)(2,1)S(1)}, u32[]{:S(2)}, u32[]{:S(2)}) collective-permute-start(bf16[256,1536]{1,0:T(8,128)(2,1)S(1)} %dynamic-slice_bitcast_fusion.11), channel_id=1, source_target_pairs={{0,8},{4,12},{8,0},{12,4},{16,24},{20,28},{24,16},{28,20},{1,9},{5... | collective-permute-start | bytes 2359304 | tf_op jit(solution)/shard_map/ppermute | solution.py:149
  782.8 33.8 %collective-permute-start.22 = (bf16[256,1536]{1,0:T(8,128)(2,1)S(1)}, bf16[256,1536]{1,0:T(8,128)(2,1)S(1)}, u32[]{:S(2)}, u32[]{:S(2)}) collective-permute-start(bf16[256,1536]{1,0:T(8,128)(2,1)S(1)} %dynamic-slice_bitcast_fusion.13), channel_id=1, source_target_pairs={{0,8},{4,12},{8,0},{12,4},{16,24},{20,28},{24,16},{28,20},{1,9},{5... | collective-permute-start | bytes 2359304 | tf_op jit(solution)/shard_map/ppermute | solution.py:149
  919.3 37.2 %collective-permute-start.28 = (bf16[512,512]{0,1:T(8,128)(2,1)}, bf16[512,512]{0,1:T(8,128)(2,1)S(1)}, u32[]{:S(2)}, u32[]{:S(2)}) collective-permute-start(bf16[512,512]{0,1:T(8,128)(2,1)} %fusion.109), channel_id=1, source_target_pairs={{0,1},{2,3},{4,5},{6,7},{8,9},{10,11},{12,13},{14,15},{16,17},{18,... | collective-permute-start | bytes 1572872 | tf_op jit(solution)/shard_map/ppermute | solution.py:492
  1008.0 169.0 %collective-permute-start.29 = (bf16[2,2,768,1024]{3,2,1,0:T(8,128)(2,1)S(1)}, bf16[2,2,768,1024]{3,2,1,0:T(8,128)(2,1)}, u32[]{:S(2)}, u32[]{:S(2)}) collective-permute-start(bf16[2,2,768,1024]{3,2,1,0:T(8,128)(2,1)S(1)} %dynamic-slice_bitcast_fusion), channel_id=1, source_target_pairs={{0,4},{4,0},{8,12},{12,8},{16,20},{20,16},{24,28},{28,24},{1,5},{5... | collective-permute-start | bytes 18874376 | tf_op jit(solution)/shard_map/ppermute | solution.py:149
  1017.3 80.4 %collective-permute-start.42 = (bf16[3,192,1536]{2,1,0:T(8,128)(2,1)S(1)}, bf16[3,192,1536]{2,1,0:T(8,128)(2,1)S(1)}, u32[]{:S(2)}, u32[]{:S(2)}) collective-permute-start(bf16[3,192,1536]{2,1,0:T(8,128)(2,1)S(1)} %pad_maximum_fusion.12), channel_id=1, source_target_pairs={{1,3},{0,1},{2,0},{3,2},{5,7},{4,5},{6,4},{7,6},{9,11},{8,9},{10,8... | collective-permute-start | bytes 5308424 | tf_op jit(solution)/shard_map/ppermute | solution.py:127
  1018.0 84.1 %collective-permute-start.41 = (bf16[3,192,1536]{2,1,0:T(8,128)(2,1)S(1)}, bf16[3,192,1536]{2,1,0:T(8,128)(2,1)S(1)}, u32[]{:S(2)}, u32[]{:S(2)}) collective-permute-start(bf16[3,192,1536]{2,1,0:T(8,128)(2,1)S(1)} %pad_maximum_fusion.8), channel_id=1, source_target_pairs={{0,3},{3,0},{4,7},{7,4},{8,11},{11,8},{12,15},{15,12},{16,19},{19,... | collective-permute-start | bytes 5308424 | tf_op jit(solution)/shard_map/ppermute | solution.py:128
  1023.4 108.9 %collective-permute-start.39 = (bf16[3,192,1536]{2,1,0:T(8,128)(2,1)S(1)}, bf16[3,192,1536]{2,1,0:T(8,128)(2,1)S(1)}, u32[]{:S(2)}, u32[]{:S(2)}) collective-permute-start(bf16[3,192,1536]{2,1,0:T(8,128)(2,1)S(1)} %get-tuple-element.139), channel_id=1, source_target_pairs={{0,1},{1,2},{2,3},{4,5},{5,6},{6,7},{8,9},{9,10},{10,11},{12,13},{... | collective-permute-start | bytes 5308424 | tf_op jit(solution)/shard_map/ppermute | solution.py:137
  1024.8 147.6 %collective-permute-start.40 = (bf16[3,192,1536]{2,1,0:T(8,128)(2,1)S(1)}, bf16[3,192,1536]{2,1,0:T(8,128)(2,1)S(1)}, u32[]{:S(2)}, u32[]{:S(2)}) collective-permute-start(bf16[3,192,1536]{2,1,0:T(8,128)(2,1)S(1)} %get-tuple-element.140), channel_id=1, source_target_pairs={{1,0},{2,1},{3,2},{5,4},{6,5},{7,6},{9,8},{10,9},{11,10},{13,12},{... | collective-permute-start | bytes 5308424 | tf_op jit(solution)/shard_map/ppermute | solution.py:138
  1097.7 89.2 %collective-permute-start.45 = (bf16[3,192,1536]{2,1,0:T(8,128)(2,1)}, bf16[3,192,1536]{2,1,0:T(8,128)(2,1)}, u32[]{:S(2)}, u32[]{:S(2)}) collective-permute-start(bf16[3,192,1536]{2,1,0:T(8,128)(2,1)} %pad_maximum_fusion.11), channel_id=1, source_target_pairs={{0,3},{3,0},{4,7},{7,4},{8,11},{11,8},{12,15},{15,12},{16,19},{19,... | collective-permute-start | bytes 5308424 | tf_op jit(solution)/shard_map/ppermute | solution.py:128
  1102.1 105.2 %collective-permute-start.43 = (bf16[3,192,1536]{2,1,0:T(8,128)(2,1)}, bf16[3,192,1536]{2,1,0:T(8,128)(2,1)}, u32[]{:S(2)}, u32[]{:S(2)}) collective-permute-start(bf16[3,192,1536]{2,1,0:T(8,128)(2,1)} %get-tuple-element.141), channel_id=1, source_target_pairs={{0,1},{1,2},{2,3},{4,5},{5,6},{6,7},{8,9},{9,10},{10,11},{12,13},{... | collective-permute-start | bytes 5308424 | tf_op jit(solution)/shard_map/ppermute | solution.py:137
  1132.2 78.1 %collective-permute-start.44 = (bf16[3,192,1536]{2,1,0:T(8,128)(2,1)}, bf16[3,192,1536]{2,1,0:T(8,128)(2,1)}, u32[]{:S(2)}, u32[]{:S(2)}) collective-permute-start(bf16[3,192,1536]{2,1,0:T(8,128)(2,1)} %get-tuple-element.142), channel_id=1, source_target_pairs={{1,0},{2,1},{3,2},{5,4},{6,5},{7,6},{9,8},{10,9},{11,10},{13,12},{... | collective-permute-start | bytes 5308424 | tf_op jit(solution)/shard_map/ppermute | solution.py:138
  1185.8 36.4 %collective-permute-start.30 = (bf16[2,384,1024]{2,1,0:T(8,128)(2,1)S(1)}, bf16[2,384,1024]{2,1,0:T(8,128)(2,1)S(1)}, u32[]{:S(2)}, u32[]{:S(2)}) collective-permute-start(bf16[2,384,1024]{2,1,0:T(8,128)(2,1)S(1)} %dynamic-slice_bitcast_fusion.4), channel_id=1, source_target_pairs={{0,8},{4,12},{8,0},{12,4},{16,24},{20,28},{24,16},{28,20},{1,9},{5... | collective-permute-start | bytes 4718600 | tf_op jit(solution)/shard_map/ppermute | solution.py:149
  1214.7 37.3 %collective-permute-start.32 = (bf16[2,384,1024]{2,1,0:T(8,128)(2,1)S(1)}, bf16[2,384,1024]{2,1,0:T(8,128)(2,1)S(1)}, u32[]{:S(2)}, u32[]{:S(2)}) collective-permute-start(bf16[2,384,1024]{2,1,0:T(8,128)(2,1)S(1)} %dynamic-slice_bitcast_fusion.3), channel_id=1, source_target_pairs={{0,16},{4,20},{8,24},{12,28},{16,0},{20,4},{24,8},{28,12},{1,17},{... | collective-permute-start | bytes 4718600 | tf_op jit(solution)/shard_map/ppermute | solution.py:149
  1222.9 45.0 %collective-permute-start.31 = (bf16[384,1024]{1,0:T(8,128)(2,1)S(1)}, bf16[384,1024]{1,0:T(8,128)(2,1)S(1)}, u32[]{:S(2)}, u32[]{:S(2)}) collective-permute-start(bf16[384,1024]{1,0:T(8,128)(2,1)S(1)} %dynamic-slice_bitcast_fusion.10), channel_id=1, source_target_pairs={{0,16},{4,20},{8,24},{12,28},{16,0},{20,4},{24,8},{28,12},{1,17},{... | collective-permute-start | bytes 2359304 | tf_op jit(solution)/shard_map/ppermute | solution.py:149
  1252.8 17.7 %collective-permute-start.33 = (bf16[384,1024]{1,0:T(8,128)(2,1)S(1)}, bf16[384,1024]{1,0:T(8,128)(2,1)S(1)}, u32[]{:S(2)}, u32[]{:S(2)}) collective-permute-start(bf16[384,1024]{1,0:T(8,128)(2,1)S(1)} %dynamic-slice_bitcast_fusion.9), channel_id=1, source_target_pairs={{0,8},{4,12},{8,0},{12,4},{16,24},{20,28},{24,16},{28,20},{1,9},{5... | collective-permute-start | bytes 2359304 | tf_op jit(solution)/shard_map/ppermute | solution.py:149
  1272.0 20.2 %collective-permute-start.34 = (bf16[192,1024]{1,0:T(8,128)(2,1)S(1)}, bf16[192,1024]{1,0:T(8,128)(2,1)S(1)}, u32[]{:S(2)}, u32[]{:S(2)}) collective-permute-start(bf16[192,1024]{1,0:T(8,128)(2,1)S(1)} %get-tuple-element.182), channel_id=1, source_target_pairs={{1,3},{0,1},{2,0},{3,2},{5,7},{4,5},{6,4},{7,6},{9,11},{8,9},{10,8... | collective-permute-start | bytes 1179656 | tf_op jit(solution)/shard_map/ppermute | solution.py:127
  1274.8 22.3 %collective-permute-start.37 = (bf16[192,1024]{1,0:T(8,128)(2,1)S(1)}, bf16[192,1024]{1,0:T(8,128)(2,1)S(1)}, u32[]{:S(2)}, u32[]{:S(2)}) collective-permute-start(bf16[192,1024]{1,0:T(8,128)(2,1)S(1)} %get-tuple-element.181), channel_id=1, source_target_pairs={{0,3},{3,0},{4,7},{7,4},{8,11},{11,8},{12,15},{15,12},{16,19},{19,... | collective-permute-start | bytes 1179656 | tf_op jit(solution)/shard_map/ppermute | solution.py:128
  1292.4 6.6 collective-permute-start.35
  1293.8 9.7 collective-permute-start.36
  (142 other events, 1898.0 us)
Sparse Core Ops, SparseCore 0:
  232.8 72.4 all-gather.5
  307.3 72.1 all-gather.7

commit v2 on v1

--- a/solution.py
+++ b/solution.py
@@ -78,6 +78,10 @@
     )
 
 
+def after(values, *earlier):
+    return lax.optimization_barrier((values, earlier))[0]
+
+
 def take(block, index):
     return lax.dynamic_index_in_dim(block, index, 0, keepdims=False)
 
@@ -96,15 +100,24 @@
     return jnp.arange(count, dtype=jnp.int32)
 
 
-def gather_slots(block):
+def gather_start(block):
+    if lax.axis_size("cols") != 4:
+        return (block, block, block)
+    above = lax.ppermute(block, "cols", [(1, 0), (2, 1), (3, 2)])
+    below = lax.ppermute(block, "cols", [(0, 1), (1, 2), (2, 3)])
+    far = lax.ppermute(block, "cols", [(0, 3), (3, 0)])
+    return (above, below, far)
+
+
+def gather_slots(block, first=None):
     count = lax.axis_size("cols")
     if count != 4:
         whole = lax.all_gather(block, "cols", axis=0)
         return [whole[i] for i in range(count)]
     place = lax.axis_index("cols")
-    above = lax.ppermute(block, "cols", [(1, 0), (2, 1), (3, 2)])
-    below = lax.ppermute(block, "cols", [(0, 1), (1, 2), (2, 3)])
-    far = lax.ppermute(block, "cols", [(0, 3), (3, 0)])
+    if first is None:
+        first = gather_start(block)
+    above, below, far = first
     payload = jnp.where(place == 1, above, jnp.where(place == 2, below, block))
     second = lax.ppermute(payload, "cols", [(3, 1), (1, 0), (0, 2), (2, 3)])
     end = (place == 0) | (place == 3)
@@ -116,10 +129,12 @@
     ]
 
 
-def reduce_slots(slots):
+def reduce_slots(slots, marks=None):
     count = lax.axis_size("cols")
     if count != 4:
         whole = jnp.stack(slots).astype(jnp.bfloat16)
+        if marks is not None:
+            marks.append((slots[0],) * 4)
         return lax.psum_scatter(whole, "cols", scatter_dimension=0).astype(jnp.float32)
     place = lax.axis_index("cols")
     own, second, third, fourth = slots
@@ -136,6 +151,8 @@
     )
     below = lax.ppermute(upward_load, "cols", [(0, 1), (1, 2), (2, 3)])
     above = lax.ppermute(downward_load, "cols", [(1, 0), (2, 1), (3, 2)])
+    if marks is not None:
+        marks.append((relay, far, below, above))
     return (
         own.astype(jnp.float32)
         + below.astype(jnp.float32)
@@ -238,7 +255,8 @@
     )
     packed = jnp.concatenate([query_weight, key_weight, value_weight, out_weight, extras], axis=1)
     packed_width = packed.shape[1]
-    packed_slots = jnp.stack(gather_slots(packed))
+    packed_first = gather_start(packed)
+    packed_slots = jnp.stack(gather_slots(packed, packed_first))
     shards = slot_shards()
     slot_of_shard = jnp.argsort(shards)
     packed_cols = jnp.take(packed_slots, slot_of_shard, axis=0)
@@ -263,16 +281,19 @@
     attention_full = packed_all[:, :, :gain_part, gain_at].reshape(-1)
     experts_full = packed_all[:, :, :gain_part, gain_at + 1].reshape(-1)
 
-    expert_weights = []
-    ahead = packed_slots
+    shard_blocks = [
+        jnp.stack([gate_weight[expert].T, upward_weight[expert].T, down_weight[expert]], axis=0)
+        for expert in range(local_experts)
+    ]
+    arrivals, expert_slots = ([], [])
+    ahead = packed_first
     for expert in range(local_experts):
-        block = jnp.stack(
-            [gate_weight[expert].T, upward_weight[expert].T, down_weight[expert]], axis=0
-        )
-        block, ahead = lax.optimization_barrier((block, ahead))
-        slots = gather_slots(block)
-        ahead = slots[1]
-        expert_weights.append(jnp.stack(slots, axis=1))
+        block = after(shard_blocks[expert], *ahead)
+        first = gather_start(block)
+        slots = gather_slots(block, first)
+        arrivals.append((first, slots[1]))
+        expert_slots.append(slots)
+        ahead = first
 
     routes_all = lax.all_gather(routes, "rows", axis=0)
     grad_all = lax.all_gather(cotangent, "rows", axis=0)
@@ -281,6 +302,7 @@
     attention_scale = attention_full.astype(jnp.float32)
     normed = rms_norm(token_float, attention_scale)
     normed_low = normed.astype(jnp.bfloat16)
+    normed_low = after(normed_low, *arrivals[0][0])
     query_lin = jnp.dot(normed_low, query_full, preferred_element_type=jnp.float32)
     key_lin = jnp.dot(normed_low, key_full, preferred_element_type=jnp.float32)
     value_low = jnp.dot(normed_low, value_full, preferred_element_type=jnp.float32).astype(
@@ -311,6 +333,7 @@
     value_tree = tree_rows[:, key_width:].reshape(2 * TOK_DEV, KV_HEADS, HEAD_DIM)
     key_index = jnp.arange(2 * TOK_DEV, dtype=jnp.int32)
     factor = HEAD_DIM ** (-0.5)
+    query_low = after(query_low, arrivals[0][1])
     query_group = query_low.reshape(TOK_DEV, KV_HEADS, group_size, HEAD_DIM)
     allowed = path_mask(local_index, key_index, parent_row)
 
@@ -331,6 +354,7 @@
     )
     log_total = highest + jnp.log(totals)
     heads_low = mixed_heads.reshape(TOK_DEV, query_width).astype(jnp.bfloat16)
+    heads_low = after(heads_low, arrivals[1][0][0], arrivals[1][0][1])
     residual = token_float + jnp.dot(heads_low, out_full, preferred_element_type=jnp.float32)
     experts_scale = experts_full.astype(jnp.float32)
     normed_two = rms_norm(residual, experts_scale)
@@ -377,10 +401,13 @@
     )
     share_rows = jnp.swapaxes(share_rows, 0, 1).reshape(local_experts, row_count * capacity, 1)
 
-    out_rows, back_rows, gate_dots, reduced = ([], [], [], [])
+    out_rows, back_rows, gate_dots, reduced, marks = ([], [], [], [], [])
     for expert in range(local_experts):
-        gate_full, upward_full, down_full = expert_weights[expert].reshape(3, -1, D)
+        weights_all = jnp.stack(expert_slots[expert], axis=1).reshape(3, -1, D)
+        gate_full, upward_full, down_full = (weights_all[0], weights_all[1], weights_all[2])
         row_block = token_rows[expert]
+        if marks:
+            row_block = after(row_block, marks[0][0])
         grad_block = grad_rows[expert].astype(jnp.float32)
         grad_expert = (share_rows[expert] * grad_block).astype(jnp.bfloat16)
 
@@ -412,7 +439,9 @@
             )
             for i in range(col_count)
         ]
-        reduced.append(reduce_slots(slots))
+        if marks:
+            slots = [after(slot, marks[0][0], marks[0][1]) for slot in slots]
+        reduced.append(reduce_slots(slots, marks))
         grad_route_in = (
             dot(grad_gate_act, gate_full, ((1,), (0,)))
             + dot(grad_upward, upward_full, ((1,), (0,)))
@@ -437,8 +466,7 @@
     grad_share_all = lax.all_gather(grad_share, "rows", axis=1, tiled=True)
     grad_shares = take(grad_share_all, row_place)
     back_sum = reduce_rows(back_part)
-    mixture = reduce_rows(out_part)
-    layer_output = (residual + mixture).astype(jnp.bfloat16)
+    back_sum = after(back_sum, *marks[0][1:])
     grad_out = cotangent.astype(jnp.float32)
 
     chosen_of = take(named, row_place)
@@ -468,6 +496,10 @@
     ).astype(jnp.bfloat16)
     grad_block = grad_heads_low.reshape(TOK_DEV, KV_HEADS, group_size, HEAD_DIM)
 
+    grad_block = after(grad_block, marks[1][0], marks[1][1])
+    out_part = after(out_part, back_sum)
+    mixture = reduce_rows(out_part)
+    layer_output = (residual + mixture).astype(jnp.bfloat16)
     attention = jnp.exp(block_scores() - log_total)
     attention_low = attention.astype(jnp.bfloat16)
     grad_attention = jnp.einsum(
@@ -489,6 +521,7 @@
         "kgqs,qkgd->skd", attention_low, grad_block, preferred_element_type=jnp.float32
     ).reshape(2 * TOK_DEV, key_width)
     tree_grads = jnp.concatenate([key_tree_grad, value_tree_grad], axis=1)
+    tree_grads = after(tree_grads, mixture)
     arrived = lax.ppermute(
         tree_grads[:TOK_DEV].astype(jnp.bfloat16), "cols", [(j, i) for i, j in pairs]
     ).astype(jnp.float32)
@@ -540,6 +573,7 @@
         ],
         axis=-1,
     )
+    packed_grad = after(packed_grad, marks[1][2], marks[1][3])
     row_sums = reduce_rows(packed_grad.reshape(row_count, col_count * depth, packed_width))
     row_sums = row_sums.astype(jnp.bfloat16).reshape(col_count, depth, packed_width)
     row_slots = jnp.take(row_sums, shards, axis=0)

time: 1320 us -> 1190 us (0.902)
  waiting for transfers between devices: 589 us -> 455 us
  other arithmetic: 130 us -> 155 us
    ppermute x20, waiting for transfers between devices: 190 us -> 134 us  [flip(): return lax.ppermute(block, 'rows', [(i, i ^ bit) for i in range(count)])]
    ppermute x3, waiting for transfers between devices: 49.8 us -> 1.92 us  [reduce_slots(): below = lax.ppermute(upward_load, 'cols', [(0, 1), (1, 2), (2, 3)])]
    ppermute x3, waiting for transfers between devices: 46 us -> 4.42 us  [reduce_slots(): above = lax.ppermute(downward_load, 'cols', [(1, 0), (2, 1), (3, 2)])]
    all_gather x1, waiting for transfers between devices: 0.01 us -> 38.2 us  [on_device(): grad_all = lax.all_gather(cotangent, 'rows', axis=0)]
    ppermute x9, waiting for transfers between devices: 158 us -> 125 us  [the longest x3 79.6 us: gather_start(): far = lax.ppermute(block, 'cols', [(0, 3), (3, 0)])]
    ppermute x3, waiting for transfers between devices: 59.6 us -> 40.2 us  [gather_slots(): second = lax.ppermute(payload, 'cols', [(3, 1), (1, 0), (0, 2), (2, 3)])]
    ppermute x3, waiting for transfers between devices: 84.8 us -> 101 us  [reduce_slots(): relay = lax.ppermute(second, 'cols', [(1, 3), (0, 1), (2, 0), (3, 2)])]
    concatenate x6 -> x1, local copies, waits for them, and re-layouts: 38.2 us -> 22.7 us  [on_device(): jnp.concatenate([by_shard(query_grad, query_part), by_shard(key_grad, key...]
  transfers between devices with their start and end apart: 48 -> 48, of which waited for: 31 -> 30; matrix products, arithmetic and copies ran while one was open for 30% -> 37% of each run, Pallas kernels for 0% -> 0%
where the time goes in v2:
time: 1190 us
  waiting for transfers between devices  455 us (38%)
  matrix products  245 us (21%)
  local copies, waits for them, and re-layouts  213 us (18%)
  other arithmetic  155 us (13%)
  starting transfers between devices  82.6 us (7%)
  blocking collectives  18.7 us (2%)
  between operations  16.7 us (1%)
    ppermute x20, waiting for transfers between devices, flip(): return lax.ppermute(block, 'rows', [(i, i ^ bit) for i in range(count)])  134 us
    ppermute x3, waiting for transfers between devices, reduce_slots(): relay = lax.ppermute(second, 'cols', [(1, 3), (0, 1), (2, 0), (3, 2)])  101 us
    dot_general x18, matrix products, dot(): lax.dot_general(one, two, (dims, ((), ())), preferred_element_type=jnp.fl...  84.7 us
    ppermute x3, waiting for transfers between devices, gather_start(): far = lax.ppermute(block, 'cols', [(0, 3), (3, 0)])  79.6 us
    ppermute x3, waiting for transfers between devices, gather_start(): below = lax.ppermute(block, 'cols', [(0, 1), (1, 2), (2, 3)])  43.8 us
    ppermute x3, waiting for transfers between devices, gather_slots(): second = lax.ppermute(payload, 'cols', [(3, 1), (1, 0), (0, 2), (2, 3)])  40.2 us
    all_gather x1, waiting for transfers between devices, on_device(): grad_all = lax.all_gather(cotangent, 'rows', axis=0)  38.2 us
    reshape x8, local copies, waits for them, and re-layouts, by_shard(): grad.astype(jnp.bfloat16).reshape(row_count, depth, col_count, width)  38 us
  transfers between devices with their start and end apart: 48, of which 30 were waited for; matrix products, arithmetic and copies ran while one was open for 37% of the time, Pallas kernels for 0%

profile of v2, /device:TPU:0, one launch (start us, length us, event | category | flops | bytes accessed | tf_op | source)
XLA Modules:
  0.0 1185.6 jit_solution(10052401073761035045)
XLA Ops:
  12.5 7.0 collective-permute-start.3
  23.5 5.9 collective-permute-done.3
  29.4 6.9 collective-permute-done.1
  38.9 9.3 collective-permute-done.2
  52.4 32.5 %collective-permute-done.4 = bf16[768,1024]{1,0:T(8,128)(2,1)S(1)} collective-permute-done((bf16[768,1024]{1,0:T(8,128)(2,1)S(1)}, bf16[768,1024]{1,0:T(8,128)(2,1)S(1)}, u32[]{:S(2)}, u32[]{:S(2)}) %collective-permute-start.4) | collective-permute-done | bytes 1572896 | tf_op jit(solution)/shard_map/ppermute | solution.py:166
  90.9 12.9 %collective-permute-done.6 = bf16[384,1024]{1,0:T(8,128)(2,1)} collective-permute-done((bf16[384,1024]{1,0:T(8,128)(2,1)}, bf16[384,1024]{1,0:T(8,128)(2,1)}, u32[]{:S(2)}, u32[]{:S(2)}) %collective-permute-start.6) | collective-permute-done | bytes 786464 | tf_op jit(solution)/shard_map/ppermute | solution.py:166
  128.6 32.7 %collective-permute-done.11 = bf16[3,192,1536]{2,1,0:T(8,128)(2,1)S(1)} collective-permute-done((bf16[3,192,1536]{2,1,0:T(8,128)(2,1)S(1)}, bf16[3,192,1536]{2,1,0:T(8,128)(2,1)S(1)}, u32[]{:S(2)}, u32[]{:S(2)}) %collective-permute-start.11) | collective-permute-done | bytes 1769504 | tf_op jit(solution)/shard_map/ppermute | solution.py:108
  161.3 36.9 %collective-permute-done.10 = bf16[3,192,1536]{2,1,0:T(8,128)(2,1)S(1)} collective-permute-done((bf16[3,192,1536]{2,1,0:T(8,128)(2,1)S(1)}, bf16[3,192,1536]{2,1,0:T(8,128)(2,1)S(1)}, u32[]{:S(2)}, u32[]{:S(2)}) %collective-permute-start.10) | collective-permute-done | bytes 1769504 | tf_op jit(solution)/shard_map/ppermute | solution.py:107
  239.3 7.1 slice_bitcast_fusion
  253.1 6.8 copy.201
  259.9 7.1 fusion.88
  267.1 6.0 copy.205
  275.7 9.8 collective-permute-done.13
  285.5 9.6 collective-permute-done.12
  296.5 10.7 fusion.12
  307.2 11.2 fusion.3
  318.4 12.1 %fusion.85 = bf16[2,128,6,512]{3,1,2,0:T(8,128)(2,1)S(1)} fusion(bf16[1024,2,128,1]{0,2,3,1:T(8,128)(2,1)S(1)} %bitcast.636, f32[2,6,512]{2,1,0:T(8,128)S(1)} %fusion.3, f32[2,6,512]{2,1,0:T(8,128)S(1)} %get-tuple-element.235, f32[2,1024,512,6]{2,1,3,0:T(8,128)} %get-tuple-element.236, pred[512,1024]{0,1:T(8,128)(4,1)S(1)} %fusion.84), kind=kOutput, calls=%fused_computation.186 | convolution fusion | flops 1642856448 | bytes 27836416 | tf_op jit(solution)/shard_map/kgqs,skd->qkgd/dot_general | solution.py:352
  339.9 41.0 %collective-permute-done.18 = bf16[3,192,1536]{2,1,0:T(8,128)(2,1)S(1)} collective-permute-done((bf16[3,192,1536]{2,1,0:T(8,128)(2,1)}, bf16[3,192,1536]{2,1,0:T(8,128)(2,1)S(1)}, u32[]{:S(2)}, u32[]{:S(2)}) %collective-permute-start.18) | collective-permute-done | bytes 1769504 | tf_op jit(solution)/shard_map/ppermute | solution.py:108
  386.0 9.2 all-gather
  403.6 21.0 %collective-permute-done.17 = bf16[3,192,1536]{2,1,0:T(8,128)(2,1)} collective-permute-done((bf16[3,192,1536]{2,1,0:T(8,128)(2,1)}, bf16[3,192,1536]{2,1,0:T(8,128)(2,1)}, u32[]{:S(2)}, u32[]{:S(2)}) %collective-permute-start.17) | collective-permute-done | bytes 1769504 | tf_op jit(solution)/shard_map/ppermute | solution.py:122
  433.5 8.0 fusion.200
  443.4 38.2 %all-gather.8.cloned.1.call-done = bf16[4096,1536]{1,0:T(8,128)(2,1)} async-done(((bf16[512,1536]{1,0:T(8,128)(2,1)}), bf16[4096,1536]{1,0:T(8,128)(2,1)}) %all-gather.8.cloned.1.call-update) | async-done | bytes 12582928 | tf_op jit(solution)/shard_map/all_gather | solution.py:299
  481.6 9.0 fusion.42
  490.7 12.1 %fusion.39 = bf16[2,8,160,1536]{3,2,0,1:T(8,128)(2,1)} fusion(bf16[8,512,1536,1]{2,1,3,0:T(8,128)(2,1)} %bitcast.586, s32[8,2,512]{2,1,0:T(2,128)S(1)} %copy.209, pred[8,2,512]{2,1,0:T(4,128)(4,1)S(1)} %copy.208), kind=kOutput, calls=%fused_computation.82 | convolution fusion | flops 4029153280 | bytes 20488192 | tf_op jit(solution)/shard_map/rlct,rtd->lrcd/dot_general | solution.py:396
  518.9 6.2 multiply_convert_fusion.4
  529.7 5.9 fusion.204
  535.8 6.0 convolution_convert_fusion.8
  566.2 31.2 %collective-permute-done.16 = bf16[3,192,1536]{2,1,0:T(8,128)(2,1)S(1)} collective-permute-done((bf16[3,192,1536]{2,1,0:T(8,128)(2,1)S(1)}, bf16[3,192,1536]{2,1,0:T(8,128)(2,1)S(1)}, u32[]{:S(2)}, u32[]{:S(2)}) %collective-permute-start.16) | collective-permute-done | bytes 1769504 | tf_op jit(solution)/shard_map/ppermute | solution.py:142
  614.8 10.7 bitcast_convert_fusion
  652.5 6.5 fusion.9
  668.2 9.1 fusion.14
  677.2 18.6 %collective-permute-done.22 = bf16[2,256,1536]{2,1,0:T(8,128)(2,1)S(1)} collective-permute-done((bf16[2,256,1536]{2,1,0:T(8,128)(2,1)S(1)}, bf16[2,256,1536]{2,1,0:T(8,128)(2,1)S(1)}, u32[]{:S(2)}, u32[]{:S(2)}) %collective-permute-start.22) | collective-permute-done | bytes 1572896 | tf_op jit(solution)/shard_map/ppermute | solution.py:166
  706.3 10.4 bitcast_convert_fusion.1
  732.8 9.5 all_gather.27
  764.7 6.5 fusion.8
  787.6 54.2 %collective-permute-done.32 = bf16[3,192,1536]{2,1,0:T(8,128)(2,1)} collective-permute-done((bf16[3,192,1536]{2,1,0:T(8,128)(2,1)}, bf16[3,192,1536]{2,1,0:T(8,128)(2,1)}, u32[]{:S(2)}, u32[]{:S(2)}) %collective-permute-start.32) | collective-permute-done | bytes 1769504 | tf_op jit(solution)/shard_map/ppermute | solution.py:142
  870.6 11.7 collective-permute-done.31
  895.5 7.2 convolution_convert_fusion
  902.7 12.6 %fusion.5 = f32[2,128,1024,1]{2,1,3,0:T(8,128)} fusion(bf16[512,2,6,128]{0,3,2,1:T(8,128)(2,1)S(1)} %bitcast.594, f32[2,6,512]{2,1,0:T(8,128)S(1)} %log_add_fusion, f32[2,1024,512,6]{2,1,3,0:T(8,128)} %get-tuple-element.236, pred[512,1024]{0,1:T(8,128)(4,1)S(1)} %copy-done.4), kind=kOutput, calls=%fused_computation.15 | convolution fusion | flops 1635778560 | bytes 28336128 | tf_op jit(solution)/shard_map/kgqs,qkgd->skd/dot_general | solution.py:520
  915.3 17.9 %fusion = (f32[2,6,512]{2,1,0:T(8,128)S(1)}, f32[2,1024,512,6]{2,1,3,0:T(8,128)}) fusion(f32[2,6,512]{2,1,0:T(8,128)S(1)} %log_add_fusion, f32[2,1024,512,6]{2,1,3,0:T(8,128)} %get-tuple-element.236, pred[512,1024]{0,1:T(8,128)(4,1)S(1)} %copy-done.4, bf16[1024,2,128,1]{0,2,3,1:T(8,128)(2,1)S(1)} %bitcast.637, bf16[512,2,6,128]{0,3,2,1:T(8,128)(2,1)} %bitcast.593), kind=kOutput, calls=%fused_computation.4 | convolution fusion | flops 1642063872 | bytes 53002240 | tf_op jit(solution)/shard_map/qkgd,skd->kgqs/dot_general | solution.py:505
  933.1 17.0 %fusion.2 = bf16[2,6,512,1024]{2,3,1,0:T(8,128)(2,1)S(1)} fusion(f32[2,1024,512,6]{2,1,3,0:T(8,128)} %get-tuple-element.241, f32[2,6,512]{2,1,0:T(8,128)S(1)} %get-tuple-element.240, f32[2,6,512]{2,1,0:T(8,128)S(1)} %log_add_fusion, f32[2,1024,512,6]{2,1,3,0:T(8,128)} %get-tuple-element.236, pred[512,1024]{0,1:T(8,128)(4,1)S(1)} %copy-done.4), kind=kLoop, calls=%fused_computation.6 | loop fusion | flops 37748736 | bytes 63488000 | tf_op jit(solution)/shard_map/convert_element_type | solution.py:511
  959.3 9.1 reshape.709
  983.9 9.1 reshape.706
  1029.1 22.7 %concatenate.56 = bf16[8,4,192,1024]{3,2,1,0:T(8,128)(2,1)} concatenate(bf16[8,4,192,384]{3,2,1,0:T(8,128)(2,1)} %bitcast.583, bf16[8,4,192,64]{3,2,1,0:T(8,128)(2,1)} %copy.234, bf16[8,4,192,64]{3,2,1,0:T(8,128)(2,1)} %copy.235, bf16[8,4,192,384]{3,2,1,0:T(8,128)(2,1)} %bitcast.582, bf16[8,4,192,4]{3,2,1,0:T(8,128)(2,1)S(1)} %bitcast.598, bf16[8,4,192,1]{3,2,1,0:T(8,128)(2,1)} %copy.236, ...), dimensions={3} | concatenate | bytes 25165824 | tf_op jit(solution)/shard_map/concatenate | solution.py:563
  1065.9 10.6 fusion.7
  1088.6 28.7 %collective-permute-done.40 = bf16[2,384,1024]{2,1,0:T(8,128)(2,1)S(1)} collective-permute-done((bf16[2,384,1024]{2,1,0:T(8,128)(2,1)S(1)}, bf16[2,384,1024]{2,1,0:T(8,128)(2,1)S(1)}, u32[]{:S(2)}, u32[]{:S(2)}) %collective-permute-start.40) | collective-permute-done | bytes 1572896 | tf_op jit(solution)/shard_map/ppermute | solution.py:166
  1124.1 12.8 %collective-permute-done.41 = bf16[384,1024]{1,0:T(8,128)(2,1)S(1)} collective-permute-done((bf16[384,1024]{1,0:T(8,128)(2,1)S(1)}, bf16[384,1024]{1,0:T(8,128)(2,1)S(1)}, u32[]{:S(2)}, u32[]{:S(2)}) %collective-permute-start.41) | collective-permute-done | bytes 786464 | tf_op jit(solution)/shard_map/ppermute | solution.py:166
  1148.1 15.1 %collective-permute-done.42 = bf16[192,1024]{1,0:T(8,128)(2,1)S(1)} collective-permute-done((bf16[192,1024]{1,0:T(8,128)(2,1)S(1)}, bf16[192,1024]{1,0:T(8,128)(2,1)S(1)}, u32[]{:S(2)}, u32[]{:S(2)}) %collective-permute-start.42) | collective-permute-done | bytes 393248 | tf_op jit(solution)/shard_map/ppermute | solution.py:142
  (628 shorter events, 456.7 us)
Async XLA Ops:
  7.2 426.3 %all-gather.6.cloned.1.call-start = ((), (), s32[]{:S(2)}) async-start(), calls=%async_computation | async-start | bytes 14155776 | tf_op jit(solution)/shard_map/all_gather | solution.py:362
  12.5 16.9 %collective-permute-start.3 = (bf16[192,1024]{1,0:T(8,128)(2,1)S(1)}, bf16[192,1024]{1,0:T(8,128)(2,1)S(1)}, u32[]{:S(2)}, u32[]{:S(2)}) collective-permute-start(bf16[192,1024]{1,0:T(8,128)(2,1)S(1)} %concatenate.45), channel_id=1, source_target_pairs={{0,3},{3,0},{4,7},{7,4},{8,11},{11,8},{12,15},{15,12},{16,19},{19,... | collective-permute-start | bytes 1179656 | tf_op jit(solution)/shard_map/ppermute | solution.py:108
  19.5 16.9 %collective-permute-start.1 = (bf16[192,1024]{1,0:T(8,128)(2,1)S(1)}, bf16[192,1024]{1,0:T(8,128)(2,1)S(1)}, u32[]{:S(2)}, u32[]{:S(2)}) collective-permute-start(bf16[192,1024]{1,0:T(8,128)(2,1)S(1)} %concatenate.45), channel_id=1, source_target_pairs={{0,1},{1,2},{2,3},{4,5},{5,6},{6,7},{8,9},{9,10},{10,11},{12,13},{... | collective-permute-start | bytes 1179656 | tf_op jit(solution)/shard_map/ppermute | solution.py:107
  20.8 16.3 %collective-permute-start = (bf16[192,1024]{1,0:T(8,128)(2,1)S(1)}, bf16[192,1024]{1,0:T(8,128)(2,1)S(1)}, u32[]{:S(2)}, u32[]{:S(2)}) collective-permute-start(bf16[192,1024]{1,0:T(8,128)(2,1)S(1)} %concatenate.45), channel_id=1, source_target_pairs={{1,0},{2,1},{3,2},{5,4},{6,5},{7,6},{9,8},{10,9},{11,10},{13,12},{... | collective-permute-start | bytes 1179656 | tf_op jit(solution)/shard_map/ppermute | solution.py:106
  37.1 11.1 collective-permute-start.2
  49.3 35.5 %collective-permute-start.4 = (bf16[768,1024]{1,0:T(8,128)(2,1)S(1)}, bf16[768,1024]{1,0:T(8,128)(2,1)S(1)}, u32[]{:S(2)}, u32[]{:S(2)}) collective-permute-start(bf16[768,1024]{1,0:T(8,128)(2,1)S(1)} %bitcast.595), channel_id=1, source_target_pairs={{0,8},{4,12},{8,0},{12,4},{16,24},{20,28},{24,16},{28,20},{1,9},{5... | collective-permute-start | bytes 4718600 | tf_op jit(solution)/shard_map/ppermute | solution.py:166
  50.9 36.4 %collective-permute-start.5 = (bf16[768,1024]{1,0:T(8,128)(2,1)S(1)}, bf16[768,1024]{1,0:T(8,128)(2,1)S(1)}, u32[]{:S(2)}, u32[]{:S(2)}) collective-permute-start(bf16[768,1024]{1,0:T(8,128)(2,1)S(1)} %bitcast.596), channel_id=1, source_target_pairs={{0,16},{4,20},{8,24},{12,28},{16,0},{20,4},{24,8},{28,12},{1,17},{... | collective-permute-start | bytes 4718600 | tf_op jit(solution)/shard_map/ppermute | solution.py:166
  85.8 18.0 %collective-permute-start.6 = (bf16[384,1024]{1,0:T(8,128)(2,1)}, bf16[384,1024]{1,0:T(8,128)(2,1)}, u32[]{:S(2)}, u32[]{:S(2)}) collective-permute-start(bf16[384,1024]{1,0:T(8,128)(2,1)} %slice.474), channel_id=1, source_target_pairs={{0,16},{4,20},{8,24},{12,28},{16,0},{20,4},{24,8},{28,12},{1,17},{... | collective-permute-start | bytes 2359304 | tf_op jit(solution)/shard_map/ppermute | solution.py:166
  89.4 17.7 %collective-permute-start.7 = (bf16[384,1024]{1,0:T(8,128)(2,1)}, bf16[384,1024]{1,0:T(8,128)(2,1)}, u32[]{:S(2)}, u32[]{:S(2)}) collective-permute-start(bf16[384,1024]{1,0:T(8,128)(2,1)} %slice.475), channel_id=1, source_target_pairs={{0,8},{4,12},{8,0},{12,4},{16,24},{20,28},{24,16},{28,20},{1,9},{5... | collective-permute-start | bytes 2359304 | tf_op jit(solution)/shard_map/ppermute | solution.py:166
  113.7 96.1 %collective-permute-start.8 = (bf16[4,768,1024]{2,1,0:T(8,128)(2,1)}, bf16[4,768,1024]{2,1,0:T(8,128)(2,1)}, u32[]{:S(2)}, u32[]{:S(2)}) collective-permute-start(bf16[4,768,1024]{2,1,0:T(8,128)(2,1)} %pad_maximum_fusion.3), channel_id=1, source_target_pairs={{0,4},{4,0},{8,12},{12,8},{16,20},{20,16},{24,28},{28,24},{1,5},{5... | collective-permute-start | bytes 18874376 | tf_op jit(solution)/shard_map/ppermute | solution.py:166
  116.2 45.1 %collective-permute-start.11 = (bf16[3,192,1536]{2,1,0:T(8,128)(2,1)S(1)}, bf16[3,192,1536]{2,1,0:T(8,128)(2,1)S(1)}, u32[]{:S(2)}, u32[]{:S(2)}) collective-permute-start(bf16[3,192,1536]{2,1,0:T(8,128)(2,1)S(1)} %pad_maximum_fusion.8), channel_id=1, source_target_pairs={{0,3},{3,0},{4,7},{7,4},{8,11},{11,8},{12,15},{15,12},{16,19},{19,... | collective-permute-start | bytes 5308424 | tf_op jit(solution)/shard_map/ppermute | solution.py:108
  121.7 76.5 %collective-permute-start.10 = (bf16[3,192,1536]{2,1,0:T(8,128)(2,1)S(1)}, bf16[3,192,1536]{2,1,0:T(8,128)(2,1)S(1)}, u32[]{:S(2)}, u32[]{:S(2)}) collective-permute-start(bf16[3,192,1536]{2,1,0:T(8,128)(2,1)S(1)} %pad_maximum_fusion.8), channel_id=1, source_target_pairs={{0,1},{1,2},{2,3},{4,5},{5,6},{6,7},{8,9},{9,10},{10,11},{12,13},{... | collective-permute-start | bytes 5308424 | tf_op jit(solution)/shard_map/ppermute | solution.py:107
  123.1 75.8 %collective-permute-start.9 = (bf16[3,192,1536]{2,1,0:T(8,128)(2,1)S(1)}, bf16[3,192,1536]{2,1,0:T(8,128)(2,1)S(1)}, u32[]{:S(2)}, u32[]{:S(2)}) collective-permute-start(bf16[3,192,1536]{2,1,0:T(8,128)(2,1)S(1)} %pad_maximum_fusion.8), channel_id=1, source_target_pairs={{1,0},{2,1},{3,2},{5,4},{6,5},{7,6},{9,8},{10,9},{11,10},{13,12},{... | collective-permute-start | bytes 5308424 | tf_op jit(solution)/shard_map/ppermute | solution.py:106
  198.9 131.7 %collective-permute-start.15 = (bf16[3,192,1536]{2,1,0:T(8,128)(2,1)}, bf16[3,192,1536]{2,1,0:T(8,128)(2,1)}, u32[]{:S(2)}, u32[]{:S(2)}) collective-permute-start(bf16[3,192,1536]{2,1,0:T(8,128)(2,1)} %pad_maximum_fusion.9), channel_id=1, source_target_pairs={{0,1},{1,2},{2,3},{4,5},{5,6},{6,7},{8,9},{9,10},{10,11},{12,13},{... | collective-permute-start | bytes 5308424 | tf_op jit(solution)/shard_map/ppermute | solution.py:107
  203.8 126.8 %collective-permute-start.14 = (bf16[3,192,1536]{2,1,0:T(8,128)(2,1)}, bf16[3,192,1536]{2,1,0:T(8,128)(2,1)}, u32[]{:S(2)}, u32[]{:S(2)}) collective-permute-start(bf16[3,192,1536]{2,1,0:T(8,128)(2,1)} %pad_maximum_fusion.9), channel_id=1, source_target_pairs={{1,0},{2,1},{3,2},{5,4},{6,5},{7,6},{9,8},{10,9},{11,10},{13,12},{... | collective-permute-start | bytes 5308424 | tf_op jit(solution)/shard_map/ppermute | solution.py:106
  207.9 77.6 %collective-permute-start.13 = (bf16[3,192,1536]{2,1,0:T(8,128)(2,1)}, bf16[3,192,1536]{2,1,0:T(8,128)(2,1)}, u32[]{:S(2)}, u32[]{:S(2)}) collective-permute-start(bf16[3,192,1536]{2,1,0:T(8,128)(2,1)} %get-tuple-element.172), channel_id=1, source_target_pairs={{3,1},{1,0},{0,2},{2,3},{7,5},{5,4},{4,6},{6,7},{11,9},{9,8},{8,10... | collective-permute-start | bytes 5308424 | tf_op jit(solution)/shard_map/ppermute | solution.py:122
  238.0 57.1 %collective-permute-start.12 = (bf16[512,512]{0,1:T(8,128)(2,1)}, bf16[512,512]{0,1:T(8,128)(2,1)}, u32[]{:S(2)}, u32[]{:S(2)}) collective-permute-start(bf16[512,512]{0,1:T(8,128)(2,1)} %get-tuple-element.228), channel_id=1, source_target_pairs={{1,0},{3,2},{5,4},{7,6},{9,8},{11,10},{13,12},{15,14},{17,16},{19,... | collective-permute-start | bytes 1572872 | tf_op jit(solution)/shard_map/ppermute | solution.py:324
  336.9 144.7 %all-gather.8.cloned.1.call-start = ((), (), s32[]{:S(2)}) async-start(), calls=%async_computation.1 | async-start | bytes 14155776 | tf_op jit(solution)/shard_map/all_gather | solution.py:299
  337.7 43.2 %collective-permute-start.18 = (bf16[3,192,1536]{2,1,0:T(8,128)(2,1)}, bf16[3,192,1536]{2,1,0:T(8,128)(2,1)S(1)}, u32[]{:S(2)}, u32[]{:S(2)}) collective-permute-start(bf16[3,192,1536]{2,1,0:T(8,128)(2,1)} %pad_maximum_fusion.9), channel_id=1, source_target_pairs={{0,3},{3,0},{4,7},{7,4},{8,11},{11,8},{12,15},{15,12},{16,19},{19,... | collective-permute-start | bytes 5308424 | tf_op jit(solution)/shard_map/ppermute | solution.py:108
  386.0 38.6 %collective-permute-start.17 = (bf16[3,192,1536]{2,1,0:T(8,128)(2,1)}, bf16[3,192,1536]{2,1,0:T(8,128)(2,1)}, u32[]{:S(2)}, u32[]{:S(2)}) collective-permute-start(bf16[3,192,1536]{2,1,0:T(8,128)(2,1)} %get-tuple-element.169), channel_id=1, source_target_pairs={{3,1},{1,0},{0,2},{2,3},{7,5},{5,4},{4,6},{6,7},{11,9},{9,8},{8,10... | collective-permute-start | bytes 5308424 | tf_op jit(solution)/shard_map/ppermute | solution.py:122
  555.7 41.7 %collective-permute-start.16 = (bf16[3,192,1536]{2,1,0:T(8,128)(2,1)S(1)}, bf16[3,192,1536]{2,1,0:T(8,128)(2,1)S(1)}, u32[]{:S(2)}, u32[]{:S(2)}) collective-permute-start(bf16[3,192,1536]{2,1,0:T(8,128)(2,1)S(1)} %pad_maximum_fusion.10), channel_id=1, source_target_pairs={{1,3},{0,1},{2,0},{3,2},{5,7},{4,5},{6,4},{7,6},{9,11},{8,9},{10,8... | collective-permute-start | bytes 5308424 | tf_op jit(solution)/shard_map/ppermute | solution.py:142
  632.0 20.5 %collective-permute-start.19 = (bf16[2,2,512,1536]{3,2,1,0:T(8,128)(2,1)}, bf16[2,2,512,1536]{3,2,1,0:T(8,128)(2,1)}, u32[]{:S(2)}, u32[]{:S(2)}) collective-permute-start(bf16[2,2,512,1536]{3,2,1,0:T(8,128)(2,1)} %dynamic-slice_bitcast_fusion.2), channel_id=1, source_target_pairs={{0,4},{4,0},{8,12},{12,8},{16,20},{20,16},{24,28},{28,24},{1,5},{5... | collective-permute-start | bytes 18874376 | tf_op jit(solution)/shard_map/ppermute | solution.py:166
  636.6 89.3 %collective-permute-start.24 = (bf16[3,192,1536]{2,1,0:T(8,128)(2,1)}, bf16[3,192,1536]{2,1,0:T(8,128)(2,1)}, u32[]{:S(2)}, u32[]{:S(2)}) collective-permute-start(bf16[3,192,1536]{2,1,0:T(8,128)(2,1)} %pad_maximum_fusion.11), channel_id=1, source_target_pairs={{0,3},{3,0},{4,7},{7,4},{8,11},{11,8},{12,15},{15,12},{16,19},{19,... | collective-permute-start | bytes 5308424 | tf_op jit(solution)/shard_map/ppermute | solution.py:143
  645.4 80.5 %collective-permute-start.26 = (bf16[3,192,1536]{2,1,0:T(8,128)(2,1)}, bf16[3,192,1536]{2,1,0:T(8,128)(2,1)}, u32[]{:S(2)}, u32[]{:S(2)}) collective-permute-start(bf16[3,192,1536]{2,1,0:T(8,128)(2,1)} %get-tuple-element.167), channel_id=1, source_target_pairs={{1,0},{2,1},{3,2},{5,4},{6,5},{7,6},{9,8},{10,9},{11,10},{13,12},{... | collective-permute-start | bytes 5308424 | tf_op jit(solution)/shard_map/ppermute | solution.py:153
  646.7 79.2 %collective-permute-start.25 = (bf16[3,192,1536]{2,1,0:T(8,128)(2,1)}, bf16[3,192,1536]{2,1,0:T(8,128)(2,1)}, u32[]{:S(2)}, u32[]{:S(2)}) collective-permute-start(bf16[3,192,1536]{2,1,0:T(8,128)(2,1)} %get-tuple-element.168), channel_id=1, source_target_pairs={{0,1},{1,2},{2,3},{4,5},{5,6},{6,7},{8,9},{9,10},{10,11},{12,13},{... | collective-permute-start | bytes 5308424 | tf_op jit(solution)/shard_map/ppermute | solution.py:152
  659.8 36.0 %collective-permute-start.22 = (bf16[2,256,1536]{2,1,0:T(8,128)(2,1)S(1)}, bf16[2,256,1536]{2,1,0:T(8,128)(2,1)S(1)}, u32[]{:S(2)}, u32[]{:S(2)}) collective-permute-start(bf16[2,256,1536]{2,1,0:T(8,128)(2,1)S(1)} %dynamic-slice_bitcast_fusion.7), channel_id=1, source_target_pairs={{0,16},{4,20},{8,24},{12,28},{16,0},{20,4},{24,8},{28,12},{1,17},{... | collective-permute-start | bytes 4718600 | tf_op jit(solution)/shard_map/ppermute | solution.py:166
  666.6 37.4 %collective-permute-start.20 = (bf16[2,256,1536]{2,1,0:T(8,128)(2,1)S(1)}, bf16[2,256,1536]{2,1,0:T(8,128)(2,1)S(1)}, u32[]{:S(2)}, u32[]{:S(2)}) collective-permute-start(bf16[2,256,1536]{2,1,0:T(8,128)(2,1)S(1)} %dynamic-slice_bitcast_fusion.8), channel_id=1, source_target_pairs={{0,8},{4,12},{8,0},{12,4},{16,24},{20,28},{24,16},{28,20},{1,9},{5... | collective-permute-start | bytes 4718600 | tf_op jit(solution)/shard_map/ppermute | solution.py:166
  697.3 22.2 %collective-permute-start.23 = (bf16[256,1536]{1,0:T(8,128)(2,1)}, bf16[256,1536]{1,0:T(8,128)(2,1)}, u32[]{:S(2)}, u32[]{:S(2)}) collective-permute-start(bf16[256,1536]{1,0:T(8,128)(2,1)} %dynamic-slice_bitcast_fusion.13), channel_id=1, source_target_pairs={{0,8},{4,12},{8,0},{12,4},{16,24},{20,28},{24,16},{28,20},{1,9},{5... | collective-permute-start | bytes 2359304 | tf_op jit(solution)/shard_map/ppermute | solution.py:166
  705.4 17.3 %collective-permute-start.21 = (bf16[256,1536]{1,0:T(8,128)(2,1)}, bf16[256,1536]{1,0:T(8,128)(2,1)}, u32[]{:S(2)}, u32[]{:S(2)}) collective-permute-start(bf16[256,1536]{1,0:T(8,128)(2,1)} %dynamic-slice_bitcast_fusion.14), channel_id=1, source_target_pairs={{0,16},{4,20},{8,24},{12,28},{16,0},{20,4},{24,8},{28,12},{1,17},{... | collective-permute-start | bytes 2359304 | tf_op jit(solution)/shard_map/ppermute | solution.py:166
  729.1 35.6 %collective-permute-start.27 = (bf16[2,2,512,1536]{3,2,1,0:T(8,128)(2,1)}, bf16[2,2,512,1536]{3,2,1,0:T(8,128)(2,1)}, u32[]{:S(2)}, u32[]{:S(2)}) collective-permute-start(bf16[2,2,512,1536]{3,2,1,0:T(8,128)(2,1)} %dynamic-slice_bitcast_fusion.1), channel_id=1, source_target_pairs={{0,4},{4,0},{8,12},{12,8},{16,20},{20,16},{24,28},{28,24},{1,5},{5... | collective-permute-start | bytes 18874376 | tf_op jit(solution)/shard_map/ppermute | solution.py:166
  761.9 80.0 %collective-permute-start.32 = (bf16[3,192,1536]{2,1,0:T(8,128)(2,1)}, bf16[3,192,1536]{2,1,0:T(8,128)(2,1)}, u32[]{:S(2)}, u32[]{:S(2)}) collective-permute-start(bf16[3,192,1536]{2,1,0:T(8,128)(2,1)} %pad_maximum_fusion.13), channel_id=1, source_target_pairs={{1,3},{0,1},{2,0},{3,2},{5,7},{4,5},{6,4},{7,6},{9,11},{8,9},{10,8... | collective-permute-start | bytes 5308424 | tf_op jit(solution)/shard_map/ppermute | solution.py:142
  776.3 83.7 %collective-permute-start.30 = (bf16[2,256,1536]{2,1,0:T(8,128)(2,1)}, bf16[2,256,1536]{2,1,0:T(8,128)(2,1)}, u32[]{:S(2)}, u32[]{:S(2)}) collective-permute-start(bf16[2,256,1536]{2,1,0:T(8,128)(2,1)} %dynamic-slice_bitcast_fusion.5), channel_id=1, source_target_pairs={{0,16},{4,20},{8,24},{12,28},{16,0},{20,4},{24,8},{28,12},{1,17},{... | collective-permute-start | bytes 4718600 | tf_op jit(solution)/shard_map/ppermute | solution.py:166
  782.2 120.5 %collective-permute-start.33 = (bf16[3,192,1536]{2,1,0:T(8,128)(2,1)}, bf16[3,192,1536]{2,1,0:T(8,128)(2,1)}, u32[]{:S(2)}, u32[]{:S(2)}) collective-permute-start(bf16[3,192,1536]{2,1,0:T(8,128)(2,1)} %pad_maximum_fusion.14), channel_id=1, source_target_pairs={{0,3},{3,0},{4,7},{7,4},{8,11},{11,8},{12,15},{15,12},{16,19},{19,... | collective-permute-start | bytes 5308424 | tf_op jit(solution)/shard_map/ppermute | solution.py:143
  786.1 78.0 %collective-permute-start.28 = (bf16[2,256,1536]{2,1,0:T(8,128)(2,1)}, bf16[2,256,1536]{2,1,0:T(8,128)(2,1)}, u32[]{:S(2)}, u32[]{:S(2)}) collective-permute-start(bf16[2,256,1536]{2,1,0:T(8,128)(2,1)} %dynamic-slice_bitcast_fusion.6), channel_id=1, source_target_pairs={{0,8},{4,12},{8,0},{12,4},{16,24},{20,28},{24,16},{28,20},{1,9},{5... | collective-permute-start | bytes 4718600 | tf_op jit(solution)/shard_map/ppermute | solution.py:166
  847.3 204.5 %collective-permute-start.36 = (bf16[3,192,1536]{2,1,0:T(8,128)(2,1)}, bf16[3,192,1536]{2,1,0:T(8,128)(2,1)}, u32[]{:S(2)}, u32[]{:S(2)}) collective-permute-start(bf16[3,192,1536]{2,1,0:T(8,128)(2,1)} %get-tuple-element.165), channel_id=1, source_target_pairs={{1,0},{2,1},{3,2},{5,4},{6,5},{7,6},{9,8},{10,9},{11,10},{13,12},{... | collective-permute-start | bytes 5308424 | tf_op jit(solution)/shard_map/ppermute | solution.py:153
  848.8 203.0 %collective-permute-start.35 = (bf16[3,192,1536]{2,1,0:T(8,128)(2,1)}, bf16[3,192,1536]{2,1,0:T(8,128)(2,1)}, u32[]{:S(2)}, u32[]{:S(2)}) collective-permute-start(bf16[3,192,1536]{2,1,0:T(8,128)(2,1)} %get-tuple-element.166), channel_id=1, source_target_pairs={{0,1},{1,2},{2,3},{4,5},{5,6},{6,7},{8,9},{9,10},{10,11},{12,13},{... | collective-permute-start | bytes 5308424 | tf_op jit(solution)/shard_map/ppermute | solution.py:152
  863.5 18.7 %collective-permute-start.31 = (bf16[256,1536]{1,0:T(8,128)(2,1)}, bf16[256,1536]{1,0:T(8,128)(2,1)}, u32[]{:S(2)}, u32[]{:S(2)}) collective-permute-start(bf16[256,1536]{1,0:T(8,128)(2,1)} %dynamic-slice_bitcast_fusion.11), channel_id=1, source_target_pairs={{0,8},{4,12},{8,0},{12,4},{16,24},{20,28},{24,16},{28,20},{1,9},{5... | collective-permute-start | bytes 2359304 | tf_op jit(solution)/shard_map/ppermute | solution.py:166
  867.4 18.5 %collective-permute-start.29 = (bf16[256,1536]{1,0:T(8,128)(2,1)}, bf16[256,1536]{1,0:T(8,128)(2,1)}, u32[]{:S(2)}, u32[]{:S(2)}) collective-permute-start(bf16[256,1536]{1,0:T(8,128)(2,1)} %dynamic-slice_bitcast_fusion.12), channel_id=1, source_target_pairs={{0,16},{4,20},{8,24},{12,28},{16,0},{20,4},{24,8},{28,12},{1,17},{... | collective-permute-start | bytes 2359304 | tf_op jit(solution)/shard_map/ppermute | solution.py:166
  975.1 28.0 %collective-permute-start.34 = (bf16[512,512]{0,1:T(8,128)(2,1)}, bf16[512,512]{0,1:T(8,128)(2,1)}, u32[]{:S(2)}, u32[]{:S(2)}) collective-permute-start(bf16[512,512]{0,1:T(8,128)(2,1)} %slice.639), channel_id=1, source_target_pairs={{0,1},{2,3},{4,5},{6,7},{8,9},{10,11},{12,13},{14,15},{16,17},{18,... | collective-permute-start | bytes 1572872 | tf_op jit(solution)/shard_map/ppermute | solution.py:525
  1055.5 10.4 collective-permute-start.37
  1080.7 36.6 %collective-permute-start.40 = (bf16[2,384,1024]{2,1,0:T(8,128)(2,1)S(1)}, bf16[2,384,1024]{2,1,0:T(8,128)(2,1)S(1)}, u32[]{:S(2)}, u32[]{:S(2)}) collective-permute-start(bf16[2,384,1024]{2,1,0:T(8,128)(2,1)S(1)} %dynamic-slice_bitcast_fusion.3), channel_id=1, source_target_pairs={{0,16},{4,20},{8,24},{12,28},{16,0},{20,4},{24,8},{28,12},{1,17},{... | collective-permute-start | bytes 4718600 | tf_op jit(solution)/shard_map/ppermute | solution.py:166
  1082.3 37.2 %collective-permute-start.38 = (bf16[2,384,1024]{2,1,0:T(8,128)(2,1)S(1)}, bf16[2,384,1024]{2,1,0:T(8,128)(2,1)S(1)}, u32[]{:S(2)}, u32[]{:S(2)}) collective-permute-start(bf16[2,384,1024]{2,1,0:T(8,128)(2,1)S(1)} %dynamic-slice_bitcast_fusion.4), channel_id=1, source_target_pairs={{0,8},{4,12},{8,0},{12,4},{16,24},{20,28},{24,16},{28,20},{1,9},{5... | collective-permute-start | bytes 4718600 | tf_op jit(solution)/shard_map/ppermute | solution.py:166
  1118.0 18.9 %collective-permute-start.41 = (bf16[384,1024]{1,0:T(8,128)(2,1)S(1)}, bf16[384,1024]{1,0:T(8,128)(2,1)S(1)}, u32[]{:S(2)}, u32[]{:S(2)}) collective-permute-start(bf16[384,1024]{1,0:T(8,128)(2,1)S(1)} %dynamic-slice_bitcast_fusion.9), channel_id=1, source_target_pairs={{0,8},{4,12},{8,0},{12,4},{16,24},{20,28},{24,16},{28,20},{1,9},{5... | collective-permute-start | bytes 2359304 | tf_op jit(solution)/shard_map/ppermute | solution.py:166
  1120.3 18.6 %collective-permute-start.39 = (bf16[384,1024]{1,0:T(8,128)(2,1)S(1)}, bf16[384,1024]{1,0:T(8,128)(2,1)S(1)}, u32[]{:S(2)}, u32[]{:S(2)}) collective-permute-start(bf16[384,1024]{1,0:T(8,128)(2,1)S(1)} %dynamic-slice_bitcast_fusion.10), channel_id=1, source_target_pairs={{0,16},{4,20},{8,24},{12,28},{16,0},{20,4},{24,8},{28,12},{1,17},{... | collective-permute-start | bytes 2359304 | tf_op jit(solution)/shard_map/ppermute | solution.py:166
  1143.0 20.1 %collective-permute-start.42 = (bf16[192,1024]{1,0:T(8,128)(2,1)S(1)}, bf16[192,1024]{1,0:T(8,128)(2,1)S(1)}, u32[]{:S(2)}, u32[]{:S(2)}) collective-permute-start(bf16[192,1024]{1,0:T(8,128)(2,1)S(1)} %get-tuple-element.208), channel_id=1, source_target_pairs={{1,3},{0,1},{2,0},{3,2},{5,7},{4,5},{6,4},{7,6},{9,11},{8,9},{10,8... | collective-permute-start | bytes 1179656 | tf_op jit(solution)/shard_map/ppermute | solution.py:142
  1144.9 23.2 %collective-permute-start.45 = (bf16[192,1024]{1,0:T(8,128)(2,1)S(1)}, bf16[192,1024]{1,0:T(8,128)(2,1)S(1)}, u32[]{:S(2)}, u32[]{:S(2)}) collective-permute-start(bf16[192,1024]{1,0:T(8,128)(2,1)S(1)} %get-tuple-element.207), channel_id=1, source_target_pairs={{0,3},{3,0},{4,7},{7,4},{8,11},{11,8},{12,15},{15,12},{16,19},{19,... | collective-permute-start | bytes 1179656 | tf_op jit(solution)/shard_map/ppermute | solution.py:143
  1163.4 6.6 collective-permute-start.43
  1164.7 9.7 collective-permute-start.44
  (155 other events, 3268.1 us)
Sparse Core Ops, SparseCore 0:
  337.0 70.5 all-gather.5
  409.5 72.1 all-gather.7

commit v3 on v1

v3 whole, which is shorter than its diff:
```python
import functools

import jax
import jax.numpy as jnp
from jax import lax
from jax.experimental import pallas as pl
from jax.experimental.pallas import tpu as pltpu
from jax.sharding import PartitionSpec as P

D = 1536
HEADS = 12
KV_HEADS = 2
HEAD_DIM = 128
TOP = 4
TOK_DEV = 512
BRANCHES = 4
LEAVES = 8
TRUNK = 256
BRANCH = 64

EPSILON = 1e-06
ROPE_BASE = 10000.0
MASKED = -1e30
LOW = jnp.bfloat16
WIDE = jnp.float32
KEY_WIDTH = KV_HEADS * HEAD_DIM
GROUP = HEADS // KV_HEADS
QUARTERS = 4
VMEM_LIMIT = 56 * 1024 * 1024

ANY = pl.BlockSpec(memory_space=pl.ANY)
SMEM = pl.BlockSpec(memory_space=pltpu.SMEM)


def nn(one, two):
    return lax.dot_general(one, two, (((1,), (0,)), ((), ())), preferred_element_type=WIDE)


def nt(one, two):
    return lax.dot_general(one, two, (((1,), (1,)), ((), ())), preferred_element_type=WIDE)


def tn(one, two):
    return lax.dot_general(one, two, (((0,), (0,)), ((), ())), preferred_element_type=WIDE)


def whole(shape):
    return pl.BlockSpec(shape, lambda *_: (0,) * len(shape))


def params():
    return pltpu.CompilerParams(vmem_limit_bytes=VMEM_LIMIT)


def turn(values, cosine, sine):
    return values * cosine + pltpu.roll(values, HEAD_DIM // 2, 1) * sine


def turn_back(values, cosine, sine):
    return values * cosine - pltpu.roll(values, HEAD_DIM // 2, 1) * sine


PIECES = tuple(
    (flip_bits + core, first, count)
    for core in (0, 1)
    for flip_bits, first, count in ((0, 0, 4), (2, 0, 4), (4, 0, 4), (6, 0, 2), (6, 2, 2))
)


def weight_copies(info, refs, target, sem, start, width):
    if len(refs) == 1:
        return [pltpu.make_async_copy(refs[0], target, sem)]
    depth = refs[0].shape[1]
    copies = []
    for ref, (flip_bits, first, count) in zip(refs, PIECES):
        row = pl.multiple_of((info[0] ^ flip_bits) * depth, depth)
        for slot in range(count):
            col = pl.multiple_of(info[2 + first + slot] * width, 128)
            copies.append(
                pltpu.make_async_copy(
                    ref.at[slot, :, pl.ds(start, width)],
                    target.at[pl.ds(row, depth), pl.ds(col, width)],
                    sem,
                )
            )
    return copies


def run_all(copies):
    for copy in copies:
        copy.start()


def wait_all(copies):
    for copy in copies:
        copy.wait()


def key_value_kernel(info, tokens, gain, cosine, sine, *rest):
    count = len(rest) - 4
    refs, (normed, out, weight, sem) = rest[:count], rest[count:]
    copies = weight_copies(info, refs, weight, sem, D // QUARTERS, 128)
    run_all(copies)
    values = tokens[...].astype(WIDE)
    factor = lax.rsqrt(jnp.mean(values * values, axis=-1, keepdims=True) + EPSILON)
    low = (values * factor * gain[...]).astype(LOW)
    normed[...] = low
    wait_all(copies)
    both = nn(low, weight[...])
    half = HEAD_DIM // 2
    first = lax.broadcasted_iota(jnp.int32, (TOK_DEV, HEAD_DIM), 1) < half
    for g in range(KV_HEADS):
        one = both[:, 256 * g : 256 * g + 128]
        two = both[:, 256 * g + 128 : 256 * g + 256]
        key = jnp.where(first, one, pltpu.roll(two, half, 1))
        value = jnp.where(first, pltpu.roll(one, half, 1), two)
        out[:, 128 * g : 128 * g + 128] = turn(key, cosine[...], sine[...]).astype(LOW)
        out[:, KEY_WIDTH + 128 * g : KEY_WIDTH + 128 * g + 128] = value.astype(LOW)


def key_value(info, tokens, gain, cosine, sine, refs):
    return pl.pallas_call(
        key_value_kernel,
        out_shape=(
            jax.ShapeDtypeStruct((TOK_DEV, D), LOW),
            jax.ShapeDtypeStruct((TOK_DEV, 2 * KEY_WIDTH), LOW),
        ),
        in_specs=[SMEM] + [pl.BlockSpec(memory_space=pltpu.VMEM)] * 4 + [ANY] * len(refs),
        out_specs=(pl.BlockSpec(memory_space=pltpu.VMEM),) * 2,
        scratch_shapes=[pltpu.VMEM((D, 2 * KEY_WIDTH), LOW), pltpu.SemaphoreType.DMA],
        compiler_params=params(),
        name="norm_key_value",
    )(info, tokens, gain, cosine, sine, *refs)


def query_kernel(info, normed, cosine, sine, *rest):
    count = len(rest) - 3
    refs, (out, weight, sem) = rest[:count], rest[count:]

    @pl.when(pl.program_id(0) == 0)
    def _():
        copies = weight_copies(info, refs, weight, sem, 0, D // QUARTERS)
        run_all(copies)
        wait_all(copies)

    at = pl.multiple_of(pl.program_id(0) * 256, 256)
    lin = nn(normed[...], weight[:, pl.ds(at, 256)])
    for h in range(2):
        out[:, 128 * h : 128 * h + 128] = turn(
            lin[:, 128 * h : 128 * h + 128], cosine[...], sine[...]
        ).astype(LOW)


def query(info, normed, cosine, sine, refs):
    return pl.pallas_call(
        query_kernel,
        grid=(D // 256,),
        out_shape=jax.ShapeDtypeStruct((TOK_DEV, D), LOW),
        in_specs=[SMEM, whole((TOK_DEV, D)), whole((TOK_DEV, 128)), whole((TOK_DEV, 128))]
        + [ANY] * len(refs),
        out_specs=pl.BlockSpec((TOK_DEV, 256), lambda i: (0, i)),
        scratch_shapes=[pltpu.VMEM((D, D), LOW), pltpu.SemaphoreType.DMA],
        compiler_params=params(),
        name="query_projection",
    )(info, normed, cosine, sine, *refs)


KEYS = TRUNK + 2 * BRANCH
CHUNKS = TOK_DEV // BRANCH


def chunk_keys(info, source, own, column, chunk):
    at = pl.multiple_of(info[6 + chunk], BRANCH)
    rows = pl.multiple_of(chunk * BRANCH, BRANCH)
    columns = slice(column, column + HEAD_DIM)
    return jnp.concatenate(
        [
            source[0:TRUNK, columns],
            source[pl.ds(at, BRANCH), columns],
            own[pl.ds(rows, BRANCH), columns],
        ],
        axis=0,
    )


def chunk_allowed(info, chunk, query_axis, shape):
    query_row = lax.broadcasted_iota(jnp.int32, shape, query_axis) & (BRANCH - 1)
    key = lax.broadcasted_iota(jnp.int32, shape, 1 - query_axis)
    leaves = info[1] == 0
    trunk = jnp.logical_and(jnp.logical_not(leaves), chunk < TRUNK // BRANCH)
    limit = jnp.where(trunk, chunk * BRANCH + query_row, TRUNK - 1)
    branch_limit = jnp.where(leaves, TRUNK + BRANCH - 1, 0)
    own_limit = jnp.where(trunk, 0, query_row + TRUNK + BRANCH)
    top = jnp.where(key < TRUNK, limit, jnp.where(key < TRUNK + BRANCH, branch_limit, own_limit))
    return key <= top


def group_rows(ref, g):
    first = g * GROUP
    return jnp.concatenate(
        [ref[:, 128 * h : 128 * h + 128] for h in range(first, first + GROUP)], axis=0
    )


def keep_source(info, partner, own, source):
    @pl.when(pl.program_id(0) == 0)
    def _():
        @pl.when(info[1] == 0)
        def _():
            source[...] = partner[...]

        @pl.when(info[1] != 0)
        def _():
            source[...] = own[...]


def attention_kernel(info, queries, own, partner, out, source):
    keep_source(info, partner, own, source)
    chunk = pl.program_id(0)
    rows = GROUP * BRANCH
    allowed = chunk_allowed(info, chunk, 0, (rows, KEYS))
    for g in range(KV_HEADS):
        keys = chunk_keys(info, source, own, 128 * g, chunk)
        values = chunk_keys(info, source, own, KEY_WIDTH + 128 * g, chunk)
        scores = nt(group_rows(queries, g), keys) * HEAD_DIM**-0.5
        scores = jnp.where(allowed, scores, MASKED)
        weights = jnp.exp(scores - jnp.max(scores, axis=1, keepdims=True))
        total = jnp.sum(weights, axis=1, keepdims=True)
        mixed = nn((weights * (1.0 / total)).astype(LOW), values).astype(LOW)
        for h in range(GROUP):
            at = (g * GROUP + h) * 128
            out[:, at : at + 128] = mixed[h * BRANCH : (h + 1) * BRANCH]


def attention(info, queries, own, partner):
    return pl.pallas_call(
        attention_kernel,
        grid=(CHUNKS,),
        out_shape=jax.ShapeDtypeStruct((TOK_DEV, D), LOW),
        in_specs=[
            SMEM,
            pl.BlockSpec((BRANCH, D), lambda i: (i, 0)),
            whole((TOK_DEV, 2 * KEY_WIDTH)),
            whole((TOK_DEV, 2 * KEY_WIDTH)),
        ],
        out_specs=pl.BlockSpec((BRANCH, D), lambda i: (i, 0)),
        scratch_shapes=[pltpu.VMEM((TOK_DEV, 2 * KEY_WIDTH), LOW)],
        compiler_params=params(),
        name="tree_attention",
    )(info, queries, own, partner)


def attention_back_kernel(
    info, queries, own, partner, grads, cosine, sine, grad_query, own_grad, source_grad, source
):
    keep_source(info, partner, own, source)
    chunk = pl.program_id(0)

    @pl.when(chunk == 0)
    def _():
        source_grad[...] = jnp.zeros_like(source_grad)

    rows = GROUP * BRANCH
    scale = HEAD_DIM**-0.5
    allowed = chunk_allowed(info, chunk, 1, (KEYS, rows))
    at = pl.multiple_of(info[6 + chunk], BRANCH)
    for g in range(KV_HEADS):
        keys = chunk_keys(info, source, own, 128 * g, chunk)
        values = chunk_keys(info, source, own, KEY_WIDTH + 128 * g, chunk)
        query_rows = group_rows(queries, g)
        grad_rows = group_rows(grads, g)
        scores = jnp.where(allowed, nt(keys, query_rows) * scale, MASKED)
        weights = jnp.exp(scores - jnp.max(scores, axis=0, keepdims=True))
        probs = weights * (1.0 / jnp.sum(weights, axis=0, keepdims=True))
        grad_probs = nt(values, grad_rows)
        mean = jnp.sum(probs * grad_probs, axis=0, keepdims=True)
        grad_scores = (probs * (grad_probs - mean)).astype(LOW)
        grad_values = nn(probs.astype(LOW), grad_rows)
        grad_keys = nn(grad_scores, query_rows) * scale
        grad_queries = tn(grad_scores, keys) * scale
        for h in range(GROUP):
            to = (g * GROUP + h) * 128
            grad_query[:, to : to + 128] = turn_back(
                grad_queries[h * BRANCH : (h + 1) * BRANCH], cosine[...], sine[...]
            ).astype(LOW)
        for column, grad in ((128 * g, grad_keys), (KEY_WIDTH + 128 * g, grad_values)):
            columns = slice(column, column + 128)
            source_grad[0:TRUNK, columns] += grad[0:TRUNK]
            source_grad[pl.ds(at, BRANCH), columns] += grad[TRUNK : TRUNK + BRANCH]
            own_grad[:, columns] = grad[TRUNK + BRANCH :]


def attention_back(info, queries, own, partner, grads, cosine, sine):
    chunked = pl.BlockSpec((BRANCH, D), lambda i: (i, 0))
    pair = (TOK_DEV, 2 * KEY_WIDTH)
    return pl.pallas_call(
        attention_back_kernel,
        grid=(CHUNKS,),
        out_shape=(
            jax.ShapeDtypeStruct((TOK_DEV, D), LOW),
            jax.ShapeDtypeStruct(pair, WIDE),
            jax.ShapeDtypeStruct(pair, WIDE),
        ),
        in_specs=[
            SMEM,
            chunked,
            whole(pair),
            whole(pair),
            chunked,
            pl.BlockSpec((BRANCH, 128), lambda i: (i, 0)),
            pl.BlockSpec((BRANCH, 128), lambda i: (i, 0)),
        ],
        out_specs=(
            chunked,
            pl.BlockSpec((BRANCH, 2 * KEY_WIDTH), lambda i: (i, 0)),
            whole(pair),
        ),
        scratch_shapes=[pltpu.VMEM(pair, LOW)],
        compiler_params=params(),
        name="tree_attention_back",
    )(info, queries, own, partner, grads, cosine, sine)


def out_kernel(info, heads, tokens, gain, *rest):
    count = len(rest) - 4
    refs, (residual, normed, weight, sem) = rest[:count], rest[count:]

    @pl.when(pl.program_id(0) == 0)
    def _():
        copies = weight_copies(info, refs, weight, sem, D // QUARTERS + 128, D // QUARTERS)
        run_all(copies)
        wait_all(copies)

    at = pl.ds(pl.multiple_of(pl.program_id(0) * 256, 256), 256)
    residual[:, at] = tokens[:, at].astype(WIDE) + nn(heads[...], weight[:, at])

    @pl.when(pl.program_id(0) == pl.num_programs(0) - 1)
    def _():
        values = residual[...]
        factor = lax.rsqrt(jnp.mean(values * values, axis=-1, keepdims=True) + EPSILON)
        normed[...] = (values * factor * gain[...]).astype(LOW)


def out_projection(info, heads, tokens, gain, refs):
    full = (TOK_DEV, D)
    return pl.pallas_call(
        out_kernel,
        grid=(D // 256,),
        out_shape=(jax.ShapeDtypeStruct(full, WIDE), jax.ShapeDtypeStruct(full, LOW)),
        in_specs=[SMEM, whole(full), whole(full), whole((1, D))] + [ANY] * len(refs),
        out_specs=(whole(full), whole(full)),
        scratch_shapes=[pltpu.VMEM((D, D), LOW), pltpu.SemaphoreType.DMA],
        compiler_params=params(),
        name="out_projection",
    )(info, heads, tokens, gain, *refs)


def dispatch_kernel(capacity, local, info, rows, grads, routes, router, *rest):
    token_outs, grad_outs = rest[:local], rest[local : 2 * local]
    share_outs, logits_out, earlier = rest[2 * local : 3 * local], rest[3 * local], rest[-1]
    total = router.shape[0]

    @pl.when(pl.program_id(0) == 0)
    def _():
        one = lax.broadcasted_iota(jnp.int32, (TOK_DEV, TOK_DEV), 0)
        two = lax.broadcasted_iota(jnp.int32, (TOK_DEV, TOK_DEV), 1)
        earlier[...] = jnp.where(one < two, 1.0, 0.0).astype(LOW)

    block = rows[0]
    logits = nt(router[...], block)
    logits_out[0] = logits
    ids = lax.broadcasted_iota(jnp.int32, (total, TOK_DEV), 0)
    hit = ids == routes[0, 0:1]
    for k in range(1, TOP):
        hit = jnp.logical_or(hit, ids == routes[0, k : k + 1])
    weights = jnp.exp(logits - jnp.max(logits, axis=0, keepdims=True))
    probs = weights / jnp.sum(weights, axis=0, keepdims=True)
    share = probs / jnp.sum(jnp.where(hit, probs, 0.0), axis=0, keepdims=True)
    hits = jnp.where(hit, 1.0, 0.0)
    rank = nn(hits.astype(LOW), earlier[...])
    place = jnp.where(hit, rank, -1.0)
    spots = lax.broadcasted_iota(jnp.int32, (capacity, TOK_DEV), 0).astype(WIDE)
    for e in range(local):
        mine = ids == info[0] * local + e
        place_row = jnp.sum(jnp.where(mine, place, 0.0), axis=0, keepdims=True)
        share_row = jnp.sum(jnp.where(mine, share, 0.0), axis=0, keepdims=True)
        chosen = spots == place_row
        onehot = jnp.where(chosen, 1.0, 0.0).astype(LOW)
        token_outs[e][0] = nn(onehot, block).astype(LOW)
        grad_outs[e][0] = nn(onehot, grads[0]).astype(LOW)
        share_outs[e][0] = jnp.sum(jnp.where(chosen, share_row, 0.0), axis=1, keepdims=True)


def dispatch(info, rows, grads, routes, router, capacity, local):
    count = rows.shape[0]
    total = router.shape[0]
    block = pl.BlockSpec((1, TOK_DEV, D), lambda i: (i, 0, 0))
    picked = pl.BlockSpec((1, capacity, D), lambda i: (i, 0, 0))
    shares = pl.BlockSpec((1, capacity, 1), lambda i: (i, 0, 0))
    return pl.pallas_call(
        functools.partial(dispatch_kernel, capacity, local),
        grid=(count,),
        out_shape=[jax.ShapeDtypeStruct((count, capacity, D), LOW)] * (2 * local)
        + [jax.ShapeDtypeStruct((count, capacity, 1), WIDE)] * local
        + [jax.ShapeDtypeStruct((count, total, TOK_DEV), WIDE)],
        in_specs=[
            SMEM,
            block,
            block,
            pl.BlockSpec((1, TOP, TOK_DEV), lambda i: (i, 0, 0)),
            whole((total, D)),
        ],
        out_specs=[picked] * (2 * local)
        + [shares] * local
        + [pl.BlockSpec((1, total, TOK_DEV), lambda i: (i, 0, 0))],
        scratch_shapes=[pltpu.VMEM((TOK_DEV, TOK_DEV), LOW)],
        compiler_params=params(),
        name="dispatch",
    )(info, rows, grads, routes, router)


def expert_kernel(slots, info, rows, grads, shares, *rest):
    count = len(rest) - 7
    refs = rest[:count]
    out_rows, back_rows, grad_rows, acts, dots, weight, sem = rest[count:]
    part = weight.shape[1] // slots

    @pl.when(pl.program_id(0) == 0)
    def _():
        def copies(ref, slot):
            return [
                pltpu.make_async_copy(
                    ref.at[pl.ds(which * part, part)],
                    weight.at[which, pl.ds(slot * part, part)],
                    sem,
                )
                for which in range(3)
            ]

        if count == slots:
            for slot in range(slots):
                run_all(copies(refs[slot], slot))
        else:
            block, second, above, below, far = refs
            low_end = info[2] == 0
            end = jnp.logical_or(low_end, info[2] == 3)
            run_all(copies(block, 0))
            run_all(copies(second, 1))

            @pl.when(low_end)
            def _():
                run_all(copies(above, 2))

            @pl.when(jnp.logical_not(low_end))
            def _():
                run_all(copies(below, 2))

            @pl.when(end)
            def _():
                run_all(copies(far, 3))

            @pl.when(jnp.logical_not(end))
            def _():
                run_all(copies(above, 3))

        for slot in range(slots):
            wait_all(copies(refs[0], slot))

    row_block = rows[...]
    share = shares[...]
    grad_float = grads[...].astype(WIDE)
    grad_low = (share * grad_float).astype(LOW)
    grad_rows[...] = grad_low
    gate_act = nt(row_block, weight[0])
    upward = nt(row_block, weight[1])
    sigmoid = 1.0 / (1.0 + jnp.exp(-gate_act))
    silu = gate_act * sigmoid
    hidden = (silu * upward).astype(LOW)
    expert_out = nn(hidden, weight[2]).astype(LOW).astype(WIDE)
    out_rows[...] = (share * expert_out).astype(LOW)
    dots[...] = jnp.sum(grad_float * expert_out, axis=1, keepdims=True)
    grad_hidden = nt(grad_low, weight[2])
    grad_gate = (grad_hidden * upward * sigmoid * (1.0 + gate_act * (1.0 - sigmoid))).astype(LOW)
    grad_up = (grad_hidden * silu).astype(LOW)
    back_rows[...] = (nn(grad_gate, weight[0]) + nn(grad_up, weight[1])).astype(LOW)
    for which, act in enumerate((grad_gate, grad_up, hidden)):
        turned = act.T
        for slot in range(slots):
            acts[slot, which * part : (which + 1) * part] = turned[
                slot * part : (slot + 1) * part
            ]


EXPERT_ROWS = 256


def expert(info, rows, grads, shares, refs, slots):
    height = rows.shape[0]
    part = refs[0].shape[0] // 3
    wide_block = pl.BlockSpec((EXPERT_ROWS, D), lambda i: (i, 0))
    thin_block = pl.BlockSpec((EXPERT_ROWS, 1), lambda i: (i, 0))
    return pl.pallas_call(
        functools.partial(expert_kernel, slots),
        grid=(height // EXPERT_ROWS,),
        out_shape=[jax.ShapeDtypeStruct((height, D), LOW)] * 3
        + [
            jax.ShapeDtypeStruct((slots, 3 * part, height), LOW),
            jax.ShapeDtypeStruct((height, 1), WIDE),
        ],
        in_specs=[SMEM, wide_block, wide_block, thin_block] + [ANY] * len(refs),
        out_specs=[wide_block] * 3
        + [pl.BlockSpec((slots, 3 * part, EXPERT_ROWS), lambda i: (0, 0, i)), thin_block],
        scratch_shapes=[pltpu.VMEM((3, slots * part, D), LOW), pltpu.SemaphoreType.DMA],
        compiler_params=params(),
        name="expert",
    )(info, rows, grads, shares, *refs)


def expert_grads_kernel(slots, rows, grads, *rest):
    acts, outs = rest[: len(slots)], rest[len(slots) :]
    part = acts[0].shape[1] // 3
    at = pl.ds(pl.multiple_of(pl.program_id(0) * 256, 256), 256)
    for act, out in zip(acts, outs):
        out[: 2 * part, :] = nn(act[0, : 2 * part], rows[:, at]).astype(LOW)
        out[2 * part :, :] = nn(act[0, 2 * part :], grads[:, at]).astype(LOW)


def expert_grads(acts, rows, grads, slots):
    _, part, height = acts.shape
    return pl.pallas_call(
        functools.partial(expert_grads_kernel, slots),
        grid=(D // 256,),
        out_shape=[jax.ShapeDtypeStruct((part, D), LOW) for _ in slots],
        in_specs=[whole((height, D))] * 2
        + [pl.BlockSpec((1, part, height), lambda i, s=slot: (s, 0, 0)) for slot in slots],
        out_specs=[pl.BlockSpec((part, 256), lambda i: (0, i)) for _ in slots],
        compiler_params=params(),
        name="expert_gradients",
    )(rows, grads, *[acts] * len(slots))


def combine_kernel(capacity, local, total, order, info, routes, *rest):
    rows, out, earlier = rest[:local], rest[local], rest[local + 1]

    @pl.when(pl.program_id(0) == 0)
    def _():
        one = lax.broadcasted_iota(jnp.int32, (TOK_DEV, TOK_DEV), 0)
        two = lax.broadcasted_iota(jnp.int32, (TOK_DEV, TOK_DEV), 1)
        earlier[...] = jnp.where(two < one, 1.0, 0.0).astype(LOW)

    ids = lax.broadcasted_iota(jnp.int32, (TOK_DEV, total), 1)
    hit = ids == routes[0, :, 0:1]
    for k in range(1, TOP):
        hit = jnp.logical_or(hit, ids == routes[0, :, k : k + 1])
    hits = jnp.where(hit, 1.0, 0.0)
    place = jnp.where(hit, nn(earlier[...], hits.astype(LOW)), -1.0)
    spots = lax.broadcasted_iota(jnp.int32, (TOK_DEV, capacity), 1).astype(WIDE)
    summed = None
    for e in range(local):
        mine = ids == info[0] * local + e
        place_col = jnp.sum(jnp.where(mine, place, 0.0), axis=1, keepdims=True)
        onehot = jnp.where(spots == place_col, 1.0, 0.0).astype(LOW)
        term = nn(onehot, rows[e][0])
        summed = term if summed is None else summed + term
    out[0] = summed.astype(LOW)


def combine(order, info, routes, rows, total):
    count, capacity = rows[0].shape[0], rows[0].shape[1]
    named = pl.BlockSpec((1, capacity, D), lambda i, order, info: (order[i], 0, 0))
    return pl.pallas_call(
        functools.partial(combine_kernel, capacity, len(rows), total),
        grid_spec=pltpu.PrefetchScalarGridSpec(
            num_scalar_prefetch=2,
            grid=(order.shape[0],),
            in_specs=[pl.BlockSpec((1, TOK_DEV, TOP), lambda i, order, info: (order[i], 0, 0))]
            + [named] * len(rows),
            out_specs=pl.BlockSpec((1, TOK_DEV, D), lambda i, order, info: (i, 0, 0)),
            scratch_shapes=[pltpu.VMEM((TOK_DEV, TOK_DEV), LOW)],
        ),
        out_shape=jax.ShapeDtypeStruct((order.shape[0], TOK_DEV, D), LOW),
        compiler_params=params(),
        name="combine",
    )(order, info, routes, *rows)


def split(values):
    high = values.astype(LOW)
    return high, (values - high.astype(WIDE)).astype(LOW)


def norm_back(values, gain, grad):
    factor = lax.rsqrt(jnp.mean(values * values, axis=-1, keepdims=True) + EPSILON)
    scaled = gain * grad
    mean = jnp.mean(values * scaled, axis=-1, keepdims=True)
    grad_values = factor * scaled - values * (factor * factor * factor * mean)
    grad_gain = jnp.sum(grad * values * factor, axis=0, keepdims=True)
    return grad_values, grad_gain


def branch_back_kernel(
    info, residual, normed, sums, cotangent, grad_logits, router, gain, *rest
):
    count = len(rest) - 7
    refs = rest[:count]
    grad_residual, grad_branch, grad_heads, grad_gain, grad_router, weight, sem = rest[count:]
    copies = weight_copies(info, refs, weight, sem, D // QUARTERS + 128, D // QUARTERS)

    @pl.when(pl.program_id(0) == 0)
    def _():
        run_all(copies)
        high, low = split(grad_logits[...])
        grad_router[...] = nn(high, normed[...]) + nn(low, normed[...])
        grad_normed = sums[...] + tn(high, router[...]) + tn(low, router[...])
        grad_values, gain_grad = norm_back(residual[...], gain[...], grad_normed)
        grad_gain[...] = gain_grad
        total = cotangent[...].astype(WIDE) + grad_values
        grad_residual[...] = total
        grad_branch[...] = total.astype(LOW)
        wait_all(copies)

    at = pl.ds(pl.multiple_of(pl.program_id(0) * 256, 256), 256)
    grad_heads[...] = nt(grad_branch[...], weight[at, :]).astype(LOW)


def branch_back(info, residual, normed, sums, cotangent, grad_logits, router, gain, refs):
    full = (TOK_DEV, D)
    total = router.shape[0]
    return pl.pallas_call(
        branch_back_kernel,
        grid=(D // 256,),
        out_shape=(
            jax.ShapeDtypeStruct(full, WIDE),
            jax.ShapeDtypeStruct(full, LOW),
            jax.ShapeDtypeStruct(full, LOW),
            jax.ShapeDtypeStruct((1, D), WIDE),
            jax.ShapeDtypeStruct((total, D), WIDE),
        ),
        in_specs=[SMEM]
        + [whole(full)] * 4
        + [whole((total, TOK_DEV)), whole((total, D)), whole((1, D))]
        + [ANY] * len(refs),
        out_specs=(
            whole(full),
            whole(full),
            pl.BlockSpec((TOK_DEV, 256), lambda i: (0, i)),
            whole((1, D)),
            whole((total, D)),
        ),
        scratch_shapes=[pltpu.VMEM((D, D), LOW), pltpu.SemaphoreType.DMA],
        compiler_params=params(),
        name="experts_norm_back",
    )(info, residual, normed, sums, cotangent, grad_logits, router, gain, *refs)


def join_grads_kernel(info, own_grad, source_grad, arrived, cosine, sine, out):
    half = HEAD_DIM // 2
    first = lax.broadcasted_iota(jnp.int32, (TOK_DEV, HEAD_DIM), 1) < half
    leaves = info[1] == 0

    def total(column):
        columns = slice(column, column + 128)
        extra = source_grad[:, columns] + arrived[:, columns].astype(WIDE)
        return own_grad[:, columns] + jnp.where(leaves, 0.0, extra)

    for g in range(KV_HEADS):
        key = turn_back(total(128 * g), cosine[...], sine[...])
        value = total(KEY_WIDTH + 128 * g)
        out[:, 256 * g : 256 * g + 128] = jnp.where(
            first, key, pltpu.roll(value, half, 1)
        ).astype(LOW)
        out[:, 256 * g + 128 : 256 * g + 256] = jnp.where(
            first, pltpu.roll(key, half, 1), value
        ).astype(LOW)


def join_grads(info, own_grad, source_grad, arrived, cosine, sine):
    vmem = pl.BlockSpec(memory_space=pltpu.VMEM)
    return pl.pallas_call(
        join_grads_kernel,
        out_shape=jax.ShapeDtypeStruct((TOK_DEV, 2 * KEY_WIDTH), LOW),
        in_specs=[SMEM] + [vmem] * 5,
        out_specs=vmem,
        compiler_params=params(),
        name="join_key_value_gradients",
    )(info, own_grad, source_grad, arrived, cosine, sine)


def token_back_kernel(info, grad_query, grad_pair, tokens, grad_residual, gain, *rest):
    count = (len(rest) - 6) // 2
    query_refs, pair_refs = rest[:count], rest[count : 2 * count]
    out, grad_gain, query_weight, pair_weight, grad_normed, sem = rest[2 * count :]

    @pl.when(pl.program_id(0) == 0)
    def _():
        copies = weight_copies(info, query_refs, query_weight, sem, 0, D // QUARTERS)
        copies += weight_copies(info, pair_refs, pair_weight, sem, D // QUARTERS, 128)
        run_all(copies)
        wait_all(copies)

    at = pl.ds(pl.multiple_of(pl.program_id(0) * 256, 256), 256)
    grad_normed[:, at] = nt(grad_query[...], query_weight[at, :]) + nt(
        grad_pair[...], pair_weight[at, :]
    )

    @pl.when(pl.program_id(0) == pl.num_programs(0) - 1)
    def _():
        grad_values, gain_grad = norm_back(
            tokens[...].astype(WIDE), gain[...], grad_normed[...]
        )
        grad_gain[...] = gain_grad
        out[...] = (grad_residual[...] + grad_values).astype(LOW)


def token_back(info, grad_query, grad_pair, tokens, grad_residual, gain, query_refs, pair_refs):
    full = (TOK_DEV, D)
    return pl.pallas_call(
        token_back_kernel,
        grid=(D // 256,),
        out_shape=(jax.ShapeDtypeStruct(full, LOW), jax.ShapeDtypeStruct((1, D), WIDE)),
        in_specs=[
            SMEM,
            whole(full),
            whole((TOK_DEV, 2 * KEY_WIDTH)),
            whole(full),
            whole(full),
            whole((1, D)),
        ]
        + [ANY] * (len(query_refs) + len(pair_refs)),
        out_specs=(whole(full), whole((1, D))),
        scratch_shapes=[
            pltpu.VMEM((D, D), LOW),
            pltpu.VMEM((D, 2 * KEY_WIDTH), LOW),
            pltpu.VMEM(full, WIDE),
            pltpu.SemaphoreType.DMA,
        ],
        compiler_params=params(),
        name="token_gradient",
    )(info, grad_query, grad_pair, tokens, grad_residual, gain, *query_refs, *pair_refs)


def weight_grads_kernel(info, normed, heads, grad_query, grad_pair, grad_branch, keep, send):
    quarter = D // QUARTERS
    depth = keep.shape[2]
    core = info[0] & 1

    def store(grads, start, width):
        low = grads.astype(LOW)
        for slot in range(QUARTERS):
            shard = info[2 + slot]
            for j in range(QUARTERS):
                piece = low[:, j * width : (j + 1) * width]
                upper, lower = piece[:depth], piece[depth:]

                @pl.when(shard == j)
                def _():
                    columns = slice(start, start + width)
                    keep[0, slot, :, columns] = jnp.where(core == 0, upper, lower)
                    send[0, slot, :, columns] = jnp.where(core == 0, lower, upper)

    store(tn(normed[...], grad_query[...]), 0, quarter)
    store(tn(normed[...], grad_pair[...]), quarter, 128)
    store(tn(heads[...], grad_branch[...]), quarter + 128, quarter)


def weight_grads(info, normed, heads, grad_query, grad_pair, grad_branch):
    full = (TOK_DEV, D)
    quarter = D // QUARTERS
    width = 2 * quarter + 128
    strip = pl.BlockSpec((TOK_DEV, quarter), lambda i, info: (0, i ^ (info[0] >> 1)))
    shape = (4, QUARTERS, quarter // 2, width)
    out = pl.BlockSpec((1,) + shape[1:], lambda i, info: (i, 0, 0, 0))

    def fixed(block):
        return pl.BlockSpec(block, lambda i, info: (0, 0))

    return pl.pallas_call(
        weight_grads_kernel,
        grid_spec=pltpu.PrefetchScalarGridSpec(
            num_scalar_prefetch=1,
            grid=(4,),
            in_specs=[
                strip,
                strip,
                fixed(full),
                fixed((TOK_DEV, 2 * KEY_WIDTH)),
                fixed(full),
            ],
            out_specs=(out, out),
        ),
        out_shape=(jax.ShapeDtypeStruct(shape, LOW),) * 2,
        compiler_params=params(),
        name="weight_gradients",
    )(info, normed, heads, grad_query, grad_pair, grad_branch)


def position_of(token_index):
    branch_place = TRUNK + (token_index - TRUNK) % BRANCH
    leaf_place = TRUNK + BRANCH + (token_index - TOK_DEV) % BRANCH
    return jnp.where(
        token_index < TRUNK, token_index, jnp.where(token_index < TOK_DEV, branch_place, leaf_place)
    )


def rotary_tables(positions):
    half_dim = HEAD_DIM // 2
    frequency = ROPE_BASE ** (-jnp.arange(half_dim, dtype=jnp.float32) / half_dim)
    angles = positions.astype(jnp.float32)[:, None] * frequency[None, :]
    cosine, sine = (jnp.cos(angles), jnp.sin(angles))
    return (
        jnp.concatenate([cosine, cosine], axis=1),
        jnp.concatenate([-sine, sine], axis=1),
    )


def after(values, *earlier):
    return lax.optimization_barrier((values, earlier))[0]


def fast_mesh():
    return lax.axis_size("rows") == 8 and lax.axis_size("cols") == 4


SLOT_SHARD = ((0, 2, 1, 3), (1, 3, 0, 2), (2, 0, 1, 3), (3, 1, 2, 0))
UP = [(0, 1), (1, 2), (2, 3)]
DOWN = [(1, 0), (2, 1), (3, 2)]
FAR = [(0, 3), (3, 0)]


def send_first(block):
    return (
        lax.ppermute(block, "cols", DOWN),
        lax.ppermute(block, "cols", UP),
        lax.ppermute(block, "cols", FAR),
    )


def send_second(block, first):
    place = lax.axis_index("cols")
    above, below, _ = first
    payload = jnp.where(place == 1, above, jnp.where(place == 2, below, block))
    return lax.ppermute(payload, "cols", [(3, 1), (1, 0), (0, 2), (2, 3)])


def slot_list(block, first, second):
    place = lax.axis_index("cols")
    above, below, far = first
    end = (place == 0) | (place == 3)
    return [
        block,
        second,
        jnp.where(place == 0, above, below),
        jnp.where(end, far, above),
    ]


def reduce_first(second, fourth):
    return (
        lax.ppermute(second, "cols", [(1, 3), (0, 1), (2, 0), (3, 2)]),
        lax.ppermute(fourth, "cols", FAR),
    )


def reduce_second(third, fourth, relay):
    place = lax.axis_index("cols")
    relayed = relay.astype(WIDE)
    upward_load = (
        jnp.where(place == 0, third, fourth).astype(WIDE) + jnp.where(place == 1, relayed, 0.0)
    ).astype(LOW)
    downward_load = (third.astype(WIDE) + jnp.where(place == 2, relayed, 0.0)).astype(LOW)
    return (
        lax.ppermute(upward_load, "cols", UP),
        lax.ppermute(downward_load, "cols", DOWN),
    )


def reduce_last(own, first, second):
    place = lax.axis_index("cols")
    relay, far = first
    below, above = second
    end = (place == 0) | (place == 3)
    return (
        own.astype(WIDE)
        + below.astype(WIDE)
        + above.astype(WIDE)
        + jnp.where(end, relay.astype(WIDE) + far.astype(WIDE), 0.0)
    )


def flip(block, bit):
    count = lax.axis_size("rows")
    return lax.ppermute(block, "rows", [(i, i ^ bit) for i in range(count)])


def add_low(one, two):
    return (one.astype(WIDE) + two.astype(WIDE)).astype(LOW)


def reduce_chips(keep, got):
    half = keep.shape[1] // 2

    def sums(chips, part):
        return jnp.stack([add_low(keep[i][part], got[i][part]) for i in chips])

    one, two = slice(0, half), slice(half, None)
    got_x = flip(sums((1, 3), one), 2)
    got_y = flip(sums((2, 3), two), 4)
    near_x = sums((0, 2), one)
    near_y = sums((0, 1), two)
    got_xy = flip(add_low(near_x[1], got_x[1]), 4)
    got_yx = flip(add_low(near_y[1], got_y[1]), 2)
    wide = [a.astype(WIDE) for a in (near_x[0], got_x[0], got_xy, near_y[0], got_y[0], got_yx)]
    return wide[0] + wide[1] + wide[2], wide[3] + wide[4] + wide[5]


def on_device(
    tokens,
    query_weight,
    key_weight,
    value_weight,
    out_weight,
    router_weight,
    attention_gain,
    experts_gain,
    gate_weight,
    upward_weight,
    down_weight,
    routes,
    leaf_parent,
    cotangent,
):
    row_count = lax.axis_size("rows")
    col_count = lax.axis_size("cols")
    row_place = lax.axis_index("rows")
    col_place = lax.axis_index("cols")
    fast = fast_mesh()
    parity = lax.rem(col_place, 2)
    tree_id = lax.div(row_place * col_count + col_place, 2)
    parent_row = lax.dynamic_slice_in_dim(leaf_parent, tree_id, 1, 0)[0]
    depth, query_part = query_weight.shape
    key_part = key_weight.shape[1]
    router_part = router_weight.shape[1]
    gain_part = attention_gain.shape[0]
    expert_total = router_part * col_count
    local_experts = gate_weight.shape[0]
    capacity = TOK_DEV * TOP // expert_total * 5 // 4

    shards = (
        jnp.asarray(SLOT_SHARD, jnp.int32)[col_place]
        if fast
        else jnp.arange(4, dtype=jnp.int32)
    )
    branch_rows = jnp.where(parity == 0, TRUNK + BRANCH * parent_row, TRUNK)
    info = jnp.concatenate(
        [jnp.stack([row_place, parity]), shards, branch_rows, jnp.zeros((2,), jnp.int32)]
    ).astype(jnp.int32)

    small = jnp.concatenate([attention_gain, experts_gain, router_weight.reshape(-1)])
    small_all = lax.all_gather(small, ("rows", "cols"), axis=0)
    attention_scale = small_all[:, :gain_part].reshape(1, D).astype(WIDE)
    experts_scale = small_all[:, gain_part : 2 * gain_part].reshape(1, D).astype(WIDE)
    router_rows = jnp.transpose(
        small_all[:, 2 * gain_part :].reshape(row_count, col_count, depth, router_part),
        (1, 3, 0, 2),
    ).reshape(expert_total, D)

    packed = jnp.concatenate([query_weight, key_weight, value_weight, out_weight], axis=1)
    shard_blocks = [
        jnp.concatenate(
            [gate_weight[expert].T, upward_weight[expert].T, down_weight[expert]], axis=0
        )
        for expert in range(local_experts)
    ]
    firsts, seconds = ([], [])
    if fast:
        packed_first = send_first(packed)
        packed_second = send_second(packed, packed_first)
        own = jnp.stack(slot_list(packed, packed_first, packed_second))
        ahead = packed_second
        for expert_at in range(local_experts):
            block = after(shard_blocks[expert_at], ahead)
            shard_blocks[expert_at] = block
            first = send_first(block)
            firsts.append(first)
            seconds.append(send_second(block, first))
            ahead = first
        beside, across = flip(own, 2), flip(own, 4)
        corner = [flip(beside[:2], 4), flip(across[2:], 2)]
        same = [own, beside, across] + corner
        same = [after(piece, firsts[0][0], firsts[0][1]) for piece in same]
        pieces = same + [flip(piece, 1) for piece in same]
        query_refs = pair_refs = out_refs = pieces
        expert_refs = [
            [shard_blocks[i], seconds[i], *firsts[i]] for i in range(local_experts)
        ]
    else:
        packed_all = lax.all_gather(lax.all_gather(packed, "cols", axis=0), "rows", axis=0)

        def unpack(start, width):
            part = packed_all[..., start : start + width]
            return jnp.swapaxes(part, 1, 2).reshape(row_count * depth, col_count * width)

        key_at = query_part
        query_refs = [unpack(0, query_part)]
        pair_refs = [
            jnp.concatenate(
                [
                    unpack(key_at, key_part).reshape(D, QUARTERS, -1),
                    unpack(key_at + key_part, key_part).reshape(D, QUARTERS, -1),
                ],
                axis=2,
            ).reshape(D, -1)
        ]
        out_refs = [unpack(key_at + 2 * key_part, query_part)]
        expert_refs = [
            [lax.all_gather(block, "cols", axis=0)[i] for i in range(col_count)]
            for block in shard_blocks
        ]

    routes_all = lax.all_gather(routes.T, "rows", axis=0)
    grad_all = lax.all_gather(cotangent, "rows", axis=0)

    local_index = (1 - parity) * TOK_DEV + jnp.arange(TOK_DEV, dtype=jnp.int32)
    cosine, sine = rotary_tables(position_of(local_index))
    normed, own_pair = key_value(info, tokens, attention_scale, cosine, sine, pair_refs)
    pairs = [(i + 1, i) for i in range(0, col_count, 2)]
    partner = lax.ppermute(own_pair, "cols", pairs)
    if fast:
        normed_query = after(normed, firsts[0][2])
    else:
        normed_query = normed
    queries = query(info, normed_query, cosine, sine, query_refs)
    if fast:
        queries = after(queries, seconds[0])
    heads = attention(info, queries, own_pair, partner)
    if fast:
        heads = after(heads, firsts[1][0], firsts[1][1])
    residual, normed_two = out_projection(info, heads, tokens, experts_scale, out_refs)
    rows_all = lax.all_gather(normed_two, "rows", axis=0)
    if fast:
        rows_all = after(rows_all, firsts[1][2])

    picked = dispatch(
        info, rows_all, grad_all, routes_all, router_rows, capacity, local_experts
    )
    height = row_count * capacity
    token_rows = [a.reshape(height, D) for a in picked[:local_experts]]
    grad_rows = [a.reshape(height, D) for a in picked[local_experts : 2 * local_experts]]
    share_rows = [a.reshape(height, 1) for a in picked[2 * local_experts : 3 * local_experts]]
    logits = lax.dynamic_index_in_dim(picked[-1], row_place, 0, keepdims=False)

    out_rows, back_rows, gate_dots, reduced, marks = ([], [], [], [], [])
    for e in range(local_experts):
        rows_in = token_rows[e]
        if fast and e == 0:
            rows_in = after(rows_in, seconds[0])
        if fast and e == 1:
            rows_in = after(rows_in, seconds[1], *marks[0])
        out_row, back_row, grad_row, acts, dots = expert(
            info, rows_in, grad_rows[e], share_rows[e], expert_refs[e], col_count
        )
        out_rows.append(out_row.reshape(row_count, capacity, D))
        back_rows.append(back_row.reshape(row_count, capacity, D))
        gate_dots.append(dots.reshape(row_count, capacity))
        if fast:
            second, fourth = expert_grads(acts, token_rows[e], grad_row, (1, 3))
            sent_first = reduce_first(second, fourth)
            marks.append([sent_first[0]])
            own_slot, third = expert_grads(acts, token_rows[e], grad_row, (0, 2))
            sent_second = reduce_second(third, fourth, sent_first[0])
            reduced.append((own_slot, sent_first, sent_second))
        else:
            slots = expert_grads(acts, token_rows[e], grad_row, tuple(range(col_count)))
            reduced.append(
                lax.psum_scatter(jnp.stack(slots), "cols", scatter_dimension=0).astype(WIDE)
            )

    routes_cols = jnp.swapaxes(routes_all, 1, 2)
    if fast:
        chips = jnp.arange(4, dtype=jnp.int32) * 2
        keep_order, send_order = (chips ^ row_place, (chips + 1) ^ row_place)

        def both_ways(rows):
            got = flip(combine(send_order, info, routes_cols, rows, expert_total), 1)
            keep = combine(keep_order, info, routes_cols, rows, expert_total)
            return reduce_chips(keep, got)

        back_sum = jnp.concatenate(both_ways(back_rows), axis=0)
        out_rows = [after(a, back_sum) for a in out_rows]
        mixture = jnp.concatenate(both_ways(out_rows), axis=0)
    else:
        order = jnp.arange(row_count, dtype=jnp.int32)

        def summed(rows):
            part = combine(order, info, routes_cols, rows, expert_total)
            return lax.psum_scatter(part, "rows", scatter_dimension=0).astype(WIDE)

        back_sum = summed(back_rows)
        mixture = summed(out_rows)
    layer_output = (residual + mixture).astype(LOW)

    ids = jnp.arange(expert_total, dtype=jnp.int32)
    named = routes_all[:, :, None, :] == ids[None, None, :, None]
    hit = jnp.any(named, axis=1)
    rank = jnp.cumsum(hit.astype(jnp.int32), axis=2) - 1
    own_at = row_place * local_experts
    own_hit = lax.dynamic_slice_in_dim(hit, own_at, local_experts, 1)
    own_rank = lax.dynamic_slice_in_dim(rank, own_at, local_experts, 1)
    dots = jnp.stack(gate_dots, axis=1)
    grad_share = jnp.where(
        own_hit, jnp.take_along_axis(dots, jnp.clip(own_rank, 0, capacity - 1), axis=2), 0.0
    )
    grad_share_all = lax.all_gather(grad_share, "rows", axis=1, tiled=True)
    grad_shares = lax.dynamic_index_in_dim(grad_share_all, row_place, 0, keepdims=False)
    chosen_of = lax.dynamic_index_in_dim(hit, row_place, 0, keepdims=False)

    def shares_out(logit_cols):
        softmax_out = jax.nn.softmax(logit_cols, axis=0)
        chosen = jnp.where(chosen_of, softmax_out, 0.0)
        return chosen / jnp.sum(chosen, axis=0, keepdims=True)

    _, router_pullback = jax.vjp(shares_out, logits)
    (grad_logits,) = router_pullback(grad_shares)

    grad_residual, grad_branch, grad_heads, experts_gain_grad, router_grad = branch_back(
        info,
        residual,
        normed_two,
        back_sum,
        cotangent,
        grad_logits,
        router_rows,
        experts_scale,
        out_refs,
    )
    grad_query, own_grad, source_grad = attention_back(
        info, queries, own_pair, partner, grad_heads, cosine, sine
    )
    arrived = lax.ppermute(source_grad.astype(LOW), "cols", [(j, i) for i, j in pairs])
    grad_pair = join_grads(info, own_grad, source_grad, arrived, cosine, sine)
    tokens_grad, attention_gain_grad = token_back(
        info, grad_query, grad_pair, tokens, grad_residual, attention_scale, query_refs, pair_refs
    )

    if fast:
        keep, send = weight_grads(info, normed, heads, grad_query, grad_pair, grad_branch)
        first_half, second_half = reduce_chips(keep, flip(send, 1))
        slots = [a.astype(LOW) for a in (*first_half, *second_half)]
        sent_first = reduce_first(slots[1], slots[3])
        sent_second = reduce_second(slots[2], slots[3], sent_first[0])
        sums = reduce_last(slots[0], sent_first, sent_second)
        expert_sums = [reduce_last(*parts) for parts in reduced]
    else:
        full_grads = [
            tn(normed, grad_query),
            *jnp.moveaxis(tn(normed, grad_pair).reshape(D, QUARTERS, 2, -1), 2, 0),
            tn(heads, grad_branch),
        ]
        packed_grad = jnp.concatenate(
            [
                grad.astype(LOW).reshape(row_count, depth, col_count, -1)
                for grad in full_grads
            ],
            axis=3,
        )
        row_sums = lax.psum_scatter(packed_grad, "rows", scatter_dimension=0)
        sums = lax.psum_scatter(row_sums, "cols", scatter_dimension=1).astype(WIDE)
        expert_sums = reduced

    small_grads = jnp.concatenate(
        [
            attention_gain_grad.reshape(-1, gain_part),
            experts_gain_grad.reshape(-1, gain_part),
            jnp.transpose(
                router_grad.reshape(col_count, router_part, row_count, depth), (2, 0, 3, 1)
            ).reshape(row_count * col_count, depth * router_part),
        ],
        axis=1,
    )
    small_sums = lax.psum_scatter(small_grads, ("rows", "cols"), scatter_dimension=0)

    key_at = query_part
    value_at = key_at + key_part
    out_at = value_at + key_part
    part = down_weight.shape[1]
    gate_grad, upward_grad, down_grad = (
        jnp.stack([sums_of[which * part : (which + 1) * part] for sums_of in expert_sums])
        for which in range(3)
    )
    return (
        layer_output,
        tokens_grad,
        sums[:, :key_at],
        sums[:, key_at:value_at],
        sums[:, value_at:out_at],
        sums[:, out_at:],
        small_sums[2 * gain_part :].reshape(depth, router_part),
        small_sums[:gain_part],
        small_sums[gain_part : 2 * gain_part],
        jnp.swapaxes(gate_grad, 1, 2),
        jnp.swapaxes(upward_grad, 1, 2),
        down_grad,
    )


def solution(mesh):
    in_specs = (
        P(("rows", "cols"), None),
        P("rows", "cols"),
        P("rows", "cols"),
        P("rows", "cols"),
        P("rows", "cols"),
        P("rows", "cols"),
        P(("rows", "cols")),
        P(("rows", "cols")),
        P("rows", None, "cols"),
        P("rows", None, "cols"),
        P("rows", "cols", None),
        P(("rows", "cols"), None),
        P(),
        P(("rows", "cols"), None),
    )
    out_specs = (
        P(("rows", "cols"), None),
        P(("rows", "cols"), None),
        P("rows", "cols"),
        P("rows", "cols"),
        P("rows", "cols"),
        P("rows", "cols"),
        P("rows", "cols"),
        P(("rows", "cols")),
        P(("rows", "cols")),
        P("rows", None, "cols"),
        P("rows", None, "cols"),
        P("rows", "cols", None),
    )
    return jax.shard_map(
        on_device, mesh=mesh, in_specs=in_specs, out_specs=out_specs, check_vma=False
    )
```

time: 1320 us -> 1170 us (0.89)
  Pallas kernels: 0 us -> 261 us
  matrix products: 256 us -> 0 us
  local copies, waits for them, and re-layouts: 222 us -> 95.1 us
  waiting for transfers between devices: 589 us -> 485 us
  blocking collectives: 18.4 us -> 122 us
  other arithmetic: 130 us -> 87.3 us
    pallas_call x0 -> x20, Pallas kernels: none -> 261 us  [the longest x2 60.3 us: expert(): pl.pallas_call(functools.partial(expert_kernel, slots), grid=(height // E...]
    dot_general x45 -> x0, matrix products: 256 us -> none  [the longest x18 94.8 us: dot(): lax.dot_general(one, two, (dims, ((), ())), preferred_element_type=jnp.fl...]
    ppermute x25, waiting for transfers between devices: 399 us -> 236 us  [the longest x3 67.3 us: reduce_second(): lax.ppermute(upward_load, 'cols', UP)]
    ppermute x20 -> x24, waiting for transfers between devices: 190 us -> 34.7 us  [flip(): return lax.ppermute(block, 'rows', [(i, i ^ bit) for i in range(count)])]
    unnamed x2 -> x4, waiting for transfers between devices: 0.71 us -> 113 us
    unnamed x0 -> x1, blocking collectives: none -> 90.3 us
    all_gather x1, waiting for transfers between devices: 0.01 us -> 74 us  [on_device(): grad_all = lax.all_gather(cotangent, 'rows', axis=0)]
    gather x2, local copies, waits for them, and re-layouts: 1.3 us -> 63.1 us  [on_device(): jnp.take_along_axis(dots, jnp.clip(own_rank, 0, capacity - 1), axis=2)]
  transfers between devices with their start and end apart: 48 -> 53, of which waited for: 31 -> 26; matrix products, arithmetic and copies ran while one was open for 30% -> 14% of each run, Pallas kernels for 0% -> 18%
where the time goes in v3:
time: 1170 us; the launch traced here: 1160 us
  waiting for transfers between devices  485 us (41%)
  Pallas kernels  261 us (22%)
  blocking collectives  122 us (10%)
  local copies, waits for them, and re-layouts  95.1 us (8%)
  starting transfers between devices  94.3 us (8%)
  other arithmetic  87.3 us (7%)
  between operations  15.1 us (1%)
    unnamed x4, waiting for transfers between devices  113 us
    unnamed x1, blocking collectives  90.3 us
    all_gather x1, waiting for transfers between devices, on_device(): grad_all = lax.all_gather(cotangent, 'rows', axis=0)  74 us
    ppermute x3, waiting for transfers between devices, reduce_second(): lax.ppermute(upward_load, 'cols', UP)  67.3 us
    gather x2, local copies, waits for them, and re-layouts, on_device(): jnp.take_along_axis(dots, jnp.clip(own_rank, 0, capacity - 1), axis=2)  63.1 us
    pallas_call x2, Pallas kernels, expert(): pl.pallas_call(functools.partial(expert_kernel, slots), grid=(height // E...  60.3 us
    ppermute x3, waiting for transfers between devices, send_first(): lax.ppermute(block, 'cols', FAR)  58.1 us
    ppermute x3, waiting for transfers between devices, reduce_first(): lax.ppermute(second, 'cols', [(1, 3), (0, 1), (2, 0), (3, 2)])  48.1 us
  transfers between devices with their start and end apart: 53, of which 26 were waited for; matrix products, arithmetic and copies ran while one was open for 14% of the time, Pallas kernels for 18%

profile of v3, /device:TPU:0, one launch (start us, length us, event | category | flops | bytes accessed | tf_op | source)
XLA Modules:
  0.0 1160.3 jit_solution(12948510891254909566)
XLA Ops:
  11.4 5.6 collective-permute-start.1
  25.4 7.2 collective-permute-done.3
  35.8 6.0 collective-permute-done.2
  43.2 4.8 collective-permute-start.5
  53.7 24.3 %collective-permute-done.7.rest_2_.rest_12_ = bf16[4,192,896]{2,1,0:T(8,128)(2,1)S(1)} collective-permute-done((bf16[4,192,896]{2,1,0:T(8,128)(2,1)S(1)}, bf16[4,192,896]{2,1,0:T(8,128)(2,1)S(1)}, u32[]{:S(2)}, u32[]{:S(2)}) %collective-permute-start.7) | collective-permute-done | bytes 1376288 | tf_op jit(solution)/shard_map/ppermute | solution.py:892
  86.9 6.8 collective-permute-done.9.rest_4_.rest_14_
  96.3 25.5 %collective-permute-done.15.rest_4_ = bf16[576,1536]{1,0:T(8,128)(2,1)S(1)} collective-permute-done((bf16[576,1536]{1,0:T(8,128)(2,1)S(1)}, bf16[576,1536]{1,0:T(8,128)(2,1)S(1)}, u32[]{:S(2)}, u32[]{:S(2)}) %collective-permute-start.15) | collective-permute-done | bytes 1769504 | tf_op jit(solution)/shard_map/ppermute | solution.py:834
  124.5 6.5 collective-permute-start.16
  133.4 5.8 collective-permute-start.19
  139.9 90.3 %all-reduce = bf16[27648]{0:T(1024)(128)(2,1)S(1)} all-reduce(bf16[27648]{0:T(1024)(128)(2,1)S(1)} %dynamic-update-slice), channel_id=2, replica_groups=mesh['rows'=8,'cols'=4] {'rows','cols'}, use_global_device_ids=true, to_apply=%add | all-reduce | flops 27648 | bytes 110592
  234.6 5.0 norm_key_value.1
  241.6 8.8 query_projection.1.queries
  255.4 11.0 tree_attention.1.heads
  266.4 10.8 out_projection.1
  285.2 10.0 all-gather.4.routes
  298.1 25.3 %collective-permute-done.20.rest_4_ = bf16[576,1536]{1,0:T(8,128)(2,1)S(1)} collective-permute-done((bf16[576,1536]{1,0:T(8,128)(2,1)}, bf16[576,1536]{1,0:T(8,128)(2,1)S(1)}, u32[]{:S(2)}, u32[]{:S(2)}) %collective-permute-start.20) | collective-permute-done | bytes 1769504 | tf_op jit(solution)/shard_map/ppermute | solution.py:834
  323.5 24.4 %all-gather.8.cloned.1.call-done = bf16[4096,1536]{1,0:T(8,128)(2,1)} async-done(((bf16[512,1536]{1,0:T(8,128)(2,1)}), bf16[4096,1536]{1,0:T(8,128)(2,1)}) %all-gather.8.cloned.1.call-update) | async-done | bytes 12582928 | tf_op jit(solution)/shard_map/all_gather | solution.py:1039
  347.9 74.0 %all-gather.10.cloned.1.call-done = bf16[4096,1536]{1,0:T(8,128)(2,1)} async-done(((bf16[512,1536]{1,0:T(8,128)(2,1)}), bf16[4096,1536]{1,0:T(8,128)(2,1)}) %all-gather.10.cloned.1.call-update) | async-done | bytes 12582928 | tf_op jit(solution)/shard_map/all_gather | solution.py:1021
  421.9 20.9 %dispatch.1 = (bf16[8,160,1536]{2,1,0:T(8,128)(2,1)}, bf16[8,160,1536]{2,1,0:T(8,128)(2,1)}, bf16[8,160,1536]{2,1,0:T(8,128)(2,1)}, bf16[8,160,1536]{2,1,0:T(8,1...) custom-call(s32[16]{0:T(128)} %concatenate.30.info, bf16[8,512,1536]{2,1,0:T(8,128)(2,1)} %bitcast.202, ...), custom_call_target="tpu_custom_call" | custom-call | tf_op jit(solution)/shard_map/dispatch/pallas_call | solution.py:400
  442.8 30.2 %expert.2 = (bf16[1280,1536]{1,0:T(8,128)(2,1)}, bf16[1280,1536]{1,0:T(8,128)(2,1)}, bf16[1280,1536]{1,0:T(8,128)(2,1)}, bf16[4,576,1280]{2,1,0:T(8,128)(2,1)}, f32[1280,1]{1,0:T(8,128)}) custom-call(s32[16]{0:T(128)} %concatenate.30.info, bf16[1280,1536]{1,0:T(8,128)(2,1)} %bitcast.189, bf16[1280,1536]{1,0:T(8,128)(2,1)} %bitcast.207, f32[1280,1]{1,0:T(8,128)} %bitcast.209, ...), custom_call_target="tpu_custom_call" | custom-call | tf_op jit(solution)/shard_map/expert/pallas_call | solution.py:502
  473.0 10.6 expert_gradients.4
  487.8 37.9 %collective-permute-done.22 = bf16[576,1536]{1,0:T(8,128)(2,1)S(1)} collective-permute-done((bf16[576,1536]{1,0:T(8,128)(2,1)}, bf16[576,1536]{1,0:T(8,128)(2,1)S(1)}, u32[]{:S(2)}, u32[]{:S(2)}) %collective-permute-start.22) | collective-permute-done | bytes 1769504 | tf_op jit(solution)/shard_map/ppermute | solution.py:859
  525.7 30.2 %expert.3 = (bf16[1280,1536]{1,0:T(8,128)(2,1)}, bf16[1280,1536]{1,0:T(8,128)(2,1)}, bf16[1280,1536]{1,0:T(8,128)(2,1)}, bf16[4,576,1280]{2,1,0:T(8,128)(2,1)}, f32[1280,1]{1,0:T(8,128)}) custom-call(s32[16]{0:T(128)} %concatenate.30.info, bf16[1280,1536]{1,0:T(8,128)(2,1)} %bitcast.186, bf16[1280,1536]{1,0:T(8,128)(2,1)} %bitcast.206, f32[1280,1]{1,0:T(8,128)} %bitcast.208, ...), custom_call_target="tpu_custom_call" | custom-call | tf_op jit(solution)/shard_map/expert/pallas_call | solution.py:502
  555.9 10.5 combine.5
  567.2 10.6 combine.4
  586.0 9.1 reduce-window.6
  596.4 10.6 expert_gradients.7
  608.3 63.1 %gather_fusion = f32[8192]{0:T(1024)S(1)} fusion(f32[8,2,160]{2,0,1:T(8,128)S(1)} %pad_maximum_fusion.15, s32[8192]{0:T(1024)S(1)} %bitcast.181), kind=kCustom, calls=%fused_computation | custom fusion | bytes 163840 | tf_op jit(solution)/shard_map/jit(take_along_axis)/gather | solution.py:1111
  676.6 21.8 %all_gather.35 = f32[8,16,512]{2,0,1:T(8,128)S(1)} all-gather(f32[8,2,512]{2,0,1:T(8,128)S(1)} %copy.74), channel_id=1, replica_groups=mesh['rows'=8,'cols'=4] {'rows'}, dimensions={1}, use_global_device_ids=true | all-gather | bytes 294912 | tf_op jit(solution)/shard_map/all_gather | solution.py:1113
  704.1 12.0 %experts_norm_back.1 = (f32[512,1536]{1,0:T(8,128)}, bf16[512,1536]{1,0:T(8,128)(2,1)}, bf16[512,1536]{1,0:T(8,128)(2,1)}, f32[1,1536]{1,0:T(1,128)}, f32[16,1536]{1,0:T(8,128)}) custom-call(s32[16]{0:T(128)} %concatenate.30.info, f32[512,1536]{1,0:T(8,128)} %get-tuple-element.80.residual, bf16[512,1536]{1,0:T(8,128)(2,1)} %get-tuple-element.81.normed, ...), custom_call_target="tpu_custom_call" | custom-call | tf_op jit(solution)/shard_map/experts_norm_back/pallas_call | solution.py:629
  716.1 15.4 %tree_attention_back.1 = (bf16[512,1536]{1,0:T(8,128)(2,1)}, f32[512,512]{1,0:T(8,128)}, f32[512,512]{1,0:T(8,128)}) custom-call(s32[16]{0:T(128)} %concatenate.30.info, bf16[512,1536]{1,0:T(8,128)(2,1)} %query_projection.1.queries, bf16[512,512]{1,0:T(8,128)(2,1)} %get-tuple-element.77.own, bf16[512,512]{1,0:T(8,128)(2,1)} %copy-done.13, ...), custom_call_target="tpu_custom_call" | custom-call | tf_op jit(solution)/shard_map/tree_attention_back/pallas_call | solution.py:296
  732.9 5.3 collective-permute-start.33
  738.2 10.6 combine.7
  753.6 14.9 %weight_gradients.1 = (bf16[4,4,192,896]{3,2,1,0:T(8,128)(2,1)}, bf16[4,4,192,896]{3,2,1,0:T(8,128)(2,1)}) custom-call(s32[16]{0:T(128)} %concatenate.30.info, bf16[512,1536]{1,0:T(8,128)(2,1)} %get-tuple-element.75.normed, bf16[512,1536]{1,0:T(8,128)(2,1)} %tree_attention.1.heads, bf16[512,1536]{1,0:T(8,128)(2,1)} %get-tuple-element.104.grad_query, ...), custom_call_target="tpu_custom_call" | custom-call | tf_op jit(solution)/shard_map/weight_gradients/pallas_call | solution.py:777
  768.6 10.7 expert_gradients.5
  783.5 5.0 fusion.1
  792.4 10.7 expert_gradients.6
  803.2 5.5 fusion.7
  808.6 15.8 %collective-permute-done.45 = bf16[576,1536]{1,0:T(8,128)(2,1)S(1)} collective-permute-done((bf16[576,1536]{1,0:T(8,128)(2,1)S(1)}, bf16[576,1536]{1,0:T(8,128)(2,1)S(1)}, u32[]{:S(2)}, u32[]{:S(2)}) %collective-permute-start.45) | collective-permute-done | bytes 1769504 | tf_op jit(solution)/shard_map/ppermute | solution.py:860
  824.4 4.2 collective-permute-start.49
  828.7 31.8 %collective-permute-done.43 = bf16[576,1536]{1,0:T(8,128)(2,1)} collective-permute-done((bf16[576,1536]{1,0:T(8,128)(2,1)}, bf16[576,1536]{1,0:T(8,128)(2,1)}, u32[]{:S(2)}, u32[]{:S(2)}) %collective-permute-start.43) | collective-permute-done | bytes 1769504 | tf_op jit(solution)/shard_map/ppermute | solution.py:872
  860.5 5.6 collective-permute-start.47
  873.0 27.5 %collective-permute-done.49 = bf16[576,1536]{1,0:T(8,128)(2,1)} collective-permute-done((bf16[576,1536]{1,0:T(8,128)(2,1)S(1)}, bf16[576,1536]{1,0:T(8,128)(2,1)}, u32[]{:S(2)}, u32[]{:S(2)}) %collective-permute-start.49) | collective-permute-done | bytes 1769504 | tf_op jit(solution)/shard_map/ppermute | solution.py:860
  900.4 35.4 %collective-permute-done.47 = bf16[576,1536]{1,0:T(8,128)(2,1)} collective-permute-done((bf16[576,1536]{1,0:T(8,128)(2,1)}, bf16[576,1536]{1,0:T(8,128)(2,1)}, u32[]{:S(2)}, u32[]{:S(2)}) %collective-permute-start.47) | collective-permute-done | bytes 1769504 | tf_op jit(solution)/shard_map/ppermute | solution.py:872
  942.0 10.7 combine.6
  976.3 13.6 %token_gradient.1 = (bf16[512,1536]{1,0:T(8,128)(2,1)}, f32[1,1536]{1,0:T(1,128)}) custom-call(s32[16]{0:T(128)} %concatenate.30.info, bf16[512,1536]{1,0:T(8,128)(2,1)} %get-tuple-element.104.grad_query, bf16[512,512]{1,0:T(8,128)(2,1)} %join_key_value_gradients.1.grad_pair, bf16[512,1536]{1,0:T(8,128)(2,1)} %tokens.5, ...), custom_call_target="tpu_custom_call" | custom-call | tf_op jit(solution)/shard_map/token_gradient/pallas_call | solution.py:717
  999.8 111.8 %all-reduce.4.cloned.1.call-done = f32[32,864]{1,0:T(8,128)} async-done(((f32[32,864]{1,0:T(8,128)}), f32[32,864]{1,0:T(8,128)}) %all-reduce.4.cloned.1.call-update) | async-done | bytes 110608
  1129.9 10.2 collective-permute-done.39
  (279 shorter events, 180.7 us)
Async XLA Ops:
  7.2 340.7 %all-gather.8.cloned.1.call-start = ((), (), s32[]{:S(2)}) async-start(), calls=%async_computation | async-start | bytes 14155776 | tf_op jit(solution)/shard_map/all_gather | solution.py:1039
  10.1 13.0 %collective-permute-start = (bf16[192,896]{1,0:T(8,128)(2,1)S(1)}, bf16[192,896]{1,0:T(8,128)(2,1)S(1)}, u32[]{:S(2)}, u32[]{:S(2)}) collective-permute-start(bf16[192,896]{1,0:T(8,128)(2,1)S(1)} %pad_maximum_fusion.11), channel_id=1, source_target_pairs={{1,0},{2,1},{3,2},{5,4},{6,5},{7,6},{9,8},{10,9},{11,10},{13,12},{... | collective-permute-start | bytes 1032200 | tf_op jit(solution)/shard_map/ppermute | solution.py:832
  11.4 14.0 %collective-permute-start.1 = (bf16[192,896]{1,0:T(8,128)(2,1)S(1)}, bf16[192,896]{1,0:T(8,128)(2,1)S(1)}, u32[]{:S(2)}, u32[]{:S(2)}) collective-permute-start(bf16[192,896]{1,0:T(8,128)(2,1)S(1)} %pad_maximum_fusion.11), channel_id=1, source_target_pairs={{0,1},{1,2},{2,3},{4,5},{5,6},{6,7},{8,9},{9,10},{10,11},{12,13},{... | collective-permute-start | bytes 1032200 | tf_op jit(solution)/shard_map/ppermute | solution.py:833
  16.9 15.7 %collective-permute-start.3 = (bf16[192,896]{1,0:T(8,128)(2,1)S(1)}, bf16[192,896]{1,0:T(8,128)(2,1)S(1)}, u32[]{:S(2)}, u32[]{:S(2)}) collective-permute-start(bf16[192,896]{1,0:T(8,128)(2,1)S(1)} %pad_maximum_fusion.11), channel_id=1, source_target_pairs={{0,3},{3,0},{4,7},{7,4},{8,11},{11,8},{12,15},{15,12},{16,19},{19,... | collective-permute-start | bytes 1032200 | tf_op jit(solution)/shard_map/ppermute | solution.py:834
  41.9 44.2 %collective-permute-start.4 = (bf16[576,1536]{1,0:T(8,128)(2,1)S(1)}, bf16[576,1536]{1,0:T(8,128)(2,1)S(1)}, u32[]{:S(2)}, u32[]{:S(2)}) collective-permute-start(bf16[576,1536]{1,0:T(8,128)(2,1)S(1)} %pad_maximum_fusion.2.rest_0_), channel_id=1, source_target_pairs={{1,0},{2,1},{3,2},{5,4},{6,5},{7,6},{9,8},{10,9},{11,10},{13,12},{... | collective-permute-start | bytes 5308424 | tf_op jit(solution)/shard_map/ppermute | solution.py:832
  43.2 43.7 %collective-permute-start.5 = (bf16[576,1536]{1,0:T(8,128)(2,1)S(1)}, bf16[576,1536]{1,0:T(8,128)(2,1)S(1)}, u32[]{:S(2)}, u32[]{:S(2)}) collective-permute-start(bf16[576,1536]{1,0:T(8,128)(2,1)S(1)} %pad_maximum_fusion.2.rest_0_), channel_id=1, source_target_pairs={{0,1},{1,2},{2,3},{4,5},{5,6},{6,7},{8,9},{9,10},{10,11},{12,13},{... | collective-permute-start | bytes 5308424 | tf_op jit(solution)/shard_map/ppermute | solution.py:833
  48.2 29.8 %collective-permute-start.7 = (bf16[4,192,896]{2,1,0:T(8,128)(2,1)S(1)}, bf16[4,192,896]{2,1,0:T(8,128)(2,1)S(1)}, u32[]{:S(2)}, u32[]{:S(2)}) collective-permute-start(bf16[4,192,896]{2,1,0:T(8,128)(2,1)S(1)} %pad_maximum_fusion.8.rest_0_.rest_10_), channel_id=1, source_target_pairs={{0,16},{4,20},{8,24},{12,28},{16,0},{20,4},{24,8},{28,12},{1,17},{... | collective-permute-start | bytes 4128776 | tf_op jit(solution)/shard_map/ppermute | solution.py:892
  49.6 30.7 %collective-permute-start.6 = (bf16[4,192,896]{2,1,0:T(8,128)(2,1)S(1)}, bf16[4,192,896]{2,1,0:T(8,128)(2,1)}, u32[]{:S(2)}, u32[]{:S(2)}) collective-permute-start(bf16[4,192,896]{2,1,0:T(8,128)(2,1)S(1)} %pad_maximum_fusion.8.rest_0_.rest_10_), channel_id=1, source_target_pairs={{0,8},{4,12},{8,0},{12,4},{16,24},{20,28},{24,16},{28,20},{1,9},{5... | collective-permute-start | bytes 4128776 | tf_op jit(solution)/shard_map/ppermute | solution.py:892
  51.1 70.7 %collective-permute-start.15 = (bf16[576,1536]{1,0:T(8,128)(2,1)S(1)}, bf16[576,1536]{1,0:T(8,128)(2,1)S(1)}, u32[]{:S(2)}, u32[]{:S(2)}) collective-permute-start(bf16[576,1536]{1,0:T(8,128)(2,1)S(1)} %pad_maximum_fusion.2.rest_0_), channel_id=1, source_target_pairs={{0,3},{3,0},{4,7},{7,4},{8,11},{11,8},{12,15},{15,12},{16,19},{19,... | collective-permute-start | bytes 5308424 | tf_op jit(solution)/shard_map/ppermute | solution.py:834
  78.1 15.6 %collective-permute-start.9 = (bf16[2,192,896]{2,1,0:T(8,128)(2,1)S(1)}, bf16[2,192,896]{2,1,0:T(8,128)(2,1)S(1)}, u32[]{:S(2)}, u32[]{:S(2)}) collective-permute-start(bf16[2,192,896]{2,1,0:T(8,128)(2,1)S(1)} %slice.502), channel_id=1, source_target_pairs={{0,8},{4,12},{8,0},{12,4},{16,24},{20,28},{24,16},{28,20},{1,9},{5... | collective-permute-start | bytes 2064392 | tf_op jit(solution)/shard_map/ppermute | solution.py:892
  86.9 45.4 %collective-permute-start.12 = (bf16[4,192,896]{2,1,0:T(8,128)(2,1)S(1)}, bf16[4,192,896]{2,1,0:T(8,128)(2,1)S(1)}, u32[]{:S(2)}, u32[]{:S(2)}) collective-permute-start(bf16[4,192,896]{2,1,0:T(8,128)(2,1)S(1)} %collective-permute-done.7.rest_2_.rest_12_), channel_id=1, source_target_pairs={{0,4},{4,0},{8,12},{12,8},{16,20},{20,16},{24,28},{28,24},{1,5},{5... | collective-permute-start | bytes 4128776 | tf_op jit(solution)/shard_map/ppermute | solution.py:892
  93.7 30.8 %collective-permute-start.14 = (bf16[2,192,896]{2,1,0:T(8,128)(2,1)S(1)}, bf16[2,192,896]{2,1,0:T(8,128)(2,1)S(1)}, u32[]{:S(2)}, u32[]{:S(2)}) collective-permute-start(bf16[2,192,896]{2,1,0:T(8,128)(2,1)S(1)} %collective-permute-done.9.rest_4_.rest_14_), channel_id=1, source_target_pairs={{0,4},{4,0},{8,12},{12,8},{16,20},{20,16},{24,28},{28,24},{1,5},{5... | collective-permute-start | bytes 2064392 | tf_op jit(solution)/shard_map/ppermute | solution.py:892
  94.3 36.7 %collective-permute-start.13 = (bf16[2,192,896]{2,1,0:T(8,128)(2,1)S(1)}, bf16[2,192,896]{2,1,0:T(8,128)(2,1)S(1)}, u32[]{:S(2)}, u32[]{:S(2)}) collective-permute-start(bf16[2,192,896]{2,1,0:T(8,128)(2,1)S(1)} %collective-permute-done.8.rest_3_.rest_13_), channel_id=1, source_target_pairs={{0,4},{4,0},{8,12},{12,8},{16,20},{20,16},{24,28},{28,24},{1,5},{5... | collective-permute-start | bytes 2064392 | tf_op jit(solution)/shard_map/ppermute | solution.py:892
  95.8 138.8 %collective-permute-start.11 = (bf16[4,192,896]{2,1,0:T(8,128)(2,1)}, bf16[4,192,896]{2,1,0:T(8,128)(2,1)}, u32[]{:S(2)}, u32[]{:S(2)}) collective-permute-start(bf16[4,192,896]{2,1,0:T(8,128)(2,1)} %collective-permute-done.6.rest_1_.rest_11_), channel_id=1, source_target_pairs={{0,4},{4,0},{8,12},{12,8},{16,20},{20,16},{24,28},{28,24},{1,5},{5... | collective-permute-start | bytes 4128776 | tf_op jit(solution)/shard_map/ppermute | solution.py:892
  123.0 111.6 %collective-permute-start.10 = (bf16[4,192,896]{2,1,0:T(8,128)(2,1)S(1)}, bf16[4,192,896]{2,1,0:T(8,128)(2,1)}, u32[]{:S(2)}, u32[]{:S(2)}) collective-permute-start(bf16[4,192,896]{2,1,0:T(8,128)(2,1)S(1)} %pad_maximum_fusion.8.rest_0_.rest_10_), channel_id=1, source_target_pairs={{0,4},{4,0},{8,12},{12,8},{16,20},{20,16},{24,28},{28,24},{1,5},{5... | collective-permute-start | bytes 4128776 | tf_op jit(solution)/shard_map/ppermute | solution.py:892
  124.5 126.0 %collective-permute-start.16 = (bf16[576,1536]{1,0:T(8,128)(2,1)}, bf16[576,1536]{1,0:T(8,128)(2,1)}, u32[]{:S(2)}, u32[]{:S(2)}) collective-permute-start(bf16[576,1536]{1,0:T(8,128)(2,1)} %select_select_fusion.1), channel_id=1, source_target_pairs={{3,1},{1,0},{0,2},{2,3},{7,5},{5,4},{4,6},{6,7},{11,9},{9,8},{8,10... | collective-permute-start | bytes 5308424 | tf_op jit(solution)/shard_map/ppermute | solution.py:842
  131.0 135.3 %collective-permute-start.18 = (bf16[576,1536]{1,0:T(8,128)(2,1)}, bf16[576,1536]{1,0:T(8,128)(2,1)}, u32[]{:S(2)}, u32[]{:S(2)}) collective-permute-start(bf16[576,1536]{1,0:T(8,128)(2,1)} %pad_maximum_fusion.3.rest_0_), channel_id=1, source_target_pairs={{1,0},{2,1},{3,2},{5,4},{6,5},{7,6},{9,8},{10,9},{11,10},{13,12},{... | collective-permute-start | bytes 5308424 | tf_op jit(solution)/shard_map/ppermute | solution.py:832
  133.4 132.9 %collective-permute-start.19 = (bf16[576,1536]{1,0:T(8,128)(2,1)}, bf16[576,1536]{1,0:T(8,128)(2,1)}, u32[]{:S(2)}, u32[]{:S(2)}) collective-permute-start(bf16[576,1536]{1,0:T(8,128)(2,1)} %pad_maximum_fusion.3.rest_0_), channel_id=1, source_target_pairs={{0,1},{1,2},{2,3},{4,5},{5,6},{6,7},{8,9},{9,10},{10,11},{12,13},{... | collective-permute-start | bytes 5308424 | tf_op jit(solution)/shard_map/ppermute | solution.py:833
  239.6 15.0 %collective-permute-start.17 = (bf16[512,512]{1,0:T(8,128)(2,1)}, bf16[512,512]{1,0:T(8,128)(2,1)S(1)}, u32[]{:S(2)}, u32[]{:S(2)}) collective-permute-start(bf16[512,512]{1,0:T(8,128)(2,1)} %get-tuple-element.77.own), channel_id=1, source_target_pairs={{1,0},{3,2},{5,4},{7,6},{9,8},{11,10},{13,12},{15,14},{17,16},{19,... | collective-permute-start | bytes 1572872 | tf_op jit(solution)/shard_map/ppermute | solution.py:1027
  277.2 144.7 %all-gather.10.cloned.1.call-start = ((), (), s32[]{:S(2)}) async-start(), calls=%async_computation.1 | async-start | bytes 14155776 | tf_op jit(solution)/shard_map/all_gather | solution.py:1021
  277.9 833.7 %all-reduce.4.cloned.1.call-start = ((), (), s32[]{:S(2)}) async-start(), calls=%async_computation.2 | async-start | bytes 229376
  278.0 45.5 %collective-permute-start.20 = (bf16[576,1536]{1,0:T(8,128)(2,1)}, bf16[576,1536]{1,0:T(8,128)(2,1)S(1)}, u32[]{:S(2)}, u32[]{:S(2)}) collective-permute-start(bf16[576,1536]{1,0:T(8,128)(2,1)} %pad_maximum_fusion.3.rest_0_), channel_id=1, source_target_pairs={{0,3},{3,0},{4,7},{7,4},{8,11},{11,8},{12,15},{15,12},{16,19},{19,... | collective-permute-start | bytes 5308424 | tf_op jit(solution)/shard_map/ppermute | solution.py:834
  298.1 189.7 %collective-permute-start.21 = (bf16[576,1536]{1,0:T(8,128)(2,1)}, bf16[576,1536]{1,0:T(8,128)(2,1)}, u32[]{:S(2)}, u32[]{:S(2)}) collective-permute-start(bf16[576,1536]{1,0:T(8,128)(2,1)} %select_select_fusion), channel_id=1, source_target_pairs={{3,1},{1,0},{0,2},{2,3},{7,5},{5,4},{4,6},{6,7},{11,9},{9,8},{8,10... | collective-permute-start | bytes 5308424 | tf_op jit(solution)/shard_map/ppermute | solution.py:842
  483.6 42.1 %collective-permute-start.22 = (bf16[576,1536]{1,0:T(8,128)(2,1)}, bf16[576,1536]{1,0:T(8,128)(2,1)S(1)}, u32[]{:S(2)}, u32[]{:S(2)}) collective-permute-start(bf16[576,1536]{1,0:T(8,128)(2,1)} %get-tuple-element.92), channel_id=1, source_target_pairs={{1,3},{0,1},{2,0},{3,2},{5,7},{4,5},{6,4},{7,6},{9,11},{8,9},{10,8... | collective-permute-start | bytes 5308424 | tf_op jit(solution)/shard_map/ppermute | solution.py:859
  582.7 88.8 %collective-permute-start.26 = (bf16[2,256,1536]{2,1,0:T(8,128)(2,1)}, bf16[2,256,1536]{2,1,0:T(8,128)(2,1)}, u32[]{:S(2)}, u32[]{:S(2)}) collective-permute-start(bf16[2,256,1536]{2,1,0:T(8,128)(2,1)} %pad_maximum_fusion.5), channel_id=1, source_target_pairs={{0,16},{4,20},{8,24},{12,28},{16,0},{20,4},{24,8},{28,12},{1,17},{... | collective-permute-start | bytes 4718600 | tf_op jit(solution)/shard_map/ppermute | solution.py:892
  584.9 86.6 %collective-permute-start.24 = (bf16[2,256,1536]{2,1,0:T(8,128)(2,1)}, bf16[2,256,1536]{2,1,0:T(8,128)(2,1)}, u32[]{:S(2)}, u32[]{:S(2)}) collective-permute-start(bf16[2,256,1536]{2,1,0:T(8,128)(2,1)} %pad_maximum_fusion.4), channel_id=1, source_target_pairs={{0,8},{4,12},{8,0},{12,4},{16,24},{20,28},{24,16},{28,20},{1,9},{5... | collective-permute-start | bytes 4718600 | tf_op jit(solution)/shard_map/ppermute | solution.py:892
  607.0 184.0 %collective-permute-start.46 = (bf16[576,1536]{1,0:T(8,128)(2,1)}, bf16[576,1536]{1,0:T(8,128)(2,1)}, u32[]{:S(2)}, u32[]{:S(2)}) collective-permute-start(bf16[576,1536]{1,0:T(8,128)(2,1)} %get-tuple-element.123), channel_id=1, source_target_pairs={{1,3},{0,1},{2,0},{3,2},{5,7},{4,5},{6,4},{7,6},{9,11},{8,9},{10,8... | collective-permute-start | bytes 5308424 | tf_op jit(solution)/shard_map/ppermute | solution.py:859
  674.4 24.8 %collective-permute-start.25 = (bf16[256,1536]{1,0:T(8,128)(2,1)S(1)}, bf16[256,1536]{1,0:T(8,128)(2,1)S(1)}, u32[]{:S(2)}, u32[]{:S(2)}) collective-permute-start(bf16[256,1536]{1,0:T(8,128)(2,1)S(1)} %get-tuple-element.182), channel_id=1, source_target_pairs={{0,16},{4,20},{8,24},{12,28},{16,0},{20,4},{24,8},{28,12},{1,17},{... | collective-permute-start | bytes 2359304 | tf_op jit(solution)/shard_map/ppermute | solution.py:892
  676.0 23.2 %collective-permute-start.27 = (bf16[256,1536]{1,0:T(8,128)(2,1)S(1)}, bf16[256,1536]{1,0:T(8,128)(2,1)S(1)}, u32[]{:S(2)}, u32[]{:S(2)}) collective-permute-start(bf16[256,1536]{1,0:T(8,128)(2,1)S(1)} %get-tuple-element.183), channel_id=1, source_target_pairs={{0,8},{4,12},{8,0},{12,4},{16,24},{20,28},{24,16},{28,20},{1,9},{5... | collective-permute-start | bytes 2359304 | tf_op jit(solution)/shard_map/ppermute | solution.py:892
  732.9 16.8 %collective-permute-start.33 = (bf16[512,512]{1,0:T(8,128)(2,1)S(1)}, bf16[512,512]{1,0:T(8,128)(2,1)S(1)}, u32[]{:S(2)}, u32[]{:S(2)}) collective-permute-start(bf16[512,512]{1,0:T(8,128)(2,1)S(1)} %convert_element_type.695), channel_id=1, source_target_pairs={{0,1},{2,3},{4,5},{6,7},{8,9},{10,11},{12,13},{14,15},{16,17},{18,... | collective-permute-start | bytes 1572872 | tf_op jit(solution)/shard_map/ppermute | solution.py:1139
  748.8 211.8 %collective-permute-start.28 = (bf16[4,512,1536]{2,1,0:T(8,128)(2,1)}, bf16[4,512,1536]{2,1,0:T(8,128)(2,1)}, u32[]{:S(2)}, u32[]{:S(2)}) collective-permute-start(bf16[4,512,1536]{2,1,0:T(8,128)(2,1)} %combine.7), channel_id=1, source_target_pairs={{0,4},{4,0},{8,12},{12,8},{16,20},{20,16},{24,28},{28,24},{1,5},{5... | collective-permute-start | bytes 18874376 | tf_op jit(solution)/shard_map/ppermute | solution.py:892
  768.5 184.2 %collective-permute-start.34 = (bf16[4,4,192,896]{3,2,1,0:T(8,128)(2,1)}, bf16[4,4,192,896]{3,2,1,0:T(8,128)(2,1)}, u32[]{:S(2)}, u32[]{:S(2)}) collective-permute-start(bf16[4,4,192,896]{3,2,1,0:T(8,128)(2,1)} %get-tuple-element.111), channel_id=1, source_target_pairs={{0,4},{4,0},{8,12},{12,8},{16,20},{20,16},{24,28},{28,24},{1,5},{5... | collective-permute-start | bytes 16515080 | tf_op jit(solution)/shard_map/ppermute | solution.py:892
  779.3 45.2 %collective-permute-start.45 = (bf16[576,1536]{1,0:T(8,128)(2,1)S(1)}, bf16[576,1536]{1,0:T(8,128)(2,1)S(1)}, u32[]{:S(2)}, u32[]{:S(2)}) collective-permute-start(bf16[576,1536]{1,0:T(8,128)(2,1)S(1)} %copy-done.16), channel_id=1, source_target_pairs={{0,3},{3,0},{4,7},{7,4},{8,11},{11,8},{12,15},{15,12},{16,19},{19,... | collective-permute-start | bytes 5308424 | tf_op jit(solution)/shard_map/ppermute | solution.py:860
  788.5 72.1 %collective-permute-start.43 = (bf16[576,1536]{1,0:T(8,128)(2,1)}, bf16[576,1536]{1,0:T(8,128)(2,1)}, u32[]{:S(2)}, u32[]{:S(2)}) collective-permute-start(bf16[576,1536]{1,0:T(8,128)(2,1)} %get-tuple-element.202), channel_id=1, source_target_pairs={{0,1},{1,2},{2,3},{4,5},{5,6},{6,7},{8,9},{9,10},{10,11},{12,13},{... | collective-permute-start | bytes 5308424 | tf_op jit(solution)/shard_map/ppermute | solution.py:872
  791.0 75.1 %collective-permute-start.44 = (bf16[576,1536]{1,0:T(8,128)(2,1)}, bf16[576,1536]{1,0:T(8,128)(2,1)}, u32[]{:S(2)}, u32[]{:S(2)}) collective-permute-start(bf16[576,1536]{1,0:T(8,128)(2,1)} %get-tuple-element.203), channel_id=1, source_target_pairs={{1,0},{2,1},{3,2},{5,4},{6,5},{7,6},{9,8},{10,9},{11,10},{13,12},{... | collective-permute-start | bytes 5308424 | tf_op jit(solution)/shard_map/ppermute | solution.py:873
  824.4 76.0 %collective-permute-start.49 = (bf16[576,1536]{1,0:T(8,128)(2,1)S(1)}, bf16[576,1536]{1,0:T(8,128)(2,1)}, u32[]{:S(2)}, u32[]{:S(2)}) collective-permute-start(bf16[576,1536]{1,0:T(8,128)(2,1)S(1)} %copy-done.17), channel_id=1, source_target_pairs={{0,3},{3,0},{4,7},{7,4},{8,11},{11,8},{12,15},{15,12},{16,19},{19,... | collective-permute-start | bytes 5308424 | tf_op jit(solution)/shard_map/ppermute | solution.py:860
  860.5 75.3 %collective-permute-start.47 = (bf16[576,1536]{1,0:T(8,128)(2,1)}, bf16[576,1536]{1,0:T(8,128)(2,1)}, u32[]{:S(2)}, u32[]{:S(2)}) collective-permute-start(bf16[576,1536]{1,0:T(8,128)(2,1)} %get-tuple-element.204), channel_id=1, source_target_pairs={{0,1},{1,2},{2,3},{4,5},{5,6},{6,7},{8,9},{9,10},{10,11},{12,13},{... | collective-permute-start | bytes 5308424 | tf_op jit(solution)/shard_map/ppermute | solution.py:872
  866.1 71.6 %collective-permute-start.48 = (bf16[576,1536]{1,0:T(8,128)(2,1)}, bf16[576,1536]{1,0:T(8,128)(2,1)}, u32[]{:S(2)}, u32[]{:S(2)}) collective-permute-start(bf16[576,1536]{1,0:T(8,128)(2,1)} %get-tuple-element.205), channel_id=1, source_target_pairs={{1,0},{2,1},{3,2},{5,4},{6,5},{7,6},{9,8},{10,9},{11,10},{13,12},{... | collective-permute-start | bytes 5308424 | tf_op jit(solution)/shard_map/ppermute | solution.py:873
  957.3 34.2 %collective-permute-start.35 = (bf16[2,2,192,896]{3,2,1,0:T(8,128)(2,1)}, bf16[2,2,192,896]{3,2,1,0:T(8,128)(2,1)}, u32[]{:S(2)}, u32[]{:S(2)}) collective-permute-start(bf16[2,2,192,896]{3,2,1,0:T(8,128)(2,1)} %pad_maximum_fusion.9), channel_id=1, source_target_pairs={{0,8},{4,12},{8,0},{12,4},{16,24},{20,28},{24,16},{28,20},{1,9},{5... | collective-permute-start | bytes 4128776 | tf_op jit(solution)/shard_map/ppermute | solution.py:892
  960.1 33.4 %collective-permute-start.37 = (bf16[2,2,192,896]{3,2,1,0:T(8,128)(2,1)}, bf16[2,2,192,896]{3,2,1,0:T(8,128)(2,1)}, u32[]{:S(2)}, u32[]{:S(2)}) collective-permute-start(bf16[2,2,192,896]{3,2,1,0:T(8,128)(2,1)} %pad_maximum_fusion.10), channel_id=1, source_target_pairs={{0,16},{4,20},{8,24},{12,28},{16,0},{20,4},{24,8},{28,12},{1,17},{... | collective-permute-start | bytes 4128776 | tf_op jit(solution)/shard_map/ppermute | solution.py:892
  964.7 148.6 %collective-permute-start.31 = (bf16[2,256,1536]{2,1,0:T(8,128)(2,1)}, bf16[2,256,1536]{2,1,0:T(8,128)(2,1)}, u32[]{:S(2)}, u32[]{:S(2)}) collective-permute-start(bf16[2,256,1536]{2,1,0:T(8,128)(2,1)} %pad_maximum_fusion.7), channel_id=1, source_target_pairs={{0,16},{4,20},{8,24},{12,28},{16,0},{20,4},{24,8},{28,12},{1,17},{... | collective-permute-start | bytes 4718600 | tf_op jit(solution)/shard_map/ppermute | solution.py:892
  967.5 145.8 %collective-permute-start.29 = (bf16[2,256,1536]{2,1,0:T(8,128)(2,1)}, bf16[2,256,1536]{2,1,0:T(8,128)(2,1)}, u32[]{:S(2)}, u32[]{:S(2)}) collective-permute-start(bf16[2,256,1536]{2,1,0:T(8,128)(2,1)} %pad_maximum_fusion.6), channel_id=1, source_target_pairs={{0,8},{4,12},{8,0},{12,4},{16,24},{20,28},{24,16},{28,20},{1,9},{5... | collective-permute-start | bytes 4718600 | tf_op jit(solution)/shard_map/ppermute | solution.py:892
  996.2 122.3 %collective-permute-start.36 = (bf16[2,192,896]{2,1,0:T(8,128)(2,1)S(1)}, bf16[2,192,896]{2,1,0:T(8,128)(2,1)S(1)}, u32[]{:S(2)}, u32[]{:S(2)}) collective-permute-start(bf16[2,192,896]{2,1,0:T(8,128)(2,1)S(1)} %get-tuple-element.191), channel_id=1, source_target_pairs={{0,16},{4,20},{8,24},{12,28},{16,0},{20,4},{24,8},{28,12},{1,17},{... | collective-permute-start | bytes 2064392 | tf_op jit(solution)/shard_map/ppermute | solution.py:892
  996.7 121.8 %collective-permute-start.38 = (bf16[2,192,896]{2,1,0:T(8,128)(2,1)S(1)}, bf16[2,192,896]{2,1,0:T(8,128)(2,1)S(1)}, u32[]{:S(2)}, u32[]{:S(2)}) collective-permute-start(bf16[2,192,896]{2,1,0:T(8,128)(2,1)S(1)} %get-tuple-element.190), channel_id=1, source_target_pairs={{0,8},{4,12},{8,0},{12,4},{16,24},{20,28},{24,16},{28,20},{1,9},{5... | collective-permute-start | bytes 2064392 | tf_op jit(solution)/shard_map/ppermute | solution.py:892
  1116.2 26.8 %collective-permute-start.30 = (bf16[256,1536]{1,0:T(8,128)(2,1)S(1)}, bf16[256,1536]{1,0:T(8,128)(2,1)S(1)}, u32[]{:S(2)}, u32[]{:S(2)}) collective-permute-start(bf16[256,1536]{1,0:T(8,128)(2,1)S(1)} %get-tuple-element.174), channel_id=1, source_target_pairs={{0,16},{4,20},{8,24},{12,28},{16,0},{20,4},{24,8},{28,12},{1,17},{... | collective-permute-start | bytes 2359304 | tf_op jit(solution)/shard_map/ppermute | solution.py:892
  1117.7 25.2 %collective-permute-start.32 = (bf16[256,1536]{1,0:T(8,128)(2,1)S(1)}, bf16[256,1536]{1,0:T(8,128)(2,1)S(1)}, u32[]{:S(2)}, u32[]{:S(2)}) collective-permute-start(bf16[256,1536]{1,0:T(8,128)(2,1)S(1)} %get-tuple-element.175), channel_id=1, source_target_pairs={{0,8},{4,12},{8,0},{12,4},{16,24},{20,28},{24,16},{28,20},{1,9},{5... | collective-permute-start | bytes 2359304 | tf_op jit(solution)/shard_map/ppermute | solution.py:892
  1121.4 18.7 %collective-permute-start.39 = (bf16[192,896]{1,0:T(8,128)(2,1)S(1)}, bf16[192,896]{1,0:T(8,128)(2,1)S(1)}, u32[]{:S(2)}, u32[]{:S(2)}) collective-permute-start(bf16[192,896]{1,0:T(8,128)(2,1)S(1)} %slice_bitcast_fusion.12), channel_id=1, source_target_pairs={{1,3},{0,1},{2,0},{3,2},{5,7},{4,5},{6,4},{7,6},{9,11},{8,9},{10,8... | collective-permute-start | bytes 1032200 | tf_op jit(solution)/shard_map/ppermute | solution.py:859
  1125.8 22.1 %collective-permute-start.42 = (bf16[192,896]{1,0:T(8,128)(2,1)S(1)}, bf16[192,896]{1,0:T(8,128)(2,1)S(1)}, u32[]{:S(2)}, u32[]{:S(2)}) collective-permute-start(bf16[192,896]{1,0:T(8,128)(2,1)S(1)} %slice_bitcast_fusion.13), channel_id=1, source_target_pairs={{0,3},{3,0},{4,7},{7,4},{8,11},{11,8},{12,15},{15,12},{16,19},{19,... | collective-permute-start | bytes 1032200 | tf_op jit(solution)/shard_map/ppermute | solution.py:860
  (44 other events, 1022.8 us)
Sparse Core Ops, SparseCore 0:
  277.3 70.5 all-gather.7
  349.7 72.1 all-gather.9
  991.6 119.9 all-reduce.3

commit v4 on v3

--- a/solution.py
+++ b/solution.py
@@ -355,68 +355,130 @@
     )(info, heads, tokens, gain, *refs)
 
 
-def dispatch_kernel(capacity, local, info, rows, grads, routes, router, *rest):
-    token_outs, grad_outs = rest[:local], rest[local : 2 * local]
-    share_outs, logits_out, earlier = rest[2 * local : 3 * local], rest[3 * local], rest[-1]
-    total = router.shape[0]
-
-    @pl.when(pl.program_id(0) == 0)
+def dispatch_kernel(capacity, local, wide, order, info, rows, grads, routes, router, *rest):
+    outs = rest[len(rest) // 2 - 1 : -2]
+    token_outs, grad_outs = outs[:local], outs[local : 2 * local]
+    share_outs, chosen_out, place_out = outs[2 * local : 3 * local], outs[-2], outs[-1]
+    onehot, logits = rest[-2:]
+    total = router.shape[1]
+    step = pl.program_id(0)
+    ids = lax.broadcasted_iota(jnp.int32, (total, TOK_DEV), 0)
+
+    def hits():
+        hit = ids == routes[0, 0:1]
+        for k in range(1, TOP):
+            hit = jnp.logical_or(hit, ids == routes[0, k : k + 1])
+        return hit
+
+    @pl.when(step == 0)
     def _():
         one = lax.broadcasted_iota(jnp.int32, (TOK_DEV, TOK_DEV), 0)
         two = lax.broadcasted_iota(jnp.int32, (TOK_DEV, TOK_DEV), 1)
-        earlier[...] = jnp.where(one < two, 1.0, 0.0).astype(LOW)
-
-    block = rows[0]
-    logits = nt(router[...], block)
-    logits_out[0] = logits
-    ids = lax.broadcasted_iota(jnp.int32, (total, TOK_DEV), 0)
-    hit = ids == routes[0, 0:1]
-    for k in range(1, TOP):
-        hit = jnp.logical_or(hit, ids == routes[0, k : k + 1])
-    weights = jnp.exp(logits - jnp.max(logits, axis=0, keepdims=True))
-    probs = weights / jnp.sum(weights, axis=0, keepdims=True)
-    share = probs / jnp.sum(jnp.where(hit, probs, 0.0), axis=0, keepdims=True)
-    hits = jnp.where(hit, 1.0, 0.0)
-    rank = nn(hits.astype(LOW), earlier[...])
-    place = jnp.where(hit, rank, -1.0)
-    spots = lax.broadcasted_iota(jnp.int32, (capacity, TOK_DEV), 0).astype(WIDE)
-    for e in range(local):
-        mine = ids == info[0] * local + e
-        place_row = jnp.sum(jnp.where(mine, place, 0.0), axis=0, keepdims=True)
-        share_row = jnp.sum(jnp.where(mine, share, 0.0), axis=0, keepdims=True)
-        chosen = spots == place_row
-        onehot = jnp.where(chosen, 1.0, 0.0).astype(LOW)
-        token_outs[e][0] = nn(onehot, block).astype(LOW)
-        grad_outs[e][0] = nn(onehot, grads[0]).astype(LOW)
-        share_outs[e][0] = jnp.sum(jnp.where(chosen, share_row, 0.0), axis=1, keepdims=True)
-
-
-def dispatch(info, rows, grads, routes, router, capacity, local):
-    count = rows.shape[0]
-    total = router.shape[0]
-    block = pl.BlockSpec((1, TOK_DEV, D), lambda i: (i, 0, 0))
-    picked = pl.BlockSpec((1, capacity, D), lambda i: (i, 0, 0))
-    shares = pl.BlockSpec((1, capacity, 1), lambda i: (i, 0, 0))
+        earlier = jnp.where(one < two, 1.0, 0.0).astype(LOW)
+        hit = hits()
+        rank = nn(jnp.where(hit, 1.0, 0.0).astype(LOW), earlier)
+        place = jnp.where(hit, rank, -1.0)
+        spots = lax.broadcasted_iota(jnp.int32, (capacity, TOK_DEV), 0).astype(WIDE)
+        place_out[0] = jnp.full(place_out.shape[1:], -1.0, WIDE)
+        for e in range(local):
+            mine = ids == info[0] * local + e
+            place_row = jnp.sum(jnp.where(mine, place, 0.0), axis=0, keepdims=True)
+            place_out[0, e : e + 1] = place_row
+            onehot[e * capacity : (e + 1) * capacity] = jnp.where(
+                spots == place_row, 1.0, 0.0
+            ).astype(LOW)
+        chosen_out[0] = onehot[...]
+        logits[...] = jnp.zeros_like(logits)
+
+    block = rows[...]
+    logits[...] += nn(block, router[...])
+    for outs_of, source in ((token_outs, block), (grad_outs, grads[0])):
+        rows_of = nn(onehot[...], source).astype(LOW)
+        for e in range(local):
+            outs_of[e][0] = rows_of[e * capacity : (e + 1) * capacity]
+
+    @pl.when(step == pl.num_programs(0) - 1)
+    def _():
+        values = logits[...].T
+        weights = jnp.exp(values - jnp.max(values, axis=0, keepdims=True))
+        share = weights / jnp.sum(jnp.where(hits(), weights, 0.0), axis=0, keepdims=True)
+        for e in range(local):
+            mine = ids == info[0] * local + e
+            share_row = jnp.sum(jnp.where(mine, share, 0.0), axis=0, keepdims=True)
+            chosen = onehot[e * capacity : (e + 1) * capacity].astype(WIDE)
+            share_outs[e][0] = jnp.sum(chosen * share_row, axis=1, keepdims=True)
+
+
+def dispatch(order, info, rows, grads, routes, router, capacity, local, earlier):
+    count = grads.shape[0]
+    total = router.shape[1]
+    wide = 512
+    picked = pl.BlockSpec((1, capacity, wide), lambda i, order, info: (order[0], 0, i))
+
+    def fixed(shape):
+        return pl.BlockSpec((1,) + shape, lambda i, order, info: (order[0], 0, 0))
+
+    out_shape = (
+        [jax.ShapeDtypeStruct((count, capacity, D), LOW)] * (2 * local)
+        + [jax.ShapeDtypeStruct((count, capacity, 1), WIDE)] * local
+        + [
+            jax.ShapeDtypeStruct((count, local * capacity, TOK_DEV), LOW),
+            jax.ShapeDtypeStruct((count, 8, TOK_DEV), WIDE),
+        ]
+    )
+    if earlier is None:
+        earlier = [jnp.zeros((8, 128), shape.dtype) for shape in out_shape]
+        aliases = {}
+    else:
+        aliases = {6 + i: i for i in range(len(out_shape))}
     return pl.pallas_call(
-        functools.partial(dispatch_kernel, capacity, local),
-        grid=(count,),
-        out_shape=[jax.ShapeDtypeStruct((count, capacity, D), LOW)] * (2 * local)
-        + [jax.ShapeDtypeStruct((count, capacity, 1), WIDE)] * local
-        + [jax.ShapeDtypeStruct((count, total, TOK_DEV), WIDE)],
-        in_specs=[
-            SMEM,
-            block,
-            block,
-            pl.BlockSpec((1, TOP, TOK_DEV), lambda i: (i, 0, 0)),
-            whole((total, D)),
-        ],
-        out_specs=[picked] * (2 * local)
-        + [shares] * local
-        + [pl.BlockSpec((1, total, TOK_DEV), lambda i: (i, 0, 0))],
-        scratch_shapes=[pltpu.VMEM((TOK_DEV, TOK_DEV), LOW)],
+        functools.partial(dispatch_kernel, capacity, local, wide),
+        grid_spec=pltpu.PrefetchScalarGridSpec(
+            num_scalar_prefetch=2,
+            grid=(D // wide,),
+            in_specs=[
+                pl.BlockSpec((TOK_DEV, wide), lambda i, order, info: (0, i)),
+                pl.BlockSpec((1, TOK_DEV, wide), lambda i, order, info: (order[1], 0, i)),
+                pl.BlockSpec((1, TOP, TOK_DEV), lambda i, order, info: (order[1], 0, 0)),
+                pl.BlockSpec((wide, total), lambda i, order, info: (i, 0)),
+            ]
+            + [ANY] * len(out_shape),
+            out_specs=[picked] * (2 * local)
+            + [fixed((capacity, 1))] * local
+            + [fixed((local * capacity, TOK_DEV)), fixed((8, TOK_DEV))],
+            scratch_shapes=[
+                pltpu.VMEM((local * capacity, TOK_DEV), LOW),
+                pltpu.VMEM((TOK_DEV, total), WIDE),
+            ],
+        ),
+        out_shape=out_shape,
+        input_output_aliases=aliases,
         compiler_params=params(),
         name="dispatch",
-    )(info, rows, grads, routes, router)
+    )(order, info, rows, grads, routes, router, *earlier)
+
+
+def spread_kernel(local, place, *rest):
+    dots, out = rest[:local], rest[local]
+    spots = lax.broadcasted_iota(jnp.int32, (dots[0].shape[1], TOK_DEV), 0).astype(WIDE)
+    for e in range(local):
+        chosen = spots == place[0, e : e + 1]
+        out[0, e : e + 1] = jnp.sum(jnp.where(chosen, dots[e][0], 0.0), axis=0, keepdims=True)
+
+
+def spread(place, dots):
+    count, capacity, _ = dots[0].shape
+    local = len(dots)
+    return pl.pallas_call(
+        functools.partial(spread_kernel, local),
+        grid=(count,),
+        out_shape=jax.ShapeDtypeStruct((count, local, TOK_DEV), WIDE),
+        in_specs=[pl.BlockSpec((1, 8, TOK_DEV), lambda i: (i, 0, 0))]
+        + [pl.BlockSpec((1, capacity, 1), lambda i: (i, 0, 0))] * local,
+        out_specs=pl.BlockSpec((1, local, TOK_DEV), lambda i: (i, 0, 0)),
+        compiler_params=params(),
+        name="spread",
+    )(place, *dots)
 
 
 def expert_kernel(slots, info, rows, grads, shares, *rest):
@@ -539,49 +601,27 @@
     )(rows, grads, *[acts] * len(slots))
 
 
-def combine_kernel(capacity, local, total, order, info, routes, *rest):
-    rows, out, earlier = rest[:local], rest[local], rest[local + 1]
-
-    @pl.when(pl.program_id(0) == 0)
-    def _():
-        one = lax.broadcasted_iota(jnp.int32, (TOK_DEV, TOK_DEV), 0)
-        two = lax.broadcasted_iota(jnp.int32, (TOK_DEV, TOK_DEV), 1)
-        earlier[...] = jnp.where(two < one, 1.0, 0.0).astype(LOW)
-
-    ids = lax.broadcasted_iota(jnp.int32, (TOK_DEV, total), 1)
-    hit = ids == routes[0, :, 0:1]
-    for k in range(1, TOP):
-        hit = jnp.logical_or(hit, ids == routes[0, :, k : k + 1])
-    hits = jnp.where(hit, 1.0, 0.0)
-    place = jnp.where(hit, nn(earlier[...], hits.astype(LOW)), -1.0)
-    spots = lax.broadcasted_iota(jnp.int32, (TOK_DEV, capacity), 1).astype(WIDE)
-    summed = None
-    for e in range(local):
-        mine = ids == info[0] * local + e
-        place_col = jnp.sum(jnp.where(mine, place, 0.0), axis=1, keepdims=True)
-        onehot = jnp.where(spots == place_col, 1.0, 0.0).astype(LOW)
-        term = nn(onehot, rows[e][0])
-        summed = term if summed is None else summed + term
-    out[0] = summed.astype(LOW)
-
-
-def combine(order, info, routes, rows, total):
-    count, capacity = rows[0].shape[0], rows[0].shape[1]
-    named = pl.BlockSpec((1, capacity, D), lambda i, order, info: (order[i], 0, 0))
+def combine_kernel(local, chosen, *rest):
+    rows, out = rest[:local], rest[local]
+    both = jnp.concatenate([ref[0] for ref in rows], axis=0)
+    out[0] = tn(chosen[0], both).astype(LOW)
+
+
+def combine(chosen, rows, first, step):
+    count, capacity, _ = rows[0].shape
+    number = (count - first + step - 1) // step
     return pl.pallas_call(
-        functools.partial(combine_kernel, capacity, len(rows), total),
-        grid_spec=pltpu.PrefetchScalarGridSpec(
-            num_scalar_prefetch=2,
-            grid=(order.shape[0],),
-            in_specs=[pl.BlockSpec((1, TOK_DEV, TOP), lambda i, order, info: (order[i], 0, 0))]
-            + [named] * len(rows),
-            out_specs=pl.BlockSpec((1, TOK_DEV, D), lambda i, order, info: (i, 0, 0)),
-            scratch_shapes=[pltpu.VMEM((TOK_DEV, TOK_DEV), LOW)],
-        ),
-        out_shape=jax.ShapeDtypeStruct((order.shape[0], TOK_DEV, D), LOW),
+        functools.partial(combine_kernel, len(rows)),
+        grid=(number,),
+        out_shape=jax.ShapeDtypeStruct((number, TOK_DEV, D), LOW),
+        in_specs=[
+            pl.BlockSpec((1,) + chosen.shape[1:], lambda i: (first + step * i, 0, 0))
+        ]
+        + [pl.BlockSpec((1, capacity, D), lambda i: (first + step * i, 0, 0))] * len(rows),
+        out_specs=pl.BlockSpec((1, TOK_DEV, D), lambda i: (i, 0, 0)),
         compiler_params=params(),
         name="combine",
-    )(order, info, routes, *rows)
+    )(chosen, *rows)
 
 
 def split(values):
@@ -598,20 +638,43 @@
     return grad_values, grad_gain
 
 
+def router_back(logits, routes, grad_shares):
+    ids = lax.broadcasted_iota(jnp.int32, logits.shape, 0)
+    hit = ids == routes[0:1]
+    for k in range(1, TOP):
+        hit = jnp.logical_or(hit, ids == routes[k : k + 1])
+    weights = jnp.exp(logits - jnp.max(logits, axis=0, keepdims=True))
+    probs = weights / jnp.sum(weights, axis=0, keepdims=True)
+    chosen = jnp.sum(jnp.where(hit, probs, 0.0), axis=0, keepdims=True)
+    grads = jnp.where(hit, grad_shares, 0.0)
+    mean = jnp.sum(probs * grads, axis=0, keepdims=True) / chosen
+    grad_probs = jnp.where(hit, (grads - mean) / chosen, 0.0)
+    return probs * (grad_probs - jnp.sum(probs * grad_probs, axis=0, keepdims=True))
+
+
 def branch_back_kernel(
-    info, residual, normed, sums, cotangent, grad_logits, router, gain, *rest
+    parts, info, residual, normed, cotangent, routes, grad_shares, router, gain, *rest
 ):
+    sums, rest = rest[:parts], rest[parts:]
     count = len(rest) - 7
     refs = rest[:count]
     grad_residual, grad_branch, grad_heads, grad_gain, grad_router, weight, sem = rest[count:]
-    copies = weight_copies(info, refs, weight, sem, D // QUARTERS + 128, D // QUARTERS)
 
     @pl.when(pl.program_id(0) == 0)
     def _():
+        copies = weight_copies(info, refs, weight, sem, D // QUARTERS + 128, D // QUARTERS)
         run_all(copies)
-        high, low = split(grad_logits[...])
+        logits = nt(router[...], normed[...])
+        high, low = split(router_back(logits, routes[...], grad_shares[...]))
         grad_router[...] = nn(high, normed[...]) + nn(low, normed[...])
-        grad_normed = sums[...] + tn(high, router[...]) + tn(low, router[...])
+        grad_normed = tn(high, router[...]) + tn(low, router[...])
+        if parts == 1:
+            grad_normed += sums[0][...]
+        else:
+            values = [ref[...].astype(WIDE) for ref in sums]
+            grad_normed += jnp.concatenate(
+                [values[0] + values[1] + values[2], values[3] + values[4] + values[5]], axis=0
+            )
         grad_values, gain_grad = norm_back(residual[...], gain[...], grad_normed)
         grad_gain[...] = gain_grad
         total = cotangent[...].astype(WIDE) + grad_values
@@ -623,11 +686,11 @@
     grad_heads[...] = nt(grad_branch[...], weight[at, :]).astype(LOW)
 
 
-def branch_back(info, residual, normed, sums, cotangent, grad_logits, router, gain, refs):
+def branch_back(info, residual, normed, sums, cotangent, routes, grad_shares, router, gain, refs):
     full = (TOK_DEV, D)
     total = router.shape[0]
     return pl.pallas_call(
-        branch_back_kernel,
+        functools.partial(branch_back_kernel, len(sums)),
         grid=(D // 256,),
         out_shape=(
             jax.ShapeDtypeStruct(full, WIDE),
@@ -637,8 +700,9 @@
             jax.ShapeDtypeStruct((total, D), WIDE),
         ),
         in_specs=[SMEM]
-        + [whole(full)] * 4
-        + [whole((total, TOK_DEV)), whole((total, D)), whole((1, D))]
+        + [whole(full)] * 3
+        + [whole((TOP, TOK_DEV)), whole((total, TOK_DEV)), whole((total, D)), whole((1, D))]
+        + [whole(part.shape) for part in sums]
         + [ANY] * len(refs),
         out_specs=(
             whole(full),
@@ -650,7 +714,7 @@
         scratch_shapes=[pltpu.VMEM((D, D), LOW), pltpu.SemaphoreType.DMA],
         compiler_params=params(),
         name="experts_norm_back",
-    )(info, residual, normed, sums, cotangent, grad_logits, router, gain, *refs)
+    )(info, residual, normed, cotangent, routes, grad_shares, router, gain, *sums, *refs)
 
 
 def join_grads_kernel(info, own_grad, source_grad, arrived, cosine, sine, out):
@@ -909,8 +973,14 @@
     near_y = sums((0, 1), two)
     got_xy = flip(add_low(near_x[1], got_x[1]), 4)
     got_yx = flip(add_low(near_y[1], got_y[1]), 2)
-    wide = [a.astype(WIDE) for a in (near_x[0], got_x[0], got_xy, near_y[0], got_y[0], got_yx)]
-    return wide[0] + wide[1] + wide[2], wide[3] + wide[4] + wide[5]
+    return (near_x[0], got_x[0], got_xy, near_y[0], got_y[0], got_yx)
+
+
+def sum_parts(parts):
+    wide = [a.astype(WIDE) for a in parts]
+    if len(wide) == 1:
+        return wide[0]
+    return jnp.concatenate([wide[0] + wide[1] + wide[2], wide[3] + wide[4] + wide[5]], axis=0)
 
 
 def on_device(
@@ -956,7 +1026,10 @@
     ).astype(jnp.int32)
 
     small = jnp.concatenate([attention_gain, experts_gain, router_weight.reshape(-1)])
-    small_all = lax.all_gather(small, ("rows", "cols"), axis=0)
+    small = jnp.pad(small, (0, 2048 - small.shape[0])).reshape(16, 128)
+    small_all = lax.all_gather(lax.all_gather(small, "cols", axis=0), "rows", axis=0)
+    small_all = small_all.reshape(row_count * col_count, -1)
+    small_all = small_all[:, : 2 * gain_part + depth * router_part]
     attention_scale = small_all[:, :gain_part].reshape(1, D).astype(WIDE)
     experts_scale = small_all[:, gain_part : 2 * gain_part].reshape(1, D).astype(WIDE)
     router_rows = jnp.transpose(
@@ -987,7 +1060,6 @@
         beside, across = flip(own, 2), flip(own, 4)
         corner = [flip(beside[:2], 4), flip(across[2:], 2)]
         same = [own, beside, across] + corner
-        same = [after(piece, firsts[0][0], firsts[0][1]) for piece in same]
         pieces = same + [flip(piece, 1) for piece in same]
         query_refs = pair_refs = out_refs = pieces
         expert_refs = [
@@ -1018,36 +1090,49 @@
         ]
 
     routes_all = lax.all_gather(routes.T, "rows", axis=0)
-    grad_all = lax.all_gather(cotangent, "rows", axis=0)
+    grad_in = after(cotangent, *pieces) if fast else cotangent
+    grad_all = lax.all_gather(grad_in, "rows", axis=0)
 
     local_index = (1 - parity) * TOK_DEV + jnp.arange(TOK_DEV, dtype=jnp.int32)
     cosine, sine = rotary_tables(position_of(local_index))
     normed, own_pair = key_value(info, tokens, attention_scale, cosine, sine, pair_refs)
     pairs = [(i + 1, i) for i in range(0, col_count, 2)]
     partner = lax.ppermute(own_pair, "cols", pairs)
+    queries = query(info, normed, cosine, sine, query_refs)
     if fast:
-        normed_query = after(normed, firsts[0][2])
+        queries = after(queries, *firsts[0])
+    heads = attention(info, queries, own_pair, partner)
+    residual, normed_two = out_projection(info, heads, tokens, experts_scale, out_refs)
+
+    if fast:
+        grad_all = after(grad_all, normed_two)
+        beside, across = flip(normed_two, 2), flip(normed_two, 4)
+        half = TOK_DEV // 2
+        corner = jnp.concatenate([flip(beside[:half], 4), flip(across[half:], 2)], axis=0)
+        near = [normed_two, beside, across, corner]
+        blocks = [block for one in near for block in (one, flip(one, 1))]
+        turns = [0, 1, 2, 3, 4, 5, 6, 7]
+        places = [row_place ^ q for q in range(row_count)]
     else:
-        normed_query = normed
-    queries = query(info, normed_query, cosine, sine, query_refs)
-    if fast:
-        queries = after(queries, seconds[0])
-    heads = attention(info, queries, own_pair, partner)
-    if fast:
-        heads = after(heads, firsts[1][0], firsts[1][1])
-    residual, normed_two = out_projection(info, heads, tokens, experts_scale, out_refs)
-    rows_all = lax.all_gather(normed_two, "rows", axis=0)
-    if fast:
-        rows_all = after(rows_all, firsts[1][2])
-
-    picked = dispatch(
-        info, rows_all, grad_all, routes_all, router_rows, capacity, local_experts
-    )
+        rows_all = lax.all_gather(normed_two, "rows", axis=0)
+        blocks = [rows_all[q] for q in range(row_count)]
+        turns = list(range(row_count))
+        places = turns
+    router_cols = router_rows.T
+    picked = None
+    for q in turns:
+        order = jnp.stack([jnp.int32(q), jnp.asarray(places[q], jnp.int32)])
+        block = blocks[q]
+        if fast and q == 4:
+            block = after(block, *firsts[1])
+        picked = dispatch(
+            order, info, block, grad_all, routes_all, router_cols, capacity, local_experts, picked
+        )
     height = row_count * capacity
     token_rows = [a.reshape(height, D) for a in picked[:local_experts]]
     grad_rows = [a.reshape(height, D) for a in picked[local_experts : 2 * local_experts]]
     share_rows = [a.reshape(height, 1) for a in picked[2 * local_experts : 3 * local_experts]]
-    logits = lax.dynamic_index_in_dim(picked[-1], row_place, 0, keepdims=False)
+    chosen, place_rows = picked[-2:]
 
     out_rows, back_rows, gate_dots, reduced, marks = ([], [], [], [], [])
     for e in range(local_experts):
@@ -1055,14 +1140,16 @@
         if fast and e == 0:
             rows_in = after(rows_in, seconds[0])
         if fast and e == 1:
-            rows_in = after(rows_in, seconds[1], *marks[0])
+            rows_in = after(rows_in, seconds[1])
         out_row, back_row, grad_row, acts, dots = expert(
             info, rows_in, grad_rows[e], share_rows[e], expert_refs[e], col_count
         )
         out_rows.append(out_row.reshape(row_count, capacity, D))
         back_rows.append(back_row.reshape(row_count, capacity, D))
-        gate_dots.append(dots.reshape(row_count, capacity))
+        gate_dots.append(dots.reshape(row_count, capacity, 1))
         if fast:
+            if e == 1:
+                acts = after(acts, *marks[0])
             second, fourth = expert_grads(acts, token_rows[e], grad_row, (1, 3))
             sent_first = reduce_first(second, fourth)
             marks.append([sent_first[0]])
@@ -1075,64 +1162,47 @@
                 lax.psum_scatter(jnp.stack(slots), "cols", scatter_dimension=0).astype(WIDE)
             )
 
-    routes_cols = jnp.swapaxes(routes_all, 1, 2)
+    spread_dots = spread(place_rows, gate_dots)
     if fast:
-        chips = jnp.arange(4, dtype=jnp.int32) * 2
-        keep_order, send_order = (chips ^ row_place, (chips + 1) ^ row_place)
+        spread_dots = jnp.take(
+            spread_dots, row_place ^ jnp.arange(row_count, dtype=jnp.int32), axis=0
+        )
+    grad_shares = lax.all_to_all(spread_dots, "rows", split_axis=0, concat_axis=0, tiled=True)
+    grad_shares = grad_shares.reshape(expert_total, TOK_DEV)
+    if fast:
+        back_rows = [after(a, *reduced[1][0:1]) for a in back_rows]
 
         def both_ways(rows):
-            got = flip(combine(send_order, info, routes_cols, rows, expert_total), 1)
-            keep = combine(keep_order, info, routes_cols, rows, expert_total)
-            return reduce_chips(keep, got)
-
-        back_sum = jnp.concatenate(both_ways(back_rows), axis=0)
-        out_rows = [after(a, back_sum) for a in out_rows]
-        mixture = jnp.concatenate(both_ways(out_rows), axis=0)
+            got = flip(combine(chosen, rows, 1, 2), 1)
+            return reduce_chips(combine(chosen, rows, 0, 2), got)
+
+        back_parts = both_ways(back_rows)
+        out_rows = [after(a, *back_parts) for a in out_rows]
+        mixture = both_ways(out_rows)
+        grad_shares = after(grad_shares, reduced[0][1][1], *reduced[0][2])
     else:
-        order = jnp.arange(row_count, dtype=jnp.int32)
 
         def summed(rows):
-            part = combine(order, info, routes_cols, rows, expert_total)
-            return lax.psum_scatter(part, "rows", scatter_dimension=0).astype(WIDE)
-
-        back_sum = summed(back_rows)
+            part = combine(chosen, rows, 0, 1)
+            return (lax.psum_scatter(part, "rows", scatter_dimension=0).astype(WIDE),)
+
+        back_parts = summed(back_rows)
         mixture = summed(out_rows)
-    layer_output = (residual + mixture).astype(LOW)
-
-    ids = jnp.arange(expert_total, dtype=jnp.int32)
-    named = routes_all[:, :, None, :] == ids[None, None, :, None]
-    hit = jnp.any(named, axis=1)
-    rank = jnp.cumsum(hit.astype(jnp.int32), axis=2) - 1
-    own_at = row_place * local_experts
-    own_hit = lax.dynamic_slice_in_dim(hit, own_at, local_experts, 1)
-    own_rank = lax.dynamic_slice_in_dim(rank, own_at, local_experts, 1)
-    dots = jnp.stack(gate_dots, axis=1)
-    grad_share = jnp.where(
-        own_hit, jnp.take_along_axis(dots, jnp.clip(own_rank, 0, capacity - 1), axis=2), 0.0
-    )
-    grad_share_all = lax.all_gather(grad_share, "rows", axis=1, tiled=True)
-    grad_shares = lax.dynamic_index_in_dim(grad_share_all, row_place, 0, keepdims=False)
-    chosen_of = lax.dynamic_index_in_dim(hit, row_place, 0, keepdims=False)
-
-    def shares_out(logit_cols):
-        softmax_out = jax.nn.softmax(logit_cols, axis=0)
-        chosen = jnp.where(chosen_of, softmax_out, 0.0)
-        return chosen / jnp.sum(chosen, axis=0, keepdims=True)
-
-    _, router_pullback = jax.vjp(shares_out, logits)
-    (grad_logits,) = router_pullback(grad_shares)
 
     grad_residual, grad_branch, grad_heads, experts_gain_grad, router_grad = branch_back(
         info,
         residual,
         normed_two,
-        back_sum,
+        back_parts,
         cotangent,
-        grad_logits,
+        routes.T,
+        grad_shares,
         router_rows,
         experts_scale,
         out_refs,
     )
+    if fast:
+        grad_heads = after(grad_heads, reduced[1][1][0])
     grad_query, own_grad, source_grad = attention_back(
         info, queries, own_pair, partner, grad_heads, cosine, sine
     )
@@ -1142,10 +1212,10 @@
         info, grad_query, grad_pair, tokens, grad_residual, attention_scale, query_refs, pair_refs
     )
 
+    layer_output = (residual + sum_parts(mixture)).astype(LOW)
     if fast:
         keep, send = weight_grads(info, normed, heads, grad_query, grad_pair, grad_branch)
-        first_half, second_half = reduce_chips(keep, flip(send, 1))
-        slots = [a.astype(LOW) for a in (*first_half, *second_half)]
+        slots = sum_parts(reduce_chips(keep, flip(send, 1))).astype(LOW)
         sent_first = reduce_first(slots[1], slots[3])
         sent_second = reduce_second(slots[2], slots[3], sent_first[0])
         sums = reduce_last(slots[0], sent_first, sent_second)
@@ -1177,7 +1247,11 @@
         ],
         axis=1,
     )
-    small_sums = lax.psum_scatter(small_grads, ("rows", "cols"), scatter_dimension=0)
+    small_grads = small_grads.reshape(row_count, -1)
+    small_grads = lax.all_to_all(small_grads, "rows", split_axis=0, concat_axis=0, tiled=True)
+    small_grads = jnp.sum(small_grads, axis=0).reshape(col_count, -1)
+    small_grads = lax.all_to_all(small_grads, "cols", split_axis=0, concat_axis=0, tiled=True)
+    small_sums = jnp.sum(small_grads, axis=0)
 
     key_at = query_part
     value_at = key_at + key_part

time: 1170 us -> 932 us (0.80)
  waiting for transfers between devices: 485 us -> 267 us
  local copies, waits for them, and re-layouts: 95.1 us -> 60.7 us
  Pallas kernels: 261 us -> 285 us
  starting transfers between devices: 94.3 us -> 116 us
  other arithmetic: 87.3 us -> 68.3 us
    unnamed x4 -> x1, waiting for transfers between devices: 113 us -> 0.02 us
    all_gather x2 -> x1, waiting for transfers between devices: 98.4 us -> 0.01 us  [on_device(): grad_all = lax.all_gather(grad_in, 'rows', axis=0)]
    unnamed x1 -> x0, blocking collectives: 90.3 us -> none
    all_gather x1 -> x2, blocking collectives: 21.8 us -> 89.1 us  [the longest x1 79.9 us: on_device(): lax.all_gather(small, 'cols', axis=0)]
    ppermute x24 -> x32, waiting for transfers between devices: 34.7 us -> 102 us  [flip(): return lax.ppermute(block, 'rows', [(i, i ^ bit) for i in range(count)])]
    gather x2 -> x1, local copies, waits for them, and re-layouts: 63.1 us -> 1.94 us  [on_device(): jnp.take(spread_dots, row_place ^ jnp.arange(row_count, dtype=jnp.int32),...]
    ppermute x3, waiting for transfers between devices: 58.1 us -> 8.44 us  [send_first(): lax.ppermute(block, 'cols', FAR)]
    ppermute x3, waiting for transfers between devices: 48.1 us -> 13.4 us  [reduce_first(): lax.ppermute(second, 'cols', [(1, 3), (0, 1), (2, 0), (3, 2)])]
  transfers between devices with their start and end apart: 53 -> 61, of which waited for: 26 -> 27; matrix products, arithmetic and copies ran while one was open for 14% -> 12% of each run, Pallas kernels for 18% -> 27%
where the time goes in v4:
time: 932 us; the launch traced here: 925 us
  Pallas kernels  285 us (31%)
  waiting for transfers between devices  267 us (29%)
  starting transfers between devices  116 us (12%)
  blocking collectives  112 us (12%)
  other arithmetic  68.3 us (7%)
  local copies, waits for them, and re-layouts  60.7 us (7%)
  between operations  15.3 us (2%)
    ppermute x32, waiting for transfers between devices, flip(): return lax.ppermute(block, 'rows', [(i, i ^ bit) for i in range(count)])  102 us
    all_gather x1, blocking collectives, on_device(): lax.all_gather(small, 'cols', axis=0)  79.9 us
    pallas_call x2, Pallas kernels, expert(): pl.pallas_call(functools.partial(expert_kernel, slots), grid=(height // E...  60.3 us
    ppermute x3, waiting for transfers between devices, reduce_second(): lax.ppermute(upward_load, 'cols', UP)  55.8 us
    pallas_call x8, Pallas kernels, dispatch(): pl.pallas_call(functools.partial(dispatch_kernel, capacity, local, wide),...  50.7 us
    pallas_call x4, Pallas kernels, expert_grads(): pl.pallas_call(functools.partial(expert_grads_kernel, slots), grid=(D //...  42.5 us
    ppermute x3, waiting for transfers between devices, reduce_first(): lax.ppermute(fourth, 'cols', FAR)  32 us
    all_to_all x1, waiting for transfers between devices, on_device(): lax.all_to_all(small_grads, 'rows', split_axis=0, concat_axis=0, tiled=True)  31.3 us
  transfers between devices with their start and end apart: 61, of which 27 were waited for; matrix products, arithmetic and copies ran while one was open for 12% of the time, Pallas kernels for 27%

profile of v4, /device:TPU:0, one launch (start us, length us, event | category | flops | bytes accessed | tf_op | source)
XLA Modules:
  0.0 924.9 jit_solution(11436031509216359996)
XLA Ops:
  11.5 5.6 collective-permute-start.1
  25.5 7.2 collective-permute-done.3
  36.8 6.2 collective-permute-done.2
  46.2 27.1 %collective-permute-done.4.rest_1_.rest_7_.rest_11_ = bf16[4,192,896]{2,1,0:T(8,128)(2,1)S(1)} collective-permute-done((bf16[4,192,896]{2,1,0:T(8,128)(2,1)S(1)}, bf16[4,192,896]{2,1,0:T(8,128)(2,1)S(1)}, u32[]{:S(2)}, u32[]{:S(2)}) %collective-permute-start.4) | collective-permute-done | bytes 1376288 | tf_op jit(solution)/shard_map/ppermute | solution.py:956
  77.1 12.2 %collective-permute-done.6.rest_3_.rest_9_.rest_13_ = bf16[2,192,896]{2,1,0:T(8,128)(2,1)S(1)} collective-permute-done((bf16[2,192,896]{2,1,0:T(8,128)(2,1)S(1)}, bf16[2,192,896]{2,1,0:T(8,128)(2,1)S(1)}, u32[]{:S(2)}, u32[]{:S(2)}) %collective-permute-start.6) | collective-permute-done | bytes 688160 | tf_op jit(solution)/shard_map/ppermute | solution.py:956
  108.4 79.9 %all_gather.21 = bf16[4,16,128]{2,1,0:T(8,128)(2,1)S(1)} all-gather(bf16[1,16,128]{2,1,0:T(8,128)(2,1)S(1)} %fusion.36), channel_id=1, replica_groups=mesh['rows'=8,'cols'=4] {'cols'}, dimensions={0}, use_global_device_ids=true | all-gather | bytes 20480 | tf_op jit(solution)/shard_map/all_gather | solution.py:1030
  188.2 9.2 all-gather
  213.6 8.8 query_projection.1.queries
  228.0 11.0 %tree_attention.1.heads = bf16[512,1536]{1,0:T(8,128)(2,1)} custom-call(s32[16]{0:T(128)} %concatenate.32.info, bf16[512,1536]{1,0:T(8,128)(2,1)} %query_projection.1.queries, bf16[512,512]{1,0:T(8,128)(2,1)} %get-tuple-element.128.own, bf16[512,512]{1,0:T(8,128)(2,1)} %collective-permute-done.16.partner), custom_call_target="tpu_custom_call" | custom-call | tf_op jit(solution)/shard_map/tree_attention/pallas_call | solution.py:236
  238.9 10.9 %out_projection.1 = (f32[512,1536]{1,0:T(8,128)}, bf16[512,1536]{1,0:T(8,128)(2,1)}) custom-call(s32[16]{0:T(128)} %concatenate.32.info, bf16[512,1536]{1,0:T(8,128)(2,1)} %tree_attention.1.heads, bf16[512,1536]{1,0:T(8,128)(2,1)} %tokens.5, f32[1,1536]{1,0:T(1,128)} %reshape.366.gain, bf16[4,192,896]{2,1,0:T(8,128)(2,1)} %copy-done, ...), custom_call_target="tpu_custom_call" | custom-call | tf_op jit(solution)/shard_map/out_projection/pallas_call | solution.py:346
  253.3 5.8 collective-permute-start.24
  261.4 24.5 %collective-permute-done.17.rows = bf16[512,1536]{1,0:T(8,128)(2,1)S(1)} collective-permute-done((bf16[512,1536]{1,0:T(8,128)(2,1)}, bf16[512,1536]{1,0:T(8,128)(2,1)S(1)}, u32[]{:S(2)}, u32[]{:S(2)}) %collective-permute-start.17) | collective-permute-done | bytes 1572896 | tf_op jit(solution)/shard_map/ppermute | solution.py:956
  300.9 10.2 %all-gather.3.routes = s32[8,4,512]{2,1,0:T(4,128)} all-gather(s32[1,4,512]{2,1,0:T(4,128)S(1)} %bitcast.172), channel_id=4, replica_groups=mesh['rows'=8,'cols'=4] {'rows'}, dimensions={0}, use_global_device_ids=true | all-gather | bytes 73728 | tf_op jit(solution)/shard_map/all_gather | solution.py:1092
  320.3 11.7 %collective-permute-done.20 = bf16[256,1536]{1,0:T(8,128)(2,1)S(1)} collective-permute-done((bf16[256,1536]{1,0:T(8,128)(2,1)S(1)}, bf16[256,1536]{1,0:T(8,128)(2,1)S(1)}, u32[]{:S(2)}, u32[]{:S(2)}) %collective-permute-start.20) | collective-permute-done | bytes 786464 | tf_op jit(solution)/shard_map/ppermute | solution.py:956
  342.5 6.4 dispatch.8
  351.3 6.3 dispatch.9
  357.6 6.3 dispatch.10
  364.0 6.3 dispatch.11
  370.3 6.3 dispatch.12
  376.6 6.4 dispatch.13
  383.0 6.3 dispatch.14
  389.4 6.3 dispatch.15
  395.7 30.2 %expert.2 = (bf16[1280,1536]{1,0:T(8,128)(2,1)}, bf16[1280,1536]{1,0:T(8,128)(2,1)}, bf16[1280,1536]{1,0:T(8,128)(2,1)}, bf16[4,576,1280]{2,1,0:T(8,128)(2,1)}, f32[1280,1]{1,0:T(8,128)}) custom-call(s32[16]{0:T(128)} %concatenate.32.info, bf16[1280,1536]{1,0:T(8,128)(2,1)} %bitcast.142, bf16[1280,1536]{1,0:T(8,128)(2,1)} %bitcast.148, f32[1280,1]{1,0:T(8,128)} %bitcast.150, ...), custom_call_target="tpu_custom_call" | custom-call | tf_op jit(solution)/shard_map/expert/pallas_call | solution.py:564
  425.8 10.7 %expert_gradients.4 = (bf16[576,1536]{1,0:T(8,128)(2,1)}, bf16[576,1536]{1,0:T(8,128)(2,1)}) custom-call(bf16[1280,1536]{1,0:T(8,128)(2,1)} %bitcast.143, bf16[1280,1536]{1,0:T(8,128)(2,1)} %get-tuple-element.204.grads, bf16[4,576,1280]{2,1,0:T(8,128)(2,1)} %get-tuple-element.205.rest_0_.rest_1_, bf16[4,576,1280]{2,1,0:T(8,128)(2,1)} %get-tuple-element.205.rest_0_.rest_1_), custom_call_target="tpu_custom_call" | custom-call | tf_op jit(solution)/shard_map/expert_gradients/pallas_call | solution.py:592
  436.5 7.7 collective-permute-start.30
  445.5 30.2 %expert.3 = (bf16[1280,1536]{1,0:T(8,128)(2,1)}, bf16[1280,1536]{1,0:T(8,128)(2,1)}, bf16[1280,1536]{1,0:T(8,128)(2,1)}, bf16[4,576,1280]{2,1,0:T(8,128)(2,1)}, f32[1280,1]{1,0:T(8,128)}) custom-call(s32[16]{0:T(128)} %concatenate.32.info, bf16[1280,1536]{1,0:T(8,128)(2,1)} %bitcast.145, bf16[1280,1536]{1,0:T(8,128)(2,1)} %bitcast.149, f32[1280,1]{1,0:T(8,128)} %bitcast.151, ...), custom_call_target="tpu_custom_call" | custom-call | tf_op jit(solution)/shard_map/expert/pallas_call | solution.py:564
  475.7 10.5 %collective-permute-done.30 = bf16[576,1536]{1,0:T(8,128)(2,1)S(1)} collective-permute-done((bf16[576,1536]{1,0:T(8,128)(2,1)}, bf16[576,1536]{1,0:T(8,128)(2,1)S(1)}, u32[]{:S(2)}, u32[]{:S(2)}) %collective-permute-start.30) | collective-permute-done | bytes 1769504 | tf_op jit(solution)/shard_map/ppermute | solution.py:923
  486.2 10.6 %expert_gradients.5 = (bf16[576,1536]{1,0:T(8,128)(2,1)}, bf16[576,1536]{1,0:T(8,128)(2,1)}) custom-call(bf16[1280,1536]{1,0:T(8,128)(2,1)} %bitcast.146, bf16[1280,1536]{1,0:T(8,128)(2,1)} %get-tuple-element.202.grads, bf16[4,576,1280]{2,1,0:T(8,128)(2,1)} %get-tuple-element.207.rest_0_.rest_1_, bf16[4,576,1280]{2,1,0:T(8,128)(2,1)} %get-tuple-element.207.rest_0_.rest_1_), custom_call_target="tpu_custom_call" | custom-call | tf_op jit(solution)/shard_map/expert_gradients/pallas_call | solution.py:592
  496.8 7.5 combine.5
  504.3 10.6 %expert_gradients.6 = (bf16[576,1536]{1,0:T(8,128)(2,1)}, bf16[576,1536]{1,0:T(8,128)(2,1)}) custom-call(bf16[1280,1536]{1,0:T(8,128)(2,1)} %bitcast.144, bf16[1280,1536]{1,0:T(8,128)(2,1)} %get-tuple-element.204.grads, bf16[4,576,1280]{2,1,0:T(8,128)(2,1)} %get-tuple-element.205.rest_0_.rest_1_, bf16[4,576,1280]{2,1,0:T(8,128)(2,1)} %get-tuple-element.205.rest_0_.rest_1_), custom_call_target="tpu_custom_call" | custom-call | tf_op jit(solution)/shard_map/expert_gradients/pallas_call | solution.py:592
  519.3 7.5 combine.4
  541.1 5.6 spread.1
  548.6 10.6 %expert_gradients.7 = (bf16[576,1536]{1,0:T(8,128)(2,1)}, bf16[576,1536]{1,0:T(8,128)(2,1)}) custom-call(bf16[1280,1536]{1,0:T(8,128)(2,1)} %bitcast.147, bf16[1280,1536]{1,0:T(8,128)(2,1)} %get-tuple-element.202.grads, bf16[4,576,1280]{2,1,0:T(8,128)(2,1)} %get-tuple-element.207.rest_0_.rest_1_, bf16[4,576,1280]{2,1,0:T(8,128)(2,1)} %get-tuple-element.207.rest_0_.rest_1_), custom_call_target="tpu_custom_call" | custom-call | tf_op jit(solution)/shard_map/expert_gradients/pallas_call | solution.py:592
  563.1 13.2 %all_to_all.24 = f32[8,2,512]{2,1,0:T(2,128)} all-to-all(f32[8,2,512]{2,1,0:T(2,128)S(1)} %broadcast_select_fusion), channel_id=1, replica_groups=mesh['rows'=8,'cols'=4] {'rows'}, dimensions={0} | all-to-all | bytes 65536 | tf_op jit(solution)/shard_map/all_to_all | solution.py:1170
  577.7 18.8 %collective-permute-done.42 = bf16[576,1536]{1,0:T(8,128)(2,1)} collective-permute-done((bf16[576,1536]{1,0:T(8,128)(2,1)}, bf16[576,1536]{1,0:T(8,128)(2,1)}, u32[]{:S(2)}, u32[]{:S(2)}) %collective-permute-start.42) | collective-permute-done | bytes 1769504 | tf_op jit(solution)/shard_map/ppermute | solution.py:936
  609.7 13.2 %collective-permute-done.33.rest_2_ = bf16[256,1536]{1,0:T(8,128)(2,1)S(1)} collective-permute-done((bf16[256,1536]{1,0:T(8,128)(2,1)S(1)}, bf16[256,1536]{1,0:T(8,128)(2,1)S(1)}, u32[]{:S(2)}, u32[]{:S(2)}) %collective-permute-start.33) | collective-permute-done | bytes 786464 | tf_op jit(solution)/shard_map/ppermute | solution.py:956
  624.4 13.5 %experts_norm_back.1 = (f32[512,1536]{1,0:T(8,128)}, bf16[512,1536]{1,0:T(8,128)(2,1)}, bf16[512,1536]{1,0:T(8,128)(2,1)}, f32[1,1536]{1,0:T(1,128)}, f32[16,1536]{1,0:T(8,128)}) custom-call(s32[16]{0:T(128)} %concatenate.32.info, f32[512,1536]{1,0:T(8,128)} %get-tuple-element.129.residual, bf16[512,1536]{1,0:T(8,128)(2,1)} %get-tuple-element.130.rows.normed, ...), custom_call_target="tpu_custom_call" | custom-call | tf_op jit(solution)/shard_map/experts_norm_back/pallas_call | solution.py:692
  637.9 15.4 %tree_attention_back.1 = (bf16[512,1536]{1,0:T(8,128)(2,1)}, f32[512,512]{1,0:T(8,128)}, f32[512,512]{1,0:T(8,128)}) custom-call(s32[16]{0:T(128)} %concatenate.32.info, bf16[512,1536]{1,0:T(8,128)(2,1)} %query_projection.1.queries, bf16[512,512]{1,0:T(8,128)(2,1)} %get-tuple-element.128.own, bf16[512,512]{1,0:T(8,128)(2,1)} %collective-permute-done.16.partner, ...), custom_call_target="tpu_custom_call" | custom-call | tf_op jit(solution)/shard_map/tree_attention_back/pallas_call | solution.py:296
  657.1 7.5 combine.7
  671.1 15.2 %weight_gradients.1 = (bf16[4,4,192,896]{3,2,1,0:T(8,128)(2,1)}, bf16[4,4,192,896]{3,2,1,0:T(8,128)(2,1)}) custom-call(s32[16]{0:T(128)} %concatenate.32.info, bf16[512,1536]{1,0:T(8,128)(2,1)} %get-tuple-element.125.normed, bf16[512,1536]{1,0:T(8,128)(2,1)} %tree_attention.1.heads, bf16[512,1536]{1,0:T(8,128)(2,1)} %get-tuple-element.224.grad_query, ...), custom_call_target="tpu_custom_call" | custom-call | tf_op jit(solution)/shard_map/weight_gradients/pallas_call | solution.py:841
  686.3 6.6 collective-permute-start.57
  701.5 30.9 %collective-permute-done.57 = bf16[576,1536]{1,0:T(8,128)(2,1)S(1)} collective-permute-done((bf16[576,1536]{1,0:T(8,128)(2,1)}, bf16[576,1536]{1,0:T(8,128)(2,1)S(1)}, u32[]{:S(2)}, u32[]{:S(2)}) %collective-permute-start.57) | collective-permute-done | bytes 1769504 | tf_op jit(solution)/shard_map/ppermute | solution.py:924
  732.4 37.0 %collective-permute-done.55 = bf16[576,1536]{1,0:T(8,128)(2,1)S(1)} collective-permute-done((bf16[576,1536]{1,0:T(8,128)(2,1)S(1)}, bf16[576,1536]{1,0:T(8,128)(2,1)S(1)}, u32[]{:S(2)}, u32[]{:S(2)}) %collective-permute-start.55) | collective-permute-done | bytes 1769504 | tf_op jit(solution)/shard_map/ppermute | solution.py:936
  771.2 7.5 combine.6
  801.2 13.5 %token_gradient.1 = (bf16[512,1536]{1,0:T(8,128)(2,1)}, f32[1,1536]{1,0:T(1,128)}) custom-call(s32[16]{0:T(128)} %concatenate.32.info, bf16[512,1536]{1,0:T(8,128)(2,1)} %get-tuple-element.224.grad_query, bf16[512,512]{1,0:T(8,128)(2,1)} %join_key_value_gradients.1.grad_pair, bf16[512,1536]{1,0:T(8,128)(2,1)} %tokens.5, ...), custom_call_target="tpu_custom_call" | custom-call | tf_op jit(solution)/shard_map/token_gradient/pallas_call | solution.py:781
  821.4 31.3 %all-to-all-done.1 = f32[8,1,3456]{2,1,0:T(1,128)S(1)} async-done(((f32[8,1,3456]{2,1,0:T(1,128)}), f32[8,1,3456]{2,1,0:T(1,128)S(1)}, u32[]{:S(2)}, u32[]{:S(2)}) %all-to-all-start.1) | async-done | bytes 110624 | tf_op jit(solution)/shard_map/all_to_all | solution.py:1251
  872.0 8.8 collective-permute-done.48
  896.7 9.4 %collective-permute-start.52 = (bf16[192,896]{1,0:T(8,128)(2,1)S(1)}, bf16[192,896]{1,0:T(8,128)(2,1)S(1)}, u32[]{:S(2)}, u32[]{:S(2)}) collective-permute-start(bf16[192,896]{1,0:T(8,128)(2,1)S(1)} %get-tuple-element.338), channel_id=1, source_target_pairs={{0,1},{1,2},{2,3},{4,5},{5,6},{6,7},{8,9},{9,10},{10,11},{12,13},{... | collective-permute-start | bytes 1032200 | tf_op jit(solution)/shard_map/ppermute | solution.py:936
  (311 shorter events, 245.5 us)
Async XLA Ops:
  7.2 334.1 %all-gather.6.cloned.1.call-start = ((), (), s32[]{:S(2)}) async-start(), calls=%async_computation.3 | async-start | bytes 14155776 | tf_op jit(solution)/shard_map/all_gather | solution.py:1094
  43.1 30.2 %collective-permute-start.4 = (bf16[4,192,896]{2,1,0:T(8,128)(2,1)S(1)}, bf16[4,192,896]{2,1,0:T(8,128)(2,1)S(1)}, u32[]{:S(2)}, u32[]{:S(2)}) collective-permute-start(bf16[4,192,896]{2,1,0:T(8,128)(2,1)S(1)} %pad_maximum_fusion.7.rest_0_.rest_6_.rest_10_), channel_id=1, source_target_pairs={{0,8},{4,12},{8,0},{12,4},{16,24},{20,28},{24,16},{28,20},{1,9},{5... | collective-permute-start | bytes 4128776 | tf_op jit(solution)/shard_map/ppermute | solution.py:956
  44.7 31.1 %collective-permute-start.5 = (bf16[4,192,896]{2,1,0:T(8,128)(2,1)S(1)}, bf16[4,192,896]{2,1,0:T(8,128)(2,1)S(1)}, u32[]{:S(2)}, u32[]{:S(2)}) collective-permute-start(bf16[4,192,896]{2,1,0:T(8,128)(2,1)S(1)} %pad_maximum_fusion.7.rest_0_.rest_6_.rest_10_), channel_id=1, source_target_pairs={{0,16},{4,20},{8,24},{12,28},{16,0},{20,4},{24,8},{28,12},{1,17},{... | collective-permute-start | bytes 4128776 | tf_op jit(solution)/shard_map/ppermute | solution.py:956
  46.2 43.6 %collective-permute-start.8 = (bf16[4,192,896]{2,1,0:T(8,128)(2,1)S(1)}, bf16[4,192,896]{2,1,0:T(8,128)(2,1)S(1)}, u32[]{:S(2)}, u32[]{:S(2)}) collective-permute-start(bf16[4,192,896]{2,1,0:T(8,128)(2,1)S(1)} %pad_maximum_fusion.7.rest_0_.rest_6_.rest_10_), channel_id=1, source_target_pairs={{0,4},{4,0},{8,12},{12,8},{16,20},{20,16},{24,28},{28,24},{1,5},{5... | collective-permute-start | bytes 4128776 | tf_op jit(solution)/shard_map/ppermute | solution.py:956
  73.4 15.9 %collective-permute-start.6 = (bf16[2,192,896]{2,1,0:T(8,128)(2,1)S(1)}, bf16[2,192,896]{2,1,0:T(8,128)(2,1)S(1)}, u32[]{:S(2)}, u32[]{:S(2)}) collective-permute-start(bf16[2,192,896]{2,1,0:T(8,128)(2,1)S(1)} %slice.524), channel_id=1, source_target_pairs={{0,16},{4,20},{8,24},{12,28},{16,0},{20,4},{24,8},{28,12},{1,17},{... | collective-permute-start | bytes 2064392 | tf_op jit(solution)/shard_map/ppermute | solution.py:956
  76.6 17.7 %collective-permute-start.9 = (bf16[4,192,896]{2,1,0:T(8,128)(2,1)S(1)}, bf16[4,192,896]{2,1,0:T(8,128)(2,1)}, u32[]{:S(2)}, u32[]{:S(2)}) collective-permute-start(bf16[4,192,896]{2,1,0:T(8,128)(2,1)S(1)} %collective-permute-done.4.rest_1_.rest_7_.rest_11_), channel_id=1, source_target_pairs={{0,4},{4,0},{8,12},{12,8},{16,20},{20,16},{24,28},{28,24},{1,5},{5... | collective-permute-start | bytes 4128776 | tf_op jit(solution)/shard_map/ppermute | solution.py:956
  98.1 124.3 %collective-permute-start.13 = (bf16[576,1536]{1,0:T(8,128)(2,1)S(1)}, bf16[576,1536]{1,0:T(8,128)(2,1)}, u32[]{:S(2)}, u32[]{:S(2)}) collective-permute-start(bf16[576,1536]{1,0:T(8,128)(2,1)S(1)} %pad_maximum_fusion.1.rest_0_), channel_id=1, source_target_pairs={{1,0},{2,1},{3,2},{5,4},{6,5},{7,6},{9,8},{10,9},{11,10},{13,12},{... | collective-permute-start | bytes 5308424 | tf_op jit(solution)/shard_map/ppermute | solution.py:896
  99.4 123.0 %collective-permute-start.14 = (bf16[576,1536]{1,0:T(8,128)(2,1)S(1)}, bf16[576,1536]{1,0:T(8,128)(2,1)S(1)}, u32[]{:S(2)}, u32[]{:S(2)}) collective-permute-start(bf16[576,1536]{1,0:T(8,128)(2,1)S(1)} %pad_maximum_fusion.1.rest_0_), channel_id=1, source_target_pairs={{0,1},{1,2},{2,3},{4,5},{5,6},{6,7},{8,9},{9,10},{10,11},{12,13},{... | collective-permute-start | bytes 5308424 | tf_op jit(solution)/shard_map/ppermute | solution.py:897
  104.0 118.4 %collective-permute-start.15 = (bf16[576,1536]{1,0:T(8,128)(2,1)S(1)}, bf16[576,1536]{1,0:T(8,128)(2,1)}, u32[]{:S(2)}, u32[]{:S(2)}) collective-permute-start(bf16[576,1536]{1,0:T(8,128)(2,1)S(1)} %pad_maximum_fusion.1.rest_0_), channel_id=1, source_target_pairs={{0,3},{3,0},{4,7},{7,4},{8,11},{11,8},{12,15},{15,12},{16,19},{19,... | collective-permute-start | bytes 5308424 | tf_op jit(solution)/shard_map/ppermute | solution.py:898
  211.6 16.4 %collective-permute-start.16 = (bf16[512,512]{1,0:T(8,128)(2,1)}, bf16[512,512]{1,0:T(8,128)(2,1)}, u32[]{:S(2)}, u32[]{:S(2)}) collective-permute-start(bf16[512,512]{1,0:T(8,128)(2,1)} %get-tuple-element.128.own), channel_id=1, source_target_pairs={{1,0},{3,2},{5,4},{7,6},{9,8},{11,10},{13,12},{15,14},{17,16},{19,... | collective-permute-start | bytes 1572872 | tf_op jit(solution)/shard_map/ppermute | solution.py:1100
  249.8 36.1 %collective-permute-start.17 = (bf16[512,1536]{1,0:T(8,128)(2,1)}, bf16[512,1536]{1,0:T(8,128)(2,1)S(1)}, u32[]{:S(2)}, u32[]{:S(2)}) collective-permute-start(bf16[512,1536]{1,0:T(8,128)(2,1)} %get-tuple-element.130.rows.normed), channel_id=1, source_target_pairs={{0,8},{4,12},{8,0},{12,4},{16,24},{20,28},{24,16},{28,20},{1,9},{5... | collective-permute-start | bytes 4718600 | tf_op jit(solution)/shard_map/ppermute | solution.py:956
  250.4 60.6 %collective-permute-start.19 = (bf16[512,1536]{1,0:T(8,128)(2,1)}, bf16[512,1536]{1,0:T(8,128)(2,1)}, u32[]{:S(2)}, u32[]{:S(2)}) collective-permute-start(bf16[512,1536]{1,0:T(8,128)(2,1)} %get-tuple-element.130.rows.normed), channel_id=1, source_target_pairs={{0,16},{4,20},{8,24},{12,28},{16,0},{20,4},{24,8},{28,12},{1,17},{... | collective-permute-start | bytes 4718600 | tf_op jit(solution)/shard_map/ppermute | solution.py:956
  252.0 81.0 %collective-permute-start.23 = (bf16[576,1536]{1,0:T(8,128)(2,1)S(1)}, bf16[576,1536]{1,0:T(8,128)(2,1)}, u32[]{:S(2)}, u32[]{:S(2)}) collective-permute-start(bf16[576,1536]{1,0:T(8,128)(2,1)S(1)} %pad_maximum_fusion.2.rest_0_), channel_id=1, source_target_pairs={{1,0},{2,1},{3,2},{5,4},{6,5},{7,6},{9,8},{10,9},{11,10},{13,12},{... | collective-permute-start | bytes 5308424 | tf_op jit(solution)/shard_map/ppermute | solution.py:896
  253.3 80.2 %collective-permute-start.24 = (bf16[576,1536]{1,0:T(8,128)(2,1)S(1)}, bf16[576,1536]{1,0:T(8,128)(2,1)}, u32[]{:S(2)}, u32[]{:S(2)}) collective-permute-start(bf16[576,1536]{1,0:T(8,128)(2,1)S(1)} %pad_maximum_fusion.2.rest_0_), channel_id=1, source_target_pairs={{0,1},{1,2},{2,3},{4,5},{5,6},{6,7},{8,9},{9,10},{10,11},{12,13},{... | collective-permute-start | bytes 5308424 | tf_op jit(solution)/shard_map/ppermute | solution.py:897
  259.1 75.7 %collective-permute-start.25 = (bf16[576,1536]{1,0:T(8,128)(2,1)S(1)}, bf16[576,1536]{1,0:T(8,128)(2,1)}, u32[]{:S(2)}, u32[]{:S(2)}) collective-permute-start(bf16[576,1536]{1,0:T(8,128)(2,1)S(1)} %pad_maximum_fusion.2.rest_0_), channel_id=1, source_target_pairs={{0,3},{3,0},{4,7},{7,4},{8,11},{11,8},{12,15},{15,12},{16,19},{19,... | collective-permute-start | bytes 5308424 | tf_op jit(solution)/shard_map/ppermute | solution.py:898
  288.0 26.8 %collective-permute-start.18 = (bf16[256,1536]{1,0:T(8,128)(2,1)}, bf16[256,1536]{1,0:T(8,128)(2,1)}, u32[]{:S(2)}, u32[]{:S(2)}) collective-permute-start(bf16[256,1536]{1,0:T(8,128)(2,1)} %slice.527), channel_id=1, source_target_pairs={{0,16},{4,20},{8,24},{12,28},{16,0},{20,4},{24,8},{28,12},{1,17},{... | collective-permute-start | bytes 2359304 | tf_op jit(solution)/shard_map/ppermute | solution.py:956
  312.2 19.8 %collective-permute-start.20 = (bf16[256,1536]{1,0:T(8,128)(2,1)S(1)}, bf16[256,1536]{1,0:T(8,128)(2,1)S(1)}, u32[]{:S(2)}, u32[]{:S(2)}) collective-permute-start(bf16[256,1536]{1,0:T(8,128)(2,1)S(1)} %slice.528), channel_id=1, source_target_pairs={{0,8},{4,12},{8,0},{12,4},{16,24},{20,28},{24,16},{28,20},{1,9},{5... | collective-permute-start | bytes 2359304 | tf_op jit(solution)/shard_map/ppermute | solution.py:956
  314.8 80.9 %collective-permute-start.28 = (bf16[576,1536]{1,0:T(8,128)(2,1)}, bf16[576,1536]{1,0:T(8,128)(2,1)}, u32[]{:S(2)}, u32[]{:S(2)}) collective-permute-start(bf16[576,1536]{1,0:T(8,128)(2,1)} %select_select_fusion.1), channel_id=1, source_target_pairs={{3,1},{1,0},{0,2},{2,3},{7,5},{5,4},{4,6},{6,7},{11,9},{9,8},{8,10... | collective-permute-start | bytes 5308424 | tf_op jit(solution)/shard_map/ppermute | solution.py:906
  332.1 16.8 %collective-permute-start.27 = (bf16[512,1536]{1,0:T(8,128)(2,1)}, bf16[512,1536]{1,0:T(8,128)(2,1)}, u32[]{:S(2)}, u32[]{:S(2)}) collective-permute-start(bf16[512,1536]{1,0:T(8,128)(2,1)} %get-tuple-element.130.rows.normed), channel_id=1, source_target_pairs={{0,4},{4,0},{8,12},{12,8},{16,20},{20,16},{24,28},{28,24},{1,5},{5... | collective-permute-start | bytes 4718600 | tf_op jit(solution)/shard_map/ppermute | solution.py:956
  333.1 30.9 %collective-permute-start.26 = (bf16[512,1536]{1,0:T(8,128)(2,1)S(1)}, bf16[512,1536]{1,0:T(8,128)(2,1)}, u32[]{:S(2)}, u32[]{:S(2)}) collective-permute-start(bf16[512,1536]{1,0:T(8,128)(2,1)S(1)} %copy-done.19), channel_id=1, source_target_pairs={{0,4},{4,0},{8,12},{12,8},{16,20},{20,16},{24,28},{28,24},{1,5},{5... | collective-permute-start | bytes 4718600 | tf_op jit(solution)/shard_map/ppermute | solution.py:956
  333.6 43.0 %collective-permute-start.22 = (bf16[512,1536]{1,0:T(8,128)(2,1)}, bf16[512,1536]{1,0:T(8,128)(2,1)}, u32[]{:S(2)}, u32[]{:S(2)}) collective-permute-start(bf16[512,1536]{1,0:T(8,128)(2,1)} %collective-permute-done.19.rows), channel_id=1, source_target_pairs={{0,4},{4,0},{8,12},{12,8},{16,20},{20,16},{24,28},{28,24},{1,5},{5... | collective-permute-start | bytes 4718600 | tf_op jit(solution)/shard_map/ppermute | solution.py:956
  334.8 54.5 %collective-permute-start.21 = (bf16[512,1536]{1,0:T(8,128)(2,1)}, bf16[512,1536]{1,0:T(8,128)(2,1)}, u32[]{:S(2)}, u32[]{:S(2)}) collective-permute-start(bf16[512,1536]{1,0:T(8,128)(2,1)} %constant_dynamic-update-slice_fusion.rows), channel_id=1, source_target_pairs={{0,4},{4,0},{8,12},{12,8},{16,20},{20,16},{24,28},{28,24},{1,5},{5... | collective-permute-start | bytes 4718600 | tf_op jit(solution)/shard_map/ppermute | solution.py:956
  348.9 95.4 %collective-permute-start.29 = (bf16[576,1536]{1,0:T(8,128)(2,1)S(1)}, bf16[576,1536]{1,0:T(8,128)(2,1)S(1)}, u32[]{:S(2)}, u32[]{:S(2)}) collective-permute-start(bf16[576,1536]{1,0:T(8,128)(2,1)S(1)} %copy-done.30), channel_id=1, source_target_pairs={{3,1},{1,0},{0,2},{2,3},{7,5},{5,4},{4,6},{6,7},{11,9},{9,8},{8,10... | collective-permute-start | bytes 5308424 | tf_op jit(solution)/shard_map/ppermute | solution.py:906
  436.5 49.7 %collective-permute-start.30 = (bf16[576,1536]{1,0:T(8,128)(2,1)}, bf16[576,1536]{1,0:T(8,128)(2,1)S(1)}, u32[]{:S(2)}, u32[]{:S(2)}) collective-permute-start(bf16[576,1536]{1,0:T(8,128)(2,1)} %get-tuple-element.206), channel_id=1, source_target_pairs={{1,3},{0,1},{2,0},{3,2},{5,7},{4,5},{6,4},{7,6},{9,11},{8,9},{10,8... | collective-permute-start | bytes 5308424 | tf_op jit(solution)/shard_map/ppermute | solution.py:923
  504.3 29.3 %collective-permute-start.31 = (bf16[4,512,1536]{2,1,0:T(8,128)(2,1)}, bf16[4,512,1536]{2,1,0:T(8,128)(2,1)}, u32[]{:S(2)}, u32[]{:S(2)}) collective-permute-start(bf16[4,512,1536]{2,1,0:T(8,128)(2,1)} %combine.5), channel_id=1, source_target_pairs={{0,4},{4,0},{8,12},{12,8},{16,20},{20,16},{24,28},{28,24},{1,5},{5... | collective-permute-start | bytes 18874376 | tf_op jit(solution)/shard_map/ppermute | solution.py:956
  514.9 45.5 %collective-permute-start.41 = (bf16[576,1536]{1,0:T(8,128)(2,1)}, bf16[576,1536]{1,0:T(8,128)(2,1)S(1)}, u32[]{:S(2)}, u32[]{:S(2)}) collective-permute-start(bf16[576,1536]{1,0:T(8,128)(2,1)} %get-tuple-element.218), channel_id=1, source_target_pairs={{0,3},{3,0},{4,7},{7,4},{8,11},{11,8},{12,15},{15,12},{16,19},{19,... | collective-permute-start | bytes 5308424 | tf_op jit(solution)/shard_map/ppermute | solution.py:924
  529.6 66.8 %collective-permute-start.42 = (bf16[576,1536]{1,0:T(8,128)(2,1)}, bf16[576,1536]{1,0:T(8,128)(2,1)}, u32[]{:S(2)}, u32[]{:S(2)}) collective-permute-start(bf16[576,1536]{1,0:T(8,128)(2,1)} %get-tuple-element.331), channel_id=1, source_target_pairs={{0,1},{1,2},{2,3},{4,5},{5,6},{6,7},{8,9},{9,10},{10,11},{12,13},{... | collective-permute-start | bytes 5308424 | tf_op jit(solution)/shard_map/ppermute | solution.py:936
  532.3 65.7 %collective-permute-start.43 = (bf16[576,1536]{1,0:T(8,128)(2,1)}, bf16[576,1536]{1,0:T(8,128)(2,1)}, u32[]{:S(2)}, u32[]{:S(2)}) collective-permute-start(bf16[576,1536]{1,0:T(8,128)(2,1)} %get-tuple-element.330), channel_id=1, source_target_pairs={{1,0},{2,1},{3,2},{5,4},{6,5},{7,6},{9,8},{10,9},{11,10},{13,12},{... | collective-permute-start | bytes 5308424 | tf_op jit(solution)/shard_map/ppermute | solution.py:937
  537.7 60.3 %collective-permute-start.32 = (bf16[2,256,1536]{2,1,0:T(8,128)(2,1)}, bf16[2,256,1536]{2,1,0:T(8,128)(2,1)}, u32[]{:S(2)}, u32[]{:S(2)}) collective-permute-start(bf16[2,256,1536]{2,1,0:T(8,128)(2,1)} %pad_maximum_fusion.3), channel_id=1, source_target_pairs={{0,8},{4,12},{8,0},{12,4},{16,24},{20,28},{24,16},{28,20},{1,9},{5... | collective-permute-start | bytes 4718600 | tf_op jit(solution)/shard_map/ppermute | solution.py:956
  539.4 58.6 %collective-permute-start.34 = (bf16[2,256,1536]{2,1,0:T(8,128)(2,1)}, bf16[2,256,1536]{2,1,0:T(8,128)(2,1)}, u32[]{:S(2)}, u32[]{:S(2)}) collective-permute-start(bf16[2,256,1536]{2,1,0:T(8,128)(2,1)} %pad_maximum_fusion.4), channel_id=1, source_target_pairs={{0,16},{4,20},{8,24},{12,28},{16,0},{20,4},{24,8},{28,12},{1,17},{... | collective-permute-start | bytes 4718600 | tf_op jit(solution)/shard_map/ppermute | solution.py:956
  561.6 76.4 %collective-permute-start.44 = (bf16[576,1536]{1,0:T(8,128)(2,1)}, bf16[576,1536]{1,0:T(8,128)(2,1)S(1)}, u32[]{:S(2)}, u32[]{:S(2)}) collective-permute-start(bf16[576,1536]{1,0:T(8,128)(2,1)} %get-tuple-element.222), channel_id=1, source_target_pairs={{1,3},{0,1},{2,0},{3,2},{5,7},{4,5},{6,4},{7,6},{9,11},{8,9},{10,8... | collective-permute-start | bytes 5308424 | tf_op jit(solution)/shard_map/ppermute | solution.py:923
  603.5 19.4 %collective-permute-start.33 = (bf16[256,1536]{1,0:T(8,128)(2,1)S(1)}, bf16[256,1536]{1,0:T(8,128)(2,1)S(1)}, u32[]{:S(2)}, u32[]{:S(2)}) collective-permute-start(bf16[256,1536]{1,0:T(8,128)(2,1)S(1)} %get-tuple-element.308), channel_id=1, source_target_pairs={{0,16},{4,20},{8,24},{12,28},{16,0},{20,4},{24,8},{28,12},{1,17},{... | collective-permute-start | bytes 2359304 | tf_op jit(solution)/shard_map/ppermute | solution.py:956
  604.4 19.1 %collective-permute-start.35 = (bf16[256,1536]{1,0:T(8,128)(2,1)S(1)}, bf16[256,1536]{1,0:T(8,128)(2,1)S(1)}, u32[]{:S(2)}, u32[]{:S(2)}) collective-permute-start(bf16[256,1536]{1,0:T(8,128)(2,1)S(1)} %get-tuple-element.306), channel_id=1, source_target_pairs={{0,8},{4,12},{8,0},{12,4},{16,24},{20,28},{24,16},{28,20},{1,9},{5... | collective-permute-start | bytes 2359304 | tf_op jit(solution)/shard_map/ppermute | solution.py:956
  664.5 122.1 %collective-permute-start.36 = (bf16[4,512,1536]{2,1,0:T(8,128)(2,1)}, bf16[4,512,1536]{2,1,0:T(8,128)(2,1)}, u32[]{:S(2)}, u32[]{:S(2)}) collective-permute-start(bf16[4,512,1536]{2,1,0:T(8,128)(2,1)} %combine.7), channel_id=1, source_target_pairs={{0,4},{4,0},{8,12},{12,8},{16,20},{20,16},{24,28},{28,24},{1,5},{5... | collective-permute-start | bytes 18874376 | tf_op jit(solution)/shard_map/ppermute | solution.py:956
  686.3 92.4 %collective-permute-start.46 = (bf16[4,4,192,896]{3,2,1,0:T(8,128)(2,1)}, bf16[4,4,192,896]{3,2,1,0:T(8,128)(2,1)}, u32[]{:S(2)}, u32[]{:S(2)}) collective-permute-start(bf16[4,4,192,896]{3,2,1,0:T(8,128)(2,1)} %get-tuple-element.231), channel_id=1, source_target_pairs={{0,4},{4,0},{8,12},{12,8},{16,20},{20,16},{24,28},{28,24},{1,5},{5... | collective-permute-start | bytes 16515080 | tf_op jit(solution)/shard_map/ppermute | solution.py:956
  686.3 46.1 %collective-permute-start.57 = (bf16[576,1536]{1,0:T(8,128)(2,1)}, bf16[576,1536]{1,0:T(8,128)(2,1)S(1)}, u32[]{:S(2)}, u32[]{:S(2)}) collective-permute-start(bf16[576,1536]{1,0:T(8,128)(2,1)} %get-tuple-element.237), channel_id=1, source_target_pairs={{0,3},{3,0},{4,7},{7,4},{8,11},{11,8},{12,15},{15,12},{16,19},{19,... | collective-permute-start | bytes 5308424 | tf_op jit(solution)/shard_map/ppermute | solution.py:924
  694.0 75.5 %collective-permute-start.55 = (bf16[576,1536]{1,0:T(8,128)(2,1)S(1)}, bf16[576,1536]{1,0:T(8,128)(2,1)S(1)}, u32[]{:S(2)}, u32[]{:S(2)}) collective-permute-start(bf16[576,1536]{1,0:T(8,128)(2,1)S(1)} %get-tuple-element.328), channel_id=1, source_target_pairs={{0,1},{1,2},{2,3},{4,5},{5,6},{6,7},{8,9},{9,10},{10,11},{12,13},{... | collective-permute-start | bytes 5308424 | tf_op jit(solution)/shard_map/ppermute | solution.py:936
  695.4 74.7 %collective-permute-start.56 = (bf16[576,1536]{1,0:T(8,128)(2,1)S(1)}, bf16[576,1536]{1,0:T(8,128)(2,1)S(1)}, u32[]{:S(2)}, u32[]{:S(2)}) collective-permute-start(bf16[576,1536]{1,0:T(8,128)(2,1)S(1)} %get-tuple-element.329), channel_id=1, source_target_pairs={{1,0},{2,1},{3,2},{5,4},{6,5},{7,6},{9,8},{10,9},{11,10},{13,12},{... | collective-permute-start | bytes 5308424 | tf_op jit(solution)/shard_map/ppermute | solution.py:937
  783.3 75.3 %collective-permute-start.47 = (bf16[2,2,192,896]{3,2,1,0:T(8,128)(2,1)}, bf16[2,2,192,896]{3,2,1,0:T(8,128)(2,1)}, u32[]{:S(2)}, u32[]{:S(2)}) collective-permute-start(bf16[2,2,192,896]{3,2,1,0:T(8,128)(2,1)} %pad_maximum_fusion.8), channel_id=1, source_target_pairs={{0,8},{4,12},{8,0},{12,4},{16,24},{20,28},{24,16},{28,20},{1,9},{5... | collective-permute-start | bytes 4128776 | tf_op jit(solution)/shard_map/ppermute | solution.py:956
  785.7 72.9 %collective-permute-start.49 = (bf16[2,2,192,896]{3,2,1,0:T(8,128)(2,1)}, bf16[2,2,192,896]{3,2,1,0:T(8,128)(2,1)}, u32[]{:S(2)}, u32[]{:S(2)}) collective-permute-start(bf16[2,2,192,896]{3,2,1,0:T(8,128)(2,1)} %pad_maximum_fusion.9), channel_id=1, source_target_pairs={{0,16},{4,20},{8,24},{12,28},{16,0},{20,4},{24,8},{28,12},{1,17},{... | collective-permute-start | bytes 4128776 | tf_op jit(solution)/shard_map/ppermute | solution.py:956
  790.7 75.2 %collective-permute-start.39 = (bf16[2,256,1536]{2,1,0:T(8,128)(2,1)}, bf16[2,256,1536]{2,1,0:T(8,128)(2,1)}, u32[]{:S(2)}, u32[]{:S(2)}) collective-permute-start(bf16[2,256,1536]{2,1,0:T(8,128)(2,1)} %pad_maximum_fusion.6), channel_id=1, source_target_pairs={{0,16},{4,20},{8,24},{12,28},{16,0},{20,4},{24,8},{28,12},{1,17},{... | collective-permute-start | bytes 4718600 | tf_op jit(solution)/shard_map/ppermute | solution.py:956
  793.1 72.8 %collective-permute-start.37 = (bf16[2,256,1536]{2,1,0:T(8,128)(2,1)}, bf16[2,256,1536]{2,1,0:T(8,128)(2,1)}, u32[]{:S(2)}, u32[]{:S(2)}) collective-permute-start(bf16[2,256,1536]{2,1,0:T(8,128)(2,1)} %pad_maximum_fusion.5), channel_id=1, source_target_pairs={{0,8},{4,12},{8,0},{12,4},{16,24},{20,28},{24,16},{28,20},{1,9},{5... | collective-permute-start | bytes 4718600 | tf_op jit(solution)/shard_map/ppermute | solution.py:956
  816.4 36.2 %all-to-all-start.1 = ((f32[8,1,3456]{2,1,0:T(1,128)}), f32[8,1,3456]{2,1,0:T(1,128)S(1)}, u32[]{:S(2)}, u32[]{:S(2)}) async-start(f32[8,1,3456]{2,1,0:T(1,128)} %all_to_all.20), calls=%async_computation.1 | async-start | bytes 221184 | tf_op jit(solution)/shard_map/all_to_all | solution.py:1251
  862.3 18.6 %collective-permute-start.48 = (bf16[2,192,896]{2,1,0:T(8,128)(2,1)}, bf16[2,192,896]{2,1,0:T(8,128)(2,1)S(1)}, u32[]{:S(2)}, u32[]{:S(2)}) collective-permute-start(bf16[2,192,896]{2,1,0:T(8,128)(2,1)} %get-tuple-element.317), channel_id=1, source_target_pairs={{0,16},{4,20},{8,24},{12,28},{16,0},{20,4},{24,8},{28,12},{1,17},{... | collective-permute-start | bytes 2064392 | tf_op jit(solution)/shard_map/ppermute | solution.py:956
  863.2 18.6 %collective-permute-start.50 = (bf16[2,192,896]{2,1,0:T(8,128)(2,1)S(1)}, bf16[2,192,896]{2,1,0:T(8,128)(2,1)}, u32[]{:S(2)}, u32[]{:S(2)}) collective-permute-start(bf16[2,192,896]{2,1,0:T(8,128)(2,1)S(1)} %get-tuple-element.316), channel_id=1, source_target_pairs={{0,8},{4,12},{8,0},{12,4},{16,24},{20,28},{24,16},{28,20},{1,9},{5... | collective-permute-start | bytes 2064392 | tf_op jit(solution)/shard_map/ppermute | solution.py:956
  869.9 37.4 %collective-permute-start.38 = (bf16[256,1536]{1,0:T(8,128)(2,1)}, bf16[256,1536]{1,0:T(8,128)(2,1)S(1)}, u32[]{:S(2)}, u32[]{:S(2)}) collective-permute-start(bf16[256,1536]{1,0:T(8,128)(2,1)} %get-tuple-element.300), channel_id=1, source_target_pairs={{0,16},{4,20},{8,24},{12,28},{16,0},{20,4},{24,8},{28,12},{1,17},{... | collective-permute-start | bytes 2359304 | tf_op jit(solution)/shard_map/ppermute | solution.py:956
  870.8 36.5 %collective-permute-start.40 = (bf16[256,1536]{1,0:T(8,128)(2,1)}, bf16[256,1536]{1,0:T(8,128)(2,1)S(1)}, u32[]{:S(2)}, u32[]{:S(2)}) collective-permute-start(bf16[256,1536]{1,0:T(8,128)(2,1)} %get-tuple-element.301), channel_id=1, source_target_pairs={{0,8},{4,12},{8,0},{12,4},{16,24},{20,28},{24,16},{28,20},{1,9},{5... | collective-permute-start | bytes 2359304 | tf_op jit(solution)/shard_map/ppermute | solution.py:956
  889.3 23.0 %collective-permute-start.54 = (bf16[192,896]{1,0:T(8,128)(2,1)S(1)}, bf16[192,896]{1,0:T(8,128)(2,1)S(1)}, u32[]{:S(2)}, u32[]{:S(2)}) collective-permute-start(bf16[192,896]{1,0:T(8,128)(2,1)S(1)} %slice_bitcast_fusion.15), channel_id=1, source_target_pairs={{0,3},{3,0},{4,7},{7,4},{8,11},{11,8},{12,15},{15,12},{16,19},{19,... | collective-permute-start | bytes 1032200 | tf_op jit(solution)/shard_map/ppermute | solution.py:924
  (62 other events, 960.4 us)
Sparse Core Ops, SparseCore 0:
  94.5 71.4 all-gather.5

commit v5 on v4

--- a/solution.py
+++ b/solution.py
@@ -61,29 +61,55 @@
 
 
 PIECES = tuple(
-    (flip_bits + core, first, count)
+    (flip_bits + core, slots)
+    for wave in ((0, 2), (1, 3))
     for core in (0, 1)
-    for flip_bits, first, count in ((0, 0, 4), (2, 0, 4), (4, 0, 4), (6, 0, 2), (6, 2, 2))
+    for flip_bits, slots in ((0, wave), (2, wave), (4, wave), (6, wave[:1]), (6, wave[1:]))
 )
+EXTRA = 16
 
 
 def weight_copies(info, refs, target, sem, start, width):
     if len(refs) == 1:
         return [pltpu.make_async_copy(refs[0], target, sem)]
-    depth = refs[0].shape[1]
+    depth = refs[0].shape[1] - EXTRA
     copies = []
-    for ref, (flip_bits, first, count) in zip(refs, PIECES):
+    for ref, (flip_bits, slots) in zip(refs, PIECES):
         row = pl.multiple_of((info[0] ^ flip_bits) * depth, depth)
-        for slot in range(count):
-            col = pl.multiple_of(info[2 + first + slot] * width, 128)
+        for at, slot in enumerate(slots):
+            col = pl.multiple_of(info[2 + slot] * width, 128)
             copies.append(
                 pltpu.make_async_copy(
-                    ref.at[slot, :, pl.ds(start, width)],
+                    ref.at[at, pl.ds(0, depth), pl.ds(start, width)],
                     target.at[pl.ds(row, depth), pl.ds(col, width)],
                     sem,
                 )
             )
     return copies
+
+
+def extras_kernel(info, *rest):
+    refs, (out, sem) = rest[:-2], rest[-2:]
+    depth = refs[0].shape[1] - EXTRA
+    copies = []
+    for ref, (flip_bits, slots) in zip(refs, PIECES):
+        for at, slot in enumerate(slots):
+            to = (info[0] ^ flip_bits) * QUARTERS + info[2 + slot]
+            copies.append(pltpu.make_async_copy(ref.at[at, pl.ds(depth, EXTRA)], out.at[to], sem))
+    run_all(copies)
+    wait_all(copies)
+
+
+def extras(info, refs):
+    return pl.pallas_call(
+        extras_kernel,
+        out_shape=jax.ShapeDtypeStruct((8 * QUARTERS, EXTRA, refs[0].shape[2]), LOW),
+        in_specs=[SMEM] + [ANY] * len(refs),
+        out_specs=pl.BlockSpec(memory_space=pltpu.VMEM),
+        scratch_shapes=[pltpu.SemaphoreType.DMA],
+        compiler_params=params(),
+        name="extra_rows",
+    )(info, *refs)
 
 
 def run_all(copies):
@@ -355,107 +381,155 @@
     )(info, heads, tokens, gain, *refs)
 
 
-def dispatch_kernel(capacity, local, wide, order, info, rows, grads, routes, router, *rest):
-    outs = rest[len(rest) // 2 - 1 : -2]
-    token_outs, grad_outs = outs[:local], outs[local : 2 * local]
-    share_outs, chosen_out, place_out = outs[2 * local : 3 * local], outs[-2], outs[-1]
-    onehot, logits = rest[-2:]
-    total = router.shape[1]
-    step = pl.program_id(0)
-    ids = lax.broadcasted_iota(jnp.int32, (total, TOK_DEV), 0)
-
-    def hits():
-        hit = ids == routes[0, 0:1]
-        for k in range(1, TOP):
-            hit = jnp.logical_or(hit, ids == routes[0, k : k + 1])
-        return hit
-
-    @pl.when(step == 0)
+def hits_of(routes, ids):
+    hit = ids == routes[0, 0:1]
+    for k in range(1, TOP):
+        hit = jnp.logical_or(hit, ids == routes[0, k : k + 1])
+    return hit
+
+
+def tables_kernel(capacity, local, total, order, info, routes, chosen_out, place_out, earlier):
+    @pl.when(pl.program_id(0) == 0)
     def _():
         one = lax.broadcasted_iota(jnp.int32, (TOK_DEV, TOK_DEV), 0)
         two = lax.broadcasted_iota(jnp.int32, (TOK_DEV, TOK_DEV), 1)
-        earlier = jnp.where(one < two, 1.0, 0.0).astype(LOW)
-        hit = hits()
-        rank = nn(jnp.where(hit, 1.0, 0.0).astype(LOW), earlier)
-        place = jnp.where(hit, rank, -1.0)
-        spots = lax.broadcasted_iota(jnp.int32, (capacity, TOK_DEV), 0).astype(WIDE)
-        place_out[0] = jnp.full(place_out.shape[1:], -1.0, WIDE)
-        for e in range(local):
-            mine = ids == info[0] * local + e
-            place_row = jnp.sum(jnp.where(mine, place, 0.0), axis=0, keepdims=True)
-            place_out[0, e : e + 1] = place_row
-            onehot[e * capacity : (e + 1) * capacity] = jnp.where(
-                spots == place_row, 1.0, 0.0
-            ).astype(LOW)
-        chosen_out[0] = onehot[...]
-        logits[...] = jnp.zeros_like(logits)
-
+        earlier[...] = jnp.where(one < two, 1.0, 0.0).astype(LOW)
+
+    ids = lax.broadcasted_iota(jnp.int32, (total, TOK_DEV), 0)
+    hit = hits_of(routes, ids)
+    rank = nn(jnp.where(hit, 1.0, 0.0).astype(LOW), earlier[...])
+    place = jnp.where(hit, rank, -1.0)
+    spots = lax.broadcasted_iota(jnp.int32, (capacity, TOK_DEV), 0).astype(WIDE)
+    place_out[0] = jnp.full(place_out.shape[1:], -1.0, WIDE)
+    for e in range(local):
+        mine = ids == info[0] * local + e
+        place_row = jnp.sum(jnp.where(mine, place, 0.0), axis=0, keepdims=True)
+        place_out[0, e : e + 1] = place_row
+        chosen_out[0, e * capacity : (e + 1) * capacity] = jnp.where(
+            spots == place_row, 1.0, 0.0
+        ).astype(LOW)
+
+
+def tables(order, info, routes, capacity, local, total):
+    count = routes.shape[0]
+    return pl.pallas_call(
+        functools.partial(tables_kernel, capacity, local, total),
+        grid_spec=pltpu.PrefetchScalarGridSpec(
+            num_scalar_prefetch=2,
+            grid=(count,),
+            in_specs=[pl.BlockSpec((1, TOP, TOK_DEV), lambda i, order, info: (order[i], 0, 0))],
+            out_specs=[
+                pl.BlockSpec((1, local * capacity, TOK_DEV), lambda i, order, info: (i, 0, 0)),
+                pl.BlockSpec((1, 8, TOK_DEV), lambda i, order, info: (i, 0, 0)),
+            ],
+            scratch_shapes=[pltpu.VMEM((TOK_DEV, TOK_DEV), LOW)],
+        ),
+        out_shape=[
+            jax.ShapeDtypeStruct((count, local * capacity, TOK_DEV), LOW),
+            jax.ShapeDtypeStruct((count, 8, TOK_DEV), WIDE),
+        ],
+        compiler_params=params(),
+        name="route_tables",
+    )(order, info, routes)
+
+
+def pick_kernel(local, order, chosen, blocks, *outs):
+    rows_of = nn(chosen[0], blocks[0]).astype(LOW)
+    capacity = outs[0].shape[1]
+    for e in range(local):
+        outs[e][0] = rows_of[e * capacity : (e + 1) * capacity]
+
+
+def pick_rows(order, chosen, blocks, local):
+    count, height, _ = chosen.shape
+    capacity = height // local
+    return pl.pallas_call(
+        functools.partial(pick_kernel, local),
+        grid_spec=pltpu.PrefetchScalarGridSpec(
+            num_scalar_prefetch=1,
+            grid=(count,),
+            in_specs=[
+                pl.BlockSpec((1, height, TOK_DEV), lambda i, order: (i, 0, 0)),
+                pl.BlockSpec((1, TOK_DEV, D), lambda i, order: (order[i], 0, 0)),
+            ],
+            out_specs=[pl.BlockSpec((1, capacity, D), lambda i, order: (i, 0, 0))] * local,
+        ),
+        out_shape=[jax.ShapeDtypeStruct((count, capacity, D), LOW)] * local,
+        compiler_params=params(),
+        name="pick_rows",
+    )(order, chosen, blocks)
+
+
+def dispatch_kernel(local, order, info, rows, chosen, routes, router, *rest):
+    outs, logits = rest[2 * local : 4 * local], rest[-1]
+    total = router.shape[1]
+    step = pl.program_id(0)
     block = rows[...]
-    logits[...] += nn(block, router[...])
-    for outs_of, source in ((token_outs, block), (grad_outs, grads[0])):
-        rows_of = nn(onehot[...], source).astype(LOW)
-        for e in range(local):
-            outs_of[e][0] = rows_of[e * capacity : (e + 1) * capacity]
+    rows_of = nn(chosen[0], block).astype(LOW)
+    capacity = outs[0].shape[1]
+    for e in range(local):
+        outs[e][0] = rows_of[e * capacity : (e + 1) * capacity]
+    part = nn(block, router[...])
+
+    @pl.when(step == 0)
+    def _():
+        logits[...] = part
+
+    @pl.when(step > 0)
+    def _():
+        logits[...] += part
 
     @pl.when(step == pl.num_programs(0) - 1)
     def _():
         values = logits[...].T
+        ids = lax.broadcasted_iota(jnp.int32, (total, TOK_DEV), 0)
         weights = jnp.exp(values - jnp.max(values, axis=0, keepdims=True))
-        share = weights / jnp.sum(jnp.where(hits(), weights, 0.0), axis=0, keepdims=True)
+        hit = hits_of(routes, ids)
+        share = weights / jnp.sum(jnp.where(hit, weights, 0.0), axis=0, keepdims=True)
         for e in range(local):
             mine = ids == info[0] * local + e
             share_row = jnp.sum(jnp.where(mine, share, 0.0), axis=0, keepdims=True)
-            chosen = onehot[e * capacity : (e + 1) * capacity].astype(WIDE)
-            share_outs[e][0] = jnp.sum(chosen * share_row, axis=1, keepdims=True)
-
-
-def dispatch(order, info, rows, grads, routes, router, capacity, local, earlier):
-    count = grads.shape[0]
+            picked = chosen[0, e * capacity : (e + 1) * capacity].astype(WIDE)
+            outs[local + e][0] = jnp.sum(picked * share_row, axis=1, keepdims=True)
+
+
+def dispatch(order, info, rows, chosen, routes, router, local, earlier):
+    count, height, _ = chosen.shape
+    capacity = height // local
     total = router.shape[1]
     wide = 512
-    picked = pl.BlockSpec((1, capacity, wide), lambda i, order, info: (order[0], 0, i))
-
-    def fixed(shape):
-        return pl.BlockSpec((1,) + shape, lambda i, order, info: (order[0], 0, 0))
-
-    out_shape = (
-        [jax.ShapeDtypeStruct((count, capacity, D), LOW)] * (2 * local)
-        + [jax.ShapeDtypeStruct((count, capacity, 1), WIDE)] * local
-        + [
-            jax.ShapeDtypeStruct((count, local * capacity, TOK_DEV), LOW),
-            jax.ShapeDtypeStruct((count, 8, TOK_DEV), WIDE),
-        ]
-    )
+    out_shape = [jax.ShapeDtypeStruct((count, capacity, D), LOW)] * local + [
+        jax.ShapeDtypeStruct((count, capacity, 1), WIDE)
+    ] * local
     if earlier is None:
         earlier = [jnp.zeros((8, 128), shape.dtype) for shape in out_shape]
         aliases = {}
     else:
         aliases = {6 + i: i for i in range(len(out_shape))}
     return pl.pallas_call(
-        functools.partial(dispatch_kernel, capacity, local, wide),
+        functools.partial(dispatch_kernel, local),
         grid_spec=pltpu.PrefetchScalarGridSpec(
             num_scalar_prefetch=2,
             grid=(D // wide,),
             in_specs=[
                 pl.BlockSpec((TOK_DEV, wide), lambda i, order, info: (0, i)),
-                pl.BlockSpec((1, TOK_DEV, wide), lambda i, order, info: (order[1], 0, i)),
+                pl.BlockSpec((1, height, TOK_DEV), lambda i, order, info: (order[0], 0, 0)),
                 pl.BlockSpec((1, TOP, TOK_DEV), lambda i, order, info: (order[1], 0, 0)),
                 pl.BlockSpec((wide, total), lambda i, order, info: (i, 0)),
             ]
             + [ANY] * len(out_shape),
-            out_specs=[picked] * (2 * local)
-            + [fixed((capacity, 1))] * local
-            + [fixed((local * capacity, TOK_DEV)), fixed((8, TOK_DEV))],
-            scratch_shapes=[
-                pltpu.VMEM((local * capacity, TOK_DEV), LOW),
-                pltpu.VMEM((TOK_DEV, total), WIDE),
-            ],
+            out_specs=[
+                pl.BlockSpec((1, capacity, wide), lambda i, order, info: (order[0], 0, i))
+            ]
+            * local
+            + [pl.BlockSpec((1, capacity, 1), lambda i, order, info: (order[0], 0, 0))] * local,
+            scratch_shapes=[pltpu.VMEM((TOK_DEV, total), WIDE)],
         ),
         out_shape=out_shape,
         input_output_aliases=aliases,
         compiler_params=params(),
         name="dispatch",
-    )(order, info, rows, grads, routes, router, *earlier)
+    )(order, info, rows, chosen, routes, router, *earlier)
 
 
 def spread_kernel(local, place, *rest):
@@ -581,10 +655,9 @@
 def expert_grads_kernel(slots, rows, grads, *rest):
     acts, outs = rest[: len(slots)], rest[len(slots) :]
     part = acts[0].shape[1] // 3
-    at = pl.ds(pl.multiple_of(pl.program_id(0) * 256, 256), 256)
     for act, out in zip(acts, outs):
-        out[: 2 * part, :] = nn(act[0, : 2 * part], rows[:, at]).astype(LOW)
-        out[2 * part :, :] = nn(act[0, 2 * part :], grads[:, at]).astype(LOW)
+        out[: 2 * part, :] = nn(act[0, : 2 * part], rows[...]).astype(LOW)
+        out[2 * part :, :] = nn(act[0, 2 * part :], grads[...]).astype(LOW)
 
 
 def expert_grads(acts, rows, grads, slots):
@@ -593,7 +666,7 @@
         functools.partial(expert_grads_kernel, slots),
         grid=(D // 256,),
         out_shape=[jax.ShapeDtypeStruct((part, D), LOW) for _ in slots],
-        in_specs=[whole((height, D))] * 2
+        in_specs=[pl.BlockSpec((height, 256), lambda i: (0, i))] * 2
         + [pl.BlockSpec((1, part, height), lambda i, s=slot: (s, 0, 0)) for slot in slots],
         out_specs=[pl.BlockSpec((part, 256), lambda i: (0, i)) for _ in slots],
         compiler_params=params(),
@@ -803,59 +876,57 @@
     )(info, grad_query, grad_pair, tokens, grad_residual, gain, *query_refs, *pair_refs)
 
 
-def weight_grads_kernel(info, normed, heads, grad_query, grad_pair, grad_branch, keep, send):
-    quarter = D // QUARTERS
-    depth = keep.shape[2]
+def weight_grads_kernel(parts, info, *rest):
+    ins, (keep, send) = rest[:-2], rest[-2:]
+    depth = D // 8
     core = info[0] & 1
-
-    def store(grads, start, width):
-        low = grads.astype(LOW)
+    chip = pl.program_id(0) ^ (info[0] >> 1)
+    start = 0
+    for strip_at, grads_at, width in parts:
+        low = tn(ins[strip_at][...], ins[grads_at][...]).astype(LOW)
+        columns = slice(start, start + width)
+        start += width
         for slot in range(QUARTERS):
-            shard = info[2 + slot]
             for j in range(QUARTERS):
-                piece = low[:, j * width : (j + 1) * width]
-                upper, lower = piece[:depth], piece[depth:]
-
-                @pl.when(shard == j)
+
+                @pl.when(info[2 + slot] == j)
                 def _():
-                    columns = slice(start, start + width)
-                    keep[0, slot, :, columns] = jnp.where(core == 0, upper, lower)
-                    send[0, slot, :, columns] = jnp.where(core == 0, lower, upper)
-
-    store(tn(normed[...], grad_query[...]), 0, quarter)
-    store(tn(normed[...], grad_pair[...]), quarter, 128)
-    store(tn(heads[...], grad_branch[...]), quarter + 128, quarter)
-
-
-def weight_grads(info, normed, heads, grad_query, grad_pair, grad_branch):
-    full = (TOK_DEV, D)
-    quarter = D // QUARTERS
-    width = 2 * quarter + 128
-    strip = pl.BlockSpec((TOK_DEV, quarter), lambda i, info: (0, i ^ (info[0] >> 1)))
-    shape = (4, QUARTERS, quarter // 2, width)
+                    piece = low[:, j * width : (j + 1) * width]
+                    upper, lower = piece[:depth], piece[depth:]
+                    keep[0, slot, :depth, columns] = jnp.where(core == 0, upper, lower)
+                    send[0, slot, :depth, columns] = jnp.where(core == 0, lower, upper)
+
+    if keep.shape[2] > depth:
+        extra = ins[-1]
+        for slot in range(QUARTERS):
+            to = info[2 + slot]
+            keep[0, slot, depth:] = extra[(chip * 2 + core) * QUARTERS + to]
+            send[0, slot, depth:] = extra[(chip * 2 + 1 - core) * QUARTERS + to]
+
+
+def weight_grads(info, strips, grads, parts, extra):
+    depth = D // 8
+    width = sum(part[2] for part in parts)
+    strip = pl.BlockSpec((TOK_DEV, 2 * depth), lambda i, info: (0, i ^ (info[0] >> 1)))
+    more = [] if extra is None else [extra]
+    shape = (4, QUARTERS, depth + EXTRA * len(more), width)
     out = pl.BlockSpec((1,) + shape[1:], lambda i, info: (i, 0, 0, 0))
-
-    def fixed(block):
-        return pl.BlockSpec(block, lambda i, info: (0, 0))
-
-    return pl.pallas_call(
-        weight_grads_kernel,
+    return pl.pallas_call(
+        functools.partial(weight_grads_kernel, parts),
         grid_spec=pltpu.PrefetchScalarGridSpec(
             num_scalar_prefetch=1,
             grid=(4,),
-            in_specs=[
-                strip,
-                strip,
-                fixed(full),
-                fixed((TOK_DEV, 2 * KEY_WIDTH)),
-                fixed(full),
+            in_specs=[strip] * len(strips)
+            + [
+                pl.BlockSpec(a.shape, lambda i, info, n=a.ndim: (0,) * n)
+                for a in (*grads, *more)
             ],
             out_specs=(out, out),
         ),
         out_shape=(jax.ShapeDtypeStruct(shape, LOW),) * 2,
         compiler_params=params(),
         name="weight_gradients",
-    )(info, normed, heads, grad_query, grad_pair, grad_branch)
+    )(info, *strips, *grads, *more)
 
 
 def position_of(token_index):
@@ -1025,19 +1096,10 @@
         [jnp.stack([row_place, parity]), shards, branch_rows, jnp.zeros((2,), jnp.int32)]
     ).astype(jnp.int32)
 
-    small = jnp.concatenate([attention_gain, experts_gain, router_weight.reshape(-1)])
-    small = jnp.pad(small, (0, 2048 - small.shape[0])).reshape(16, 128)
-    small_all = lax.all_gather(lax.all_gather(small, "cols", axis=0), "rows", axis=0)
-    small_all = small_all.reshape(row_count * col_count, -1)
-    small_all = small_all[:, : 2 * gain_part + depth * router_part]
-    attention_scale = small_all[:, :gain_part].reshape(1, D).astype(WIDE)
-    experts_scale = small_all[:, gain_part : 2 * gain_part].reshape(1, D).astype(WIDE)
-    router_rows = jnp.transpose(
-        small_all[:, 2 * gain_part :].reshape(row_count, col_count, depth, router_part),
-        (1, 3, 0, 2),
-    ).reshape(expert_total, D)
-
     packed = jnp.concatenate([query_weight, key_weight, value_weight, out_weight], axis=1)
+    local_index = (1 - parity) * TOK_DEV + jnp.arange(TOK_DEV, dtype=jnp.int32)
+    cosine, sine = rotary_tables(position_of(local_index))
+    routes_all = lax.all_gather(routes.T, "rows", axis=0)
     shard_blocks = [
         jnp.concatenate(
             [gate_weight[expert].T, upward_weight[expert].T, down_weight[expert]], axis=0
@@ -1046,9 +1108,20 @@
     ]
     firsts, seconds = ([], [])
     if fast:
+        wide = packed.shape[1]
+        gains = jnp.concatenate([attention_gain, experts_gain])[None, :]
+        packed = jnp.concatenate(
+            [
+                packed,
+                jnp.pad(router_weight.T, ((0, 0), (0, wide - depth))),
+                jnp.pad(gains, ((0, 0), (0, wide - 2 * gain_part))),
+                jnp.zeros((EXTRA - router_part - 1, wide), LOW),
+            ],
+            axis=0,
+        )
         packed_first = send_first(packed)
         packed_second = send_second(packed, packed_first)
-        own = jnp.stack(slot_list(packed, packed_first, packed_second))
+        slots = slot_list(packed, packed_first, packed_second)
         ahead = packed_second
         for expert_at in range(local_experts):
             block = after(shard_blocks[expert_at], ahead)
@@ -1057,14 +1130,23 @@
             firsts.append(first)
             seconds.append(send_second(block, first))
             ahead = first
-        beside, across = flip(own, 2), flip(own, 4)
-        corner = [flip(beside[:2], 4), flip(across[2:], 2)]
-        same = [own, beside, across] + corner
-        pieces = same + [flip(piece, 1) for piece in same]
+        pieces, owns = ([], [])
+        for wave in ((0, 2), (1, 3)):
+            own = jnp.stack([slots[i] for i in wave])
+            if wave[0] == 0:
+                own = after(own, routes_all, info, cosine, sine)
+            beside, across = flip(own, 2), flip(own, 4)
+            same = [own, beside, across, flip(beside[:1], 4), flip(across[1:], 2)]
+            pieces += same + [flip(piece, 1) for piece in same]
+            owns.append(own)
         query_refs = pair_refs = out_refs = pieces
         expert_refs = [
             [shard_blocks[i], seconds[i], *firsts[i]] for i in range(local_experts)
         ]
+        extra_rows = extras(info, pieces)
+        router_all = extra_rows[:, :router_part, :depth]
+        attention_scale = extra_rows[:, router_part, :gain_part]
+        experts_scale = extra_rows[:, router_part, gain_part : 2 * gain_part]
     else:
         packed_all = lax.all_gather(lax.all_gather(packed, "cols", axis=0), "rows", axis=0)
 
@@ -1084,17 +1166,31 @@
             ).reshape(D, -1)
         ]
         out_refs = [unpack(key_at + 2 * key_part, query_part)]
+        axes = ("rows", "cols")
+        router_all = jnp.swapaxes(lax.all_gather(router_weight, axes, axis=0), 1, 2)
+        attention_scale = lax.all_gather(attention_gain, axes, axis=0)
+        experts_scale = lax.all_gather(experts_gain, axes, axis=0)
         expert_refs = [
             [lax.all_gather(block, "cols", axis=0)[i] for i in range(col_count)]
             for block in shard_blocks
         ]
 
-    routes_all = lax.all_gather(routes.T, "rows", axis=0)
+    attention_scale = attention_scale.reshape(1, D).astype(WIDE)
+    experts_scale = experts_scale.reshape(1, D).astype(WIDE)
+    router_rows = jnp.transpose(
+        router_all.reshape(row_count, col_count, router_part, depth), (1, 2, 0, 3)
+    ).reshape(expert_total, D)
+    router_cols = router_rows.T
+    if fast:
+        near_rows = row_place ^ jnp.arange(row_count, dtype=jnp.int32)
+    else:
+        near_rows = jnp.arange(row_count, dtype=jnp.int32)
+    chosen, place_rows = tables(
+        near_rows, info, routes_all, capacity, local_experts, expert_total
+    )
     grad_in = after(cotangent, *pieces) if fast else cotangent
     grad_all = lax.all_gather(grad_in, "rows", axis=0)
 
-    local_index = (1 - parity) * TOK_DEV + jnp.arange(TOK_DEV, dtype=jnp.int32)
-    cosine, sine = rotary_tables(position_of(local_index))
     normed, own_pair = key_value(info, tokens, attention_scale, cosine, sine, pair_refs)
     pairs = [(i + 1, i) for i in range(0, col_count, 2)]
     partner = lax.ppermute(own_pair, "cols", pairs)
@@ -1105,34 +1201,42 @@
     residual, normed_two = out_projection(info, heads, tokens, experts_scale, out_refs)
 
     if fast:
+        beside, across = flip(normed_two, 2), flip(normed_two, 4)
+        beside_in = flip(normed_two, 1)
         grad_all = after(grad_all, normed_two)
-        beside, across = flip(normed_two, 2), flip(normed_two, 4)
-        half = TOK_DEV // 2
-        corner = jnp.concatenate([flip(beside[:half], 4), flip(across[half:], 2)], axis=0)
-        near = [normed_two, beside, across, corner]
-        blocks = [block for one in near for block in (one, flip(one, 1))]
-        turns = [0, 1, 2, 3, 4, 5, 6, 7]
-        places = [row_place ^ q for q in range(row_count)]
     else:
         rows_all = lax.all_gather(normed_two, "rows", axis=0)
-        blocks = [rows_all[q] for q in range(row_count)]
-        turns = list(range(row_count))
-        places = turns
-    router_cols = router_rows.T
-    picked = None
-    for q in turns:
-        order = jnp.stack([jnp.int32(q), jnp.asarray(places[q], jnp.int32)])
-        block = blocks[q]
-        if fast and q == 4:
-            block = after(block, *firsts[1])
-        picked = dispatch(
-            order, info, block, grad_all, routes_all, router_cols, capacity, local_experts, picked
+    grad_rows = pick_rows(near_rows, chosen, grad_all, local_experts)
+
+    def place_block(q, block, picked):
+        order = jnp.stack([jnp.int32(q), near_rows[q]])
+        return dispatch(
+            order, info, block, chosen, routes_all, router_cols, local_experts, picked
         )
+
+    if fast:
+        half = TOK_DEV // 2
+        picked = place_block(0, normed_two, None)
+        picked = place_block(1, beside_in, picked)
+        beside, across = after((beside, across), picked, grad_rows)
+        corner = [flip(beside[:half], 4), flip(across[half:], 2)]
+        picked = place_block(2, beside, picked)
+        picked = place_block(4, across, picked)
+        picked = place_block(3, flip(beside, 1), picked)
+        picked = place_block(5, flip(across, 1), picked)
+        corner = jnp.concatenate(after(corner, picked), axis=0)
+        corner_in = flip(corner, 1)
+        picked = place_block(6, corner, picked)
+        corner_in = after(corner_in, picked, *firsts[1])
+        picked = place_block(7, corner_in, picked)
+    else:
+        picked = None
+        for q in range(row_count):
+            picked = place_block(q, rows_all[q], picked)
     height = row_count * capacity
     token_rows = [a.reshape(height, D) for a in picked[:local_experts]]
-    grad_rows = [a.reshape(height, D) for a in picked[local_experts : 2 * local_experts]]
-    share_rows = [a.reshape(height, 1) for a in picked[2 * local_experts : 3 * local_experts]]
-    chosen, place_rows = picked[-2:]
+    grad_rows = [a.reshape(height, D) for a in grad_rows]
+    share_rows = [a.reshape(height, 1) for a in picked[local_experts:]]
 
     out_rows, back_rows, gate_dots, reduced, marks = ([], [], [], [], [])
     for e in range(local_experts):
@@ -1140,7 +1244,7 @@
         if fast and e == 0:
             rows_in = after(rows_in, seconds[0])
         if fast and e == 1:
-            rows_in = after(rows_in, seconds[1])
+            rows_in = after(rows_in, seconds[1], own_slot, third)
         out_row, back_row, grad_row, acts, dots = expert(
             info, rows_in, grad_rows[e], share_rows[e], expert_refs[e], col_count
         )
@@ -1149,10 +1253,11 @@
         gate_dots.append(dots.reshape(row_count, capacity, 1))
         if fast:
             if e == 1:
-                acts = after(acts, *marks[0])
+                got = flip(combine(chosen, back_rows, 1, 2), 1)
+                acts = after(acts, got, marks[0][0])
             second, fourth = expert_grads(acts, token_rows[e], grad_row, (1, 3))
             sent_first = reduce_first(second, fourth)
-            marks.append([sent_first[0]])
+            marks.append(sent_first)
             own_slot, third = expert_grads(acts, token_rows[e], grad_row, (0, 2))
             sent_second = reduce_second(third, fourth, sent_first[0])
             reduced.append((own_slot, sent_first, sent_second))
@@ -1164,22 +1269,12 @@
 
     spread_dots = spread(place_rows, gate_dots)
     if fast:
-        spread_dots = jnp.take(
-            spread_dots, row_place ^ jnp.arange(row_count, dtype=jnp.int32), axis=0
-        )
+        spread_dots = jnp.take(spread_dots, near_rows, axis=0)
     grad_shares = lax.all_to_all(spread_dots, "rows", split_axis=0, concat_axis=0, tiled=True)
     grad_shares = grad_shares.reshape(expert_total, TOK_DEV)
     if fast:
-        back_rows = [after(a, *reduced[1][0:1]) for a in back_rows]
-
-        def both_ways(rows):
-            got = flip(combine(chosen, rows, 1, 2), 1)
-            return reduce_chips(combine(chosen, rows, 0, 2), got)
-
-        back_parts = both_ways(back_rows)
-        out_rows = [after(a, *back_parts) for a in out_rows]
-        mixture = both_ways(out_rows)
-        grad_shares = after(grad_shares, reduced[0][1][1], *reduced[0][2])
+        back_parts = reduce_chips(combine(chosen, back_rows, 0, 2), got)
+        grad_shares = after(grad_shares, own_slot, third, *reduced[0][1], *reduced[0][2])
     else:
 
         def summed(rows):
@@ -1202,24 +1297,77 @@
         out_refs,
     )
     if fast:
-        grad_heads = after(grad_heads, reduced[1][1][0])
+        out_rows = [after(a, grad_heads) for a in out_rows]
+        out_got = flip(combine(chosen, out_rows, 1, 2), 1)
+        router_parts = jnp.transpose(
+            router_grad.astype(LOW).reshape(col_count, router_part, row_count, depth),
+            (2, 0, 1, 3),
+        ).reshape(row_count * col_count, router_part, depth)
+        gain_rows = experts_gain_grad.astype(LOW).reshape(row_count * col_count, 1, gain_part)
+        extra = jnp.concatenate(
+            [
+                jnp.pad(router_parts, ((0, 0), (0, 0), (0, query_part - depth))),
+                jnp.pad(gain_rows, ((0, 0), (0, 0), (0, query_part - gain_part))),
+                jnp.zeros(
+                    (row_count * col_count, EXTRA - router_part - 1, query_part), LOW
+                ),
+            ],
+            axis=1,
+        )
+        out_keep, out_send = weight_grads(
+            info, [heads], [grad_branch], ((0, 1, query_part),), extra
+        )
+        out_sent = flip(out_send, 1)
     grad_query, own_grad, source_grad = attention_back(
         info, queries, own_pair, partner, grad_heads, cosine, sine
     )
     arrived = lax.ppermute(source_grad.astype(LOW), "cols", [(j, i) for i, j in pairs])
     grad_pair = join_grads(info, own_grad, source_grad, arrived, cosine, sine)
+    if fast:
+        keep, send = weight_grads(
+            info,
+            [normed],
+            [grad_query, grad_pair],
+            ((0, 1, query_part), (0, 2, 2 * key_part)),
+            None,
+        )
+        sent = flip(send, 1)
+        grad_pair = after(grad_pair, keep)
     tokens_grad, attention_gain_grad = token_back(
         info, grad_query, grad_pair, tokens, grad_residual, attention_scale, query_refs, pair_refs
     )
 
-    layer_output = (residual + sum_parts(mixture)).astype(LOW)
     if fast:
-        keep, send = weight_grads(info, normed, heads, grad_query, grad_pair, grad_branch)
-        slots = sum_parts(reduce_chips(keep, flip(send, 1))).astype(LOW)
-        sent_first = reduce_first(slots[1], slots[3])
-        sent_second = reduce_second(slots[2], slots[3], sent_first[0])
-        sums = reduce_last(slots[0], sent_first, sent_second)
+        out_slots = sum_parts(reduce_chips(out_keep, out_sent)).astype(LOW)
+        mixture = reduce_chips(combine(chosen, out_rows, 0, 2), out_got)
+        slots = sum_parts(reduce_chips(keep, sent))
+        own_slots = [owns[0][0], owns[1][0], owns[0][1], owns[1][1]]
+        width = query_part + 2 * key_part
+        gain_sums = sum(
+            jnp.sum(own_slots[i][:depth, :width].astype(WIDE) * slots[i], axis=1)
+            for i in range(4)
+        )
+        own_gains = lax.dynamic_slice_in_dim(attention_scale[0], row_place * depth, depth, 0)
+        gain_sums = (gain_sums / own_gains).reshape(col_count, 1, gain_part)
+        gain_sums = jnp.pad(
+            jnp.take(gain_sums, shards, axis=0),
+            ((0, 0), (0, EXTRA - 1), (0, width - gain_part)),
+        )
+        slots = jnp.concatenate([slots, gain_sums], axis=1).astype(LOW)
+
+        def cols_sum(slots):
+            sent_first = reduce_first(slots[1], slots[3])
+            sent_second = reduce_second(slots[2], slots[3], sent_first[0])
+            return reduce_last(slots[0], sent_first, sent_second)
+
+        out_sums = cols_sum(out_slots)
+        sums = cols_sum(slots)
         expert_sums = [reduce_last(*parts) for parts in reduced]
+        router_sum = out_sums[depth : depth + router_part, :depth].T
+        experts_gain_sum = out_sums[depth + router_part, :gain_part]
+        attention_gain_sum = sums[depth, :gain_part]
+        out_sum = out_sums[:depth]
+        sums = sums[:depth]
     else:
         full_grads = [
             tn(normed, grad_query),
@@ -1236,23 +1384,27 @@
         row_sums = lax.psum_scatter(packed_grad, "rows", scatter_dimension=0)
         sums = lax.psum_scatter(row_sums, "cols", scatter_dimension=1).astype(WIDE)
         expert_sums = reduced
-
-    small_grads = jnp.concatenate(
-        [
-            attention_gain_grad.reshape(-1, gain_part),
-            experts_gain_grad.reshape(-1, gain_part),
-            jnp.transpose(
-                router_grad.reshape(col_count, router_part, row_count, depth), (2, 0, 3, 1)
-            ).reshape(row_count * col_count, depth * router_part),
-        ],
-        axis=1,
-    )
-    small_grads = small_grads.reshape(row_count, -1)
-    small_grads = lax.all_to_all(small_grads, "rows", split_axis=0, concat_axis=0, tiled=True)
-    small_grads = jnp.sum(small_grads, axis=0).reshape(col_count, -1)
-    small_grads = lax.all_to_all(small_grads, "cols", split_axis=0, concat_axis=0, tiled=True)
-    small_sums = jnp.sum(small_grads, axis=0)
-
+        small_grads = jnp.concatenate(
+            [
+                attention_gain_grad.reshape(-1, gain_part),
+                experts_gain_grad.reshape(-1, gain_part),
+                jnp.transpose(
+                    router_grad.reshape(col_count, router_part, row_count, depth), (2, 0, 3, 1)
+                ).reshape(row_count * col_count, depth * router_part),
+            ],
+            axis=1,
+        )
+        small_grads = small_grads.reshape(row_count, -1)
+        small_grads = lax.all_to_all(small_grads, "rows", split_axis=0, concat_axis=0, tiled=True)
+        small_grads = jnp.sum(small_grads, axis=0).reshape(col_count, -1)
+        small_grads = lax.all_to_all(small_grads, "cols", split_axis=0, concat_axis=0, tiled=True)
+        small_sums = jnp.sum(small_grads, axis=0)
+        attention_gain_sum = small_sums[:gain_part]
+        experts_gain_sum = small_sums[gain_part : 2 * gain_part]
+        router_sum = small_sums[2 * gain_part :].reshape(depth, router_part)
+        out_sum = sums[:, query_part + 2 * key_part :]
+
+    layer_output = (residual + sum_parts(mixture)).astype(LOW)
     key_at = query_part
     value_at = key_at + key_part
     out_at = value_at + key_part
@@ -1267,10 +1419,10 @@
         sums[:, :key_at],
         sums[:, key_at:value_at],
         sums[:, value_at:out_at],
-        sums[:, out_at:],
-        small_sums[2 * gain_part :].reshape(depth, router_part),
-        small_sums[:gain_part],
-        small_sums[gain_part : 2 * gain_part],
+        out_sum,
+        router_sum,
+        attention_gain_sum,
+        experts_gain_sum,
         jnp.swapaxes(gate_grad, 1, 2),
         jnp.swapaxes(upward_grad, 1, 2),
         down_grad,

time: 932 us -> 933 us (level)
  blocking collectives: 112 us -> 10.2 us
  waiting for transfers between devices: 267 us -> 349 us
  local copies, waits for them, and re-layouts: 60.7 us -> 40.9 us
  Pallas kernels: 285 us -> 298 us
  other arithmetic: 68.3 us -> 80 us
  starting transfers between devices: 116 us -> 127 us
    all_gather x2 -> x0, blocking collectives: 89.1 us -> none  [the longest x1 79.9 us: on_device(): lax.all_gather(small, 'cols', axis=0)]
    ppermute x3 -> x4, waiting for transfers between devices: 13.4 us -> 73.2 us  [reduce_first(): lax.ppermute(second, 'cols', [(1, 3), (0, 1), (2, 0), (3, 2)])]
    ppermute x3 -> x4, waiting for transfers between devices: 5.09 us -> 61.2 us  [reduce_second(): lax.ppermute(downward_load, 'cols', DOWN)]
    ppermute x3 -> x4, waiting for transfers between devices: 55.8 us -> 0.01 us  [reduce_second(): lax.ppermute(upward_load, 'cols', UP)]
    ppermute x3, waiting for transfers between devices: 2.33 us -> 51.8 us  [send_first(): lax.ppermute(block, 'cols', DOWN)]
    ppermute x3 -> x4, waiting for transfers between devices: 32 us -> 0.01 us  [reduce_first(): lax.ppermute(fourth, 'cols', FAR)]
    ppermute x3, waiting for transfers between devices: 6.17 us -> 31.4 us  [send_second(): return lax.ppermute(payload, 'cols', [(3, 1), (1, 0), (0, 2), (2, 3)])]
    all_to_all x2 -> x1, waiting for transfers between devices: 31.3 us -> 12.1 us  [on_device(): lax.all_to_all(spread_dots, 'rows', split_axis=0, concat_axis=0, tiled=True)]
  transfers between devices with their start and end apart: 61 -> 78, of which waited for: 27 -> 30; matrix products, arithmetic and copies ran while one was open for 12% -> 11% of each run, Pallas kernels for 27% -> 28%
where the time goes in v5:
time: 933 us; the launch traced here: 921 us
  waiting for transfers between devices  349 us (37%)
  Pallas kernels  298 us (32%)
  starting transfers between devices  127 us (14%)
  other arithmetic  80 us (9%)
  local copies, waits for them, and re-layouts  40.9 us (4%)
  between operations  15.9 us (2%)
  blocking collectives  10.2 us (1%)
    ppermute x46, waiting for transfers between devices, flip(): return lax.ppermute(block, 'rows', [(i, i ^ bit) for i in range(count)])  101 us
    ppermute x4, waiting for transfers between devices, reduce_first(): lax.ppermute(second, 'cols', [(1, 3), (0, 1), (2, 0), (3, 2)])  73.2 us
    ppermute x4, waiting for transfers between devices, reduce_second(): lax.ppermute(downward_load, 'cols', DOWN)  61.2 us
    pallas_call x2, Pallas kernels, expert(): pl.pallas_call(functools.partial(expert_kernel, slots), grid=(height // E...  60.5 us
    ppermute x3, waiting for transfers between devices, send_first(): lax.ppermute(block, 'cols', DOWN)  51.8 us
    pallas_call x8, Pallas kernels, dispatch(): pl.pallas_call(functools.partial(dispatch_kernel, local), grid_spec=pltpu...  41.3 us
    pallas_call x4, Pallas kernels, expert_grads(): pl.pallas_call(functools.partial(expert_grads_kernel, slots), grid=(D //...  39.3 us
    ppermute x46, starting transfers between devices, flip(): return lax.ppermute(block, 'rows', [(i, i ^ bit) for i in range(count)])  32.4 us
  transfers between devices with their start and end apart: 78, of which 30 were waited for; matrix products, arithmetic and copies ran while one was open for 11% of the time, Pallas kernels for 28%

profile of v5, /device:TPU:0, one launch (start us, length us, event | category | flops | bytes accessed | tf_op | source)
XLA Modules:
  0.0 920.8 jit_solution(16327869543396872287)
XLA Ops:
  12.4 5.6 collective-permute-start.1
  24.4 10.2 %all-gather.2.routes = s32[8,4,512]{2,1,0:T(4,128)} all-gather(s32[1,4,512]{2,1,0:T(4,128)S(1)} %bitcast.228), channel_id=2, replica_groups=mesh['rows'=8,'cols'=4] {'rows'}, dimensions={0}, use_global_device_ids=true | all-gather | bytes 73728 | tf_op jit(solution)/shard_map/all_gather | solution.py:1102
  41.1 14.2 %collective-permute-done.3.rest_2_.rest_8_.rest_22_ = bf16[2,208,896]{2,1,0:T(8,128)(2,1)S(1)} collective-permute-done((bf16[2,208,896]{2,1,0:T(8,128)(2,1)S(1)}, bf16[2,208,896]{2,1,0:T(8,128)(2,1)S(1)}, u32[]{:S(2)}, u32[]{:S(2)}) %collective-permute-start.3) | collective-permute-done | bytes 745504 | tf_op jit(solution)/shard_map/ppermute | solution.py:1027
  59.7 7.3 collective-permute-done.5.rest_4_.rest_10_.rest_24_
  67.0 16.1 %collective-permute-done.4.rest_3_.rest_9_.rest_23_ = bf16[1,208,896]{2,1,0:T(8,128)(2,1)S(1)} collective-permute-done((bf16[1,208,896]{2,1,0:T(8,128)(2,1)S(1)}, bf16[1,208,896]{2,1,0:T(8,128)(2,1)S(1)}, u32[]{:S(2)}, u32[]{:S(2)}) %collective-permute-start.4) | collective-permute-done | bytes 372768 | tf_op jit(solution)/shard_map/ppermute | solution.py:1027
  87.8 7.2 collective-permute-done.15.rest_13_.rest_19_.rest_33_
  124.3 8.8 query_projection.1.queries
  133.1 51.8 %collective-permute-done.22.rest_2_ = bf16[576,1536]{1,0:T(8,128)(2,1)} collective-permute-done((bf16[576,1536]{1,0:T(8,128)(2,1)S(1)}, bf16[576,1536]{1,0:T(8,128)(2,1)}, u32[]{:S(2)}, u32[]{:S(2)}) %collective-permute-start.22) | collective-permute-done | bytes 1769504 | tf_op jit(solution)/shard_map/ppermute | solution.py:967
  185.2 10.2 %collective-permute-done.25.partner = bf16[512,512]{1,0:T(8,128)(2,1)} collective-permute-done((bf16[512,512]{1,0:T(8,128)(2,1)}, bf16[512,512]{1,0:T(8,128)(2,1)}, u32[]{:S(2)}, u32[]{:S(2)}) %collective-permute-start.25) | collective-permute-done | bytes 524320 | tf_op jit(solution)/shard_map/ppermute | solution.py:1196
  195.4 10.9 %tree_attention.1.heads.rest_0_ = bf16[512,1536]{1,0:T(8,128)(2,1)} custom-call(s32[16]{0:T(128)} %concatenate.43.info, bf16[512,1536]{1,0:T(8,128)(2,1)} %query_projection.1.queries, bf16[512,512]{1,0:T(8,128)(2,1)} %get-tuple-element.105.own, bf16[512,512]{1,0:T(8,128)(2,1)} %collective-permute-done.25.partner), custom_call_target="tpu_custom_call" | custom-call | tf_op jit(solution)/shard_map/tree_attention/pallas_call | solution.py:262
  206.3 10.9 %out_projection.1 = (f32[512,1536]{1,0:T(8,128)}, bf16[512,1536]{1,0:T(8,128)(2,1)}) custom-call(s32[16]{0:T(128)} %concatenate.43.info, bf16[512,1536]{1,0:T(8,128)(2,1)} %tree_attention.1.heads.rest_0_, bf16[512,1536]{1,0:T(8,128)(2,1)} %tokens.5, f32[1,1536]{1,0:T(1,128)} %reshape.492.gain, bf16[2,208,896]{2,1,0:T(8,128)(2,1)} %copy-done, ...), custom_call_target="tpu_custom_call" | custom-call | tf_op jit(solution)/shard_map/out_projection/pallas_call | solution.py:372
  220.8 6.0 collective-permute-start.35
  227.3 6.2 route_tables.1
  245.6 5.2 dispatch.8
  250.8 5.2 dispatch.9
  256.0 13.1 %pick_rows.1 = (bf16[8,160,1536]{2,1,0:T(8,128)(2,1)}, bf16[8,160,1536]{2,1,0:T(8,128)(2,1)}) custom-call(s32[8]{0:T(128)} %iota_xor_fusion.order, bf16[8,320,512]{2,1,0:T(8,128)(2,1)} %get-tuple-element.107.chosen, bf16[8,512,1536]{2,1,0:T(8,128)(2,1)} %bitcast.216), custom_call_target="tpu_custom_call" | custom-call | tf_op jit(solution)/shard_map/pick_rows/pallas_call | solution.py:446
  283.9 5.2 dispatch.10
  289.0 5.2 dispatch.11
  294.8 5.2 dispatch.12
  312.8 5.2 dispatch.14
  317.9 7.8 collective-permute-done.36.rest_4_
  325.7 5.2 dispatch.15
  330.9 31.4 %collective-permute-done.37.rest_1_ = bf16[576,1536]{1,0:T(8,128)(2,1)} collective-permute-done((bf16[576,1536]{1,0:T(8,128)(2,1)}, bf16[576,1536]{1,0:T(8,128)(2,1)}, u32[]{:S(2)}, u32[]{:S(2)}) %collective-permute-start.37) | collective-permute-done | bytes 1769504 | tf_op jit(solution)/shard_map/ppermute | solution.py:977
  362.3 30.2 %expert.2 = (bf16[1280,1536]{1,0:T(8,128)(2,1)}, bf16[1280,1536]{1,0:T(8,128)(2,1)}, bf16[1280,1536]{1,0:T(8,128)(2,1)}, bf16[4,576,1280]{2,1,0:T(8,128)(2,1)}, f32[1280,1]{1,0:T(8,128)}) custom-call(s32[16]{0:T(128)} %concatenate.43.info, bf16[1280,1536]{1,0:T(8,128)(2,1)} %bitcast.196, bf16[1280,1536]{1,0:T(8,128)(2,1)} %bitcast.218, f32[1280,1]{1,0:T(8,128)} %bitcast.202, ...), custom_call_target="tpu_custom_call" | custom-call | tf_op jit(solution)/shard_map/expert/pallas_call | solution.py:638
  392.5 9.8 %expert_gradients.4 = (bf16[576,1536]{1,0:T(8,128)(2,1)}, bf16[576,1536]{1,0:T(8,128)(2,1)}) custom-call(bf16[1280,1536]{1,0:T(8,128)(2,1)} %bitcast.197, bf16[1280,1536]{1,0:T(8,128)(2,1)} %get-tuple-element.154.grads, bf16[4,576,1280]{2,1,0:T(8,128)(2,1)} %get-tuple-element.155.rest_0_.rest_1_, bf16[4,576,1280]{2,1,0:T(8,128)(2,1)} %get-tuple-element.155.rest_0_.rest_1_), custom_call_target="tpu_custom_call" | custom-call | tf_op jit(solution)/shard_map/expert_gradients/pallas_call | solution.py:665
  403.5 30.2 %expert.3 = (bf16[1280,1536]{1,0:T(8,128)(2,1)}, bf16[1280,1536]{1,0:T(8,128)(2,1)}, bf16[1280,1536]{1,0:T(8,128)(2,1)}, bf16[4,576,1280]{2,1,0:T(8,128)(2,1)}, f32[1280,1]{1,0:T(8,128)}) custom-call(s32[16]{0:T(128)} %concatenate.43.info, bf16[1280,1536]{1,0:T(8,128)(2,1)} %bitcast.199, bf16[1280,1536]{1,0:T(8,128)(2,1)} %bitcast.217, f32[1280,1]{1,0:T(8,128)} %bitcast.203, ...), custom_call_target="tpu_custom_call" | custom-call | tf_op jit(solution)/shard_map/expert/pallas_call | solution.py:638
  433.8 7.5 combine.4
  441.2 9.8 %expert_gradients.5 = (bf16[576,1536]{1,0:T(8,128)(2,1)}, bf16[576,1536]{1,0:T(8,128)(2,1)}) custom-call(bf16[1280,1536]{1,0:T(8,128)(2,1)} %bitcast.198, bf16[1280,1536]{1,0:T(8,128)(2,1)} %get-tuple-element.154.grads, bf16[4,576,1280]{2,1,0:T(8,128)(2,1)} %get-tuple-element.155.rest_0_.rest_1_, bf16[4,576,1280]{2,1,0:T(8,128)(2,1)} %get-tuple-element.155.rest_0_.rest_1_), custom_call_target="tpu_custom_call" | custom-call | tf_op jit(solution)/shard_map/expert_gradients/pallas_call | solution.py:665
  451.0 12.8 %collective-permute-start.40 = (bf16[576,1536]{1,0:T(8,128)(2,1)}, bf16[576,1536]{1,0:T(8,128)(2,1)S(1)}, u32[]{:S(2)}, u32[]{:S(2)}) collective-permute-start(bf16[576,1536]{1,0:T(8,128)(2,1)} %get-tuple-element.165), channel_id=1, source_target_pairs={{1,3},{0,1},{2,0},{3,2},{5,7},{4,5},{6,4},{7,6},{9,11},{8,9},{10,8... | collective-permute-start | bytes 5308424 | tf_op jit(solution)/shard_map/ppermute | solution.py:994
  463.8 7.5 combine.5
  473.3 68.6 %collective-permute-done.40 = bf16[576,1536]{1,0:T(8,128)(2,1)S(1)} collective-permute-done((bf16[576,1536]{1,0:T(8,128)(2,1)}, bf16[576,1536]{1,0:T(8,128)(2,1)S(1)}, u32[]{:S(2)}, u32[]{:S(2)}) %collective-permute-start.40) | collective-permute-done | bytes 1769504 | tf_op jit(solution)/shard_map/ppermute | solution.py:994
  541.8 5.6 fusion.3
  557.7 5.6 spread.1
  568.8 9.8 %expert_gradients.7 = (bf16[576,1536]{1,0:T(8,128)(2,1)}, bf16[576,1536]{1,0:T(8,128)(2,1)}) custom-call(bf16[1280,1536]{1,0:T(8,128)(2,1)} %bitcast.200, bf16[1280,1536]{1,0:T(8,128)(2,1)} %get-tuple-element.161.grads, bf16[4,576,1280]{2,1,0:T(8,128)(2,1)} %get-tuple-element.166.rest_0_.rest_1_, bf16[4,576,1280]{2,1,0:T(8,128)(2,1)} %get-tuple-element.166.rest_0_.rest_1_), custom_call_target="tpu_custom_call" | custom-call | tf_op jit(solution)/shard_map/expert_gradients/pallas_call | solution.py:665
  581.4 12.1 %all-to-all-done = f32[8,2,512]{2,1,0:T(2,128)S(1)} async-done(((f32[8,2,512]{2,1,0:T(2,128)}), f32[8,2,512]{2,1,0:T(2,128)S(1)}, u32[]{:S(2)}, u32[]{:S(2)}) %all-to-all-start) | async-done | bytes 32800 | tf_op jit(solution)/shard_map/all_to_all | solution.py:1273
  594.1 9.9 %expert_gradients.6 = (bf16[576,1536]{1,0:T(8,128)(2,1)}, bf16[576,1536]{1,0:T(8,128)(2,1)}) custom-call(bf16[1280,1536]{1,0:T(8,128)(2,1)} %bitcast.201, bf16[1280,1536]{1,0:T(8,128)(2,1)} %get-tuple-element.161.grads, bf16[4,576,1280]{2,1,0:T(8,128)(2,1)} %get-tuple-element.166.rest_0_.rest_1_, bf16[4,576,1280]{2,1,0:T(8,128)(2,1)} %get-tuple-element.166.rest_0_.rest_1_), custom_call_target="tpu_custom_call" | custom-call | tf_op jit(solution)/shard_map/expert_gradients/pallas_call | solution.py:665
  608.4 60.6 %collective-permute-done.43 = bf16[576,1536]{1,0:T(8,128)(2,1)} collective-permute-done((bf16[576,1536]{1,0:T(8,128)(2,1)}, bf16[576,1536]{1,0:T(8,128)(2,1)}, u32[]{:S(2)}, u32[]{:S(2)}) %collective-permute-start.43) | collective-permute-done | bytes 1769504 | tf_op jit(solution)/shard_map/ppermute | solution.py:1008
  689.1 13.4 %experts_norm_back.1 = (f32[512,1536]{1,0:T(8,128)}, bf16[512,1536]{1,0:T(8,128)(2,1)}, bf16[512,1536]{1,0:T(8,128)(2,1)}, f32[1,1536]{1,0:T(1,128)}, f32[16,1536]{1,0:T(8,128)}) custom-call(s32[16]{0:T(128)} %concatenate.43.info, f32[512,1536]{1,0:T(8,128)} %get-tuple-element.106.residual, bf16[512,1536]{1,0:T(8,128)(2,1)} %get-tuple-element.108.rows.normed, ...), custom_call_target="tpu_custom_call" | custom-call | tf_op jit(solution)/shard_map/experts_norm_back/pallas_call | solution.py:765
  705.2 8.1 weight_gradients.3
  714.2 15.5 %tree_attention_back.1 = (bf16[512,1536]{1,0:T(8,128)(2,1)}, f32[512,512]{1,0:T(8,128)}, f32[512,512]{1,0:T(8,128)}) custom-call(s32[16]{0:T(128)} %concatenate.43.info, bf16[512,1536]{1,0:T(8,128)(2,1)} %query_projection.1.queries, bf16[512,512]{1,0:T(8,128)(2,1)} %get-tuple-element.105.own, bf16[512,512]{1,0:T(8,128)(2,1)} %collective-permute-done.25.partner, ...), custom_call_target="tpu_custom_call" | custom-call | tf_op jit(solution)/shard_map/tree_attention_back/pallas_call | solution.py:322
  731.8 5.6 collective-permute-start.53
  741.1 7.5 combine.7
  751.9 10.1 %weight_gradients.2 = (bf16[4,4,192,512]{3,2,1,0:T(8,128)(2,1)}, bf16[4,4,192,512]{3,2,1,0:T(8,128)(2,1)}) custom-call(s32[16]{0:T(128)} %concatenate.43.info, bf16[512,1536]{1,0:T(8,128)(2,1)} %get-tuple-element.102.normed.rest_0_, bf16[512,1536]{1,0:T(8,128)(2,1)} %get-tuple-element.175.rest_1_.grad_query, ...), custom_call_target="tpu_custom_call" | custom-call | tf_op jit(solution)/shard_map/weight_gradients/pallas_call | solution.py:914
  762.6 7.4 combine.6
  770.0 13.5 %token_gradient.1 = (bf16[512,1536]{1,0:T(8,128)(2,1)}, f32[1,1536]{1,0:T(1,128)}) custom-call(s32[16]{0:T(128)} %concatenate.43.info, bf16[512,1536]{1,0:T(8,128)(2,1)} %get-tuple-element.175.rest_1_.grad_query, bf16[512,512]{1,0:T(8,128)(2,1)} %join_key_value_gradients.1.rest_2_.grad_pair, bf16[512,1536]{1,0:T(8,128)(2,1)} %tokens.5, ...), custom_call_target="tpu_custom_call" | custom-call | tf_op jit(solution)/shard_map/token_gradient/pallas_call | solution.py:854
  795.3 10.9 %collective-permute-done.64 = bf16[2,2,208,384]{3,2,1,0:T(8,128)(2,1)S(1)} collective-permute-done((bf16[2,2,208,384]{3,2,1,0:T(8,128)(2,1)S(1)}, bf16[2,2,208,384]{3,2,1,0:T(8,128)(2,1)S(1)}, u32[]{:S(2)}, u32[]{:S(2)}) %collective-permute-start.64) | collective-permute-done | bytes 639008 | tf_op jit(solution)/shard_map/ppermute | solution.py:1027
  870.9 15.4 %collective-permute-done.51 = bf16[2,256,1536]{2,1,0:T(8,128)(2,1)S(1)} collective-permute-done((bf16[2,256,1536]{2,1,0:T(8,128)(2,1)}, bf16[2,256,1536]{2,1,0:T(8,128)(2,1)S(1)}, u32[]{:S(2)}, u32[]{:S(2)}) %collective-permute-start.51) | collective-permute-done | bytes 1572896 | tf_op jit(solution)/shard_map/ppermute | solution.py:1027
  898.8 9.2 %collective-permute-done.50 = bf16[256,1536]{1,0:T(8,128)(2,1)S(1)} collective-permute-done((bf16[256,1536]{1,0:T(8,128)(2,1)}, bf16[256,1536]{1,0:T(8,128)(2,1)S(1)}, u32[]{:S(2)}, u32[]{:S(2)}) %collective-permute-start.50) | collective-permute-done | bytes 786464 | tf_op jit(solution)/shard_map/ppermute | solution.py:1027
  (389 shorter events, 254.3 us)
Async XLA Ops:
  7.2 248.8 %all-gather.5.cloned.1.call-start = ((), (), s32[]{:S(2)}) async-start(), calls=%async_computation.1 | async-start | bytes 14155776 | tf_op jit(solution)/shard_map/all_gather | solution.py:1192
  11.1 24.7 %collective-permute-start = (bf16[208,896]{1,0:T(8,128)(2,1)S(1)}, bf16[208,896]{1,0:T(8,128)(2,1)S(1)}, u32[]{:S(2)}, u32[]{:S(2)}) collective-permute-start(bf16[208,896]{1,0:T(8,128)(2,1)S(1)} %fusion.50), channel_id=1, source_target_pairs={{1,0},{2,1},{3,2},{5,4},{6,5},{7,6},{9,8},{10,9},{11,10},{13,12},{... | collective-permute-start | bytes 1118216 | tf_op jit(solution)/shard_map/ppermute | solution.py:967
  12.4 23.4 %collective-permute-start.1 = (bf16[208,896]{1,0:T(8,128)(2,1)S(1)}, bf16[208,896]{1,0:T(8,128)(2,1)S(1)}, u32[]{:S(2)}, u32[]{:S(2)}) collective-permute-start(bf16[208,896]{1,0:T(8,128)(2,1)S(1)} %fusion.50), channel_id=1, source_target_pairs={{0,1},{1,2},{2,3},{4,5},{5,6},{6,7},{8,9},{9,10},{10,11},{12,13},{... | collective-permute-start | bytes 1118216 | tf_op jit(solution)/shard_map/ppermute | solution.py:968
  36.3 19.0 %collective-permute-start.3 = (bf16[2,208,896]{2,1,0:T(8,128)(2,1)S(1)}, bf16[2,208,896]{2,1,0:T(8,128)(2,1)S(1)}, u32[]{:S(2)}, u32[]{:S(2)}) collective-permute-start(bf16[2,208,896]{2,1,0:T(8,128)(2,1)S(1)} %pad_maximum_fusion.9.rest_0_.rest_6_.rest_20_), channel_id=1, source_target_pairs={{0,16},{4,20},{8,24},{12,28},{16,0},{20,4},{24,8},{28,12},{1,17},{... | collective-permute-start | bytes 2236424 | tf_op jit(solution)/shard_map/ppermute | solution.py:1027
  37.8 21.2 %collective-permute-start.2 = (bf16[2,208,896]{2,1,0:T(8,128)(2,1)S(1)}, bf16[2,208,896]{2,1,0:T(8,128)(2,1)S(1)}, u32[]{:S(2)}, u32[]{:S(2)}) collective-permute-start(bf16[2,208,896]{2,1,0:T(8,128)(2,1)S(1)} %pad_maximum_fusion.9.rest_0_.rest_6_.rest_20_), channel_id=1, source_target_pairs={{0,8},{4,12},{8,0},{12,4},{16,24},{20,28},{24,16},{28,20},{1,9},{5... | collective-permute-start | bytes 2236424 | tf_op jit(solution)/shard_map/ppermute | solution.py:1027
  38.4 18.3 %collective-permute-start.11 = (bf16[208,896]{1,0:T(8,128)(2,1)S(1)}, bf16[208,896]{1,0:T(8,128)(2,1)S(1)}, u32[]{:S(2)}, u32[]{:S(2)}) collective-permute-start(bf16[208,896]{1,0:T(8,128)(2,1)S(1)} %get-tuple-element.290), channel_id=1, source_target_pairs={{3,1},{1,0},{0,2},{2,3},{7,5},{5,4},{4,6},{6,7},{11,9},{9,8},{8,10... | collective-permute-start | bytes 1118216 | tf_op jit(solution)/shard_map/ppermute | solution.py:977
  56.9 26.2 %collective-permute-start.13 = (bf16[2,208,896]{2,1,0:T(8,128)(2,1)S(1)}, bf16[2,208,896]{2,1,0:T(8,128)(2,1)S(1)}, u32[]{:S(2)}, u32[]{:S(2)}) collective-permute-start(bf16[2,208,896]{2,1,0:T(8,128)(2,1)S(1)} %pad_maximum_fusion.10.rest_10_.rest_16_.rest_30_), channel_id=1, source_target_pairs={{0,8},{4,12},{8,0},{12,4},{16,24},{20,28},{24,16},{28,20},{1,9},{5... | collective-permute-start | bytes 2236424 | tf_op jit(solution)/shard_map/ppermute | solution.py:1027
  57.5 26.0 %collective-permute-start.14 = (bf16[2,208,896]{2,1,0:T(8,128)(2,1)S(1)}, bf16[2,208,896]{2,1,0:T(8,128)(2,1)S(1)}, u32[]{:S(2)}, u32[]{:S(2)}) collective-permute-start(bf16[2,208,896]{2,1,0:T(8,128)(2,1)S(1)} %pad_maximum_fusion.10.rest_10_.rest_16_.rest_30_), channel_id=1, source_target_pairs={{0,16},{4,20},{8,24},{12,28},{16,0},{20,4},{24,8},{28,12},{1,17},{... | collective-permute-start | bytes 2236424 | tf_op jit(solution)/shard_map/ppermute | solution.py:1027
  59.0 24.0 %collective-permute-start.4 = (bf16[1,208,896]{2,1,0:T(8,128)(2,1)S(1)}, bf16[1,208,896]{2,1,0:T(8,128)(2,1)S(1)}, u32[]{:S(2)}, u32[]{:S(2)}) collective-permute-start(bf16[1,208,896]{2,1,0:T(8,128)(2,1)S(1)} %slice.742), channel_id=1, source_target_pairs={{0,16},{4,20},{8,24},{12,28},{16,0},{20,4},{24,8},{28,12},{1,17},{... | collective-permute-start | bytes 1118216 | tf_op jit(solution)/shard_map/ppermute | solution.py:1027
  59.7 24.1 %collective-permute-start.6 = (bf16[2,208,896]{2,1,0:T(8,128)(2,1)S(1)}, bf16[2,208,896]{2,1,0:T(8,128)(2,1)S(1)}, u32[]{:S(2)}, u32[]{:S(2)}) collective-permute-start(bf16[2,208,896]{2,1,0:T(8,128)(2,1)S(1)} %pad_maximum_fusion.9.rest_0_.rest_6_.rest_20_), channel_id=1, source_target_pairs={{0,4},{4,0},{8,12},{12,8},{16,20},{20,16},{24,28},{28,24},{1,5},{5... | collective-permute-start | bytes 2236424 | tf_op jit(solution)/shard_map/ppermute | solution.py:1027
  103.6 81.4 %collective-permute-start.22 = (bf16[576,1536]{1,0:T(8,128)(2,1)S(1)}, bf16[576,1536]{1,0:T(8,128)(2,1)}, u32[]{:S(2)}, u32[]{:S(2)}) collective-permute-start(bf16[576,1536]{1,0:T(8,128)(2,1)S(1)} %pad_maximum_fusion.1.rest_0_), channel_id=1, source_target_pairs={{1,0},{2,1},{3,2},{5,4},{6,5},{7,6},{9,8},{10,9},{11,10},{13,12},{... | collective-permute-start | bytes 5308424 | tf_op jit(solution)/shard_map/ppermute | solution.py:967
  104.9 80.1 %collective-permute-start.23 = (bf16[576,1536]{1,0:T(8,128)(2,1)S(1)}, bf16[576,1536]{1,0:T(8,128)(2,1)S(1)}, u32[]{:S(2)}, u32[]{:S(2)}) collective-permute-start(bf16[576,1536]{1,0:T(8,128)(2,1)S(1)} %pad_maximum_fusion.1.rest_0_), channel_id=1, source_target_pairs={{0,1},{1,2},{2,3},{4,5},{5,6},{6,7},{8,9},{9,10},{10,11},{12,13},{... | collective-permute-start | bytes 5308424 | tf_op jit(solution)/shard_map/ppermute | solution.py:968
  109.5 75.7 %collective-permute-start.24 = (bf16[576,1536]{1,0:T(8,128)(2,1)S(1)}, bf16[576,1536]{1,0:T(8,128)(2,1)}, u32[]{:S(2)}, u32[]{:S(2)}) collective-permute-start(bf16[576,1536]{1,0:T(8,128)(2,1)S(1)} %pad_maximum_fusion.1.rest_0_), channel_id=1, source_target_pairs={{0,3},{3,0},{4,7},{7,4},{8,11},{11,8},{12,15},{15,12},{16,19},{19,... | collective-permute-start | bytes 5308424 | tf_op jit(solution)/shard_map/ppermute | solution.py:969
  122.3 73.1 %collective-permute-start.25 = (bf16[512,512]{1,0:T(8,128)(2,1)}, bf16[512,512]{1,0:T(8,128)(2,1)}, u32[]{:S(2)}, u32[]{:S(2)}) collective-permute-start(bf16[512,512]{1,0:T(8,128)(2,1)} %get-tuple-element.105.own), channel_id=1, source_target_pairs={{1,0},{3,2},{5,4},{7,6},{9,8},{11,10},{13,12},{15,14},{17,16},{19,... | collective-permute-start | bytes 1572872 | tf_op jit(solution)/shard_map/ppermute | solution.py:1196
  217.3 33.6 %collective-permute-start.28 = (bf16[512,1536]{1,0:T(8,128)(2,1)}, bf16[512,1536]{1,0:T(8,128)(2,1)}, u32[]{:S(2)}, u32[]{:S(2)}) collective-permute-start(bf16[512,1536]{1,0:T(8,128)(2,1)} %get-tuple-element.108.rows.normed), channel_id=1, source_target_pairs={{0,4},{4,0},{8,12},{12,8},{16,20},{20,16},{24,28},{28,24},{1,5},{5... | collective-permute-start | bytes 4718600 | tf_op jit(solution)/shard_map/ppermute | solution.py:1027
  217.3 51.8 %collective-permute-start.26 = (bf16[512,1536]{1,0:T(8,128)(2,1)}, bf16[512,1536]{1,0:T(8,128)(2,1)}, u32[]{:S(2)}, u32[]{:S(2)}) collective-permute-start(bf16[512,1536]{1,0:T(8,128)(2,1)} %get-tuple-element.108.rows.normed), channel_id=1, source_target_pairs={{0,8},{4,12},{8,0},{12,4},{16,24},{20,28},{24,16},{28,20},{1,9},{5... | collective-permute-start | bytes 4718600 | tf_op jit(solution)/shard_map/ppermute | solution.py:1027
  218.8 50.3 %collective-permute-start.27 = (bf16[512,1536]{1,0:T(8,128)(2,1)}, bf16[512,1536]{1,0:T(8,128)(2,1)}, u32[]{:S(2)}, u32[]{:S(2)}) collective-permute-start(bf16[512,1536]{1,0:T(8,128)(2,1)} %get-tuple-element.108.rows.normed), channel_id=1, source_target_pairs={{0,16},{4,20},{8,24},{12,28},{16,0},{20,4},{24,8},{28,12},{1,17},{... | collective-permute-start | bytes 4718600 | tf_op jit(solution)/shard_map/ppermute | solution.py:1027
  219.5 59.0 %collective-permute-start.34 = (bf16[576,1536]{1,0:T(8,128)(2,1)S(1)}, bf16[576,1536]{1,0:T(8,128)(2,1)}, u32[]{:S(2)}, u32[]{:S(2)}) collective-permute-start(bf16[576,1536]{1,0:T(8,128)(2,1)S(1)} %pad_maximum_fusion.2.rest_0_), channel_id=1, source_target_pairs={{1,0},{2,1},{3,2},{5,4},{6,5},{7,6},{9,8},{10,9},{11,10},{13,12},{... | collective-permute-start | bytes 5308424 | tf_op jit(solution)/shard_map/ppermute | solution.py:967
  220.8 59.7 %collective-permute-start.35 = (bf16[576,1536]{1,0:T(8,128)(2,1)S(1)}, bf16[576,1536]{1,0:T(8,128)(2,1)}, u32[]{:S(2)}, u32[]{:S(2)}) collective-permute-start(bf16[576,1536]{1,0:T(8,128)(2,1)S(1)} %pad_maximum_fusion.2.rest_0_), channel_id=1, source_target_pairs={{0,1},{1,2},{2,3},{4,5},{5,6},{6,7},{8,9},{9,10},{10,11},{12,13},{... | collective-permute-start | bytes 5308424 | tf_op jit(solution)/shard_map/ppermute | solution.py:968
  269.1 25.1 %collective-permute-start.32 = (bf16[512,1536]{1,0:T(8,128)(2,1)}, bf16[512,1536]{1,0:T(8,128)(2,1)}, u32[]{:S(2)}, u32[]{:S(2)}) collective-permute-start(bf16[512,1536]{1,0:T(8,128)(2,1)} %collective-permute-done.26.rows), channel_id=1, source_target_pairs={{0,4},{4,0},{8,12},{12,8},{16,20},{20,16},{24,28},{28,24},{1,5},{5... | collective-permute-start | bytes 4718600 | tf_op jit(solution)/shard_map/ppermute | solution.py:1027
  269.2 30.8 %collective-permute-start.31 = (bf16[512,1536]{1,0:T(8,128)(2,1)}, bf16[512,1536]{1,0:T(8,128)(2,1)}, u32[]{:S(2)}, u32[]{:S(2)}) collective-permute-start(bf16[512,1536]{1,0:T(8,128)(2,1)} %collective-permute-done.27.rows), channel_id=1, source_target_pairs={{0,4},{4,0},{8,12},{12,8},{16,20},{20,16},{24,28},{28,24},{1,5},{5... | collective-permute-start | bytes 4718600 | tf_op jit(solution)/shard_map/ppermute | solution.py:1027
  276.9 32.2 %collective-permute-start.29 = (bf16[256,1536]{1,0:T(8,128)(2,1)}, bf16[256,1536]{1,0:T(8,128)(2,1)}, u32[]{:S(2)}, u32[]{:S(2)}) collective-permute-start(bf16[256,1536]{1,0:T(8,128)(2,1)} %slice.617), channel_id=1, source_target_pairs={{0,16},{4,20},{8,24},{12,28},{16,0},{20,4},{24,8},{28,12},{1,17},{... | collective-permute-start | bytes 2359304 | tf_op jit(solution)/shard_map/ppermute | solution.py:1027
  278.4 30.6 %collective-permute-start.30 = (bf16[256,1536]{1,0:T(8,128)(2,1)}, bf16[256,1536]{1,0:T(8,128)(2,1)}, u32[]{:S(2)}, u32[]{:S(2)}) collective-permute-start(bf16[256,1536]{1,0:T(8,128)(2,1)} %slice.618), channel_id=1, source_target_pairs={{0,8},{4,12},{8,0},{12,4},{16,24},{20,28},{24,16},{28,20},{1,9},{5... | collective-permute-start | bytes 2359304 | tf_op jit(solution)/shard_map/ppermute | solution.py:1027
  280.5 45.3 %collective-permute-start.36 = (bf16[576,1536]{1,0:T(8,128)(2,1)S(1)}, bf16[576,1536]{1,0:T(8,128)(2,1)S(1)}, u32[]{:S(2)}, u32[]{:S(2)}) collective-permute-start(bf16[576,1536]{1,0:T(8,128)(2,1)S(1)} %pad_maximum_fusion.2.rest_0_), channel_id=1, source_target_pairs={{0,3},{3,0},{4,7},{7,4},{8,11},{11,8},{12,15},{15,12},{16,19},{19,... | collective-permute-start | bytes 5308424 | tf_op jit(solution)/shard_map/ppermute | solution.py:969
  294.2 68.1 %collective-permute-start.37 = (bf16[576,1536]{1,0:T(8,128)(2,1)}, bf16[576,1536]{1,0:T(8,128)(2,1)}, u32[]{:S(2)}, u32[]{:S(2)}) collective-permute-start(bf16[576,1536]{1,0:T(8,128)(2,1)} %select_select_fusion.1), channel_id=1, source_target_pairs={{3,1},{1,0},{0,2},{2,3},{7,5},{5,4},{4,6},{6,7},{11,9},{9,8},{8,10... | collective-permute-start | bytes 5308424 | tf_op jit(solution)/shard_map/ppermute | solution.py:977
  300.0 102.3 %collective-permute-start.38 = (bf16[576,1536]{1,0:T(8,128)(2,1)}, bf16[576,1536]{1,0:T(8,128)(2,1)S(1)}, u32[]{:S(2)}, u32[]{:S(2)}) collective-permute-start(bf16[576,1536]{1,0:T(8,128)(2,1)} %select_select_fusion), channel_id=1, source_target_pairs={{3,1},{1,0},{0,2},{2,3},{7,5},{5,4},{4,6},{6,7},{11,9},{9,8},{8,10... | collective-permute-start | bytes 5308424 | tf_op jit(solution)/shard_map/ppermute | solution.py:977
  441.2 110.1 %collective-permute-start.39 = (bf16[4,512,1536]{2,1,0:T(8,128)(2,1)}, bf16[4,512,1536]{2,1,0:T(8,128)(2,1)S(1)}, u32[]{:S(2)}, u32[]{:S(2)}) collective-permute-start(bf16[4,512,1536]{2,1,0:T(8,128)(2,1)} %combine.4), channel_id=1, source_target_pairs={{0,4},{4,0},{8,12},{12,8},{16,20},{20,16},{24,28},{28,24},{1,5},{5... | collective-permute-start | bytes 18874376 | tf_op jit(solution)/shard_map/ppermute | solution.py:1027
  451.0 90.8 %collective-permute-start.40 = (bf16[576,1536]{1,0:T(8,128)(2,1)}, bf16[576,1536]{1,0:T(8,128)(2,1)S(1)}, u32[]{:S(2)}, u32[]{:S(2)}) collective-permute-start(bf16[576,1536]{1,0:T(8,128)(2,1)} %get-tuple-element.165), channel_id=1, source_target_pairs={{1,3},{0,1},{2,0},{3,2},{5,7},{4,5},{6,4},{7,6},{9,11},{8,9},{10,8... | collective-permute-start | bytes 5308424 | tf_op jit(solution)/shard_map/ppermute | solution.py:994
  471.3 107.2 %collective-permute-start.41 = (bf16[576,1536]{1,0:T(8,128)(2,1)}, bf16[576,1536]{1,0:T(8,128)(2,1)}, u32[]{:S(2)}, u32[]{:S(2)}) collective-permute-start(bf16[576,1536]{1,0:T(8,128)(2,1)} %get-tuple-element.169), channel_id=1, source_target_pairs={{0,3},{3,0},{4,7},{7,4},{8,11},{11,8},{12,15},{15,12},{16,19},{19,... | collective-permute-start | bytes 5308424 | tf_op jit(solution)/shard_map/ppermute | solution.py:995
  547.4 56.6 %collective-permute-start.42 = (bf16[576,1536]{1,0:T(8,128)(2,1)}, bf16[576,1536]{1,0:T(8,128)(2,1)}, u32[]{:S(2)}, u32[]{:S(2)}) collective-permute-start(bf16[576,1536]{1,0:T(8,128)(2,1)} %get-tuple-element.277), channel_id=1, source_target_pairs={{0,1},{1,2},{2,3},{4,5},{5,6},{6,7},{8,9},{9,10},{10,11},{12,13},{... | collective-permute-start | bytes 5308424 | tf_op jit(solution)/shard_map/ppermute | solution.py:1007
  550.0 119.0 %collective-permute-start.43 = (bf16[576,1536]{1,0:T(8,128)(2,1)}, bf16[576,1536]{1,0:T(8,128)(2,1)}, u32[]{:S(2)}, u32[]{:S(2)}) collective-permute-start(bf16[576,1536]{1,0:T(8,128)(2,1)} %get-tuple-element.276), channel_id=1, source_target_pairs={{1,0},{2,1},{3,2},{5,4},{6,5},{7,6},{9,8},{10,9},{11,10},{13,12},{... | collective-permute-start | bytes 5308424 | tf_op jit(solution)/shard_map/ppermute | solution.py:1008
  554.4 114.5 %collective-permute-start.44 = (bf16[2,256,1536]{2,1,0:T(8,128)(2,1)}, bf16[2,256,1536]{2,1,0:T(8,128)(2,1)}, u32[]{:S(2)}, u32[]{:S(2)}) collective-permute-start(bf16[2,256,1536]{2,1,0:T(8,128)(2,1)} %pad_maximum_fusion.3), channel_id=1, source_target_pairs={{0,8},{4,12},{8,0},{12,4},{16,24},{20,28},{24,16},{28,20},{1,9},{5... | collective-permute-start | bytes 4718600 | tf_op jit(solution)/shard_map/ppermute | solution.py:1027
  557.2 111.8 %collective-permute-start.46 = (bf16[2,256,1536]{2,1,0:T(8,128)(2,1)}, bf16[2,256,1536]{2,1,0:T(8,128)(2,1)}, u32[]{:S(2)}, u32[]{:S(2)}) collective-permute-start(bf16[2,256,1536]{2,1,0:T(8,128)(2,1)} %pad_maximum_fusion.4), channel_id=1, source_target_pairs={{0,16},{4,20},{8,24},{12,28},{16,0},{20,4},{24,8},{28,12},{1,17},{... | collective-permute-start | bytes 4718600 | tf_op jit(solution)/shard_map/ppermute | solution.py:1027
  565.4 28.1 %all-to-all-start = ((f32[8,2,512]{2,1,0:T(2,128)}), f32[8,2,512]{2,1,0:T(2,128)S(1)}, u32[]{:S(2)}, u32[]{:S(2)}) async-start(f32[8,2,512]{2,1,0:T(2,128)} %broadcast_select_fusion.1), calls=%async_computation | async-start | bytes 65536 | tf_op jit(solution)/shard_map/all_to_all | solution.py:1273
  578.6 101.2 %collective-permute-start.72 = (bf16[576,1536]{1,0:T(8,128)(2,1)}, bf16[576,1536]{1,0:T(8,128)(2,1)}, u32[]{:S(2)}, u32[]{:S(2)}) collective-permute-start(bf16[576,1536]{1,0:T(8,128)(2,1)} %get-tuple-element.189), channel_id=1, source_target_pairs={{1,3},{0,1},{2,0},{3,2},{5,7},{4,5},{6,4},{7,6},{9,11},{8,9},{10,8... | collective-permute-start | bytes 5308424 | tf_op jit(solution)/shard_map/ppermute | solution.py:994
  604.1 158.0 %collective-permute-start.75 = (bf16[576,1536]{1,0:T(8,128)(2,1)}, bf16[576,1536]{1,0:T(8,128)(2,1)}, u32[]{:S(2)}, u32[]{:S(2)}) collective-permute-start(bf16[576,1536]{1,0:T(8,128)(2,1)} %get-tuple-element.188), channel_id=1, source_target_pairs={{0,3},{3,0},{4,7},{7,4},{8,11},{11,8},{12,15},{15,12},{16,19},{19,... | collective-permute-start | bytes 5308424 | tf_op jit(solution)/shard_map/ppermute | solution.py:995
  684.1 99.4 %collective-permute-start.73 = (bf16[576,1536]{1,0:T(8,128)(2,1)}, bf16[576,1536]{1,0:T(8,128)(2,1)}, u32[]{:S(2)}, u32[]{:S(2)}) collective-permute-start(bf16[576,1536]{1,0:T(8,128)(2,1)} %get-tuple-element.274), channel_id=1, source_target_pairs={{0,1},{1,2},{2,3},{4,5},{5,6},{6,7},{8,9},{9,10},{10,11},{12,13},{... | collective-permute-start | bytes 5308424 | tf_op jit(solution)/shard_map/ppermute | solution.py:1007
  686.6 96.9 %collective-permute-start.74 = (bf16[576,1536]{1,0:T(8,128)(2,1)}, bf16[576,1536]{1,0:T(8,128)(2,1)}, u32[]{:S(2)}, u32[]{:S(2)}) collective-permute-start(bf16[576,1536]{1,0:T(8,128)(2,1)} %get-tuple-element.275), channel_id=1, source_target_pairs={{1,0},{2,1},{3,2},{5,4},{6,5},{7,6},{9,8},{10,9},{11,10},{13,12},{... | collective-permute-start | bytes 5308424 | tf_op jit(solution)/shard_map/ppermute | solution.py:1008
  713.3 74.6 %collective-permute-start.63 = (bf16[4,4,208,384]{3,2,1,0:T(8,128)(2,1)}, bf16[4,4,208,384]{3,2,1,0:T(8,128)(2,1)}, u32[]{:S(2)}, u32[]{:S(2)}) collective-permute-start(bf16[4,4,208,384]{3,2,1,0:T(8,128)(2,1)} %get-tuple-element.187), channel_id=1, source_target_pairs={{0,4},{4,0},{8,12},{12,8},{16,20},{20,16},{24,28},{28,24},{1,5},{5... | collective-permute-start | bytes 7667720 | tf_op jit(solution)/shard_map/ppermute | solution.py:1027
  748.6 100.1 %collective-permute-start.48 = (bf16[4,512,1536]{2,1,0:T(8,128)(2,1)}, bf16[4,512,1536]{2,1,0:T(8,128)(2,1)}, u32[]{:S(2)}, u32[]{:S(2)}) collective-permute-start(bf16[4,512,1536]{2,1,0:T(8,128)(2,1)} %combine.7), channel_id=1, source_target_pairs={{0,4},{4,0},{8,12},{12,8},{16,20},{20,16},{24,28},{28,24},{1,5},{5... | collective-permute-start | bytes 18874376 | tf_op jit(solution)/shard_map/ppermute | solution.py:1027
  762.1 48.9 %collective-permute-start.54 = (bf16[4,4,192,512]{3,2,1,0:T(8,128)(2,1)}, bf16[4,4,192,512]{3,2,1,0:T(8,128)(2,1)}, u32[]{:S(2)}, u32[]{:S(2)}) collective-permute-start(bf16[4,4,192,512]{3,2,1,0:T(8,128)(2,1)} %get-tuple-element.182), channel_id=1, source_target_pairs={{0,4},{4,0},{8,12},{12,8},{16,20},{20,16},{24,28},{28,24},{1,5},{5... | collective-permute-start | bytes 9437192 | tf_op jit(solution)/shard_map/ppermute | solution.py:1027
  812.9 21.5 %collective-permute-start.57 = (bf16[2,2,192,512]{3,2,1,0:T(8,128)(2,1)S(1)}, bf16[2,2,192,512]{3,2,1,0:T(8,128)(2,1)S(1)}, u32[]{:S(2)}, u32[]{:S(2)}) collective-permute-start(bf16[2,2,192,512]{3,2,1,0:T(8,128)(2,1)S(1)} %pad_maximum_fusion.8), channel_id=1, source_target_pairs={{0,16},{4,20},{8,24},{12,28},{16,0},{20,4},{24,8},{28,12},{1,17},{... | collective-permute-start | bytes 2359304 | tf_op jit(solution)/shard_map/ppermute | solution.py:1027
  813.6 22.1 %collective-permute-start.55 = (bf16[2,2,192,512]{3,2,1,0:T(8,128)(2,1)S(1)}, bf16[2,2,192,512]{3,2,1,0:T(8,128)(2,1)S(1)}, u32[]{:S(2)}, u32[]{:S(2)}) collective-permute-start(bf16[2,2,192,512]{3,2,1,0:T(8,128)(2,1)S(1)} %pad_maximum_fusion.7), channel_id=1, source_target_pairs={{0,8},{4,12},{8,0},{12,4},{16,24},{20,28},{24,16},{28,20},{1,9},{5... | collective-permute-start | bytes 2359304 | tf_op jit(solution)/shard_map/ppermute | solution.py:1027
  852.8 33.5 %collective-permute-start.51 = (bf16[2,256,1536]{2,1,0:T(8,128)(2,1)}, bf16[2,256,1536]{2,1,0:T(8,128)(2,1)S(1)}, u32[]{:S(2)}, u32[]{:S(2)}) collective-permute-start(bf16[2,256,1536]{2,1,0:T(8,128)(2,1)} %pad_maximum_fusion.6), channel_id=1, source_target_pairs={{0,16},{4,20},{8,24},{12,28},{16,0},{20,4},{24,8},{28,12},{1,17},{... | collective-permute-start | bytes 4718600 | tf_op jit(solution)/shard_map/ppermute | solution.py:1027
  855.5 33.3 %collective-permute-start.49 = (bf16[2,256,1536]{2,1,0:T(8,128)(2,1)}, bf16[2,256,1536]{2,1,0:T(8,128)(2,1)}, u32[]{:S(2)}, u32[]{:S(2)}) collective-permute-start(bf16[2,256,1536]{2,1,0:T(8,128)(2,1)} %pad_maximum_fusion.5), channel_id=1, source_target_pairs={{0,8},{4,12},{8,0},{12,4},{16,24},{20,28},{24,16},{28,20},{1,9},{5... | collective-permute-start | bytes 4718600 | tf_op jit(solution)/shard_map/ppermute | solution.py:1027
  860.0 35.9 %collective-permute-start.62 = (bf16[208,512]{1,0:T(8,128)(2,1)S(1)}, bf16[208,512]{1,0:T(8,128)(2,1)S(1)}, u32[]{:S(2)}, u32[]{:S(2)}) collective-permute-start(bf16[208,512]{1,0:T(8,128)(2,1)S(1)} %get-tuple-element.286), channel_id=1, source_target_pairs={{0,3},{3,0},{4,7},{7,4},{8,11},{11,8},{12,15},{15,12},{16,19},{19,... | collective-permute-start | bytes 638984 | tf_op jit(solution)/shard_map/ppermute | solution.py:995
  866.8 29.1 %collective-permute-start.60 = (bf16[208,512]{1,0:T(8,128)(2,1)S(1)}, bf16[208,512]{1,0:T(8,128)(2,1)S(1)}, u32[]{:S(2)}, u32[]{:S(2)}) collective-permute-start(bf16[208,512]{1,0:T(8,128)(2,1)S(1)} %get-tuple-element.284), channel_id=1, source_target_pairs={{0,1},{1,2},{2,3},{4,5},{5,6},{6,7},{8,9},{9,10},{10,11},{12,13},{... | collective-permute-start | bytes 638984 | tf_op jit(solution)/shard_map/ppermute | solution.py:1007
  869.6 26.3 %collective-permute-start.61 = (bf16[208,512]{1,0:T(8,128)(2,1)S(1)}, bf16[208,512]{1,0:T(8,128)(2,1)S(1)}, u32[]{:S(2)}, u32[]{:S(2)}) collective-permute-start(bf16[208,512]{1,0:T(8,128)(2,1)S(1)} %get-tuple-element.285), channel_id=1, source_target_pairs={{1,0},{2,1},{3,2},{5,4},{6,5},{7,6},{9,8},{10,9},{11,10},{13,12},{... | collective-permute-start | bytes 638984 | tf_op jit(solution)/shard_map/ppermute | solution.py:1008
  (91 other events, 1486.0 us)
Sparse Core Ops, SparseCore 0:
  100.0 70.7 all-gather.4

commit v6 on v5

--- a/solution.py
+++ b/solution.py
@@ -48,6 +48,9 @@
     return pl.BlockSpec(shape, lambda *_: (0,) * len(shape))
 
 
+LITTLE = pl.CostEstimate(flops=1, bytes_accessed=1, transcendentals=0)
+
+
 def params():
     return pltpu.CompilerParams(vmem_limit_bytes=VMEM_LIMIT)
 
@@ -62,9 +65,14 @@
 
 PIECES = tuple(
     (flip_bits + core, slots)
-    for wave in ((0, 2), (1, 3))
     for core in (0, 1)
-    for flip_bits, slots in ((0, wave), (2, wave), (4, wave), (6, wave[:1]), (6, wave[1:]))
+    for flip_bits, slots in (
+        (0, (0, 1, 2, 3)),
+        (2, (0, 1, 2, 3)),
+        (4, (0, 1, 2, 3)),
+        (6, (0, 1)),
+        (6, (2, 3)),
+    )
 )
 EXTRA = 16
 
@@ -108,6 +116,7 @@
         out_specs=pl.BlockSpec(memory_space=pltpu.VMEM),
         scratch_shapes=[pltpu.SemaphoreType.DMA],
         compiler_params=params(),
+        cost_estimate=LITTLE,
         name="extra_rows",
     )(info, *refs)
 
@@ -155,6 +164,7 @@
         out_specs=(pl.BlockSpec(memory_space=pltpu.VMEM),) * 2,
         scratch_shapes=[pltpu.VMEM((D, 2 * KEY_WIDTH), LOW), pltpu.SemaphoreType.DMA],
         compiler_params=params(),
+        cost_estimate=LITTLE,
         name="norm_key_value",
     )(info, tokens, gain, cosine, sine, *refs)
 
@@ -187,6 +197,7 @@
         out_specs=pl.BlockSpec((TOK_DEV, 256), lambda i: (0, i)),
         scratch_shapes=[pltpu.VMEM((D, D), LOW), pltpu.SemaphoreType.DMA],
         compiler_params=params(),
+        cost_estimate=LITTLE,
         name="query_projection",
     )(info, normed, cosine, sine, *refs)
 
@@ -272,6 +283,7 @@
         out_specs=pl.BlockSpec((BRANCH, D), lambda i: (i, 0)),
         scratch_shapes=[pltpu.VMEM((TOK_DEV, 2 * KEY_WIDTH), LOW)],
         compiler_params=params(),
+        cost_estimate=LITTLE,
         name="tree_attention",
     )(info, queries, own, partner)
 
@@ -343,6 +355,7 @@
         ),
         scratch_shapes=[pltpu.VMEM(pair, LOW)],
         compiler_params=params(),
+        cost_estimate=LITTLE,
         name="tree_attention_back",
     )(info, queries, own, partner, grads, cosine, sine)
 
@@ -377,6 +390,7 @@
         out_specs=(whole(full), whole(full)),
         scratch_shapes=[pltpu.VMEM((D, D), LOW), pltpu.SemaphoreType.DMA],
         compiler_params=params(),
+        cost_estimate=LITTLE,
         name="out_projection",
     )(info, heads, tokens, gain, *refs)
 
@@ -429,6 +443,7 @@
             jax.ShapeDtypeStruct((count, 8, TOK_DEV), WIDE),
         ],
         compiler_params=params(),
+        cost_estimate=LITTLE,
         name="route_tables",
     )(order, info, routes)
 
@@ -456,11 +471,12 @@
         ),
         out_shape=[jax.ShapeDtypeStruct((count, capacity, D), LOW)] * local,
         compiler_params=params(),
+        cost_estimate=LITTLE,
         name="pick_rows",
     )(order, chosen, blocks)
 
 
-def dispatch_kernel(local, order, info, rows, chosen, routes, router, *rest):
+def dispatch_kernel(local, near, info, rows, chosen, routes, router, *rest):
     outs, logits = rest[2 * local : 4 * local], rest[-1]
     total = router.shape[1]
     step = pl.program_id(0)
@@ -493,7 +509,7 @@
             outs[local + e][0] = jnp.sum(picked * share_row, axis=1, keepdims=True)
 
 
-def dispatch(order, info, rows, chosen, routes, router, local, earlier):
+def dispatch(at, near, info, rows, chosen, routes, router, local, earlier):
     count, height, _ = chosen.shape
     capacity = height // local
     total = router.shape[1]
@@ -512,24 +528,25 @@
             num_scalar_prefetch=2,
             grid=(D // wide,),
             in_specs=[
-                pl.BlockSpec((TOK_DEV, wide), lambda i, order, info: (0, i)),
-                pl.BlockSpec((1, height, TOK_DEV), lambda i, order, info: (order[0], 0, 0)),
-                pl.BlockSpec((1, TOP, TOK_DEV), lambda i, order, info: (order[1], 0, 0)),
-                pl.BlockSpec((wide, total), lambda i, order, info: (i, 0)),
+                pl.BlockSpec((TOK_DEV, wide), lambda i, near, info: (0, i)),
+                pl.BlockSpec((1, height, TOK_DEV), lambda i, near, info: (at, 0, 0)),
+                pl.BlockSpec((1, TOP, TOK_DEV), lambda i, near, info: (near[at], 0, 0)),
+                pl.BlockSpec((wide, total), lambda i, near, info: (i, 0)),
             ]
             + [ANY] * len(out_shape),
             out_specs=[
-                pl.BlockSpec((1, capacity, wide), lambda i, order, info: (order[0], 0, i))
+                pl.BlockSpec((1, capacity, wide), lambda i, near, info: (at, 0, i))
             ]
             * local
-            + [pl.BlockSpec((1, capacity, 1), lambda i, order, info: (order[0], 0, 0))] * local,
+            + [pl.BlockSpec((1, capacity, 1), lambda i, near, info: (at, 0, 0))] * local,
             scratch_shapes=[pltpu.VMEM((TOK_DEV, total), WIDE)],
         ),
         out_shape=out_shape,
         input_output_aliases=aliases,
         compiler_params=params(),
+        cost_estimate=LITTLE,
         name="dispatch",
-    )(order, info, rows, chosen, routes, router, *earlier)
+    )(near, info, rows, chosen, routes, router, *earlier)
 
 
 def spread_kernel(local, place, *rest):
@@ -551,6 +568,7 @@
         + [pl.BlockSpec((1, capacity, 1), lambda i: (i, 0, 0))] * local,
         out_specs=pl.BlockSpec((1, local, TOK_DEV), lambda i: (i, 0, 0)),
         compiler_params=params(),
+        cost_estimate=LITTLE,
         name="spread",
     )(place, *dots)
 
@@ -648,6 +666,7 @@
         + [pl.BlockSpec((slots, 3 * part, EXPERT_ROWS), lambda i: (0, 0, i)), thin_block],
         scratch_shapes=[pltpu.VMEM((3, slots * part, D), LOW), pltpu.SemaphoreType.DMA],
         compiler_params=params(),
+        cost_estimate=LITTLE,
         name="expert",
     )(info, rows, grads, shares, *refs)
 
@@ -670,6 +689,7 @@
         + [pl.BlockSpec((1, part, height), lambda i, s=slot: (s, 0, 0)) for slot in slots],
         out_specs=[pl.BlockSpec((part, 256), lambda i: (0, i)) for _ in slots],
         compiler_params=params(),
+        cost_estimate=LITTLE,
         name="expert_gradients",
     )(rows, grads, *[acts] * len(slots))
 
@@ -693,6 +713,7 @@
         + [pl.BlockSpec((1, capacity, D), lambda i: (first + step * i, 0, 0))] * len(rows),
         out_specs=pl.BlockSpec((1, TOK_DEV, D), lambda i: (i, 0, 0)),
         compiler_params=params(),
+        cost_estimate=LITTLE,
         name="combine",
     )(chosen, *rows)
 
@@ -786,6 +807,7 @@
         ),
         scratch_shapes=[pltpu.VMEM((D, D), LOW), pltpu.SemaphoreType.DMA],
         compiler_params=params(),
+        cost_estimate=LITTLE,
         name="experts_norm_back",
     )(info, residual, normed, cotangent, routes, grad_shares, router, gain, *sums, *refs)
 
@@ -819,6 +841,7 @@
         in_specs=[SMEM] + [vmem] * 5,
         out_specs=vmem,
         compiler_params=params(),
+        cost_estimate=LITTLE,
         name="join_key_value_gradients",
     )(info, own_grad, source_grad, arrived, cosine, sine)
 
@@ -872,6 +895,7 @@
             pltpu.SemaphoreType.DMA,
         ],
         compiler_params=params(),
+        cost_estimate=LITTLE,
         name="token_gradient",
     )(info, grad_query, grad_pair, tokens, grad_residual, gain, *query_refs, *pair_refs)
 
@@ -925,6 +949,7 @@
         ),
         out_shape=(jax.ShapeDtypeStruct(shape, LOW),) * 2,
         compiler_params=params(),
+        cost_estimate=LITTLE,
         name="weight_gradients",
     )(info, *strips, *grads, *more)
 
@@ -962,12 +987,11 @@
 FAR = [(0, 3), (3, 0)]
 
 
-def send_first(block):
-    return (
-        lax.ppermute(block, "cols", DOWN),
-        lax.ppermute(block, "cols", UP),
-        lax.ppermute(block, "cols", FAR),
-    )
+def send_first(block, chain=False):
+    above = lax.ppermute(block, "cols", DOWN)
+    below = lax.ppermute(block, "cols", UP)
+    later = after(block, above, below) if chain else block
+    return above, below, lax.ppermute(later, "cols", FAR)
 
 
 def send_second(block, first):
@@ -1031,7 +1055,7 @@
     return (one.astype(WIDE) + two.astype(WIDE)).astype(LOW)
 
 
-def reduce_chips(keep, got):
+def reduce_chips(keep, got, hold=()):
     half = keep.shape[1] // 2
 
     def sums(chips, part):
@@ -1040,6 +1064,8 @@
     one, two = slice(0, half), slice(half, None)
     got_x = flip(sums((1, 3), one), 2)
     got_y = flip(sums((2, 3), two), 4)
+    if hold:
+        got_x, got_y = after((got_x, got_y), *hold)
     near_x = sums((0, 2), one)
     near_y = sums((0, 1), two)
     got_xy = flip(add_low(near_x[1], got_x[1]), 4)
@@ -1099,7 +1125,6 @@
     packed = jnp.concatenate([query_weight, key_weight, value_weight, out_weight], axis=1)
     local_index = (1 - parity) * TOK_DEV + jnp.arange(TOK_DEV, dtype=jnp.int32)
     cosine, sine = rotary_tables(position_of(local_index))
-    routes_all = lax.all_gather(routes.T, "rows", axis=0)
     shard_blocks = [
         jnp.concatenate(
             [gate_weight[expert].T, upward_weight[expert].T, down_weight[expert]], axis=0
@@ -1115,30 +1140,27 @@
                 packed,
                 jnp.pad(router_weight.T, ((0, 0), (0, wide - depth))),
                 jnp.pad(gains, ((0, 0), (0, wide - 2 * gain_part))),
-                jnp.zeros((EXTRA - router_part - 1, wide), LOW),
+                jnp.pad(routes.T.astype(LOW), ((0, 0), (0, wide - TOK_DEV))),
+                jnp.zeros((EXTRA - router_part - 1 - TOP, wide), LOW),
             ],
             axis=0,
         )
         packed_first = send_first(packed)
         packed_second = send_second(packed, packed_first)
-        slots = slot_list(packed, packed_first, packed_second)
-        ahead = packed_second
+        own = jnp.stack(slot_list(packed, packed_first, packed_second))
+        ahead = packed_first[:2]
         for expert_at in range(local_experts):
-            block = after(shard_blocks[expert_at], ahead)
+            block = after(shard_blocks[expert_at], *ahead)
             shard_blocks[expert_at] = block
-            first = send_first(block)
+            first = send_first(block, chain=True)
             firsts.append(first)
             seconds.append(send_second(block, first))
-            ahead = first
-        pieces, owns = ([], [])
-        for wave in ((0, 2), (1, 3)):
-            own = jnp.stack([slots[i] for i in wave])
-            if wave[0] == 0:
-                own = after(own, routes_all, info, cosine, sine)
-            beside, across = flip(own, 2), flip(own, 4)
-            same = [own, beside, across, flip(beside[:1], 4), flip(across[1:], 2)]
-            pieces += same + [flip(piece, 1) for piece in same]
-            owns.append(own)
+            ahead = (first[2], seconds[-1])
+        own = after(own, info, cosine, sine)
+        beside, across = flip(own, 2), flip(own, 4)
+        beside, across = after((beside, across), *firsts[0][:2])
+        same = [own, beside, across, flip(beside[:2], 4), flip(across[2:], 2)]
+        pieces = same + [flip(piece, 1) for piece in same]
         query_refs = pair_refs = out_refs = pieces
         expert_refs = [
             [shard_blocks[i], seconds[i], *firsts[i]] for i in range(local_experts)
@@ -1147,6 +1169,11 @@
         router_all = extra_rows[:, :router_part, :depth]
         attention_scale = extra_rows[:, router_part, :gain_part]
         experts_scale = extra_rows[:, router_part, gain_part : 2 * gain_part]
+        routes_all = lax.dynamic_index_in_dim(
+            extra_rows.reshape(row_count, col_count, EXTRA, -1), col_place, 1, keepdims=False
+        )
+        routes_all = routes_all[:, router_part + 1 : router_part + 1 + TOP, :TOK_DEV]
+        routes_all = routes_all.astype(jnp.int32)
     else:
         packed_all = lax.all_gather(lax.all_gather(packed, "cols", axis=0), "rows", axis=0)
 
@@ -1166,6 +1193,7 @@
             ).reshape(D, -1)
         ]
         out_refs = [unpack(key_at + 2 * key_part, query_part)]
+        routes_all = lax.all_gather(routes.T, "rows", axis=0)
         axes = ("rows", "cols")
         router_all = jnp.swapaxes(lax.all_gather(router_weight, axes, axis=0), 1, 2)
         attention_scale = lax.all_gather(attention_gain, axes, axis=0)
@@ -1195,30 +1223,28 @@
     pairs = [(i + 1, i) for i in range(0, col_count, 2)]
     partner = lax.ppermute(own_pair, "cols", pairs)
     queries = query(info, normed, cosine, sine, query_refs)
-    if fast:
-        queries = after(queries, *firsts[0])
     heads = attention(info, queries, own_pair, partner)
     residual, normed_two = out_projection(info, heads, tokens, experts_scale, out_refs)
 
     if fast:
         beside, across = flip(normed_two, 2), flip(normed_two, 4)
         beside_in = flip(normed_two, 1)
+        chosen = after(chosen, firsts[0][2], seconds[0])
         grad_all = after(grad_all, normed_two)
     else:
         rows_all = lax.all_gather(normed_two, "rows", axis=0)
     grad_rows = pick_rows(near_rows, chosen, grad_all, local_experts)
 
     def place_block(q, block, picked):
-        order = jnp.stack([jnp.int32(q), near_rows[q]])
         return dispatch(
-            order, info, block, chosen, routes_all, router_cols, local_experts, picked
+            q, near_rows, info, block, chosen, routes_all, router_cols, local_experts, picked
         )
 
     if fast:
         half = TOK_DEV // 2
         picked = place_block(0, normed_two, None)
         picked = place_block(1, beside_in, picked)
-        beside, across = after((beside, across), picked, grad_rows)
+        beside, across = after((beside, across), picked, grad_rows, *firsts[1][:2])
         corner = [flip(beside[:half], 4), flip(across[half:], 2)]
         picked = place_block(2, beside, picked)
         picked = place_block(4, across, picked)
@@ -1227,7 +1253,6 @@
         corner = jnp.concatenate(after(corner, picked), axis=0)
         corner_in = flip(corner, 1)
         picked = place_block(6, corner, picked)
-        corner_in = after(corner_in, picked, *firsts[1])
         picked = place_block(7, corner_in, picked)
     else:
         picked = None
@@ -1241,10 +1266,8 @@
     out_rows, back_rows, gate_dots, reduced, marks = ([], [], [], [], [])
     for e in range(local_experts):
         rows_in = token_rows[e]
-        if fast and e == 0:
-            rows_in = after(rows_in, seconds[0])
         if fast and e == 1:
-            rows_in = after(rows_in, seconds[1], own_slot, third)
+            rows_in = after(rows_in, firsts[1][2], seconds[1], own_slot, third)
         out_row, back_row, grad_row, acts, dots = expert(
             info, rows_in, grad_rows[e], share_rows[e], expert_refs[e], col_count
         )
@@ -1254,9 +1277,15 @@
         if fast:
             if e == 1:
                 got = flip(combine(chosen, back_rows, 1, 2), 1)
-                acts = after(acts, got, marks[0][0])
+                acts = after(acts, got)
             second, fourth = expert_grads(acts, token_rows[e], grad_row, (1, 3))
-            sent_first = reduce_first(second, fourth)
+            if e == 1:
+                got = after(got, *marks[0], second)
+                waits = reduced[0][2]
+                second_out, fourth_out = after((second, fourth), *waits)
+            else:
+                second_out, fourth_out = second, fourth
+            sent_first = reduce_first(second_out, fourth_out)
             marks.append(sent_first)
             own_slot, third = expert_grads(acts, token_rows[e], grad_row, (0, 2))
             sent_second = reduce_second(third, fourth, sent_first[0])
@@ -1274,7 +1303,9 @@
     grad_shares = grad_shares.reshape(expert_total, TOK_DEV)
     if fast:
         back_parts = reduce_chips(combine(chosen, back_rows, 0, 2), got)
-        grad_shares = after(grad_shares, own_slot, third, *reduced[0][1], *reduced[0][2])
+        out_got = flip(combine(chosen, out_rows, 1, 2), 1)
+        out_keep = combine(chosen, out_rows, 0, 2)
+        grad_shares = after(grad_shares, own_slot, third, out_keep, out_got, *reduced[0][2])
     else:
 
         def summed(rows):
@@ -1297,8 +1328,6 @@
         out_refs,
     )
     if fast:
-        out_rows = [after(a, grad_heads) for a in out_rows]
-        out_got = flip(combine(chosen, out_rows, 1, 2), 1)
         router_parts = jnp.transpose(
             router_grad.astype(LOW).reshape(col_count, router_part, row_count, depth),
             (2, 0, 1, 3),
@@ -1306,18 +1335,12 @@
         gain_rows = experts_gain_grad.astype(LOW).reshape(row_count * col_count, 1, gain_part)
         extra = jnp.concatenate(
             [
-                jnp.pad(router_parts, ((0, 0), (0, 0), (0, query_part - depth))),
-                jnp.pad(gain_rows, ((0, 0), (0, 0), (0, query_part - gain_part))),
-                jnp.zeros(
-                    (row_count * col_count, EXTRA - router_part - 1, query_part), LOW
-                ),
+                jnp.pad(router_parts, ((0, 0), (0, 0), (0, wide - depth))),
+                jnp.pad(gain_rows, ((0, 0), (0, 0), (0, wide - gain_part))),
+                jnp.zeros((row_count * col_count, EXTRA - router_part - 1, wide), LOW),
             ],
             axis=1,
         )
-        out_keep, out_send = weight_grads(
-            info, [heads], [grad_branch], ((0, 1, query_part),), extra
-        )
-        out_sent = flip(out_send, 1)
     grad_query, own_grad, source_grad = attention_back(
         info, queries, own_pair, partner, grad_heads, cosine, sine
     )
@@ -1326,10 +1349,10 @@
     if fast:
         keep, send = weight_grads(
             info,
-            [normed],
-            [grad_query, grad_pair],
-            ((0, 1, query_part), (0, 2, 2 * key_part)),
-            None,
+            [normed, heads],
+            [grad_query, grad_pair, grad_branch],
+            ((0, 2, query_part), (0, 3, 2 * key_part), (1, 4, query_part)),
+            extra,
         )
         sent = flip(send, 1)
         grad_pair = after(grad_pair, keep)
@@ -1338,35 +1361,31 @@
     )
 
     if fast:
-        out_slots = sum_parts(reduce_chips(out_keep, out_sent)).astype(LOW)
-        mixture = reduce_chips(combine(chosen, out_rows, 0, 2), out_got)
-        slots = sum_parts(reduce_chips(keep, sent))
-        own_slots = [owns[0][0], owns[1][0], owns[0][1], owns[1][1]]
+        mixture = reduce_chips(out_keep, out_got)
+        slots = sum_parts(reduce_chips(keep, sent, marks[1]))
         width = query_part + 2 * key_part
         gain_sums = sum(
-            jnp.sum(own_slots[i][:depth, :width].astype(WIDE) * slots[i], axis=1)
+            jnp.sum(own[i, :depth, :width].astype(WIDE) * slots[i, :depth, :width], axis=1)
             for i in range(4)
         )
         own_gains = lax.dynamic_slice_in_dim(attention_scale[0], row_place * depth, depth, 0)
         gain_sums = (gain_sums / own_gains).reshape(col_count, 1, gain_part)
         gain_sums = jnp.pad(
             jnp.take(gain_sums, shards, axis=0),
-            ((0, 0), (0, EXTRA - 1), (0, width - gain_part)),
+            ((0, 0), (depth + router_part + 1, EXTRA - router_part - 2), (0, wide - gain_part)),
         )
-        slots = jnp.concatenate([slots, gain_sums], axis=1).astype(LOW)
+        slots = (slots + gain_sums).astype(LOW)
 
         def cols_sum(slots):
             sent_first = reduce_first(slots[1], slots[3])
             sent_second = reduce_second(slots[2], slots[3], sent_first[0])
             return reduce_last(slots[0], sent_first, sent_second)
 
-        out_sums = cols_sum(out_slots)
         sums = cols_sum(slots)
         expert_sums = [reduce_last(*parts) for parts in reduced]
-        router_sum = out_sums[depth : depth + router_part, :depth].T
-        experts_gain_sum = out_sums[depth + router_part, :gain_part]
-        attention_gain_sum = sums[depth, :gain_part]
-        out_sum = out_sums[:depth]
+        router_sum = sums[depth : depth + router_part, :depth].T
+        experts_gain_sum = sums[depth + router_part, :gain_part]
+        attention_gain_sum = sums[depth + router_part + 1, :gain_part]
         sums = sums[:depth]
     else:
         full_grads = [
@@ -1402,7 +1421,6 @@
         attention_gain_sum = small_sums[:gain_part]
         experts_gain_sum = small_sums[gain_part : 2 * gain_part]
         router_sum = small_sums[2 * gain_part :].reshape(depth, router_part)
-        out_sum = sums[:, query_part + 2 * key_part :]
 
     layer_output = (residual + sum_parts(mixture)).astype(LOW)
     key_at = query_part
@@ -1419,7 +1437,7 @@
         sums[:, :key_at],
         sums[:, key_at:value_at],
         sums[:, value_at:out_at],
-        out_sum,
+        sums[:, out_at:],
         router_sum,
         attention_gain_sum,
         experts_gain_sum,

time: 933 us -> 882 us (0.945)
  waiting for transfers between devices: 349 us -> 261 us
  starting transfers between devices: 127 us -> 172 us
  blocking collectives: 10.2 us -> 0 us
    ppermute x4 -> x3, waiting for transfers between devices: 61.2 us -> 4.42 us  [reduce_second(): lax.ppermute(downward_load, 'cols', DOWN)]
    ppermute x4 -> x3, starting transfers between devices: 11.6 us -> 59.7 us  [reduce_second(): lax.ppermute(upward_load, 'cols', UP)]
    ppermute x46 -> x32, waiting for transfers between devices: 101 us -> 62.1 us  [flip(): return lax.ppermute(block, 'rows', [(i, i ^ bit) for i in range(count)])]
    ppermute x9, waiting for transfers between devices: 59.9 us -> 77.3 us  [the longest x3 46.5 us: send_first(): return (above, below, lax.ppermute(later, 'cols', FAR))]
    ppermute x4 -> x3, starting transfers between devices: 20.2 us -> 4.61 us  [reduce_first(): lax.ppermute(second, 'cols', [(1, 3), (0, 1), (2, 0), (3, 2)])]
    ppermute x4 -> x3, starting transfers between devices: 12.9 us -> 27 us  [reduce_first(): lax.ppermute(fourth, 'cols', FAR)]
    another operation x12 -> x1, other arithmetic: 12.1 us -> 0.22 us  [on_device(): own = jnp.stack(slot_list(packed, packed_first, packed_second))]
    all_to_all x1, waiting for transfers between devices: 12.1 us -> 0.87 us  [on_device(): lax.all_to_all(spread_dots, 'rows', split_axis=0, concat_axis=0, tiled=True)]
  transfers between devices with their start and end apart: 78 -> 60, of which waited for: 30 -> 25; matrix products, arithmetic and copies ran while one was open for 11% -> 10% of each run, Pallas kernels for 28% -> 24%
where the time goes in v6:
time: 882 us; the launch traced here: 873 us
  Pallas kernels  296 us (34%)
  waiting for transfers between devices  261 us (30%)
  starting transfers between devices  172 us (20%)
  other arithmetic  78.5 us (9%)
  local copies, waits for them, and re-layouts  50.1 us (6%)
  between operations  15.3 us (2%)
    ppermute x3, waiting for transfers between devices, reduce_first(): lax.ppermute(second, 'cols', [(1, 3), (0, 1), (2, 0), (3, 2)])  82.4 us
    ppermute x32, waiting for transfers between devices, flip(): return lax.ppermute(block, 'rows', [(i, i ^ bit) for i in range(count)])  62.1 us
    pallas_call x2, Pallas kernels, expert(): pl.pallas_call(functools.partial(expert_kernel, slots), grid=(height // E...  60.3 us
    ppermute x3, starting transfers between devices, reduce_second(): lax.ppermute(upward_load, 'cols', UP)  59.7 us
    ppermute x3, waiting for transfers between devices, send_first(): return (above, below, lax.ppermute(later, 'cols', FAR))  46.5 us
    pallas_call x8, Pallas kernels, dispatch(): pl.pallas_call(functools.partial(dispatch_kernel, local), grid_spec=pltpu...  41.1 us
    pallas_call x4, Pallas kernels, expert_grads(): pl.pallas_call(functools.partial(expert_grads_kernel, slots), grid=(D //...  39.8 us
    ppermute x3, waiting for transfers between devices, send_first(): above = lax.ppermute(block, 'cols', DOWN)  30.5 us
  transfers between devices with their start and end apart: 60, of which 25 were waited for; matrix products, arithmetic and copies ran while one was open for 10% of the time, Pallas kernels for 24%

profile of v6, /device:TPU:0, one launch (start us, length us, event | category | flops | bytes accessed | tf_op | source)
XLA Modules:
  0.0 873.1 jit_solution(17132222897275163906)
XLA Ops:
  13.9 5.6 collective-permute-start.1
  29.3 7.2 collective-permute-done.3
  43.3 5.7 collective-permute-start.7
  54.9 30.5 %collective-permute-done.6.rest_2_ = bf16[576,1536]{1,0:T(8,128)(2,1)} collective-permute-done((bf16[576,1536]{1,0:T(8,128)(2,1)}, bf16[576,1536]{1,0:T(8,128)(2,1)}, u32[]{:S(2)}, u32[]{:S(2)}) %collective-permute-start.6) | collective-permute-done | bytes 1769504 | tf_op jit(solution)/shard_map/ppermute | solution.py:991
  89.2 13.0 %collective-permute-done.8.rest_3_.rest_9_.rest_13_ = bf16[2,208,896]{2,1,0:T(8,128)(2,1)S(1)} collective-permute-done((bf16[2,208,896]{2,1,0:T(8,128)(2,1)S(1)}, bf16[2,208,896]{2,1,0:T(8,128)(2,1)S(1)}, u32[]{:S(2)}, u32[]{:S(2)}) %collective-permute-start.8) | collective-permute-done | bytes 745504 | tf_op jit(solution)/shard_map/ppermute | solution.py:1051
  113.5 5.3 collective-permute-start.16
  129.9 24.2 %collective-permute-done.17.rest_1_ = bf16[576,1536]{1,0:T(8,128)(2,1)S(1)} collective-permute-done((bf16[576,1536]{1,0:T(8,128)(2,1)}, bf16[576,1536]{1,0:T(8,128)(2,1)S(1)}, u32[]{:S(2)}, u32[]{:S(2)}) %collective-permute-start.17) | collective-permute-done | bytes 1769504 | tf_op jit(solution)/shard_map/ppermute | solution.py:1001
  155.3 39.3 %collective-permute-done.16.rest_4_ = bf16[576,1536]{1,0:T(8,128)(2,1)} collective-permute-done((bf16[576,1536]{1,0:T(8,128)(2,1)}, bf16[576,1536]{1,0:T(8,128)(2,1)}, u32[]{:S(2)}, u32[]{:S(2)}) %collective-permute-start.16) | collective-permute-done | bytes 1769504 | tf_op jit(solution)/shard_map/ppermute | solution.py:994
  195.9 6.3 collective-permute-start.22
  202.2 8.9 %query_projection.1.queries = bf16[512,1536]{1,0:T(8,128)(2,1)} custom-call(s32[16]{0:T(128)} %concatenate.36.info, bf16[512,1536]{1,0:T(8,128)(2,1)} %get-tuple-element.108.normed.rest_0_, f32[512,128]{1,0:T(8,128)} %get-tuple-element.284.cosine, f32[512,128]{1,0:T(8,128)} %get-tuple-element.285.sine, bf16[4,208,896]{2,1,0:T(8,128)(2,1)} %copy-done, ...), custom_call_target="tpu_custom_call" | custom-call | flops 1 | bytes 1 | tf_op jit(solution)/shard_map/query_projection/pallas_call | solution.py:191
  211.8 11.0 %tree_attention.1.heads.rest_1_ = bf16[512,1536]{1,0:T(8,128)(2,1)} custom-call(s32[16]{0:T(128)} %concatenate.36.info, bf16[512,1536]{1,0:T(8,128)(2,1)} %query_projection.1.queries, bf16[512,512]{1,0:T(8,128)(2,1)} %get-tuple-element.109.own, bf16[512,512]{1,0:T(8,128)(2,1)} %collective-permute-done.15.partner), custom_call_target="tpu_custom_call" | custom-call | flops 1 | bytes 1 | tf_op jit(solution)/shard_map/tree_attention/pallas_call | solution.py:273
  222.7 10.7 %out_projection.1 = (f32[512,1536]{1,0:T(8,128)}, bf16[512,1536]{1,0:T(8,128)(2,1)}) custom-call(s32[16]{0:T(128)} %concatenate.36.info, bf16[512,1536]{1,0:T(8,128)(2,1)} %tree_attention.1.heads.rest_1_, bf16[512,1536]{1,0:T(8,128)(2,1)} %tokens.5, f32[1,1536]{1,0:T(1,128)} %reshape.454.gain, bf16[4,208,896]{2,1,0:T(8,128)(2,1)} %copy-done, ...), custom_call_target="tpu_custom_call" | custom-call | flops 1 | bytes 1 | tf_op jit(solution)/shard_map/out_projection/pallas_call | solution.py:385
  238.4 6.2 route_tables.1
  250.6 5.1 dispatch.8
  255.8 5.1 dispatch.9
  260.9 13.1 %pick_rows.1 = (bf16[8,160,1536]{2,1,0:T(8,128)(2,1)}, bf16[8,160,1536]{2,1,0:T(8,128)(2,1)}) custom-call(s32[8]{0:T(128)} %iota_xor_fusion.order.near, bf16[8,320,512]{2,1,0:T(8,128)(2,1)} %get-tuple-element.113.chosen, bf16[8,512,1536]{2,1,0:T(8,128)(2,1)} %bitcast.165), custom_call_target="tpu_custom_call" | custom-call | flops 1 | bytes 1 | tf_op jit(solution)/shard_map/pick_rows/pallas_call | solution.py:461
  281.7 5.1 dispatch.10
  286.8 5.2 dispatch.11
  295.3 5.1 dispatch.12
  301.6 5.2 dispatch.13
  309.2 5.1 dispatch.14
  319.5 30.2 %expert.2 = (bf16[1280,1536]{1,0:T(8,128)(2,1)}, bf16[1280,1536]{1,0:T(8,128)(2,1)}, bf16[1280,1536]{1,0:T(8,128)(2,1)}, bf16[4,576,1280]{2,1,0:T(8,128)(2,1)}, f32[1280,1]{1,0:T(8,128)}) custom-call(s32[16]{0:T(128)} %concatenate.36.info, bf16[1280,1536]{1,0:T(8,128)(2,1)} %bitcast.141, bf16[1280,1536]{1,0:T(8,128)(2,1)} %bitcast.169, f32[1280,1]{1,0:T(8,128)} %bitcast.147, ...), custom_call_target="tpu_custom_call" | custom-call | flops 1 | bytes 1 | tf_op jit(solution)/shard_map/expert/pallas_call | solution.py:656
  349.7 9.9 %expert_gradients.4 = (bf16[576,1536]{1,0:T(8,128)(2,1)}, bf16[576,1536]{1,0:T(8,128)(2,1)}) custom-call(bf16[1280,1536]{1,0:T(8,128)(2,1)} %bitcast.142, bf16[1280,1536]{1,0:T(8,128)(2,1)} %get-tuple-element.157.grads, bf16[4,576,1280]{2,1,0:T(8,128)(2,1)} %get-tuple-element.158.rest_0_.rest_1_, bf16[4,576,1280]{2,1,0:T(8,128)(2,1)} %get-tuple-element.158.rest_0_.rest_1_), custom_call_target="tpu_custom_call" | custom-call | flops 1 | bytes 1 | tf_op jit(solution)/shard_map/expert_gradients/pallas_call | solution.py:684
  361.6 30.1 %expert.3 = (bf16[1280,1536]{1,0:T(8,128)(2,1)}, bf16[1280,1536]{1,0:T(8,128)(2,1)}, bf16[1280,1536]{1,0:T(8,128)(2,1)}, bf16[4,576,1280]{2,1,0:T(8,128)(2,1)}, f32[1280,1]{1,0:T(8,128)}) custom-call(s32[16]{0:T(128)} %concatenate.36.info, bf16[1280,1536]{1,0:T(8,128)(2,1)} %bitcast.144, bf16[1280,1536]{1,0:T(8,128)(2,1)} %bitcast.168, f32[1280,1]{1,0:T(8,128)} %bitcast.148, ...), custom_call_target="tpu_custom_call" | custom-call | flops 1 | bytes 1 | tf_op jit(solution)/shard_map/expert/pallas_call | solution.py:656
  391.7 7.5 combine.6
  399.2 7.7 combine.5
  407.4 9.8 %expert_gradients.6 = (bf16[576,1536]{1,0:T(8,128)(2,1)}, bf16[576,1536]{1,0:T(8,128)(2,1)}) custom-call(bf16[1280,1536]{1,0:T(8,128)(2,1)} %bitcast.143, bf16[1280,1536]{1,0:T(8,128)(2,1)} %get-tuple-element.157.grads, bf16[4,576,1280]{2,1,0:T(8,128)(2,1)} %get-tuple-element.158.rest_0_.rest_1_, bf16[4,576,1280]{2,1,0:T(8,128)(2,1)} %get-tuple-element.158.rest_0_.rest_1_), custom_call_target="tpu_custom_call" | custom-call | flops 1 | bytes 1 | tf_op jit(solution)/shard_map/expert_gradients/pallas_call | solution.py:684
  421.4 7.5 combine.7
  428.9 67.9 %collective-permute-done.36 = bf16[576,1536]{1,0:T(8,128)(2,1)S(1)} collective-permute-done((bf16[576,1536]{1,0:T(8,128)(2,1)}, bf16[576,1536]{1,0:T(8,128)(2,1)S(1)}, u32[]{:S(2)}, u32[]{:S(2)}) %collective-permute-start.36) | collective-permute-done | bytes 1769504 | tf_op jit(solution)/shard_map/ppermute | solution.py:1018
  496.8 5.5 fusion.3
  510.4 10.3 %expert_gradients.7 = (bf16[576,1536]{1,0:T(8,128)(2,1)}, bf16[576,1536]{1,0:T(8,128)(2,1)}) custom-call(bf16[1280,1536]{1,0:T(8,128)(2,1)} %bitcast.145, bf16[1280,1536]{1,0:T(8,128)(2,1)} %get-tuple-element.167.grads, bf16[4,576,1280]{2,1,0:T(8,128)(2,1)} %get-tuple-element.171.rest_0_.rest_1_, bf16[4,576,1280]{2,1,0:T(8,128)(2,1)} %get-tuple-element.171.rest_0_.rest_1_), custom_call_target="tpu_custom_call" | custom-call | flops 1 | bytes 1 | tf_op jit(solution)/shard_map/expert_gradients/pallas_call | solution.py:684
  528.7 5.6 spread.1
  540.1 7.5 combine.4
  549.1 10.0 %expert_gradients.5 = (bf16[576,1536]{1,0:T(8,128)(2,1)}, bf16[576,1536]{1,0:T(8,128)(2,1)}) custom-call(bf16[1280,1536]{1,0:T(8,128)(2,1)} %bitcast.146, bf16[1280,1536]{1,0:T(8,128)(2,1)} %get-tuple-element.167.grads, bf16[4,576,1280]{2,1,0:T(8,128)(2,1)} %get-tuple-element.171.rest_0_.rest_1_, bf16[4,576,1280]{2,1,0:T(8,128)(2,1)} %get-tuple-element.171.rest_0_.rest_1_), custom_call_target="tpu_custom_call" | custom-call | flops 1 | bytes 1 | tf_op jit(solution)/shard_map/expert_gradients/pallas_call | solution.py:684
  570.4 12.8 %collective-permute-done.41.rest_2_ = bf16[256,1536]{1,0:T(8,128)(2,1)S(1)} collective-permute-done((bf16[256,1536]{1,0:T(8,128)(2,1)S(1)}, bf16[256,1536]{1,0:T(8,128)(2,1)S(1)}, u32[]{:S(2)}, u32[]{:S(2)}) %collective-permute-start.41) | collective-permute-done | bytes 786464 | tf_op jit(solution)/shard_map/ppermute | solution.py:1051
  585.0 13.5 %experts_norm_back.1 = (f32[512,1536]{1,0:T(8,128)}, bf16[512,1536]{1,0:T(8,128)(2,1)}, bf16[512,1536]{1,0:T(8,128)(2,1)}, f32[1,1536]{1,0:T(1,128)}, f32[16,1536]{1,0:T(8,128)}) custom-call(s32[16]{0:T(128)} %concatenate.36.info, f32[512,1536]{1,0:T(8,128)} %get-tuple-element.110.residual, bf16[512,1536]{1,0:T(8,128)(2,1)} %get-tuple-element.114.rows.normed, ...), custom_call_target="tpu_custom_call" | custom-call | flops 1 | bytes 1 | tf_op jit(solution)/shard_map/experts_norm_back/pallas_call | solution.py:786
  598.5 15.5 %tree_attention_back.1 = (bf16[512,1536]{1,0:T(8,128)(2,1)}, f32[512,512]{1,0:T(8,128)}, f32[512,512]{1,0:T(8,128)}) custom-call(s32[16]{0:T(128)} %concatenate.36.info, bf16[512,1536]{1,0:T(8,128)(2,1)} %query_projection.1.queries, bf16[512,512]{1,0:T(8,128)(2,1)} %get-tuple-element.109.own, bf16[512,512]{1,0:T(8,128)(2,1)} %collective-permute-done.15.partner, ...), custom_call_target="tpu_custom_call" | custom-call | flops 1 | bytes 1 | tf_op jit(solution)/shard_map/tree_attention_back/pallas_call | solution.py:334
  621.3 8.8 %collective-permute-done.44.arrived = bf16[512,512]{1,0:T(8,128)(2,1)S(1)} collective-permute-done((bf16[512,512]{1,0:T(8,128)(2,1)S(1)}, bf16[512,512]{1,0:T(8,128)(2,1)S(1)}, u32[]{:S(2)}, u32[]{:S(2)}) %collective-permute-start.44) | collective-permute-done | bytes 524320 | tf_op jit(solution)/shard_map/ppermute | solution.py:1347
  634.2 16.1 %weight_gradients.1 = (bf16[4,4,208,896]{3,2,1,0:T(8,128)(2,1)}, bf16[4,4,208,896]{3,2,1,0:T(8,128)(2,1)}) custom-call(s32[16]{0:T(128)} %concatenate.36.info, bf16[512,1536]{1,0:T(8,128)(2,1)} %get-tuple-element.108.normed.rest_0_, bf16[512,1536]{1,0:T(8,128)(2,1)} %tree_attention.1.heads.rest_1_, bf16[512,1536]{1,0:T(8,128)(2,1)} %get-tuple-element.180.rest_2_.grad_query, ...), custom_call_target="tpu_custom_call" | custom-call | flops 1 | bytes 1 | tf_op jit(solution)/shard_map/weight_gradients/pallas_call | solution.py:938
  666.6 17.0 %collective-permute-start.49 = (bf16[576,1536]{1,0:T(8,128)(2,1)}, bf16[576,1536]{1,0:T(8,128)(2,1)}, u32[]{:S(2)}, u32[]{:S(2)}) collective-permute-start(bf16[576,1536]{1,0:T(8,128)(2,1)} %get-tuple-element.193), channel_id=1, source_target_pairs={{0,3},{3,0},{4,7},{7,4},{8,11},{11,8},{12,15},{15,12},{16,19},{19,... | collective-permute-start | bytes 5308424 | tf_op jit(solution)/shard_map/ppermute | solution.py:1019
  683.7 7.8 collective-permute-done.33
  698.5 13.8 %collective-permute-done.48 = bf16[576,1536]{1,0:T(8,128)(2,1)} collective-permute-done((bf16[576,1536]{1,0:T(8,128)(2,1)}, bf16[576,1536]{1,0:T(8,128)(2,1)}, u32[]{:S(2)}, u32[]{:S(2)}) %collective-permute-start.48) | collective-permute-done | bytes 1769504 | tf_op jit(solution)/shard_map/ppermute | solution.py:1018
  716.7 43.4 %collective-permute-start.56 = (bf16[576,1536]{1,0:T(8,128)(2,1)}, bf16[576,1536]{1,0:T(8,128)(2,1)}, u32[]{:S(2)}, u32[]{:S(2)}) collective-permute-start(bf16[576,1536]{1,0:T(8,128)(2,1)} %get-tuple-element.258), channel_id=1, source_target_pairs={{0,1},{1,2},{2,3},{4,5},{5,6},{6,7},{8,9},{9,10},{10,11},{12,13},{... | collective-permute-start | bytes 5308424 | tf_op jit(solution)/shard_map/ppermute | solution.py:1031
  775.5 13.5 %token_gradient.1 = (bf16[512,1536]{1,0:T(8,128)(2,1)}, f32[1,1536]{1,0:T(1,128)}) custom-call(s32[16]{0:T(128)} %concatenate.36.info, bf16[512,1536]{1,0:T(8,128)(2,1)} %get-tuple-element.180.rest_2_.grad_query, bf16[512,512]{1,0:T(8,128)(2,1)} %join_key_value_gradients.1.rest_3_.grad_pair, bf16[512,1536]{1,0:T(8,128)(2,1)} %tokens.5, ...), custom_call_target="tpu_custom_call" | custom-call | flops 1 | bytes 1 | tf_op jit(solution)/shard_map/token_gradient/pallas_call | solution.py:877
  789.1 11.1 %collective-permute-done.47 = bf16[2,2,208,896]{3,2,1,0:T(8,128)(2,1)} collective-permute-done((bf16[2,2,208,896]{3,2,1,0:T(8,128)(2,1)}, bf16[2,2,208,896]{3,2,1,0:T(8,128)(2,1)}, u32[]{:S(2)}, u32[]{:S(2)}) %collective-permute-start.47) | collective-permute-done | bytes 1490976 | tf_op jit(solution)/shard_map/ppermute | solution.py:1051
  810.5 9.6 %collective-permute-done.50 = bf16[2,208,896]{2,1,0:T(8,128)(2,1)S(1)} collective-permute-done((bf16[2,208,896]{2,1,0:T(8,128)(2,1)S(1)}, bf16[2,208,896]{2,1,0:T(8,128)(2,1)S(1)}, u32[]{:S(2)}, u32[]{:S(2)}) %collective-permute-start.50) | collective-permute-done | bytes 745504 | tf_op jit(solution)/shard_map/ppermute | solution.py:1051
  833.9 5.8 collective-permute-start.55
  840.6 12.2 %collective-permute-start.53 = (bf16[208,896]{1,0:T(8,128)(2,1)S(1)}, bf16[208,896]{1,0:T(8,128)(2,1)S(1)}, u32[]{:S(2)}, u32[]{:S(2)}) collective-permute-start(bf16[208,896]{1,0:T(8,128)(2,1)S(1)} %get-tuple-element.262), channel_id=1, source_target_pairs={{0,1},{1,2},{2,3},{4,5},{5,6},{6,7},{8,9},{9,10},{10,11},{12,13},{... | collective-permute-start | bytes 1118216 | tf_op jit(solution)/shard_map/ppermute | solution.py:1031
  (313 shorter events, 224.8 us)
Async XLA Ops:
  7.2 253.7 %all-gather.3.cloned.1.call-start = ((), (), s32[]{:S(2)}) async-start(), calls=%async_computation.1 | async-start | bytes 14155776 | tf_op jit(solution)/shard_map/all_gather | solution.py:1220
  19.5 17.0 %collective-permute-start.3 = (bf16[208,896]{1,0:T(8,128)(2,1)S(1)}, bf16[208,896]{1,0:T(8,128)(2,1)}, u32[]{:S(2)}, u32[]{:S(2)}) collective-permute-start(bf16[208,896]{1,0:T(8,128)(2,1)S(1)} %concatenate.39), channel_id=1, source_target_pairs={{0,3},{3,0},{4,7},{7,4},{8,11},{11,8},{12,15},{15,12},{16,19},{19,... | collective-permute-start | bytes 1118216 | tf_op jit(solution)/shard_map/ppermute | solution.py:994
  42.0 43.4 %collective-permute-start.6 = (bf16[576,1536]{1,0:T(8,128)(2,1)}, bf16[576,1536]{1,0:T(8,128)(2,1)}, u32[]{:S(2)}, u32[]{:S(2)}) collective-permute-start(bf16[576,1536]{1,0:T(8,128)(2,1)} %pad_maximum_fusion.1.rest_0_), channel_id=1, source_target_pairs={{1,0},{2,1},{3,2},{5,4},{6,5},{7,6},{9,8},{10,9},{11,10},{13,12},{... | collective-permute-start | bytes 5308424 | tf_op jit(solution)/shard_map/ppermute | solution.py:991
  43.3 42.1 %collective-permute-start.7 = (bf16[576,1536]{1,0:T(8,128)(2,1)}, bf16[576,1536]{1,0:T(8,128)(2,1)}, u32[]{:S(2)}, u32[]{:S(2)}) collective-permute-start(bf16[576,1536]{1,0:T(8,128)(2,1)} %pad_maximum_fusion.1.rest_0_), channel_id=1, source_target_pairs={{0,1},{1,2},{2,3},{4,5},{5,6},{6,7},{8,9},{9,10},{10,11},{12,13},{... | collective-permute-start | bytes 5308424 | tf_op jit(solution)/shard_map/ppermute | solution.py:992
  51.8 33.6 %collective-permute-start.4 = (bf16[4,208,896]{2,1,0:T(8,128)(2,1)S(1)}, bf16[4,208,896]{2,1,0:T(8,128)(2,1)S(1)}, u32[]{:S(2)}, u32[]{:S(2)}) collective-permute-start(bf16[4,208,896]{2,1,0:T(8,128)(2,1)S(1)} %pad_maximum_fusion.7.rest_0_.rest_6_.rest_10_), channel_id=1, source_target_pairs={{0,8},{4,12},{8,0},{12,4},{16,24},{20,28},{24,16},{28,20},{1,9},{5... | collective-permute-start | bytes 4472840 | tf_op jit(solution)/shard_map/ppermute | solution.py:1051
  53.4 32.0 %collective-permute-start.5 = (bf16[4,208,896]{2,1,0:T(8,128)(2,1)S(1)}, bf16[4,208,896]{2,1,0:T(8,128)(2,1)S(1)}, u32[]{:S(2)}, u32[]{:S(2)}) collective-permute-start(bf16[4,208,896]{2,1,0:T(8,128)(2,1)S(1)} %pad_maximum_fusion.7.rest_0_.rest_6_.rest_10_), channel_id=1, source_target_pairs={{0,16},{4,20},{8,24},{12,28},{16,0},{20,4},{24,8},{28,12},{1,17},{... | collective-permute-start | bytes 4472840 | tf_op jit(solution)/shard_map/ppermute | solution.py:1051
  54.9 48.6 %collective-permute-start.10 = (bf16[4,208,896]{2,1,0:T(8,128)(2,1)S(1)}, bf16[4,208,896]{2,1,0:T(8,128)(2,1)S(1)}, u32[]{:S(2)}, u32[]{:S(2)}) collective-permute-start(bf16[4,208,896]{2,1,0:T(8,128)(2,1)S(1)} %pad_maximum_fusion.7.rest_0_.rest_6_.rest_10_), channel_id=1, source_target_pairs={{0,4},{4,0},{8,12},{12,8},{16,20},{20,16},{24,28},{28,24},{1,5},{5... | collective-permute-start | bytes 4472840 | tf_op jit(solution)/shard_map/ppermute | solution.py:1051
  85.5 16.7 %collective-permute-start.8 = (bf16[2,208,896]{2,1,0:T(8,128)(2,1)S(1)}, bf16[2,208,896]{2,1,0:T(8,128)(2,1)S(1)}, u32[]{:S(2)}, u32[]{:S(2)}) collective-permute-start(bf16[2,208,896]{2,1,0:T(8,128)(2,1)S(1)} %slice.450), channel_id=1, source_target_pairs={{0,16},{4,20},{8,24},{12,28},{16,0},{20,4},{24,8},{28,12},{1,17},{... | collective-permute-start | bytes 2236424 | tf_op jit(solution)/shard_map/ppermute | solution.py:1051
  87.1 16.4 %collective-permute-start.9 = (bf16[2,208,896]{2,1,0:T(8,128)(2,1)S(1)}, bf16[2,208,896]{2,1,0:T(8,128)(2,1)S(1)}, u32[]{:S(2)}, u32[]{:S(2)}) collective-permute-start(bf16[2,208,896]{2,1,0:T(8,128)(2,1)S(1)} %slice.451), channel_id=1, source_target_pairs={{0,8},{4,12},{8,0},{12,4},{16,24},{20,28},{24,16},{28,20},{1,9},{5... | collective-permute-start | bytes 2236424 | tf_op jit(solution)/shard_map/ppermute | solution.py:1051
  88.7 17.1 %collective-permute-start.11 = (bf16[4,208,896]{2,1,0:T(8,128)(2,1)S(1)}, bf16[4,208,896]{2,1,0:T(8,128)(2,1)S(1)}, u32[]{:S(2)}, u32[]{:S(2)}) collective-permute-start(bf16[4,208,896]{2,1,0:T(8,128)(2,1)S(1)} %collective-permute-done.4.rest_1_.rest_7_.rest_11_), channel_id=1, source_target_pairs={{0,4},{4,0},{8,12},{12,8},{16,20},{20,16},{24,28},{28,24},{1,5},{5... | collective-permute-start | bytes 4472840 | tf_op jit(solution)/shard_map/ppermute | solution.py:1051
  88.7 19.1 %collective-permute-start.12 = (bf16[4,208,896]{2,1,0:T(8,128)(2,1)S(1)}, bf16[4,208,896]{2,1,0:T(8,128)(2,1)}, u32[]{:S(2)}, u32[]{:S(2)}) collective-permute-start(bf16[4,208,896]{2,1,0:T(8,128)(2,1)S(1)} %collective-permute-done.5.rest_2_.rest_8_.rest_12_), channel_id=1, source_target_pairs={{0,4},{4,0},{8,12},{12,8},{16,20},{20,16},{24,28},{28,24},{1,5},{5... | collective-permute-start | bytes 4472840 | tf_op jit(solution)/shard_map/ppermute | solution.py:1051
  110.8 43.4 %collective-permute-start.17 = (bf16[576,1536]{1,0:T(8,128)(2,1)}, bf16[576,1536]{1,0:T(8,128)(2,1)S(1)}, u32[]{:S(2)}, u32[]{:S(2)}) collective-permute-start(bf16[576,1536]{1,0:T(8,128)(2,1)} %select_select_fusion.1), channel_id=1, source_target_pairs={{3,1},{1,0},{0,2},{2,3},{7,5},{5,4},{4,6},{6,7},{11,9},{9,8},{8,10... | collective-permute-start | bytes 5308424 | tf_op jit(solution)/shard_map/ppermute | solution.py:1001
  113.5 81.1 %collective-permute-start.16 = (bf16[576,1536]{1,0:T(8,128)(2,1)}, bf16[576,1536]{1,0:T(8,128)(2,1)}, u32[]{:S(2)}, u32[]{:S(2)}) collective-permute-start(bf16[576,1536]{1,0:T(8,128)(2,1)} %pad_maximum_fusion.1.rest_0_), channel_id=1, source_target_pairs={{0,3},{3,0},{4,7},{7,4},{8,11},{11,8},{12,15},{15,12},{16,19},{19,... | collective-permute-start | bytes 5308424 | tf_op jit(solution)/shard_map/ppermute | solution.py:994
  128.4 83.3 %collective-permute-start.15 = (bf16[512,512]{1,0:T(8,128)(2,1)}, bf16[512,512]{1,0:T(8,128)(2,1)}, u32[]{:S(2)}, u32[]{:S(2)}) collective-permute-start(bf16[512,512]{1,0:T(8,128)(2,1)} %get-tuple-element.109.own), channel_id=1, source_target_pairs={{1,0},{3,2},{5,4},{7,6},{9,8},{11,10},{13,12},{15,14},{17,16},{19,... | collective-permute-start | bytes 1572872 | tf_op jit(solution)/shard_map/ppermute | solution.py:1224
  194.6 79.4 %collective-permute-start.21 = (bf16[576,1536]{1,0:T(8,128)(2,1)S(1)}, bf16[576,1536]{1,0:T(8,128)(2,1)S(1)}, u32[]{:S(2)}, u32[]{:S(2)}) collective-permute-start(bf16[576,1536]{1,0:T(8,128)(2,1)S(1)} %pad_maximum_fusion.2.rest_0_), channel_id=1, source_target_pairs={{1,0},{2,1},{3,2},{5,4},{6,5},{7,6},{9,8},{10,9},{11,10},{13,12},{... | collective-permute-start | bytes 5308424 | tf_op jit(solution)/shard_map/ppermute | solution.py:991
  195.9 78.2 %collective-permute-start.22 = (bf16[576,1536]{1,0:T(8,128)(2,1)S(1)}, bf16[576,1536]{1,0:T(8,128)(2,1)}, u32[]{:S(2)}, u32[]{:S(2)}) collective-permute-start(bf16[576,1536]{1,0:T(8,128)(2,1)S(1)} %pad_maximum_fusion.2.rest_0_), channel_id=1, source_target_pairs={{0,1},{1,2},{2,3},{4,5},{5,6},{6,7},{8,9},{9,10},{10,11},{12,13},{... | collective-permute-start | bytes 5308424 | tf_op jit(solution)/shard_map/ppermute | solution.py:992
  233.4 22.4 %collective-permute-start.20 = (bf16[512,1536]{1,0:T(8,128)(2,1)}, bf16[512,1536]{1,0:T(8,128)(2,1)}, u32[]{:S(2)}, u32[]{:S(2)}) collective-permute-start(bf16[512,1536]{1,0:T(8,128)(2,1)} %get-tuple-element.114.rows.normed), channel_id=1, source_target_pairs={{0,4},{4,0},{8,12},{12,8},{16,20},{20,16},{24,28},{28,24},{1,5},{5... | collective-permute-start | bytes 4718600 | tf_op jit(solution)/shard_map/ppermute | solution.py:1051
  233.5 40.6 %collective-permute-start.18 = (bf16[512,1536]{1,0:T(8,128)(2,1)}, bf16[512,1536]{1,0:T(8,128)(2,1)}, u32[]{:S(2)}, u32[]{:S(2)}) collective-permute-start(bf16[512,1536]{1,0:T(8,128)(2,1)} %get-tuple-element.114.rows.normed), channel_id=1, source_target_pairs={{0,8},{4,12},{8,0},{12,4},{16,24},{20,28},{24,16},{28,20},{1,9},{5... | collective-permute-start | bytes 4718600 | tf_op jit(solution)/shard_map/ppermute | solution.py:1051
  235.0 39.1 %collective-permute-start.19 = (bf16[512,1536]{1,0:T(8,128)(2,1)}, bf16[512,1536]{1,0:T(8,128)(2,1)}, u32[]{:S(2)}, u32[]{:S(2)}) collective-permute-start(bf16[512,1536]{1,0:T(8,128)(2,1)} %get-tuple-element.114.rows.normed), channel_id=1, source_target_pairs={{0,16},{4,20},{8,24},{12,28},{16,0},{20,4},{24,8},{28,12},{1,17},{... | collective-permute-start | bytes 4718600 | tf_op jit(solution)/shard_map/ppermute | solution.py:1051
  274.1 17.9 %collective-permute-start.26 = (bf16[512,1536]{1,0:T(8,128)(2,1)}, bf16[512,1536]{1,0:T(8,128)(2,1)}, u32[]{:S(2)}, u32[]{:S(2)}) collective-permute-start(bf16[512,1536]{1,0:T(8,128)(2,1)} %collective-permute-done.18.rows), channel_id=1, source_target_pairs={{0,4},{4,0},{8,12},{12,8},{16,20},{20,16},{24,28},{28,24},{1,5},{5... | collective-permute-start | bytes 4718600 | tf_op jit(solution)/shard_map/ppermute | solution.py:1051
  274.2 26.2 %collective-permute-start.25 = (bf16[512,1536]{1,0:T(8,128)(2,1)}, bf16[512,1536]{1,0:T(8,128)(2,1)S(1)}, u32[]{:S(2)}, u32[]{:S(2)}) collective-permute-start(bf16[512,1536]{1,0:T(8,128)(2,1)} %collective-permute-done.19.rows), channel_id=1, source_target_pairs={{0,4},{4,0},{8,12},{12,8},{16,20},{20,16},{24,28},{28,24},{1,5},{5... | collective-permute-start | bytes 4718600 | tf_op jit(solution)/shard_map/ppermute | solution.py:1051
  278.9 27.8 %collective-permute-start.23 = (bf16[256,1536]{1,0:T(8,128)(2,1)}, bf16[256,1536]{1,0:T(8,128)(2,1)S(1)}, u32[]{:S(2)}, u32[]{:S(2)}) collective-permute-start(bf16[256,1536]{1,0:T(8,128)(2,1)} %slice.459), channel_id=1, source_target_pairs={{0,16},{4,20},{8,24},{12,28},{16,0},{20,4},{24,8},{28,12},{1,17},{... | collective-permute-start | bytes 2359304 | tf_op jit(solution)/shard_map/ppermute | solution.py:1051
  279.7 27.1 %collective-permute-start.24 = (bf16[256,1536]{1,0:T(8,128)(2,1)}, bf16[256,1536]{1,0:T(8,128)(2,1)}, u32[]{:S(2)}, u32[]{:S(2)}) collective-permute-start(bf16[256,1536]{1,0:T(8,128)(2,1)} %slice.460), channel_id=1, source_target_pairs={{0,8},{4,12},{8,0},{12,4},{16,24},{20,28},{24,16},{28,20},{1,9},{5... | collective-permute-start | bytes 2359304 | tf_op jit(solution)/shard_map/ppermute | solution.py:1051
  281.7 78.2 %collective-permute-start.29 = (bf16[576,1536]{1,0:T(8,128)(2,1)}, bf16[576,1536]{1,0:T(8,128)(2,1)S(1)}, u32[]{:S(2)}, u32[]{:S(2)}) collective-permute-start(bf16[576,1536]{1,0:T(8,128)(2,1)} %select_select_fusion), channel_id=1, source_target_pairs={{3,1},{1,0},{0,2},{2,3},{7,5},{5,4},{4,6},{6,7},{11,9},{9,8},{8,10... | collective-permute-start | bytes 5308424 | tf_op jit(solution)/shard_map/ppermute | solution.py:1001
  292.0 67.8 %collective-permute-start.28 = (bf16[576,1536]{1,0:T(8,128)(2,1)S(1)}, bf16[576,1536]{1,0:T(8,128)(2,1)S(1)}, u32[]{:S(2)}, u32[]{:S(2)}) collective-permute-start(bf16[576,1536]{1,0:T(8,128)(2,1)S(1)} %pad_maximum_fusion.2.rest_0_), channel_id=1, source_target_pairs={{0,3},{3,0},{4,7},{7,4},{8,11},{11,8},{12,15},{15,12},{16,19},{19,... | collective-permute-start | bytes 5308424 | tf_op jit(solution)/shard_map/ppermute | solution.py:994
  399.2 108.6 %collective-permute-start.35 = (bf16[4,512,1536]{2,1,0:T(8,128)(2,1)}, bf16[4,512,1536]{2,1,0:T(8,128)(2,1)S(1)}, u32[]{:S(2)}, u32[]{:S(2)}) collective-permute-start(bf16[4,512,1536]{2,1,0:T(8,128)(2,1)} %combine.6), channel_id=1, source_target_pairs={{0,4},{4,0},{8,12},{12,8},{16,20},{20,16},{24,28},{28,24},{1,5},{5... | collective-permute-start | bytes 18874376 | tf_op jit(solution)/shard_map/ppermute | solution.py:1051
  406.9 152.2 %collective-permute-start.30 = (bf16[4,512,1536]{2,1,0:T(8,128)(2,1)}, bf16[4,512,1536]{2,1,0:T(8,128)(2,1)}, u32[]{:S(2)}, u32[]{:S(2)}) collective-permute-start(bf16[4,512,1536]{2,1,0:T(8,128)(2,1)} %combine.5), channel_id=1, source_target_pairs={{0,4},{4,0},{8,12},{12,8},{16,20},{20,16},{24,28},{28,24},{1,5},{5... | collective-permute-start | bytes 18874376 | tf_op jit(solution)/shard_map/ppermute | solution.py:1051
  417.1 79.7 %collective-permute-start.36 = (bf16[576,1536]{1,0:T(8,128)(2,1)}, bf16[576,1536]{1,0:T(8,128)(2,1)S(1)}, u32[]{:S(2)}, u32[]{:S(2)}) collective-permute-start(bf16[576,1536]{1,0:T(8,128)(2,1)} %get-tuple-element.175), channel_id=1, source_target_pairs={{1,3},{0,1},{2,0},{3,2},{5,7},{4,5},{6,4},{7,6},{9,11},{8,9},{10,8... | collective-permute-start | bytes 5308424 | tf_op jit(solution)/shard_map/ppermute | solution.py:1018
  417.1 103.5 %collective-permute-start.39 = (bf16[576,1536]{1,0:T(8,128)(2,1)}, bf16[576,1536]{1,0:T(8,128)(2,1)}, u32[]{:S(2)}, u32[]{:S(2)}) collective-permute-start(bf16[576,1536]{1,0:T(8,128)(2,1)} %get-tuple-element.174), channel_id=1, source_target_pairs={{0,3},{3,0},{4,7},{7,4},{8,11},{11,8},{12,15},{15,12},{16,19},{19,... | collective-permute-start | bytes 5308424 | tf_op jit(solution)/shard_map/ppermute | solution.py:1019
  502.3 56.7 %collective-permute-start.37 = (bf16[576,1536]{1,0:T(8,128)(2,1)}, bf16[576,1536]{1,0:T(8,128)(2,1)}, u32[]{:S(2)}, u32[]{:S(2)}) collective-permute-start(bf16[576,1536]{1,0:T(8,128)(2,1)} %get-tuple-element.261), channel_id=1, source_target_pairs={{0,1},{1,2},{2,3},{4,5},{5,6},{6,7},{8,9},{9,10},{10,11},{12,13},{... | collective-permute-start | bytes 5308424 | tf_op jit(solution)/shard_map/ppermute | solution.py:1031
  506.5 52.6 %collective-permute-start.38 = (bf16[576,1536]{1,0:T(8,128)(2,1)}, bf16[576,1536]{1,0:T(8,128)(2,1)}, u32[]{:S(2)}, u32[]{:S(2)}) collective-permute-start(bf16[576,1536]{1,0:T(8,128)(2,1)} %get-tuple-element.260), channel_id=1, source_target_pairs={{1,0},{2,1},{3,2},{5,4},{6,5},{7,6},{9,8},{10,9},{11,10},{13,12},{... | collective-permute-start | bytes 5308424 | tf_op jit(solution)/shard_map/ppermute | solution.py:1032
  524.7 34.4 %collective-permute-start.40 = (bf16[2,256,1536]{2,1,0:T(8,128)(2,1)}, bf16[2,256,1536]{2,1,0:T(8,128)(2,1)}, u32[]{:S(2)}, u32[]{:S(2)}) collective-permute-start(bf16[2,256,1536]{2,1,0:T(8,128)(2,1)} %pad_maximum_fusion.5), channel_id=1, source_target_pairs={{0,8},{4,12},{8,0},{12,4},{16,24},{20,28},{24,16},{28,20},{1,9},{5... | collective-permute-start | bytes 4718600 | tf_op jit(solution)/shard_map/ppermute | solution.py:1051
  527.5 31.6 %collective-permute-start.42 = (bf16[2,256,1536]{2,1,0:T(8,128)(2,1)}, bf16[2,256,1536]{2,1,0:T(8,128)(2,1)}, u32[]{:S(2)}, u32[]{:S(2)}) collective-permute-start(bf16[2,256,1536]{2,1,0:T(8,128)(2,1)} %pad_maximum_fusion.6), channel_id=1, source_target_pairs={{0,16},{4,20},{8,24},{12,28},{16,0},{20,4},{24,8},{28,12},{1,17},{... | collective-permute-start | bytes 4718600 | tf_op jit(solution)/shard_map/ppermute | solution.py:1051
  563.6 19.6 %collective-permute-start.41 = (bf16[256,1536]{1,0:T(8,128)(2,1)S(1)}, bf16[256,1536]{1,0:T(8,128)(2,1)S(1)}, u32[]{:S(2)}, u32[]{:S(2)}) collective-permute-start(bf16[256,1536]{1,0:T(8,128)(2,1)S(1)} %get-tuple-element.230), channel_id=1, source_target_pairs={{0,16},{4,20},{8,24},{12,28},{16,0},{20,4},{24,8},{28,12},{1,17},{... | collective-permute-start | bytes 2359304 | tf_op jit(solution)/shard_map/ppermute | solution.py:1051
  564.9 19.3 %collective-permute-start.43 = (bf16[256,1536]{1,0:T(8,128)(2,1)S(1)}, bf16[256,1536]{1,0:T(8,128)(2,1)S(1)}, u32[]{:S(2)}, u32[]{:S(2)}) collective-permute-start(bf16[256,1536]{1,0:T(8,128)(2,1)S(1)} %get-tuple-element.228), channel_id=1, source_target_pairs={{0,8},{4,12},{8,0},{12,4},{16,24},{20,28},{24,16},{28,20},{1,9},{5... | collective-permute-start | bytes 2359304 | tf_op jit(solution)/shard_map/ppermute | solution.py:1051
  650.3 109.8 %collective-permute-start.45 = (bf16[4,4,208,896]{3,2,1,0:T(8,128)(2,1)}, bf16[4,4,208,896]{3,2,1,0:T(8,128)(2,1)}, u32[]{:S(2)}, u32[]{:S(2)}) collective-permute-start(bf16[4,4,208,896]{3,2,1,0:T(8,128)(2,1)} %get-tuple-element.190), channel_id=1, source_target_pairs={{0,4},{4,0},{8,12},{12,8},{16,20},{20,16},{24,28},{28,24},{1,5},{5... | collective-permute-start | bytes 17891336 | tf_op jit(solution)/shard_map/ppermute | solution.py:1051
  654.3 37.1 %collective-permute-start.33 = (bf16[2,256,1536]{2,1,0:T(8,128)(2,1)}, bf16[2,256,1536]{2,1,0:T(8,128)(2,1)}, u32[]{:S(2)}, u32[]{:S(2)}) collective-permute-start(bf16[2,256,1536]{2,1,0:T(8,128)(2,1)} %pad_maximum_fusion.4), channel_id=1, source_target_pairs={{0,16},{4,20},{8,24},{12,28},{16,0},{20,4},{24,8},{28,12},{1,17},{... | collective-permute-start | bytes 4718600 | tf_op jit(solution)/shard_map/ppermute | solution.py:1051
  656.4 36.8 %collective-permute-start.31 = (bf16[2,256,1536]{2,1,0:T(8,128)(2,1)}, bf16[2,256,1536]{2,1,0:T(8,128)(2,1)}, u32[]{:S(2)}, u32[]{:S(2)}) collective-permute-start(bf16[2,256,1536]{2,1,0:T(8,128)(2,1)} %pad_maximum_fusion.3), channel_id=1, source_target_pairs={{0,8},{4,12},{8,0},{12,4},{16,24},{20,28},{24,16},{28,20},{1,9},{5... | collective-permute-start | bytes 4718600 | tf_op jit(solution)/shard_map/ppermute | solution.py:1051
  657.8 54.5 %collective-permute-start.48 = (bf16[576,1536]{1,0:T(8,128)(2,1)}, bf16[576,1536]{1,0:T(8,128)(2,1)}, u32[]{:S(2)}, u32[]{:S(2)}) collective-permute-start(bf16[576,1536]{1,0:T(8,128)(2,1)} %get-tuple-element.192), channel_id=1, source_target_pairs={{1,3},{0,1},{2,0},{3,2},{5,7},{4,5},{6,4},{7,6},{9,11},{8,9},{10,8... | collective-permute-start | bytes 5308424 | tf_op jit(solution)/shard_map/ppermute | solution.py:1018
  666.6 122.4 %collective-permute-start.49 = (bf16[576,1536]{1,0:T(8,128)(2,1)}, bf16[576,1536]{1,0:T(8,128)(2,1)}, u32[]{:S(2)}, u32[]{:S(2)}) collective-permute-start(bf16[576,1536]{1,0:T(8,128)(2,1)} %get-tuple-element.193), channel_id=1, source_target_pairs={{0,3},{3,0},{4,7},{7,4},{8,11},{11,8},{12,15},{15,12},{16,19},{19,... | collective-permute-start | bytes 5308424 | tf_op jit(solution)/shard_map/ppermute | solution.py:1019
  695.9 70.7 %collective-permute-start.32 = (bf16[256,1536]{1,0:T(8,128)(2,1)S(1)}, bf16[256,1536]{1,0:T(8,128)(2,1)S(1)}, u32[]{:S(2)}, u32[]{:S(2)}) collective-permute-start(bf16[256,1536]{1,0:T(8,128)(2,1)S(1)} %get-tuple-element.238), channel_id=1, source_target_pairs={{0,16},{4,20},{8,24},{12,28},{16,0},{20,4},{24,8},{28,12},{1,17},{... | collective-permute-start | bytes 2359304 | tf_op jit(solution)/shard_map/ppermute | solution.py:1051
  697.1 70.6 %collective-permute-start.34 = (bf16[256,1536]{1,0:T(8,128)(2,1)S(1)}, bf16[256,1536]{1,0:T(8,128)(2,1)S(1)}, u32[]{:S(2)}, u32[]{:S(2)}) collective-permute-start(bf16[256,1536]{1,0:T(8,128)(2,1)S(1)} %get-tuple-element.239), channel_id=1, source_target_pairs={{0,8},{4,12},{8,0},{12,4},{16,24},{20,28},{24,16},{28,20},{1,9},{5... | collective-permute-start | bytes 2359304 | tf_op jit(solution)/shard_map/ppermute | solution.py:1051
  716.7 89.5 %collective-permute-start.56 = (bf16[576,1536]{1,0:T(8,128)(2,1)}, bf16[576,1536]{1,0:T(8,128)(2,1)}, u32[]{:S(2)}, u32[]{:S(2)}) collective-permute-start(bf16[576,1536]{1,0:T(8,128)(2,1)} %get-tuple-element.258), channel_id=1, source_target_pairs={{0,1},{1,2},{2,3},{4,5},{5,6},{6,7},{8,9},{9,10},{10,11},{12,13},{... | collective-permute-start | bytes 5308424 | tf_op jit(solution)/shard_map/ppermute | solution.py:1031
  760.1 46.1 %collective-permute-start.57 = (bf16[576,1536]{1,0:T(8,128)(2,1)}, bf16[576,1536]{1,0:T(8,128)(2,1)}, u32[]{:S(2)}, u32[]{:S(2)}) collective-permute-start(bf16[576,1536]{1,0:T(8,128)(2,1)} %get-tuple-element.259), channel_id=1, source_target_pairs={{1,0},{2,1},{3,2},{5,4},{6,5},{7,6},{9,8},{10,9},{11,10},{13,12},{... | collective-permute-start | bytes 5308424 | tf_op jit(solution)/shard_map/ppermute | solution.py:1032
  766.6 33.6 %collective-permute-start.47 = (bf16[2,2,208,896]{3,2,1,0:T(8,128)(2,1)}, bf16[2,2,208,896]{3,2,1,0:T(8,128)(2,1)}, u32[]{:S(2)}, u32[]{:S(2)}) collective-permute-start(bf16[2,2,208,896]{3,2,1,0:T(8,128)(2,1)} %pad_maximum_fusion.9), channel_id=1, source_target_pairs={{0,16},{4,20},{8,24},{12,28},{16,0},{20,4},{24,8},{28,12},{1,17},{... | collective-permute-start | bytes 4472840 | tf_op jit(solution)/shard_map/ppermute | solution.py:1051
  767.7 33.4 %collective-permute-start.46 = (bf16[2,2,208,896]{3,2,1,0:T(8,128)(2,1)}, bf16[2,2,208,896]{3,2,1,0:T(8,128)(2,1)}, u32[]{:S(2)}, u32[]{:S(2)}) collective-permute-start(bf16[2,2,208,896]{3,2,1,0:T(8,128)(2,1)} %pad_maximum_fusion.8), channel_id=1, source_target_pairs={{0,8},{4,12},{8,0},{12,4},{16,24},{20,28},{24,16},{28,20},{1,9},{5... | collective-permute-start | bytes 4472840 | tf_op jit(solution)/shard_map/ppermute | solution.py:1051
  833.9 23.5 %collective-permute-start.55 = (bf16[208,896]{1,0:T(8,128)(2,1)S(1)}, bf16[208,896]{1,0:T(8,128)(2,1)S(1)}, u32[]{:S(2)}, u32[]{:S(2)}) collective-permute-start(bf16[208,896]{1,0:T(8,128)(2,1)S(1)} %get-tuple-element.264), channel_id=1, source_target_pairs={{0,3},{3,0},{4,7},{7,4},{8,11},{11,8},{12,15},{15,12},{16,19},{19,... | collective-permute-start | bytes 1118216 | tf_op jit(solution)/shard_map/ppermute | solution.py:1019
  840.6 17.3 %collective-permute-start.53 = (bf16[208,896]{1,0:T(8,128)(2,1)S(1)}, bf16[208,896]{1,0:T(8,128)(2,1)S(1)}, u32[]{:S(2)}, u32[]{:S(2)}) collective-permute-start(bf16[208,896]{1,0:T(8,128)(2,1)S(1)} %get-tuple-element.262), channel_id=1, source_target_pairs={{0,1},{1,2},{2,3},{4,5},{5,6},{6,7},{8,9},{9,10},{10,11},{12,13},{... | collective-permute-start | bytes 1118216 | tf_op jit(solution)/shard_map/ppermute | solution.py:1031
  (61 other events, 889.3 us)
Sparse Core Ops, SparseCore 0:
  107.9 72.6 all-gather.2

commit v7 on v6

--- a/solution.py
+++ b/solution.py
@@ -63,16 +63,17 @@
     return values * cosine - pltpu.roll(values, HEAD_DIM // 2, 1) * sine
 
 
-PIECES = tuple(
-    (flip_bits + core, slots)
-    for core in (0, 1)
-    for flip_bits, slots in (
-        (0, (0, 1, 2, 3)),
-        (2, (0, 1, 2, 3)),
-        (4, (0, 1, 2, 3)),
-        (6, (0, 1)),
-        (6, (2, 3)),
-    )
+SLOTS = range(4)
+PIECES = (
+    tuple((0, slot) for slot in SLOTS),
+    tuple((2, slot) for slot in SLOTS),
+    tuple((4, slot) for slot in SLOTS),
+    ((6, 0), (6, 1)),
+    ((6, 2), (6, 3)),
+    tuple((1, slot) for slot in SLOTS),
+    tuple((flip_bits, slot) for flip_bits in (3, 5) for slot in SLOTS),
+    ((7, 0), (7, 1)),
+    ((7, 2), (7, 3)),
 )
 EXTRA = 16
 
@@ -82,9 +83,9 @@
         return [pltpu.make_async_copy(refs[0], target, sem)]
     depth = refs[0].shape[1] - EXTRA
     copies = []
-    for ref, (flip_bits, slots) in zip(refs, PIECES):
-        row = pl.multiple_of((info[0] ^ flip_bits) * depth, depth)
-        for at, slot in enumerate(slots):
+    for ref, parts in zip(refs, PIECES):
+        for at, (flip_bits, slot) in enumerate(parts):
+            row = pl.multiple_of((info[0] ^ flip_bits) * depth, depth)
             col = pl.multiple_of(info[2 + slot] * width, 128)
             copies.append(
                 pltpu.make_async_copy(
@@ -100,8 +101,8 @@
     refs, (out, sem) = rest[:-2], rest[-2:]
     depth = refs[0].shape[1] - EXTRA
     copies = []
-    for ref, (flip_bits, slots) in zip(refs, PIECES):
-        for at, slot in enumerate(slots):
+    for ref, parts in zip(refs, PIECES):
+        for at, (flip_bits, slot) in enumerate(parts):
             to = (info[0] ^ flip_bits) * QUARTERS + info[2 + slot]
             copies.append(pltpu.make_async_copy(ref.at[at, pl.ds(depth, EXTRA)], out.at[to], sem))
     run_all(copies)
@@ -987,23 +988,24 @@
 FAR = [(0, 3), (3, 0)]
 
 
-def send_first(block, chain=False):
-    above = lax.ppermute(block, "cols", DOWN)
-    below = lax.ppermute(block, "cols", UP)
-    later = after(block, above, below) if chain else block
-    return above, below, lax.ppermute(later, "cols", FAR)
-
-
-def send_second(block, first):
+def send_near(block):
+    return lax.ppermute(block, "cols", DOWN), lax.ppermute(block, "cols", UP)
+
+
+def send_far(block):
+    return lax.ppermute(block, "cols", FAR)
+
+
+def send_second(block, near):
     place = lax.axis_index("cols")
-    above, below, _ = first
+    above, below = near
     payload = jnp.where(place == 1, above, jnp.where(place == 2, below, block))
     return lax.ppermute(payload, "cols", [(3, 1), (1, 0), (0, 2), (2, 3)])
 
 
-def slot_list(block, first, second):
+def slot_list(block, near, second, far):
     place = lax.axis_index("cols")
-    above, below, far = first
+    above, below = near
     end = (place == 0) | (place == 3)
     return [
         block,
@@ -1013,11 +1015,9 @@
     ]
 
 
-def reduce_first(second, fourth):
-    return (
-        lax.ppermute(second, "cols", [(1, 3), (0, 1), (2, 0), (3, 2)]),
-        lax.ppermute(fourth, "cols", FAR),
-    )
+def reduce_first(second, fourth, chain=False):
+    relay = lax.ppermute(second, "cols", [(1, 3), (0, 1), (2, 0), (3, 2)])
+    return relay, lax.ppermute(after(fourth, relay) if chain else fourth, "cols", FAR)
 
 
 def reduce_second(third, fourth, relay):
@@ -1055,7 +1055,7 @@
     return (one.astype(WIDE) + two.astype(WIDE)).astype(LOW)
 
 
-def reduce_chips(keep, got, hold=()):
+def reduce_chips(keep, got):
     half = keep.shape[1] // 2
 
     def sums(chips, part):
@@ -1064,8 +1064,6 @@
     one, two = slice(0, half), slice(half, None)
     got_x = flip(sums((1, 3), one), 2)
     got_y = flip(sums((2, 3), two), 4)
-    if hold:
-        got_x, got_y = after((got_x, got_y), *hold)
     near_x = sums((0, 2), one)
     near_y = sums((0, 1), two)
     got_xy = flip(add_low(near_x[1], got_x[1]), 4)
@@ -1131,7 +1129,7 @@
         )
         for expert in range(local_experts)
     ]
-    firsts, seconds = ([], [])
+    nears, seconds, fars = ([], [], [])
     if fast:
         wide = packed.shape[1]
         gains = jnp.concatenate([attention_gain, experts_gain])[None, :]
@@ -1145,26 +1143,28 @@
             ],
             axis=0,
         )
-        packed_first = send_first(packed)
-        packed_second = send_second(packed, packed_first)
-        own = jnp.stack(slot_list(packed, packed_first, packed_second))
-        ahead = packed_first[:2]
-        for expert_at in range(local_experts):
-            block = after(shard_blocks[expert_at], *ahead)
+        packed_near = send_near(packed)
+        packed_far = send_far(packed)
+        packed_second = send_second(packed, packed_near)
+        own = jnp.stack(slot_list(packed, packed_near, packed_second, packed_far))
+
+        def gather_expert(*earlier):
+            expert_at = len(nears)
+            block = after(shard_blocks[expert_at], *earlier)
             shard_blocks[expert_at] = block
-            first = send_first(block, chain=True)
-            firsts.append(first)
-            seconds.append(send_second(block, first))
-            ahead = (first[2], seconds[-1])
+            nears.append(send_near(block))
+            seconds.append(send_second(block, nears[expert_at]))
+
+        gather_expert(*packed_near)
         own = after(own, info, cosine, sine)
         beside, across = flip(own, 2), flip(own, 4)
-        beside, across = after((beside, across), *firsts[0][:2])
-        same = [own, beside, across, flip(beside[:2], 4), flip(across[2:], 2)]
-        pieces = same + [flip(piece, 1) for piece in same]
+        own_in = flip(own, 1)
+        beside, across = after((beside, across), own_in, *nears[0])
+        corner = [flip(beside[:2], 4), flip(across[2:], 2)]
+        pair_in = flip(jnp.concatenate([beside, across], axis=0), 1)
+        corner_in = [flip(piece, 1) for piece in corner]
+        pieces = [own, beside, across, *corner, own_in, pair_in, *corner_in]
         query_refs = pair_refs = out_refs = pieces
-        expert_refs = [
-            [shard_blocks[i], seconds[i], *firsts[i]] for i in range(local_experts)
-        ]
         extra_rows = extras(info, pieces)
         router_all = extra_rows[:, :router_part, :depth]
         attention_scale = extra_rows[:, router_part, :gain_part]
@@ -1223,13 +1223,16 @@
     pairs = [(i + 1, i) for i in range(0, col_count, 2)]
     partner = lax.ppermute(own_pair, "cols", pairs)
     queries = query(info, normed, cosine, sine, query_refs)
+    if fast:
+        queries = after(queries, seconds[0])
+        fars.append(send_far(after(shard_blocks[0], seconds[0], queries)))
     heads = attention(info, queries, own_pair, partner)
     residual, normed_two = out_projection(info, heads, tokens, experts_scale, out_refs)
 
     if fast:
         beside, across = flip(normed_two, 2), flip(normed_two, 4)
         beside_in = flip(normed_two, 1)
-        chosen = after(chosen, firsts[0][2], seconds[0])
+        gather_expert(fars[0], normed_two)
         grad_all = after(grad_all, normed_two)
     else:
         rows_all = lax.all_gather(normed_two, "rows", axis=0)
@@ -1244,16 +1247,22 @@
         half = TOK_DEV // 2
         picked = place_block(0, normed_two, None)
         picked = place_block(1, beside_in, picked)
-        beside, across = after((beside, across), picked, grad_rows, *firsts[1][:2])
+        beside, across = after((beside, across), picked, grad_rows, *nears[1])
         corner = [flip(beside[:half], 4), flip(across[half:], 2)]
         picked = place_block(2, beside, picked)
         picked = place_block(4, across, picked)
-        picked = place_block(3, flip(beside, 1), picked)
-        picked = place_block(5, flip(across, 1), picked)
+        beside_in = flip(beside, 1)
+        across_in = flip(after(across, beside_in), 1)
+        picked = place_block(3, beside_in, picked)
+        picked = place_block(5, across_in, picked)
         corner = jnp.concatenate(after(corner, picked), axis=0)
         corner_in = flip(corner, 1)
         picked = place_block(6, corner, picked)
         picked = place_block(7, corner_in, picked)
+        fars.append(send_far(after(shard_blocks[1], seconds[1], picked)))
+        expert_refs = [
+            [shard_blocks[i], seconds[i], *nears[i], fars[i]] for i in range(local_experts)
+        ]
     else:
         picked = None
         for q in range(row_count):
@@ -1266,8 +1275,10 @@
     out_rows, back_rows, gate_dots, reduced, marks = ([], [], [], [], [])
     for e in range(local_experts):
         rows_in = token_rows[e]
+        if fast and e == 0:
+            rows_in = after(rows_in, seconds[1])
         if fast and e == 1:
-            rows_in = after(rows_in, firsts[1][2], seconds[1], own_slot, third)
+            rows_in = after(rows_in, fars[1], second, fourth, own_slot, third)
         out_row, back_row, grad_row, acts, dots = expert(
             info, rows_in, grad_rows[e], share_rows[e], expert_refs[e], col_count
         )
@@ -1276,16 +1287,17 @@
         gate_dots.append(dots.reshape(row_count, capacity, 1))
         if fast:
             if e == 1:
+                back_rows = after(back_rows, marks[0][0])
                 got = flip(combine(chosen, back_rows, 1, 2), 1)
                 acts = after(acts, got)
             second, fourth = expert_grads(acts, token_rows[e], grad_row, (1, 3))
             if e == 1:
-                got = after(got, *marks[0], second)
-                waits = reduced[0][2]
-                second_out, fourth_out = after((second, fourth), *waits)
+                second_out, fourth_out = after(
+                    (second, fourth), marks[0][1], *reduced[0][2]
+                )
             else:
                 second_out, fourth_out = second, fourth
-            sent_first = reduce_first(second_out, fourth_out)
+            sent_first = reduce_first(second_out, fourth_out, chain=True)
             marks.append(sent_first)
             own_slot, third = expert_grads(acts, token_rows[e], grad_row, (0, 2))
             sent_second = reduce_second(third, fourth, sent_first[0])
@@ -1302,10 +1314,14 @@
     grad_shares = lax.all_to_all(spread_dots, "rows", split_axis=0, concat_axis=0, tiled=True)
     grad_shares = grad_shares.reshape(expert_total, TOK_DEV)
     if fast:
-        back_parts = reduce_chips(combine(chosen, back_rows, 0, 2), got)
+        back_keep = combine(chosen, back_rows, 0, 2)
+        back_parts = reduce_chips(back_keep, got)
+        out_rows = [after(a, back_keep) for a in out_rows]
         out_got = flip(combine(chosen, out_rows, 1, 2), 1)
         out_keep = combine(chosen, out_rows, 0, 2)
-        grad_shares = after(grad_shares, own_slot, third, out_keep, out_got, *reduced[0][2])
+        grad_shares = after(
+            grad_shares, own_slot, third, out_keep, out_got, marks[0][1], *reduced[0][2]
+        )
     else:
 
         def summed(rows):
@@ -1347,6 +1363,7 @@
     arrived = lax.ppermute(source_grad.astype(LOW), "cols", [(j, i) for i, j in pairs])
     grad_pair = join_grads(info, own_grad, source_grad, arrived, cosine, sine)
     if fast:
+        grad_branch = after(grad_branch, marks[1][0])
         keep, send = weight_grads(
             info,
             [normed, heads],
@@ -1362,7 +1379,7 @@
 
     if fast:
         mixture = reduce_chips(out_keep, out_got)
-        slots = sum_parts(reduce_chips(keep, sent, marks[1]))
+        slots = sum_parts(reduce_chips(keep, sent))
         width = query_part + 2 * key_part
         gain_sums = sum(
             jnp.sum(own[i, :depth, :width].astype(WIDE) * slots[i, :depth, :width], axis=1)

time: 882 us -> 842 us (0.955)
  starting transfers between devices: 172 us -> 101 us
  waiting for transfers between devices: 261 us -> 290 us
    ppermute x15, waiting for transfers between devices: 160 us -> 53.9 us  [the longest x6 31.1 us: send_near(): return (lax.ppermute(block, 'cols', DOWN), lax.ppermute(block, 'cols', UP))]
    ppermute x1, waiting for transfers between devices: 0.01 us -> 49.5 us  [on_device(): partner = lax.ppermute(own_pair, 'cols', pairs)]
    ppermute x3, starting transfers between devices: 59.7 us -> 15.3 us  [reduce_second(): lax.ppermute(upward_load, 'cols', UP)]
    ppermute x3, waiting for transfers between devices: 4.42 us -> 33.1 us  [reduce_second(): lax.ppermute(downward_load, 'cols', DOWN)]
    ppermute x3, waiting for transfers between devices: 0.47 us -> 27 us  [reduce_second(): lax.ppermute(upward_load, 'cols', UP)]
    ppermute x15, starting transfers between devices: 65.4 us -> 45.1 us  [the longest x6 21.2 us: send_near(): return (lax.ppermute(block, 'cols', DOWN), lax.ppermute(block, 'cols', UP))]
    ppermute x32 -> x31, waiting for transfers between devices: 62.1 us -> 77.9 us  [flip(): return lax.ppermute(block, 'rows', [(i, i ^ bit) for i in range(count)])]
    all_to_all x1, waiting for transfers between devices: 0.87 us -> 15.2 us  [on_device(): lax.all_to_all(spread_dots, 'rows', split_axis=0, concat_axis=0, tiled=True)]
  transfers between devices with their start and end apart: 60 -> 59, of which waited for: 25 -> 25; matrix products, arithmetic and copies ran while one was open for 10% -> 11% of each run, Pallas kernels for 24% -> 33%
where the time goes in v7:
time: 842 us; the launch traced here: 831 us
  Pallas kernels  297 us (35%)
  waiting for transfers between devices  290 us (34%)
  starting transfers between devices  101 us (12%)
  other arithmetic  79.6 us (9%)
  local copies, waits for them, and re-layouts  47.6 us (6%)
  between operations  15.6 us (2%)
    ppermute x31, waiting for transfers between devices, flip(): return lax.ppermute(block, 'rows', [(i, i ^ bit) for i in range(count)])  77.9 us
    pallas_call x2, Pallas kernels, expert(): pl.pallas_call(functools.partial(expert_kernel, slots), grid=(height // E...  60.4 us
    ppermute x1, waiting for transfers between devices, on_device(): partner = lax.ppermute(own_pair, 'cols', pairs)  49.5 us
    pallas_call x8, Pallas kernels, dispatch(): pl.pallas_call(functools.partial(dispatch_kernel, local), grid_spec=pltpu...  41.2 us
    pallas_call x4, Pallas kernels, expert_grads(): pl.pallas_call(functools.partial(expert_grads_kernel, slots), grid=(D //...  39.5 us
    ppermute x3, waiting for transfers between devices, reduce_second(): lax.ppermute(downward_load, 'cols', DOWN)  33.1 us
    ppermute x6, waiting for transfers between devices, send_near(): return (lax.ppermute(block, 'cols', DOWN), lax.ppermute(block, 'cols', UP))  31.1 us
    pallas_call x4, Pallas kernels, combine(): pl.pallas_call(functools.partial(combine_kernel, len(rows)), grid=(number...  30.9 us
  transfers between devices with their start and end apart: 59, of which 25 were waited for; matrix products, arithmetic and copies ran while one was open for 11% of the time, Pallas kernels for 33%

profile of v7, /device:TPU:0, one launch (start us, length us, event | category | flops | bytes accessed | tf_op | source)
XLA Modules:
  0.0 830.9 jit_solution(8630778773976665265)
XLA Ops:
  14.0 5.6 collective-permute-start.1
  28.6 7.9 collective-permute-done.3
  43.3 5.8 collective-permute-start.8
  56.5 29.8 %collective-permute-done.7.rest_2_ = bf16[576,1536]{1,0:T(8,128)(2,1)S(1)} collective-permute-done((bf16[576,1536]{1,0:T(8,128)(2,1)S(1)}, bf16[576,1536]{1,0:T(8,128)(2,1)S(1)}, u32[]{:S(2)}, u32[]{:S(2)}) %collective-permute-start.7) | collective-permute-done | bytes 1769504 | tf_op jit(solution)/shard_map/ppermute | solution.py:992
  91.3 15.8 %collective-permute-done.9.rest_3_.rest_9_.rest_12_ = bf16[2,208,896]{2,1,0:T(8,128)(2,1)S(1)} collective-permute-done((bf16[2,208,896]{2,1,0:T(8,128)(2,1)S(1)}, bf16[2,208,896]{2,1,0:T(8,128)(2,1)S(1)}, u32[]{:S(2)}, u32[]{:S(2)}) %collective-permute-start.9) | collective-permute-done | bytes 745504 | tf_op jit(solution)/shard_map/ppermute | solution.py:1051
  122.4 5.0 norm_key_value.1
  127.4 9.0 %query_projection.1.queries = bf16[512,1536]{1,0:T(8,128)(2,1)} custom-call(s32[16]{0:T(128)} %concatenate.39.info, bf16[512,1536]{1,0:T(8,128)(2,1)} %get-tuple-element.114.normed.rest_0_, f32[512,128]{1,0:T(8,128)} %get-tuple-element.296.cosine, f32[512,128]{1,0:T(8,128)} %get-tuple-element.297.sine, bf16[4,208,896]{2,1,0:T(8,128)(2,1)} %copy-done.1, ...), custom_call_target="tpu_custom_call" | custom-call | flops 1 | bytes 1 | tf_op jit(solution)/shard_map/query_projection/pallas_call | solution.py:192
  136.4 20.9 %collective-permute-done.14.rest_1_ = bf16[576,1536]{1,0:T(8,128)(2,1)} collective-permute-done((bf16[576,1536]{1,0:T(8,128)(2,1)}, bf16[576,1536]{1,0:T(8,128)(2,1)}, u32[]{:S(2)}, u32[]{:S(2)}) %collective-permute-start.14) | collective-permute-done | bytes 1769504 | tf_op jit(solution)/shard_map/ppermute | solution.py:1003
  162.9 49.5 %collective-permute-done.15.partner = bf16[512,512]{1,0:T(8,128)(2,1)S(1)} collective-permute-done((bf16[512,512]{1,0:T(8,128)(2,1)S(1)}, bf16[512,512]{1,0:T(8,128)(2,1)S(1)}, u32[]{:S(2)}, u32[]{:S(2)}) %collective-permute-start.15) | collective-permute-done | bytes 524320 | tf_op jit(solution)/shard_map/ppermute | solution.py:1224
  213.2 11.0 %tree_attention.1.heads.rest_1_ = bf16[512,1536]{1,0:T(8,128)(2,1)} custom-call(s32[16]{0:T(128)} %concatenate.39.info, bf16[512,1536]{1,0:T(8,128)(2,1)} %query_projection.1.queries, bf16[512,512]{1,0:T(8,128)(2,1)} %get-tuple-element.116.own, bf16[512,512]{1,0:T(8,128)(2,1)} %copy-done.31), custom_call_target="tpu_custom_call" | custom-call | flops 1 | bytes 1 | tf_op jit(solution)/shard_map/tree_attention/pallas_call | solution.py:274
  224.4 11.3 %out_projection.1 = (f32[512,1536]{1,0:T(8,128)}, bf16[512,1536]{1,0:T(8,128)(2,1)}) custom-call(s32[16]{0:T(128)} %concatenate.39.info, bf16[512,1536]{1,0:T(8,128)(2,1)} %tree_attention.1.heads.rest_1_, bf16[512,1536]{1,0:T(8,128)(2,1)} %tokens.5, f32[1,1536]{1,0:T(1,128)} %reshape.454.gain, bf16[4,208,896]{2,1,0:T(8,128)(2,1)} %copy-done.1, ...), custom_call_target="tpu_custom_call" | custom-call | flops 1 | bytes 1 | tf_op jit(solution)/shard_map/out_projection/pallas_call | solution.py:386
  237.0 6.0 collective-permute-start.21
  248.0 6.2 route_tables.1
  260.2 5.1 dispatch.8
  265.3 5.1 dispatch.9
  270.5 13.1 %pick_rows.1 = (bf16[8,160,1536]{2,1,0:T(8,128)(2,1)}, bf16[8,160,1536]{2,1,0:T(8,128)(2,1)}) custom-call(s32[8]{0:T(128)} %iota_xor_fusion.order.near, bf16[8,320,512]{2,1,0:T(8,128)(2,1)} %get-tuple-element.118.chosen, bf16[8,512,1536]{2,1,0:T(8,128)(2,1)} %bitcast.165), custom_call_target="tpu_custom_call" | custom-call | flops 1 | bytes 1 | tf_op jit(solution)/shard_map/pick_rows/pallas_call | solution.py:462
  295.5 5.2 dispatch.10
  300.7 5.2 dispatch.11
  305.8 5.1 dispatch.12
  312.2 5.2 dispatch.13
  319.8 5.1 dispatch.14
  326.2 5.2 dispatch.15
  337.6 30.2 %expert.2 = (bf16[1280,1536]{1,0:T(8,128)(2,1)}, bf16[1280,1536]{1,0:T(8,128)(2,1)}, bf16[1280,1536]{1,0:T(8,128)(2,1)}, bf16[4,576,1280]{2,1,0:T(8,128)(2,1)}, f32[1280,1]{1,0:T(8,128)}) custom-call(s32[16]{0:T(128)} %concatenate.39.info, bf16[1280,1536]{1,0:T(8,128)(2,1)} %bitcast.141, bf16[1280,1536]{1,0:T(8,128)(2,1)} %bitcast.169, f32[1280,1]{1,0:T(8,128)} %bitcast.147, ...), custom_call_target="tpu_custom_call" | custom-call | flops 1 | bytes 1 | tf_op jit(solution)/shard_map/expert/pallas_call | solution.py:657
  367.8 9.8 %expert_gradients.4 = (bf16[576,1536]{1,0:T(8,128)(2,1)}, bf16[576,1536]{1,0:T(8,128)(2,1)}) custom-call(bf16[1280,1536]{1,0:T(8,128)(2,1)} %bitcast.142, bf16[1280,1536]{1,0:T(8,128)(2,1)} %get-tuple-element.167.grads, bf16[4,576,1280]{2,1,0:T(8,128)(2,1)} %get-tuple-element.168.rest_0_.rest_1_, bf16[4,576,1280]{2,1,0:T(8,128)(2,1)} %get-tuple-element.168.rest_0_.rest_1_), custom_call_target="tpu_custom_call" | custom-call | flops 1 | bytes 1 | tf_op jit(solution)/shard_map/expert_gradients/pallas_call | solution.py:685
  378.1 9.8 %expert_gradients.5 = (bf16[576,1536]{1,0:T(8,128)(2,1)}, bf16[576,1536]{1,0:T(8,128)(2,1)}) custom-call(bf16[1280,1536]{1,0:T(8,128)(2,1)} %bitcast.143, bf16[1280,1536]{1,0:T(8,128)(2,1)} %get-tuple-element.167.grads, bf16[4,576,1280]{2,1,0:T(8,128)(2,1)} %get-tuple-element.168.rest_0_.rest_1_, bf16[4,576,1280]{2,1,0:T(8,128)(2,1)} %get-tuple-element.168.rest_0_.rest_1_), custom_call_target="tpu_custom_call" | custom-call | flops 1 | bytes 1 | tf_op jit(solution)/shard_map/expert_gradients/pallas_call | solution.py:685
  387.9 30.2 %expert.3 = (bf16[1280,1536]{1,0:T(8,128)(2,1)}, bf16[1280,1536]{1,0:T(8,128)(2,1)}, bf16[1280,1536]{1,0:T(8,128)(2,1)}, bf16[4,576,1280]{2,1,0:T(8,128)(2,1)}, f32[1280,1]{1,0:T(8,128)}) custom-call(s32[16]{0:T(128)} %concatenate.39.info, bf16[1280,1536]{1,0:T(8,128)(2,1)} %bitcast.144, bf16[1280,1536]{1,0:T(8,128)(2,1)} %bitcast.168, f32[1280,1]{1,0:T(8,128)} %bitcast.148, ...), custom_call_target="tpu_custom_call" | custom-call | flops 1 | bytes 1 | tf_op jit(solution)/shard_map/expert/pallas_call | solution.py:657
  418.6 8.1 combine.7
  426.7 7.5 combine.4
  434.2 7.9 combine.6
  447.0 6.9 collective-permute-start.37
  465.0 26.6 %collective-permute-done.37 = bf16[576,1536]{1,0:T(8,128)(2,1)} collective-permute-done((bf16[576,1536]{1,0:T(8,128)(2,1)S(1)}, bf16[576,1536]{1,0:T(8,128)(2,1)}, u32[]{:S(2)}, u32[]{:S(2)}) %collective-permute-start.37) | collective-permute-done | bytes 1769504 | tf_op jit(solution)/shard_map/ppermute | solution.py:1031
  492.8 5.6 spread.1
  504.0 7.5 combine.5
  511.4 15.2 %all-to-all-done = f32[8,2,512]{2,1,0:T(2,128)S(1)} async-done(((f32[8,2,512]{2,1,0:T(2,128)}), f32[8,2,512]{2,1,0:T(2,128)S(1)}, u32[]{:S(2)}, u32[]{:S(2)}) %all-to-all-start) | async-done | bytes 32800 | tf_op jit(solution)/shard_map/all_to_all | solution.py:1314
  527.3 9.9 %expert_gradients.7 = (bf16[576,1536]{1,0:T(8,128)(2,1)}, bf16[576,1536]{1,0:T(8,128)(2,1)}) custom-call(bf16[1280,1536]{1,0:T(8,128)(2,1)} %bitcast.145, bf16[1280,1536]{1,0:T(8,128)(2,1)} %get-tuple-element.183.grads, bf16[4,576,1280]{2,1,0:T(8,128)(2,1)} %get-tuple-element.185.rest_0_.rest_1_, bf16[4,576,1280]{2,1,0:T(8,128)(2,1)} %get-tuple-element.185.rest_0_.rest_1_), custom_call_target="tpu_custom_call" | custom-call | flops 1 | bytes 1 | tf_op jit(solution)/shard_map/expert_gradients/pallas_call | solution.py:685
  537.2 9.9 %expert_gradients.6 = (bf16[576,1536]{1,0:T(8,128)(2,1)}, bf16[576,1536]{1,0:T(8,128)(2,1)}) custom-call(bf16[1280,1536]{1,0:T(8,128)(2,1)} %bitcast.146, bf16[1280,1536]{1,0:T(8,128)(2,1)} %get-tuple-element.183.grads, bf16[4,576,1280]{2,1,0:T(8,128)(2,1)} %get-tuple-element.185.rest_0_.rest_1_, bf16[4,576,1280]{2,1,0:T(8,128)(2,1)} %get-tuple-element.185.rest_0_.rest_1_), custom_call_target="tpu_custom_call" | custom-call | flops 1 | bytes 1 | tf_op jit(solution)/shard_map/expert_gradients/pallas_call | solution.py:685
  562.5 12.4 %collective-permute-done.40.rest_2_ = bf16[256,1536]{1,0:T(8,128)(2,1)S(1)} collective-permute-done((bf16[256,1536]{1,0:T(8,128)(2,1)S(1)}, bf16[256,1536]{1,0:T(8,128)(2,1)S(1)}, u32[]{:S(2)}, u32[]{:S(2)}) %collective-permute-start.40) | collective-permute-done | bytes 786464 | tf_op jit(solution)/shard_map/ppermute | solution.py:1051
  576.7 13.4 %experts_norm_back.1 = (f32[512,1536]{1,0:T(8,128)}, bf16[512,1536]{1,0:T(8,128)(2,1)}, bf16[512,1536]{1,0:T(8,128)(2,1)}, f32[1,1536]{1,0:T(1,128)}, f32[16,1536]{1,0:T(8,128)}) custom-call(s32[16]{0:T(128)} %concatenate.39.info, f32[512,1536]{1,0:T(8,128)} %get-tuple-element.117.residual, bf16[512,1536]{1,0:T(8,128)(2,1)} %get-tuple-element.119.rows.normed, ...), custom_call_target="tpu_custom_call" | custom-call | flops 1 | bytes 1 | tf_op jit(solution)/shard_map/experts_norm_back/pallas_call | solution.py:787
  590.1 15.4 %tree_attention_back.1 = (bf16[512,1536]{1,0:T(8,128)(2,1)}, f32[512,512]{1,0:T(8,128)}, f32[512,512]{1,0:T(8,128)}) custom-call(s32[16]{0:T(128)} %concatenate.39.info, bf16[512,1536]{1,0:T(8,128)(2,1)} %query_projection.1.queries, bf16[512,512]{1,0:T(8,128)(2,1)} %get-tuple-element.116.own, bf16[512,512]{1,0:T(8,128)(2,1)} %copy-done.31, ...), custom_call_target="tpu_custom_call" | custom-call | flops 1 | bytes 1 | tf_op jit(solution)/shard_map/tree_attention_back/pallas_call | solution.py:335
  610.9 8.2 collective-permute-done.43.arrived
  623.2 15.9 %weight_gradients.1 = (bf16[4,4,208,896]{3,2,1,0:T(8,128)(2,1)}, bf16[4,4,208,896]{3,2,1,0:T(8,128)(2,1)}) custom-call(s32[16]{0:T(128)} %concatenate.39.info, bf16[512,1536]{1,0:T(8,128)(2,1)} %get-tuple-element.114.normed.rest_0_, bf16[512,1536]{1,0:T(8,128)(2,1)} %tree_attention.1.heads.rest_1_, bf16[512,1536]{1,0:T(8,128)(2,1)} %get-tuple-element.191.rest_2_.grad_query, ...), custom_call_target="tpu_custom_call" | custom-call | flops 1 | bytes 1 | tf_op jit(solution)/shard_map/weight_gradients/pallas_call | solution.py:939
  653.1 27.2 %collective-permute-done.33 = bf16[2,256,1536]{2,1,0:T(8,128)(2,1)} collective-permute-done((bf16[2,256,1536]{2,1,0:T(8,128)(2,1)}, bf16[2,256,1536]{2,1,0:T(8,128)(2,1)}, u32[]{:S(2)}, u32[]{:S(2)}) %collective-permute-start.33) | collective-permute-done | bytes 1572896 | tf_op jit(solution)/shard_map/ppermute | solution.py:1051
  690.3 7.1 collective-permute-start.54
  698.7 6.0 collective-permute-start.56
  717.4 13.3 %token_gradient.1 = (bf16[512,1536]{1,0:T(8,128)(2,1)}, f32[1,1536]{1,0:T(1,128)}) custom-call(s32[16]{0:T(128)} %concatenate.39.info, bf16[512,1536]{1,0:T(8,128)(2,1)} %get-tuple-element.191.rest_2_.grad_query, bf16[512,512]{1,0:T(8,128)(2,1)} %join_key_value_gradients.1.rest_3_.grad_pair, bf16[512,1536]{1,0:T(8,128)(2,1)} %tokens.5, ...), custom_call_target="tpu_custom_call" | custom-call | flops 1 | bytes 1 | tf_op jit(solution)/shard_map/token_gradient/pallas_call | solution.py:878
  730.8 11.9 %collective-permute-done.48 = bf16[2,2,208,896]{3,2,1,0:T(8,128)(2,1)} collective-permute-done((bf16[2,2,208,896]{3,2,1,0:T(8,128)(2,1)}, bf16[2,2,208,896]{3,2,1,0:T(8,128)(2,1)}, u32[]{:S(2)}, u32[]{:S(2)}) %collective-permute-start.48) | collective-permute-done | bytes 1490976 | tf_op jit(solution)/shard_map/ppermute | solution.py:1051
  747.9 28.7 %collective-permute-done.55 = bf16[576,1536]{1,0:T(8,128)(2,1)} collective-permute-done((bf16[576,1536]{1,0:T(8,128)(2,1)}, bf16[576,1536]{1,0:T(8,128)(2,1)}, u32[]{:S(2)}, u32[]{:S(2)}) %collective-permute-start.55) | collective-permute-done | bytes 1769504 | tf_op jit(solution)/shard_map/ppermute | solution.py:1032
  794.7 14.3 %collective-permute-done.50 = bf16[208,896]{1,0:T(8,128)(2,1)S(1)} collective-permute-done((bf16[208,896]{1,0:T(8,128)(2,1)S(1)}, bf16[208,896]{1,0:T(8,128)(2,1)S(1)}, u32[]{:S(2)}, u32[]{:S(2)}) %collective-permute-start.50) | collective-permute-done | bytes 372768 | tf_op jit(solution)/shard_map/ppermute | solution.py:1019
  (330 shorter events, 218.4 us)
Async XLA Ops:
  7.2 263.3 %all-gather.3.cloned.1.call-start = ((), (), s32[]{:S(2)}) async-start(), calls=%async_computation.1 | async-start | bytes 14155776 | tf_op jit(solution)/shard_map/all_gather | solution.py:1220
  42.0 44.3 %collective-permute-start.7 = (bf16[576,1536]{1,0:T(8,128)(2,1)S(1)}, bf16[576,1536]{1,0:T(8,128)(2,1)S(1)}, u32[]{:S(2)}, u32[]{:S(2)}) collective-permute-start(bf16[576,1536]{1,0:T(8,128)(2,1)S(1)} %pad_maximum_fusion.2.rest_0_), channel_id=1, source_target_pairs={{1,0},{2,1},{3,2},{5,4},{6,5},{7,6},{9,8},{10,9},{11,10},{13,12},{... | collective-permute-start | bytes 5308424 | tf_op jit(solution)/shard_map/ppermute | solution.py:992
  43.3 43.0 %collective-permute-start.8 = (bf16[576,1536]{1,0:T(8,128)(2,1)S(1)}, bf16[576,1536]{1,0:T(8,128)(2,1)}, u32[]{:S(2)}, u32[]{:S(2)}) collective-permute-start(bf16[576,1536]{1,0:T(8,128)(2,1)S(1)} %pad_maximum_fusion.2.rest_0_), channel_id=1, source_target_pairs={{0,1},{1,2},{2,3},{4,5},{5,6},{6,7},{8,9},{9,10},{10,11},{12,13},{... | collective-permute-start | bytes 5308424 | tf_op jit(solution)/shard_map/ppermute | solution.py:992
  53.4 32.8 %collective-permute-start.4 = (bf16[4,208,896]{2,1,0:T(8,128)(2,1)S(1)}, bf16[4,208,896]{2,1,0:T(8,128)(2,1)S(1)}, u32[]{:S(2)}, u32[]{:S(2)}) collective-permute-start(bf16[4,208,896]{2,1,0:T(8,128)(2,1)S(1)} %pad_maximum_fusion.8.rest_0_.rest_6_.rest_9_), channel_id=1, source_target_pairs={{0,8},{4,12},{8,0},{12,4},{16,24},{20,28},{24,16},{28,20},{1,9},{5... | collective-permute-start | bytes 4472840 | tf_op jit(solution)/shard_map/ppermute | solution.py:1051
  55.0 31.3 %collective-permute-start.5 = (bf16[4,208,896]{2,1,0:T(8,128)(2,1)S(1)}, bf16[4,208,896]{2,1,0:T(8,128)(2,1)S(1)}, u32[]{:S(2)}, u32[]{:S(2)}) collective-permute-start(bf16[4,208,896]{2,1,0:T(8,128)(2,1)S(1)} %pad_maximum_fusion.8.rest_0_.rest_6_.rest_9_), channel_id=1, source_target_pairs={{0,16},{4,20},{8,24},{12,28},{16,0},{20,4},{24,8},{28,12},{1,17},{... | collective-permute-start | bytes 4472840 | tf_op jit(solution)/shard_map/ppermute | solution.py:1051
  56.5 29.8 %collective-permute-start.6 = (bf16[4,208,896]{2,1,0:T(8,128)(2,1)S(1)}, bf16[4,208,896]{2,1,0:T(8,128)(2,1)}, u32[]{:S(2)}, u32[]{:S(2)}) collective-permute-start(bf16[4,208,896]{2,1,0:T(8,128)(2,1)S(1)} %pad_maximum_fusion.8.rest_0_.rest_6_.rest_9_), channel_id=1, source_target_pairs={{0,4},{4,0},{8,12},{12,8},{16,20},{20,16},{24,28},{28,24},{1,5},{5... | collective-permute-start | bytes 4472840 | tf_op jit(solution)/shard_map/ppermute | solution.py:1051
  87.8 23.8 %collective-permute-start.11 = (bf16[8,208,896]{2,1,0:T(8,128)(2,1)S(1)}, bf16[8,208,896]{2,1,0:T(8,128)(2,1)S(1)}, u32[]{:S(2)}, u32[]{:S(2)}) collective-permute-start(bf16[8,208,896]{2,1,0:T(8,128)(2,1)S(1)} %pad_maximum_fusion), channel_id=1, source_target_pairs={{0,4},{4,0},{8,12},{12,8},{16,20},{20,16},{24,28},{28,24},{1,5},{5... | collective-permute-start | bytes 8945672 | tf_op jit(solution)/shard_map/ppermute | solution.py:1051
  88.0 19.0 %collective-permute-start.9 = (bf16[2,208,896]{2,1,0:T(8,128)(2,1)S(1)}, bf16[2,208,896]{2,1,0:T(8,128)(2,1)S(1)}, u32[]{:S(2)}, u32[]{:S(2)}) collective-permute-start(bf16[2,208,896]{2,1,0:T(8,128)(2,1)S(1)} %slice.450), channel_id=1, source_target_pairs={{0,16},{4,20},{8,24},{12,28},{16,0},{20,4},{24,8},{28,12},{1,17},{... | collective-permute-start | bytes 2236424 | tf_op jit(solution)/shard_map/ppermute | solution.py:1051
  89.7 18.7 %collective-permute-start.10 = (bf16[2,208,896]{2,1,0:T(8,128)(2,1)S(1)}, bf16[2,208,896]{2,1,0:T(8,128)(2,1)S(1)}, u32[]{:S(2)}, u32[]{:S(2)}) collective-permute-start(bf16[2,208,896]{2,1,0:T(8,128)(2,1)S(1)} %slice.451), channel_id=1, source_target_pairs={{0,8},{4,12},{8,0},{12,4},{16,24},{20,28},{24,16},{28,20},{1,9},{5... | collective-permute-start | bytes 2236424 | tf_op jit(solution)/shard_map/ppermute | solution.py:1051
  115.6 41.7 %collective-permute-start.14 = (bf16[576,1536]{1,0:T(8,128)(2,1)}, bf16[576,1536]{1,0:T(8,128)(2,1)}, u32[]{:S(2)}, u32[]{:S(2)}) collective-permute-start(bf16[576,1536]{1,0:T(8,128)(2,1)} %select_select_fusion.1), channel_id=1, source_target_pairs={{3,1},{1,0},{0,2},{2,3},{7,5},{5,4},{4,6},{6,7},{11,9},{9,8},{8,10... | collective-permute-start | bytes 5308424 | tf_op jit(solution)/shard_map/ppermute | solution.py:1003
  157.4 78.3 %collective-permute-start.19 = (bf16[576,1536]{1,0:T(8,128)(2,1)S(1)}, bf16[576,1536]{1,0:T(8,128)(2,1)}, u32[]{:S(2)}, u32[]{:S(2)}) collective-permute-start(bf16[576,1536]{1,0:T(8,128)(2,1)S(1)} %copy-done.10), channel_id=1, source_target_pairs={{0,3},{3,0},{4,7},{7,4},{8,11},{11,8},{12,15},{15,12},{16,19},{19,... | collective-permute-start | bytes 5308424 | tf_op jit(solution)/shard_map/ppermute | solution.py:996
  160.9 51.5 %collective-permute-start.15 = (bf16[512,512]{1,0:T(8,128)(2,1)S(1)}, bf16[512,512]{1,0:T(8,128)(2,1)S(1)}, u32[]{:S(2)}, u32[]{:S(2)}) collective-permute-start(bf16[512,512]{1,0:T(8,128)(2,1)S(1)} %copy-done.30), channel_id=1, source_target_pairs={{1,0},{3,2},{5,4},{7,6},{9,8},{11,10},{13,12},{15,14},{17,16},{19,... | collective-permute-start | bytes 1572872 | tf_op jit(solution)/shard_map/ppermute | solution.py:1224
  235.7 47.9 %collective-permute-start.20 = (bf16[576,1536]{1,0:T(8,128)(2,1)S(1)}, bf16[576,1536]{1,0:T(8,128)(2,1)S(1)}, u32[]{:S(2)}, u32[]{:S(2)}) collective-permute-start(bf16[576,1536]{1,0:T(8,128)(2,1)S(1)} %pad_maximum_fusion.3.rest_0_), channel_id=1, source_target_pairs={{1,0},{2,1},{3,2},{5,4},{6,5},{7,6},{9,8},{10,9},{11,10},{13,12},{... | collective-permute-start | bytes 5308424 | tf_op jit(solution)/shard_map/ppermute | solution.py:992
  237.0 46.6 %collective-permute-start.21 = (bf16[576,1536]{1,0:T(8,128)(2,1)S(1)}, bf16[576,1536]{1,0:T(8,128)(2,1)}, u32[]{:S(2)}, u32[]{:S(2)}) collective-permute-start(bf16[576,1536]{1,0:T(8,128)(2,1)S(1)} %pad_maximum_fusion.3.rest_0_), channel_id=1, source_target_pairs={{0,1},{1,2},{2,3},{4,5},{5,6},{6,7},{8,9},{9,10},{10,11},{12,13},{... | collective-permute-start | bytes 5308424 | tf_op jit(solution)/shard_map/ppermute | solution.py:992
  243.0 22.4 %collective-permute-start.18 = (bf16[512,1536]{1,0:T(8,128)(2,1)}, bf16[512,1536]{1,0:T(8,128)(2,1)}, u32[]{:S(2)}, u32[]{:S(2)}) collective-permute-start(bf16[512,1536]{1,0:T(8,128)(2,1)} %get-tuple-element.119.rows.normed), channel_id=1, source_target_pairs={{0,4},{4,0},{8,12},{12,8},{16,20},{20,16},{24,28},{28,24},{1,5},{5... | collective-permute-start | bytes 4718600 | tf_op jit(solution)/shard_map/ppermute | solution.py:1051
  243.0 40.5 %collective-permute-start.16 = (bf16[512,1536]{1,0:T(8,128)(2,1)}, bf16[512,1536]{1,0:T(8,128)(2,1)}, u32[]{:S(2)}, u32[]{:S(2)}) collective-permute-start(bf16[512,1536]{1,0:T(8,128)(2,1)} %get-tuple-element.119.rows.normed), channel_id=1, source_target_pairs={{0,8},{4,12},{8,0},{12,4},{16,24},{20,28},{24,16},{28,20},{1,9},{5... | collective-permute-start | bytes 4718600 | tf_op jit(solution)/shard_map/ppermute | solution.py:1051
  244.6 39.0 %collective-permute-start.17 = (bf16[512,1536]{1,0:T(8,128)(2,1)}, bf16[512,1536]{1,0:T(8,128)(2,1)}, u32[]{:S(2)}, u32[]{:S(2)}) collective-permute-start(bf16[512,1536]{1,0:T(8,128)(2,1)} %get-tuple-element.119.rows.normed), channel_id=1, source_target_pairs={{0,16},{4,20},{8,24},{12,28},{16,0},{20,4},{24,8},{28,12},{1,17},{... | collective-permute-start | bytes 4718600 | tf_op jit(solution)/shard_map/ppermute | solution.py:1051
  287.4 23.5 %collective-permute-start.25 = (bf16[512,1536]{1,0:T(8,128)(2,1)}, bf16[512,1536]{1,0:T(8,128)(2,1)S(1)}, u32[]{:S(2)}, u32[]{:S(2)}) collective-permute-start(bf16[512,1536]{1,0:T(8,128)(2,1)} %collective-permute-done.17.rows), channel_id=1, source_target_pairs={{0,4},{4,0},{8,12},{12,8},{16,20},{20,16},{24,28},{28,24},{1,5},{5... | collective-permute-start | bytes 4718600 | tf_op jit(solution)/shard_map/ppermute | solution.py:1051
  291.7 25.6 %collective-permute-start.22 = (bf16[256,1536]{1,0:T(8,128)(2,1)}, bf16[256,1536]{1,0:T(8,128)(2,1)S(1)}, u32[]{:S(2)}, u32[]{:S(2)}) collective-permute-start(bf16[256,1536]{1,0:T(8,128)(2,1)} %slice.459), channel_id=1, source_target_pairs={{0,16},{4,20},{8,24},{12,28},{16,0},{20,4},{24,8},{28,12},{1,17},{... | collective-permute-start | bytes 2359304 | tf_op jit(solution)/shard_map/ppermute | solution.py:1051
  292.6 24.8 %collective-permute-start.23 = (bf16[256,1536]{1,0:T(8,128)(2,1)}, bf16[256,1536]{1,0:T(8,128)(2,1)}, u32[]{:S(2)}, u32[]{:S(2)}) collective-permute-start(bf16[256,1536]{1,0:T(8,128)(2,1)} %slice.460), channel_id=1, source_target_pairs={{0,8},{4,12},{8,0},{12,4},{16,24},{20,28},{24,16},{28,20},{1,9},{5... | collective-permute-start | bytes 2359304 | tf_op jit(solution)/shard_map/ppermute | solution.py:1051
  294.5 40.5 %collective-permute-start.27 = (bf16[576,1536]{1,0:T(8,128)(2,1)}, bf16[576,1536]{1,0:T(8,128)(2,1)S(1)}, u32[]{:S(2)}, u32[]{:S(2)}) collective-permute-start(bf16[576,1536]{1,0:T(8,128)(2,1)} %select_select_fusion), channel_id=1, source_target_pairs={{3,1},{1,0},{0,2},{2,3},{7,5},{5,4},{4,6},{6,7},{11,9},{9,8},{8,10... | collective-permute-start | bytes 5308424 | tf_op jit(solution)/shard_map/ppermute | solution.py:1003
  335.1 52.8 %collective-permute-start.28 = (bf16[576,1536]{1,0:T(8,128)(2,1)S(1)}, bf16[576,1536]{1,0:T(8,128)(2,1)}, u32[]{:S(2)}, u32[]{:S(2)}) collective-permute-start(bf16[576,1536]{1,0:T(8,128)(2,1)S(1)} %pad_maximum_fusion.3.rest_0_), channel_id=1, source_target_pairs={{0,3},{3,0},{4,7},{7,4},{8,11},{11,8},{12,15},{15,12},{16,19},{19,... | collective-permute-start | bytes 5308424 | tf_op jit(solution)/shard_map/ppermute | solution.py:996
  377.7 41.0 %collective-permute-start.29 = (bf16[576,1536]{1,0:T(8,128)(2,1)}, bf16[576,1536]{1,0:T(8,128)(2,1)S(1)}, u32[]{:S(2)}, u32[]{:S(2)}) collective-permute-start(bf16[576,1536]{1,0:T(8,128)(2,1)} %get-tuple-element.169), channel_id=1, source_target_pairs={{1,3},{0,1},{2,0},{3,2},{5,7},{4,5},{6,4},{7,6},{9,11},{8,9},{10,8... | collective-permute-start | bytes 5308424 | tf_op jit(solution)/shard_map/ppermute | solution.py:1019
  426.7 31.5 %collective-permute-start.35 = (bf16[4,512,1536]{2,1,0:T(8,128)(2,1)}, bf16[4,512,1536]{2,1,0:T(8,128)(2,1)}, u32[]{:S(2)}, u32[]{:S(2)}) collective-permute-start(bf16[4,512,1536]{2,1,0:T(8,128)(2,1)} %combine.7), channel_id=1, source_target_pairs={{0,4},{4,0},{8,12},{12,8},{16,20},{20,16},{24,28},{28,24},{1,5},{5... | collective-permute-start | bytes 18874376 | tf_op jit(solution)/shard_map/ppermute | solution.py:1051
  442.1 108.9 %collective-permute-start.30 = (bf16[4,512,1536]{2,1,0:T(8,128)(2,1)}, bf16[4,512,1536]{2,1,0:T(8,128)(2,1)}, u32[]{:S(2)}, u32[]{:S(2)}) collective-permute-start(bf16[4,512,1536]{2,1,0:T(8,128)(2,1)} %combine.6), channel_id=1, source_target_pairs={{0,4},{4,0},{8,12},{12,8},{16,20},{20,16},{24,28},{28,24},{1,5},{5... | collective-permute-start | bytes 18874376 | tf_op jit(solution)/shard_map/ppermute | solution.py:1051
  447.0 44.6 %collective-permute-start.37 = (bf16[576,1536]{1,0:T(8,128)(2,1)S(1)}, bf16[576,1536]{1,0:T(8,128)(2,1)}, u32[]{:S(2)}, u32[]{:S(2)}) collective-permute-start(bf16[576,1536]{1,0:T(8,128)(2,1)S(1)} %get-tuple-element.273), channel_id=1, source_target_pairs={{0,1},{1,2},{2,3},{4,5},{5,6},{6,7},{8,9},{9,10},{10,11},{12,13},{... | collective-permute-start | bytes 5308424 | tf_op jit(solution)/shard_map/ppermute | solution.py:1031
  453.8 93.3 %collective-permute-start.38 = (bf16[576,1536]{1,0:T(8,128)(2,1)}, bf16[576,1536]{1,0:T(8,128)(2,1)S(1)}, u32[]{:S(2)}, u32[]{:S(2)}) collective-permute-start(bf16[576,1536]{1,0:T(8,128)(2,1)} %get-tuple-element.272), channel_id=1, source_target_pairs={{1,0},{2,1},{3,2},{5,4},{6,5},{7,6},{9,8},{10,9},{11,10},{13,12},{... | collective-permute-start | bytes 5308424 | tf_op jit(solution)/shard_map/ppermute | solution.py:1032
  455.1 92.0 %collective-permute-start.36 = (bf16[576,1536]{1,0:T(8,128)(2,1)}, bf16[576,1536]{1,0:T(8,128)(2,1)}, u32[]{:S(2)}, u32[]{:S(2)}) collective-permute-start(bf16[576,1536]{1,0:T(8,128)(2,1)} %get-tuple-element.188), channel_id=1, source_target_pairs={{0,3},{3,0},{4,7},{7,4},{8,11},{11,8},{12,15},{15,12},{16,19},{19,... | collective-permute-start | bytes 5308424 | tf_op jit(solution)/shard_map/ppermute | solution.py:1020
  462.2 88.8 %collective-permute-start.39 = (bf16[2,256,1536]{2,1,0:T(8,128)(2,1)}, bf16[2,256,1536]{2,1,0:T(8,128)(2,1)}, u32[]{:S(2)}, u32[]{:S(2)}) collective-permute-start(bf16[2,256,1536]{2,1,0:T(8,128)(2,1)} %pad_maximum_fusion.6), channel_id=1, source_target_pairs={{0,8},{4,12},{8,0},{12,4},{16,24},{20,28},{24,16},{28,20},{1,9},{5... | collective-permute-start | bytes 4718600 | tf_op jit(solution)/shard_map/ppermute | solution.py:1051
  491.6 59.4 %collective-permute-start.41 = (bf16[2,256,1536]{2,1,0:T(8,128)(2,1)}, bf16[2,256,1536]{2,1,0:T(8,128)(2,1)}, u32[]{:S(2)}, u32[]{:S(2)}) collective-permute-start(bf16[2,256,1536]{2,1,0:T(8,128)(2,1)} %pad_maximum_fusion.7), channel_id=1, source_target_pairs={{0,16},{4,20},{8,24},{12,28},{16,0},{20,4},{24,8},{28,12},{1,17},{... | collective-permute-start | bytes 4718600 | tf_op jit(solution)/shard_map/ppermute | solution.py:1051
  500.5 26.2 %all-to-all-start = ((f32[8,2,512]{2,1,0:T(2,128)}), f32[8,2,512]{2,1,0:T(2,128)S(1)}, u32[]{:S(2)}, u32[]{:S(2)}) async-start(f32[8,2,512]{2,1,0:T(2,128)} %broadcast_select_fusion), calls=%async_computation | async-start | bytes 65536 | tf_op jit(solution)/shard_map/all_to_all | solution.py:1314
  548.4 61.3 %collective-permute-start.44 = (bf16[576,1536]{1,0:T(8,128)(2,1)}, bf16[576,1536]{1,0:T(8,128)(2,1)S(1)}, u32[]{:S(2)}, u32[]{:S(2)}) collective-permute-start(bf16[576,1536]{1,0:T(8,128)(2,1)} %get-tuple-element.197), channel_id=1, source_target_pairs={{1,3},{0,1},{2,0},{3,2},{5,7},{4,5},{6,4},{7,6},{9,11},{8,9},{10,8... | collective-permute-start | bytes 5308424 | tf_op jit(solution)/shard_map/ppermute | solution.py:1019
  555.6 19.3 %collective-permute-start.40 = (bf16[256,1536]{1,0:T(8,128)(2,1)S(1)}, bf16[256,1536]{1,0:T(8,128)(2,1)S(1)}, u32[]{:S(2)}, u32[]{:S(2)}) collective-permute-start(bf16[256,1536]{1,0:T(8,128)(2,1)S(1)} %get-tuple-element.242), channel_id=1, source_target_pairs={{0,16},{4,20},{8,24},{12,28},{16,0},{20,4},{24,8},{28,12},{1,17},{... | collective-permute-start | bytes 2359304 | tf_op jit(solution)/shard_map/ppermute | solution.py:1051
  556.8 19.0 %collective-permute-start.42 = (bf16[256,1536]{1,0:T(8,128)(2,1)S(1)}, bf16[256,1536]{1,0:T(8,128)(2,1)S(1)}, u32[]{:S(2)}, u32[]{:S(2)}) collective-permute-start(bf16[256,1536]{1,0:T(8,128)(2,1)S(1)} %get-tuple-element.240), channel_id=1, source_target_pairs={{0,8},{4,12},{8,0},{12,4},{16,24},{20,28},{24,16},{28,20},{1,9},{5... | collective-permute-start | bytes 2359304 | tf_op jit(solution)/shard_map/ppermute | solution.py:1051
  639.2 59.6 %collective-permute-start.45 = (bf16[4,4,208,896]{3,2,1,0:T(8,128)(2,1)}, bf16[4,4,208,896]{3,2,1,0:T(8,128)(2,1)}, u32[]{:S(2)}, u32[]{:S(2)}) collective-permute-start(bf16[4,4,208,896]{3,2,1,0:T(8,128)(2,1)} %get-tuple-element.205), channel_id=1, source_target_pairs={{0,4},{4,0},{8,12},{12,8},{16,20},{20,16},{24,28},{28,24},{1,5},{5... | collective-permute-start | bytes 17891336 | tf_op jit(solution)/shard_map/ppermute | solution.py:1051
  643.2 37.1 %collective-permute-start.33 = (bf16[2,256,1536]{2,1,0:T(8,128)(2,1)}, bf16[2,256,1536]{2,1,0:T(8,128)(2,1)}, u32[]{:S(2)}, u32[]{:S(2)}) collective-permute-start(bf16[2,256,1536]{2,1,0:T(8,128)(2,1)} %pad_maximum_fusion.5), channel_id=1, source_target_pairs={{0,16},{4,20},{8,24},{12,28},{16,0},{20,4},{24,8},{28,12},{1,17},{... | collective-permute-start | bytes 4718600 | tf_op jit(solution)/shard_map/ppermute | solution.py:1051
  645.3 36.8 %collective-permute-start.31 = (bf16[2,256,1536]{2,1,0:T(8,128)(2,1)}, bf16[2,256,1536]{2,1,0:T(8,128)(2,1)}, u32[]{:S(2)}, u32[]{:S(2)}) collective-permute-start(bf16[2,256,1536]{2,1,0:T(8,128)(2,1)} %pad_maximum_fusion.4), channel_id=1, source_target_pairs={{0,8},{4,12},{8,0},{12,4},{16,24},{20,28},{24,16},{28,20},{1,9},{5... | collective-permute-start | bytes 4718600 | tf_op jit(solution)/shard_map/ppermute | solution.py:1051
  684.7 25.1 %collective-permute-start.32 = (bf16[256,1536]{1,0:T(8,128)(2,1)S(1)}, bf16[256,1536]{1,0:T(8,128)(2,1)S(1)}, u32[]{:S(2)}, u32[]{:S(2)}) collective-permute-start(bf16[256,1536]{1,0:T(8,128)(2,1)S(1)} %get-tuple-element.250), channel_id=1, source_target_pairs={{0,16},{4,20},{8,24},{12,28},{16,0},{20,4},{24,8},{28,12},{1,17},{... | collective-permute-start | bytes 2359304 | tf_op jit(solution)/shard_map/ppermute | solution.py:1051
  686.0 24.6 %collective-permute-start.34 = (bf16[256,1536]{1,0:T(8,128)(2,1)S(1)}, bf16[256,1536]{1,0:T(8,128)(2,1)S(1)}, u32[]{:S(2)}, u32[]{:S(2)}) collective-permute-start(bf16[256,1536]{1,0:T(8,128)(2,1)S(1)} %get-tuple-element.251), channel_id=1, source_target_pairs={{0,8},{4,12},{8,0},{12,4},{16,24},{20,28},{24,16},{28,20},{1,9},{5... | collective-permute-start | bytes 2359304 | tf_op jit(solution)/shard_map/ppermute | solution.py:1051
  690.3 57.6 %collective-permute-start.54 = (bf16[576,1536]{1,0:T(8,128)(2,1)}, bf16[576,1536]{1,0:T(8,128)(2,1)}, u32[]{:S(2)}, u32[]{:S(2)}) collective-permute-start(bf16[576,1536]{1,0:T(8,128)(2,1)} %get-tuple-element.270), channel_id=1, source_target_pairs={{0,1},{1,2},{2,3},{4,5},{5,6},{6,7},{8,9},{9,10},{10,11},{12,13},{... | collective-permute-start | bytes 5308424 | tf_op jit(solution)/shard_map/ppermute | solution.py:1031
  697.4 79.2 %collective-permute-start.55 = (bf16[576,1536]{1,0:T(8,128)(2,1)}, bf16[576,1536]{1,0:T(8,128)(2,1)}, u32[]{:S(2)}, u32[]{:S(2)}) collective-permute-start(bf16[576,1536]{1,0:T(8,128)(2,1)} %get-tuple-element.271), channel_id=1, source_target_pairs={{1,0},{2,1},{3,2},{5,4},{6,5},{7,6},{9,8},{10,9},{11,10},{13,12},{... | collective-permute-start | bytes 5308424 | tf_op jit(solution)/shard_map/ppermute | solution.py:1032
  698.7 77.9 %collective-permute-start.56 = (bf16[576,1536]{1,0:T(8,128)(2,1)}, bf16[576,1536]{1,0:T(8,128)(2,1)}, u32[]{:S(2)}, u32[]{:S(2)}) collective-permute-start(bf16[576,1536]{1,0:T(8,128)(2,1)} %get-tuple-element.207), channel_id=1, source_target_pairs={{0,3},{3,0},{4,7},{7,4},{8,11},{11,8},{12,15},{15,12},{16,19},{19,... | collective-permute-start | bytes 5308424 | tf_op jit(solution)/shard_map/ppermute | solution.py:1020
  709.8 32.8 %collective-permute-start.48 = (bf16[2,2,208,896]{3,2,1,0:T(8,128)(2,1)}, bf16[2,2,208,896]{3,2,1,0:T(8,128)(2,1)}, u32[]{:S(2)}, u32[]{:S(2)}) collective-permute-start(bf16[2,2,208,896]{3,2,1,0:T(8,128)(2,1)} %pad_maximum_fusion.10), channel_id=1, source_target_pairs={{0,16},{4,20},{8,24},{12,28},{16,0},{20,4},{24,8},{28,12},{1,17},{... | collective-permute-start | bytes 4472840 | tf_op jit(solution)/shard_map/ppermute | solution.py:1051
  710.6 32.6 %collective-permute-start.46 = (bf16[2,2,208,896]{3,2,1,0:T(8,128)(2,1)}, bf16[2,2,208,896]{3,2,1,0:T(8,128)(2,1)}, u32[]{:S(2)}, u32[]{:S(2)}) collective-permute-start(bf16[2,2,208,896]{3,2,1,0:T(8,128)(2,1)} %pad_maximum_fusion.9), channel_id=1, source_target_pairs={{0,8},{4,12},{8,0},{12,4},{16,24},{20,28},{24,16},{28,20},{1,9},{5... | collective-permute-start | bytes 4472840 | tf_op jit(solution)/shard_map/ppermute | solution.py:1051
  746.0 34.4 %collective-permute-start.47 = (bf16[2,208,896]{2,1,0:T(8,128)(2,1)S(1)}, bf16[2,208,896]{2,1,0:T(8,128)(2,1)S(1)}, u32[]{:S(2)}, u32[]{:S(2)}) collective-permute-start(bf16[2,208,896]{2,1,0:T(8,128)(2,1)S(1)} %get-tuple-element.258), channel_id=1, source_target_pairs={{0,16},{4,20},{8,24},{12,28},{16,0},{20,4},{24,8},{28,12},{1,17},{... | collective-permute-start | bytes 2236424 | tf_op jit(solution)/shard_map/ppermute | solution.py:1051
  747.2 33.1 %collective-permute-start.49 = (bf16[2,208,896]{2,1,0:T(8,128)(2,1)S(1)}, bf16[2,208,896]{2,1,0:T(8,128)(2,1)S(1)}, u32[]{:S(2)}, u32[]{:S(2)}) collective-permute-start(bf16[2,208,896]{2,1,0:T(8,128)(2,1)S(1)} %get-tuple-element.259), channel_id=1, source_target_pairs={{0,8},{4,12},{8,0},{12,4},{16,24},{20,28},{24,16},{28,20},{1,9},{5... | collective-permute-start | bytes 2236424 | tf_op jit(solution)/shard_map/ppermute | solution.py:1051
  789.8 19.1 %collective-permute-start.50 = (bf16[208,896]{1,0:T(8,128)(2,1)S(1)}, bf16[208,896]{1,0:T(8,128)(2,1)S(1)}, u32[]{:S(2)}, u32[]{:S(2)}) collective-permute-start(bf16[208,896]{1,0:T(8,128)(2,1)S(1)} %get-tuple-element.277), channel_id=1, source_target_pairs={{1,3},{0,1},{2,0},{3,2},{5,7},{4,5},{6,4},{7,6},{9,11},{8,9},{10,8... | collective-permute-start | bytes 1118216 | tf_op jit(solution)/shard_map/ppermute | solution.py:1019
  792.6 22.4 %collective-permute-start.53 = (bf16[208,896]{1,0:T(8,128)(2,1)S(1)}, bf16[208,896]{1,0:T(8,128)(2,1)S(1)}, u32[]{:S(2)}, u32[]{:S(2)}) collective-permute-start(bf16[208,896]{1,0:T(8,128)(2,1)S(1)} %get-tuple-element.276), channel_id=1, source_target_pairs={{0,3},{3,0},{4,7},{7,4},{8,11},{11,8},{12,15},{15,12},{16,19},{19,... | collective-permute-start | bytes 1118216 | tf_op jit(solution)/shard_map/ppermute | solution.py:1020
  (69 other events, 1109.3 us)
Sparse Core Ops, SparseCore 0:
  111.8 71.5 all-gather.2

commit v8 on v7

--- a/solution.py
+++ b/solution.py
@@ -1017,7 +1017,7 @@
 
 def reduce_first(second, fourth, chain=False):
     relay = lax.ppermute(second, "cols", [(1, 3), (0, 1), (2, 0), (3, 2)])
-    return relay, lax.ppermute(after(fourth, relay) if chain else fourth, "cols", FAR)
+    return relay, None if chain else lax.ppermute(fourth, "cols", FAR)
 
 
 def reduce_second(third, fourth, relay):
@@ -1055,20 +1055,31 @@
     return (one.astype(WIDE) + two.astype(WIDE)).astype(LOW)
 
 
-def reduce_chips(keep, got):
+def chip_sums(keep, got, chips, part):
+    return jnp.stack([add_low(keep[i][part], got[i][part]) for i in chips])
+
+
+def halves(keep):
     half = keep.shape[1] // 2
-
-    def sums(chips, part):
-        return jnp.stack([add_low(keep[i][part], got[i][part]) for i in chips])
-
-    one, two = slice(0, half), slice(half, None)
-    got_x = flip(sums((1, 3), one), 2)
-    got_y = flip(sums((2, 3), two), 4)
-    near_x = sums((0, 2), one)
-    near_y = sums((0, 1), two)
+    return slice(0, half), slice(half, None)
+
+
+def chips_first(keep, got):
+    one, two = halves(keep)
+    return chip_sums(keep, got, (1, 3), one), chip_sums(keep, got, (2, 3), two)
+
+
+def chips_second(keep, got, got_x, got_y):
+    one, two = halves(keep)
+    near_x = chip_sums(keep, got, (0, 2), one)
+    near_y = chip_sums(keep, got, (0, 1), two)
     got_xy = flip(add_low(near_x[1], got_x[1]), 4)
     got_yx = flip(add_low(near_y[1], got_y[1]), 2)
     return (near_x[0], got_x[0], got_xy, near_y[0], got_y[0], got_yx)
+
+
+def send_chips(sums):
+    return flip(sums[0], 2), flip(sums[1], 4)
 
 
 def sum_parts(parts):
@@ -1216,16 +1227,15 @@
     chosen, place_rows = tables(
         near_rows, info, routes_all, capacity, local_experts, expert_total
     )
-    grad_in = after(cotangent, *pieces) if fast else cotangent
+    tokens_in = after(tokens, seconds[0]) if fast else tokens
+    normed, own_pair = key_value(info, tokens_in, attention_scale, cosine, sine, pair_refs)
+    grad_in = after(cotangent, normed) if fast else cotangent
     grad_all = lax.all_gather(grad_in, "rows", axis=0)
-
-    normed, own_pair = key_value(info, tokens, attention_scale, cosine, sine, pair_refs)
     pairs = [(i + 1, i) for i in range(0, col_count, 2)]
     partner = lax.ppermute(own_pair, "cols", pairs)
     queries = query(info, normed, cosine, sine, query_refs)
     if fast:
-        queries = after(queries, seconds[0])
-        fars.append(send_far(after(shard_blocks[0], seconds[0], queries)))
+        fars.append(send_far(after(shard_blocks[0], seconds[0], partner, queries)))
     heads = attention(info, queries, own_pair, partner)
     residual, normed_two = out_projection(info, heads, tokens, experts_scale, out_refs)
 
@@ -1273,6 +1283,7 @@
     share_rows = [a.reshape(height, 1) for a in picked[local_experts:]]
 
     out_rows, back_rows, gate_dots, reduced, marks = ([], [], [], [], [])
+    grad_slots = []
     for e in range(local_experts):
         rows_in = token_rows[e]
         if fast and e == 0:
@@ -1291,17 +1302,11 @@
                 got = flip(combine(chosen, back_rows, 1, 2), 1)
                 acts = after(acts, got)
             second, fourth = expert_grads(acts, token_rows[e], grad_row, (1, 3))
-            if e == 1:
-                second_out, fourth_out = after(
-                    (second, fourth), marks[0][1], *reduced[0][2]
-                )
-            else:
-                second_out, fourth_out = second, fourth
-            sent_first = reduce_first(second_out, fourth_out, chain=True)
-            marks.append(sent_first)
+            if e == 0:
+                relay, _ = reduce_first(second, fourth, chain=True)
+                marks.append((relay,))
             own_slot, third = expert_grads(acts, token_rows[e], grad_row, (0, 2))
-            sent_second = reduce_second(third, fourth, sent_first[0])
-            reduced.append((own_slot, sent_first, sent_second))
+            grad_slots.append((own_slot, second, third, fourth))
         else:
             slots = expert_grads(acts, token_rows[e], grad_row, tuple(range(col_count)))
             reduced.append(
@@ -1315,13 +1320,21 @@
     grad_shares = grad_shares.reshape(expert_total, TOK_DEV)
     if fast:
         back_keep = combine(chosen, back_rows, 0, 2)
-        back_parts = reduce_chips(back_keep, got)
-        out_rows = [after(a, back_keep) for a in out_rows]
+        sent_second = reduce_second(grad_slots[0][2], grad_slots[0][3], marks[0][0])
+        far_back = lax.ppermute(
+            after(grad_slots[0][3], *sent_second, *grad_slots[1], spread_dots), "cols", FAR
+        )
+        reduced.append((grad_slots[0][0], (marks[0][0], far_back), sent_second))
+        back_first = chips_first(back_keep, got)
+        back_parts = chips_second(back_keep, got, *send_chips(back_first))
+        out_rows = [after(a, *back_first) for a in out_rows]
         out_got = flip(combine(chosen, out_rows, 1, 2), 1)
         out_keep = combine(chosen, out_rows, 0, 2)
-        grad_shares = after(
-            grad_shares, own_slot, third, out_keep, out_got, marks[0][1], *reduced[0][2]
+        relay, _ = reduce_first(
+            after(grad_slots[1][1], far_back, back_parts[2], back_parts[5]), fourth, chain=True
         )
+        marks.append((relay,))
+        grad_shares = after(grad_shares, own_slot, third, out_keep, out_got, far_back)
     else:
 
         def summed(rows):
@@ -1344,6 +1357,9 @@
         out_refs,
     )
     if fast:
+        out_first = chips_first(out_keep, out_got)
+        out_flips = send_chips(out_first)
+        grad_heads = after(grad_heads, *out_first)
         router_parts = jnp.transpose(
             router_grad.astype(LOW).reshape(col_count, router_part, row_count, depth),
             (2, 0, 1, 3),
@@ -1363,7 +1379,7 @@
     arrived = lax.ppermute(source_grad.astype(LOW), "cols", [(j, i) for i, j in pairs])
     grad_pair = join_grads(info, own_grad, source_grad, arrived, cosine, sine)
     if fast:
-        grad_branch = after(grad_branch, marks[1][0])
+        grad_branch = after(grad_branch, marks[1][0], *out_flips)
         keep, send = weight_grads(
             info,
             [normed, heads],
@@ -1372,14 +1388,18 @@
             extra,
         )
         sent = flip(send, 1)
+        sent_second = reduce_second(grad_slots[1][2], grad_slots[1][3], marks[1][0])
         grad_pair = after(grad_pair, keep)
     tokens_grad, attention_gain_grad = token_back(
         info, grad_query, grad_pair, tokens, grad_residual, attention_scale, query_refs, pair_refs
     )
 
     if fast:
-        mixture = reduce_chips(out_keep, out_got)
-        slots = sum_parts(reduce_chips(keep, sent))
+        far_back = lax.ppermute(after(grad_slots[1][3], *sent_second, tokens_grad), "cols", FAR)
+        reduced.append((grad_slots[1][0], (marks[1][0], far_back), sent_second))
+        mixture = chips_second(out_keep, out_got, *out_flips)
+        sent_chips = send_chips(chips_first(keep, sent))
+        slots = sum_parts(chips_second(keep, sent, *sent_chips))
         width = query_part + 2 * key_part
         gain_sums = sum(
             jnp.sum(own[i, :depth, :width].astype(WIDE) * slots[i, :depth, :width], axis=1)

time: 842 us -> 816 us (0.969)
  waiting for transfers between devices: 290 us -> 223 us
  blocking collectives: 0 us -> 34.7 us
    ppermute x1, waiting for transfers between devices: 49.5 us -> 4.63 us  [on_device(): partner = lax.ppermute(own_pair, 'cols', pairs)]
    all_to_all x0 -> x1, blocking collectives: none -> 34.7 us  [on_device(): lax.all_to_all(spread_dots, 'rows', split_axis=0, concat_axis=0, tiled=True)]
    ppermute x3, waiting for transfers between devices: 0.01 us -> 27.3 us  [the longest x1 27.3 us: on_device(): lax.ppermute(after(grad_slots[0][3], *sent_second, *grad_slots[1], spread...]
    ppermute x3, waiting for transfers between devices: 33.1 us -> 15.1 us  [reduce_second(): lax.ppermute(downward_load, 'cols', DOWN)]
    all_to_all x1 -> x0, waiting for transfers between devices: 15.2 us -> none  [on_device(): lax.all_to_all(spread_dots, 'rows', split_axis=0, concat_axis=0, tiled=True)]
    ppermute x3, waiting for transfers between devices: 7.95 us -> 21.9 us  [send_far(): return lax.ppermute(block, 'cols', FAR)]
    ppermute x3, waiting for transfers between devices: 14.8 us -> 3.3 us  [reduce_first(): relay = lax.ppermute(second, 'cols', [(1, 3), (0, 1), (2, 0), (3, 2)])]
  transfers between devices with their start and end apart: 59 -> 58, of which waited for: 25 -> 28; matrix products, arithmetic and copies ran while one was open for 11% -> 11% of each run, Pallas kernels for 33% -> 32%
where the time goes in v8:
time: 816 us; the launch traced here: 805 us
  Pallas kernels  298 us (37%)
  waiting for transfers between devices  223 us (27%)
  starting transfers between devices  102 us (12%)
  other arithmetic  78.9 us (10%)
  local copies, waits for them, and re-layouts  52.1 us (6%)
  blocking collectives  34.7 us (4%)
  between operations  15.6 us (2%)
    ppermute x31, waiting for transfers between devices, flip(): return lax.ppermute(block, 'rows', [(i, i ^ bit) for i in range(count)])  73.9 us
    pallas_call x2, Pallas kernels, expert(): pl.pallas_call(functools.partial(expert_kernel, slots), grid=(height // E...  60.3 us
    pallas_call x8, Pallas kernels, dispatch(): pl.pallas_call(functools.partial(dispatch_kernel, local), grid_spec=pltpu...  41.2 us
    pallas_call x4, Pallas kernels, expert_grads(): pl.pallas_call(functools.partial(expert_grads_kernel, slots), grid=(D //...  39.5 us
    all_to_all x1, blocking collectives, on_device(): lax.all_to_all(spread_dots, 'rows', split_axis=0, concat_axis=0, tiled=True)  34.7 us
    ppermute x6, waiting for transfers between devices, send_near(): return (lax.ppermute(block, 'cols', DOWN), lax.ppermute(block, 'cols', UP))  30.5 us
    pallas_call x4, Pallas kernels, combine(): pl.pallas_call(functools.partial(combine_kernel, len(rows)), grid=(number...  30 us
    ppermute x1, waiting for transfers between devices, on_device(): lax.ppermute(after(grad_slots[0][3], *sent_second, *grad_slots[1], spread...  27.3 us
  transfers between devices with their start and end apart: 58, of which 28 were waited for; matrix products, arithmetic and copies ran while one was open for 11% of the time, Pallas kernels for 32%

profile of v8, /device:TPU:0, one launch (start us, length us, event | category | flops | bytes accessed | tf_op | source)
XLA Modules:
  0.0 804.8 jit_solution(16619845841998002714)
XLA Ops:
  14.0 5.6 collective-permute-start.1
  28.6 7.9 collective-permute-done.6
  43.3 5.7 collective-permute-start.3
  57.1 29.1 %collective-permute-done.2.rest_2_ = bf16[576,1536]{1,0:T(8,128)(2,1)S(1)} collective-permute-done((bf16[576,1536]{1,0:T(8,128)(2,1)S(1)}, bf16[576,1536]{1,0:T(8,128)(2,1)S(1)}, u32[]{:S(2)}, u32[]{:S(2)}) %collective-permute-start.2) | collective-permute-done | bytes 1769504 | tf_op jit(solution)/shard_map/ppermute | solution.py:992
  95.1 15.2 %collective-permute-done.10.rest_3_.rest_9_.rest_12_ = bf16[2,208,896]{2,1,0:T(8,128)(2,1)S(1)} collective-permute-done((bf16[2,208,896]{2,1,0:T(8,128)(2,1)S(1)}, bf16[2,208,896]{2,1,0:T(8,128)(2,1)S(1)}, u32[]{:S(2)}, u32[]{:S(2)}) %collective-permute-start.10) | collective-permute-done | bytes 745504 | tf_op jit(solution)/shard_map/ppermute | solution.py:1051
  111.8 18.2 %collective-permute-done.4.rest_1_ = bf16[576,1536]{1,0:T(8,128)(2,1)S(1)} collective-permute-done((bf16[576,1536]{1,0:T(8,128)(2,1)S(1)}, bf16[576,1536]{1,0:T(8,128)(2,1)S(1)}, u32[]{:S(2)}, u32[]{:S(2)}) %collective-permute-start.4) | collective-permute-done | bytes 1769504 | tf_op jit(solution)/shard_map/ppermute | solution.py:1003
  145.7 8.9 %query_projection.1.queries = bf16[512,1536]{1,0:T(8,128)(2,1)} custom-call(s32[16]{0:T(128)} %concatenate.39.info, bf16[512,1536]{1,0:T(8,128)(2,1)} %get-tuple-element.115.normed.rest_0_, f32[512,128]{1,0:T(8,128)} %get-tuple-element.298.cosine, f32[512,128]{1,0:T(8,128)} %get-tuple-element.299.sine, bf16[4,208,896]{2,1,0:T(8,128)(2,1)} %copy-done.1, ...), custom_call_target="tpu_custom_call" | custom-call | flops 1 | bytes 1 | tf_op jit(solution)/shard_map/query_projection/pallas_call | solution.py:192
  164.2 11.1 %tree_attention.1.heads.rest_1_ = bf16[512,1536]{1,0:T(8,128)(2,1)} custom-call(s32[16]{0:T(128)} %concatenate.39.info, bf16[512,1536]{1,0:T(8,128)(2,1)} %query_projection.1.queries, bf16[512,512]{1,0:T(8,128)(2,1)} %get-tuple-element.116.own, bf16[512,512]{1,0:T(8,128)(2,1)} %copy-done.32), custom_call_target="tpu_custom_call" | custom-call | flops 1 | bytes 1 | tf_op jit(solution)/shard_map/tree_attention/pallas_call | solution.py:274
  175.4 12.5 %out_projection.1 = (f32[512,1536]{1,0:T(8,128)}, bf16[512,1536]{1,0:T(8,128)(2,1)}) custom-call(s32[16]{0:T(128)} %concatenate.39.info, bf16[512,1536]{1,0:T(8,128)(2,1)} %tree_attention.1.heads.rest_1_, bf16[512,1536]{1,0:T(8,128)(2,1)} %tokens.4, f32[1,1536]{1,0:T(1,128)} %reshape.454.gain, bf16[4,208,896]{2,1,0:T(8,128)(2,1)} %copy-done.1, ...), custom_call_target="tpu_custom_call" | custom-call | flops 1 | bytes 1 | tf_op jit(solution)/shard_map/out_projection/pallas_call | solution.py:386
  187.9 13.9 %collective-permute-done.19.rest_4_ = bf16[576,1536]{1,0:T(8,128)(2,1)} collective-permute-done((bf16[576,1536]{1,0:T(8,128)(2,1)S(1)}, bf16[576,1536]{1,0:T(8,128)(2,1)}, u32[]{:S(2)}, u32[]{:S(2)}) %collective-permute-start.19) | collective-permute-done | bytes 1769504 | tf_op jit(solution)/shard_map/ppermute | solution.py:996
  203.2 6.0 collective-permute-start.21
  213.4 6.2 route_tables.1
  225.6 5.2 dispatch.8
  230.8 5.2 dispatch.9
  236.0 13.1 %pick_rows.1 = (bf16[8,160,1536]{2,1,0:T(8,128)(2,1)}, bf16[8,160,1536]{2,1,0:T(8,128)(2,1)}) custom-call(s32[8]{0:T(128)} %iota_xor_fusion.order.near, bf16[8,320,512]{2,1,0:T(8,128)(2,1)} %get-tuple-element.118.chosen, bf16[8,512,1536]{2,1,0:T(8,128)(2,1)} %bitcast.161), custom_call_target="tpu_custom_call" | custom-call | flops 1 | bytes 1 | tf_op jit(solution)/shard_map/pick_rows/pallas_call | solution.py:462
  268.0 5.2 dispatch.11
  273.2 5.1 dispatch.12
  279.6 5.2 dispatch.13
  287.2 5.1 dispatch.14
  305.0 30.2 %expert.2 = (bf16[1280,1536]{1,0:T(8,128)(2,1)}, bf16[1280,1536]{1,0:T(8,128)(2,1)}, bf16[1280,1536]{1,0:T(8,128)(2,1)}, bf16[4,576,1280]{2,1,0:T(8,128)(2,1)}, f32[1280,1]{1,0:T(8,128)}) custom-call(s32[16]{0:T(128)} %concatenate.39.info, bf16[1280,1536]{1,0:T(8,128)(2,1)} %bitcast.141, bf16[1280,1536]{1,0:T(8,128)(2,1)} %bitcast.165, f32[1280,1]{1,0:T(8,128)} %bitcast.147, ...), custom_call_target="tpu_custom_call" | custom-call | flops 1 | bytes 1 | tf_op jit(solution)/shard_map/expert/pallas_call | solution.py:657
  335.2 9.9 %expert_gradients.4 = (bf16[576,1536]{1,0:T(8,128)(2,1)}, bf16[576,1536]{1,0:T(8,128)(2,1)}) custom-call(bf16[1280,1536]{1,0:T(8,128)(2,1)} %bitcast.142, bf16[1280,1536]{1,0:T(8,128)(2,1)} %get-tuple-element.167.grads, bf16[4,576,1280]{2,1,0:T(8,128)(2,1)} %get-tuple-element.168.rest_0_.rest_1_, bf16[4,576,1280]{2,1,0:T(8,128)(2,1)} %get-tuple-element.168.rest_0_.rest_1_), custom_call_target="tpu_custom_call" | custom-call | flops 1 | bytes 1 | tf_op jit(solution)/shard_map/expert_gradients/pallas_call | solution.py:685
  345.5 9.8 %expert_gradients.5 = (bf16[576,1536]{1,0:T(8,128)(2,1)}, bf16[576,1536]{1,0:T(8,128)(2,1)}) custom-call(bf16[1280,1536]{1,0:T(8,128)(2,1)} %bitcast.143, bf16[1280,1536]{1,0:T(8,128)(2,1)} %get-tuple-element.167.grads, bf16[4,576,1280]{2,1,0:T(8,128)(2,1)} %get-tuple-element.168.rest_0_.rest_1_, bf16[4,576,1280]{2,1,0:T(8,128)(2,1)} %get-tuple-element.168.rest_0_.rest_1_), custom_call_target="tpu_custom_call" | custom-call | flops 1 | bytes 1 | tf_op jit(solution)/shard_map/expert_gradients/pallas_call | solution.py:685
  355.3 30.1 %expert.3 = (bf16[1280,1536]{1,0:T(8,128)(2,1)}, bf16[1280,1536]{1,0:T(8,128)(2,1)}, bf16[1280,1536]{1,0:T(8,128)(2,1)}, bf16[4,576,1280]{2,1,0:T(8,128)(2,1)}, f32[1280,1]{1,0:T(8,128)}) custom-call(s32[16]{0:T(128)} %concatenate.39.info, bf16[1280,1536]{1,0:T(8,128)(2,1)} %bitcast.144, bf16[1280,1536]{1,0:T(8,128)(2,1)} %bitcast.164, f32[1280,1]{1,0:T(8,128)} %bitcast.148, ...), custom_call_target="tpu_custom_call" | custom-call | flops 1 | bytes 1 | tf_op jit(solution)/shard_map/expert/pallas_call | solution.py:657
  386.0 7.5 combine.5
  393.5 7.5 combine.4
  411.6 7.6 combine.7
  422.3 5.3 collective-permute-start.36
  430.9 5.6 spread.1
  438.6 9.9 %expert_gradients.7 = (bf16[576,1536]{1,0:T(8,128)(2,1)}, bf16[576,1536]{1,0:T(8,128)(2,1)}) custom-call(bf16[1280,1536]{1,0:T(8,128)(2,1)} %bitcast.145, bf16[1280,1536]{1,0:T(8,128)(2,1)} %get-tuple-element.183.grads, bf16[4,576,1280]{2,1,0:T(8,128)(2,1)} %get-tuple-element.185.rest_0_.rest_1_, bf16[4,576,1280]{2,1,0:T(8,128)(2,1)} %get-tuple-element.185.rest_0_.rest_1_), custom_call_target="tpu_custom_call" | custom-call | flops 1 | bytes 1 | tf_op jit(solution)/shard_map/expert_gradients/pallas_call | solution.py:685
  448.5 9.9 %expert_gradients.6 = (bf16[576,1536]{1,0:T(8,128)(2,1)}, bf16[576,1536]{1,0:T(8,128)(2,1)}) custom-call(bf16[1280,1536]{1,0:T(8,128)(2,1)} %bitcast.146, bf16[1280,1536]{1,0:T(8,128)(2,1)} %get-tuple-element.183.grads, bf16[4,576,1280]{2,1,0:T(8,128)(2,1)} %get-tuple-element.185.rest_0_.rest_1_, bf16[4,576,1280]{2,1,0:T(8,128)(2,1)} %get-tuple-element.185.rest_0_.rest_1_), custom_call_target="tpu_custom_call" | custom-call | flops 1 | bytes 1 | tf_op jit(solution)/shard_map/expert_gradients/pallas_call | solution.py:685
  458.4 6.5 collective-permute-done.36
  465.0 5.3 collective-permute-done.37
  479.3 7.4 combine.6
  486.7 27.3 %collective-permute-done.38 = bf16[576,1536]{1,0:T(8,128)(2,1)} collective-permute-done((bf16[576,1536]{1,0:T(8,128)(2,1)}, bf16[576,1536]{1,0:T(8,128)(2,1)}, u32[]{:S(2)}, u32[]{:S(2)}) %collective-permute-start.38) | collective-permute-done | bytes 1769504 | tf_op jit(solution)/shard_map/ppermute | solution.py:1324
  523.0 34.7 %all_to_all.5 = f32[8,2,512]{2,1,0:T(2,128)} all-to-all(f32[8,2,512]{2,1,0:T(2,128)S(1)} %copy-done.48), channel_id=1, replica_groups=mesh['rows'=8,'cols'=4] {'rows'}, dimensions={0} | all-to-all | bytes 65536 | tf_op jit(solution)/shard_map/all_to_all | solution.py:1319
  563.3 13.5 %experts_norm_back.1 = (f32[512,1536]{1,0:T(8,128)}, bf16[512,1536]{1,0:T(8,128)(2,1)}, bf16[512,1536]{1,0:T(8,128)(2,1)}, f32[1,1536]{1,0:T(1,128)}, f32[16,1536]{1,0:T(8,128)}) custom-call(s32[16]{0:T(128)} %concatenate.39.info, f32[512,1536]{1,0:T(8,128)} %get-tuple-element.117.residual, bf16[512,1536]{1,0:T(8,128)(2,1)} %get-tuple-element.119.rows.normed, ...), custom_call_target="tpu_custom_call" | custom-call | flops 1 | bytes 1 | tf_op jit(solution)/shard_map/experts_norm_back/pallas_call | solution.py:787
  576.8 15.4 %tree_attention_back.1 = (bf16[512,1536]{1,0:T(8,128)(2,1)}, f32[512,512]{1,0:T(8,128)}, f32[512,512]{1,0:T(8,128)}) custom-call(s32[16]{0:T(128)} %concatenate.39.info, bf16[512,1536]{1,0:T(8,128)(2,1)} %query_projection.1.queries, bf16[512,512]{1,0:T(8,128)(2,1)} %get-tuple-element.116.own, bf16[512,512]{1,0:T(8,128)(2,1)} %copy-done.32, ...), custom_call_target="tpu_custom_call" | custom-call | flops 1 | bytes 1 | tf_op jit(solution)/shard_map/tree_attention_back/pallas_call | solution.py:335
  611.3 16.7 %weight_gradients.1 = (bf16[4,4,208,896]{3,2,1,0:T(8,128)(2,1)}, bf16[4,4,208,896]{3,2,1,0:T(8,128)(2,1)}) custom-call(s32[16]{0:T(128)} %concatenate.39.info, bf16[512,1536]{1,0:T(8,128)(2,1)} %get-tuple-element.115.normed.rest_0_, bf16[512,1536]{1,0:T(8,128)(2,1)} %tree_attention.1.heads.rest_1_, bf16[512,1536]{1,0:T(8,128)(2,1)} %get-tuple-element.194.rest_2_.grad_query, ...), custom_call_target="tpu_custom_call" | custom-call | flops 1 | bytes 1 | tf_op jit(solution)/shard_map/weight_gradients/pallas_call | solution.py:939
  630.9 5.6 collective-permute-start.54
  639.3 6.2 fusion.5
  645.4 13.5 %token_gradient.1 = (bf16[512,1536]{1,0:T(8,128)(2,1)}, f32[1,1536]{1,0:T(1,128)}) custom-call(s32[16]{0:T(128)} %concatenate.39.info, bf16[512,1536]{1,0:T(8,128)(2,1)} %get-tuple-element.194.rest_2_.grad_query, bf16[512,512]{1,0:T(8,128)(2,1)} %join_key_value_gradients.1.rest_3_.grad_pair, bf16[512,1536]{1,0:T(8,128)(2,1)} %tokens.4, ...), custom_call_target="tpu_custom_call" | custom-call | flops 1 | bytes 1 | tf_op jit(solution)/shard_map/token_gradient/pallas_call | solution.py:878
  658.9 15.2 %collective-permute-done.54 = bf16[576,1536]{1,0:T(8,128)(2,1)} collective-permute-done((bf16[576,1536]{1,0:T(8,128)(2,1)}, bf16[576,1536]{1,0:T(8,128)(2,1)}, u32[]{:S(2)}, u32[]{:S(2)}) %collective-permute-start.54) | collective-permute-done | bytes 1769504 | tf_op jit(solution)/shard_map/ppermute | solution.py:1031
  674.1 5.4 collective-permute-done.55
  694.1 10.6 %collective-permute-done.33 = bf16[256,1536]{1,0:T(8,128)(2,1)S(1)} collective-permute-done((bf16[256,1536]{1,0:T(8,128)(2,1)S(1)}, bf16[256,1536]{1,0:T(8,128)(2,1)S(1)}, u32[]{:S(2)}, u32[]{:S(2)}) %collective-permute-start.33) | collective-permute-done | bytes 786464 | tf_op jit(solution)/shard_map/ppermute | solution.py:1051
  710.3 24.6 %collective-permute-done.48 = bf16[2,2,208,896]{3,2,1,0:T(8,128)(2,1)S(1)} collective-permute-done((bf16[2,2,208,896]{3,2,1,0:T(8,128)(2,1)S(1)}, bf16[2,2,208,896]{3,2,1,0:T(8,128)(2,1)S(1)}, u32[]{:S(2)}, u32[]{:S(2)}) %collective-permute-start.48) | collective-permute-done | bytes 1490976 | tf_op jit(solution)/shard_map/ppermute | solution.py:1051
  742.4 12.3 %collective-permute-done.47 = bf16[2,208,896]{2,1,0:T(8,128)(2,1)S(1)} collective-permute-done((bf16[2,208,896]{2,1,0:T(8,128)(2,1)S(1)}, bf16[2,208,896]{2,1,0:T(8,128)(2,1)S(1)}, u32[]{:S(2)}, u32[]{:S(2)}) %collective-permute-start.47) | collective-permute-done | bytes 745504 | tf_op jit(solution)/shard_map/ppermute | solution.py:1051
  766.5 5.3 collective-permute-start.53
  774.6 9.7 %collective-permute-start.51 = (bf16[208,896]{1,0:T(8,128)(2,1)S(1)}, bf16[208,896]{1,0:T(8,128)(2,1)S(1)}, u32[]{:S(2)}, u32[]{:S(2)}) collective-permute-start(bf16[208,896]{1,0:T(8,128)(2,1)S(1)} %get-tuple-element.274), channel_id=1, source_target_pairs={{0,1},{1,2},{2,3},{4,5},{5,6},{6,7},{8,9},{9,10},{10,11},{12,13},{... | collective-permute-start | bytes 1118216 | tf_op jit(solution)/shard_map/ppermute | solution.py:1031
  (329 shorter events, 236.1 us)
Async XLA Ops:
  7.2 228.8 %all-gather.3.cloned.1.call-start = ((), (), s32[]{:S(2)}) async-start(), calls=%async_computation.1 | async-start | bytes 14155776 | tf_op jit(solution)/shard_map/all_gather | solution.py:1233
  19.5 17.0 %collective-permute-start.6 = (bf16[208,896]{1,0:T(8,128)(2,1)S(1)}, bf16[208,896]{1,0:T(8,128)(2,1)}, u32[]{:S(2)}, u32[]{:S(2)}) collective-permute-start(bf16[208,896]{1,0:T(8,128)(2,1)S(1)} %concatenate.43), channel_id=1, source_target_pairs={{0,3},{3,0},{4,7},{7,4},{8,11},{11,8},{12,15},{15,12},{16,19},{19,... | collective-permute-start | bytes 1118216 | tf_op jit(solution)/shard_map/ppermute | solution.py:996
  42.0 44.3 %collective-permute-start.2 = (bf16[576,1536]{1,0:T(8,128)(2,1)S(1)}, bf16[576,1536]{1,0:T(8,128)(2,1)S(1)}, u32[]{:S(2)}, u32[]{:S(2)}) collective-permute-start(bf16[576,1536]{1,0:T(8,128)(2,1)S(1)} %pad_maximum_fusion.2.rest_0_), channel_id=1, source_target_pairs={{1,0},{2,1},{3,2},{5,4},{6,5},{7,6},{9,8},{10,9},{11,10},{13,12},{... | collective-permute-start | bytes 5308424 | tf_op jit(solution)/shard_map/ppermute | solution.py:992
  43.3 43.0 %collective-permute-start.3 = (bf16[576,1536]{1,0:T(8,128)(2,1)S(1)}, bf16[576,1536]{1,0:T(8,128)(2,1)}, u32[]{:S(2)}, u32[]{:S(2)}) collective-permute-start(bf16[576,1536]{1,0:T(8,128)(2,1)S(1)} %pad_maximum_fusion.2.rest_0_), channel_id=1, source_target_pairs={{0,1},{1,2},{2,3},{4,5},{5,6},{6,7},{8,9},{9,10},{10,11},{12,13},{... | collective-permute-start | bytes 5308424 | tf_op jit(solution)/shard_map/ppermute | solution.py:992
  54.0 32.2 %collective-permute-start.7 = (bf16[4,208,896]{2,1,0:T(8,128)(2,1)S(1)}, bf16[4,208,896]{2,1,0:T(8,128)(2,1)S(1)}, u32[]{:S(2)}, u32[]{:S(2)}) collective-permute-start(bf16[4,208,896]{2,1,0:T(8,128)(2,1)S(1)} %pad_maximum_fusion.8.rest_0_.rest_6_.rest_9_), channel_id=1, source_target_pairs={{0,8},{4,12},{8,0},{12,4},{16,24},{20,28},{24,16},{28,20},{1,9},{5... | collective-permute-start | bytes 4472840 | tf_op jit(solution)/shard_map/ppermute | solution.py:1051
  55.6 31.1 %collective-permute-start.8 = (bf16[4,208,896]{2,1,0:T(8,128)(2,1)S(1)}, bf16[4,208,896]{2,1,0:T(8,128)(2,1)S(1)}, u32[]{:S(2)}, u32[]{:S(2)}) collective-permute-start(bf16[4,208,896]{2,1,0:T(8,128)(2,1)S(1)} %pad_maximum_fusion.8.rest_0_.rest_6_.rest_9_), channel_id=1, source_target_pairs={{0,16},{4,20},{8,24},{12,28},{16,0},{20,4},{24,8},{28,12},{1,17},{... | collective-permute-start | bytes 4472840 | tf_op jit(solution)/shard_map/ppermute | solution.py:1051
  57.1 29.6 %collective-permute-start.9 = (bf16[4,208,896]{2,1,0:T(8,128)(2,1)S(1)}, bf16[4,208,896]{2,1,0:T(8,128)(2,1)}, u32[]{:S(2)}, u32[]{:S(2)}) collective-permute-start(bf16[4,208,896]{2,1,0:T(8,128)(2,1)S(1)} %pad_maximum_fusion.8.rest_0_.rest_6_.rest_9_), channel_id=1, source_target_pairs={{0,4},{4,0},{8,12},{12,8},{16,20},{20,16},{24,28},{28,24},{1,5},{5... | collective-permute-start | bytes 4472840 | tf_op jit(solution)/shard_map/ppermute | solution.py:1051
  87.0 44.2 %collective-permute-start.12 = (bf16[8,208,896]{2,1,0:T(8,128)(2,1)S(1)}, bf16[8,208,896]{2,1,0:T(8,128)(2,1)S(1)}, u32[]{:S(2)}, u32[]{:S(2)}) collective-permute-start(bf16[8,208,896]{2,1,0:T(8,128)(2,1)S(1)} %pad_maximum_fusion), channel_id=1, source_target_pairs={{0,4},{4,0},{8,12},{12,8},{16,20},{20,16},{24,28},{28,24},{1,5},{5... | collective-permute-start | bytes 8945672 | tf_op jit(solution)/shard_map/ppermute | solution.py:1051
  87.9 42.1 %collective-permute-start.4 = (bf16[576,1536]{1,0:T(8,128)(2,1)S(1)}, bf16[576,1536]{1,0:T(8,128)(2,1)S(1)}, u32[]{:S(2)}, u32[]{:S(2)}) collective-permute-start(bf16[576,1536]{1,0:T(8,128)(2,1)S(1)} %select_select_fusion.1), channel_id=1, source_target_pairs={{3,1},{1,0},{0,2},{2,3},{7,5},{5,4},{4,6},{6,7},{11,9},{9,8},{8,10... | collective-permute-start | bytes 5308424 | tf_op jit(solution)/shard_map/ppermute | solution.py:1003
  92.1 18.3 %collective-permute-start.10 = (bf16[2,208,896]{2,1,0:T(8,128)(2,1)S(1)}, bf16[2,208,896]{2,1,0:T(8,128)(2,1)S(1)}, u32[]{:S(2)}, u32[]{:S(2)}) collective-permute-start(bf16[2,208,896]{2,1,0:T(8,128)(2,1)S(1)} %slice.450), channel_id=1, source_target_pairs={{0,16},{4,20},{8,24},{12,28},{16,0},{20,4},{24,8},{28,12},{1,17},{... | collective-permute-start | bytes 2236424 | tf_op jit(solution)/shard_map/ppermute | solution.py:1051
  93.6 18.2 %collective-permute-start.11 = (bf16[2,208,896]{2,1,0:T(8,128)(2,1)S(1)}, bf16[2,208,896]{2,1,0:T(8,128)(2,1)S(1)}, u32[]{:S(2)}, u32[]{:S(2)}) collective-permute-start(bf16[2,208,896]{2,1,0:T(8,128)(2,1)S(1)} %slice.451), channel_id=1, source_target_pairs={{0,8},{4,12},{8,0},{12,4},{16,24},{20,28},{24,16},{28,20},{1,9},{5... | collective-permute-start | bytes 2236424 | tf_op jit(solution)/shard_map/ppermute | solution.py:1051
  110.4 19.6 %collective-permute-start.13 = (bf16[2,208,896]{2,1,0:T(8,128)(2,1)S(1)}, bf16[2,208,896]{2,1,0:T(8,128)(2,1)S(1)}, u32[]{:S(2)}, u32[]{:S(2)}) collective-permute-start(bf16[2,208,896]{2,1,0:T(8,128)(2,1)S(1)} %collective-permute-done.10.rest_3_.rest_9_.rest_12_), channel_id=1, source_target_pairs={{0,4},{4,0},{8,12},{12,8},{16,20},{20,16},{24,28},{28,24},{1,5},{5... | collective-permute-start | bytes 2236424 | tf_op jit(solution)/shard_map/ppermute | solution.py:1051
  111.8 18.2 %collective-permute-start.14 = (bf16[2,208,896]{2,1,0:T(8,128)(2,1)S(1)}, bf16[2,208,896]{2,1,0:T(8,128)(2,1)S(1)}, u32[]{:S(2)}, u32[]{:S(2)}) collective-permute-start(bf16[2,208,896]{2,1,0:T(8,128)(2,1)S(1)} %collective-permute-done.11.rest_4_.rest_10_.rest_13_), channel_id=1, source_target_pairs={{0,4},{4,0},{8,12},{12,8},{16,20},{20,16},{24,28},{28,24},{1,5},{5... | collective-permute-start | bytes 2236424 | tf_op jit(solution)/shard_map/ppermute | solution.py:1051
  144.3 14.9 %collective-permute-start.15 = (bf16[512,512]{1,0:T(8,128)(2,1)S(1)}, bf16[512,512]{1,0:T(8,128)(2,1)S(1)}, u32[]{:S(2)}, u32[]{:S(2)}) collective-permute-start(bf16[512,512]{1,0:T(8,128)(2,1)S(1)} %copy-done.31), channel_id=1, source_target_pairs={{1,0},{3,2},{5,4},{7,6},{9,8},{11,10},{13,12},{15,14},{17,16},{19,... | collective-permute-start | bytes 1572872 | tf_op jit(solution)/shard_map/ppermute | solution.py:1235
  159.2 42.7 %collective-permute-start.19 = (bf16[576,1536]{1,0:T(8,128)(2,1)S(1)}, bf16[576,1536]{1,0:T(8,128)(2,1)}, u32[]{:S(2)}, u32[]{:S(2)}) collective-permute-start(bf16[576,1536]{1,0:T(8,128)(2,1)S(1)} %copy-done.11), channel_id=1, source_target_pairs={{0,3},{3,0},{4,7},{7,4},{8,11},{11,8},{12,15},{15,12},{16,19},{19,... | collective-permute-start | bytes 5308424 | tf_op jit(solution)/shard_map/ppermute | solution.py:996
  201.9 47.3 %collective-permute-start.20 = (bf16[576,1536]{1,0:T(8,128)(2,1)S(1)}, bf16[576,1536]{1,0:T(8,128)(2,1)S(1)}, u32[]{:S(2)}, u32[]{:S(2)}) collective-permute-start(bf16[576,1536]{1,0:T(8,128)(2,1)S(1)} %pad_maximum_fusion.3.rest_0_), channel_id=1, source_target_pairs={{1,0},{2,1},{3,2},{5,4},{6,5},{7,6},{9,8},{10,9},{11,10},{13,12},{... | collective-permute-start | bytes 5308424 | tf_op jit(solution)/shard_map/ppermute | solution.py:992
  203.2 46.0 %collective-permute-start.21 = (bf16[576,1536]{1,0:T(8,128)(2,1)S(1)}, bf16[576,1536]{1,0:T(8,128)(2,1)}, u32[]{:S(2)}, u32[]{:S(2)}) collective-permute-start(bf16[576,1536]{1,0:T(8,128)(2,1)S(1)} %pad_maximum_fusion.3.rest_0_), channel_id=1, source_target_pairs={{0,1},{1,2},{2,3},{4,5},{5,6},{6,7},{8,9},{9,10},{10,11},{12,13},{... | collective-permute-start | bytes 5308424 | tf_op jit(solution)/shard_map/ppermute | solution.py:992
  209.1 21.7 %collective-permute-start.18 = (bf16[512,1536]{1,0:T(8,128)(2,1)}, bf16[512,1536]{1,0:T(8,128)(2,1)}, u32[]{:S(2)}, u32[]{:S(2)}) collective-permute-start(bf16[512,1536]{1,0:T(8,128)(2,1)} %get-tuple-element.119.rows.normed), channel_id=1, source_target_pairs={{0,4},{4,0},{8,12},{12,8},{16,20},{20,16},{24,28},{28,24},{1,5},{5... | collective-permute-start | bytes 4718600 | tf_op jit(solution)/shard_map/ppermute | solution.py:1051
  209.2 39.9 %collective-permute-start.16 = (bf16[512,1536]{1,0:T(8,128)(2,1)}, bf16[512,1536]{1,0:T(8,128)(2,1)}, u32[]{:S(2)}, u32[]{:S(2)}) collective-permute-start(bf16[512,1536]{1,0:T(8,128)(2,1)} %get-tuple-element.119.rows.normed), channel_id=1, source_target_pairs={{0,8},{4,12},{8,0},{12,4},{16,24},{20,28},{24,16},{28,20},{1,9},{5... | collective-permute-start | bytes 4718600 | tf_op jit(solution)/shard_map/ppermute | solution.py:1051
  209.3 39.8 %collective-permute-start.17 = (bf16[512,1536]{1,0:T(8,128)(2,1)}, bf16[512,1536]{1,0:T(8,128)(2,1)}, u32[]{:S(2)}, u32[]{:S(2)}) collective-permute-start(bf16[512,1536]{1,0:T(8,128)(2,1)} %get-tuple-element.119.rows.normed), channel_id=1, source_target_pairs={{0,16},{4,20},{8,24},{12,28},{16,0},{20,4},{24,8},{28,12},{1,17},{... | collective-permute-start | bytes 4718600 | tf_op jit(solution)/shard_map/ppermute | solution.py:1051
  253.0 25.4 %collective-permute-start.25 = (bf16[512,1536]{1,0:T(8,128)(2,1)}, bf16[512,1536]{1,0:T(8,128)(2,1)S(1)}, u32[]{:S(2)}, u32[]{:S(2)}) collective-permute-start(bf16[512,1536]{1,0:T(8,128)(2,1)} %collective-permute-done.17.rows), channel_id=1, source_target_pairs={{0,4},{4,0},{8,12},{12,8},{16,20},{20,16},{24,28},{28,24},{1,5},{5... | collective-permute-start | bytes 4718600 | tf_op jit(solution)/shard_map/ppermute | solution.py:1051
  257.3 27.5 %collective-permute-start.22 = (bf16[256,1536]{1,0:T(8,128)(2,1)}, bf16[256,1536]{1,0:T(8,128)(2,1)S(1)}, u32[]{:S(2)}, u32[]{:S(2)}) collective-permute-start(bf16[256,1536]{1,0:T(8,128)(2,1)} %slice.459), channel_id=1, source_target_pairs={{0,16},{4,20},{8,24},{12,28},{16,0},{20,4},{24,8},{28,12},{1,17},{... | collective-permute-start | bytes 2359304 | tf_op jit(solution)/shard_map/ppermute | solution.py:1051
  257.5 27.3 %collective-permute-start.23 = (bf16[256,1536]{1,0:T(8,128)(2,1)}, bf16[256,1536]{1,0:T(8,128)(2,1)}, u32[]{:S(2)}, u32[]{:S(2)}) collective-permute-start(bf16[256,1536]{1,0:T(8,128)(2,1)} %slice.460), channel_id=1, source_target_pairs={{0,8},{4,12},{8,0},{12,4},{16,24},{20,28},{24,16},{28,20},{1,9},{5... | collective-permute-start | bytes 2359304 | tf_op jit(solution)/shard_map/ppermute | solution.py:1051
  260.8 40.7 %collective-permute-start.27 = (bf16[576,1536]{1,0:T(8,128)(2,1)}, bf16[576,1536]{1,0:T(8,128)(2,1)S(1)}, u32[]{:S(2)}, u32[]{:S(2)}) collective-permute-start(bf16[576,1536]{1,0:T(8,128)(2,1)} %select_select_fusion), channel_id=1, source_target_pairs={{3,1},{1,0},{0,2},{2,3},{7,5},{5,4},{4,6},{6,7},{11,9},{9,8},{8,10... | collective-permute-start | bytes 5308424 | tf_op jit(solution)/shard_map/ppermute | solution.py:1003
  301.5 53.8 %collective-permute-start.28 = (bf16[576,1536]{1,0:T(8,128)(2,1)S(1)}, bf16[576,1536]{1,0:T(8,128)(2,1)}, u32[]{:S(2)}, u32[]{:S(2)}) collective-permute-start(bf16[576,1536]{1,0:T(8,128)(2,1)S(1)} %pad_maximum_fusion.3.rest_0_), channel_id=1, source_target_pairs={{0,3},{3,0},{4,7},{7,4},{8,11},{11,8},{12,15},{15,12},{16,19},{19,... | collective-permute-start | bytes 5308424 | tf_op jit(solution)/shard_map/ppermute | solution.py:996
  345.1 41.0 %collective-permute-start.29 = (bf16[576,1536]{1,0:T(8,128)(2,1)}, bf16[576,1536]{1,0:T(8,128)(2,1)S(1)}, u32[]{:S(2)}, u32[]{:S(2)}) collective-permute-start(bf16[576,1536]{1,0:T(8,128)(2,1)} %get-tuple-element.169), channel_id=1, source_target_pairs={{1,3},{0,1},{2,0},{3,2},{5,7},{4,5},{6,4},{7,6},{9,11},{8,9},{10,8... | collective-permute-start | bytes 5308424 | tf_op jit(solution)/shard_map/ppermute | solution.py:1019
  419.2 95.0 %collective-permute-start.31 = (bf16[4,512,1536]{2,1,0:T(8,128)(2,1)}, bf16[4,512,1536]{2,1,0:T(8,128)(2,1)}, u32[]{:S(2)}, u32[]{:S(2)}) collective-permute-start(bf16[4,512,1536]{2,1,0:T(8,128)(2,1)} %combine.7), channel_id=1, source_target_pairs={{0,4},{4,0},{8,12},{12,8},{16,20},{20,16},{24,28},{28,24},{1,5},{5... | collective-permute-start | bytes 18874376 | tf_op jit(solution)/shard_map/ppermute | solution.py:1051
  422.3 42.7 %collective-permute-start.36 = (bf16[576,1536]{1,0:T(8,128)(2,1)}, bf16[576,1536]{1,0:T(8,128)(2,1)}, u32[]{:S(2)}, u32[]{:S(2)}) collective-permute-start(bf16[576,1536]{1,0:T(8,128)(2,1)} %get-tuple-element.273), channel_id=1, source_target_pairs={{0,1},{1,2},{2,3},{4,5},{5,6},{6,7},{8,9},{9,10},{10,11},{12,13},{... | collective-permute-start | bytes 5308424 | tf_op jit(solution)/shard_map/ppermute | solution.py:1031
  427.5 42.8 %collective-permute-start.37 = (bf16[576,1536]{1,0:T(8,128)(2,1)}, bf16[576,1536]{1,0:T(8,128)(2,1)}, u32[]{:S(2)}, u32[]{:S(2)}) collective-permute-start(bf16[576,1536]{1,0:T(8,128)(2,1)} %get-tuple-element.272), channel_id=1, source_target_pairs={{1,0},{2,1},{3,2},{5,4},{6,5},{7,6},{9,8},{10,9},{11,10},{13,12},{... | collective-permute-start | bytes 5308424 | tf_op jit(solution)/shard_map/ppermute | solution.py:1032
  428.8 43.6 %collective-permute-start.41 = (bf16[2,256,1536]{2,1,0:T(8,128)(2,1)}, bf16[2,256,1536]{2,1,0:T(8,128)(2,1)}, u32[]{:S(2)}, u32[]{:S(2)}) collective-permute-start(bf16[2,256,1536]{2,1,0:T(8,128)(2,1)} %pad_maximum_fusion.5), channel_id=1, source_target_pairs={{0,16},{4,20},{8,24},{12,28},{16,0},{20,4},{24,8},{28,12},{1,17},{... | collective-permute-start | bytes 4718600 | tf_op jit(solution)/shard_map/ppermute | solution.py:1051
  430.6 41.8 %collective-permute-start.39 = (bf16[2,256,1536]{2,1,0:T(8,128)(2,1)}, bf16[2,256,1536]{2,1,0:T(8,128)(2,1)}, u32[]{:S(2)}, u32[]{:S(2)}) collective-permute-start(bf16[2,256,1536]{2,1,0:T(8,128)(2,1)} %pad_maximum_fusion.4), channel_id=1, source_target_pairs={{0,8},{4,12},{8,0},{12,4},{16,24},{20,28},{24,16},{28,20},{1,9},{5... | collective-permute-start | bytes 4718600 | tf_op jit(solution)/shard_map/ppermute | solution.py:1051
  470.3 43.8 %collective-permute-start.38 = (bf16[576,1536]{1,0:T(8,128)(2,1)}, bf16[576,1536]{1,0:T(8,128)(2,1)}, u32[]{:S(2)}, u32[]{:S(2)}) collective-permute-start(bf16[576,1536]{1,0:T(8,128)(2,1)} %get-tuple-element.190), channel_id=1, source_target_pairs={{0,3},{3,0},{4,7},{7,4},{8,11},{11,8},{12,15},{15,12},{16,19},{19,... | collective-permute-start | bytes 5308424 | tf_op jit(solution)/shard_map/ppermute | solution.py:1324
  477.3 36.8 %collective-permute-start.40 = (bf16[256,1536]{1,0:T(8,128)(2,1)}, bf16[256,1536]{1,0:T(8,128)(2,1)S(1)}, u32[]{:S(2)}, u32[]{:S(2)}) collective-permute-start(bf16[256,1536]{1,0:T(8,128)(2,1)} %get-tuple-element.242), channel_id=1, source_target_pairs={{0,16},{4,20},{8,24},{12,28},{16,0},{20,4},{24,8},{28,12},{1,17},{... | collective-permute-start | bytes 2359304 | tf_op jit(solution)/shard_map/ppermute | solution.py:1051
  479.0 35.1 %collective-permute-start.42 = (bf16[256,1536]{1,0:T(8,128)(2,1)}, bf16[256,1536]{1,0:T(8,128)(2,1)S(1)}, u32[]{:S(2)}, u32[]{:S(2)}) collective-permute-start(bf16[256,1536]{1,0:T(8,128)(2,1)} %get-tuple-element.240), channel_id=1, source_target_pairs={{0,8},{4,12},{8,0},{12,4},{16,24},{20,28},{24,16},{28,20},{1,9},{5... | collective-permute-start | bytes 2359304 | tf_op jit(solution)/shard_map/ppermute | solution.py:1051
  514.1 97.2 %collective-permute-start.44 = (bf16[576,1536]{1,0:T(8,128)(2,1)}, bf16[576,1536]{1,0:T(8,128)(2,1)S(1)}, u32[]{:S(2)}, u32[]{:S(2)}) collective-permute-start(bf16[576,1536]{1,0:T(8,128)(2,1)} %get-tuple-element.198), channel_id=1, source_target_pairs={{1,3},{0,1},{2,0},{3,2},{5,7},{4,5},{6,4},{7,6},{9,11},{8,9},{10,8... | collective-permute-start | bytes 5308424 | tf_op jit(solution)/shard_map/ppermute | solution.py:1019
  519.6 91.7 %collective-permute-start.34 = (bf16[2,256,1536]{2,1,0:T(8,128)(2,1)}, bf16[2,256,1536]{2,1,0:T(8,128)(2,1)}, u32[]{:S(2)}, u32[]{:S(2)}) collective-permute-start(bf16[2,256,1536]{2,1,0:T(8,128)(2,1)} %pad_maximum_fusion.7), channel_id=1, source_target_pairs={{0,16},{4,20},{8,24},{12,28},{16,0},{20,4},{24,8},{28,12},{1,17},{... | collective-permute-start | bytes 4718600 | tf_op jit(solution)/shard_map/ppermute | solution.py:1051
  522.7 88.6 %collective-permute-start.32 = (bf16[2,256,1536]{2,1,0:T(8,128)(2,1)}, bf16[2,256,1536]{2,1,0:T(8,128)(2,1)}, u32[]{:S(2)}, u32[]{:S(2)}) collective-permute-start(bf16[2,256,1536]{2,1,0:T(8,128)(2,1)} %pad_maximum_fusion.6), channel_id=1, source_target_pairs={{0,8},{4,12},{8,0},{12,4},{16,24},{20,28},{24,16},{28,20},{1,9},{5... | collective-permute-start | bytes 4718600 | tf_op jit(solution)/shard_map/ppermute | solution.py:1051
  628.1 57.7 %collective-permute-start.45 = (bf16[4,4,208,896]{3,2,1,0:T(8,128)(2,1)}, bf16[4,4,208,896]{3,2,1,0:T(8,128)(2,1)}, u32[]{:S(2)}, u32[]{:S(2)}) collective-permute-start(bf16[4,4,208,896]{3,2,1,0:T(8,128)(2,1)} %get-tuple-element.206), channel_id=1, source_target_pairs={{0,4},{4,0},{8,12},{12,8},{16,20},{20,16},{24,28},{28,24},{1,5},{5... | collective-permute-start | bytes 17891336 | tf_op jit(solution)/shard_map/ppermute | solution.py:1051
  630.9 43.2 %collective-permute-start.54 = (bf16[576,1536]{1,0:T(8,128)(2,1)}, bf16[576,1536]{1,0:T(8,128)(2,1)}, u32[]{:S(2)}, u32[]{:S(2)}) collective-permute-start(bf16[576,1536]{1,0:T(8,128)(2,1)} %get-tuple-element.271), channel_id=1, source_target_pairs={{0,1},{1,2},{2,3},{4,5},{5,6},{6,7},{8,9},{9,10},{10,11},{12,13},{... | collective-permute-start | bytes 5308424 | tf_op jit(solution)/shard_map/ppermute | solution.py:1031
  636.6 42.9 %collective-permute-start.55 = (bf16[576,1536]{1,0:T(8,128)(2,1)}, bf16[576,1536]{1,0:T(8,128)(2,1)}, u32[]{:S(2)}, u32[]{:S(2)}) collective-permute-start(bf16[576,1536]{1,0:T(8,128)(2,1)} %get-tuple-element.270), channel_id=1, source_target_pairs={{1,0},{2,1},{3,2},{5,4},{6,5},{7,6},{9,8},{10,9},{11,10},{13,12},{... | collective-permute-start | bytes 5308424 | tf_op jit(solution)/shard_map/ppermute | solution.py:1032
  679.5 59.7 %collective-permute-start.56 = (bf16[576,1536]{1,0:T(8,128)(2,1)S(1)}, bf16[576,1536]{1,0:T(8,128)(2,1)S(1)}, u32[]{:S(2)}, u32[]{:S(2)}) collective-permute-start(bf16[576,1536]{1,0:T(8,128)(2,1)S(1)} %copy-done.37), channel_id=1, source_target_pairs={{0,3},{3,0},{4,7},{7,4},{8,11},{11,8},{12,15},{15,12},{16,19},{19,... | collective-permute-start | bytes 5308424 | tf_op jit(solution)/shard_map/ppermute | solution.py:1398
  684.2 20.5 %collective-permute-start.33 = (bf16[256,1536]{1,0:T(8,128)(2,1)S(1)}, bf16[256,1536]{1,0:T(8,128)(2,1)S(1)}, u32[]{:S(2)}, u32[]{:S(2)}) collective-permute-start(bf16[256,1536]{1,0:T(8,128)(2,1)S(1)} %get-tuple-element.246), channel_id=1, source_target_pairs={{0,16},{4,20},{8,24},{12,28},{16,0},{20,4},{24,8},{28,12},{1,17},{... | collective-permute-start | bytes 2359304 | tf_op jit(solution)/shard_map/ppermute | solution.py:1051
  685.5 20.5 %collective-permute-start.35 = (bf16[256,1536]{1,0:T(8,128)(2,1)S(1)}, bf16[256,1536]{1,0:T(8,128)(2,1)S(1)}, u32[]{:S(2)}, u32[]{:S(2)}) collective-permute-start(bf16[256,1536]{1,0:T(8,128)(2,1)S(1)} %get-tuple-element.247), channel_id=1, source_target_pairs={{0,8},{4,12},{8,0},{12,4},{16,24},{20,28},{24,16},{28,20},{1,9},{5... | collective-permute-start | bytes 2359304 | tf_op jit(solution)/shard_map/ppermute | solution.py:1051
  689.4 45.5 %collective-permute-start.48 = (bf16[2,2,208,896]{3,2,1,0:T(8,128)(2,1)S(1)}, bf16[2,2,208,896]{3,2,1,0:T(8,128)(2,1)S(1)}, u32[]{:S(2)}, u32[]{:S(2)}) collective-permute-start(bf16[2,2,208,896]{3,2,1,0:T(8,128)(2,1)S(1)} %pad_maximum_fusion.10), channel_id=1, source_target_pairs={{0,16},{4,20},{8,24},{12,28},{16,0},{20,4},{24,8},{28,12},{1,17},{... | collective-permute-start | bytes 4472840 | tf_op jit(solution)/shard_map/ppermute | solution.py:1051
  690.6 45.3 %collective-permute-start.46 = (bf16[2,2,208,896]{3,2,1,0:T(8,128)(2,1)S(1)}, bf16[2,2,208,896]{3,2,1,0:T(8,128)(2,1)S(1)}, u32[]{:S(2)}, u32[]{:S(2)}) collective-permute-start(bf16[2,2,208,896]{3,2,1,0:T(8,128)(2,1)S(1)} %pad_maximum_fusion.9), channel_id=1, source_target_pairs={{0,8},{4,12},{8,0},{12,4},{16,24},{20,28},{24,16},{28,20},{1,9},{5... | collective-permute-start | bytes 4472840 | tf_op jit(solution)/shard_map/ppermute | solution.py:1051
  737.9 16.8 %collective-permute-start.47 = (bf16[2,208,896]{2,1,0:T(8,128)(2,1)S(1)}, bf16[2,208,896]{2,1,0:T(8,128)(2,1)S(1)}, u32[]{:S(2)}, u32[]{:S(2)}) collective-permute-start(bf16[2,208,896]{2,1,0:T(8,128)(2,1)S(1)} %get-tuple-element.258), channel_id=1, source_target_pairs={{0,16},{4,20},{8,24},{12,28},{16,0},{20,4},{24,8},{28,12},{1,17},{... | collective-permute-start | bytes 2236424 | tf_op jit(solution)/shard_map/ppermute | solution.py:1051
  738.8 16.5 %collective-permute-start.49 = (bf16[2,208,896]{2,1,0:T(8,128)(2,1)S(1)}, bf16[2,208,896]{2,1,0:T(8,128)(2,1)S(1)}, u32[]{:S(2)}, u32[]{:S(2)}) collective-permute-start(bf16[2,208,896]{2,1,0:T(8,128)(2,1)S(1)} %get-tuple-element.259), channel_id=1, source_target_pairs={{0,8},{4,12},{8,0},{12,4},{16,24},{20,28},{24,16},{28,20},{1,9},{5... | collective-permute-start | bytes 2236424 | tf_op jit(solution)/shard_map/ppermute | solution.py:1051
  766.5 22.5 %collective-permute-start.53 = (bf16[208,896]{1,0:T(8,128)(2,1)S(1)}, bf16[208,896]{1,0:T(8,128)(2,1)S(1)}, u32[]{:S(2)}, u32[]{:S(2)}) collective-permute-start(bf16[208,896]{1,0:T(8,128)(2,1)S(1)} %get-tuple-element.276), channel_id=1, source_target_pairs={{0,3},{3,0},{4,7},{7,4},{8,11},{11,8},{12,15},{15,12},{16,19},{19,... | collective-permute-start | bytes 1118216 | tf_op jit(solution)/shard_map/ppermute | solution.py:1020
  (69 other events, 1027.8 us)
Sparse Core Ops, SparseCore 0:
  143.4 73.3 all-gather.2

commit v9 on v8

--- a/solution.py
+++ b/solution.py
@@ -63,16 +63,17 @@
     return values * cosine - pltpu.roll(values, HEAD_DIM // 2, 1) * sine
 
 
-SLOTS = range(4)
 PIECES = (
-    tuple((0, slot) for slot in SLOTS),
-    tuple((2, slot) for slot in SLOTS),
-    tuple((4, slot) for slot in SLOTS),
-    ((6, 0), (6, 1)),
+    ((0, 0), (2, 0), (4, 0), (6, 0)),
+    ((1, 0), (3, 0), (5, 0), (7, 0)),
+    ((0, 1), (0, 2), (0, 3)),
+    ((2, 1), (2, 2), (2, 3)),
+    ((4, 1), (4, 2), (4, 3)),
+    ((6, 1),),
     ((6, 2), (6, 3)),
-    tuple((1, slot) for slot in SLOTS),
-    tuple((flip_bits, slot) for flip_bits in (3, 5) for slot in SLOTS),
-    ((7, 0), (7, 1)),
+    ((1, 1), (1, 2), (1, 3)),
+    ((3, 1), (3, 2), (3, 3), (5, 1), (5, 2), (5, 3)),
+    ((7, 1),),
     ((7, 2), (7, 3)),
 )
 EXTRA = 16
@@ -695,28 +696,46 @@
     )(rows, grads, *[acts] * len(slots))
 
 
-def combine_kernel(local, chosen, *rest):
-    rows, out = rest[:local], rest[local]
+SHARE_ROWS = 32
+
+
+def combine_kernel(local, info, chosen, *rest):
+    rows, dots, out = rest[:local], rest[local:-1], rest[-1]
     both = jnp.concatenate([ref[0] for ref in rows], axis=0)
-    out[0] = tn(chosen[0], both).astype(LOW)
-
-
-def combine(chosen, rows, first, step):
+    out[0, :TOK_DEV] = tn(chosen[0], both).astype(LOW)
+    if dots:
+        capacity = rows[0].shape[1]
+        row = lax.broadcasted_iota(jnp.int32, (SHARE_ROWS, D), 0)
+        values = jnp.zeros((SHARE_ROWS, D), WIDE)
+        for e in range(local):
+            picked = chosen[0, e * capacity : (e + 1) * capacity].astype(WIDE)
+            high, low = split(jnp.sum(picked * dots[e][0], axis=0, keepdims=True))
+            pieces = [high.astype(WIDE), low.astype(WIDE)]
+            pieces.append(jnp.zeros((1, D - 2 * TOK_DEV), WIDE))
+            line = jnp.concatenate(pieces, axis=1)
+            values = jnp.where(row == info[0] * local + e, line, values)
+        out[0, TOK_DEV:] = values.astype(LOW)
+
+
+def combine(info, chosen, rows, first, step, dots=()):
     count, capacity, _ = rows[0].shape
     number = (count - first + step - 1) // step
+    height = TOK_DEV + (SHARE_ROWS if dots else 0)
     return pl.pallas_call(
         functools.partial(combine_kernel, len(rows)),
         grid=(number,),
-        out_shape=jax.ShapeDtypeStruct((number, TOK_DEV, D), LOW),
+        out_shape=jax.ShapeDtypeStruct((number, height, D), LOW),
         in_specs=[
-            pl.BlockSpec((1,) + chosen.shape[1:], lambda i: (first + step * i, 0, 0))
+            SMEM,
+            pl.BlockSpec((1,) + chosen.shape[1:], lambda i: (first + step * i, 0, 0)),
         ]
-        + [pl.BlockSpec((1, capacity, D), lambda i: (first + step * i, 0, 0))] * len(rows),
-        out_specs=pl.BlockSpec((1, TOK_DEV, D), lambda i: (i, 0, 0)),
+        + [pl.BlockSpec((1, capacity, D), lambda i: (first + step * i, 0, 0))] * len(rows)
+        + [pl.BlockSpec((1, capacity, 1), lambda i: (first + step * i, 0, 0))] * len(dots),
+        out_specs=pl.BlockSpec((1, height, D), lambda i: (i, 0, 0)),
         compiler_params=params(),
         cost_estimate=LITTLE,
         name="combine",
-    )(chosen, *rows)
+    )(info, chosen, *rows, *dots)
 
 
 def split(values):
@@ -748,9 +767,10 @@
 
 
 def branch_back_kernel(
-    parts, info, residual, normed, cotangent, routes, grad_shares, router, gain, *rest
+    parts, info, residual, normed, cotangent, routes, router, gain, *rest
 ):
     sums, rest = rest[:parts], rest[parts:]
+    experts = router.shape[0]
     count = len(rest) - 7
     refs = rest[:count]
     grad_residual, grad_branch, grad_heads, grad_gain, grad_router, weight, sem = rest[count:]
@@ -760,16 +780,20 @@
         copies = weight_copies(info, refs, weight, sem, D // QUARTERS + 128, D // QUARTERS)
         run_all(copies)
         logits = nt(router[...], normed[...])
-        high, low = split(router_back(logits, routes[...], grad_shares[...]))
+        if parts == 2:
+            back_sum, grad_shares = sums[0][...], sums[1][...]
+        else:
+            values = [ref[...].astype(WIDE) for ref in sums]
+            upper = values[0] + values[1] + values[2]
+            lower = values[3] + values[4] + values[5]
+            last = lower.shape[0] - SHARE_ROWS
+            shares = lower[last : last + experts]
+            grad_shares = shares[:, :TOK_DEV] + shares[:, TOK_DEV : 2 * TOK_DEV]
+            back_sum = jnp.concatenate([upper, lower[:last]], axis=0)
+        high, low = split(router_back(logits, routes[...], grad_shares))
         grad_router[...] = nn(high, normed[...]) + nn(low, normed[...])
         grad_normed = tn(high, router[...]) + tn(low, router[...])
-        if parts == 1:
-            grad_normed += sums[0][...]
-        else:
-            values = [ref[...].astype(WIDE) for ref in sums]
-            grad_normed += jnp.concatenate(
-                [values[0] + values[1] + values[2], values[3] + values[4] + values[5]], axis=0
-            )
+        grad_normed += back_sum
         grad_values, gain_grad = norm_back(residual[...], gain[...], grad_normed)
         grad_gain[...] = gain_grad
         total = cotangent[...].astype(WIDE) + grad_values
@@ -781,7 +805,7 @@
     grad_heads[...] = nt(grad_branch[...], weight[at, :]).astype(LOW)
 
 
-def branch_back(info, residual, normed, sums, cotangent, routes, grad_shares, router, gain, refs):
+def branch_back(info, residual, normed, sums, cotangent, routes, router, gain, refs):
     full = (TOK_DEV, D)
     total = router.shape[0]
     return pl.pallas_call(
@@ -796,7 +820,7 @@
         ),
         in_specs=[SMEM]
         + [whole(full)] * 3
-        + [whole((TOP, TOK_DEV)), whole((total, TOK_DEV)), whole((total, D)), whole((1, D))]
+        + [whole((TOP, TOK_DEV)), whole((total, D)), whole((1, D))]
         + [whole(part.shape) for part in sums]
         + [ANY] * len(refs),
         out_specs=(
@@ -810,7 +834,7 @@
         compiler_params=params(),
         cost_estimate=LITTLE,
         name="experts_norm_back",
-    )(info, residual, normed, cotangent, routes, grad_shares, router, gain, *sums, *refs)
+    )(info, residual, normed, cotangent, routes, router, gain, *sums, *refs)
 
 
 def join_grads_kernel(info, own_grad, source_grad, arrived, cosine, sine, out):
@@ -1141,6 +1165,14 @@
         for expert in range(local_experts)
     ]
     nears, seconds, fars = ([], [], [])
+    routes_all = lax.all_gather(routes.T, "rows", axis=0)
+    if fast:
+        near_rows = row_place ^ jnp.arange(row_count, dtype=jnp.int32)
+    else:
+        near_rows = jnp.arange(row_count, dtype=jnp.int32)
+    chosen, place_rows = tables(
+        near_rows, info, routes_all, capacity, local_experts, expert_total
+    )
     if fast:
         wide = packed.shape[1]
         gains = jnp.concatenate([attention_gain, experts_gain])[None, :]
@@ -1149,15 +1181,14 @@
                 packed,
                 jnp.pad(router_weight.T, ((0, 0), (0, wide - depth))),
                 jnp.pad(gains, ((0, 0), (0, wide - 2 * gain_part))),
-                jnp.pad(routes.T.astype(LOW), ((0, 0), (0, wide - TOK_DEV))),
-                jnp.zeros((EXTRA - router_part - 1 - TOP, wide), LOW),
+                jnp.zeros((EXTRA - router_part - 1, wide), LOW),
             ],
             axis=0,
         )
         packed_near = send_near(packed)
         packed_far = send_far(packed)
         packed_second = send_second(packed, packed_near)
-        own = jnp.stack(slot_list(packed, packed_near, packed_second, packed_far))
+        slots = slot_list(packed, packed_near, packed_second, packed_far)
 
         def gather_expert(*earlier):
             expert_at = len(nears)
@@ -1167,24 +1198,23 @@
             seconds.append(send_second(block, nears[expert_at]))
 
         gather_expert(*packed_near)
-        own = after(own, info, cosine, sine)
-        beside, across = flip(own, 2), flip(own, 4)
-        own_in = flip(own, 1)
-        beside, across = after((beside, across), own_in, *nears[0])
-        corner = [flip(beside[:2], 4), flip(across[2:], 2)]
+        first = after(packed[None], routes_all)
+        first_four = jnp.concatenate([first] + [flip(first, bits) for bits in (2, 4, 6)], axis=0)
+        others = jnp.stack(slots[1:])
+        others = after(others, info, cosine, sine, first_four)
+        beside, across = flip(others, 2), flip(others, 4)
+        first_in, others_in = flip(first_four, 1), flip(others, 1)
+        beside, across = after((beside, across), first_in, others_in, chosen, *nears[0])
+        corner = [flip(beside[:1], 4), flip(across[1:], 2)]
         pair_in = flip(jnp.concatenate([beside, across], axis=0), 1)
         corner_in = [flip(piece, 1) for piece in corner]
-        pieces = [own, beside, across, *corner, own_in, pair_in, *corner_in]
+        pieces = [first_four, first_in, others, beside, across, *corner]
+        pieces += [others_in, pair_in, *corner_in]
         query_refs = pair_refs = out_refs = pieces
         extra_rows = extras(info, pieces)
         router_all = extra_rows[:, :router_part, :depth]
         attention_scale = extra_rows[:, router_part, :gain_part]
         experts_scale = extra_rows[:, router_part, gain_part : 2 * gain_part]
-        routes_all = lax.dynamic_index_in_dim(
-            extra_rows.reshape(row_count, col_count, EXTRA, -1), col_place, 1, keepdims=False
-        )
-        routes_all = routes_all[:, router_part + 1 : router_part + 1 + TOP, :TOK_DEV]
-        routes_all = routes_all.astype(jnp.int32)
     else:
         packed_all = lax.all_gather(lax.all_gather(packed, "cols", axis=0), "rows", axis=0)
 
@@ -1204,7 +1234,6 @@
             ).reshape(D, -1)
         ]
         out_refs = [unpack(key_at + 2 * key_part, query_part)]
-        routes_all = lax.all_gather(routes.T, "rows", axis=0)
         axes = ("rows", "cols")
         router_all = jnp.swapaxes(lax.all_gather(router_weight, axes, axis=0), 1, 2)
         attention_scale = lax.all_gather(attention_gain, axes, axis=0)
@@ -1220,20 +1249,13 @@
         router_all.reshape(row_count, col_count, router_part, depth), (1, 2, 0, 3)
     ).reshape(expert_total, D)
     router_cols = router_rows.T
-    if fast:
-        near_rows = row_place ^ jnp.arange(row_count, dtype=jnp.int32)
-    else:
-        near_rows = jnp.arange(row_count, dtype=jnp.int32)
-    chosen, place_rows = tables(
-        near_rows, info, routes_all, capacity, local_experts, expert_total
-    )
-    tokens_in = after(tokens, seconds[0]) if fast else tokens
-    normed, own_pair = key_value(info, tokens_in, attention_scale, cosine, sine, pair_refs)
-    grad_in = after(cotangent, normed) if fast else cotangent
+    normed, own_pair = key_value(info, tokens, attention_scale, cosine, sine, pair_refs)
+    grad_in = after(cotangent, *corner) if fast else cotangent
     grad_all = lax.all_gather(grad_in, "rows", axis=0)
     pairs = [(i + 1, i) for i in range(0, col_count, 2)]
     partner = lax.ppermute(own_pair, "cols", pairs)
-    queries = query(info, normed, cosine, sine, query_refs)
+    normed_in = after(normed, seconds[0]) if fast else normed
+    queries = query(info, normed_in, cosine, sine, query_refs)
     if fast:
         fars.append(send_far(after(shard_blocks[0], seconds[0], partner, queries)))
     heads = attention(info, queries, own_pair, partner)
@@ -1299,7 +1321,7 @@
         if fast:
             if e == 1:
                 back_rows = after(back_rows, marks[0][0])
-                got = flip(combine(chosen, back_rows, 1, 2), 1)
+                got = flip(combine(info, chosen, back_rows, 1, 2, gate_dots), 1)
                 acts = after(acts, got)
             second, fourth = expert_grads(acts, token_rows[e], grad_row, (1, 3))
             if e == 0:
@@ -1313,36 +1335,29 @@
                 lax.psum_scatter(jnp.stack(slots), "cols", scatter_dimension=0).astype(WIDE)
             )
 
-    spread_dots = spread(place_rows, gate_dots)
     if fast:
-        spread_dots = jnp.take(spread_dots, near_rows, axis=0)
-    grad_shares = lax.all_to_all(spread_dots, "rows", split_axis=0, concat_axis=0, tiled=True)
-    grad_shares = grad_shares.reshape(expert_total, TOK_DEV)
-    if fast:
-        back_keep = combine(chosen, back_rows, 0, 2)
+        back_keep = combine(info, chosen, back_rows, 0, 2, gate_dots)
+        back_first = chips_first(back_keep, got)
         sent_second = reduce_second(grad_slots[0][2], grad_slots[0][3], marks[0][0])
+        back_parts = chips_second(back_keep, got, *send_chips(back_first))
+        out_rows = [after(a, back_parts[1], back_parts[4]) for a in out_rows]
+        out_got = flip(combine(info, chosen, out_rows, 1, 2), 1)
+        out_keep = combine(info, chosen, out_rows, 0, 2)
         far_back = lax.ppermute(
-            after(grad_slots[0][3], *sent_second, *grad_slots[1], spread_dots), "cols", FAR
+            after(grad_slots[0][3], *sent_second, out_keep), "cols", FAR
         )
         reduced.append((grad_slots[0][0], (marks[0][0], far_back), sent_second))
-        back_first = chips_first(back_keep, got)
-        back_parts = chips_second(back_keep, got, *send_chips(back_first))
-        out_rows = [after(a, *back_first) for a in out_rows]
-        out_got = flip(combine(chosen, out_rows, 1, 2), 1)
-        out_keep = combine(chosen, out_rows, 0, 2)
-        relay, _ = reduce_first(
-            after(grad_slots[1][1], far_back, back_parts[2], back_parts[5]), fourth, chain=True
-        )
-        marks.append((relay,))
-        grad_shares = after(grad_shares, own_slot, third, out_keep, out_got, far_back)
+        back_parts = after(back_parts, out_keep, out_got)
     else:
+        spread_dots = spread(place_rows, gate_dots)
+        grad_shares = lax.all_to_all(spread_dots, "rows", split_axis=0, concat_axis=0, tiled=True)
 
         def summed(rows):
-            part = combine(chosen, rows, 0, 1)
-            return (lax.psum_scatter(part, "rows", scatter_dimension=0).astype(WIDE),)
-
-        back_parts = summed(back_rows)
-        mixture = summed(out_rows)
+            part = combine(info, chosen, rows, 0, 1)
+            return lax.psum_scatter(part, "rows", scatter_dimension=0).astype(WIDE)
+
+        back_parts = (summed(back_rows), grad_shares.reshape(expert_total, TOK_DEV))
+        mixture = (summed(out_rows),)
 
     grad_residual, grad_branch, grad_heads, experts_gain_grad, router_grad = branch_back(
         info,
@@ -1351,12 +1366,13 @@
         back_parts,
         cotangent,
         routes.T,
-        grad_shares,
         router_rows,
         experts_scale,
         out_refs,
     )
     if fast:
+        relay, _ = reduce_first(after(grad_slots[1][1], far_back, grad_heads), fourth, chain=True)
+        marks.append((relay,))
         out_first = chips_first(out_keep, out_got)
         out_flips = send_chips(out_first)
         grad_heads = after(grad_heads, *out_first)
@@ -1379,7 +1395,7 @@
     arrived = lax.ppermute(source_grad.astype(LOW), "cols", [(j, i) for i, j in pairs])
     grad_pair = join_grads(info, own_grad, source_grad, arrived, cosine, sine)
     if fast:
-        grad_branch = after(grad_branch, marks[1][0], *out_flips)
+        grad_branch = after(grad_branch, *out_flips)
         keep, send = weight_grads(
             info,
             [normed, heads],
@@ -1387,6 +1403,7 @@
             ((0, 2, query_part), (0, 3, 2 * key_part), (1, 4, query_part)),
             extra,
         )
+        send = after(send, marks[1][0])
         sent = flip(send, 1)
         sent_second = reduce_second(grad_slots[1][2], grad_slots[1][3], marks[1][0])
         grad_pair = after(grad_pair, keep)
@@ -1395,14 +1412,18 @@
     )
 
     if fast:
-        far_back = lax.ppermute(after(grad_slots[1][3], *sent_second, tokens_grad), "cols", FAR)
+        sent_first = chips_first(keep, sent)
+        sent_chips = send_chips(sent_first)
+        far_back = lax.ppermute(
+            after(grad_slots[1][3], *sent_second, tokens_grad, *sent_first), "cols", FAR
+        )
         reduced.append((grad_slots[1][0], (marks[1][0], far_back), sent_second))
         mixture = chips_second(out_keep, out_got, *out_flips)
-        sent_chips = send_chips(chips_first(keep, sent))
         slots = sum_parts(chips_second(keep, sent, *sent_chips))
         width = query_part + 2 * key_part
+        own_slots = [packed, *others]
         gain_sums = sum(
-            jnp.sum(own[i, :depth, :width].astype(WIDE) * slots[i, :depth, :width], axis=1)
+            jnp.sum(own_slots[i][:depth, :width].astype(WIDE) * slots[i, :depth, :width], axis=1)
             for i in range(4)
         )
         own_gains = lax.dynamic_slice_in_dim(attention_scale[0], row_place * depth, depth, 0)

time: 816 us -> 818 us (level)
  waiting for transfers between devices: 223 us -> 264 us
  blocking collectives: 34.7 us -> 12.4 us
    ppermute x31 -> x35, waiting for transfers between devices: 73.9 us -> 122 us  [flip(): return lax.ppermute(block, 'rows', [(i, i ^ bit) for i in range(count)])]
    all_to_all x1 -> x0, blocking collectives: 34.7 us -> none  [on_device(): lax.all_to_all(spread_dots, 'rows', split_axis=0, concat_axis=0, tiled=True)]
    ppermute x3, waiting for transfers between devices: 15.1 us -> 37 us  [reduce_second(): lax.ppermute(downward_load, 'cols', DOWN)]
    ppermute x2, waiting for transfers between devices: 27.3 us -> 7.57 us  [the longest x1 7.57 us: on_device(): lax.ppermute(after(grad_slots[1][3], *sent_second, tokens_grad, *sent_fir...]
    ppermute x3, waiting for transfers between devices: 22.2 us -> 4.58 us  [reduce_second(): lax.ppermute(upward_load, 'cols', UP)]
    ppermute x6, waiting for transfers between devices: 30.5 us -> 13.4 us  [send_near(): return (lax.ppermute(block, 'cols', DOWN), lax.ppermute(block, 'cols', UP))]
    ppermute x1, waiting for transfers between devices: 3.05 us -> 18.5 us  [on_device(): lax.ppermute(source_grad.astype(LOW), 'cols', [(j, i) for i, j in pairs])]
    all_gather x0 -> x1, blocking collectives: none -> 12.4 us  [on_device(): routes_all = lax.all_gather(routes.T, 'rows', axis=0)]
  transfers between devices with their start and end apart: 58 -> 62, of which waited for: 28 -> 33; matrix products, arithmetic and copies ran while one was open for 11% -> 11% of each run, Pallas kernels for 32% -> 34%
where the time goes in v9:
time: 818 us; the launch traced here: 806 us
  Pallas kernels  293 us (36%)
  waiting for transfers between devices  264 us (32%)
  starting transfers between devices  101 us (12%)
  other arithmetic  71 us (9%)
  local copies, waits for them, and re-layouts  49.7 us (6%)
  between operations  15.6 us (2%)
  blocking collectives  12.4 us (2%)
    ppermute x35, waiting for transfers between devices, flip(): return lax.ppermute(block, 'rows', [(i, i ^ bit) for i in range(count)])  122 us
    pallas_call x2, Pallas kernels, expert(): pl.pallas_call(functools.partial(expert_kernel, slots), grid=(height // E...  60.3 us
    pallas_call x8, Pallas kernels, dispatch(): pl.pallas_call(functools.partial(dispatch_kernel, local), grid_spec=pltpu...  41.2 us
    pallas_call x4, Pallas kernels, expert_grads(): pl.pallas_call(functools.partial(expert_grads_kernel, slots), grid=(D //...  39.4 us
    ppermute x3, waiting for transfers between devices, reduce_second(): lax.ppermute(downward_load, 'cols', DOWN)  37 us
    ppermute x3, waiting for transfers between devices, send_second(): return lax.ppermute(payload, 'cols', [(3, 1), (1, 0), (0, 2), (2, 3)])  32.5 us
    pallas_call x4, Pallas kernels, combine(): pl.pallas_call(functools.partial(combine_kernel, len(rows)), grid=(number...  31.1 us
    ppermute x35, starting transfers between devices, flip(): return lax.ppermute(block, 'rows', [(i, i ^ bit) for i in range(count)])  25.7 us
  transfers between devices with their start and end apart: 62, of which 33 were waited for; matrix products, arithmetic and copies ran while one was open for 11% of the time, Pallas kernels for 34%

profile of v9, /device:TPU:0, one launch (start us, length us, event | category | flops | bytes accessed | tf_op | source)
XLA Modules:
  0.0 805.9 jit_solution(3000847468395799787)
XLA Ops:
  9.0 12.4 %all-gather.2.routes = s32[8,4,512]{2,1,0:T(4,128)} all-gather(s32[1,4,512]{2,1,0:T(4,128)} %bitcast.202), channel_id=2, replica_groups=mesh['rows'=8,'cols'=4] {'rows'}, dimensions={0}, use_global_device_ids=true | all-gather | bytes 73728 | tf_op jit(solution)/shard_map/all_gather | solution.py:1168
  32.3 6.6 collective-permute-start.7
  46.0 7.2 collective-permute-done.7
  70.9 6.2 route_tables.1
  77.0 18.3 %collective-permute-done.9.rest_4_.rest_10_.rest_15_ = bf16[3,208,896]{2,1,0:T(8,128)(2,1)S(1)} collective-permute-done((bf16[3,208,896]{2,1,0:T(8,128)(2,1)S(1)}, bf16[3,208,896]{2,1,0:T(8,128)(2,1)S(1)}, u32[]{:S(2)}, u32[]{:S(2)}) %collective-permute-start.9) | collective-permute-done | bytes 1118240 | tf_op jit(solution)/shard_map/ppermute | solution.py:1075
  96.3 8.8 %collective-permute-done.12.rest_3_ = bf16[576,1536]{1,0:T(8,128)(2,1)S(1)} collective-permute-done((bf16[576,1536]{1,0:T(8,128)(2,1)S(1)}, bf16[576,1536]{1,0:T(8,128)(2,1)S(1)}, u32[]{:S(2)}, u32[]{:S(2)}) %collective-permute-start.12) | collective-permute-done | bytes 1769504 | tf_op jit(solution)/shard_map/ppermute | solution.py:1016
  111.9 9.0 %collective-permute-done.13.rest_5_.rest_11_.rest_16_ = bf16[1,208,896]{2,1,0:T(8,128)(2,1)S(1)} collective-permute-done((bf16[1,208,896]{2,1,0:T(8,128)(2,1)S(1)}, bf16[1,208,896]{2,1,0:T(8,128)(2,1)S(1)}, u32[]{:S(2)}, u32[]{:S(2)}) %collective-permute-start.13) | collective-permute-done | bytes 372768 | tf_op jit(solution)/shard_map/ppermute | solution.py:1075
  121.0 6.9 collective-permute-done.14.rest_6_.rest_12_.rest_17_
  148.8 25.5 %collective-permute-done.18.rest_1_ = bf16[576,1536]{1,0:T(8,128)(2,1)} collective-permute-done((bf16[576,1536]{1,0:T(8,128)(2,1)}, bf16[576,1536]{1,0:T(8,128)(2,1)}, u32[]{:S(2)}, u32[]{:S(2)}) %collective-permute-start.18) | collective-permute-done | bytes 1769504 | tf_op jit(solution)/shard_map/ppermute | solution.py:1027
  174.3 8.9 %query_projection.1.queries = bf16[512,1536]{1,0:T(8,128)(2,1)} custom-call(s32[16]{0:T(128)} %concatenate.45.info, bf16[512,1536]{1,0:T(8,128)(2,1)} %get-tuple-element.123.normed.rest_0_, f32[512,128]{1,0:T(8,128)} %get-tuple-element.321.cosine, f32[512,128]{1,0:T(8,128)} %get-tuple-element.322.sine, ...), custom_call_target="tpu_custom_call" | custom-call | flops 1 | bytes 1 | tf_op jit(solution)/shard_map/query_projection/pallas_call | solution.py:193
  187.9 11.3 %tree_attention.1.heads.rest_1_ = bf16[512,1536]{1,0:T(8,128)(2,1)} custom-call(s32[16]{0:T(128)} %concatenate.45.info, bf16[512,1536]{1,0:T(8,128)(2,1)} %query_projection.1.queries, bf16[512,512]{1,0:T(8,128)(2,1)} %get-tuple-element.124.own, bf16[512,512]{1,0:T(8,128)(2,1)} %copy-done.33), custom_call_target="tpu_custom_call" | custom-call | flops 1 | bytes 1 | tf_op jit(solution)/shard_map/tree_attention/pallas_call | solution.py:275
  199.4 11.4 %out_projection.1 = (f32[512,1536]{1,0:T(8,128)}, bf16[512,1536]{1,0:T(8,128)(2,1)}) custom-call(s32[16]{0:T(128)} %concatenate.45.info, bf16[512,1536]{1,0:T(8,128)(2,1)} %tree_attention.1.heads.rest_1_, bf16[512,1536]{1,0:T(8,128)(2,1)} %tokens.5, f32[1,1536]{1,0:T(1,128)} %reshape.417.gain, ...), custom_call_target="tpu_custom_call" | custom-call | flops 1 | bytes 1 | tf_op jit(solution)/shard_map/out_projection/pallas_call | solution.py:387
  210.7 14.9 %collective-permute-done.23.rest_4_ = bf16[576,1536]{1,0:T(8,128)(2,1)} collective-permute-done((bf16[576,1536]{1,0:T(8,128)(2,1)S(1)}, bf16[576,1536]{1,0:T(8,128)(2,1)}, u32[]{:S(2)}, u32[]{:S(2)}) %collective-permute-start.23) | collective-permute-done | bytes 1769504 | tf_op jit(solution)/shard_map/ppermute | solution.py:1020
  236.8 5.2 dispatch.8
  242.0 5.1 dispatch.9
  247.2 13.1 %pick_rows.1 = (bf16[8,160,1536]{2,1,0:T(8,128)(2,1)}, bf16[8,160,1536]{2,1,0:T(8,128)(2,1)}) custom-call(s32[8]{0:T(128)} %iota_xor_fusion.order.near, bf16[8,320,512]{2,1,0:T(8,128)(2,1)} %get-tuple-element.118.chosen, bf16[8,512,1536]{2,1,0:T(8,128)(2,1)} %bitcast.188), custom_call_target="tpu_custom_call" | custom-call | flops 1 | bytes 1 | tf_op jit(solution)/shard_map/pick_rows/pallas_call | solution.py:463
  260.2 5.6 collective-permute-done.21.rows
  286.7 5.2 dispatch.11
  305.9 5.2 dispatch.14
  321.3 5.3 collective-permute-start.32
  326.6 30.2 %expert.2 = (bf16[1280,1536]{1,0:T(8,128)(2,1)}, bf16[1280,1536]{1,0:T(8,128)(2,1)}, bf16[1280,1536]{1,0:T(8,128)(2,1)}, bf16[4,576,1280]{2,1,0:T(8,128)(2,1)}, f32[1280,1]{1,0:T(8,128)}) custom-call(s32[16]{0:T(128)} %concatenate.45.info, bf16[1280,1536]{1,0:T(8,128)(2,1)} %bitcast.166, bf16[1280,1536]{1,0:T(8,128)(2,1)} %bitcast.192, f32[1280,1]{1,0:T(8,128)} %bitcast.172, ...), custom_call_target="tpu_custom_call" | custom-call | flops 1 | bytes 1 | tf_op jit(solution)/shard_map/expert/pallas_call | solution.py:658
  356.9 9.8 %expert_gradients.4 = (bf16[576,1536]{1,0:T(8,128)(2,1)}, bf16[576,1536]{1,0:T(8,128)(2,1)}) custom-call(bf16[1280,1536]{1,0:T(8,128)(2,1)} %bitcast.167, bf16[1280,1536]{1,0:T(8,128)(2,1)} %get-tuple-element.174.grads, bf16[4,576,1280]{2,1,0:T(8,128)(2,1)} %get-tuple-element.175.rest_0_.rest_1_, bf16[4,576,1280]{2,1,0:T(8,128)(2,1)} %get-tuple-element.175.rest_0_.rest_1_), custom_call_target="tpu_custom_call" | custom-call | flops 1 | bytes 1 | tf_op jit(solution)/shard_map/expert_gradients/pallas_call | solution.py:686
  367.2 9.8 %expert_gradients.5 = (bf16[576,1536]{1,0:T(8,128)(2,1)}, bf16[576,1536]{1,0:T(8,128)(2,1)}) custom-call(bf16[1280,1536]{1,0:T(8,128)(2,1)} %bitcast.168, bf16[1280,1536]{1,0:T(8,128)(2,1)} %get-tuple-element.174.grads, bf16[4,576,1280]{2,1,0:T(8,128)(2,1)} %get-tuple-element.175.rest_0_.rest_1_, bf16[4,576,1280]{2,1,0:T(8,128)(2,1)} %get-tuple-element.175.rest_0_.rest_1_), custom_call_target="tpu_custom_call" | custom-call | flops 1 | bytes 1 | tf_op jit(solution)/shard_map/expert_gradients/pallas_call | solution.py:686
  378.2 30.1 %expert.3 = (bf16[1280,1536]{1,0:T(8,128)(2,1)}, bf16[1280,1536]{1,0:T(8,128)(2,1)}, bf16[1280,1536]{1,0:T(8,128)(2,1)}, bf16[4,576,1280]{2,1,0:T(8,128)(2,1)}, f32[1280,1]{1,0:T(8,128)}) custom-call(s32[16]{0:T(128)} %concatenate.45.info, bf16[1280,1536]{1,0:T(8,128)(2,1)} %bitcast.169, bf16[1280,1536]{1,0:T(8,128)(2,1)} %bitcast.191, f32[1280,1]{1,0:T(8,128)} %bitcast.173, ...), custom_call_target="tpu_custom_call" | custom-call | flops 1 | bytes 1 | tf_op jit(solution)/shard_map/expert/pallas_call | solution.py:658
  408.3 8.4 %combine.5 = bf16[4,544,1536]{2,1,0:T(8,128)(2,1)} custom-call(s32[16]{0:T(128)} %concatenate.45.info, bf16[8,320,512]{2,1,0:T(8,128)(2,1)} %get-tuple-element.118.chosen, bf16[8,160,1536]{2,1,0:T(8,128)(2,1)} %bitcast.184, bf16[8,160,1536]{2,1,0:T(8,128)(2,1)} %bitcast.186, f32[8,160,1]{2,1,0:T(8,128)} %bitcast.193, f32[8,160,1]{2,1,0:T(8,128)} %bitcast.195), custom_call_target="tpu_custom_call" | custom-call | flops 1 | bytes 1 | tf_op jit(solution)/shard_map/combine/pallas_call | solution.py:724
  416.7 7.7 combine.4
  434.0 36.3 %collective-permute-done.35 = bf16[2,272,1536]{2,1,0:T(8,128)(2,1)S(1)} collective-permute-done((bf16[2,272,1536]{2,1,0:T(8,128)(2,1)S(1)}, bf16[2,272,1536]{2,1,0:T(8,128)(2,1)S(1)}, u32[]{:S(2)}, u32[]{:S(2)}) %collective-permute-start.35) | collective-permute-done | bytes 1671200 | tf_op jit(solution)/shard_map/ppermute | solution.py:1075
  472.8 7.6 combine.7
  484.7 6.1 collective-permute-start.45
  490.8 7.5 combine.6
  498.2 28.4 %collective-permute-done.46 = bf16[576,1536]{1,0:T(8,128)(2,1)} collective-permute-done((bf16[576,1536]{1,0:T(8,128)(2,1)}, bf16[576,1536]{1,0:T(8,128)(2,1)}, u32[]{:S(2)}, u32[]{:S(2)}) %collective-permute-start.46) | collective-permute-done | bytes 1769504 | tf_op jit(solution)/shard_map/ppermute | solution.py:1056
  528.1 8.0 collective-permute-start.47
  543.2 9.8 %expert_gradients.6 = (bf16[576,1536]{1,0:T(8,128)(2,1)}, bf16[576,1536]{1,0:T(8,128)(2,1)}) custom-call(bf16[1280,1536]{1,0:T(8,128)(2,1)} %bitcast.170, bf16[1280,1536]{1,0:T(8,128)(2,1)} %get-tuple-element.209.grads, bf16[4,576,1280]{2,1,0:T(8,128)(2,1)} %get-tuple-element.211.rest_0_.rest_1_, bf16[4,576,1280]{2,1,0:T(8,128)(2,1)} %get-tuple-element.211.rest_0_.rest_1_), custom_call_target="tpu_custom_call" | custom-call | flops 1 | bytes 1 | tf_op jit(solution)/shard_map/expert_gradients/pallas_call | solution.py:686
  552.9 8.0 collective-permute-done.43.rest_5_
  562.5 14.3 %experts_norm_back.1 = (f32[512,1536]{1,0:T(8,128)}, bf16[512,1536]{1,0:T(8,128)(2,1)}, bf16[512,1536]{1,0:T(8,128)(2,1)}, f32[1,1536]{1,0:T(1,128)}, f32[16,1536]{1,0:T(8,128)}) custom-call(s32[16]{0:T(128)} %concatenate.45.info, f32[512,1536]{1,0:T(8,128)} %get-tuple-element.125.residual, bf16[512,1536]{1,0:T(8,128)(2,1)} %get-tuple-element.126.rows.normed, ...), custom_call_target="tpu_custom_call" | custom-call | flops 1 | bytes 1 | tf_op jit(solution)/shard_map/experts_norm_back/pallas_call | solution.py:811
  584.3 15.4 %tree_attention_back.1 = (bf16[512,1536]{1,0:T(8,128)(2,1)}, f32[512,512]{1,0:T(8,128)}, f32[512,512]{1,0:T(8,128)}) custom-call(s32[16]{0:T(128)} %concatenate.45.info, bf16[512,1536]{1,0:T(8,128)(2,1)} %query_projection.1.queries, bf16[512,512]{1,0:T(8,128)(2,1)} %get-tuple-element.124.own, bf16[512,512]{1,0:T(8,128)(2,1)} %copy-done.33, ...), custom_call_target="tpu_custom_call" | custom-call | flops 1 | bytes 1 | tf_op jit(solution)/shard_map/tree_attention_back/pallas_call | solution.py:336
  606.1 18.5 %collective-permute-done.44.arrived = bf16[512,512]{1,0:T(8,128)(2,1)S(1)} collective-permute-done((bf16[512,512]{1,0:T(8,128)(2,1)S(1)}, bf16[512,512]{1,0:T(8,128)(2,1)S(1)}, u32[]{:S(2)}, u32[]{:S(2)}) %collective-permute-start.44) | collective-permute-done | bytes 524320 | tf_op jit(solution)/shard_map/ppermute | solution.py:1395
  628.5 15.9 %weight_gradients.1 = (bf16[4,4,208,896]{3,2,1,0:T(8,128)(2,1)}, bf16[4,4,208,896]{3,2,1,0:T(8,128)(2,1)}) custom-call(s32[16]{0:T(128)} %concatenate.45.info, bf16[512,1536]{1,0:T(8,128)(2,1)} %get-tuple-element.123.normed.rest_0_, bf16[512,1536]{1,0:T(8,128)(2,1)} %tree_attention.1.heads.rest_1_, bf16[512,1536]{1,0:T(8,128)(2,1)} %get-tuple-element.197.rest_2_.grad_query, ...), custom_call_target="tpu_custom_call" | custom-call | flops 1 | bytes 1 | tf_op jit(solution)/shard_map/weight_gradients/pallas_call | solution.py:963
  647.0 10.0 %expert_gradients.7 = (bf16[576,1536]{1,0:T(8,128)(2,1)}, bf16[576,1536]{1,0:T(8,128)(2,1)}) custom-call(bf16[1280,1536]{1,0:T(8,128)(2,1)} %bitcast.171, bf16[1280,1536]{1,0:T(8,128)(2,1)} %get-tuple-element.209.grads, bf16[4,576,1280]{2,1,0:T(8,128)(2,1)} %get-tuple-element.211.rest_0_.rest_1_, bf16[4,576,1280]{2,1,0:T(8,128)(2,1)} %get-tuple-element.211.rest_0_.rest_1_), custom_call_target="tpu_custom_call" | custom-call | flops 1 | bytes 1 | tf_op jit(solution)/shard_map/expert_gradients/pallas_call | solution.py:686
  663.4 6.7 collective-permute-start.58
  670.1 5.6 fusion.5
  681.3 13.3 %token_gradient.1 = (bf16[512,1536]{1,0:T(8,128)(2,1)}, f32[1,1536]{1,0:T(1,128)}) custom-call(s32[16]{0:T(128)} %concatenate.45.info, bf16[512,1536]{1,0:T(8,128)(2,1)} %get-tuple-element.197.rest_2_.grad_query, bf16[512,512]{1,0:T(8,128)(2,1)} %join_key_value_gradients.1.rest_3_.grad_pair, bf16[512,1536]{1,0:T(8,128)(2,1)} %tokens.5, ...), custom_call_target="tpu_custom_call" | custom-call | flops 1 | bytes 1 | tf_op jit(solution)/shard_map/token_gradient/pallas_call | solution.py:902
  699.8 6.1 collective-permute-done.59
  707.4 6.2 collective-permute-start.60
  720.4 12.1 %collective-permute-done.52 = bf16[2,2,208,896]{3,2,1,0:T(8,128)(2,1)S(1)} collective-permute-done((bf16[2,2,208,896]{3,2,1,0:T(8,128)(2,1)S(1)}, bf16[2,2,208,896]{3,2,1,0:T(8,128)(2,1)S(1)}, u32[]{:S(2)}, u32[]{:S(2)}) %collective-permute-start.52) | collective-permute-done | bytes 1490976 | tf_op jit(solution)/shard_map/ppermute | solution.py:1075
  732.5 7.6 collective-permute-done.50
  744.2 7.6 collective-permute-done.60
  754.5 5.2 collective-permute-done.51
  (359 shorter events, 246.0 us)
Async XLA Ops:
  7.2 240.0 %all-gather.5.cloned.1.call-start = ((), (), s32[]{:S(2)}) async-start(), calls=%async_computation | async-start | bytes 14155776 | tf_op jit(solution)/shard_map/all_gather | solution.py:1254
  23.4 35.3 %collective-permute-start.2 = (bf16[1,208,896]{2,1,0:T(8,128)(2,1)S(1)}, bf16[1,208,896]{2,1,0:T(8,128)(2,1)}, u32[]{:S(2)}, u32[]{:S(2)}) collective-permute-start(bf16[1,208,896]{2,1,0:T(8,128)(2,1)S(1)} %fusion.63), channel_id=1, source_target_pairs={{0,24},{4,28},{8,16},{12,20},{16,8},{20,12},{24,0},{28,4},{1,25},{... | collective-permute-start | bytes 1118216 | tf_op jit(solution)/shard_map/ppermute | solution.py:1075
  24.9 32.0 %collective-permute-start.1 = (bf16[1,208,896]{2,1,0:T(8,128)(2,1)S(1)}, bf16[1,208,896]{2,1,0:T(8,128)(2,1)}, u32[]{:S(2)}, u32[]{:S(2)}) collective-permute-start(bf16[1,208,896]{2,1,0:T(8,128)(2,1)S(1)} %fusion.63), channel_id=1, source_target_pairs={{0,16},{4,20},{8,24},{12,28},{16,0},{20,4},{24,8},{28,12},{1,17},{... | collective-permute-start | bytes 1118216 | tf_op jit(solution)/shard_map/ppermute | solution.py:1075
  27.5 17.1 %collective-permute-start.5 = (bf16[208,896]{1,0:T(8,128)(2,1)}, bf16[208,896]{1,0:T(8,128)(2,1)S(1)}, u32[]{:S(2)}, u32[]{:S(2)}) collective-permute-start(bf16[208,896]{1,0:T(8,128)(2,1)} %fusion.47), channel_id=1, source_target_pairs={{0,1},{1,2},{2,3},{4,5},{5,6},{6,7},{8,9},{9,10},{10,11},{12,13},{... | collective-permute-start | bytes 1118216 | tf_op jit(solution)/shard_map/ppermute | solution.py:1016
  31.0 14.9 %collective-permute-start.4 = (bf16[208,896]{1,0:T(8,128)(2,1)}, bf16[208,896]{1,0:T(8,128)(2,1)S(1)}, u32[]{:S(2)}, u32[]{:S(2)}) collective-permute-start(bf16[208,896]{1,0:T(8,128)(2,1)} %fusion.47), channel_id=1, source_target_pairs={{1,0},{2,1},{3,2},{5,4},{6,5},{7,6},{9,8},{10,9},{11,10},{13,12},{... | collective-permute-start | bytes 1118216 | tf_op jit(solution)/shard_map/ppermute | solution.py:1016
  32.3 20.9 %collective-permute-start.7 = (bf16[208,896]{1,0:T(8,128)(2,1)}, bf16[208,896]{1,0:T(8,128)(2,1)S(1)}, u32[]{:S(2)}, u32[]{:S(2)}) collective-permute-start(bf16[208,896]{1,0:T(8,128)(2,1)} %fusion.47), channel_id=1, source_target_pairs={{0,3},{3,0},{4,7},{7,4},{8,11},{11,8},{12,15},{15,12},{16,19},{19,... | collective-permute-start | bytes 1118216 | tf_op jit(solution)/shard_map/ppermute | solution.py:1020
  65.2 39.9 %collective-permute-start.12 = (bf16[576,1536]{1,0:T(8,128)(2,1)S(1)}, bf16[576,1536]{1,0:T(8,128)(2,1)S(1)}, u32[]{:S(2)}, u32[]{:S(2)}) collective-permute-start(bf16[576,1536]{1,0:T(8,128)(2,1)S(1)} %pad_maximum_fusion.2.rest_0_), channel_id=1, source_target_pairs={{0,1},{1,2},{2,3},{4,5},{5,6},{6,7},{8,9},{9,10},{10,11},{12,13},{... | collective-permute-start | bytes 5308424 | tf_op jit(solution)/shard_map/ppermute | solution.py:1016
  66.9 42.8 %collective-permute-start.11 = (bf16[576,1536]{1,0:T(8,128)(2,1)S(1)}, bf16[576,1536]{1,0:T(8,128)(2,1)}, u32[]{:S(2)}, u32[]{:S(2)}) collective-permute-start(bf16[576,1536]{1,0:T(8,128)(2,1)S(1)} %pad_maximum_fusion.2.rest_0_), channel_id=1, source_target_pairs={{1,0},{2,1},{3,2},{5,4},{6,5},{7,6},{9,8},{10,9},{11,10},{13,12},{... | collective-permute-start | bytes 5308424 | tf_op jit(solution)/shard_map/ppermute | solution.py:1016
  68.2 28.1 %collective-permute-start.3 = (bf16[4,208,896]{2,1,0:T(8,128)(2,1)}, bf16[4,208,896]{2,1,0:T(8,128)(2,1)}, u32[]{:S(2)}, u32[]{:S(2)}) collective-permute-start(bf16[4,208,896]{2,1,0:T(8,128)(2,1)} %constant_dynamic-update-slice_fusion.rest_0_.rest_6_.rest_11_), channel_id=1, source_target_pairs={{0,4},{4,0},{8,12},{12,8},{16,20},{20,16},{24,28},{28,24},{1,5},{5... | collective-permute-start | bytes 4472840 | tf_op jit(solution)/shard_map/ppermute | solution.py:1075
  68.3 27.0 %collective-permute-start.9 = (bf16[3,208,896]{2,1,0:T(8,128)(2,1)S(1)}, bf16[3,208,896]{2,1,0:T(8,128)(2,1)S(1)}, u32[]{:S(2)}, u32[]{:S(2)}) collective-permute-start(bf16[3,208,896]{2,1,0:T(8,128)(2,1)S(1)} %pad_maximum_fusion.10.rest_2_.rest_8_.rest_13_), channel_id=1, source_target_pairs={{0,16},{4,20},{8,24},{12,28},{16,0},{20,4},{24,8},{28,12},{1,17},{... | collective-permute-start | bytes 3354632 | tf_op jit(solution)/shard_map/ppermute | solution.py:1075
  69.6 26.7 %collective-permute-start.8 = (bf16[3,208,896]{2,1,0:T(8,128)(2,1)S(1)}, bf16[3,208,896]{2,1,0:T(8,128)(2,1)S(1)}, u32[]{:S(2)}, u32[]{:S(2)}) collective-permute-start(bf16[3,208,896]{2,1,0:T(8,128)(2,1)S(1)} %pad_maximum_fusion.10.rest_2_.rest_8_.rest_13_), channel_id=1, source_target_pairs={{0,8},{4,12},{8,0},{12,4},{16,24},{20,28},{24,16},{28,20},{1,9},{5... | collective-permute-start | bytes 3354632 | tf_op jit(solution)/shard_map/ppermute | solution.py:1075
  109.7 18.1 %collective-permute-start.14 = (bf16[2,208,896]{2,1,0:T(8,128)(2,1)S(1)}, bf16[2,208,896]{2,1,0:T(8,128)(2,1)S(1)}, u32[]{:S(2)}, u32[]{:S(2)}) collective-permute-start(bf16[2,208,896]{2,1,0:T(8,128)(2,1)S(1)} %slice.447), channel_id=1, source_target_pairs={{0,8},{4,12},{8,0},{12,4},{16,24},{20,28},{24,16},{28,20},{1,9},{5... | collective-permute-start | bytes 2236424 | tf_op jit(solution)/shard_map/ppermute | solution.py:1075
  131.6 42.8 %collective-permute-start.18 = (bf16[576,1536]{1,0:T(8,128)(2,1)}, bf16[576,1536]{1,0:T(8,128)(2,1)}, u32[]{:S(2)}, u32[]{:S(2)}) collective-permute-start(bf16[576,1536]{1,0:T(8,128)(2,1)} %select_select_fusion.1), channel_id=1, source_target_pairs={{3,1},{1,0},{0,2},{2,3},{7,5},{5,4},{4,6},{6,7},{11,9},{9,8},{8,10... | collective-permute-start | bytes 5308424 | tf_op jit(solution)/shard_map/ppermute | solution.py:1027
  147.5 35.8 %collective-permute-start.19 = (bf16[512,512]{1,0:T(8,128)(2,1)}, bf16[512,512]{1,0:T(8,128)(2,1)S(1)}, u32[]{:S(2)}, u32[]{:S(2)}) collective-permute-start(bf16[512,512]{1,0:T(8,128)(2,1)} %get-tuple-element.124.own), channel_id=1, source_target_pairs={{1,0},{3,2},{5,4},{7,6},{9,8},{11,10},{13,12},{15,14},{17,16},{19,... | collective-permute-start | bytes 1572872 | tf_op jit(solution)/shard_map/ppermute | solution.py:1256
  183.3 42.3 %collective-permute-start.23 = (bf16[576,1536]{1,0:T(8,128)(2,1)S(1)}, bf16[576,1536]{1,0:T(8,128)(2,1)}, u32[]{:S(2)}, u32[]{:S(2)}) collective-permute-start(bf16[576,1536]{1,0:T(8,128)(2,1)S(1)} %copy-done.11), channel_id=1, source_target_pairs={{0,3},{3,0},{4,7},{7,4},{8,11},{11,8},{12,15},{15,12},{16,19},{19,... | collective-permute-start | bytes 5308424 | tf_op jit(solution)/shard_map/ppermute | solution.py:1020
  225.7 41.1 %collective-permute-start.25 = (bf16[576,1536]{1,0:T(8,128)(2,1)S(1)}, bf16[576,1536]{1,0:T(8,128)(2,1)S(1)}, u32[]{:S(2)}, u32[]{:S(2)}) collective-permute-start(bf16[576,1536]{1,0:T(8,128)(2,1)S(1)} %pad_maximum_fusion.3.rest_0_), channel_id=1, source_target_pairs={{0,1},{1,2},{2,3},{4,5},{5,6},{6,7},{8,9},{9,10},{10,11},{12,13},{... | collective-permute-start | bytes 5308424 | tf_op jit(solution)/shard_map/ppermute | solution.py:1016
  227.1 39.7 %collective-permute-start.24 = (bf16[576,1536]{1,0:T(8,128)(2,1)S(1)}, bf16[576,1536]{1,0:T(8,128)(2,1)}, u32[]{:S(2)}, u32[]{:S(2)}) collective-permute-start(bf16[576,1536]{1,0:T(8,128)(2,1)S(1)} %pad_maximum_fusion.3.rest_0_), channel_id=1, source_target_pairs={{1,0},{2,1},{3,2},{5,4},{6,5},{7,6},{9,8},{10,9},{11,10},{13,12},{... | collective-permute-start | bytes 5308424 | tf_op jit(solution)/shard_map/ppermute | solution.py:1016
  228.7 37.1 %collective-permute-start.21 = (bf16[512,1536]{1,0:T(8,128)(2,1)}, bf16[512,1536]{1,0:T(8,128)(2,1)}, u32[]{:S(2)}, u32[]{:S(2)}) collective-permute-start(bf16[512,1536]{1,0:T(8,128)(2,1)} %get-tuple-element.126.rows.normed), channel_id=1, source_target_pairs={{0,16},{4,20},{8,24},{12,28},{16,0},{20,4},{24,8},{28,12},{1,17},{... | collective-permute-start | bytes 4718600 | tf_op jit(solution)/shard_map/ppermute | solution.py:1075
  230.0 36.8 %collective-permute-start.20 = (bf16[512,1536]{1,0:T(8,128)(2,1)}, bf16[512,1536]{1,0:T(8,128)(2,1)}, u32[]{:S(2)}, u32[]{:S(2)}) collective-permute-start(bf16[512,1536]{1,0:T(8,128)(2,1)} %get-tuple-element.126.rows.normed), channel_id=1, source_target_pairs={{0,8},{4,12},{8,0},{12,4},{16,24},{20,28},{24,16},{28,20},{1,9},{5... | collective-permute-start | bytes 4718600 | tf_op jit(solution)/shard_map/ppermute | solution.py:1075
  270.6 26.4 %collective-permute-start.29 = (bf16[512,1536]{1,0:T(8,128)(2,1)}, bf16[512,1536]{1,0:T(8,128)(2,1)S(1)}, u32[]{:S(2)}, u32[]{:S(2)}) collective-permute-start(bf16[512,1536]{1,0:T(8,128)(2,1)} %collective-permute-done.21.rows), channel_id=1, source_target_pairs={{0,4},{4,0},{8,12},{12,8},{16,20},{20,16},{24,28},{28,24},{1,5},{5... | collective-permute-start | bytes 4718600 | tf_op jit(solution)/shard_map/ppermute | solution.py:1075
  274.9 28.5 %collective-permute-start.27 = (bf16[256,1536]{1,0:T(8,128)(2,1)}, bf16[256,1536]{1,0:T(8,128)(2,1)S(1)}, u32[]{:S(2)}, u32[]{:S(2)}) collective-permute-start(bf16[256,1536]{1,0:T(8,128)(2,1)} %slice.455), channel_id=1, source_target_pairs={{0,8},{4,12},{8,0},{12,4},{16,24},{20,28},{24,16},{28,20},{1,9},{5... | collective-permute-start | bytes 2359304 | tf_op jit(solution)/shard_map/ppermute | solution.py:1075
  276.0 27.4 %collective-permute-start.26 = (bf16[256,1536]{1,0:T(8,128)(2,1)}, bf16[256,1536]{1,0:T(8,128)(2,1)}, u32[]{:S(2)}, u32[]{:S(2)}) collective-permute-start(bf16[256,1536]{1,0:T(8,128)(2,1)} %slice.454), channel_id=1, source_target_pairs={{0,16},{4,20},{8,24},{12,28},{16,0},{20,4},{24,8},{28,12},{1,17},{... | collective-permute-start | bytes 2359304 | tf_op jit(solution)/shard_map/ppermute | solution.py:1075
  278.4 42.9 %collective-permute-start.31 = (bf16[576,1536]{1,0:T(8,128)(2,1)}, bf16[576,1536]{1,0:T(8,128)(2,1)S(1)}, u32[]{:S(2)}, u32[]{:S(2)}) collective-permute-start(bf16[576,1536]{1,0:T(8,128)(2,1)} %select_select_fusion), channel_id=1, source_target_pairs={{3,1},{1,0},{0,2},{2,3},{7,5},{5,4},{4,6},{6,7},{11,9},{9,8},{8,10... | collective-permute-start | bytes 5308424 | tf_op jit(solution)/shard_map/ppermute | solution.py:1027
  321.3 55.7 %collective-permute-start.32 = (bf16[576,1536]{1,0:T(8,128)(2,1)S(1)}, bf16[576,1536]{1,0:T(8,128)(2,1)S(1)}, u32[]{:S(2)}, u32[]{:S(2)}) collective-permute-start(bf16[576,1536]{1,0:T(8,128)(2,1)S(1)} %pad_maximum_fusion.3.rest_0_), channel_id=1, source_target_pairs={{0,3},{3,0},{4,7},{7,4},{8,11},{11,8},{12,15},{15,12},{16,19},{19,... | collective-permute-start | bytes 5308424 | tf_op jit(solution)/shard_map/ppermute | solution.py:1020
  366.7 41.6 %collective-permute-start.33 = (bf16[576,1536]{1,0:T(8,128)(2,1)}, bf16[576,1536]{1,0:T(8,128)(2,1)S(1)}, u32[]{:S(2)}, u32[]{:S(2)}) collective-permute-start(bf16[576,1536]{1,0:T(8,128)(2,1)} %get-tuple-element.176), channel_id=1, source_target_pairs={{1,3},{0,1},{2,0},{3,2},{5,7},{4,5},{6,4},{7,6},{9,11},{8,9},{10,8... | collective-permute-start | bytes 5308424 | tf_op jit(solution)/shard_map/ppermute | solution.py:1043
  431.7 38.6 %collective-permute-start.35 = (bf16[2,272,1536]{2,1,0:T(8,128)(2,1)S(1)}, bf16[2,272,1536]{2,1,0:T(8,128)(2,1)S(1)}, u32[]{:S(2)}, u32[]{:S(2)}) collective-permute-start(bf16[2,272,1536]{2,1,0:T(8,128)(2,1)S(1)} %pad_maximum_fusion.4), channel_id=1, source_target_pairs={{0,8},{4,12},{8,0},{12,4},{16,24},{20,28},{24,16},{28,20},{1,9},{5... | collective-permute-start | bytes 5013512 | tf_op jit(solution)/shard_map/ppermute | solution.py:1075
  432.7 38.7 %collective-permute-start.36 = (bf16[2,272,1536]{2,1,0:T(8,128)(2,1)S(1)}, bf16[2,272,1536]{2,1,0:T(8,128)(2,1)S(1)}, u32[]{:S(2)}, u32[]{:S(2)}) collective-permute-start(bf16[2,272,1536]{2,1,0:T(8,128)(2,1)S(1)} %pad_maximum_fusion.5), channel_id=1, source_target_pairs={{0,16},{4,20},{8,24},{12,28},{16,0},{20,4},{24,8},{28,12},{1,17},{... | collective-permute-start | bytes 5013512 | tf_op jit(solution)/shard_map/ppermute | solution.py:1075
  480.5 81.1 %collective-permute-start.37 = (bf16[4,512,1536]{2,1,0:T(8,128)(2,1)}, bf16[4,512,1536]{2,1,0:T(8,128)(2,1)}, u32[]{:S(2)}, u32[]{:S(2)}) collective-permute-start(bf16[4,512,1536]{2,1,0:T(8,128)(2,1)} %combine.7), channel_id=1, source_target_pairs={{0,4},{4,0},{8,12},{12,8},{16,20},{20,16},{24,28},{28,24},{1,5},{5... | collective-permute-start | bytes 18874376 | tf_op jit(solution)/shard_map/ppermute | solution.py:1075
  483.4 43.2 %collective-permute-start.46 = (bf16[576,1536]{1,0:T(8,128)(2,1)}, bf16[576,1536]{1,0:T(8,128)(2,1)}, u32[]{:S(2)}, u32[]{:S(2)}) collective-permute-start(bf16[576,1536]{1,0:T(8,128)(2,1)} %get-tuple-element.294), channel_id=1, source_target_pairs={{1,0},{2,1},{3,2},{5,4},{6,5},{7,6},{9,8},{10,9},{11,10},{13,12},{... | collective-permute-start | bytes 5308424 | tf_op jit(solution)/shard_map/ppermute | solution.py:1056
  484.7 43.4 %collective-permute-start.45 = (bf16[576,1536]{1,0:T(8,128)(2,1)}, bf16[576,1536]{1,0:T(8,128)(2,1)}, u32[]{:S(2)}, u32[]{:S(2)}) collective-permute-start(bf16[576,1536]{1,0:T(8,128)(2,1)} %get-tuple-element.295), channel_id=1, source_target_pairs={{0,1},{1,2},{2,3},{4,5},{5,6},{6,7},{8,9},{9,10},{10,11},{12,13},{... | collective-permute-start | bytes 5308424 | tf_op jit(solution)/shard_map/ppermute | solution.py:1055
  528.1 48.7 %collective-permute-start.47 = (bf16[576,1536]{1,0:T(8,128)(2,1)}, bf16[576,1536]{1,0:T(8,128)(2,1)}, u32[]{:S(2)}, u32[]{:S(2)}) collective-permute-start(bf16[576,1536]{1,0:T(8,128)(2,1)} %get-tuple-element.213), channel_id=1, source_target_pairs={{0,3},{3,0},{4,7},{7,4},{8,11},{11,8},{12,15},{15,12},{16,19},{19,... | collective-permute-start | bytes 5308424 | tf_op jit(solution)/shard_map/ppermute | solution.py:1346
  541.1 19.8 %collective-permute-start.43 = (bf16[272,1536]{1,0:T(8,128)(2,1)}, bf16[272,1536]{1,0:T(8,128)(2,1)S(1)}, u32[]{:S(2)}, u32[]{:S(2)}) collective-permute-start(bf16[272,1536]{1,0:T(8,128)(2,1)} %get-tuple-element.262), channel_id=1, source_target_pairs={{0,8},{4,12},{8,0},{12,4},{16,24},{20,28},{24,16},{28,20},{1,9},{5... | collective-permute-start | bytes 2506760 | tf_op jit(solution)/shard_map/ppermute | solution.py:1075
  542.0 19.5 %collective-permute-start.42 = (bf16[272,1536]{1,0:T(8,128)(2,1)}, bf16[272,1536]{1,0:T(8,128)(2,1)S(1)}, u32[]{:S(2)}, u32[]{:S(2)}) collective-permute-start(bf16[272,1536]{1,0:T(8,128)(2,1)} %get-tuple-element.264), channel_id=1, source_target_pairs={{0,16},{4,20},{8,24},{12,28},{16,0},{20,4},{24,8},{28,12},{1,17},{... | collective-permute-start | bytes 2506760 | tf_op jit(solution)/shard_map/ppermute | solution.py:1075
  576.8 67.6 %collective-permute-start.48 = (bf16[576,1536]{1,0:T(8,128)(2,1)}, bf16[576,1536]{1,0:T(8,128)(2,1)S(1)}, u32[]{:S(2)}, u32[]{:S(2)}) collective-permute-start(bf16[576,1536]{1,0:T(8,128)(2,1)} %get-tuple-element.214), channel_id=1, source_target_pairs={{1,3},{0,1},{2,0},{3,2},{5,7},{4,5},{6,4},{7,6},{9,11},{8,9},{10,8... | collective-permute-start | bytes 5308424 | tf_op jit(solution)/shard_map/ppermute | solution.py:1043
  580.9 47.6 %collective-permute-start.40 = (bf16[2,256,1536]{2,1,0:T(8,128)(2,1)}, bf16[2,256,1536]{2,1,0:T(8,128)(2,1)}, u32[]{:S(2)}, u32[]{:S(2)}) collective-permute-start(bf16[2,256,1536]{2,1,0:T(8,128)(2,1)} %pad_maximum_fusion.7), channel_id=1, source_target_pairs={{0,16},{4,20},{8,24},{12,28},{16,0},{20,4},{24,8},{28,12},{1,17},{... | collective-permute-start | bytes 4718600 | tf_op jit(solution)/shard_map/ppermute | solution.py:1075
  583.4 45.1 %collective-permute-start.38 = (bf16[2,256,1536]{2,1,0:T(8,128)(2,1)}, bf16[2,256,1536]{2,1,0:T(8,128)(2,1)}, u32[]{:S(2)}, u32[]{:S(2)}) collective-permute-start(bf16[2,256,1536]{2,1,0:T(8,128)(2,1)} %pad_maximum_fusion.6), channel_id=1, source_target_pairs={{0,8},{4,12},{8,0},{12,4},{16,24},{20,28},{24,16},{28,20},{1,9},{5... | collective-permute-start | bytes 4718600 | tf_op jit(solution)/shard_map/ppermute | solution.py:1075
  601.0 23.6 %collective-permute-start.44 = (bf16[512,512]{1,0:T(8,128)(2,1)S(1)}, bf16[512,512]{1,0:T(8,128)(2,1)S(1)}, u32[]{:S(2)}, u32[]{:S(2)}) collective-permute-start(bf16[512,512]{1,0:T(8,128)(2,1)S(1)} %convert_element_type.669), channel_id=1, source_target_pairs={{0,1},{2,3},{4,5},{6,7},{8,9},{10,11},{12,13},{14,15},{16,17},{18,... | collective-permute-start | bytes 1572872 | tf_op jit(solution)/shard_map/ppermute | solution.py:1395
  644.4 50.3 %collective-permute-start.49 = (bf16[4,4,208,896]{3,2,1,0:T(8,128)(2,1)}, bf16[4,4,208,896]{3,2,1,0:T(8,128)(2,1)}, u32[]{:S(2)}, u32[]{:S(2)}) collective-permute-start(bf16[4,4,208,896]{3,2,1,0:T(8,128)(2,1)} %get-tuple-element.215), channel_id=1, source_target_pairs={{0,4},{4,0},{8,12},{12,8},{16,20},{20,16},{24,28},{28,24},{1,5},{5... | collective-permute-start | bytes 17891336 | tf_op jit(solution)/shard_map/ppermute | solution.py:1075
  662.1 43.7 %collective-permute-start.59 = (bf16[576,1536]{1,0:T(8,128)(2,1)}, bf16[576,1536]{1,0:T(8,128)(2,1)S(1)}, u32[]{:S(2)}, u32[]{:S(2)}) collective-permute-start(bf16[576,1536]{1,0:T(8,128)(2,1)} %get-tuple-element.292), channel_id=1, source_target_pairs={{1,0},{2,1},{3,2},{5,4},{6,5},{7,6},{9,8},{10,9},{11,10},{13,12},{... | collective-permute-start | bytes 5308424 | tf_op jit(solution)/shard_map/ppermute | solution.py:1056
  663.4 44.0 %collective-permute-start.58 = (bf16[576,1536]{1,0:T(8,128)(2,1)}, bf16[576,1536]{1,0:T(8,128)(2,1)}, u32[]{:S(2)}, u32[]{:S(2)}) collective-permute-start(bf16[576,1536]{1,0:T(8,128)(2,1)} %get-tuple-element.293), channel_id=1, source_target_pairs={{0,1},{1,2},{2,3},{4,5},{5,6},{6,7},{8,9},{9,10},{10,11},{12,13},{... | collective-permute-start | bytes 5308424 | tf_op jit(solution)/shard_map/ppermute | solution.py:1055
  679.4 36.2 %collective-permute-start.39 = (bf16[256,1536]{1,0:T(8,128)(2,1)}, bf16[256,1536]{1,0:T(8,128)(2,1)}, u32[]{:S(2)}, u32[]{:S(2)}) collective-permute-start(bf16[256,1536]{1,0:T(8,128)(2,1)} %get-tuple-element.272), channel_id=1, source_target_pairs={{0,16},{4,20},{8,24},{12,28},{16,0},{20,4},{24,8},{28,12},{1,17},{... | collective-permute-start | bytes 2359304 | tf_op jit(solution)/shard_map/ppermute | solution.py:1075
  680.5 35.0 %collective-permute-start.41 = (bf16[256,1536]{1,0:T(8,128)(2,1)}, bf16[256,1536]{1,0:T(8,128)(2,1)}, u32[]{:S(2)}, u32[]{:S(2)}) collective-permute-start(bf16[256,1536]{1,0:T(8,128)(2,1)} %get-tuple-element.273), channel_id=1, source_target_pairs={{0,8},{4,12},{8,0},{12,4},{16,24},{20,28},{24,16},{28,20},{1,9},{5... | collective-permute-start | bytes 2359304 | tf_op jit(solution)/shard_map/ppermute | solution.py:1075
  698.4 34.1 %collective-permute-start.52 = (bf16[2,2,208,896]{3,2,1,0:T(8,128)(2,1)S(1)}, bf16[2,2,208,896]{3,2,1,0:T(8,128)(2,1)S(1)}, u32[]{:S(2)}, u32[]{:S(2)}) collective-permute-start(bf16[2,2,208,896]{3,2,1,0:T(8,128)(2,1)S(1)} %pad_maximum_fusion.9), channel_id=1, source_target_pairs={{0,16},{4,20},{8,24},{12,28},{16,0},{20,4},{24,8},{28,12},{1,17},{... | collective-permute-start | bytes 4472840 | tf_op jit(solution)/shard_map/ppermute | solution.py:1075
  705.8 34.3 %collective-permute-start.50 = (bf16[2,2,208,896]{3,2,1,0:T(8,128)(2,1)S(1)}, bf16[2,2,208,896]{3,2,1,0:T(8,128)(2,1)S(1)}, u32[]{:S(2)}, u32[]{:S(2)}) collective-permute-start(bf16[2,2,208,896]{3,2,1,0:T(8,128)(2,1)S(1)} %pad_maximum_fusion.8), channel_id=1, source_target_pairs={{0,8},{4,12},{8,0},{12,4},{16,24},{20,28},{24,16},{28,20},{1,9},{5... | collective-permute-start | bytes 4472840 | tf_op jit(solution)/shard_map/ppermute | solution.py:1075
  707.4 44.4 %collective-permute-start.60 = (bf16[576,1536]{1,0:T(8,128)(2,1)S(1)}, bf16[576,1536]{1,0:T(8,128)(2,1)S(1)}, u32[]{:S(2)}, u32[]{:S(2)}) collective-permute-start(bf16[576,1536]{1,0:T(8,128)(2,1)S(1)} %copy-done.38), channel_id=1, source_target_pairs={{0,3},{3,0},{4,7},{7,4},{8,11},{11,8},{12,15},{15,12},{16,19},{19,... | collective-permute-start | bytes 5308424 | tf_op jit(solution)/shard_map/ppermute | solution.py:1417
  742.1 17.6 %collective-permute-start.51 = (bf16[2,208,896]{2,1,0:T(8,128)(2,1)S(1)}, bf16[2,208,896]{2,1,0:T(8,128)(2,1)S(1)}, u32[]{:S(2)}, u32[]{:S(2)}) collective-permute-start(bf16[2,208,896]{2,1,0:T(8,128)(2,1)S(1)} %get-tuple-element.280), channel_id=1, source_target_pairs={{0,16},{4,20},{8,24},{12,28},{16,0},{20,4},{24,8},{28,12},{1,17},{... | collective-permute-start | bytes 2236424 | tf_op jit(solution)/shard_map/ppermute | solution.py:1075
  743.3 17.2 %collective-permute-start.53 = (bf16[2,208,896]{2,1,0:T(8,128)(2,1)S(1)}, bf16[2,208,896]{2,1,0:T(8,128)(2,1)S(1)}, u32[]{:S(2)}, u32[]{:S(2)}) collective-permute-start(bf16[2,208,896]{2,1,0:T(8,128)(2,1)S(1)} %get-tuple-element.281), channel_id=1, source_target_pairs={{0,8},{4,12},{8,0},{12,4},{16,24},{20,28},{24,16},{28,20},{1,9},{5... | collective-permute-start | bytes 2236424 | tf_op jit(solution)/shard_map/ppermute | solution.py:1075
  772.4 17.2 %collective-permute-start.57 = (bf16[208,896]{1,0:T(8,128)(2,1)S(1)}, bf16[208,896]{1,0:T(8,128)(2,1)S(1)}, u32[]{:S(2)}, u32[]{:S(2)}) collective-permute-start(bf16[208,896]{1,0:T(8,128)(2,1)S(1)} %get-tuple-element.298), channel_id=1, source_target_pairs={{0,3},{3,0},{4,7},{7,4},{8,11},{11,8},{12,15},{15,12},{16,19},{19,... | collective-permute-start | bytes 1118216 | tf_op jit(solution)/shard_map/ppermute | solution.py:1044
  (87 other events, 1281.1 us)
Sparse Core Ops, SparseCore 0:
  128.0 70.2 all-gather.4

commit v10 on v9

--- a/solution.py
+++ b/solution.py
@@ -63,17 +63,16 @@
     return values * cosine - pltpu.roll(values, HEAD_DIM // 2, 1) * sine
 
 
+SLOTS = range(4)
 PIECES = (
-    ((0, 0), (2, 0), (4, 0), (6, 0)),
-    ((1, 0), (3, 0), (5, 0), (7, 0)),
-    ((0, 1), (0, 2), (0, 3)),
-    ((2, 1), (2, 2), (2, 3)),
-    ((4, 1), (4, 2), (4, 3)),
-    ((6, 1),),
+    tuple((0, slot) for slot in SLOTS),
+    tuple((1, slot) for slot in SLOTS),
+    tuple((2, slot) for slot in SLOTS),
+    tuple((4, slot) for slot in SLOTS),
+    ((6, 0), (6, 1)),
     ((6, 2), (6, 3)),
-    ((1, 1), (1, 2), (1, 3)),
-    ((3, 1), (3, 2), (3, 3), (5, 1), (5, 2), (5, 3)),
-    ((7, 1),),
+    tuple((flip_bits, slot) for flip_bits in (3, 5) for slot in SLOTS),
+    ((7, 0), (7, 1)),
     ((7, 2), (7, 3)),
 )
 EXTRA = 16
@@ -404,7 +403,7 @@
     return hit
 
 
-def tables_kernel(capacity, local, total, order, info, routes, chosen_out, place_out, earlier):
+def tables_kernel(capacity, local, total, info, routes, chosen_out, place_out, earlier):
     @pl.when(pl.program_id(0) == 0)
     def _():
         one = lax.broadcasted_iota(jnp.int32, (TOK_DEV, TOK_DEV), 0)
@@ -426,20 +425,17 @@
         ).astype(LOW)
 
 
-def tables(order, info, routes, capacity, local, total):
+def tables(info, routes, capacity, local, total):
     count = routes.shape[0]
     return pl.pallas_call(
         functools.partial(tables_kernel, capacity, local, total),
-        grid_spec=pltpu.PrefetchScalarGridSpec(
-            num_scalar_prefetch=2,
-            grid=(count,),
-            in_specs=[pl.BlockSpec((1, TOP, TOK_DEV), lambda i, order, info: (order[i], 0, 0))],
-            out_specs=[
-                pl.BlockSpec((1, local * capacity, TOK_DEV), lambda i, order, info: (i, 0, 0)),
-                pl.BlockSpec((1, 8, TOK_DEV), lambda i, order, info: (i, 0, 0)),
-            ],
-            scratch_shapes=[pltpu.VMEM((TOK_DEV, TOK_DEV), LOW)],
-        ),
+        grid=(count,),
+        in_specs=[SMEM, pl.BlockSpec((1, TOP, TOK_DEV), lambda i: (i, 0, 0))],
+        out_specs=[
+            pl.BlockSpec((1, local * capacity, TOK_DEV), lambda i: (i, 0, 0)),
+            pl.BlockSpec((1, 8, TOK_DEV), lambda i: (i, 0, 0)),
+        ],
+        scratch_shapes=[pltpu.VMEM((TOK_DEV, TOK_DEV), LOW)],
         out_shape=[
             jax.ShapeDtypeStruct((count, local * capacity, TOK_DEV), LOW),
             jax.ShapeDtypeStruct((count, 8, TOK_DEV), WIDE),
@@ -447,38 +443,36 @@
         compiler_params=params(),
         cost_estimate=LITTLE,
         name="route_tables",
-    )(order, info, routes)
-
-
-def pick_kernel(local, order, chosen, blocks, *outs):
-    rows_of = nn(chosen[0], blocks[0]).astype(LOW)
-    capacity = outs[0].shape[1]
-    for e in range(local):
-        outs[e][0] = rows_of[e * capacity : (e + 1) * capacity]
-
-
-def pick_rows(order, chosen, blocks, local):
+    )(info, routes)
+
+
+def pick_kernel(local, chosen, *rest):
     count, height, _ = chosen.shape
     capacity = height // local
+    for q in range(count):
+        rows_of = nn(chosen[q], rest[q][...]).astype(LOW)
+        for e in range(local):
+            rest[count + e][q] = rows_of[e * capacity : (e + 1) * capacity]
+
+
+def pick_rows(chosen, blocks, local):
+    count, height, _ = chosen.shape
+    capacity = height // local
+    wide = 256
     return pl.pallas_call(
         functools.partial(pick_kernel, local),
-        grid_spec=pltpu.PrefetchScalarGridSpec(
-            num_scalar_prefetch=1,
-            grid=(count,),
-            in_specs=[
-                pl.BlockSpec((1, height, TOK_DEV), lambda i, order: (i, 0, 0)),
-                pl.BlockSpec((1, TOK_DEV, D), lambda i, order: (order[i], 0, 0)),
-            ],
-            out_specs=[pl.BlockSpec((1, capacity, D), lambda i, order: (i, 0, 0))] * local,
-        ),
+        grid=(D // wide,),
+        in_specs=[whole(chosen.shape)]
+        + [pl.BlockSpec((TOK_DEV, wide), lambda i: (0, i))] * count,
+        out_specs=[pl.BlockSpec((count, capacity, wide), lambda i: (0, 0, i))] * local,
         out_shape=[jax.ShapeDtypeStruct((count, capacity, D), LOW)] * local,
         compiler_params=params(),
         cost_estimate=LITTLE,
         name="pick_rows",
-    )(order, chosen, blocks)
-
-
-def dispatch_kernel(local, near, info, rows, chosen, routes, router, *rest):
+    )(chosen, *blocks)
+
+
+def dispatch_kernel(local, info, rows, chosen, routes, router, *rest):
     outs, logits = rest[2 * local : 4 * local], rest[-1]
     total = router.shape[1]
     step = pl.program_id(0)
@@ -511,7 +505,7 @@
             outs[local + e][0] = jnp.sum(picked * share_row, axis=1, keepdims=True)
 
 
-def dispatch(at, near, info, rows, chosen, routes, router, local, earlier):
+def dispatch(at, info, rows, chosen, routes, router, local, earlier):
     count, height, _ = chosen.shape
     capacity = height // local
     total = router.shape[1]
@@ -523,32 +517,27 @@
         earlier = [jnp.zeros((8, 128), shape.dtype) for shape in out_shape]
         aliases = {}
     else:
-        aliases = {6 + i: i for i in range(len(out_shape))}
+        aliases = {5 + i: i for i in range(len(out_shape))}
     return pl.pallas_call(
         functools.partial(dispatch_kernel, local),
-        grid_spec=pltpu.PrefetchScalarGridSpec(
-            num_scalar_prefetch=2,
-            grid=(D // wide,),
-            in_specs=[
-                pl.BlockSpec((TOK_DEV, wide), lambda i, near, info: (0, i)),
-                pl.BlockSpec((1, height, TOK_DEV), lambda i, near, info: (at, 0, 0)),
-                pl.BlockSpec((1, TOP, TOK_DEV), lambda i, near, info: (near[at], 0, 0)),
-                pl.BlockSpec((wide, total), lambda i, near, info: (i, 0)),
-            ]
-            + [ANY] * len(out_shape),
-            out_specs=[
-                pl.BlockSpec((1, capacity, wide), lambda i, near, info: (at, 0, i))
-            ]
-            * local
-            + [pl.BlockSpec((1, capacity, 1), lambda i, near, info: (at, 0, 0))] * local,
-            scratch_shapes=[pltpu.VMEM((TOK_DEV, total), WIDE)],
-        ),
+        grid=(D // wide,),
+        in_specs=[
+            SMEM,
+            pl.BlockSpec((TOK_DEV, wide), lambda i: (0, i)),
+            pl.BlockSpec((1, height, TOK_DEV), lambda i: (at, 0, 0)),
+            pl.BlockSpec((1, TOP, TOK_DEV), lambda i: (at, 0, 0)),
+            pl.BlockSpec((wide, total), lambda i: (i, 0)),
+        ]
+        + [ANY] * len(out_shape),
+        out_specs=[pl.BlockSpec((1, capacity, wide), lambda i: (at, 0, i))] * local
+        + [pl.BlockSpec((1, capacity, 1), lambda i: (at, 0, 0))] * local,
+        scratch_shapes=[pltpu.VMEM((TOK_DEV, total), WIDE)],
         out_shape=out_shape,
         input_output_aliases=aliases,
         compiler_params=params(),
         cost_estimate=LITTLE,
         name="dispatch",
-    )(near, info, rows, chosen, routes, router, *earlier)
+    )(info, rows, chosen, routes, router, *earlier)
 
 
 def spread_kernel(local, place, *rest):
@@ -575,52 +564,23 @@
     )(place, *dots)
 
 
-def expert_kernel(slots, info, rows, grads, shares, *rest):
-    count = len(rest) - 7
-    refs = rest[:count]
-    out_rows, back_rows, grad_rows, acts, dots, weight, sem = rest[count:]
+def expert_kernel(slots, rows, grads, shares, source, *rest):
+    out_rows, back_rows, grad_rows, acts, dots, weight, sem = rest
     part = weight.shape[1] // slots
 
     @pl.when(pl.program_id(0) == 0)
     def _():
-        def copies(ref, slot):
-            return [
-                pltpu.make_async_copy(
-                    ref.at[pl.ds(which * part, part)],
-                    weight.at[which, pl.ds(slot * part, part)],
-                    sem,
-                )
-                for which in range(3)
-            ]
-
-        if count == slots:
-            for slot in range(slots):
-                run_all(copies(refs[slot], slot))
-        else:
-            block, second, above, below, far = refs
-            low_end = info[2] == 0
-            end = jnp.logical_or(low_end, info[2] == 3)
-            run_all(copies(block, 0))
-            run_all(copies(second, 1))
-
-            @pl.when(low_end)
-            def _():
-                run_all(copies(above, 2))
-
-            @pl.when(jnp.logical_not(low_end))
-            def _():
-                run_all(copies(below, 2))
-
-            @pl.when(end)
-            def _():
-                run_all(copies(far, 3))
-
-            @pl.when(jnp.logical_not(end))
-            def _():
-                run_all(copies(above, 3))
-
-        for slot in range(slots):
-            wait_all(copies(refs[0], slot))
+        copies = [
+            pltpu.make_async_copy(
+                source.at[slot, pl.ds(which * part, part)],
+                weight.at[which, pl.ds(slot * part, part)],
+                sem,
+            )
+            for slot in range(slots)
+            for which in range(3)
+        ]
+        run_all(copies)
+        wait_all(copies)
 
     row_block = rows[...]
     share = shares[...]
@@ -650,9 +610,9 @@
 EXPERT_ROWS = 256
 
 
-def expert(info, rows, grads, shares, refs, slots):
+def expert(rows, grads, shares, weights):
     height = rows.shape[0]
-    part = refs[0].shape[0] // 3
+    slots, part = weights.shape[0], weights.shape[1] // 3
     wide_block = pl.BlockSpec((EXPERT_ROWS, D), lambda i: (i, 0))
     thin_block = pl.BlockSpec((EXPERT_ROWS, 1), lambda i: (i, 0))
     return pl.pallas_call(
@@ -663,37 +623,37 @@
             jax.ShapeDtypeStruct((slots, 3 * part, height), LOW),
             jax.ShapeDtypeStruct((height, 1), WIDE),
         ],
-        in_specs=[SMEM, wide_block, wide_block, thin_block] + [ANY] * len(refs),
+        in_specs=[wide_block, wide_block, thin_block, ANY],
         out_specs=[wide_block] * 3
         + [pl.BlockSpec((slots, 3 * part, EXPERT_ROWS), lambda i: (0, 0, i)), thin_block],
         scratch_shapes=[pltpu.VMEM((3, slots * part, D), LOW), pltpu.SemaphoreType.DMA],
         compiler_params=params(),
         cost_estimate=LITTLE,
         name="expert",
-    )(info, rows, grads, shares, *refs)
-
-
-def expert_grads_kernel(slots, rows, grads, *rest):
-    acts, outs = rest[: len(slots)], rest[len(slots) :]
-    part = acts[0].shape[1] // 3
-    for act, out in zip(acts, outs):
-        out[: 2 * part, :] = nn(act[0, : 2 * part], rows[...]).astype(LOW)
-        out[2 * part :, :] = nn(act[0, 2 * part :], grads[...]).astype(LOW)
-
-
-def expert_grads(acts, rows, grads, slots):
-    _, part, height = acts.shape
-    return pl.pallas_call(
-        functools.partial(expert_grads_kernel, slots),
+    )(rows, grads, shares, weights)
+
+
+def expert_grads_kernel(acts, rows, grads, out):
+    slots, height, _ = acts.shape
+    part = height // 3
+    for slot in range(slots):
+        out[slot, : 2 * part] = nn(acts[slot, : 2 * part], rows[...]).astype(LOW)
+        out[slot, 2 * part :] = nn(acts[slot, 2 * part :], grads[...]).astype(LOW)
+
+
+def expert_grads(acts, rows, grads):
+    slots, part, height = acts.shape
+    strip = pl.BlockSpec((height, 256), lambda i: (0, i))
+    return pl.pallas_call(
+        expert_grads_kernel,
         grid=(D // 256,),
-        out_shape=[jax.ShapeDtypeStruct((part, D), LOW) for _ in slots],
-        in_specs=[pl.BlockSpec((height, 256), lambda i: (0, i))] * 2
-        + [pl.BlockSpec((1, part, height), lambda i, s=slot: (s, 0, 0)) for slot in slots],
-        out_specs=[pl.BlockSpec((part, 256), lambda i: (0, i)) for _ in slots],
+        out_shape=jax.ShapeDtypeStruct((slots, part, D), LOW),
+        in_specs=[whole(acts.shape), strip, strip],
+        out_specs=pl.BlockSpec((slots, part, 256), lambda i: (0, 0, i)),
         compiler_params=params(),
         cost_estimate=LITTLE,
         name="expert_gradients",
-    )(rows, grads, *[acts] * len(slots))
+    )(acts, rows, grads)
 
 
 SHARE_ROWS = 32
@@ -1039,9 +999,9 @@
     ]
 
 
-def reduce_first(second, fourth, chain=False):
+def reduce_first(second, fourth):
     relay = lax.ppermute(second, "cols", [(1, 3), (0, 1), (2, 0), (3, 2)])
-    return relay, None if chain else lax.ppermute(fourth, "cols", FAR)
+    return relay, lax.ppermute(fourth, "cols", FAR)
 
 
 def reduce_second(third, fourth, relay):
@@ -1100,6 +1060,11 @@
     got_xy = flip(add_low(near_x[1], got_x[1]), 4)
     got_yx = flip(add_low(near_y[1], got_y[1]), 2)
     return (near_x[0], got_x[0], got_xy, near_y[0], got_y[0], got_yx)
+
+
+def turn_corner(beside, across):
+    half = beside.shape[0] // 2
+    return jnp.concatenate([flip(beside[:half], 4), flip(across[half:], 2)], axis=0)
 
 
 def send_chips(sums):
@@ -1164,15 +1129,11 @@
         )
         for expert in range(local_experts)
     ]
-    nears, seconds, fars = ([], [], [])
-    routes_all = lax.all_gather(routes.T, "rows", axis=0)
-    if fast:
-        near_rows = row_place ^ jnp.arange(row_count, dtype=jnp.int32)
-    else:
-        near_rows = jnp.arange(row_count, dtype=jnp.int32)
-    chosen, place_rows = tables(
-        near_rows, info, routes_all, capacity, local_experts, expert_total
-    )
+    expert_weights = []
+    for block in shard_blocks:
+        if expert_weights:
+            block = after(block, expert_weights[-1])
+        expert_weights.append(lax.all_gather(block, "cols", axis=0))
     if fast:
         wide = packed.shape[1]
         gains = jnp.concatenate([attention_gain, experts_gain])[None, :]
@@ -1181,35 +1142,29 @@
                 packed,
                 jnp.pad(router_weight.T, ((0, 0), (0, wide - depth))),
                 jnp.pad(gains, ((0, 0), (0, wide - 2 * gain_part))),
-                jnp.zeros((EXTRA - router_part - 1, wide), LOW),
+                jnp.pad(routes.T.astype(LOW), ((0, 0), (0, wide - TOK_DEV))),
+                jnp.zeros((EXTRA - router_part - 1 - TOP, wide), LOW),
             ],
             axis=0,
         )
         packed_near = send_near(packed)
         packed_far = send_far(packed)
         packed_second = send_second(packed, packed_near)
-        slots = slot_list(packed, packed_near, packed_second, packed_far)
-
-        def gather_expert(*earlier):
-            expert_at = len(nears)
-            block = after(shard_blocks[expert_at], *earlier)
-            shard_blocks[expert_at] = block
-            nears.append(send_near(block))
-            seconds.append(send_second(block, nears[expert_at]))
-
-        gather_expert(*packed_near)
-        first = after(packed[None], routes_all)
-        first_four = jnp.concatenate([first] + [flip(first, bits) for bits in (2, 4, 6)], axis=0)
-        others = jnp.stack(slots[1:])
-        others = after(others, info, cosine, sine, first_four)
-        beside, across = flip(others, 2), flip(others, 4)
-        first_in, others_in = flip(first_four, 1), flip(others, 1)
-        beside, across = after((beside, across), first_in, others_in, chosen, *nears[0])
-        corner = [flip(beside[:1], 4), flip(across[1:], 2)]
+        grad_flips = (flip(cotangent, 2), flip(cotangent, 4))
+        own = jnp.stack(slot_list(packed, packed_near, packed_second, packed_far))
+        own = after(own, info, cosine, sine, *grad_flips)
+        beside, across = flip(own, 2), flip(own, 4)
+        own_in = flip(own, 1)
+        beside, across = after((beside, across), own_in)
+        corner = [flip(beside[:2], 4), flip(across[2:], 2)]
         pair_in = flip(jnp.concatenate([beside, across], axis=0), 1)
         corner_in = [flip(piece, 1) for piece in corner]
-        pieces = [first_four, first_in, others, beside, across, *corner]
-        pieces += [others_in, pair_in, *corner_in]
+        pieces = [own, own_in, beside, across, *corner, pair_in, *corner_in]
+        at = depth + router_part + 1
+        near_slots = [own, own_in, beside, pair_in, across, pair_in[4:], corner[0], corner_in[0]]
+        routes_all = jnp.stack([part[0, at : at + TOP, :TOK_DEV] for part in near_slots])
+        routes_all = routes_all.astype(jnp.int32)
+        chosen, place_rows = tables(info, routes_all, capacity, local_experts, expert_total)
         query_refs = pair_refs = out_refs = pieces
         extra_rows = extras(info, pieces)
         router_all = extra_rows[:, :router_part, :depth]
@@ -1234,14 +1189,12 @@
             ).reshape(D, -1)
         ]
         out_refs = [unpack(key_at + 2 * key_part, query_part)]
+        routes_all = lax.all_gather(routes.T, "rows", axis=0)
+        chosen, place_rows = tables(info, routes_all, capacity, local_experts, expert_total)
         axes = ("rows", "cols")
         router_all = jnp.swapaxes(lax.all_gather(router_weight, axes, axis=0), 1, 2)
         attention_scale = lax.all_gather(attention_gain, axes, axis=0)
         experts_scale = lax.all_gather(experts_gain, axes, axis=0)
-        expert_refs = [
-            [lax.all_gather(block, "cols", axis=0)[i] for i in range(col_count)]
-            for block in shard_blocks
-        ]
 
     attention_scale = attention_scale.reshape(1, D).astype(WIDE)
     experts_scale = experts_scale.reshape(1, D).astype(WIDE)
@@ -1250,37 +1203,42 @@
     ).reshape(expert_total, D)
     router_cols = router_rows.T
     normed, own_pair = key_value(info, tokens, attention_scale, cosine, sine, pair_refs)
-    grad_in = after(cotangent, *corner) if fast else cotangent
-    grad_all = lax.all_gather(grad_in, "rows", axis=0)
     pairs = [(i + 1, i) for i in range(0, col_count, 2)]
     partner = lax.ppermute(own_pair, "cols", pairs)
-    normed_in = after(normed, seconds[0]) if fast else normed
-    queries = query(info, normed_in, cosine, sine, query_refs)
+    queries = query(info, normed, cosine, sine, query_refs)
     if fast:
-        fars.append(send_far(after(shard_blocks[0], seconds[0], partner, queries)))
+        grad_flips = after(grad_flips, own_pair)
+        grad_corner = turn_corner(*grad_flips)
+        queries = after(queries, grad_corner)
     heads = attention(info, queries, own_pair, partner)
+    if fast:
+        grad_near = [cotangent, *grad_flips, grad_corner]
+        grad_blocks = [block for one in grad_near for block in (one, flip(one, 1))]
+        heads = after(heads, *grad_blocks, expert_weights[0])
+    else:
+        grad_all = lax.all_gather(cotangent, "rows", axis=0)
+        grad_blocks = [grad_all[q] for q in range(row_count)]
     residual, normed_two = out_projection(info, heads, tokens, experts_scale, out_refs)
 
     if fast:
         beside, across = flip(normed_two, 2), flip(normed_two, 4)
         beside_in = flip(normed_two, 1)
-        gather_expert(fars[0], normed_two)
-        grad_all = after(grad_all, normed_two)
     else:
         rows_all = lax.all_gather(normed_two, "rows", axis=0)
-    grad_rows = pick_rows(near_rows, chosen, grad_all, local_experts)
+    grad_rows = pick_rows(chosen, grad_blocks, local_experts)
 
     def place_block(q, block, picked):
         return dispatch(
-            q, near_rows, info, block, chosen, routes_all, router_cols, local_experts, picked
+            q, info, block, chosen, routes_all, router_cols, local_experts, picked
         )
 
     if fast:
         half = TOK_DEV // 2
         picked = place_block(0, normed_two, None)
         picked = place_block(1, beside_in, picked)
-        beside, across = after((beside, across), picked, grad_rows, *nears[1])
+        beside, across = after((beside, across), picked)
         corner = [flip(beside[:half], 4), flip(across[half:], 2)]
+        picked = after(picked, *grad_rows)
         picked = place_block(2, beside, picked)
         picked = place_block(4, across, picked)
         beside_in = flip(beside, 1)
@@ -1291,10 +1249,6 @@
         corner_in = flip(corner, 1)
         picked = place_block(6, corner, picked)
         picked = place_block(7, corner_in, picked)
-        fars.append(send_far(after(shard_blocks[1], seconds[1], picked)))
-        expert_refs = [
-            [shard_blocks[i], seconds[i], *nears[i], fars[i]] for i in range(local_experts)
-        ]
     else:
         picked = None
         for q in range(row_count):
@@ -1304,50 +1258,33 @@
     grad_rows = [a.reshape(height, D) for a in grad_rows]
     share_rows = [a.reshape(height, 1) for a in picked[local_experts:]]
 
-    out_rows, back_rows, gate_dots, reduced, marks = ([], [], [], [], [])
-    grad_slots = []
+    out_rows, back_rows, gate_dots, reduced = ([], [], [], [])
     for e in range(local_experts):
-        rows_in = token_rows[e]
-        if fast and e == 0:
-            rows_in = after(rows_in, seconds[1])
-        if fast and e == 1:
-            rows_in = after(rows_in, fars[1], second, fourth, own_slot, third)
+        rows_in = after(token_rows[e], *reduced_in) if e else token_rows[e]
         out_row, back_row, grad_row, acts, dots = expert(
-            info, rows_in, grad_rows[e], share_rows[e], expert_refs[e], col_count
+            rows_in, grad_rows[e], share_rows[e], expert_weights[e]
         )
         out_rows.append(out_row.reshape(row_count, capacity, D))
         back_rows.append(back_row.reshape(row_count, capacity, D))
         gate_dots.append(dots.reshape(row_count, capacity, 1))
-        if fast:
-            if e == 1:
-                back_rows = after(back_rows, marks[0][0])
-                got = flip(combine(info, chosen, back_rows, 1, 2, gate_dots), 1)
-                acts = after(acts, got)
-            second, fourth = expert_grads(acts, token_rows[e], grad_row, (1, 3))
-            if e == 0:
-                relay, _ = reduce_first(second, fourth, chain=True)
-                marks.append((relay,))
-            own_slot, third = expert_grads(acts, token_rows[e], grad_row, (0, 2))
-            grad_slots.append((own_slot, second, third, fourth))
-        else:
-            slots = expert_grads(acts, token_rows[e], grad_row, tuple(range(col_count)))
-            reduced.append(
-                lax.psum_scatter(jnp.stack(slots), "cols", scatter_dimension=0).astype(WIDE)
-            )
+        if fast and e == 1:
+            got = flip(combine(info, chosen, back_rows, 1, 2, gate_dots), 1)
+            back_keep = combine(info, chosen, back_rows, 0, 2, gate_dots)
+            back_first = chips_first(back_keep, got)
+            acts = after(acts, *back_first)
+            back_flips = send_chips(back_first)
+        slots = expert_grads(acts, token_rows[e], grad_row)
+        reduced_in = (slots,)
+        if e:
+            slots = after(slots, reduced[-1])
+        reduced.append(lax.psum_scatter(slots, "cols", scatter_dimension=0, tiled=False))
 
     if fast:
-        back_keep = combine(info, chosen, back_rows, 0, 2, gate_dots)
-        back_first = chips_first(back_keep, got)
-        sent_second = reduce_second(grad_slots[0][2], grad_slots[0][3], marks[0][0])
-        back_parts = chips_second(back_keep, got, *send_chips(back_first))
+        back_parts = chips_second(back_keep, got, *after(back_flips, slots))
         out_rows = [after(a, back_parts[1], back_parts[4]) for a in out_rows]
         out_got = flip(combine(info, chosen, out_rows, 1, 2), 1)
         out_keep = combine(info, chosen, out_rows, 0, 2)
-        far_back = lax.ppermute(
-            after(grad_slots[0][3], *sent_second, out_keep), "cols", FAR
-        )
-        reduced.append((grad_slots[0][0], (marks[0][0], far_back), sent_second))
-        back_parts = after(back_parts, out_keep, out_got)
+        back_parts = after(back_parts, out_keep, out_got, slots, reduced[0])
     else:
         spread_dots = spread(place_rows, gate_dots)
         grad_shares = lax.all_to_all(spread_dots, "rows", split_axis=0, concat_axis=0, tiled=True)
@@ -1371,8 +1308,6 @@
         out_refs,
     )
     if fast:
-        relay, _ = reduce_first(after(grad_slots[1][1], far_back, grad_heads), fourth, chain=True)
-        marks.append((relay,))
         out_first = chips_first(out_keep, out_got)
         out_flips = send_chips(out_first)
         grad_heads = after(grad_heads, *out_first)
@@ -1403,9 +1338,7 @@
             ((0, 2, query_part), (0, 3, 2 * key_part), (1, 4, query_part)),
             extra,
         )
-        send = after(send, marks[1][0])
         sent = flip(send, 1)
-        sent_second = reduce_second(grad_slots[1][2], grad_slots[1][3], marks[1][0])
         grad_pair = after(grad_pair, keep)
     tokens_grad, attention_gain_grad = token_back(
         info, grad_query, grad_pair, tokens, grad_residual, attention_scale, query_refs, pair_refs
@@ -1414,14 +1347,10 @@
     if fast:
         sent_first = chips_first(keep, sent)
         sent_chips = send_chips(sent_first)
-        far_back = lax.ppermute(
-            after(grad_slots[1][3], *sent_second, tokens_grad, *sent_first), "cols", FAR
-        )
-        reduced.append((grad_slots[1][0], (marks[1][0], far_back), sent_second))
         mixture = chips_second(out_keep, out_got, *out_flips)
         slots = sum_parts(chips_second(keep, sent, *sent_chips))
         width = query_part + 2 * key_part
-        own_slots = [packed, *others]
+        own_slots = own
         gain_sums = sum(
             jnp.sum(own_slots[i][:depth, :width].astype(WIDE) * slots[i, :depth, :width], axis=1)
             for i in range(4)
@@ -1440,7 +1369,6 @@
             return reduce_last(slots[0], sent_first, sent_second)
 
         sums = cols_sum(slots)
-        expert_sums = [reduce_last(*parts) for parts in reduced]
         router_sum = sums[depth : depth + router_part, :depth].T
         experts_gain_sum = sums[depth + router_part, :gain_part]
         attention_gain_sum = sums[depth + router_part + 1, :gain_part]
@@ -1460,7 +1388,6 @@
         )
         row_sums = lax.psum_scatter(packed_grad, "rows", scatter_dimension=0)
         sums = lax.psum_scatter(row_sums, "cols", scatter_dimension=1).astype(WIDE)
-        expert_sums = reduced
         small_grads = jnp.concatenate(
             [
                 attention_gain_grad.reshape(-1, gain_part),
@@ -1485,6 +1412,7 @@
     value_at = key_at + key_part
     out_at = value_at + key_part
     part = down_weight.shape[1]
+    expert_sums = [block.astype(WIDE) for block in reduced]
     gate_grad, upward_grad, down_grad = (
         jnp.stack([sums_of[which * part : (which + 1) * part] for sums_of in expert_sums])
         for which in range(3)

time: 818 us -> 837 us (1.023)
  waiting for transfers between devices: 264 us -> 372 us
  starting transfers between devices: 101 us -> 59.2 us
  Pallas kernels: 293 us -> 277 us
  blocking collectives: 12.4 us -> 0 us
  other arithmetic: 71 us -> 59.7 us
    ppermute x35 -> x39, waiting for transfers between devices: 122 us -> 178 us  [flip(): return lax.ppermute(block, 'rows', [(i, i ^ bit) for i in range(count)])]
    ppermute x1, waiting for transfers between devices: 0.01 us -> 49.4 us  [on_device(): partner = lax.ppermute(own_pair, 'cols', pairs)]
    reduce_scatter x0 -> x2, waiting for transfers between devices: none -> 47 us  [on_device(): lax.psum_scatter(slots, 'cols', scatter_dimension=0, tiled=False)]
    ppermute x3 -> x1, waiting for transfers between devices: 37 us -> 4.42 us  [reduce_second(): lax.ppermute(downward_load, 'cols', DOWN)]
    pallas_call x13 -> x11, Pallas kernels: 93.6 us -> 77.5 us  [the longest x8 35.9 us: dispatch(): pl.pallas_call(functools.partial(dispatch_kernel, local), grid=(D // wide...]
    ppermute x3 -> x1, starting transfers between devices: 18.3 us -> 3.21 us  [reduce_first(): return (relay, lax.ppermute(fourth, 'cols', FAR))]
    all_gather x1 -> x2, waiting for transfers between devices: 0.02 us -> 13.2 us  [on_device(): expert_weights.append(lax.all_gather(block, 'cols', axis=0))]
    all_gather x1 -> x0, blocking collectives: 12.4 us -> none  [on_device(): routes_all = lax.all_gather(routes.T, 'rows', axis=0)]
  transfers between devices with their start and end apart: 62 -> 53, of which waited for: 33 -> 29; matrix products, arithmetic and copies ran while one was open for 11% -> 10% of each run, Pallas kernels for 34% -> 32%
where the time goes in v10:
time: 837 us; the launch traced here: 829 us
  waiting for transfers between devices  372 us (44%)
  Pallas kernels  277 us (33%)
  other arithmetic  59.7 us (7%)
  starting transfers between devices  59.2 us (7%)
  local copies, waits for them, and re-layouts  45.7 us (5%)
  between operations  15 us (2%)
    ppermute x39, waiting for transfers between devices, flip(): return lax.ppermute(block, 'rows', [(i, i ^ bit) for i in range(count)])  178 us
    pallas_call x2, Pallas kernels, expert(): pl.pallas_call(functools.partial(expert_kernel, slots), grid=(height // E...  61.5 us
    ppermute x1, waiting for transfers between devices, on_device(): partner = lax.ppermute(own_pair, 'cols', pairs)  49.4 us
    reduce_scatter x2, waiting for transfers between devices, on_device(): lax.psum_scatter(slots, 'cols', scatter_dimension=0, tiled=False)  47 us
    pallas_call x8, Pallas kernels, dispatch(): pl.pallas_call(functools.partial(dispatch_kernel, local), grid=(D // wide...  35.9 us
    pallas_call x4, Pallas kernels, combine(): pl.pallas_call(functools.partial(combine_kernel, len(rows)), grid=(number...  31.5 us
    pallas_call x2, Pallas kernels, expert_grads(): pl.pallas_call(expert_grads_kernel, grid=(D // 256,), out_shape=jax.Shape...  29.4 us
    ppermute x39, starting transfers between devices, flip(): return lax.ppermute(block, 'rows', [(i, i ^ bit) for i in range(count)])  27.4 us
  transfers between devices with their start and end apart: 53, of which 29 were waited for; matrix products, arithmetic and copies ran while one was open for 10% of the time, Pallas kernels for 32%

profile of v10, /device:TPU:0, one launch (start us, length us, event | category | flops | bytes accessed | tf_op | source)
XLA Modules:
  0.0 828.7 jit_solution(16192838290006170227)
XLA Ops:
  23.3 5.6 collective-permute-start.3
  32.3 14.4 %collective-permute-done.3 = bf16[208,896]{1,0:T(8,128)(2,1)} collective-permute-done((bf16[208,896]{1,0:T(8,128)(2,1)S(1)}, bf16[208,896]{1,0:T(8,128)(2,1)}, u32[]{:S(2)}, u32[]{:S(2)}) %collective-permute-start.3) | collective-permute-done | bytes 372768 | tf_op jit(solution)/shard_map/ppermute | solution.py:980
  46.7 14.6 %collective-permute-done.1 = bf16[208,896]{1,0:T(8,128)(2,1)} collective-permute-done((bf16[208,896]{1,0:T(8,128)(2,1)S(1)}, bf16[208,896]{1,0:T(8,128)(2,1)}, u32[]{:S(2)}, u32[]{:S(2)}) %collective-permute-start.1) | collective-permute-done | bytes 372768 | tf_op jit(solution)/shard_map/ppermute | solution.py:976
  61.3 4.9 collective-permute-done
  71.3 23.2 %collective-permute-done.2 = bf16[208,896]{1,0:T(8,128)(2,1)} collective-permute-done((bf16[208,896]{1,0:T(8,128)(2,1)}, bf16[208,896]{1,0:T(8,128)(2,1)}, u32[]{:S(2)}, u32[]{:S(2)}) %collective-permute-start.2) | collective-permute-done | bytes 372768 | tf_op jit(solution)/shard_map/ppermute | solution.py:987
  97.0 32.8 %collective-permute-done.8.rest_3_.rest_9_.rest_12_ = bf16[4,208,896]{2,1,0:T(8,128)(2,1)S(1)} collective-permute-done((bf16[4,208,896]{2,1,0:T(8,128)(2,1)S(1)}, bf16[4,208,896]{2,1,0:T(8,128)(2,1)S(1)}, u32[]{:S(2)}, u32[]{:S(2)}) %collective-permute-start.8) | collective-permute-done | bytes 1490976 | tf_op jit(solution)/shard_map/ppermute | solution.py:1035
  134.9 17.0 %collective-permute-done.10.rest_5_.rest_11_.rest_14_ = bf16[2,208,896]{2,1,0:T(8,128)(2,1)} collective-permute-done((bf16[2,208,896]{2,1,0:T(8,128)(2,1)S(1)}, bf16[2,208,896]{2,1,0:T(8,128)(2,1)}, u32[]{:S(2)}, u32[]{:S(2)}) %collective-permute-start.10) | collective-permute-done | bytes 745504 | tf_op jit(solution)/shard_map/ppermute | solution.py:1035
  153.8 13.2 %all-gather.5.cloned.1.call-done = bf16[2304,1536]{1,0:T(8,128)(2,1)} async-done(((bf16[576,1536]{1,0:T(8,128)(2,1)}), bf16[2304,1536]{1,0:T(8,128)(2,1)}) %all-gather.5.cloned.1.call-update) | async-done | bytes 7077904 | tf_op jit(solution)/shard_map/all_gather | solution.py:1136
  173.1 5.6 norm_key_value.1
  181.9 17.8 %collective-permute-done.14 = bf16[256,1536]{1,0:T(8,128)(2,1)S(1)} collective-permute-done((bf16[256,1536]{1,0:T(8,128)(2,1)S(1)}, bf16[256,1536]{1,0:T(8,128)(2,1)S(1)}, u32[]{:S(2)}, u32[]{:S(2)}) %collective-permute-start.14) | collective-permute-done | bytes 786464 | tf_op jit(solution)/shard_map/ppermute | solution.py:1035
  203.4 8.9 %query_projection.1.queries = bf16[512,1536]{1,0:T(8,128)(2,1)} custom-call(s32[16]{0:T(128)} %concatenate.42.info, bf16[512,1536]{1,0:T(8,128)(2,1)} %get-tuple-element.108.normed.rest_0_, f32[512,128]{1,0:T(8,128)} %get-tuple-element.284.cosine, f32[512,128]{1,0:T(8,128)} %get-tuple-element.285.sine, bf16[4,208,896]{2,1,0:T(8,128)(2,1)} %copy-done.1, ...), custom_call_target="tpu_custom_call" | custom-call | flops 1 | bytes 1 | tf_op jit(solution)/shard_map/query_projection/pallas_call | solution.py:192
  213.0 49.4 %collective-permute-done.16.partner = bf16[512,512]{1,0:T(8,128)(2,1)} collective-permute-done((bf16[512,512]{1,0:T(8,128)(2,1)}, bf16[512,512]{1,0:T(8,128)(2,1)}, u32[]{:S(2)}, u32[]{:S(2)}) %collective-permute-start.16) | collective-permute-done | bytes 524320 | tf_op jit(solution)/shard_map/ppermute | solution.py:1207
  262.3 11.0 %tree_attention.1.heads.rest_1_ = bf16[512,1536]{1,0:T(8,128)(2,1)} custom-call(s32[16]{0:T(128)} %concatenate.42.info, bf16[512,1536]{1,0:T(8,128)(2,1)} %query_projection.1.queries, bf16[512,512]{1,0:T(8,128)(2,1)} %get-tuple-element.109.own, bf16[512,512]{1,0:T(8,128)(2,1)} %collective-permute-done.16.partner), custom_call_target="tpu_custom_call" | custom-call | flops 1 | bytes 1 | tf_op jit(solution)/shard_map/tree_attention/pallas_call | solution.py:274
  273.3 10.8 %out_projection.1 = (f32[512,1536]{1,0:T(8,128)}, bf16[512,1536]{1,0:T(8,128)(2,1)}) custom-call(s32[16]{0:T(128)} %concatenate.42.info, bf16[512,1536]{1,0:T(8,128)(2,1)} %tree_attention.1.heads.rest_1_, bf16[512,1536]{1,0:T(8,128)(2,1)} %tokens.5, f32[1,1536]{1,0:T(1,128)} %reshape.424.gain, bf16[4,208,896]{2,1,0:T(8,128)(2,1)} %copy-done.1, ...), custom_call_target="tpu_custom_call" | custom-call | flops 1 | bytes 1 | tf_op jit(solution)/shard_map/out_projection/pallas_call | solution.py:386
  293.8 5.6 route_tables.1
  302.6 4.5 dispatch.8
  307.1 4.5 dispatch.9
  311.6 9.6 %collective-permute-done.22.rows = bf16[512,1536]{1,0:T(8,128)(2,1)S(1)} collective-permute-done((bf16[512,1536]{1,0:T(8,128)(2,1)}, bf16[512,1536]{1,0:T(8,128)(2,1)S(1)}, u32[]{:S(2)}, u32[]{:S(2)}) %collective-permute-start.22) | collective-permute-done | bytes 1572896 | tf_op jit(solution)/shard_map/ppermute | solution.py:1035
  329.3 12.2 %pick_rows.1 = (bf16[8,160,1536]{2,1,0:T(8,128)(2,1)}, bf16[8,160,1536]{2,1,0:T(8,128)(2,1)}) custom-call(bf16[8,320,512]{2,1,0:T(8,128)(2,1)} %get-tuple-element.115.chosen, bf16[512,1536]{1,0:T(8,128)(2,1)} %cotangent.1, bf16[512,1536]{1,0:T(8,128)(2,1)} %collective-permute-done.17.rest_1_, bf16[512,1536]{1,0:T(8,128)(2,1)} %collective-permute-done.4.rest_2_, ...), custom_call_target="tpu_custom_call" | custom-call | flops 1 | bytes 1 | tf_op jit(solution)/shard_map/pick_rows/pallas_call | solution.py:462
  341.5 4.5 dispatch.10
  346.0 4.5 dispatch.11
  350.5 4.5 dispatch.12
  356.2 4.4 dispatch.13
  361.9 4.5 dispatch.14
  367.5 4.5 dispatch.15
  372.0 30.2 %expert.2 = (bf16[1280,1536]{1,0:T(8,128)(2,1)}, bf16[1280,1536]{1,0:T(8,128)(2,1)}, bf16[1280,1536]{1,0:T(8,128)(2,1)}, bf16[4,576,1280]{2,1,0:T(8,128)(2,1)}, f32[1280,1]{1,0:T(8,128)}) custom-call(bf16[1280,1536]{1,0:T(8,128)(2,1)} %bitcast.163, bf16[1280,1536]{1,0:T(8,128)(2,1)} %bitcast.184, f32[1280,1]{1,0:T(8,128)} %bitcast.167, ...), custom_call_target="tpu_custom_call" | custom-call | flops 1 | bytes 1 | tf_op jit(solution)/shard_map/expert/pallas_call | solution.py:618
  402.2 14.6 %expert_gradients.2 = bf16[4,576,1536]{2,1,0:T(8,128)(2,1)} custom-call(bf16[4,576,1280]{2,1,0:T(8,128)(2,1)} %get-tuple-element.161.acts, bf16[1280,1536]{1,0:T(8,128)(2,1)} %bitcast.164, bf16[1280,1536]{1,0:T(8,128)(2,1)} %get-tuple-element.162.grads), custom_call_target="tpu_custom_call" | custom-call | flops 1 | bytes 1 | tf_op jit(solution)/shard_map/expert_gradients/pallas_call | solution.py:647
  416.9 31.3 %expert.3 = (bf16[1280,1536]{1,0:T(8,128)(2,1)}, bf16[1280,1536]{1,0:T(8,128)(2,1)}, bf16[1280,1536]{1,0:T(8,128)(2,1)}, bf16[4,576,1280]{2,1,0:T(8,128)(2,1)}, f32[1280,1]{1,0:T(8,128)}) custom-call(bf16[1280,1536]{1,0:T(8,128)(2,1)} %bitcast.165, bf16[1280,1536]{1,0:T(8,128)(2,1)} %bitcast.183, f32[1280,1]{1,0:T(8,128)} %bitcast.168, ...), custom_call_target="tpu_custom_call" | custom-call | flops 1 | bytes 1 | tf_op jit(solution)/shard_map/expert/pallas_call | solution.py:618
  448.2 7.8 combine.5
  456.0 7.7 combine.4
  467.0 5.2 add_convert_fusion.7
  476.0 14.8 %expert_gradients.3 = bf16[4,576,1536]{2,1,0:T(8,128)(2,1)} custom-call(bf16[4,576,1280]{2,1,0:T(8,128)(2,1)} %get-tuple-element.170.acts, bf16[1280,1536]{1,0:T(8,128)(2,1)} %bitcast.166, bf16[1280,1536]{1,0:T(8,128)(2,1)} %get-tuple-element.171.grads), custom_call_target="tpu_custom_call" | custom-call | flops 1 | bytes 1 | tf_op jit(solution)/shard_map/expert_gradients/pallas_call | solution.py:647
  490.8 47.0 %reduce-scatter.3.cloned.1.call-done = bf16[1,576,1536]{2,1,0:T(8,128)(2,1)} async-done(((bf16[4,576,1536]{2,1,0:T(8,128)(2,1)}), bf16[1,576,1536]{2,1,0:T(8,128)(2,1)}) %reduce-scatter.3.cloned.1.call-update) | async-done | bytes 1769488 | tf_op jit(solution)/shard_map/reduce_scatter | solution.py:1280
  540.0 7.5 combine.7
  547.6 8.5 %combine.6 = bf16[4,512,1536]{2,1,0:T(8,128)(2,1)} custom-call(s32[16]{0:T(128)} %concatenate.42.info, bf16[8,320,512]{2,1,0:T(8,128)(2,1)} %get-tuple-element.115.chosen, bf16[8,160,1536]{2,1,0:T(8,128)(2,1)} %bitcast.174, bf16[8,160,1536]{2,1,0:T(8,128)(2,1)} %bitcast.176), custom_call_target="tpu_custom_call" | custom-call | flops 1 | bytes 1 | tf_op jit(solution)/shard_map/combine/pallas_call | solution.py:684
  567.3 4.3 fusion.10
  572.8 47.3 %collective-permute-done.38.rest_5_ = bf16[272,1536]{1,0:T(8,128)(2,1)S(1)} collective-permute-done((bf16[272,1536]{1,0:T(8,128)(2,1)S(1)}, bf16[272,1536]{1,0:T(8,128)(2,1)S(1)}, u32[]{:S(2)}, u32[]{:S(2)}) %collective-permute-start.38) | collective-permute-done | bytes 835616 | tf_op jit(solution)/shard_map/ppermute | solution.py:1035
  621.3 13.5 %experts_norm_back.1 = (f32[512,1536]{1,0:T(8,128)}, bf16[512,1536]{1,0:T(8,128)(2,1)}, bf16[512,1536]{1,0:T(8,128)(2,1)}, f32[1,1536]{1,0:T(1,128)}, f32[16,1536]{1,0:T(8,128)}) custom-call(s32[16]{0:T(128)} %concatenate.42.info, f32[512,1536]{1,0:T(8,128)} %get-tuple-element.114.residual, bf16[512,1536]{1,0:T(8,128)(2,1)} %get-tuple-element.116.rows.normed, ...), custom_call_target="tpu_custom_call" | custom-call | flops 1 | bytes 1 | tf_op jit(solution)/shard_map/experts_norm_back/pallas_call | solution.py:771
  634.9 15.4 %tree_attention_back.1 = (bf16[512,1536]{1,0:T(8,128)(2,1)}, f32[512,512]{1,0:T(8,128)}, f32[512,512]{1,0:T(8,128)}) custom-call(s32[16]{0:T(128)} %concatenate.42.info, bf16[512,1536]{1,0:T(8,128)(2,1)} %query_projection.1.queries, bf16[512,512]{1,0:T(8,128)(2,1)} %get-tuple-element.109.own, bf16[512,512]{1,0:T(8,128)(2,1)} %collective-permute-done.16.partner, ...), custom_call_target="tpu_custom_call" | custom-call | flops 1 | bytes 1 | tf_op jit(solution)/shard_map/tree_attention_back/pallas_call | solution.py:335
  656.5 21.6 %collective-permute-done.39.arrived = bf16[512,512]{1,0:T(8,128)(2,1)S(1)} collective-permute-done((bf16[512,512]{1,0:T(8,128)(2,1)S(1)}, bf16[512,512]{1,0:T(8,128)(2,1)S(1)}, u32[]{:S(2)}, u32[]{:S(2)}) %collective-permute-start.39) | collective-permute-done | bytes 524320 | tf_op jit(solution)/shard_map/ppermute | solution.py:1330
  682.1 16.1 %weight_gradients.1 = (bf16[4,4,208,896]{3,2,1,0:T(8,128)(2,1)}, bf16[4,4,208,896]{3,2,1,0:T(8,128)(2,1)}) custom-call(s32[16]{0:T(128)} %concatenate.42.info, bf16[512,1536]{1,0:T(8,128)(2,1)} %get-tuple-element.108.normed.rest_0_, bf16[512,1536]{1,0:T(8,128)(2,1)} %tree_attention.1.heads.rest_1_, bf16[512,1536]{1,0:T(8,128)(2,1)} %get-tuple-element.186.rest_2_.grad_query, ...), custom_call_target="tpu_custom_call" | custom-call | flops 1 | bytes 1 | tf_op jit(solution)/shard_map/weight_gradients/pallas_call | solution.py:923
  700.1 8.1 collective-permute-done.40
  724.3 13.3 %token_gradient.1 = (bf16[512,1536]{1,0:T(8,128)(2,1)}, f32[1,1536]{1,0:T(1,128)}) custom-call(s32[16]{0:T(128)} %concatenate.42.info, bf16[512,1536]{1,0:T(8,128)(2,1)} %get-tuple-element.186.rest_2_.grad_query, bf16[512,512]{1,0:T(8,128)(2,1)} %join_key_value_gradients.1.rest_3_.grad_pair, bf16[512,1536]{1,0:T(8,128)(2,1)} %tokens.5, ...), custom_call_target="tpu_custom_call" | custom-call | flops 1 | bytes 1 | tf_op jit(solution)/shard_map/token_gradient/pallas_call | solution.py:862
  737.7 11.1 %collective-permute-done.43 = bf16[2,2,208,896]{3,2,1,0:T(8,128)(2,1)S(1)} collective-permute-done((bf16[2,2,208,896]{3,2,1,0:T(8,128)(2,1)}, bf16[2,2,208,896]{3,2,1,0:T(8,128)(2,1)S(1)}, u32[]{:S(2)}, u32[]{:S(2)}) %collective-permute-start.43) | collective-permute-done | bytes 1490976 | tf_op jit(solution)/shard_map/ppermute | solution.py:1035
  756.3 9.4 %collective-permute-done.34 = bf16[256,1536]{1,0:T(8,128)(2,1)} collective-permute-done((bf16[256,1536]{1,0:T(8,128)(2,1)}, bf16[256,1536]{1,0:T(8,128)(2,1)}, u32[]{:S(2)}, u32[]{:S(2)}) %collective-permute-start.34) | collective-permute-done | bytes 786464 | tf_op jit(solution)/shard_map/ppermute | solution.py:1035
  772.5 8.3 collective-permute-done.42
  798.4 10.4 %collective-permute-start.46 = (bf16[208,896]{1,0:T(8,128)(2,1)S(1)}, bf16[208,896]{1,0:T(8,128)(2,1)S(1)}, u32[]{:S(2)}, u32[]{:S(2)}) collective-permute-start(bf16[208,896]{1,0:T(8,128)(2,1)S(1)} %get-tuple-element.255), channel_id=1, source_target_pairs={{0,1},{1,2},{2,3},{4,5},{5,6},{6,7},{8,9},{9,10},{10,11},{12,13},{... | collective-permute-start | bytes 1118216 | tf_op jit(solution)/shard_map/ppermute | solution.py:1015
  813.8 4.4 collective-permute-done.47
  (316 shorter events, 163.4 us)
Async XLA Ops:
  7.2 159.8 %all-gather.5.cloned.1.call-start = ((), (), s32[]{:S(2)}) async-start(), calls=%async_computation.4 | async-start | bytes 8847360 | tf_op jit(solution)/shard_map/all_gather | solution.py:1136
  12.1 404.8 %all-gather.7.cloned.1.call-start = ((), (), s32[]{:S(2)}) async-start(), calls=%async_computation.5 | async-start | bytes 8847360 | tf_op jit(solution)/shard_map/all_gather | solution.py:1136
  13.4 82.3 %collective-permute-start.5 = (bf16[512,1536]{1,0:T(8,128)(2,1)S(1)}, bf16[512,1536]{1,0:T(8,128)(2,1)S(1)}, u32[]{:S(2)}, u32[]{:S(2)}) collective-permute-start(bf16[512,1536]{1,0:T(8,128)(2,1)S(1)} %copy-done.9), channel_id=1, source_target_pairs={{0,16},{4,20},{8,24},{12,28},{16,0},{20,4},{24,8},{28,12},{1,17},{... | collective-permute-start | bytes 4718600 | tf_op jit(solution)/shard_map/ppermute | solution.py:1035
  16.4 79.3 %collective-permute-start.4 = (bf16[512,1536]{1,0:T(8,128)(2,1)S(1)}, bf16[512,1536]{1,0:T(8,128)(2,1)}, u32[]{:S(2)}, u32[]{:S(2)}) collective-permute-start(bf16[512,1536]{1,0:T(8,128)(2,1)S(1)} %copy-done.9), channel_id=1, source_target_pairs={{0,8},{4,12},{8,0},{12,4},{16,24},{20,28},{24,16},{28,20},{1,9},{5... | collective-permute-start | bytes 4718600 | tf_op jit(solution)/shard_map/ppermute | solution.py:1035
  23.3 23.4 %collective-permute-start.3 = (bf16[208,896]{1,0:T(8,128)(2,1)S(1)}, bf16[208,896]{1,0:T(8,128)(2,1)}, u32[]{:S(2)}, u32[]{:S(2)}) collective-permute-start(bf16[208,896]{1,0:T(8,128)(2,1)S(1)} %concatenate.45), channel_id=1, source_target_pairs={{0,3},{3,0},{4,7},{7,4},{8,11},{11,8},{12,15},{15,12},{16,19},{19,... | collective-permute-start | bytes 1118216 | tf_op jit(solution)/shard_map/ppermute | solution.py:980
  28.9 32.4 %collective-permute-start.1 = (bf16[208,896]{1,0:T(8,128)(2,1)S(1)}, bf16[208,896]{1,0:T(8,128)(2,1)}, u32[]{:S(2)}, u32[]{:S(2)}) collective-permute-start(bf16[208,896]{1,0:T(8,128)(2,1)S(1)} %concatenate.45), channel_id=1, source_target_pairs={{0,1},{1,2},{2,3},{4,5},{5,6},{6,7},{8,9},{9,10},{10,11},{12,13},{... | collective-permute-start | bytes 1118216 | tf_op jit(solution)/shard_map/ppermute | solution.py:976
  31.0 35.2 %collective-permute-start = (bf16[208,896]{1,0:T(8,128)(2,1)S(1)}, bf16[208,896]{1,0:T(8,128)(2,1)}, u32[]{:S(2)}, u32[]{:S(2)}) collective-permute-start(bf16[208,896]{1,0:T(8,128)(2,1)S(1)} %concatenate.45), channel_id=1, source_target_pairs={{1,0},{2,1},{3,2},{5,4},{6,5},{7,6},{9,8},{10,9},{11,10},{13,12},{... | collective-permute-start | bytes 1118216 | tf_op jit(solution)/shard_map/ppermute | solution.py:976
  68.4 26.1 %collective-permute-start.2 = (bf16[208,896]{1,0:T(8,128)(2,1)}, bf16[208,896]{1,0:T(8,128)(2,1)}, u32[]{:S(2)}, u32[]{:S(2)}) collective-permute-start(bf16[208,896]{1,0:T(8,128)(2,1)} %get-tuple-element.278), channel_id=1, source_target_pairs={{3,1},{1,0},{0,2},{2,3},{7,5},{5,4},{4,6},{6,7},{11,9},{9,8},{8,10... | collective-permute-start | bytes 1118216 | tf_op jit(solution)/shard_map/ppermute | solution.py:987
  95.8 34.0 %collective-permute-start.8 = (bf16[4,208,896]{2,1,0:T(8,128)(2,1)S(1)}, bf16[4,208,896]{2,1,0:T(8,128)(2,1)S(1)}, u32[]{:S(2)}, u32[]{:S(2)}) collective-permute-start(bf16[4,208,896]{2,1,0:T(8,128)(2,1)S(1)} %pad_maximum_fusion.8.rest_0_.rest_6_.rest_9_), channel_id=1, source_target_pairs={{0,16},{4,20},{8,24},{12,28},{16,0},{20,4},{24,8},{28,12},{1,17},{... | collective-permute-start | bytes 4472840 | tf_op jit(solution)/shard_map/ppermute | solution.py:1035
  96.8 33.7 %collective-permute-start.7 = (bf16[4,208,896]{2,1,0:T(8,128)(2,1)S(1)}, bf16[4,208,896]{2,1,0:T(8,128)(2,1)S(1)}, u32[]{:S(2)}, u32[]{:S(2)}) collective-permute-start(bf16[4,208,896]{2,1,0:T(8,128)(2,1)S(1)} %pad_maximum_fusion.8.rest_0_.rest_6_.rest_9_), channel_id=1, source_target_pairs={{0,8},{4,12},{8,0},{12,4},{16,24},{20,28},{24,16},{28,20},{1,9},{5... | collective-permute-start | bytes 4472840 | tf_op jit(solution)/shard_map/ppermute | solution.py:1035
  97.0 33.6 %collective-permute-start.6 = (bf16[4,208,896]{2,1,0:T(8,128)(2,1)S(1)}, bf16[4,208,896]{2,1,0:T(8,128)(2,1)}, u32[]{:S(2)}, u32[]{:S(2)}) collective-permute-start(bf16[4,208,896]{2,1,0:T(8,128)(2,1)S(1)} %pad_maximum_fusion.8.rest_0_.rest_6_.rest_9_), channel_id=1, source_target_pairs={{0,4},{4,0},{8,12},{12,8},{16,20},{20,16},{24,28},{28,24},{1,5},{5... | collective-permute-start | bytes 4472840 | tf_op jit(solution)/shard_map/ppermute | solution.py:1035
  132.6 34.5 %collective-permute-start.11 = (bf16[8,208,896]{2,1,0:T(8,128)(2,1)}, bf16[8,208,896]{2,1,0:T(8,128)(2,1)S(1)}, u32[]{:S(2)}, u32[]{:S(2)}) collective-permute-start(bf16[8,208,896]{2,1,0:T(8,128)(2,1)} %pad_maximum_fusion), channel_id=1, source_target_pairs={{0,4},{4,0},{8,12},{12,8},{16,20},{20,16},{24,28},{28,24},{1,5},{5... | collective-permute-start | bytes 8945672 | tf_op jit(solution)/shard_map/ppermute | solution.py:1035
  132.7 19.2 %collective-permute-start.10 = (bf16[2,208,896]{2,1,0:T(8,128)(2,1)S(1)}, bf16[2,208,896]{2,1,0:T(8,128)(2,1)}, u32[]{:S(2)}, u32[]{:S(2)}) collective-permute-start(bf16[2,208,896]{2,1,0:T(8,128)(2,1)S(1)} %slice.492), channel_id=1, source_target_pairs={{0,8},{4,12},{8,0},{12,4},{16,24},{20,28},{24,16},{28,20},{1,9},{5... | collective-permute-start | bytes 2236424 | tf_op jit(solution)/shard_map/ppermute | solution.py:1035
  133.3 18.9 %collective-permute-start.9 = (bf16[2,208,896]{2,1,0:T(8,128)(2,1)S(1)}, bf16[2,208,896]{2,1,0:T(8,128)(2,1)}, u32[]{:S(2)}, u32[]{:S(2)}) collective-permute-start(bf16[2,208,896]{2,1,0:T(8,128)(2,1)S(1)} %slice.491), channel_id=1, source_target_pairs={{0,16},{4,20},{8,24},{12,28},{16,0},{20,4},{24,8},{28,12},{1,17},{... | collective-permute-start | bytes 2236424 | tf_op jit(solution)/shard_map/ppermute | solution.py:1035
  151.9 15.1 %collective-permute-start.13 = (bf16[2,208,896]{2,1,0:T(8,128)(2,1)}, bf16[2,208,896]{2,1,0:T(8,128)(2,1)}, u32[]{:S(2)}, u32[]{:S(2)}) collective-permute-start(bf16[2,208,896]{2,1,0:T(8,128)(2,1)} %collective-permute-done.10.rest_5_.rest_11_.rest_14_), channel_id=1, source_target_pairs={{0,4},{4,0},{8,12},{12,8},{16,20},{20,16},{24,28},{28,24},{1,5},{5... | collective-permute-start | bytes 2236424 | tf_op jit(solution)/shard_map/ppermute | solution.py:1035
  152.2 14.8 %collective-permute-start.12 = (bf16[2,208,896]{2,1,0:T(8,128)(2,1)}, bf16[2,208,896]{2,1,0:T(8,128)(2,1)}, u32[]{:S(2)}, u32[]{:S(2)}) collective-permute-start(bf16[2,208,896]{2,1,0:T(8,128)(2,1)} %collective-permute-done.9.rest_4_.rest_10_.rest_13_), channel_id=1, source_target_pairs={{0,4},{4,0},{8,12},{12,8},{16,20},{20,16},{24,28},{28,24},{1,5},{5... | collective-permute-start | bytes 2236424 | tf_op jit(solution)/shard_map/ppermute | solution.py:1035
  167.0 370.8 %reduce-scatter.3.cloned.1.call-start = ((), (), s32[]{:S(2)}) async-start(), calls=%async_computation.2 | async-start | bytes 8847360 | tf_op jit(solution)/shard_map/reduce_scatter | solution.py:1280
  180.2 19.5 %collective-permute-start.14 = (bf16[256,1536]{1,0:T(8,128)(2,1)S(1)}, bf16[256,1536]{1,0:T(8,128)(2,1)S(1)}, u32[]{:S(2)}, u32[]{:S(2)}) collective-permute-start(bf16[256,1536]{1,0:T(8,128)(2,1)S(1)} %slice.494), channel_id=1, source_target_pairs={{0,16},{4,20},{8,24},{12,28},{16,0},{20,4},{24,8},{28,12},{1,17},{... | collective-permute-start | bytes 2359304 | tf_op jit(solution)/shard_map/ppermute | solution.py:1035
  180.9 19.8 %collective-permute-start.15 = (bf16[256,1536]{1,0:T(8,128)(2,1)S(1)}, bf16[256,1536]{1,0:T(8,128)(2,1)S(1)}, u32[]{:S(2)}, u32[]{:S(2)}) collective-permute-start(bf16[256,1536]{1,0:T(8,128)(2,1)S(1)} %slice.495), channel_id=1, source_target_pairs={{0,8},{4,12},{8,0},{12,4},{16,24},{20,28},{24,16},{28,20},{1,9},{5... | collective-permute-start | bytes 2359304 | tf_op jit(solution)/shard_map/ppermute | solution.py:1035
  181.4 91.9 %collective-permute-start.17 = (bf16[512,1536]{1,0:T(8,128)(2,1)S(1)}, bf16[512,1536]{1,0:T(8,128)(2,1)}, u32[]{:S(2)}, u32[]{:S(2)}) collective-permute-start(bf16[512,1536]{1,0:T(8,128)(2,1)S(1)} %copy-done.10), channel_id=1, source_target_pairs={{0,4},{4,0},{8,12},{12,8},{16,20},{20,16},{24,28},{28,24},{1,5},{5... | collective-permute-start | bytes 4718600 | tf_op jit(solution)/shard_map/ppermute | solution.py:1035
  181.4 91.9 %collective-permute-start.18 = (bf16[512,1536]{1,0:T(8,128)(2,1)}, bf16[512,1536]{1,0:T(8,128)(2,1)}, u32[]{:S(2)}, u32[]{:S(2)}) collective-permute-start(bf16[512,1536]{1,0:T(8,128)(2,1)} %collective-permute-done.4.rest_2_), channel_id=1, source_target_pairs={{0,4},{4,0},{8,12},{12,8},{16,20},{20,16},{24,28},{28,24},{1,5},{5... | collective-permute-start | bytes 4718600 | tf_op jit(solution)/shard_map/ppermute | solution.py:1035
  181.9 91.4 %collective-permute-start.19 = (bf16[512,1536]{1,0:T(8,128)(2,1)S(1)}, bf16[512,1536]{1,0:T(8,128)(2,1)}, u32[]{:S(2)}, u32[]{:S(2)}) collective-permute-start(bf16[512,1536]{1,0:T(8,128)(2,1)S(1)} %copy-done.15), channel_id=1, source_target_pairs={{0,4},{4,0},{8,12},{12,8},{16,20},{20,16},{24,28},{28,24},{1,5},{5... | collective-permute-start | bytes 4718600 | tf_op jit(solution)/shard_map/ppermute | solution.py:1035
  201.6 71.7 %collective-permute-start.20 = (bf16[512,1536]{1,0:T(8,128)(2,1)}, bf16[512,1536]{1,0:T(8,128)(2,1)}, u32[]{:S(2)}, u32[]{:S(2)}) collective-permute-start(bf16[512,1536]{1,0:T(8,128)(2,1)} %constant_dynamic-update-slice_fusion.rest_6_), channel_id=1, source_target_pairs={{0,4},{4,0},{8,12},{12,8},{16,20},{20,16},{24,28},{28,24},{1,5},{5... | collective-permute-start | bytes 4718600 | tf_op jit(solution)/shard_map/ppermute | solution.py:1035
  201.6 60.7 %collective-permute-start.16 = (bf16[512,512]{1,0:T(8,128)(2,1)}, bf16[512,512]{1,0:T(8,128)(2,1)}, u32[]{:S(2)}, u32[]{:S(2)}) collective-permute-start(bf16[512,512]{1,0:T(8,128)(2,1)} %get-tuple-element.109.own), channel_id=1, source_target_pairs={{1,0},{3,2},{5,4},{7,6},{9,8},{11,10},{13,12},{15,14},{17,16},{19,... | collective-permute-start | bytes 1572872 | tf_op jit(solution)/shard_map/ppermute | solution.py:1207
  284.2 22.9 %collective-permute-start.23 = (bf16[512,1536]{1,0:T(8,128)(2,1)}, bf16[512,1536]{1,0:T(8,128)(2,1)}, u32[]{:S(2)}, u32[]{:S(2)}) collective-permute-start(bf16[512,1536]{1,0:T(8,128)(2,1)} %get-tuple-element.116.rows.normed), channel_id=1, source_target_pairs={{0,4},{4,0},{8,12},{12,8},{16,20},{20,16},{24,28},{28,24},{1,5},{5... | collective-permute-start | bytes 4718600 | tf_op jit(solution)/shard_map/ppermute | solution.py:1035
  284.4 36.9 %collective-permute-start.22 = (bf16[512,1536]{1,0:T(8,128)(2,1)}, bf16[512,1536]{1,0:T(8,128)(2,1)S(1)}, u32[]{:S(2)}, u32[]{:S(2)}) collective-permute-start(bf16[512,1536]{1,0:T(8,128)(2,1)} %get-tuple-element.116.rows.normed), channel_id=1, source_target_pairs={{0,16},{4,20},{8,24},{12,28},{16,0},{20,4},{24,8},{28,12},{1,17},{... | collective-permute-start | bytes 4718600 | tf_op jit(solution)/shard_map/ppermute | solution.py:1035
  285.9 36.6 %collective-permute-start.21 = (bf16[512,1536]{1,0:T(8,128)(2,1)}, bf16[512,1536]{1,0:T(8,128)(2,1)S(1)}, u32[]{:S(2)}, u32[]{:S(2)}) collective-permute-start(bf16[512,1536]{1,0:T(8,128)(2,1)} %get-tuple-element.116.rows.normed), channel_id=1, source_target_pairs={{0,8},{4,12},{8,0},{12,4},{16,24},{20,28},{24,16},{28,20},{1,9},{5... | collective-permute-start | bytes 4718600 | tf_op jit(solution)/shard_map/ppermute | solution.py:1035
  325.9 29.1 %collective-permute-start.27 = (bf16[512,1536]{1,0:T(8,128)(2,1)S(1)}, bf16[512,1536]{1,0:T(8,128)(2,1)S(1)}, u32[]{:S(2)}, u32[]{:S(2)}) collective-permute-start(bf16[512,1536]{1,0:T(8,128)(2,1)S(1)} %collective-permute-done.22.rows), channel_id=1, source_target_pairs={{0,4},{4,0},{8,12},{12,8},{16,20},{20,16},{24,28},{28,24},{1,5},{5... | collective-permute-start | bytes 4718600 | tf_op jit(solution)/shard_map/ppermute | solution.py:1035
  327.2 33.4 %collective-permute-start.25 = (bf16[256,1536]{1,0:T(8,128)(2,1)}, bf16[256,1536]{1,0:T(8,128)(2,1)S(1)}, u32[]{:S(2)}, u32[]{:S(2)}) collective-permute-start(bf16[256,1536]{1,0:T(8,128)(2,1)} %slice.510), channel_id=1, source_target_pairs={{0,8},{4,12},{8,0},{12,4},{16,24},{20,28},{24,16},{28,20},{1,9},{5... | collective-permute-start | bytes 2359304 | tf_op jit(solution)/shard_map/ppermute | solution.py:1035
  328.7 31.9 %collective-permute-start.24 = (bf16[256,1536]{1,0:T(8,128)(2,1)S(1)}, bf16[256,1536]{1,0:T(8,128)(2,1)S(1)}, u32[]{:S(2)}, u32[]{:S(2)}) collective-permute-start(bf16[256,1536]{1,0:T(8,128)(2,1)S(1)} %slice.509), channel_id=1, source_target_pairs={{0,16},{4,20},{8,24},{12,28},{16,0},{20,4},{24,8},{28,12},{1,17},{... | collective-permute-start | bytes 2359304 | tf_op jit(solution)/shard_map/ppermute | solution.py:1035
  416.9 373.2 %reduce-scatter.5.cloned.1.call-start = ((), (), s32[]{:S(2)}) async-start(), calls=%async_computation.3 | async-start | bytes 8847360 | tf_op jit(solution)/shard_map/reduce_scatter | solution.py:1280
  456.0 10.9 %collective-permute-start.29 = (bf16[4,544,1536]{2,1,0:T(8,128)(2,1)}, bf16[4,544,1536]{2,1,0:T(8,128)(2,1)S(1)}, u32[]{:S(2)}, u32[]{:S(2)}) collective-permute-start(bf16[4,544,1536]{2,1,0:T(8,128)(2,1)} %combine.5), channel_id=1, source_target_pairs={{0,4},{4,0},{8,12},{12,8},{16,20},{20,16},{24,28},{28,24},{1,5},{5... | collective-permute-start | bytes 20054024 | tf_op jit(solution)/shard_map/ppermute | solution.py:1035
  473.5 64.2 %collective-permute-start.30 = (bf16[2,272,1536]{2,1,0:T(8,128)(2,1)}, bf16[2,272,1536]{2,1,0:T(8,128)(2,1)S(1)}, u32[]{:S(2)}, u32[]{:S(2)}) collective-permute-start(bf16[2,272,1536]{2,1,0:T(8,128)(2,1)} %pad_maximum_fusion.4), channel_id=1, source_target_pairs={{0,8},{4,12},{8,0},{12,4},{16,24},{20,28},{24,16},{28,20},{1,9},{5... | collective-permute-start | bytes 5013512 | tf_op jit(solution)/shard_map/ppermute | solution.py:1035
  474.9 62.9 %collective-permute-start.31 = (bf16[2,272,1536]{2,1,0:T(8,128)(2,1)}, bf16[2,272,1536]{2,1,0:T(8,128)(2,1)S(1)}, u32[]{:S(2)}, u32[]{:S(2)}) collective-permute-start(bf16[2,272,1536]{2,1,0:T(8,128)(2,1)} %pad_maximum_fusion.5), channel_id=1, source_target_pairs={{0,16},{4,20},{8,24},{12,28},{16,0},{20,4},{24,8},{28,12},{1,17},{... | collective-permute-start | bytes 5013512 | tf_op jit(solution)/shard_map/ppermute | solution.py:1035
  563.0 119.0 %collective-permute-start.35 = (bf16[2,256,1536]{2,1,0:T(8,128)(2,1)}, bf16[2,256,1536]{2,1,0:T(8,128)(2,1)}, u32[]{:S(2)}, u32[]{:S(2)}) collective-permute-start(bf16[2,256,1536]{2,1,0:T(8,128)(2,1)} %pad_maximum_fusion.7), channel_id=1, source_target_pairs={{0,16},{4,20},{8,24},{12,28},{16,0},{20,4},{24,8},{28,12},{1,17},{... | collective-permute-start | bytes 4718600 | tf_op jit(solution)/shard_map/ppermute | solution.py:1035
  565.8 116.2 %collective-permute-start.33 = (bf16[2,256,1536]{2,1,0:T(8,128)(2,1)}, bf16[2,256,1536]{2,1,0:T(8,128)(2,1)}, u32[]{:S(2)}, u32[]{:S(2)}) collective-permute-start(bf16[2,256,1536]{2,1,0:T(8,128)(2,1)} %pad_maximum_fusion.6), channel_id=1, source_target_pairs={{0,8},{4,12},{8,0},{12,4},{16,24},{20,28},{24,16},{28,20},{1,9},{5... | collective-permute-start | bytes 4718600 | tf_op jit(solution)/shard_map/ppermute | solution.py:1035
  571.6 48.5 %collective-permute-start.38 = (bf16[272,1536]{1,0:T(8,128)(2,1)S(1)}, bf16[272,1536]{1,0:T(8,128)(2,1)S(1)}, u32[]{:S(2)}, u32[]{:S(2)}) collective-permute-start(bf16[272,1536]{1,0:T(8,128)(2,1)S(1)} %get-tuple-element.228), channel_id=1, source_target_pairs={{0,8},{4,12},{8,0},{12,4},{16,24},{20,28},{24,16},{28,20},{1,9},{5... | collective-permute-start | bytes 2506760 | tf_op jit(solution)/shard_map/ppermute | solution.py:1035
  572.3 47.8 %collective-permute-start.37 = (bf16[272,1536]{1,0:T(8,128)(2,1)S(1)}, bf16[272,1536]{1,0:T(8,128)(2,1)S(1)}, u32[]{:S(2)}, u32[]{:S(2)}) collective-permute-start(bf16[272,1536]{1,0:T(8,128)(2,1)S(1)} %get-tuple-element.230), channel_id=1, source_target_pairs={{0,16},{4,20},{8,24},{12,28},{16,0},{20,4},{24,8},{28,12},{1,17},{... | collective-permute-start | bytes 2506760 | tf_op jit(solution)/shard_map/ppermute | solution.py:1035
  651.6 26.5 %collective-permute-start.39 = (bf16[512,512]{1,0:T(8,128)(2,1)S(1)}, bf16[512,512]{1,0:T(8,128)(2,1)S(1)}, u32[]{:S(2)}, u32[]{:S(2)}) collective-permute-start(bf16[512,512]{1,0:T(8,128)(2,1)S(1)} %convert_element_type.630), channel_id=1, source_target_pairs={{0,1},{2,3},{4,5},{6,7},{8,9},{10,11},{12,13},{14,15},{16,17},{18,... | collective-permute-start | bytes 1572872 | tf_op jit(solution)/shard_map/ppermute | solution.py:1330
  713.0 35.7 %collective-permute-start.43 = (bf16[2,2,208,896]{3,2,1,0:T(8,128)(2,1)}, bf16[2,2,208,896]{3,2,1,0:T(8,128)(2,1)S(1)}, u32[]{:S(2)}, u32[]{:S(2)}) collective-permute-start(bf16[2,2,208,896]{3,2,1,0:T(8,128)(2,1)} %pad_maximum_fusion.10), channel_id=1, source_target_pairs={{0,16},{4,20},{8,24},{12,28},{16,0},{20,4},{24,8},{28,12},{1,17},{... | collective-permute-start | bytes 4472840 | tf_op jit(solution)/shard_map/ppermute | solution.py:1035
  714.9 35.8 %collective-permute-start.41 = (bf16[2,2,208,896]{3,2,1,0:T(8,128)(2,1)}, bf16[2,2,208,896]{3,2,1,0:T(8,128)(2,1)}, u32[]{:S(2)}, u32[]{:S(2)}) collective-permute-start(bf16[2,2,208,896]{3,2,1,0:T(8,128)(2,1)} %pad_maximum_fusion.9), channel_id=1, source_target_pairs={{0,8},{4,12},{8,0},{12,4},{16,24},{20,28},{24,16},{28,20},{1,9},{5... | collective-permute-start | bytes 4472840 | tf_op jit(solution)/shard_map/ppermute | solution.py:1035
  720.4 45.2 %collective-permute-start.34 = (bf16[256,1536]{1,0:T(8,128)(2,1)}, bf16[256,1536]{1,0:T(8,128)(2,1)}, u32[]{:S(2)}, u32[]{:S(2)}) collective-permute-start(bf16[256,1536]{1,0:T(8,128)(2,1)} %get-tuple-element.238), channel_id=1, source_target_pairs={{0,16},{4,20},{8,24},{12,28},{16,0},{20,4},{24,8},{28,12},{1,17},{... | collective-permute-start | bytes 2359304 | tf_op jit(solution)/shard_map/ppermute | solution.py:1035
  721.9 45.7 %collective-permute-start.36 = (bf16[256,1536]{1,0:T(8,128)(2,1)}, bf16[256,1536]{1,0:T(8,128)(2,1)}, u32[]{:S(2)}, u32[]{:S(2)}) collective-permute-start(bf16[256,1536]{1,0:T(8,128)(2,1)} %get-tuple-element.239), channel_id=1, source_target_pairs={{0,8},{4,12},{8,0},{12,4},{16,24},{20,28},{24,16},{28,20},{1,9},{5... | collective-permute-start | bytes 2359304 | tf_op jit(solution)/shard_map/ppermute | solution.py:1035
  753.3 27.4 %collective-permute-start.42 = (bf16[2,208,896]{2,1,0:T(8,128)(2,1)S(1)}, bf16[2,208,896]{2,1,0:T(8,128)(2,1)S(1)}, u32[]{:S(2)}, u32[]{:S(2)}) collective-permute-start(bf16[2,208,896]{2,1,0:T(8,128)(2,1)S(1)} %get-tuple-element.246), channel_id=1, source_target_pairs={{0,16},{4,20},{8,24},{12,28},{16,0},{20,4},{24,8},{28,12},{1,17},{... | collective-permute-start | bytes 2236424 | tf_op jit(solution)/shard_map/ppermute | solution.py:1035
  754.8 27.5 %collective-permute-start.44 = (bf16[2,208,896]{2,1,0:T(8,128)(2,1)S(1)}, bf16[2,208,896]{2,1,0:T(8,128)(2,1)S(1)}, u32[]{:S(2)}, u32[]{:S(2)}) collective-permute-start(bf16[2,208,896]{2,1,0:T(8,128)(2,1)S(1)} %get-tuple-element.247), channel_id=1, source_target_pairs={{0,8},{4,12},{8,0},{12,4},{16,24},{20,28},{24,16},{28,20},{1,9},{5... | collective-permute-start | bytes 2236424 | tf_op jit(solution)/shard_map/ppermute | solution.py:1035
  787.5 10.6 %collective-permute-start.45 = (bf16[208,896]{1,0:T(8,128)(2,1)S(1)}, bf16[208,896]{1,0:T(8,128)(2,1)S(1)}, u32[]{:S(2)}, u32[]{:S(2)}) collective-permute-start(bf16[208,896]{1,0:T(8,128)(2,1)S(1)} %get-tuple-element.261), channel_id=1, source_target_pairs={{1,3},{0,1},{2,0},{3,2},{5,7},{4,5},{6,4},{7,6},{9,11},{8,9},{10,8... | collective-permute-start | bytes 1118216 | tf_op jit(solution)/shard_map/ppermute | solution.py:1003
  793.4 20.0 %collective-permute-start.48 = (bf16[208,896]{1,0:T(8,128)(2,1)S(1)}, bf16[208,896]{1,0:T(8,128)(2,1)S(1)}, u32[]{:S(2)}, u32[]{:S(2)}) collective-permute-start(bf16[208,896]{1,0:T(8,128)(2,1)S(1)} %get-tuple-element.260), channel_id=1, source_target_pairs={{0,3},{3,0},{4,7},{7,4},{8,11},{11,8},{12,15},{15,12},{16,19},{19,... | collective-permute-start | bytes 1118216 | tf_op jit(solution)/shard_map/ppermute | solution.py:1004
  798.4 15.5 %collective-permute-start.46 = (bf16[208,896]{1,0:T(8,128)(2,1)S(1)}, bf16[208,896]{1,0:T(8,128)(2,1)S(1)}, u32[]{:S(2)}, u32[]{:S(2)}) collective-permute-start(bf16[208,896]{1,0:T(8,128)(2,1)S(1)} %get-tuple-element.255), channel_id=1, source_target_pairs={{0,1},{1,2},{2,3},{4,5},{5,6},{6,7},{8,9},{9,10},{10,11},{12,13},{... | collective-permute-start | bytes 1118216 | tf_op jit(solution)/shard_map/ppermute | solution.py:1015
  (63 other events, 576.5 us)
Sparse Core Ops, SparseCore 0:
  12.2 154.7 all-gather.4
  169.1 135.2 all-gather.6
  417.0 120.7 reduce-scatter.2
  547.7 133.7 reduce-scatter.4

commit v11 on v10

--- a/solution.py
+++ b/solution.py
@@ -76,6 +76,9 @@
     ((7, 2), (7, 3)),
 )
 EXTRA = 16
+
+
+STEP = 768
 
 
 def weight_copies(info, refs, target, sem, start, width):
@@ -180,9 +183,9 @@
         run_all(copies)
         wait_all(copies)
 
-    at = pl.multiple_of(pl.program_id(0) * 256, 256)
-    lin = nn(normed[...], weight[:, pl.ds(at, 256)])
-    for h in range(2):
+    at = pl.multiple_of(pl.program_id(0) * STEP, STEP)
+    lin = nn(normed[...], weight[:, pl.ds(at, STEP)])
+    for h in range(STEP // HEAD_DIM):
         out[:, 128 * h : 128 * h + 128] = turn(
             lin[:, 128 * h : 128 * h + 128], cosine[...], sine[...]
         ).astype(LOW)
@@ -191,11 +194,11 @@
 def query(info, normed, cosine, sine, refs):
     return pl.pallas_call(
         query_kernel,
-        grid=(D // 256,),
+        grid=(D // STEP,),
         out_shape=jax.ShapeDtypeStruct((TOK_DEV, D), LOW),
         in_specs=[SMEM, whole((TOK_DEV, D)), whole((TOK_DEV, 128)), whole((TOK_DEV, 128))]
         + [ANY] * len(refs),
-        out_specs=pl.BlockSpec((TOK_DEV, 256), lambda i: (0, i)),
+        out_specs=pl.BlockSpec((TOK_DEV, STEP), lambda i: (0, i)),
         scratch_shapes=[pltpu.VMEM((D, D), LOW), pltpu.SemaphoreType.DMA],
         compiler_params=params(),
         cost_estimate=LITTLE,
@@ -371,7 +374,7 @@
         run_all(copies)
         wait_all(copies)
 
-    at = pl.ds(pl.multiple_of(pl.program_id(0) * 256, 256), 256)
+    at = pl.ds(pl.multiple_of(pl.program_id(0) * STEP, STEP), STEP)
     residual[:, at] = tokens[:, at].astype(WIDE) + nn(heads[...], weight[:, at])
 
     @pl.when(pl.program_id(0) == pl.num_programs(0) - 1)
@@ -385,7 +388,7 @@
     full = (TOK_DEV, D)
     return pl.pallas_call(
         out_kernel,
-        grid=(D // 256,),
+        grid=(D // STEP,),
         out_shape=(jax.ShapeDtypeStruct(full, WIDE), jax.ShapeDtypeStruct(full, LOW)),
         in_specs=[SMEM, whole(full), whole(full), whole((1, D))] + [ANY] * len(refs),
         out_specs=(whole(full), whole(full)),
@@ -446,26 +449,46 @@
     )(info, routes)
 
 
-def pick_kernel(local, chosen, *rest):
-    count, height, _ = chosen.shape
-    capacity = height // local
+def pick_kernel(local, count, chosen, *rest):
+    blocks, outs = rest[:count], rest[count : count + local]
+    picks, block_in, out_block, sem_in, sem_out = rest[count + local :]
+    capacity = outs[0].shape[1]
+    copies = [
+        (
+            pltpu.make_async_copy(chosen.at[q], picks.at[q], sem_in.at[q, 0]),
+            pltpu.make_async_copy(blocks[q], block_in.at[q], sem_in.at[q, 1]),
+        )
+        for q in range(count)
+    ]
+    for pair in copies:
+        run_all(pair)
+    sent = []
     for q in range(count):
-        rows_of = nn(chosen[q], rest[q][...]).astype(LOW)
+        wait_all(copies[q])
+        out_block[q] = nn(picks[q], block_in[q]).astype(LOW)
         for e in range(local):
-            rest[count + e][q] = rows_of[e * capacity : (e + 1) * capacity]
+            copy = pltpu.make_async_copy(
+                out_block.at[q, pl.ds(e * capacity, capacity)], outs[e].at[q], sem_out.at[q, e]
+            )
+            copy.start()
+            sent.append(copy)
+    wait_all(sent)
 
 
 def pick_rows(chosen, blocks, local):
     count, height, _ = chosen.shape
-    capacity = height // local
-    wide = 256
-    return pl.pallas_call(
-        functools.partial(pick_kernel, local),
-        grid=(D // wide,),
-        in_specs=[whole(chosen.shape)]
-        + [pl.BlockSpec((TOK_DEV, wide), lambda i: (0, i))] * count,
-        out_specs=[pl.BlockSpec((count, capacity, wide), lambda i: (0, 0, i))] * local,
-        out_shape=[jax.ShapeDtypeStruct((count, capacity, D), LOW)] * local,
+    return pl.pallas_call(
+        functools.partial(pick_kernel, local, count),
+        in_specs=[ANY] * (1 + count),
+        out_specs=[ANY] * local,
+        out_shape=[jax.ShapeDtypeStruct((count, height // local, D), LOW)] * local,
+        scratch_shapes=[
+            pltpu.VMEM((count, height, TOK_DEV), LOW),
+            pltpu.VMEM((count, TOK_DEV, D), LOW),
+            pltpu.VMEM((count, height, D), LOW),
+            pltpu.SemaphoreType.DMA((count, 2)),
+            pltpu.SemaphoreType.DMA((count, local)),
+        ],
         compiler_params=params(),
         cost_estimate=LITTLE,
         name="pick_rows",
@@ -509,7 +532,7 @@
     count, height, _ = chosen.shape
     capacity = height // local
     total = router.shape[1]
-    wide = 512
+    wide = D
     out_shape = [jax.ShapeDtypeStruct((count, capacity, D), LOW)] * local + [
         jax.ShapeDtypeStruct((count, capacity, 1), WIDE)
     ] * local
@@ -564,23 +587,52 @@
     )(place, *dots)
 
 
-def expert_kernel(slots, rows, grads, shares, source, *rest):
-    out_rows, back_rows, grad_rows, acts, dots, weight, sem = rest
+def expert_kernel(slots, info, rows, grads, shares, *rest):
+    refs, (out_rows, back_rows, grad_rows, acts, dots, weight, sem) = rest[:-7], rest[-7:]
     part = weight.shape[1] // slots
 
     @pl.when(pl.program_id(0) == 0)
     def _():
-        copies = [
-            pltpu.make_async_copy(
-                source.at[slot, pl.ds(which * part, part)],
-                weight.at[which, pl.ds(slot * part, part)],
-                sem,
-            )
-            for slot in range(slots)
-            for which in range(3)
-        ]
-        run_all(copies)
-        wait_all(copies)
+        def copies(ref, slot):
+            return [
+                pltpu.make_async_copy(
+                    ref.at[pl.ds(which * part, part)],
+                    weight.at[which, pl.ds(pl.multiple_of(slot * part, part), part)],
+                    sem,
+                )
+                for which in range(3)
+            ]
+
+        if len(refs) == 1:
+            for slot in range(slots):
+                run_all(copies(refs[0].at[slot], slot))
+            for slot in range(slots):
+                wait_all(copies(refs[0].at[slot], slot))
+        else:
+            block, second, above, below, far = refs
+            low_end = info[2] == 0
+            end = jnp.logical_or(low_end, info[2] == 3)
+            run_all(copies(block, info[2]))
+            run_all(copies(second, info[3]))
+
+            @pl.when(low_end)
+            def _():
+                run_all(copies(above, info[4]))
+
+            @pl.when(jnp.logical_not(low_end))
+            def _():
+                run_all(copies(below, info[4]))
+
+            @pl.when(end)
+            def _():
+                run_all(copies(far, info[5]))
+
+            @pl.when(jnp.logical_not(end))
+            def _():
+                run_all(copies(above, info[5]))
+
+            for slot in range(slots):
+                wait_all(copies(block, slot))
 
     row_block = rows[...]
     share = shares[...]
@@ -610,9 +662,9 @@
 EXPERT_ROWS = 256
 
 
-def expert(rows, grads, shares, weights):
+def expert(info, rows, grads, shares, refs, slots):
     height = rows.shape[0]
-    slots, part = weights.shape[0], weights.shape[1] // 3
+    part = refs[0].shape[-2] // 3
     wide_block = pl.BlockSpec((EXPERT_ROWS, D), lambda i: (i, 0))
     thin_block = pl.BlockSpec((EXPERT_ROWS, 1), lambda i: (i, 0))
     return pl.pallas_call(
@@ -623,14 +675,14 @@
             jax.ShapeDtypeStruct((slots, 3 * part, height), LOW),
             jax.ShapeDtypeStruct((height, 1), WIDE),
         ],
-        in_specs=[wide_block, wide_block, thin_block, ANY],
+        in_specs=[SMEM, wide_block, wide_block, thin_block] + [ANY] * len(refs),
         out_specs=[wide_block] * 3
         + [pl.BlockSpec((slots, 3 * part, EXPERT_ROWS), lambda i: (0, 0, i)), thin_block],
         scratch_shapes=[pltpu.VMEM((3, slots * part, D), LOW), pltpu.SemaphoreType.DMA],
         compiler_params=params(),
         cost_estimate=LITTLE,
         name="expert",
-    )(rows, grads, shares, weights)
+    )(info, rows, grads, shares, *refs)
 
 
 def expert_grads_kernel(acts, rows, grads, out):
@@ -659,43 +711,140 @@
 SHARE_ROWS = 32
 
 
-def combine_kernel(local, info, chosen, *rest):
-    rows, dots, out = rest[:local], rest[local:-1], rest[-1]
-    both = jnp.concatenate([ref[0] for ref in rows], axis=0)
-    out[0, :TOK_DEV] = tn(chosen[0], both).astype(LOW)
-    if dots:
-        capacity = rows[0].shape[1]
-        row = lax.broadcasted_iota(jnp.int32, (SHARE_ROWS, D), 0)
-        values = jnp.zeros((SHARE_ROWS, D), WIDE)
-        for e in range(local):
-            picked = chosen[0, e * capacity : (e + 1) * capacity].astype(WIDE)
-            high, low = split(jnp.sum(picked * dots[e][0], axis=0, keepdims=True))
-            pieces = [high.astype(WIDE), low.astype(WIDE)]
-            pieces.append(jnp.zeros((1, D - 2 * TOK_DEV), WIDE))
-            line = jnp.concatenate(pieces, axis=1)
-            values = jnp.where(row == info[0] * local + e, line, values)
-        out[0, TOK_DEV:] = values.astype(LOW)
+def combine_kernel(local, first, step, info, chosen, *rest):
+    rows, dots, out = rest[:local], rest[local:-6], rest[-6]
+    picks, rows_in, out_block, sem_in, sem_out = rest[-5:]
+    number = out.shape[0]
+    capacity = rows[0].shape[1]
+    copies = []
+    for n in range(number):
+        q = first + step * n
+        copies.append(
+            [pltpu.make_async_copy(chosen.at[q], picks.at[n], sem_in.at[n, local])]
+            + [
+                pltpu.make_async_copy(
+                    rows[e].at[q],
+                    rows_in.at[n, pl.ds(e * capacity, capacity)],
+                    sem_in.at[n, e],
+                )
+                for e in range(local)
+            ]
+        )
+    for group in copies:
+        run_all(group)
+    sent = []
+    for n in range(number):
+        wait_all(copies[n])
+        out_block[n, :TOK_DEV] = tn(picks[n], rows_in[n]).astype(LOW)
+        if dots:
+            row = lax.broadcasted_iota(jnp.int32, (SHARE_ROWS, D), 0)
+            values = jnp.zeros((SHARE_ROWS, D), WIDE)
+            for e in range(local):
+                picked = picks[n, e * capacity : (e + 1) * capacity].astype(WIDE)
+                share = picked * dots[e][first + step * n]
+                high, low = split(jnp.sum(share, axis=0, keepdims=True))
+                pieces = [high.astype(WIDE), low.astype(WIDE)]
+                pieces.append(jnp.zeros((1, D - 2 * TOK_DEV), WIDE))
+                line = jnp.concatenate(pieces, axis=1)
+                values = jnp.where(row == info[0] * local + e, line, values)
+            out_block[n, TOK_DEV:] = values.astype(LOW)
+        copy = pltpu.make_async_copy(out_block.at[n], out.at[n], sem_out.at[n])
+        copy.start()
+        sent.append(copy)
+    wait_all(sent)
 
 
 def combine(info, chosen, rows, first, step, dots=()):
     count, capacity, _ = rows[0].shape
+    local = len(rows)
     number = (count - first + step - 1) // step
     height = TOK_DEV + (SHARE_ROWS if dots else 0)
     return pl.pallas_call(
-        functools.partial(combine_kernel, len(rows)),
-        grid=(number,),
+        functools.partial(combine_kernel, local, first, step),
         out_shape=jax.ShapeDtypeStruct((number, height, D), LOW),
-        in_specs=[
-            SMEM,
-            pl.BlockSpec((1,) + chosen.shape[1:], lambda i: (first + step * i, 0, 0)),
-        ]
-        + [pl.BlockSpec((1, capacity, D), lambda i: (first + step * i, 0, 0))] * len(rows)
-        + [pl.BlockSpec((1, capacity, 1), lambda i: (first + step * i, 0, 0))] * len(dots),
-        out_specs=pl.BlockSpec((1, height, D), lambda i: (i, 0, 0)),
+        in_specs=[SMEM, ANY]
+        + [ANY] * local
+        + [pl.BlockSpec(memory_space=pltpu.VMEM)] * len(dots),
+        out_specs=ANY,
+        scratch_shapes=[
+            pltpu.VMEM((number, local * capacity, TOK_DEV), LOW),
+            pltpu.VMEM((number, local * capacity, D), LOW),
+            pltpu.VMEM((number, height, D), LOW),
+            pltpu.SemaphoreType.DMA((number, local + 1)),
+            pltpu.SemaphoreType.DMA((number,)),
+        ],
         compiler_params=params(),
         cost_estimate=LITTLE,
         name="combine",
     )(info, chosen, *rows, *dots)
+
+
+def chip_adds_kernel(keep, got, send_x, send_y, near_x, near_y, one, two, sem_in, sem_out):
+    half = send_x.shape[1]
+    copies = [
+        (
+            pltpu.make_async_copy(keep.at[i], one.at[i], sem_in.at[i, 0]),
+            pltpu.make_async_copy(got.at[i], two.at[i], sem_in.at[i, 1]),
+        )
+        for i in range(4)
+    ]
+    for pair in copies:
+        run_all(pair)
+    sent = []
+    for i in range(4):
+        wait_all(copies[i])
+        one[i] = (one[i].astype(WIDE) + two[i].astype(WIDE)).astype(LOW)
+        upper = (near_x, send_x)[i % 2].at[i // 2]
+        lower = (near_y, send_y)[i // 2].at[i % 2]
+        for part, to in enumerate((upper, lower)):
+            copy = pltpu.make_async_copy(
+                one.at[i, pl.ds(part * half, half)], to, sem_out.at[i, part]
+            )
+            copy.start()
+            sent.append(copy)
+    wait_all(sent)
+
+
+def chip_adds(keep, got):
+    _, height, width = keep.shape
+    shape = jax.ShapeDtypeStruct((2, height // 2, width), LOW)
+    return pl.pallas_call(
+        chip_adds_kernel,
+        out_shape=(shape,) * 4,
+        in_specs=[ANY, ANY],
+        out_specs=(ANY,) * 4,
+        scratch_shapes=[
+            pltpu.VMEM(keep.shape, LOW),
+            pltpu.VMEM(keep.shape, LOW),
+            pltpu.SemaphoreType.DMA((4, 2)),
+            pltpu.SemaphoreType.DMA((4, 2)),
+        ],
+        compiler_params=params(),
+        cost_estimate=LITTLE,
+        name="chip_sums",
+    )(keep, got)
+
+
+def corner_adds_kernel(near_x, got_x, near_y, got_y, send_y, send_x):
+    send_y[...] = (near_x[0].astype(WIDE) + got_x[0].astype(WIDE)).astype(LOW)
+    send_x[...] = (near_y[0].astype(WIDE) + got_y[0].astype(WIDE)).astype(LOW)
+
+
+def corner_adds(near_x, got_x, near_y, got_y):
+    _, half, width = near_x.shape
+    rows = half
+    block = pl.BlockSpec((1, rows, width), lambda i: (1, i, 0))
+    out = pl.BlockSpec((rows, width), lambda i: (i, 0))
+    return pl.pallas_call(
+        corner_adds_kernel,
+        grid=(half // rows,),
+        out_shape=(jax.ShapeDtypeStruct((half, width), LOW),) * 2,
+        in_specs=[block] * 4,
+        out_specs=(out, out),
+        compiler_params=params(),
+        cost_estimate=LITTLE,
+        name="corner_sums",
+    )(near_x, got_x, near_y, got_y)
 
 
 def split(values):
@@ -743,7 +892,9 @@
         if parts == 2:
             back_sum, grad_shares = sums[0][...], sums[1][...]
         else:
-            values = [ref[...].astype(WIDE) for ref in sums]
+            values = [
+                (ref[0] if len(ref.shape) == 3 else ref[...]).astype(WIDE) for ref in sums
+            ]
             upper = values[0] + values[1] + values[2]
             lower = values[3] + values[4] + values[5]
             last = lower.shape[0] - SHARE_ROWS
@@ -761,7 +912,7 @@
         grad_branch[...] = total.astype(LOW)
         wait_all(copies)
 
-    at = pl.ds(pl.multiple_of(pl.program_id(0) * 256, 256), 256)
+    at = pl.ds(pl.multiple_of(pl.program_id(0) * STEP, STEP), STEP)
     grad_heads[...] = nt(grad_branch[...], weight[at, :]).astype(LOW)
 
 
@@ -770,7 +921,7 @@
     total = router.shape[0]
     return pl.pallas_call(
         functools.partial(branch_back_kernel, len(sums)),
-        grid=(D // 256,),
+        grid=(D // STEP,),
         out_shape=(
             jax.ShapeDtypeStruct(full, WIDE),
             jax.ShapeDtypeStruct(full, LOW),
@@ -781,12 +932,12 @@
         in_specs=[SMEM]
         + [whole(full)] * 3
         + [whole((TOP, TOK_DEV)), whole((total, D)), whole((1, D))]
-        + [whole(part.shape) for part in sums]
+        + [whole(part.shape if part.ndim == 2 else (1,) + part.shape[1:]) for part in sums]
         + [ANY] * len(refs),
         out_specs=(
             whole(full),
             whole(full),
-            pl.BlockSpec((TOK_DEV, 256), lambda i: (0, i)),
+            pl.BlockSpec((TOK_DEV, STEP), lambda i: (0, i)),
             whole((1, D)),
             whole((total, D)),
         ),
@@ -843,7 +994,7 @@
         run_all(copies)
         wait_all(copies)
 
-    at = pl.ds(pl.multiple_of(pl.program_id(0) * 256, 256), 256)
+    at = pl.ds(pl.multiple_of(pl.program_id(0) * STEP, STEP), STEP)
     grad_normed[:, at] = nt(grad_query[...], query_weight[at, :]) + nt(
         grad_pair[...], pair_weight[at, :]
     )
@@ -861,7 +1012,7 @@
     full = (TOK_DEV, D)
     return pl.pallas_call(
         token_back_kernel,
-        grid=(D // 256,),
+        grid=(D // STEP,),
         out_shape=(jax.ShapeDtypeStruct(full, LOW), jax.ShapeDtypeStruct((1, D), WIDE)),
         in_specs=[
             SMEM,
@@ -885,16 +1036,14 @@
     )(info, grad_query, grad_pair, tokens, grad_residual, gain, *query_refs, *pair_refs)
 
 
-def weight_grads_kernel(parts, info, *rest):
+def weight_grads_kernel(parts, whole_rows, info, *rest):
     ins, (keep, send) = rest[:-2], rest[-2:]
     depth = D // 8
     core = info[0] & 1
     chip = pl.program_id(0) ^ (info[0] >> 1)
-    start = 0
-    for strip_at, grads_at, width in parts:
+    for strip_at, grads_at, start, width in parts:
         low = tn(ins[strip_at][...], ins[grads_at][...]).astype(LOW)
         columns = slice(start, start + width)
-        start += width
         for slot in range(QUARTERS):
             for j in range(QUARTERS):
 
@@ -904,8 +1053,12 @@
                     upper, lower = piece[:depth], piece[depth:]
                     keep[0, slot, :depth, columns] = jnp.where(core == 0, upper, lower)
                     send[0, slot, :depth, columns] = jnp.where(core == 0, lower, upper)
-
-    if keep.shape[2] > depth:
+                    if not whole_rows:
+                        blank = jnp.zeros((EXTRA, width), LOW)
+                        keep[0, slot, depth:, columns] = blank
+                        send[0, slot, depth:, columns] = blank
+
+    if whole_rows:
         extra = ins[-1]
         for slot in range(QUARTERS):
             to = info[2 + slot]
@@ -913,15 +1066,26 @@
             send[0, slot, depth:] = extra[(chip * 2 + 1 - core) * QUARTERS + to]
 
 
-def weight_grads(info, strips, grads, parts, extra):
+def weight_grads(info, strips, grads, parts, extra, earlier=()):
     depth = D // 8
-    width = sum(part[2] for part in parts)
     strip = pl.BlockSpec((TOK_DEV, 2 * depth), lambda i, info: (0, i ^ (info[0] >> 1)))
     more = [] if extra is None else [extra]
-    shape = (4, QUARTERS, depth + EXTRA * len(more), width)
-    out = pl.BlockSpec((1,) + shape[1:], lambda i, info: (i, 0, 0, 0))
-    return pl.pallas_call(
-        functools.partial(weight_grads_kernel, parts),
+    width = 2 * D // QUARTERS + 128
+    shape = (4, QUARTERS, depth + EXTRA, width)
+    if earlier:
+        out = pl.BlockSpec((1, QUARTERS, depth + EXTRA, 128), lambda i, info: (i, 0, 0, 3))
+    else:
+        out = pl.BlockSpec((1,) + shape[1:], lambda i, info: (i, 0, 0, 0))
+    inputs = [*strips, *grads, *more]
+
+    def kernel(info, *rest):
+        count = len(inputs)
+        weight_grads_kernel(
+            parts, extra is not None, info, *rest[:count], *rest[count + len(earlier) :]
+        )
+
+    return pl.pallas_call(
+        kernel,
         grid_spec=pltpu.PrefetchScalarGridSpec(
             num_scalar_prefetch=1,
             grid=(4,),
@@ -929,14 +1093,16 @@
             + [
                 pl.BlockSpec(a.shape, lambda i, info, n=a.ndim: (0,) * n)
                 for a in (*grads, *more)
-            ],
+            ]
+            + [ANY] * len(earlier),
             out_specs=(out, out),
         ),
         out_shape=(jax.ShapeDtypeStruct(shape, LOW),) * 2,
+        input_output_aliases={1 + len(inputs) + i: i for i in range(len(earlier))},
         compiler_params=params(),
         cost_estimate=LITTLE,
         name="weight_gradients",
-    )(info, *strips, *grads, *more)
+    )(info, *inputs, *earlier)
 
 
 def position_of(token_index):
@@ -1039,27 +1205,9 @@
     return (one.astype(WIDE) + two.astype(WIDE)).astype(LOW)
 
 
-def chip_sums(keep, got, chips, part):
-    return jnp.stack([add_low(keep[i][part], got[i][part]) for i in chips])
-
-
-def halves(keep):
-    half = keep.shape[1] // 2
-    return slice(0, half), slice(half, None)
-
-
-def chips_first(keep, got):
-    one, two = halves(keep)
-    return chip_sums(keep, got, (1, 3), one), chip_sums(keep, got, (2, 3), two)
-
-
-def chips_second(keep, got, got_x, got_y):
-    one, two = halves(keep)
-    near_x = chip_sums(keep, got, (0, 2), one)
-    near_y = chip_sums(keep, got, (0, 1), two)
-    got_xy = flip(add_low(near_x[1], got_x[1]), 4)
-    got_yx = flip(add_low(near_y[1], got_y[1]), 2)
-    return (near_x[0], got_x[0], got_xy, near_y[0], got_y[0], got_yx)
+def chips_second(near_x, near_y, got_x, got_y):
+    for_y, for_x = corner_adds(near_x, got_x, near_y, got_y)
+    return (near_x, got_x, flip(for_y, 4), near_y, got_y, flip(for_x, 2))
 
 
 def turn_corner(beside, across):
@@ -1072,7 +1220,7 @@
 
 
 def sum_parts(parts):
-    wide = [a.astype(WIDE) for a in parts]
+    wide = [(a[0] if a.ndim == 3 else a).astype(WIDE) for a in parts]
     if len(wide) == 1:
         return wide[0]
     return jnp.concatenate([wide[0] + wide[1] + wide[2], wide[3] + wide[4] + wide[5]], axis=0)
@@ -1129,11 +1277,7 @@
         )
         for expert in range(local_experts)
     ]
-    expert_weights = []
-    for block in shard_blocks:
-        if expert_weights:
-            block = after(block, expert_weights[-1])
-        expert_weights.append(lax.all_gather(block, "cols", axis=0))
+    expert_refs = []
     if fast:
         wide = packed.shape[1]
         gains = jnp.concatenate([attention_gain, experts_gain])[None, :]
@@ -1150,12 +1294,15 @@
         packed_near = send_near(packed)
         packed_far = send_far(packed)
         packed_second = send_second(packed, packed_near)
+        first_block = after(shard_blocks[0], *packed_near)
+        first_near = send_near(first_block)
+        first_second = send_second(first_block, first_near)
         grad_flips = (flip(cotangent, 2), flip(cotangent, 4))
         own = jnp.stack(slot_list(packed, packed_near, packed_second, packed_far))
         own = after(own, info, cosine, sine, *grad_flips)
         beside, across = flip(own, 2), flip(own, 4)
         own_in = flip(own, 1)
-        beside, across = after((beside, across), own_in)
+        beside, across = after((beside, across), own_in, *first_near)
         corner = [flip(beside[:2], 4), flip(across[2:], 2)]
         pair_in = flip(jnp.concatenate([beside, across], axis=0), 1)
         corner_in = [flip(piece, 1) for piece in corner]
@@ -1202,19 +1349,21 @@
         router_all.reshape(row_count, col_count, router_part, depth), (1, 2, 0, 3)
     ).reshape(expert_total, D)
     router_cols = router_rows.T
-    normed, own_pair = key_value(info, tokens, attention_scale, cosine, sine, pair_refs)
+    tokens_in = after(tokens, first_second, chosen) if fast else tokens
+    normed, own_pair = key_value(info, tokens_in, attention_scale, cosine, sine, pair_refs)
     pairs = [(i + 1, i) for i in range(0, col_count, 2)]
     partner = lax.ppermute(own_pair, "cols", pairs)
     queries = query(info, normed, cosine, sine, query_refs)
     if fast:
+        first_far = send_far(after(first_block, partner, queries))
+        expert_refs.append([first_block, first_second, *first_near, first_far])
         grad_flips = after(grad_flips, own_pair)
         grad_corner = turn_corner(*grad_flips)
-        queries = after(queries, grad_corner)
     heads = attention(info, queries, own_pair, partner)
     if fast:
         grad_near = [cotangent, *grad_flips, grad_corner]
         grad_blocks = [block for one in grad_near for block in (one, flip(one, 1))]
-        heads = after(heads, *grad_blocks, expert_weights[0])
+        heads = after(heads, grad_corner)
     else:
         grad_all = lax.all_gather(cotangent, "rows", axis=0)
         grad_blocks = [grad_all[q] for q in range(row_count)]
@@ -1223,8 +1372,11 @@
     if fast:
         beside, across = flip(normed_two, 2), flip(normed_two, 4)
         beside_in = flip(normed_two, 1)
+        later_block = after(shard_blocks[1], first_far, normed_two)
+        expert_refs.append([lax.all_gather(later_block, "cols", axis=0)])
     else:
         rows_all = lax.all_gather(normed_two, "rows", axis=0)
+        expert_refs = [[lax.all_gather(block, "cols", axis=0)] for block in shard_blocks]
     grad_rows = pick_rows(chosen, grad_blocks, local_experts)
 
     def place_block(q, block, picked):
@@ -1262,7 +1414,7 @@
     for e in range(local_experts):
         rows_in = after(token_rows[e], *reduced_in) if e else token_rows[e]
         out_row, back_row, grad_row, acts, dots = expert(
-            rows_in, grad_rows[e], share_rows[e], expert_weights[e]
+            info, rows_in, grad_rows[e], share_rows[e], expert_refs[e], col_count
         )
         out_rows.append(out_row.reshape(row_count, capacity, D))
         back_rows.append(back_row.reshape(row_count, capacity, D))
@@ -1270,21 +1422,21 @@
         if fast and e == 1:
             got = flip(combine(info, chosen, back_rows, 1, 2, gate_dots), 1)
             back_keep = combine(info, chosen, back_rows, 0, 2, gate_dots)
-            back_first = chips_first(back_keep, got)
-            acts = after(acts, *back_first)
-            back_flips = send_chips(back_first)
+            for_x, for_y, near_x, near_y = chip_adds(back_keep, got)
+            acts = after(acts, for_x)
+            back_flips = send_chips((for_x, for_y))
         slots = expert_grads(acts, token_rows[e], grad_row)
         reduced_in = (slots,)
-        if e:
-            slots = after(slots, reduced[-1])
-        reduced.append(lax.psum_scatter(slots, "cols", scatter_dimension=0, tiled=False))
+        if e and fast:
+            back_parts = chips_second(near_x, near_y, *after(back_flips, slots))
+        else:
+            reduced.append(lax.psum_scatter(slots, "cols", scatter_dimension=0, tiled=False))
 
     if fast:
-        back_parts = chips_second(back_keep, got, *after(back_flips, slots))
         out_rows = [after(a, back_parts[1], back_parts[4]) for a in out_rows]
         out_got = flip(combine(info, chosen, out_rows, 1, 2), 1)
         out_keep = combine(info, chosen, out_rows, 0, 2)
-        back_parts = after(back_parts, out_keep, out_got, slots, reduced[0])
+        back_parts = after(back_parts, out_keep, out_got, slots)
     else:
         spread_dots = spread(place_rows, gate_dots)
         grad_shares = lax.all_to_all(spread_dots, "rows", split_axis=0, concat_axis=0, tiled=True)
@@ -1308,9 +1460,12 @@
         out_refs,
     )
     if fast:
-        out_first = chips_first(out_keep, out_got)
-        out_flips = send_chips(out_first)
-        grad_heads = after(grad_heads, *out_first)
+        out_keep = after(out_keep, back_parts[2], back_parts[5], reduced[0])
+        out_first = chip_adds(out_keep, out_got)
+        slots = after(slots, reduced[0], out_first[0])
+        reduced.append(lax.psum_scatter(slots, "cols", scatter_dimension=0, tiled=False))
+        out_flips = send_chips(out_first[:2])
+        grad_heads = after(grad_heads, out_first[0])
         router_parts = jnp.transpose(
             router_grad.astype(LOW).reshape(col_count, router_part, row_count, depth),
             (2, 0, 1, 3),
@@ -1328,15 +1483,22 @@
         info, queries, own_pair, partner, grad_heads, cosine, sine
     )
     arrived = lax.ppermute(source_grad.astype(LOW), "cols", [(j, i) for i, j in pairs])
+    if fast:
+        parts = ((0, 2, 0, query_part), (1, 3, query_part + 2 * key_part, query_part))
+        out_flips = after(out_flips, grad_query)
+        near_x, near_y = out_first[2:]
+        for_y, for_x = corner_adds(near_x, out_flips[0], near_y, out_flips[1])
+        mixture = (near_x, out_flips[0], flip(for_y, 4))
+        mixture += (near_y, out_flips[1], flip(for_x, 2))
+        grad_branch = after(grad_branch, for_y)
+        keep_send = weight_grads(
+            info, [normed, heads], [grad_query, grad_branch], parts, extra
+        )
+        arrived = after(arrived, *keep_send)
     grad_pair = join_grads(info, own_grad, source_grad, arrived, cosine, sine)
     if fast:
-        grad_branch = after(grad_branch, *out_flips)
         keep, send = weight_grads(
-            info,
-            [normed, heads],
-            [grad_query, grad_pair, grad_branch],
-            ((0, 2, query_part), (0, 3, 2 * key_part), (1, 4, query_part)),
-            extra,
+            info, [normed], [grad_pair], ((0, 1, 0, 2 * key_part),), None, keep_send
         )
         sent = flip(send, 1)
         grad_pair = after(grad_pair, keep)
@@ -1345,10 +1507,12 @@
     )
 
     if fast:
-        sent_first = chips_first(keep, sent)
-        sent_chips = send_chips(sent_first)
-        mixture = chips_second(out_keep, out_got, *out_flips)
-        slots = sum_parts(chips_second(keep, sent, *sent_chips))
+        flat = (4, col_count * (depth + EXTRA), wide)
+        sent = after(sent, mixture[2], mixture[5])
+        sent_first = chip_adds(keep.reshape(flat), sent.reshape(flat))
+        sent_chips = send_chips(sent_first[:2])
+        slots = sum_parts(chips_second(*sent_first[2:], *sent_chips))
+        slots = slots.reshape(col_count, depth + EXTRA, wide)
         width = query_part + 2 * key_part
         own_slots = own
         gain_sums = sum(

time: 837 us -> 755 us (0.902)
  waiting for transfers between devices: 372 us -> 264 us
  starting transfers between devices: 59.2 us -> 90 us
  other arithmetic: 59.7 us -> 32.6 us
  Pallas kernels: 277 us -> 297 us
    ppermute x1, waiting for transfers between devices: 49.4 us -> 5.36 us  [on_device(): partner = lax.ppermute(own_pair, 'cols', pairs)]
    pallas_call x9 -> x16, Pallas kernels: 93 us -> 122 us  [the longest x4 30.7 us: combine(): pl.pallas_call(functools.partial(combine_kernel, local, first, step), out...]
    convert_element_type x6 -> x0, other arithmetic: 22.8 us -> none  [add_low(): return (one.astype(WIDE) + two.astype(WIDE)).astype(LOW)]
    ppermute x1, waiting for transfers between devices: 21.6 us -> 2.57 us  [on_device(): lax.ppermute(source_grad.astype(LOW), 'cols', [(j, i) for i, j in pairs])]
    reduce_scatter x2, waiting for transfers between devices: 47 us -> 31.5 us  [on_device(): lax.psum_scatter(slots, 'cols', scatter_dimension=0, tiled=False)]
    all_gather x2 -> x1, waiting for transfers between devices: 13.2 us -> 0.01 us  [on_device(): expert_refs.append([lax.all_gather(later_block, 'cols', axis=0)])]
    ppermute x1, starting transfers between devices: 3.21 us -> 14.9 us  [reduce_first(): return (relay, lax.ppermute(fourth, 'cols', FAR))]
    ppermute x2 -> x4, starting transfers between devices: 3.36 us -> 14.8 us  [send_near(): return (lax.ppermute(block, 'cols', DOWN), lax.ppermute(block, 'cols', UP))]
  transfers between devices with their start and end apart: 53 -> 56, of which waited for: 29 -> 34; matrix products, arithmetic and copies ran while one was open for 10% -> 7% of each run, Pallas kernels for 32% -> 33%
where the time goes in v11:
time: 755 us; the launch traced here: 744 us
  Pallas kernels  297 us (39%)
  waiting for transfers between devices  264 us (35%)
  starting transfers between devices  90 us (12%)
  local copies, waits for them, and re-layouts  45.4 us (6%)
  other arithmetic  32.6 us (4%)
  between operations  15.2 us (2%)
    ppermute x39, waiting for transfers between devices, flip(): return lax.ppermute(block, 'rows', [(i, i ^ bit) for i in range(count)])  168 us
    pallas_call x2, Pallas kernels, expert(): pl.pallas_call(functools.partial(expert_kernel, slots), grid=(height // E...  60.8 us
    reduce_scatter x2, waiting for transfers between devices, on_device(): lax.psum_scatter(slots, 'cols', scatter_dimension=0, tiled=False)  31.5 us
    pallas_call x4, Pallas kernels, combine(): pl.pallas_call(functools.partial(combine_kernel, local, first, step), out...  30.7 us
    pallas_call x8, Pallas kernels, dispatch(): pl.pallas_call(functools.partial(dispatch_kernel, local), grid=(D // wide...  29.3 us
    pallas_call x2, Pallas kernels, expert_grads(): pl.pallas_call(expert_grads_kernel, grid=(D // 256,), out_shape=jax.Shape...  29.1 us
    ppermute x39, starting transfers between devices, flip(): return lax.ppermute(block, 'rows', [(i, i ^ bit) for i in range(count)])  24.7 us
    ppermute x4, waiting for transfers between devices, send_near(): return (lax.ppermute(block, 'cols', DOWN), lax.ppermute(block, 'cols', UP))  23.2 us
  transfers between devices with their start and end apart: 56, of which 34 were waited for; matrix products, arithmetic and copies ran while one was open for 7% of the time, Pallas kernels for 33%

profile of v11, /device:TPU:0, one launch (start us, length us, event | category | flops | bytes accessed | tf_op | source)
XLA Modules:
  0.0 743.9 jit_solution(4406698342337927778)
XLA Ops:
  14.1 6.3 collective-permute-start.1
  20.4 3.7 collective-permute-start.6
  32.0 4.7 collective-permute-done.6
  44.6 5.8 collective-permute-start.3
  55.4 4.7 collective-permute-done.7.rest_2_
  63.4 23.2 %collective-permute-done.2.rest_2_ = bf16[576,1536]{1,0:T(8,128)(2,1)S(1)} collective-permute-done((bf16[576,1536]{1,0:T(8,128)(2,1)S(1)}, bf16[576,1536]{1,0:T(8,128)(2,1)S(1)}, u32[]{:S(2)}, u32[]{:S(2)}) %collective-permute-start.2) | collective-permute-done | bytes 1769504 | tf_op jit(solution)/shard_map/ppermute | solution.py:1142
  86.6 9.8 %collective-permute-done.10.rest_2_.rest_8_.rest_11_ = bf16[4,208,896]{2,1,0:T(8,128)(2,1)S(1)} collective-permute-done((bf16[4,208,896]{2,1,0:T(8,128)(2,1)S(1)}, bf16[4,208,896]{2,1,0:T(8,128)(2,1)S(1)}, u32[]{:S(2)}, u32[]{:S(2)}) %collective-permute-start.10) | collective-permute-done | bytes 1490976 | tf_op jit(solution)/shard_map/ppermute | solution.py:1201
  103.8 12.5 %collective-permute-done.13.rest_4_.rest_10_.rest_13_ = bf16[2,208,896]{2,1,0:T(8,128)(2,1)S(1)} collective-permute-done((bf16[2,208,896]{2,1,0:T(8,128)(2,1)S(1)}, bf16[2,208,896]{2,1,0:T(8,128)(2,1)S(1)}, u32[]{:S(2)}, u32[]{:S(2)}) %collective-permute-start.13) | collective-permute-done | bytes 745504 | tf_op jit(solution)/shard_map/ppermute | solution.py:1201
  119.3 5.6 route_tables.1
  125.0 17.4 %collective-permute-done.4.rest_1_ = bf16[576,1536]{1,0:T(8,128)(2,1)S(1)} collective-permute-done((bf16[576,1536]{1,0:T(8,128)(2,1)}, bf16[576,1536]{1,0:T(8,128)(2,1)S(1)}, u32[]{:S(2)}, u32[]{:S(2)}) %collective-permute-start.4) | collective-permute-done | bytes 1769504 | tf_op jit(solution)/shard_map/ppermute | solution.py:1153
  147.8 5.0 norm_key_value.1
  154.1 8.3 %query_projection.1.queries = bf16[512,1536]{1,0:T(8,128)(2,1)} custom-call(s32[16]{0:T(128)} %concatenate.42.info, bf16[512,1536]{1,0:T(8,128)(2,1)} %get-tuple-element.138.normed.rest_0_, f32[512,128]{1,0:T(8,128)} %get-tuple-element.316.cosine, f32[512,128]{1,0:T(8,128)} %get-tuple-element.317.sine, bf16[4,208,896]{2,1,0:T(8,128)(2,1)} %copy-done.1, ...), custom_call_target="tpu_custom_call" | custom-call | flops 1 | bytes 1 | tf_op jit(solution)/shard_map/query_projection/pallas_call | solution.py:195
  162.4 5.4 collective-permute-done.17.partner
  167.8 4.0 collective-permute-start.32
  178.6 11.0 %tree_attention.1.heads.rest_1_ = bf16[512,1536]{1,0:T(8,128)(2,1)} custom-call(s32[16]{0:T(128)} %concatenate.42.info, bf16[512,1536]{1,0:T(8,128)(2,1)} %query_projection.1.queries, bf16[512,512]{1,0:T(8,128)(2,1)} %get-tuple-element.139.own, bf16[512,512]{1,0:T(8,128)(2,1)} %copy-done.39), custom_call_target="tpu_custom_call" | custom-call | flops 1 | bytes 1 | tf_op jit(solution)/shard_map/tree_attention/pallas_call | solution.py:277
  194.6 9.8 %out_projection.1 = (f32[512,1536]{1,0:T(8,128)}, bf16[512,1536]{1,0:T(8,128)(2,1)}) custom-call(s32[16]{0:T(128)} %concatenate.42.info, bf16[512,1536]{1,0:T(8,128)(2,1)} %tree_attention.1.heads.rest_1_, bf16[512,1536]{1,0:T(8,128)(2,1)} %tokens.4, f32[1,1536]{1,0:T(1,128)} %reshape.312.gain, bf16[4,208,896]{2,1,0:T(8,128)(2,1)} %copy-done.1, ...), custom_call_target="tpu_custom_call" | custom-call | flops 1 | bytes 1 | tf_op jit(solution)/shard_map/out_projection/pallas_call | solution.py:389
  204.5 5.8 collective-permute-done.32.rest_4_
  214.5 3.9 dispatch.8
  218.4 3.8 dispatch.9
  222.2 25.4 %collective-permute-done.20.rows = bf16[512,1536]{1,0:T(8,128)(2,1)} collective-permute-done((bf16[512,1536]{1,0:T(8,128)(2,1)S(1)}, bf16[512,1536]{1,0:T(8,128)(2,1)}, u32[]{:S(2)}, u32[]{:S(2)}) %collective-permute-start.20) | collective-permute-done | bytes 1572896 | tf_op jit(solution)/shard_map/ppermute | solution.py:1201
  248.7 4.9 collective-permute-done.25.rows
  263.7 9.3 %pick_rows.1 = (bf16[8,160,1536]{2,1,0:T(8,128)(2,1)}, bf16[8,160,1536]{2,1,0:T(8,128)(2,1)}) custom-call(bf16[8,320,512]{2,1,0:T(8,128)(2,1)} %get-tuple-element.136.chosen, bf16[512,1536]{1,0:T(8,128)(2,1)} %cotangent.1, bf16[512,1536]{1,0:T(8,128)(2,1)} %copy-done.41, bf16[512,1536]{1,0:T(8,128)(2,1)} %collective-permute-done.7.rest_2_, ...), custom_call_target="tpu_custom_call" | custom-call | flops 1 | bytes 1 | tf_op jit(solution)/shard_map/pick_rows/pallas_call | solution.py:480
  283.8 3.6 dispatch.13
  299.4 30.7 %expert.2 = (bf16[1280,1536]{1,0:T(8,128)(2,1)}, bf16[1280,1536]{1,0:T(8,128)(2,1)}, bf16[1280,1536]{1,0:T(8,128)(2,1)}, bf16[4,576,1280]{2,1,0:T(8,128)(2,1)}, f32[1280,1]{1,0:T(8,128)}) custom-call(s32[16]{0:T(128)} %concatenate.42.info, bf16[1280,1536]{1,0:T(8,128)(2,1)} %bitcast.145, bf16[1280,1536]{1,0:T(8,128)(2,1)} %bitcast.164, f32[1280,1]{1,0:T(8,128)} %bitcast.149, ...), custom_call_target="tpu_custom_call" | custom-call | flops 1 | bytes 1 | tf_op jit(solution)/shard_map/expert/pallas_call | solution.py:670
  330.1 14.6 %expert_gradients.2 = bf16[4,576,1536]{2,1,0:T(8,128)(2,1)} custom-call(bf16[4,576,1280]{2,1,0:T(8,128)(2,1)} %get-tuple-element.190.acts, bf16[1280,1536]{1,0:T(8,128)(2,1)} %bitcast.146, bf16[1280,1536]{1,0:T(8,128)(2,1)} %get-tuple-element.191.grads), custom_call_target="tpu_custom_call" | custom-call | flops 1 | bytes 1 | tf_op jit(solution)/shard_map/expert_gradients/pallas_call | solution.py:699
  344.7 30.1 %expert.3 = (bf16[1280,1536]{1,0:T(8,128)(2,1)}, bf16[1280,1536]{1,0:T(8,128)(2,1)}, bf16[1280,1536]{1,0:T(8,128)(2,1)}, bf16[4,576,1280]{2,1,0:T(8,128)(2,1)}, f32[1280,1]{1,0:T(8,128)}) custom-call(s32[16]{0:T(128)} %concatenate.42.info, bf16[1280,1536]{1,0:T(8,128)(2,1)} %bitcast.147, bf16[1280,1536]{1,0:T(8,128)(2,1)} %bitcast.165, f32[1280,1]{1,0:T(8,128)} %bitcast.150, ...), custom_call_target="tpu_custom_call" | custom-call | flops 1 | bytes 1 | tf_op jit(solution)/shard_map/expert/pallas_call | solution.py:670
  374.8 8.0 %combine.5 = bf16[4,544,1536]{2,1,0:T(8,128)(2,1)} custom-call(s32[16]{0:T(128)} %concatenate.42.info, bf16[8,320,512]{2,1,0:T(8,128)(2,1)} %get-tuple-element.136.chosen, bf16[8,160,1536]{2,1,0:T(8,128)(2,1)} %bitcast.158, bf16[8,160,1536]{2,1,0:T(8,128)(2,1)} %bitcast.160, f32[8,160,1]{2,1,0:T(8,128)} %bitcast.167, f32[8,160,1]{2,1,0:T(8,128)} %bitcast.169), custom_call_target="tpu_custom_call" | custom-call | flops 1 | bytes 1 | tf_op jit(solution)/shard_map/combine/pallas_call | solution.py:762
  383.2 8.0 %combine.4.keep = bf16[4,544,1536]{2,1,0:T(8,128)(2,1)} custom-call(s32[16]{0:T(128)} %concatenate.42.info, bf16[8,320,512]{2,1,0:T(8,128)(2,1)} %get-tuple-element.136.chosen, bf16[8,160,1536]{2,1,0:T(8,128)(2,1)} %bitcast.159, bf16[8,160,1536]{2,1,0:T(8,128)(2,1)} %bitcast.161, f32[8,160,1]{2,1,0:T(8,128)} %bitcast.168, f32[8,160,1]{2,1,0:T(8,128)} %bitcast.170), custom_call_target="tpu_custom_call" | custom-call | flops 1 | bytes 1 | tf_op jit(solution)/shard_map/combine/pallas_call | solution.py:762
  393.9 7.8 %chip_sums.3 = (bf16[2,272,1536]{2,1,0:T(8,128)(2,1)}, bf16[2,272,1536]{2,1,0:T(8,128)(2,1)}, bf16[2,272,1536]{2,1,0:T(8,128)(2,1)}, bf16[2,272,1536]{2,1,0:T(8,128)(2,1)}) custom-call(bf16[4,544,1536]{2,1,0:T(8,128)(2,1)} %combine.4.keep, bf16[4,544,1536]{2,1,0:T(8,128)(2,1)} %collective-permute-done.33.got), custom_call_target="tpu_custom_call" | custom-call | flops 1 | bytes 1 | tf_op jit(solution)/shard_map/chip_sums/pallas_call | solution.py:811
  403.8 14.6 %expert_gradients.3 = bf16[4,576,1536]{2,1,0:T(8,128)(2,1)} custom-call(bf16[4,576,1280]{2,1,0:T(8,128)(2,1)} %get-tuple-element.201.acts, bf16[1280,1536]{1,0:T(8,128)(2,1)} %bitcast.148, bf16[1280,1536]{1,0:T(8,128)(2,1)} %get-tuple-element.202.grads), custom_call_target="tpu_custom_call" | custom-call | flops 1 | bytes 1 | tf_op jit(solution)/shard_map/expert_gradients/pallas_call | solution.py:699
  418.3 22.2 %collective-permute-done.34.got_x.rest_1_ = bf16[2,272,1536]{2,1,0:T(8,128)(2,1)S(1)} collective-permute-done((bf16[2,272,1536]{2,1,0:T(8,128)(2,1)}, bf16[2,272,1536]{2,1,0:T(8,128)(2,1)S(1)}, u32[]{:S(2)}, u32[]{:S(2)}) %collective-permute-start.34) | collective-permute-done | bytes 1671200 | tf_op jit(solution)/shard_map/ppermute | solution.py:1201
  441.7 7.3 combine.7
  453.7 7.3 combine.6.keep
  461.0 12.7 %collective-permute-done.36.rest_2_ = bf16[272,1536]{1,0:T(8,128)(2,1)} collective-permute-done((bf16[272,1536]{1,0:T(8,128)(2,1)}, bf16[272,1536]{1,0:T(8,128)(2,1)}, u32[]{:S(2)}, u32[]{:S(2)}) %collective-permute-start.36) | collective-permute-done | bytes 835616 | tf_op jit(solution)/shard_map/ppermute | solution.py:1201
  474.0 31.5 %reduce-scatter.3.cloned.1.call-done = bf16[1,576,1536]{2,1,0:T(8,128)(2,1)} async-done(((bf16[4,576,1536]{2,1,0:T(8,128)(2,1)}), bf16[1,576,1536]{2,1,0:T(8,128)(2,1)}) %reduce-scatter.3.cloned.1.call-update) | async-done | bytes 1769488 | tf_op jit(solution)/shard_map/reduce_scatter | solution.py:1433
  505.5 7.4 chip_sums.4
  515.9 12.4 %experts_norm_back.1 = (f32[512,1536]{1,0:T(8,128)}, bf16[512,1536]{1,0:T(8,128)(2,1)}, bf16[512,1536]{1,0:T(8,128)(2,1)}, f32[1,1536]{1,0:T(1,128)}, f32[16,1536]{1,0:T(8,128)}) custom-call(s32[16]{0:T(128)} %concatenate.42.info, f32[512,1536]{1,0:T(8,128)} %get-tuple-element.143.residual, bf16[512,1536]{1,0:T(8,128)(2,1)} %get-tuple-element.144.rows.normed, ...), custom_call_target="tpu_custom_call" | custom-call | flops 1 | bytes 1 | tf_op jit(solution)/shard_map/experts_norm_back/pallas_call | solution.py:922
  528.3 15.4 %tree_attention_back.1 = (bf16[512,1536]{1,0:T(8,128)(2,1)}, f32[512,512]{1,0:T(8,128)}, f32[512,512]{1,0:T(8,128)}) custom-call(s32[16]{0:T(128)} %concatenate.42.info, bf16[512,1536]{1,0:T(8,128)(2,1)} %query_projection.1.queries, bf16[512,512]{1,0:T(8,128)(2,1)} %get-tuple-element.139.own, bf16[512,512]{1,0:T(8,128)(2,1)} %copy-done.39, ...), custom_call_target="tpu_custom_call" | custom-call | flops 1 | bytes 1 | tf_op jit(solution)/shard_map/tree_attention_back/pallas_call | solution.py:338
  545.9 4.2 collective-permute-start.43
  556.4 13.6 %weight_gradients.2 = (bf16[4,4,208,896]{3,2,1,0:T(8,128)(2,1)}, bf16[4,4,208,896]{3,2,1,0:T(8,128)(2,1)}) custom-call(s32[16]{0:T(128)} %concatenate.42.info, bf16[512,1536]{1,0:T(8,128)(2,1)} %get-tuple-element.138.normed.rest_0_, bf16[512,1536]{1,0:T(8,128)(2,1)} %tree_attention.1.heads.rest_1_, bf16[512,1536]{1,0:T(8,128)(2,1)} %get-tuple-element.224.rest_2_.grad_query, ...), custom_call_target="tpu_custom_call" | custom-call | flops 1 | bytes 1 | tf_op jit(solution)/shard_map/weight_gradients/pallas_call | solution.py:1087
  575.7 5.8 weight_gradients.3
  582.7 18.8 %collective-permute-done.42 = bf16[256,1536]{1,0:T(8,128)(2,1)S(1)} collective-permute-done((bf16[256,1536]{1,0:T(8,128)(2,1)S(1)}, bf16[256,1536]{1,0:T(8,128)(2,1)S(1)}, u32[]{:S(2)}, u32[]{:S(2)}) %collective-permute-start.42) | collective-permute-done | bytes 786464 | tf_op jit(solution)/shard_map/ppermute | solution.py:1201
  604.5 7.3 chip_sums.5
  617.7 28.6 %collective-permute-done.45.got_x = bf16[2,416,896]{2,1,0:T(8,128)(2,1)S(1)} collective-permute-done((bf16[2,416,896]{2,1,0:T(8,128)(2,1)}, bf16[2,416,896]{2,1,0:T(8,128)(2,1)S(1)}, u32[]{:S(2)}, u32[]{:S(2)}) %collective-permute-start.45) | collective-permute-done | bytes 1490976 | tf_op jit(solution)/shard_map/ppermute | solution.py:1201
  653.7 12.7 %token_gradient.1 = (bf16[512,1536]{1,0:T(8,128)(2,1)}, f32[1,1536]{1,0:T(1,128)}) custom-call(s32[16]{0:T(128)} %concatenate.42.info, bf16[512,1536]{1,0:T(8,128)(2,1)} %get-tuple-element.224.rest_2_.grad_query, bf16[512,512]{1,0:T(8,128)(2,1)} %join_key_value_gradients.1.rest_1_.grad_pair, bf16[512,1536]{1,0:T(8,128)(2,1)} %tokens.4, ...), custom_call_target="tpu_custom_call" | custom-call | flops 1 | bytes 1 | tf_op jit(solution)/shard_map/token_gradient/pallas_call | solution.py:1013
  670.0 13.3 %collective-permute-done.47 = bf16[416,896]{1,0:T(8,128)(2,1)S(1)} collective-permute-done((bf16[416,896]{1,0:T(8,128)(2,1)S(1)}, bf16[416,896]{1,0:T(8,128)(2,1)S(1)}, u32[]{:S(2)}, u32[]{:S(2)}) %collective-permute-start.47) | collective-permute-done | bytes 745504 | tf_op jit(solution)/shard_map/ppermute | solution.py:1201
  689.2 14.9 %collective-permute-start.52 = (bf16[208,896]{1,0:T(8,128)(2,1)S(1)}, bf16[208,896]{1,0:T(8,128)(2,1)S(1)}, u32[]{:S(2)}, u32[]{:S(2)}) collective-permute-start(bf16[208,896]{1,0:T(8,128)(2,1)S(1)} %get-tuple-element.290), channel_id=1, source_target_pairs={{0,3},{3,0},{4,7},{7,4},{8,11},{11,8},{12,15},{15,12},{16,19},{19,... | collective-permute-start | bytes 1118216 | tf_op jit(solution)/shard_map/ppermute | solution.py:1170
  707.8 13.4 %collective-permute-start.50 = (bf16[208,896]{1,0:T(8,128)(2,1)S(1)}, bf16[208,896]{1,0:T(8,128)(2,1)S(1)}, u32[]{:S(2)}, u32[]{:S(2)}) collective-permute-start(bf16[208,896]{1,0:T(8,128)(2,1)S(1)} %get-tuple-element.285), channel_id=1, source_target_pairs={{0,1},{1,2},{2,3},{4,5},{5,6},{6,7},{8,9},{9,10},{10,11},{12,13},{... | collective-permute-start | bytes 1118216 | tf_op jit(solution)/shard_map/ppermute | solution.py:1181
  (329 shorter events, 172.6 us)
Async XLA Ops:
  7.2 337.5 %all-gather.3.cloned.1.call-start = ((), (), s32[]{:S(2)}) async-start(), calls=%async_computation.4 | async-start | bytes 8847360 | tf_op jit(solution)/shard_map/all_gather | solution.py:1376
  12.7 19.3 %collective-permute-start = (bf16[208,896]{1,0:T(8,128)(2,1)S(1)}, bf16[208,896]{1,0:T(8,128)(2,1)}, u32[]{:S(2)}, u32[]{:S(2)}) collective-permute-start(bf16[208,896]{1,0:T(8,128)(2,1)S(1)} %concatenate.46), channel_id=1, source_target_pairs={{1,0},{2,1},{3,2},{5,4},{6,5},{7,6},{9,8},{10,9},{11,10},{13,12},{... | collective-permute-start | bytes 1118216 | tf_op jit(solution)/shard_map/ppermute | solution.py:1142
  14.1 17.9 %collective-permute-start.1 = (bf16[208,896]{1,0:T(8,128)(2,1)S(1)}, bf16[208,896]{1,0:T(8,128)(2,1)}, u32[]{:S(2)}, u32[]{:S(2)}) collective-permute-start(bf16[208,896]{1,0:T(8,128)(2,1)S(1)} %concatenate.46), channel_id=1, source_target_pairs={{0,1},{1,2},{2,3},{4,5},{5,6},{6,7},{8,9},{9,10},{10,11},{12,13},{... | collective-permute-start | bytes 1118216 | tf_op jit(solution)/shard_map/ppermute | solution.py:1142
  20.4 16.3 %collective-permute-start.6 = (bf16[208,896]{1,0:T(8,128)(2,1)S(1)}, bf16[208,896]{1,0:T(8,128)(2,1)}, u32[]{:S(2)}, u32[]{:S(2)}) collective-permute-start(bf16[208,896]{1,0:T(8,128)(2,1)S(1)} %concatenate.46), channel_id=1, source_target_pairs={{0,3},{3,0},{4,7},{7,4},{8,11},{11,8},{12,15},{15,12},{16,19},{19,... | collective-permute-start | bytes 1118216 | tf_op jit(solution)/shard_map/ppermute | solution.py:1146
  24.2 36.0 %collective-permute-start.7 = (bf16[512,1536]{1,0:T(8,128)(2,1)}, bf16[512,1536]{1,0:T(8,128)(2,1)}, u32[]{:S(2)}, u32[]{:S(2)}) collective-permute-start(bf16[512,1536]{1,0:T(8,128)(2,1)} %cotangent.1), channel_id=1, source_target_pairs={{0,8},{4,12},{8,0},{12,4},{16,24},{20,28},{24,16},{28,20},{1,9},{5... | collective-permute-start | bytes 4718600 | tf_op jit(solution)/shard_map/ppermute | solution.py:1201
  25.7 35.6 %collective-permute-start.8 = (bf16[512,1536]{1,0:T(8,128)(2,1)}, bf16[512,1536]{1,0:T(8,128)(2,1)}, u32[]{:S(2)}, u32[]{:S(2)}) collective-permute-start(bf16[512,1536]{1,0:T(8,128)(2,1)} %cotangent.1), channel_id=1, source_target_pairs={{0,16},{4,20},{8,24},{12,28},{16,0},{20,4},{24,8},{28,12},{1,17},{... | collective-permute-start | bytes 4718600 | tf_op jit(solution)/shard_map/ppermute | solution.py:1201
  38.9 15.2 %collective-permute-start.5 = (bf16[208,896]{1,0:T(8,128)(2,1)}, bf16[208,896]{1,0:T(8,128)(2,1)}, u32[]{:S(2)}, u32[]{:S(2)}) collective-permute-start(bf16[208,896]{1,0:T(8,128)(2,1)} %get-tuple-element.308), channel_id=1, source_target_pairs={{3,1},{1,0},{0,2},{2,3},{7,5},{5,4},{4,6},{6,7},{11,9},{9,8},{8,10... | collective-permute-start | bytes 1118216 | tf_op jit(solution)/shard_map/ppermute | solution.py:1153
  43.3 43.3 %collective-permute-start.2 = (bf16[576,1536]{1,0:T(8,128)(2,1)S(1)}, bf16[576,1536]{1,0:T(8,128)(2,1)S(1)}, u32[]{:S(2)}, u32[]{:S(2)}) collective-permute-start(bf16[576,1536]{1,0:T(8,128)(2,1)S(1)} %pad_maximum_fusion.3.rest_0_), channel_id=1, source_target_pairs={{1,0},{2,1},{3,2},{5,4},{6,5},{7,6},{9,8},{10,9},{11,10},{13,12},{... | collective-permute-start | bytes 5308424 | tf_op jit(solution)/shard_map/ppermute | solution.py:1142
  44.6 42.0 %collective-permute-start.3 = (bf16[576,1536]{1,0:T(8,128)(2,1)S(1)}, bf16[576,1536]{1,0:T(8,128)(2,1)}, u32[]{:S(2)}, u32[]{:S(2)}) collective-permute-start(bf16[576,1536]{1,0:T(8,128)(2,1)S(1)} %pad_maximum_fusion.3.rest_0_), channel_id=1, source_target_pairs={{0,1},{1,2},{2,3},{4,5},{5,6},{6,7},{8,9},{9,10},{10,11},{12,13},{... | collective-permute-start | bytes 5308424 | tf_op jit(solution)/shard_map/ppermute | solution.py:1142
  61.3 25.3 %collective-permute-start.9 = (bf16[4,208,896]{2,1,0:T(8,128)(2,1)S(1)}, bf16[4,208,896]{2,1,0:T(8,128)(2,1)S(1)}, u32[]{:S(2)}, u32[]{:S(2)}) collective-permute-start(bf16[4,208,896]{2,1,0:T(8,128)(2,1)S(1)} %pad_maximum_fusion.5.rest_0_.rest_6_.rest_9_), channel_id=1, source_target_pairs={{0,4},{4,0},{8,12},{12,8},{16,20},{20,16},{24,28},{28,24},{1,5},{5... | collective-permute-start | bytes 4472840 | tf_op jit(solution)/shard_map/ppermute | solution.py:1201
  61.3 35.1 %collective-permute-start.10 = (bf16[4,208,896]{2,1,0:T(8,128)(2,1)S(1)}, bf16[4,208,896]{2,1,0:T(8,128)(2,1)S(1)}, u32[]{:S(2)}, u32[]{:S(2)}) collective-permute-start(bf16[4,208,896]{2,1,0:T(8,128)(2,1)S(1)} %pad_maximum_fusion.5.rest_0_.rest_6_.rest_9_), channel_id=1, source_target_pairs={{0,8},{4,12},{8,0},{12,4},{16,24},{20,28},{24,16},{28,20},{1,9},{5... | collective-permute-start | bytes 4472840 | tf_op jit(solution)/shard_map/ppermute | solution.py:1201
  61.9 34.8 %collective-permute-start.11 = (bf16[4,208,896]{2,1,0:T(8,128)(2,1)S(1)}, bf16[4,208,896]{2,1,0:T(8,128)(2,1)S(1)}, u32[]{:S(2)}, u32[]{:S(2)}) collective-permute-start(bf16[4,208,896]{2,1,0:T(8,128)(2,1)S(1)} %pad_maximum_fusion.5.rest_0_.rest_6_.rest_9_), channel_id=1, source_target_pairs={{0,16},{4,20},{8,24},{12,28},{16,0},{20,4},{24,8},{28,12},{1,17},{... | collective-permute-start | bytes 4472840 | tf_op jit(solution)/shard_map/ppermute | solution.py:1201
  97.0 20.7 %collective-permute-start.12 = (bf16[8,208,896]{2,1,0:T(8,128)(2,1)S(1)}, bf16[8,208,896]{2,1,0:T(8,128)(2,1)S(1)}, u32[]{:S(2)}, u32[]{:S(2)}) collective-permute-start(bf16[8,208,896]{2,1,0:T(8,128)(2,1)S(1)} %pad_maximum_fusion), channel_id=1, source_target_pairs={{0,4},{4,0},{8,12},{12,8},{16,20},{20,16},{24,28},{28,24},{1,5},{5... | collective-permute-start | bytes 8945672 | tf_op jit(solution)/shard_map/ppermute | solution.py:1201
  97.2 19.1 %collective-permute-start.13 = (bf16[2,208,896]{2,1,0:T(8,128)(2,1)S(1)}, bf16[2,208,896]{2,1,0:T(8,128)(2,1)S(1)}, u32[]{:S(2)}, u32[]{:S(2)}) collective-permute-start(bf16[2,208,896]{2,1,0:T(8,128)(2,1)S(1)} %slice.200), channel_id=1, source_target_pairs={{0,16},{4,20},{8,24},{12,28},{16,0},{20,4},{24,8},{28,12},{1,17},{... | collective-permute-start | bytes 2236424 | tf_op jit(solution)/shard_map/ppermute | solution.py:1201
  98.8 18.9 %collective-permute-start.15 = (bf16[2,208,896]{2,1,0:T(8,128)(2,1)S(1)}, bf16[2,208,896]{2,1,0:T(8,128)(2,1)}, u32[]{:S(2)}, u32[]{:S(2)}) collective-permute-start(bf16[2,208,896]{2,1,0:T(8,128)(2,1)S(1)} %slice.203), channel_id=1, source_target_pairs={{0,8},{4,12},{8,0},{12,4},{16,24},{20,28},{24,16},{28,20},{1,9},{5... | collective-permute-start | bytes 2236424 | tf_op jit(solution)/shard_map/ppermute | solution.py:1201
  101.7 40.7 %collective-permute-start.4 = (bf16[576,1536]{1,0:T(8,128)(2,1)}, bf16[576,1536]{1,0:T(8,128)(2,1)S(1)}, u32[]{:S(2)}, u32[]{:S(2)}) collective-permute-start(bf16[576,1536]{1,0:T(8,128)(2,1)} %select_select_fusion), channel_id=1, source_target_pairs={{3,1},{1,0},{0,2},{2,3},{7,5},{5,4},{4,6},{6,7},{11,9},{9,8},{8,10... | collective-permute-start | bytes 5308424 | tf_op jit(solution)/shard_map/ppermute | solution.py:1153
  117.6 24.7 %collective-permute-start.16 = (bf16[2,208,896]{2,1,0:T(8,128)(2,1)}, bf16[2,208,896]{2,1,0:T(8,128)(2,1)S(1)}, u32[]{:S(2)}, u32[]{:S(2)}) collective-permute-start(bf16[2,208,896]{2,1,0:T(8,128)(2,1)} %collective-permute-done.15.rest_5_.rest_11_.rest_14_), channel_id=1, source_target_pairs={{0,4},{4,0},{8,12},{12,8},{16,20},{20,16},{24,28},{28,24},{1,5},{5... | collective-permute-start | bytes 2236424 | tf_op jit(solution)/shard_map/ppermute | solution.py:1201
  152.8 15.0 %collective-permute-start.17 = (bf16[512,512]{1,0:T(8,128)(2,1)}, bf16[512,512]{1,0:T(8,128)(2,1)S(1)}, u32[]{:S(2)}, u32[]{:S(2)}) collective-permute-start(bf16[512,512]{1,0:T(8,128)(2,1)} %get-tuple-element.139.own), channel_id=1, source_target_pairs={{1,0},{3,2},{5,4},{7,6},{9,8},{11,10},{13,12},{15,14},{17,16},{19,... | collective-permute-start | bytes 1572872 | tf_op jit(solution)/shard_map/ppermute | solution.py:1355
  167.8 42.4 %collective-permute-start.32 = (bf16[576,1536]{1,0:T(8,128)(2,1)S(1)}, bf16[576,1536]{1,0:T(8,128)(2,1)}, u32[]{:S(2)}, u32[]{:S(2)}) collective-permute-start(bf16[576,1536]{1,0:T(8,128)(2,1)S(1)} %copy-done.11), channel_id=1, source_target_pairs={{0,3},{3,0},{4,7},{7,4},{8,11},{11,8},{12,15},{15,12},{16,19},{19,... | collective-permute-start | bytes 5308424 | tf_op jit(solution)/shard_map/ppermute | solution.py:1146
  173.8 17.6 %collective-permute-start.18 = (bf16[256,1536]{1,0:T(8,128)(2,1)}, bf16[256,1536]{1,0:T(8,128)(2,1)}, u32[]{:S(2)}, u32[]{:S(2)}) collective-permute-start(bf16[256,1536]{1,0:T(8,128)(2,1)} %slice.205), channel_id=1, source_target_pairs={{0,16},{4,20},{8,24},{12,28},{16,0},{20,4},{24,8},{28,12},{1,17},{... | collective-permute-start | bytes 2359304 | tf_op jit(solution)/shard_map/ppermute | solution.py:1201
  176.4 17.2 %collective-permute-start.19 = (bf16[256,1536]{1,0:T(8,128)(2,1)}, bf16[256,1536]{1,0:T(8,128)(2,1)S(1)}, u32[]{:S(2)}, u32[]{:S(2)}) collective-permute-start(bf16[256,1536]{1,0:T(8,128)(2,1)} %slice.206), channel_id=1, source_target_pairs={{0,8},{4,12},{8,0},{12,4},{16,24},{20,28},{24,16},{28,20},{1,9},{5... | collective-permute-start | bytes 2359304 | tf_op jit(solution)/shard_map/ppermute | solution.py:1201
  210.3 295.2 %reduce-scatter.3.cloned.1.call-start = ((), (), s32[]{:S(2)}) async-start(), calls=%async_computation.2 | async-start | bytes 8847360 | tf_op jit(solution)/shard_map/reduce_scatter | solution.py:1433
  210.6 36.9 %collective-permute-start.20 = (bf16[512,1536]{1,0:T(8,128)(2,1)S(1)}, bf16[512,1536]{1,0:T(8,128)(2,1)}, u32[]{:S(2)}, u32[]{:S(2)}) collective-permute-start(bf16[512,1536]{1,0:T(8,128)(2,1)S(1)} %copy-done.16), channel_id=1, source_target_pairs={{0,8},{4,12},{8,0},{12,4},{16,24},{20,28},{24,16},{28,20},{1,9},{5... | collective-permute-start | bytes 4718600 | tf_op jit(solution)/shard_map/ppermute | solution.py:1201
  211.2 36.5 %collective-permute-start.21 = (bf16[512,1536]{1,0:T(8,128)(2,1)S(1)}, bf16[512,1536]{1,0:T(8,128)(2,1)S(1)}, u32[]{:S(2)}, u32[]{:S(2)}) collective-permute-start(bf16[512,1536]{1,0:T(8,128)(2,1)S(1)} %copy-done.16), channel_id=1, source_target_pairs={{0,16},{4,20},{8,24},{12,28},{16,0},{20,4},{24,8},{28,12},{1,17},{... | collective-permute-start | bytes 4718600 | tf_op jit(solution)/shard_map/ppermute | solution.py:1201
  248.7 13.8 %collective-permute-start.30 = (bf16[512,1536]{1,0:T(8,128)(2,1)}, bf16[512,1536]{1,0:T(8,128)(2,1)S(1)}, u32[]{:S(2)}, u32[]{:S(2)}) collective-permute-start(bf16[512,1536]{1,0:T(8,128)(2,1)} %constant_dynamic-update-slice_fusion.8.rest_6_), channel_id=1, source_target_pairs={{0,4},{4,0},{8,12},{12,8},{16,20},{20,16},{24,28},{28,24},{1,5},{5... | collective-permute-start | bytes 4718600 | tf_op jit(solution)/shard_map/ppermute | solution.py:1201
  253.7 30.1 %collective-permute-start.26 = (bf16[512,1536]{1,0:T(8,128)(2,1)S(1)}, bf16[512,1536]{1,0:T(8,128)(2,1)}, u32[]{:S(2)}, u32[]{:S(2)}) collective-permute-start(bf16[512,1536]{1,0:T(8,128)(2,1)S(1)} %collective-permute-done.21.rows), channel_id=1, source_target_pairs={{0,4},{4,0},{8,12},{12,8},{16,20},{20,16},{24,28},{28,24},{1,5},{5... | collective-permute-start | bytes 4718600 | tf_op jit(solution)/shard_map/ppermute | solution.py:1201
  256.9 30.5 %collective-permute-start.23 = (bf16[256,1536]{1,0:T(8,128)(2,1)}, bf16[256,1536]{1,0:T(8,128)(2,1)}, u32[]{:S(2)}, u32[]{:S(2)}) collective-permute-start(bf16[256,1536]{1,0:T(8,128)(2,1)} %slice.209), channel_id=1, source_target_pairs={{0,16},{4,20},{8,24},{12,28},{16,0},{20,4},{24,8},{28,12},{1,17},{... | collective-permute-start | bytes 2359304 | tf_op jit(solution)/shard_map/ppermute | solution.py:1201
  257.0 30.4 %collective-permute-start.24 = (bf16[256,1536]{1,0:T(8,128)(2,1)}, bf16[256,1536]{1,0:T(8,128)(2,1)}, u32[]{:S(2)}, u32[]{:S(2)}) collective-permute-start(bf16[256,1536]{1,0:T(8,128)(2,1)} %slice.210), channel_id=1, source_target_pairs={{0,8},{4,12},{8,0},{12,4},{16,24},{20,28},{24,16},{28,20},{1,9},{5... | collective-permute-start | bytes 2359304 | tf_op jit(solution)/shard_map/ppermute | solution.py:1201
  383.0 347.0 %reduce-scatter.5.cloned.1.call-start = ((), (), s32[]{:S(2)}) async-start(), calls=%async_computation.3 | async-start | bytes 8847360 | tf_op jit(solution)/shard_map/reduce_scatter | solution.py:1466
  401.7 38.8 %collective-permute-start.34 = (bf16[2,272,1536]{2,1,0:T(8,128)(2,1)}, bf16[2,272,1536]{2,1,0:T(8,128)(2,1)S(1)}, u32[]{:S(2)}, u32[]{:S(2)}) collective-permute-start(bf16[2,272,1536]{2,1,0:T(8,128)(2,1)} %get-tuple-element.198), channel_id=1, source_target_pairs={{0,8},{4,12},{8,0},{12,4},{16,24},{20,28},{24,16},{28,20},{1,9},{5... | collective-permute-start | bytes 5013512 | tf_op jit(solution)/shard_map/ppermute | solution.py:1201
  403.2 38.5 %collective-permute-start.35 = (bf16[2,272,1536]{2,1,0:T(8,128)(2,1)}, bf16[2,272,1536]{2,1,0:T(8,128)(2,1)S(1)}, u32[]{:S(2)}, u32[]{:S(2)}) collective-permute-start(bf16[2,272,1536]{2,1,0:T(8,128)(2,1)} %get-tuple-element.199), channel_id=1, source_target_pairs={{0,16},{4,20},{8,24},{12,28},{16,0},{20,4},{24,8},{28,12},{1,17},{... | collective-permute-start | bytes 5013512 | tf_op jit(solution)/shard_map/ppermute | solution.py:1201
  449.0 24.9 %collective-permute-start.38 = (bf16[4,512,1536]{2,1,0:T(8,128)(2,1)}, bf16[4,512,1536]{2,1,0:T(8,128)(2,1)}, u32[]{:S(2)}, u32[]{:S(2)}) collective-permute-start(bf16[4,512,1536]{2,1,0:T(8,128)(2,1)} %combine.7), channel_id=1, source_target_pairs={{0,4},{4,0},{8,12},{12,8},{16,20},{20,16},{24,28},{28,24},{1,5},{5... | collective-permute-start | bytes 18874376 | tf_op jit(solution)/shard_map/ppermute | solution.py:1201
  452.4 21.3 %collective-permute-start.36 = (bf16[272,1536]{1,0:T(8,128)(2,1)}, bf16[272,1536]{1,0:T(8,128)(2,1)}, u32[]{:S(2)}, u32[]{:S(2)}) collective-permute-start(bf16[272,1536]{1,0:T(8,128)(2,1)} %get-tuple-element.210), channel_id=1, source_target_pairs={{0,16},{4,20},{8,24},{12,28},{16,0},{20,4},{24,8},{28,12},{1,17},{... | collective-permute-start | bytes 2506760 | tf_op jit(solution)/shard_map/ppermute | solution.py:1201
  452.9 21.0 %collective-permute-start.37 = (bf16[272,1536]{1,0:T(8,128)(2,1)}, bf16[272,1536]{1,0:T(8,128)(2,1)}, u32[]{:S(2)}, u32[]{:S(2)}) collective-permute-start(bf16[272,1536]{1,0:T(8,128)(2,1)} %get-tuple-element.211), channel_id=1, source_target_pairs={{0,8},{4,12},{8,0},{12,4},{16,24},{20,28},{24,16},{28,20},{1,9},{5... | collective-permute-start | bytes 2506760 | tf_op jit(solution)/shard_map/ppermute | solution.py:1201
  512.8 38.7 %collective-permute-start.39 = (bf16[2,256,1536]{2,1,0:T(8,128)(2,1)}, bf16[2,256,1536]{2,1,0:T(8,128)(2,1)S(1)}, u32[]{:S(2)}, u32[]{:S(2)}) collective-permute-start(bf16[2,256,1536]{2,1,0:T(8,128)(2,1)} %get-tuple-element.216), channel_id=1, source_target_pairs={{0,8},{4,12},{8,0},{12,4},{16,24},{20,28},{24,16},{28,20},{1,9},{5... | collective-permute-start | bytes 4718600 | tf_op jit(solution)/shard_map/ppermute | solution.py:1201
  514.4 37.2 %collective-permute-start.40 = (bf16[2,256,1536]{2,1,0:T(8,128)(2,1)}, bf16[2,256,1536]{2,1,0:T(8,128)(2,1)S(1)}, u32[]{:S(2)}, u32[]{:S(2)}) collective-permute-start(bf16[2,256,1536]{2,1,0:T(8,128)(2,1)} %get-tuple-element.217), channel_id=1, source_target_pairs={{0,16},{4,20},{8,24},{12,28},{16,0},{20,4},{24,8},{28,12},{1,17},{... | collective-permute-start | bytes 4718600 | tf_op jit(solution)/shard_map/ppermute | solution.py:1201
  545.9 26.7 %collective-permute-start.43 = (bf16[512,512]{1,0:T(8,128)(2,1)}, bf16[512,512]{1,0:T(8,128)(2,1)}, u32[]{:S(2)}, u32[]{:S(2)}) collective-permute-start(bf16[512,512]{1,0:T(8,128)(2,1)} %convert_element_type.158), channel_id=1, source_target_pairs={{0,1},{2,3},{4,5},{6,7},{8,9},{10,11},{12,13},{14,15},{16,17},{18,... | collective-permute-start | bytes 1572872 | tf_op jit(solution)/shard_map/ppermute | solution.py:1485
  581.5 20.3 %collective-permute-start.44 = (bf16[4,4,208,896]{3,2,1,0:T(8,128)(2,1)}, bf16[4,4,208,896]{3,2,1,0:T(8,128)(2,1)S(1)}, u32[]{:S(2)}, u32[]{:S(2)}) collective-permute-start(bf16[4,4,208,896]{3,2,1,0:T(8,128)(2,1)} %get-tuple-element.243), channel_id=1, source_target_pairs={{0,4},{4,0},{8,12},{12,8},{16,20},{20,16},{24,28},{28,24},{1,5},{5... | collective-permute-start | bytes 17891336 | tf_op jit(solution)/shard_map/ppermute | solution.py:1201
  581.5 20.0 %collective-permute-start.42 = (bf16[256,1536]{1,0:T(8,128)(2,1)S(1)}, bf16[256,1536]{1,0:T(8,128)(2,1)S(1)}, u32[]{:S(2)}, u32[]{:S(2)}) collective-permute-start(bf16[256,1536]{1,0:T(8,128)(2,1)S(1)} %copy-done.62), channel_id=1, source_target_pairs={{0,8},{4,12},{8,0},{12,4},{16,24},{20,28},{24,16},{28,20},{1,9},{5... | collective-permute-start | bytes 2359304 | tf_op jit(solution)/shard_map/ppermute | solution.py:1201
  582.2 19.6 %collective-permute-start.41 = (bf16[256,1536]{1,0:T(8,128)(2,1)S(1)}, bf16[256,1536]{1,0:T(8,128)(2,1)S(1)}, u32[]{:S(2)}, u32[]{:S(2)}) collective-permute-start(bf16[256,1536]{1,0:T(8,128)(2,1)S(1)} %copy-done.61), channel_id=1, source_target_pairs={{0,16},{4,20},{8,24},{12,28},{16,0},{20,4},{24,8},{28,12},{1,17},{... | collective-permute-start | bytes 2359304 | tf_op jit(solution)/shard_map/ppermute | solution.py:1201
  611.8 34.5 %collective-permute-start.45 = (bf16[2,416,896]{2,1,0:T(8,128)(2,1)}, bf16[2,416,896]{2,1,0:T(8,128)(2,1)S(1)}, u32[]{:S(2)}, u32[]{:S(2)}) collective-permute-start(bf16[2,416,896]{2,1,0:T(8,128)(2,1)} %get-tuple-element.246), channel_id=1, source_target_pairs={{0,8},{4,12},{8,0},{12,4},{16,24},{20,28},{24,16},{28,20},{1,9},{5... | collective-permute-start | bytes 4472840 | tf_op jit(solution)/shard_map/ppermute | solution.py:1201
  613.4 34.0 %collective-permute-start.46 = (bf16[2,416,896]{2,1,0:T(8,128)(2,1)}, bf16[2,416,896]{2,1,0:T(8,128)(2,1)}, u32[]{:S(2)}, u32[]{:S(2)}) collective-permute-start(bf16[2,416,896]{2,1,0:T(8,128)(2,1)} %get-tuple-element.248), channel_id=1, source_target_pairs={{0,16},{4,20},{8,24},{12,28},{16,0},{20,4},{24,8},{28,12},{1,17},{... | collective-permute-start | bytes 4472840 | tf_op jit(solution)/shard_map/ppermute | solution.py:1201
  650.6 17.9 %collective-permute-start.48 = (bf16[416,896]{1,0:T(8,128)(2,1)}, bf16[416,896]{1,0:T(8,128)(2,1)S(1)}, u32[]{:S(2)}, u32[]{:S(2)}) collective-permute-start(bf16[416,896]{1,0:T(8,128)(2,1)} %get-tuple-element.250), channel_id=1, source_target_pairs={{0,8},{4,12},{8,0},{12,4},{16,24},{20,28},{24,16},{28,20},{1,9},{5... | collective-permute-start | bytes 2236424 | tf_op jit(solution)/shard_map/ppermute | solution.py:1201
  666.5 16.9 %collective-permute-start.47 = (bf16[416,896]{1,0:T(8,128)(2,1)S(1)}, bf16[416,896]{1,0:T(8,128)(2,1)S(1)}, u32[]{:S(2)}, u32[]{:S(2)}) collective-permute-start(bf16[416,896]{1,0:T(8,128)(2,1)S(1)} %copy-done.63), channel_id=1, source_target_pairs={{0,16},{4,20},{8,24},{12,28},{16,0},{20,4},{24,8},{28,12},{1,17},{... | collective-permute-start | bytes 2236424 | tf_op jit(solution)/shard_map/ppermute | solution.py:1201
  686.1 20.2 %collective-permute-start.49 = (bf16[208,896]{1,0:T(8,128)(2,1)S(1)}, bf16[208,896]{1,0:T(8,128)(2,1)S(1)}, u32[]{:S(2)}, u32[]{:S(2)}) collective-permute-start(bf16[208,896]{1,0:T(8,128)(2,1)S(1)} %get-tuple-element.291), channel_id=1, source_target_pairs={{1,3},{0,1},{2,0},{3,2},{5,7},{4,5},{6,4},{7,6},{9,11},{8,9},{10,8... | collective-permute-start | bytes 1118216 | tf_op jit(solution)/shard_map/ppermute | solution.py:1169
  689.2 33.6 %collective-permute-start.52 = (bf16[208,896]{1,0:T(8,128)(2,1)S(1)}, bf16[208,896]{1,0:T(8,128)(2,1)S(1)}, u32[]{:S(2)}, u32[]{:S(2)}) collective-permute-start(bf16[208,896]{1,0:T(8,128)(2,1)S(1)} %get-tuple-element.290), channel_id=1, source_target_pairs={{0,3},{3,0},{4,7},{7,4},{8,11},{11,8},{12,15},{15,12},{16,19},{19,... | collective-permute-start | bytes 1118216 | tf_op jit(solution)/shard_map/ppermute | solution.py:1170
  706.5 18.2 %collective-permute-start.51 = (bf16[208,896]{1,0:T(8,128)(2,1)S(1)}, bf16[208,896]{1,0:T(8,128)(2,1)S(1)}, u32[]{:S(2)}, u32[]{:S(2)}) collective-permute-start(bf16[208,896]{1,0:T(8,128)(2,1)S(1)} %get-tuple-element.286), channel_id=1, source_target_pairs={{1,0},{2,1},{3,2},{5,4},{6,5},{7,6},{9,8},{10,9},{11,10},{13,12},{... | collective-permute-start | bytes 1118216 | tf_op jit(solution)/shard_map/ppermute | solution.py:1182
  707.8 18.4 %collective-permute-start.50 = (bf16[208,896]{1,0:T(8,128)(2,1)S(1)}, bf16[208,896]{1,0:T(8,128)(2,1)S(1)}, u32[]{:S(2)}, u32[]{:S(2)}) collective-permute-start(bf16[208,896]{1,0:T(8,128)(2,1)S(1)} %get-tuple-element.285), channel_id=1, source_target_pairs={{0,1},{1,2},{2,3},{4,5},{5,6},{6,7},{8,9},{9,10},{10,11},{12,13},{... | collective-permute-start | bytes 1118216 | tf_op jit(solution)/shard_map/ppermute | solution.py:1181
  (73 other events, 666.6 us)
Sparse Core Ops, SparseCore 0:
  210.4 126.0 all-gather.2
  383.1 122.3 reduce-scatter.2
  516.0 131.6 reduce-scatter.4

commit v12 on v11

--- a/solution.py
+++ b/solution.py
@@ -1146,6 +1146,10 @@
     return lax.ppermute(block, "cols", FAR)
 
 
+def send_over(block):
+    return lax.ppermute(block, "cols", [(0, 2), (1, 3), (2, 0), (3, 1)])
+
+
 def send_second(block, near):
     place = lax.axis_index("cols")
     above, below = near
@@ -1165,35 +1169,16 @@
     ]
 
 
-def reduce_first(second, fourth):
-    relay = lax.ppermute(second, "cols", [(1, 3), (0, 1), (2, 0), (3, 2)])
-    return relay, lax.ppermute(fourth, "cols", FAR)
-
-
-def reduce_second(third, fourth, relay):
+def reduce_slots(slots):
     place = lax.axis_index("cols")
-    relayed = relay.astype(WIDE)
-    upward_load = (
-        jnp.where(place == 0, third, fourth).astype(WIDE) + jnp.where(place == 1, relayed, 0.0)
-    ).astype(LOW)
-    downward_load = (third.astype(WIDE) + jnp.where(place == 2, relayed, 0.0)).astype(LOW)
-    return (
-        lax.ppermute(upward_load, "cols", UP),
-        lax.ppermute(downward_load, "cols", DOWN),
+    own, second, third, fourth = slots
+    arrived = (
+        lax.ppermute(jnp.where(place == 0, third, fourth), "cols", UP),
+        lax.ppermute(third, "cols", DOWN),
+        send_over(second),
+        send_far(fourth),
     )
-
-
-def reduce_last(own, first, second):
-    place = lax.axis_index("cols")
-    relay, far = first
-    below, above = second
-    end = (place == 0) | (place == 3)
-    return (
-        own.astype(WIDE)
-        + below.astype(WIDE)
-        + above.astype(WIDE)
-        + jnp.where(end, relay.astype(WIDE) + far.astype(WIDE), 0.0)
-    )
+    return own.astype(WIDE) + sum(block.astype(WIDE) for block in arrived)
 
 
 def flip(block, bit):
@@ -1293,19 +1278,20 @@
         )
         packed_near = send_near(packed)
         packed_far = send_far(packed)
-        packed_second = send_second(packed, packed_near)
+        packed_second = send_over(packed)
         first_block = after(shard_blocks[0], *packed_near)
         first_near = send_near(first_block)
         first_second = send_second(first_block, first_near)
-        grad_flips = (flip(cotangent, 2), flip(cotangent, 4))
         own = jnp.stack(slot_list(packed, packed_near, packed_second, packed_far))
-        own = after(own, info, cosine, sine, *grad_flips)
+        own = after(own, info, cosine, sine)
         beside, across = flip(own, 2), flip(own, 4)
         own_in = flip(own, 1)
         beside, across = after((beside, across), own_in, *first_near)
         corner = [flip(beside[:2], 4), flip(across[2:], 2)]
         pair_in = flip(jnp.concatenate([beside, across], axis=0), 1)
         corner_in = [flip(piece, 1) for piece in corner]
+        grad_in = after(cotangent, *corner)
+        grad_flips = (flip(grad_in, 2), flip(grad_in, 4))
         pieces = [own, own_in, beside, across, *corner, pair_in, *corner_in]
         at = depth + router_part + 1
         near_slots = [own, own_in, beside, pair_in, across, pair_in[4:], corner[0], corner_in[0]]
@@ -1357,13 +1343,13 @@
     if fast:
         first_far = send_far(after(first_block, partner, queries))
         expert_refs.append([first_block, first_second, *first_near, first_far])
-        grad_flips = after(grad_flips, own_pair)
+        grad_flips = after(grad_flips, queries)
         grad_corner = turn_corner(*grad_flips)
     heads = attention(info, queries, own_pair, partner)
     if fast:
+        heads = after(heads, grad_corner)
         grad_near = [cotangent, *grad_flips, grad_corner]
         grad_blocks = [block for one in grad_near for block in (one, flip(one, 1))]
-        heads = after(heads, grad_corner)
     else:
         grad_all = lax.all_gather(cotangent, "rows", axis=0)
         grad_blocks = [grad_all[q] for q in range(row_count)]
@@ -1388,13 +1374,12 @@
         half = TOK_DEV // 2
         picked = place_block(0, normed_two, None)
         picked = place_block(1, beside_in, picked)
-        beside, across = after((beside, across), picked)
+        beside, across = after((beside, across), picked, *grad_rows)
         corner = [flip(beside[:half], 4), flip(across[half:], 2)]
-        picked = after(picked, *grad_rows)
         picked = place_block(2, beside, picked)
         picked = place_block(4, across, picked)
         beside_in = flip(beside, 1)
-        across_in = flip(after(across, beside_in), 1)
+        across_in = flip(across, 1)
         picked = place_block(3, beside_in, picked)
         picked = place_block(5, across_in, picked)
         corner = jnp.concatenate(after(corner, picked), axis=0)
@@ -1428,15 +1413,16 @@
         slots = expert_grads(acts, token_rows[e], grad_row)
         reduced_in = (slots,)
         if e and fast:
-            back_parts = chips_second(near_x, near_y, *after(back_flips, slots))
+            out_got = flip(combine(info, chosen, out_rows, 1, 2), 1)
+            out_keep = combine(info, chosen, out_rows, 0, 2)
+            back_flips = after(back_flips, slots, out_keep)
+            back_parts = chips_second(near_x, near_y, *back_flips)
         else:
             reduced.append(lax.psum_scatter(slots, "cols", scatter_dimension=0, tiled=False))
 
     if fast:
-        out_rows = [after(a, back_parts[1], back_parts[4]) for a in out_rows]
-        out_got = flip(combine(info, chosen, out_rows, 1, 2), 1)
-        out_keep = combine(info, chosen, out_rows, 0, 2)
-        back_parts = after(back_parts, out_keep, out_got, slots)
+        out_first = chip_adds(out_keep, out_got)
+        back_parts = after(back_parts, out_first[0])
     else:
         spread_dots = spread(place_rows, gate_dots)
         grad_shares = lax.all_to_all(spread_dots, "rows", split_axis=0, concat_axis=0, tiled=True)
@@ -1460,12 +1446,7 @@
         out_refs,
     )
     if fast:
-        out_keep = after(out_keep, back_parts[2], back_parts[5], reduced[0])
-        out_first = chip_adds(out_keep, out_got)
-        slots = after(slots, reduced[0], out_first[0])
-        reduced.append(lax.psum_scatter(slots, "cols", scatter_dimension=0, tiled=False))
-        out_flips = send_chips(out_first[:2])
-        grad_heads = after(grad_heads, out_first[0])
+        out_flips = send_chips(after(out_first[:2], back_parts[2], back_parts[5]))
         router_parts = jnp.transpose(
             router_grad.astype(LOW).reshape(col_count, router_part, row_count, depth),
             (2, 0, 1, 3),
@@ -1485,6 +1466,8 @@
     arrived = lax.ppermute(source_grad.astype(LOW), "cols", [(j, i) for i, j in pairs])
     if fast:
         parts = ((0, 2, 0, query_part), (1, 3, query_part + 2 * key_part, query_part))
+        slots = after(slots, reduced[0], grad_query)
+        reduced.append(lax.psum_scatter(slots, "cols", scatter_dimension=0, tiled=False))
         out_flips = after(out_flips, grad_query)
         near_x, near_y = out_first[2:]
         for_y, for_x = corner_adds(near_x, out_flips[0], near_y, out_flips[1])
@@ -1494,7 +1477,7 @@
         keep_send = weight_grads(
             info, [normed, heads], [grad_query, grad_branch], parts, extra
         )
-        arrived = after(arrived, *keep_send)
+        arrived = after(arrived, *keep_send, mixture[2], mixture[5])
     grad_pair = join_grads(info, own_grad, source_grad, arrived, cosine, sine)
     if fast:
         keep, send = weight_grads(
@@ -1508,9 +1491,8 @@
 
     if fast:
         flat = (4, col_count * (depth + EXTRA), wide)
-        sent = after(sent, mixture[2], mixture[5])
         sent_first = chip_adds(keep.reshape(flat), sent.reshape(flat))
-        sent_chips = send_chips(sent_first[:2])
+        sent_chips = after(send_chips(sent_first[:2]), tokens_grad)
         slots = sum_parts(chips_second(*sent_first[2:], *sent_chips))
         slots = slots.reshape(col_count, depth + EXTRA, wide)
         width = query_part + 2 * key_part
@@ -1525,14 +1507,9 @@
             jnp.take(gain_sums, shards, axis=0),
             ((0, 0), (depth + router_part + 1, EXTRA - router_part - 2), (0, wide - gain_part)),
         )
-        slots = (slots + gain_sums).astype(LOW)
-
-        def cols_sum(slots):
-            sent_first = reduce_first(slots[1], slots[3])
-            sent_second = reduce_second(slots[2], slots[3], sent_first[0])
-            return reduce_last(slots[0], sent_first, sent_second)
-
-        sums = cols_sum(slots)
+        slots = after((slots + gain_sums).astype(LOW), reduced[1])
+
+        sums = reduce_slots(slots)
         router_sum = sums[depth : depth + router_part, :depth].T
         experts_gain_sum = sums[depth + router_part, :gain_part]
         attention_gain_sum = sums[depth + router_part + 1, :gain_part]

time: 755 us -> 694 us (0.919)
  waiting for transfers between devices: 264 us -> 200 us
    reduce_scatter x2, waiting for transfers between devices: 31.5 us -> 0.01 us  [on_device(): lax.psum_scatter(slots, 'cols', scatter_dimension=0, tiled=False)]
    ppermute x39, waiting for transfers between devices: 168 us -> 143 us  [flip(): return lax.ppermute(block, 'rows', [(i, i ^ bit) for i in range(count)])]
    ppermute x4, waiting for transfers between devices: 23.2 us -> 0.01 us  [send_near(): return (lax.ppermute(block, 'cols', DOWN), lax.ppermute(block, 'cols', UP))]
    ppermute x4, waiting for transfers between devices: 5.66 us -> 24.3 us  [the longest x2 24.3 us: send_over(): return lax.ppermute(block, 'cols', [(0, 2), (1, 3), (2, 0), (3, 1)])]
    ppermute x4, starting transfers between devices: 32.3 us -> 17.2 us  [the longest x2 14.4 us: send_over(): return lax.ppermute(block, 'cols', [(0, 2), (1, 3), (2, 0), (3, 1)])]
    ppermute x4, starting transfers between devices: 14.8 us -> 28.1 us  [send_near(): return (lax.ppermute(block, 'cols', DOWN), lax.ppermute(block, 'cols', UP))]
    unnamed x143 -> x141, local copies, waits for them, and re-layouts: 16.9 us -> 26.2 us
    ppermute x2 -> x1, waiting for transfers between devices: 17.4 us -> 11.3 us  [send_second(): return lax.ppermute(payload, 'cols', [(3, 1), (1, 0), (0, 2), (2, 3)])]
  transfers between devices with their start and end apart: 56 -> 56, of which waited for: 34 -> 31; matrix products, arithmetic and copies ran while one was open for 7% -> 7% of each run, Pallas kernels for 33% -> 43%
where the time goes in v12:
time: 694 us; the launch traced here: 683 us
  Pallas kernels  296 us (43%)
  waiting for transfers between devices  200 us (29%)
  starting transfers between devices  90.1 us (13%)
  local copies, waits for them, and re-layouts  49.7 us (7%)
  other arithmetic  31.9 us (5%)
  between operations  14.8 us (2%)
    ppermute x39, waiting for transfers between devices, flip(): return lax.ppermute(block, 'rows', [(i, i ^ bit) for i in range(count)])  143 us
    pallas_call x2, Pallas kernels, expert(): pl.pallas_call(functools.partial(expert_kernel, slots), grid=(height // E...  60.9 us
    pallas_call x4, Pallas kernels, combine(): pl.pallas_call(functools.partial(combine_kernel, local, first, step), out...  31.2 us
    pallas_call x2, Pallas kernels, expert_grads(): pl.pallas_call(expert_grads_kernel, grid=(D // 256,), out_shape=jax.Shape...  29.3 us
    pallas_call x8, Pallas kernels, dispatch(): pl.pallas_call(functools.partial(dispatch_kernel, local), grid=(D // wide...  28.6 us
    ppermute x4, starting transfers between devices, send_near(): return (lax.ppermute(block, 'cols', DOWN), lax.ppermute(block, 'cols', UP))  28.1 us
    ppermute x39, starting transfers between devices, flip(): return lax.ppermute(block, 'rows', [(i, i ^ bit) for i in range(count)])  27.9 us
    unnamed x141, local copies, waits for them, and re-layouts  26.2 us
  transfers between devices with their start and end apart: 56, of which 31 were waited for; matrix products, arithmetic and copies ran while one was open for 7% of the time, Pallas kernels for 43%

profile of v12, /device:TPU:0, one launch (start us, length us, event | category | flops | bytes accessed | tf_op | source)
XLA Modules:
  0.0 683.2 jit_solution(2044147850649954590)
XLA Ops:
  14.1 6.3 collective-permute-start.1
  20.4 3.7 collective-permute-start.6
  32.6 19.1 %collective-permute-start.3 = (bf16[576,1536]{1,0:T(8,128)(2,1)S(1)}, bf16[576,1536]{1,0:T(8,128)(2,1)}, u32[]{:S(2)}, u32[]{:S(2)}) collective-permute-start(bf16[576,1536]{1,0:T(8,128)(2,1)S(1)} %pad_maximum_fusion.3.rest_0_), channel_id=1, source_target_pairs={{0,1},{1,2},{2,3},{4,5},{5,6},{6,7},{8,9},{9,10},{10,11},{12,13},{... | collective-permute-start | bytes 5308424 | tf_op jit(solution)/shard_map/ppermute | solution.py:1142
  57.4 31.8 %collective-permute-done.8.rest_2_.rest_8_.rest_11_ = bf16[4,208,896]{2,1,0:T(8,128)(2,1)S(1)} collective-permute-done((bf16[4,208,896]{2,1,0:T(8,128)(2,1)S(1)}, bf16[4,208,896]{2,1,0:T(8,128)(2,1)S(1)}, u32[]{:S(2)}, u32[]{:S(2)}) %collective-permute-start.8) | collective-permute-done | bytes 1490976 | tf_op jit(solution)/shard_map/ppermute | solution.py:1186
  105.8 8.4 %collective-permute-done.11.rest_4_.rest_10_.rest_13_ = bf16[2,208,896]{2,1,0:T(8,128)(2,1)S(1)} collective-permute-done((bf16[2,208,896]{2,1,0:T(8,128)(2,1)S(1)}, bf16[2,208,896]{2,1,0:T(8,128)(2,1)S(1)}, u32[]{:S(2)}, u32[]{:S(2)}) %collective-permute-start.11) | collective-permute-done | bytes 745504 | tf_op jit(solution)/shard_map/ppermute | solution.py:1186
  119.7 5.6 route_tables.1
  130.7 11.3 %collective-permute-done.4.rest_1_ = bf16[576,1536]{1,0:T(8,128)(2,1)} collective-permute-done((bf16[576,1536]{1,0:T(8,128)(2,1)}, bf16[576,1536]{1,0:T(8,128)(2,1)}, u32[]{:S(2)}, u32[]{:S(2)}) %collective-permute-start.4) | collective-permute-done | bytes 1769504 | tf_op jit(solution)/shard_map/ppermute | solution.py:1157
  142.0 5.0 norm_key_value.1
  148.3 8.3 %query_projection.1.queries = bf16[512,1536]{1,0:T(8,128)(2,1)} custom-call(s32[16]{0:T(128)} %concatenate.42.info, bf16[512,1536]{1,0:T(8,128)(2,1)} %get-tuple-element.134.normed.rest_0_, f32[512,128]{1,0:T(8,128)} %get-tuple-element.306.cosine, f32[512,128]{1,0:T(8,128)} %get-tuple-element.307.sine, bf16[4,208,896]{2,1,0:T(8,128)(2,1)} %copy-done.1, ...), custom_call_target="tpu_custom_call" | custom-call | flops 1 | bytes 1 | tf_op jit(solution)/shard_map/query_projection/pallas_call | solution.py:195
  156.6 6.3 collective-permute-done.15.partner
  174.3 11.0 %tree_attention.1.heads.rest_1_ = bf16[512,1536]{1,0:T(8,128)(2,1)} custom-call(s32[16]{0:T(128)} %concatenate.42.info, bf16[512,1536]{1,0:T(8,128)(2,1)} %query_projection.1.queries, bf16[512,512]{1,0:T(8,128)(2,1)} %get-tuple-element.135.own, bf16[512,512]{1,0:T(8,128)(2,1)} %copy-done.40), custom_call_target="tpu_custom_call" | custom-call | flops 1 | bytes 1 | tf_op jit(solution)/shard_map/tree_attention/pallas_call | solution.py:277
  189.2 9.8 %out_projection.1 = (f32[512,1536]{1,0:T(8,128)}, bf16[512,1536]{1,0:T(8,128)(2,1)}) custom-call(s32[16]{0:T(128)} %concatenate.42.info, bf16[512,1536]{1,0:T(8,128)(2,1)} %tree_attention.1.heads.rest_1_, bf16[512,1536]{1,0:T(8,128)(2,1)} %tokens.4, f32[1,1536]{1,0:T(1,128)} %reshape.305.gain, bf16[4,208,896]{2,1,0:T(8,128)(2,1)} %copy-done.1, ...), custom_call_target="tpu_custom_call" | custom-call | flops 1 | bytes 1 | tf_op jit(solution)/shard_map/out_projection/pallas_call | solution.py:389
  199.1 7.0 %collective-permute-done.32.rest_4_ = bf16[576,1536]{1,0:T(8,128)(2,1)} collective-permute-done((bf16[576,1536]{1,0:T(8,128)(2,1)S(1)}, bf16[576,1536]{1,0:T(8,128)(2,1)}, u32[]{:S(2)}, u32[]{:S(2)}) %collective-permute-start.32) | collective-permute-done | bytes 1769504 | tf_op jit(solution)/shard_map/ppermute | solution.py:1146
  211.3 5.4 collective-permute-done.24.rest_3_
  221.6 3.6 dispatch.8
  225.3 9.3 %pick_rows.1 = (bf16[8,160,1536]{2,1,0:T(8,128)(2,1)}, bf16[8,160,1536]{2,1,0:T(8,128)(2,1)}) custom-call(bf16[8,320,512]{2,1,0:T(8,128)(2,1)} %get-tuple-element.132.chosen, bf16[512,1536]{1,0:T(8,128)(2,1)} %cotangent.1, bf16[512,1536]{1,0:T(8,128)(2,1)} %copy-done.41, bf16[512,1536]{1,0:T(8,128)(2,1)} %collective-permute-done.16.rest_2_, ...), custom_call_target="tpu_custom_call" | custom-call | flops 1 | bytes 1 | tf_op jit(solution)/shard_map/pick_rows/pallas_call | solution.py:480
  234.6 3.6 dispatch.9
  238.1 8.4 %collective-permute-done.20.rows = bf16[512,1536]{1,0:T(8,128)(2,1)} collective-permute-done((bf16[512,1536]{1,0:T(8,128)(2,1)S(1)}, bf16[512,1536]{1,0:T(8,128)(2,1)}, u32[]{:S(2)}, u32[]{:S(2)}) %collective-permute-start.20) | collective-permute-done | bytes 1572896 | tf_op jit(solution)/shard_map/ppermute | solution.py:1186
  246.5 7.8 %collective-permute-done.21.rows = bf16[512,1536]{1,0:T(8,128)(2,1)S(1)} collective-permute-done((bf16[512,1536]{1,0:T(8,128)(2,1)S(1)}, bf16[512,1536]{1,0:T(8,128)(2,1)S(1)}, u32[]{:S(2)}, u32[]{:S(2)}) %collective-permute-start.21) | collective-permute-done | bytes 1572896 | tf_op jit(solution)/shard_map/ppermute | solution.py:1186
  258.0 3.6 dispatch.10
  266.3 3.6 dispatch.12
  271.0 3.6 dispatch.13
  277.1 3.6 dispatch.14
  285.4 30.7 %expert.2 = (bf16[1280,1536]{1,0:T(8,128)(2,1)}, bf16[1280,1536]{1,0:T(8,128)(2,1)}, bf16[1280,1536]{1,0:T(8,128)(2,1)}, bf16[4,576,1280]{2,1,0:T(8,128)(2,1)}, f32[1280,1]{1,0:T(8,128)}) custom-call(s32[16]{0:T(128)} %concatenate.42.info, bf16[1280,1536]{1,0:T(8,128)(2,1)} %bitcast.149, bf16[1280,1536]{1,0:T(8,128)(2,1)} %bitcast.167, f32[1280,1]{1,0:T(8,128)} %bitcast.153, ...), custom_call_target="tpu_custom_call" | custom-call | flops 1 | bytes 1 | tf_op jit(solution)/shard_map/expert/pallas_call | solution.py:670
  316.1 14.6 %expert_gradients.2 = bf16[4,576,1536]{2,1,0:T(8,128)(2,1)} custom-call(bf16[4,576,1280]{2,1,0:T(8,128)(2,1)} %get-tuple-element.181.acts, bf16[1280,1536]{1,0:T(8,128)(2,1)} %bitcast.150, bf16[1280,1536]{1,0:T(8,128)(2,1)} %get-tuple-element.182.grads), custom_call_target="tpu_custom_call" | custom-call | flops 1 | bytes 1 | tf_op jit(solution)/shard_map/expert_gradients/pallas_call | solution.py:699
  331.7 30.2 %expert.3 = (bf16[1280,1536]{1,0:T(8,128)(2,1)}, bf16[1280,1536]{1,0:T(8,128)(2,1)}, bf16[1280,1536]{1,0:T(8,128)(2,1)}, bf16[4,576,1280]{2,1,0:T(8,128)(2,1)}, f32[1280,1]{1,0:T(8,128)}) custom-call(s32[16]{0:T(128)} %concatenate.42.info, bf16[1280,1536]{1,0:T(8,128)(2,1)} %bitcast.151, bf16[1280,1536]{1,0:T(8,128)(2,1)} %bitcast.168, f32[1280,1]{1,0:T(8,128)} %bitcast.154, ...), custom_call_target="tpu_custom_call" | custom-call | flops 1 | bytes 1 | tf_op jit(solution)/shard_map/expert/pallas_call | solution.py:670
  362.0 8.0 %combine.7 = bf16[4,544,1536]{2,1,0:T(8,128)(2,1)} custom-call(s32[16]{0:T(128)} %concatenate.42.info, bf16[8,320,512]{2,1,0:T(8,128)(2,1)} %get-tuple-element.132.chosen, bf16[8,160,1536]{2,1,0:T(8,128)(2,1)} %bitcast.160, bf16[8,160,1536]{2,1,0:T(8,128)(2,1)} %bitcast.164, f32[8,160,1]{2,1,0:T(8,128)} %bitcast.169, f32[8,160,1]{2,1,0:T(8,128)} %bitcast.171), custom_call_target="tpu_custom_call" | custom-call | flops 1 | bytes 1 | tf_op jit(solution)/shard_map/combine/pallas_call | solution.py:762
  370.1 7.3 %combine.5 = bf16[4,512,1536]{2,1,0:T(8,128)(2,1)} custom-call(s32[16]{0:T(128)} %concatenate.42.info, bf16[8,320,512]{2,1,0:T(8,128)(2,1)} %get-tuple-element.132.chosen, bf16[8,160,1536]{2,1,0:T(8,128)(2,1)} %bitcast.158, bf16[8,160,1536]{2,1,0:T(8,128)(2,1)} %bitcast.162), custom_call_target="tpu_custom_call" | custom-call | flops 1 | bytes 1 | tf_op jit(solution)/shard_map/combine/pallas_call | solution.py:762
  378.0 8.1 %combine.6.keep = bf16[4,544,1536]{2,1,0:T(8,128)(2,1)} custom-call(s32[16]{0:T(128)} %concatenate.42.info, bf16[8,320,512]{2,1,0:T(8,128)(2,1)} %get-tuple-element.132.chosen, bf16[8,160,1536]{2,1,0:T(8,128)(2,1)} %bitcast.161, bf16[8,160,1536]{2,1,0:T(8,128)(2,1)} %bitcast.165, f32[8,160,1]{2,1,0:T(8,128)} %bitcast.170, f32[8,160,1]{2,1,0:T(8,128)} %bitcast.172), custom_call_target="tpu_custom_call" | custom-call | flops 1 | bytes 1 | tf_op jit(solution)/shard_map/combine/pallas_call | solution.py:762
  388.9 7.8 %chip_sums.4 = (bf16[2,272,1536]{2,1,0:T(8,128)(2,1)}, bf16[2,272,1536]{2,1,0:T(8,128)(2,1)}, bf16[2,272,1536]{2,1,0:T(8,128)(2,1)}, bf16[2,272,1536]{2,1,0:T(8,128)(2,1)}) custom-call(bf16[4,544,1536]{2,1,0:T(8,128)(2,1)} %combine.6.keep, bf16[4,544,1536]{2,1,0:T(8,128)(2,1)} %copy-done.15), custom_call_target="tpu_custom_call" | custom-call | flops 1 | bytes 1 | tf_op jit(solution)/shard_map/chip_sums/pallas_call | solution.py:811
  399.6 7.7 %combine.4.keep = bf16[4,512,1536]{2,1,0:T(8,128)(2,1)} custom-call(s32[16]{0:T(128)} %concatenate.42.info, bf16[8,320,512]{2,1,0:T(8,128)(2,1)} %get-tuple-element.132.chosen, bf16[8,160,1536]{2,1,0:T(8,128)(2,1)} %bitcast.159, bf16[8,160,1536]{2,1,0:T(8,128)(2,1)} %bitcast.163), custom_call_target="tpu_custom_call" | custom-call | flops 1 | bytes 1 | tf_op jit(solution)/shard_map/combine/pallas_call | solution.py:762
  407.4 14.7 %expert_gradients.3 = bf16[4,576,1536]{2,1,0:T(8,128)(2,1)} custom-call(bf16[4,576,1280]{2,1,0:T(8,128)(2,1)} %get-tuple-element.198.acts, bf16[1280,1536]{1,0:T(8,128)(2,1)} %bitcast.152, bf16[1280,1536]{1,0:T(8,128)(2,1)} %get-tuple-element.199.grads), custom_call_target="tpu_custom_call" | custom-call | flops 1 | bytes 1 | tf_op jit(solution)/shard_map/expert_gradients/pallas_call | solution.py:699
  422.0 13.3 %collective-permute-done.35.got_x.rest_1_ = bf16[2,272,1536]{2,1,0:T(8,128)(2,1)S(1)} collective-permute-done((bf16[2,272,1536]{2,1,0:T(8,128)(2,1)}, bf16[2,272,1536]{2,1,0:T(8,128)(2,1)S(1)}, u32[]{:S(2)}, u32[]{:S(2)}) %collective-permute-start.35) | collective-permute-done | bytes 1671200 | tf_op jit(solution)/shard_map/ppermute | solution.py:1186
  443.3 7.4 %chip_sums.3 = (bf16[2,256,1536]{2,1,0:T(8,128)(2,1)}, bf16[2,256,1536]{2,1,0:T(8,128)(2,1)}, bf16[2,256,1536]{2,1,0:T(8,128)(2,1)}, bf16[2,256,1536]{2,1,0:T(8,128)(2,1)}) custom-call(bf16[4,512,1536]{2,1,0:T(8,128)(2,1)} %combine.4.keep, bf16[4,512,1536]{2,1,0:T(8,128)(2,1)} %collective-permute-done.33.got), custom_call_target="tpu_custom_call" | custom-call | flops 1 | bytes 1 | tf_op jit(solution)/shard_map/chip_sums/pallas_call | solution.py:811
  450.7 10.0 %collective-permute-done.37.rest_2_ = bf16[272,1536]{1,0:T(8,128)(2,1)S(1)} collective-permute-done((bf16[272,1536]{1,0:T(8,128)(2,1)}, bf16[272,1536]{1,0:T(8,128)(2,1)S(1)}, u32[]{:S(2)}, u32[]{:S(2)}) %collective-permute-start.37) | collective-permute-done | bytes 835616 | tf_op jit(solution)/shard_map/ppermute | solution.py:1186
  463.6 12.0 %experts_norm_back.1 = (f32[512,1536]{1,0:T(8,128)}, bf16[512,1536]{1,0:T(8,128)(2,1)}, bf16[512,1536]{1,0:T(8,128)(2,1)}, f32[1,1536]{1,0:T(1,128)}, f32[16,1536]{1,0:T(8,128)}) custom-call(s32[16]{0:T(128)} %concatenate.42.info, f32[512,1536]{1,0:T(8,128)} %get-tuple-element.140.residual, bf16[512,1536]{1,0:T(8,128)(2,1)} %get-tuple-element.141.rows.normed, ...), custom_call_target="tpu_custom_call" | custom-call | flops 1 | bytes 1 | tf_op jit(solution)/shard_map/experts_norm_back/pallas_call | solution.py:922
  475.6 15.4 %tree_attention_back.1 = (bf16[512,1536]{1,0:T(8,128)(2,1)}, f32[512,512]{1,0:T(8,128)}, f32[512,512]{1,0:T(8,128)}) custom-call(s32[16]{0:T(128)} %concatenate.42.info, bf16[512,1536]{1,0:T(8,128)(2,1)} %query_projection.1.queries, bf16[512,512]{1,0:T(8,128)(2,1)} %get-tuple-element.135.own, bf16[512,512]{1,0:T(8,128)(2,1)} %copy-done.40, ...), custom_call_target="tpu_custom_call" | custom-call | flops 1 | bytes 1 | tf_op jit(solution)/shard_map/tree_attention_back/pallas_call | solution.py:338
  491.1 5.3 collective-permute-done.39.got_x
  506.0 13.6 %weight_gradients.2 = (bf16[4,4,208,896]{3,2,1,0:T(8,128)(2,1)}, bf16[4,4,208,896]{3,2,1,0:T(8,128)(2,1)}) custom-call(s32[16]{0:T(128)} %concatenate.42.info, bf16[512,1536]{1,0:T(8,128)(2,1)} %get-tuple-element.134.normed.rest_0_, bf16[512,1536]{1,0:T(8,128)(2,1)} %tree_attention.1.heads.rest_1_, bf16[512,1536]{1,0:T(8,128)(2,1)} %get-tuple-element.214.rest_2_.grad_query, ...), custom_call_target="tpu_custom_call" | custom-call | flops 1 | bytes 1 | tf_op jit(solution)/shard_map/weight_gradients/pallas_call | solution.py:1087
  519.7 7.2 %collective-permute-done.43.arrived = bf16[512,512]{1,0:T(8,128)(2,1)S(1)} collective-permute-done((bf16[512,512]{1,0:T(8,128)(2,1)S(1)}, bf16[512,512]{1,0:T(8,128)(2,1)S(1)}, u32[]{:S(2)}, u32[]{:S(2)}) %collective-permute-start.43) | collective-permute-done | bytes 524320 | tf_op jit(solution)/shard_map/ppermute | solution.py:1466
  530.7 5.7 weight_gradients.3
  536.5 10.0 %collective-permute-done.44 = bf16[4,4,208,896]{3,2,1,0:T(8,128)(2,1)} collective-permute-done((bf16[4,4,208,896]{3,2,1,0:T(8,128)(2,1)}, bf16[4,4,208,896]{3,2,1,0:T(8,128)(2,1)}, u32[]{:S(2)}, u32[]{:S(2)}) %collective-permute-start.44) | collective-permute-done | bytes 5963808 | tf_op jit(solution)/shard_map/ppermute | solution.py:1186
  546.4 7.2 %chip_sums.5 = (bf16[2,416,896]{2,1,0:T(8,128)(2,1)}, bf16[2,416,896]{2,1,0:T(8,128)(2,1)}, bf16[2,416,896]{2,1,0:T(8,128)(2,1)}, bf16[2,416,896]{2,1,0:T(8,128)(2,1)}) custom-call(bf16[4,832,896]{2,1,0:T(8,128)(2,1)} %bitcast.155, bf16[4,832,896]{2,1,0:T(8,128)(2,1)} %bitcast.41.got), custom_call_target="tpu_custom_call" | custom-call | flops 1 | bytes 1 | tf_op jit(solution)/shard_map/chip_sums/pallas_call | solution.py:811
  562.2 12.5 %token_gradient.1 = (bf16[512,1536]{1,0:T(8,128)(2,1)}, f32[1,1536]{1,0:T(1,128)}) custom-call(s32[16]{0:T(128)} %concatenate.42.info, bf16[512,1536]{1,0:T(8,128)(2,1)} %get-tuple-element.214.rest_2_.grad_query, bf16[512,512]{1,0:T(8,128)(2,1)} %join_key_value_gradients.1.rest_1_.grad_pair, bf16[512,1536]{1,0:T(8,128)(2,1)} %tokens.4, ...), custom_call_target="tpu_custom_call" | custom-call | flops 1 | bytes 1 | tf_op jit(solution)/shard_map/token_gradient/pallas_call | solution.py:1013
  574.7 13.9 %collective-permute-done.45.got_x = bf16[2,416,896]{2,1,0:T(8,128)(2,1)S(1)} collective-permute-done((bf16[2,416,896]{2,1,0:T(8,128)(2,1)}, bf16[2,416,896]{2,1,0:T(8,128)(2,1)S(1)}, u32[]{:S(2)}, u32[]{:S(2)}) %collective-permute-start.45) | collective-permute-done | bytes 1490976 | tf_op jit(solution)/shard_map/ppermute | solution.py:1186
  600.3 11.9 %collective-permute-done.47 = bf16[416,896]{1,0:T(8,128)(2,1)S(1)} collective-permute-done((bf16[416,896]{1,0:T(8,128)(2,1)}, bf16[416,896]{1,0:T(8,128)(2,1)S(1)}, u32[]{:S(2)}, u32[]{:S(2)}) %collective-permute-start.47) | collective-permute-done | bytes 745504 | tf_op jit(solution)/shard_map/ppermute | solution.py:1186
  620.2 13.7 %collective-permute-start.51 = (bf16[208,896]{1,0:T(8,128)(2,1)S(1)}, bf16[208,896]{1,0:T(8,128)(2,1)S(1)}, u32[]{:S(2)}, u32[]{:S(2)}) collective-permute-start(bf16[208,896]{1,0:T(8,128)(2,1)S(1)} %get-tuple-element.281), channel_id=1, source_target_pairs={{0,2},{1,3},{2,0},{3,1},{4,6},{5,7},{6,4},{7,5},{8,10},{9,11},{10,... | collective-permute-start | bytes 1118216 | tf_op jit(solution)/shard_map/ppermute | solution.py:1150
  640.3 24.3 %collective-permute-done.51 = bf16[208,896]{1,0:T(8,128)(2,1)S(1)} collective-permute-done((bf16[208,896]{1,0:T(8,128)(2,1)S(1)}, bf16[208,896]{1,0:T(8,128)(2,1)S(1)}, u32[]{:S(2)}, u32[]{:S(2)}) %collective-permute-start.51) | collective-permute-done | bytes 372768 | tf_op jit(solution)/shard_map/ppermute | solution.py:1150
  (328 shorter events, 170.0 us)
Async XLA Ops:
  7.2 324.6 %all-gather.3.cloned.1.call-start = ((), (), s32[]{:S(2)}) async-start(), calls=%async_computation.4 | async-start | bytes 8847360 | tf_op jit(solution)/shard_map/all_gather | solution.py:1362
  12.7 18.6 %collective-permute-start = (bf16[208,896]{1,0:T(8,128)(2,1)S(1)}, bf16[208,896]{1,0:T(8,128)(2,1)}, u32[]{:S(2)}, u32[]{:S(2)}) collective-permute-start(bf16[208,896]{1,0:T(8,128)(2,1)S(1)} %concatenate.46), channel_id=1, source_target_pairs={{1,0},{2,1},{3,2},{5,4},{6,5},{7,6},{9,8},{10,9},{11,10},{13,12},{... | collective-permute-start | bytes 1118216 | tf_op jit(solution)/shard_map/ppermute | solution.py:1142
  14.1 17.2 %collective-permute-start.1 = (bf16[208,896]{1,0:T(8,128)(2,1)S(1)}, bf16[208,896]{1,0:T(8,128)(2,1)}, u32[]{:S(2)}, u32[]{:S(2)}) collective-permute-start(bf16[208,896]{1,0:T(8,128)(2,1)S(1)} %concatenate.46), channel_id=1, source_target_pairs={{0,1},{1,2},{2,3},{4,5},{5,6},{6,7},{8,9},{9,10},{10,11},{12,13},{... | collective-permute-start | bytes 1118216 | tf_op jit(solution)/shard_map/ppermute | solution.py:1142
  20.4 31.3 %collective-permute-start.6 = (bf16[208,896]{1,0:T(8,128)(2,1)S(1)}, bf16[208,896]{1,0:T(8,128)(2,1)}, u32[]{:S(2)}, u32[]{:S(2)}) collective-permute-start(bf16[208,896]{1,0:T(8,128)(2,1)S(1)} %concatenate.46), channel_id=1, source_target_pairs={{0,3},{3,0},{4,7},{7,4},{8,11},{11,8},{12,15},{15,12},{16,19},{19,... | collective-permute-start | bytes 1118216 | tf_op jit(solution)/shard_map/ppermute | solution.py:1146
  24.1 28.7 %collective-permute-start.5 = (bf16[208,896]{1,0:T(8,128)(2,1)S(1)}, bf16[208,896]{1,0:T(8,128)(2,1)}, u32[]{:S(2)}, u32[]{:S(2)}) collective-permute-start(bf16[208,896]{1,0:T(8,128)(2,1)S(1)} %concatenate.46), channel_id=1, source_target_pairs={{0,2},{1,3},{2,0},{3,1},{4,6},{5,7},{6,4},{7,5},{8,10},{9,11},{10,... | collective-permute-start | bytes 1118216 | tf_op jit(solution)/shard_map/ppermute | solution.py:1150
  31.3 58.8 %collective-permute-start.2 = (bf16[576,1536]{1,0:T(8,128)(2,1)S(1)}, bf16[576,1536]{1,0:T(8,128)(2,1)S(1)}, u32[]{:S(2)}, u32[]{:S(2)}) collective-permute-start(bf16[576,1536]{1,0:T(8,128)(2,1)S(1)} %pad_maximum_fusion.3.rest_0_), channel_id=1, source_target_pairs={{1,0},{2,1},{3,2},{5,4},{6,5},{7,6},{9,8},{10,9},{11,10},{13,12},{... | collective-permute-start | bytes 5308424 | tf_op jit(solution)/shard_map/ppermute | solution.py:1142
  32.6 58.8 %collective-permute-start.3 = (bf16[576,1536]{1,0:T(8,128)(2,1)S(1)}, bf16[576,1536]{1,0:T(8,128)(2,1)}, u32[]{:S(2)}, u32[]{:S(2)}) collective-permute-start(bf16[576,1536]{1,0:T(8,128)(2,1)S(1)} %pad_maximum_fusion.3.rest_0_), channel_id=1, source_target_pairs={{0,1},{1,2},{2,3},{4,5},{5,6},{6,7},{8,9},{9,10},{10,11},{12,13},{... | collective-permute-start | bytes 5308424 | tf_op jit(solution)/shard_map/ppermute | solution.py:1142
  54.2 35.1 %collective-permute-start.8 = (bf16[4,208,896]{2,1,0:T(8,128)(2,1)S(1)}, bf16[4,208,896]{2,1,0:T(8,128)(2,1)S(1)}, u32[]{:S(2)}, u32[]{:S(2)}) collective-permute-start(bf16[4,208,896]{2,1,0:T(8,128)(2,1)S(1)} %pad_maximum_fusion.5.rest_0_.rest_6_.rest_9_), channel_id=1, source_target_pairs={{0,8},{4,12},{8,0},{12,4},{16,24},{20,28},{24,16},{28,20},{1,9},{5... | collective-permute-start | bytes 4472840 | tf_op jit(solution)/shard_map/ppermute | solution.py:1186
  55.4 34.7 %collective-permute-start.9 = (bf16[4,208,896]{2,1,0:T(8,128)(2,1)S(1)}, bf16[4,208,896]{2,1,0:T(8,128)(2,1)S(1)}, u32[]{:S(2)}, u32[]{:S(2)}) collective-permute-start(bf16[4,208,896]{2,1,0:T(8,128)(2,1)S(1)} %pad_maximum_fusion.5.rest_0_.rest_6_.rest_9_), channel_id=1, source_target_pairs={{0,16},{4,20},{8,24},{12,28},{16,0},{20,4},{24,8},{28,12},{1,17},{... | collective-permute-start | bytes 4472840 | tf_op jit(solution)/shard_map/ppermute | solution.py:1186
  93.3 23.4 %collective-permute-start.10 = (bf16[8,208,896]{2,1,0:T(8,128)(2,1)}, bf16[8,208,896]{2,1,0:T(8,128)(2,1)S(1)}, u32[]{:S(2)}, u32[]{:S(2)}) collective-permute-start(bf16[8,208,896]{2,1,0:T(8,128)(2,1)} %pad_maximum_fusion), channel_id=1, source_target_pairs={{0,4},{4,0},{8,12},{12,8},{16,20},{20,16},{24,28},{28,24},{1,5},{5... | collective-permute-start | bytes 8945672 | tf_op jit(solution)/shard_map/ppermute | solution.py:1186
  95.0 19.1 %collective-permute-start.11 = (bf16[2,208,896]{2,1,0:T(8,128)(2,1)S(1)}, bf16[2,208,896]{2,1,0:T(8,128)(2,1)S(1)}, u32[]{:S(2)}, u32[]{:S(2)}) collective-permute-start(bf16[2,208,896]{2,1,0:T(8,128)(2,1)S(1)} %slice.184), channel_id=1, source_target_pairs={{0,16},{4,20},{8,24},{12,28},{16,0},{20,4},{24,8},{28,12},{1,17},{... | collective-permute-start | bytes 2236424 | tf_op jit(solution)/shard_map/ppermute | solution.py:1186
  96.6 18.8 %collective-permute-start.13 = (bf16[2,208,896]{2,1,0:T(8,128)(2,1)S(1)}, bf16[2,208,896]{2,1,0:T(8,128)(2,1)S(1)}, u32[]{:S(2)}, u32[]{:S(2)}) collective-permute-start(bf16[2,208,896]{2,1,0:T(8,128)(2,1)S(1)} %slice.187), channel_id=1, source_target_pairs={{0,8},{4,12},{8,0},{12,4},{16,24},{20,28},{24,16},{28,20},{1,9},{5... | collective-permute-start | bytes 2236424 | tf_op jit(solution)/shard_map/ppermute | solution.py:1186
  100.2 41.8 %collective-permute-start.4 = (bf16[576,1536]{1,0:T(8,128)(2,1)}, bf16[576,1536]{1,0:T(8,128)(2,1)}, u32[]{:S(2)}, u32[]{:S(2)}) collective-permute-start(bf16[576,1536]{1,0:T(8,128)(2,1)} %select_select_fusion), channel_id=1, source_target_pairs={{3,1},{1,0},{0,2},{2,3},{7,5},{5,4},{4,6},{6,7},{11,9},{9,8},{8,10... | collective-permute-start | bytes 5308424 | tf_op jit(solution)/shard_map/ppermute | solution.py:1157
  115.4 50.9 %collective-permute-start.16 = (bf16[512,1536]{1,0:T(8,128)(2,1)}, bf16[512,1536]{1,0:T(8,128)(2,1)}, u32[]{:S(2)}, u32[]{:S(2)}) collective-permute-start(bf16[512,1536]{1,0:T(8,128)(2,1)} %cotangent.1), channel_id=1, source_target_pairs={{0,8},{4,12},{8,0},{12,4},{16,24},{20,28},{24,16},{28,20},{1,9},{5... | collective-permute-start | bytes 4718600 | tf_op jit(solution)/shard_map/ppermute | solution.py:1186
  116.1 50.2 %collective-permute-start.17 = (bf16[512,1536]{1,0:T(8,128)(2,1)}, bf16[512,1536]{1,0:T(8,128)(2,1)}, u32[]{:S(2)}, u32[]{:S(2)}) collective-permute-start(bf16[512,1536]{1,0:T(8,128)(2,1)} %cotangent.1), channel_id=1, source_target_pairs={{0,16},{4,20},{8,24},{12,28},{16,0},{20,4},{24,8},{28,12},{1,17},{... | collective-permute-start | bytes 4718600 | tf_op jit(solution)/shard_map/ppermute | solution.py:1186
  147.0 15.9 %collective-permute-start.15 = (bf16[512,512]{1,0:T(8,128)(2,1)}, bf16[512,512]{1,0:T(8,128)(2,1)S(1)}, u32[]{:S(2)}, u32[]{:S(2)}) collective-permute-start(bf16[512,512]{1,0:T(8,128)(2,1)} %get-tuple-element.135.own), channel_id=1, source_target_pairs={{1,0},{3,2},{5,4},{7,6},{9,8},{11,10},{13,12},{15,14},{17,16},{19,... | collective-permute-start | bytes 1572872 | tf_op jit(solution)/shard_map/ppermute | solution.py:1341
  162.9 43.1 %collective-permute-start.32 = (bf16[576,1536]{1,0:T(8,128)(2,1)S(1)}, bf16[576,1536]{1,0:T(8,128)(2,1)}, u32[]{:S(2)}, u32[]{:S(2)}) collective-permute-start(bf16[576,1536]{1,0:T(8,128)(2,1)S(1)} %copy-done.12), channel_id=1, source_target_pairs={{0,3},{3,0},{4,7},{7,4},{8,11},{11,8},{12,15},{15,12},{16,19},{19,... | collective-permute-start | bytes 5308424 | tf_op jit(solution)/shard_map/ppermute | solution.py:1146
  168.4 17.6 %collective-permute-start.18 = (bf16[256,1536]{1,0:T(8,128)(2,1)}, bf16[256,1536]{1,0:T(8,128)(2,1)}, u32[]{:S(2)}, u32[]{:S(2)}) collective-permute-start(bf16[256,1536]{1,0:T(8,128)(2,1)} %slice.189), channel_id=1, source_target_pairs={{0,16},{4,20},{8,24},{12,28},{16,0},{20,4},{24,8},{28,12},{1,17},{... | collective-permute-start | bytes 2359304 | tf_op jit(solution)/shard_map/ppermute | solution.py:1186
  171.0 17.3 %collective-permute-start.19 = (bf16[256,1536]{1,0:T(8,128)(2,1)}, bf16[256,1536]{1,0:T(8,128)(2,1)S(1)}, u32[]{:S(2)}, u32[]{:S(2)}) collective-permute-start(bf16[256,1536]{1,0:T(8,128)(2,1)} %slice.190), channel_id=1, source_target_pairs={{0,8},{4,12},{8,0},{12,4},{16,24},{20,28},{24,16},{28,20},{1,9},{5... | collective-permute-start | bytes 2359304 | tf_op jit(solution)/shard_map/ppermute | solution.py:1186
  206.0 352.3 %reduce-scatter.3.cloned.1.call-start = ((), (), s32[]{:S(2)}) async-start(), calls=%async_computation.2 | async-start | bytes 8847360 | tf_op jit(solution)/shard_map/reduce_scatter | solution.py:1421
  206.9 18.4 %collective-permute-start.25 = (bf16[512,1536]{1,0:T(8,128)(2,1)}, bf16[512,1536]{1,0:T(8,128)(2,1)}, u32[]{:S(2)}, u32[]{:S(2)}) collective-permute-start(bf16[512,1536]{1,0:T(8,128)(2,1)} %collective-permute-done.17.rest_4_), channel_id=1, source_target_pairs={{0,4},{4,0},{8,12},{12,8},{16,20},{20,16},{24,28},{28,24},{1,5},{5... | collective-permute-start | bytes 4718600 | tf_op jit(solution)/shard_map/ppermute | solution.py:1186
  207.0 18.3 %collective-permute-start.26 = (bf16[512,1536]{1,0:T(8,128)(2,1)}, bf16[512,1536]{1,0:T(8,128)(2,1)}, u32[]{:S(2)}, u32[]{:S(2)}) collective-permute-start(bf16[512,1536]{1,0:T(8,128)(2,1)} %constant_dynamic-update-slice_fusion.8.rest_6_), channel_id=1, source_target_pairs={{0,4},{4,0},{8,12},{12,8},{16,20},{20,16},{24,28},{28,24},{1,5},{5... | collective-permute-start | bytes 4718600 | tf_op jit(solution)/shard_map/ppermute | solution.py:1186
  207.4 27.2 %collective-permute-start.22 = (bf16[512,1536]{1,0:T(8,128)(2,1)S(1)}, bf16[512,1536]{1,0:T(8,128)(2,1)}, u32[]{:S(2)}, u32[]{:S(2)}) collective-permute-start(bf16[512,1536]{1,0:T(8,128)(2,1)S(1)} %copy-done.18), channel_id=1, source_target_pairs={{0,4},{4,0},{8,12},{12,8},{16,20},{20,16},{24,28},{28,24},{1,5},{5... | collective-permute-start | bytes 4718600 | tf_op jit(solution)/shard_map/ppermute | solution.py:1186
  210.0 36.5 %collective-permute-start.20 = (bf16[512,1536]{1,0:T(8,128)(2,1)S(1)}, bf16[512,1536]{1,0:T(8,128)(2,1)}, u32[]{:S(2)}, u32[]{:S(2)}) collective-permute-start(bf16[512,1536]{1,0:T(8,128)(2,1)S(1)} %copy-done.18), channel_id=1, source_target_pairs={{0,8},{4,12},{8,0},{12,4},{16,24},{20,28},{24,16},{28,20},{1,9},{5... | collective-permute-start | bytes 4718600 | tf_op jit(solution)/shard_map/ppermute | solution.py:1186
  217.9 36.4 %collective-permute-start.21 = (bf16[512,1536]{1,0:T(8,128)(2,1)S(1)}, bf16[512,1536]{1,0:T(8,128)(2,1)S(1)}, u32[]{:S(2)}, u32[]{:S(2)}) collective-permute-start(bf16[512,1536]{1,0:T(8,128)(2,1)S(1)} %copy-done.18), channel_id=1, source_target_pairs={{0,16},{4,20},{8,24},{12,28},{16,0},{20,4},{24,8},{28,12},{1,17},{... | collective-permute-start | bytes 4718600 | tf_op jit(solution)/shard_map/ppermute | solution.py:1186
  254.3 15.6 %collective-permute-start.29 = (bf16[512,1536]{1,0:T(8,128)(2,1)S(1)}, bf16[512,1536]{1,0:T(8,128)(2,1)S(1)}, u32[]{:S(2)}, u32[]{:S(2)}) collective-permute-start(bf16[512,1536]{1,0:T(8,128)(2,1)S(1)} %collective-permute-done.21.rows), channel_id=1, source_target_pairs={{0,4},{4,0},{8,12},{12,8},{16,20},{20,16},{24,28},{28,24},{1,5},{5... | collective-permute-start | bytes 4718600 | tf_op jit(solution)/shard_map/ppermute | solution.py:1186
  256.1 19.5 %collective-permute-start.27 = (bf16[256,1536]{1,0:T(8,128)(2,1)S(1)}, bf16[256,1536]{1,0:T(8,128)(2,1)S(1)}, u32[]{:S(2)}, u32[]{:S(2)}) collective-permute-start(bf16[256,1536]{1,0:T(8,128)(2,1)S(1)} %slice.193), channel_id=1, source_target_pairs={{0,16},{4,20},{8,24},{12,28},{16,0},{20,4},{24,8},{28,12},{1,17},{... | collective-permute-start | bytes 2359304 | tf_op jit(solution)/shard_map/ppermute | solution.py:1186
  256.7 19.1 %collective-permute-start.28 = (bf16[256,1536]{1,0:T(8,128)(2,1)S(1)}, bf16[256,1536]{1,0:T(8,128)(2,1)S(1)}, u32[]{:S(2)}, u32[]{:S(2)}) collective-permute-start(bf16[256,1536]{1,0:T(8,128)(2,1)S(1)} %slice.194), channel_id=1, source_target_pairs={{0,8},{4,12},{8,0},{12,4},{16,24},{20,28},{24,16},{28,20},{1,9},{5... | collective-permute-start | bytes 2359304 | tf_op jit(solution)/shard_map/ppermute | solution.py:1186
  330.7 337.6 %reduce-scatter.5.cloned.1.call-start = ((), (), s32[]{:S(2)}) async-start(), calls=%async_computation.3 | async-start | bytes 8847360 | tf_op jit(solution)/shard_map/reduce_scatter | solution.py:1470
  370.0 16.1 %collective-permute-start.34 = (bf16[4,544,1536]{2,1,0:T(8,128)(2,1)}, bf16[4,544,1536]{2,1,0:T(8,128)(2,1)S(1)}, u32[]{:S(2)}, u32[]{:S(2)}) collective-permute-start(bf16[4,544,1536]{2,1,0:T(8,128)(2,1)} %combine.7), channel_id=1, source_target_pairs={{0,4},{4,0},{8,12},{12,8},{16,20},{20,16},{24,28},{28,24},{1,5},{5... | collective-permute-start | bytes 20054024 | tf_op jit(solution)/shard_map/ppermute | solution.py:1186
  377.5 65.8 %collective-permute-start.33 = (bf16[4,512,1536]{2,1,0:T(8,128)(2,1)}, bf16[4,512,1536]{2,1,0:T(8,128)(2,1)}, u32[]{:S(2)}, u32[]{:S(2)}) collective-permute-start(bf16[4,512,1536]{2,1,0:T(8,128)(2,1)} %combine.5), channel_id=1, source_target_pairs={{0,4},{4,0},{8,12},{12,8},{16,20},{20,16},{24,28},{28,24},{1,5},{5... | collective-permute-start | bytes 18874376 | tf_op jit(solution)/shard_map/ppermute | solution.py:1186
  396.6 38.7 %collective-permute-start.35 = (bf16[2,272,1536]{2,1,0:T(8,128)(2,1)}, bf16[2,272,1536]{2,1,0:T(8,128)(2,1)S(1)}, u32[]{:S(2)}, u32[]{:S(2)}) collective-permute-start(bf16[2,272,1536]{2,1,0:T(8,128)(2,1)} %get-tuple-element.195), channel_id=1, source_target_pairs={{0,8},{4,12},{8,0},{12,4},{16,24},{20,28},{24,16},{28,20},{1,9},{5... | collective-permute-start | bytes 5013512 | tf_op jit(solution)/shard_map/ppermute | solution.py:1186
  398.2 38.4 %collective-permute-start.36 = (bf16[2,272,1536]{2,1,0:T(8,128)(2,1)}, bf16[2,272,1536]{2,1,0:T(8,128)(2,1)S(1)}, u32[]{:S(2)}, u32[]{:S(2)}) collective-permute-start(bf16[2,272,1536]{2,1,0:T(8,128)(2,1)} %get-tuple-element.196), channel_id=1, source_target_pairs={{0,16},{4,20},{8,24},{12,28},{16,0},{20,4},{24,8},{28,12},{1,17},{... | collective-permute-start | bytes 5013512 | tf_op jit(solution)/shard_map/ppermute | solution.py:1186
  441.0 19.7 %collective-permute-start.37 = (bf16[272,1536]{1,0:T(8,128)(2,1)}, bf16[272,1536]{1,0:T(8,128)(2,1)S(1)}, u32[]{:S(2)}, u32[]{:S(2)}) collective-permute-start(bf16[272,1536]{1,0:T(8,128)(2,1)} %get-tuple-element.203), channel_id=1, source_target_pairs={{0,16},{4,20},{8,24},{12,28},{16,0},{20,4},{24,8},{28,12},{1,17},{... | collective-permute-start | bytes 2506760 | tf_op jit(solution)/shard_map/ppermute | solution.py:1186
  442.5 19.4 %collective-permute-start.38 = (bf16[272,1536]{1,0:T(8,128)(2,1)}, bf16[272,1536]{1,0:T(8,128)(2,1)S(1)}, u32[]{:S(2)}, u32[]{:S(2)}) collective-permute-start(bf16[272,1536]{1,0:T(8,128)(2,1)} %get-tuple-element.204), channel_id=1, source_target_pairs={{0,8},{4,12},{8,0},{12,4},{16,24},{20,28},{24,16},{28,20},{1,9},{5... | collective-permute-start | bytes 2506760 | tf_op jit(solution)/shard_map/ppermute | solution.py:1186
  461.9 34.4 %collective-permute-start.39 = (bf16[2,256,1536]{2,1,0:T(8,128)(2,1)}, bf16[2,256,1536]{2,1,0:T(8,128)(2,1)}, u32[]{:S(2)}, u32[]{:S(2)}) collective-permute-start(bf16[2,256,1536]{2,1,0:T(8,128)(2,1)} %get-tuple-element.207), channel_id=1, source_target_pairs={{0,8},{4,12},{8,0},{12,4},{16,24},{20,28},{24,16},{28,20},{1,9},{5... | collective-permute-start | bytes 4718600 | tf_op jit(solution)/shard_map/ppermute | solution.py:1186
  463.1 34.4 %collective-permute-start.40 = (bf16[2,256,1536]{2,1,0:T(8,128)(2,1)}, bf16[2,256,1536]{2,1,0:T(8,128)(2,1)S(1)}, u32[]{:S(2)}, u32[]{:S(2)}) collective-permute-start(bf16[2,256,1536]{2,1,0:T(8,128)(2,1)} %get-tuple-element.208), channel_id=1, source_target_pairs={{0,16},{4,20},{8,24},{12,28},{16,0},{20,4},{24,8},{28,12},{1,17},{... | collective-permute-start | bytes 4718600 | tf_op jit(solution)/shard_map/ppermute | solution.py:1186
  501.9 24.9 %collective-permute-start.41 = (bf16[256,1536]{1,0:T(8,128)(2,1)}, bf16[256,1536]{1,0:T(8,128)(2,1)S(1)}, u32[]{:S(2)}, u32[]{:S(2)}) collective-permute-start(bf16[256,1536]{1,0:T(8,128)(2,1)} %get-tuple-element.218), channel_id=1, source_target_pairs={{0,16},{4,20},{8,24},{12,28},{16,0},{20,4},{24,8},{28,12},{1,17},{... | collective-permute-start | bytes 2359304 | tf_op jit(solution)/shard_map/ppermute | solution.py:1186
  502.5 24.3 %collective-permute-start.42 = (bf16[256,1536]{1,0:T(8,128)(2,1)}, bf16[256,1536]{1,0:T(8,128)(2,1)S(1)}, u32[]{:S(2)}, u32[]{:S(2)}) collective-permute-start(bf16[256,1536]{1,0:T(8,128)(2,1)} %get-tuple-element.219), channel_id=1, source_target_pairs={{0,8},{4,12},{8,0},{12,4},{16,24},{20,28},{24,16},{28,20},{1,9},{5... | collective-permute-start | bytes 2359304 | tf_op jit(solution)/shard_map/ppermute | solution.py:1186
  503.1 23.7 %collective-permute-start.43 = (bf16[512,512]{1,0:T(8,128)(2,1)S(1)}, bf16[512,512]{1,0:T(8,128)(2,1)S(1)}, u32[]{:S(2)}, u32[]{:S(2)}) collective-permute-start(bf16[512,512]{1,0:T(8,128)(2,1)S(1)} %convert_element_type.144), channel_id=1, source_target_pairs={{0,1},{2,3},{4,5},{6,7},{8,9},{10,11},{12,13},{14,15},{16,17},{18,... | collective-permute-start | bytes 1572872 | tf_op jit(solution)/shard_map/ppermute | solution.py:1466
  553.7 35.0 %collective-permute-start.45 = (bf16[2,416,896]{2,1,0:T(8,128)(2,1)}, bf16[2,416,896]{2,1,0:T(8,128)(2,1)S(1)}, u32[]{:S(2)}, u32[]{:S(2)}) collective-permute-start(bf16[2,416,896]{2,1,0:T(8,128)(2,1)} %get-tuple-element.235), channel_id=1, source_target_pairs={{0,8},{4,12},{8,0},{12,4},{16,24},{20,28},{24,16},{28,20},{1,9},{5... | collective-permute-start | bytes 4472840 | tf_op jit(solution)/shard_map/ppermute | solution.py:1186
  555.3 34.6 %collective-permute-start.46 = (bf16[2,416,896]{2,1,0:T(8,128)(2,1)}, bf16[2,416,896]{2,1,0:T(8,128)(2,1)S(1)}, u32[]{:S(2)}, u32[]{:S(2)}) collective-permute-start(bf16[2,416,896]{2,1,0:T(8,128)(2,1)} %get-tuple-element.236), channel_id=1, source_target_pairs={{0,16},{4,20},{8,24},{12,28},{16,0},{20,4},{24,8},{28,12},{1,17},{... | collective-permute-start | bytes 4472840 | tf_op jit(solution)/shard_map/ppermute | solution.py:1186
  594.3 17.9 %collective-permute-start.47 = (bf16[416,896]{1,0:T(8,128)(2,1)}, bf16[416,896]{1,0:T(8,128)(2,1)S(1)}, u32[]{:S(2)}, u32[]{:S(2)}) collective-permute-start(bf16[416,896]{1,0:T(8,128)(2,1)} %get-tuple-element.240), channel_id=1, source_target_pairs={{0,16},{4,20},{8,24},{12,28},{16,0},{20,4},{24,8},{28,12},{1,17},{... | collective-permute-start | bytes 2236424 | tf_op jit(solution)/shard_map/ppermute | solution.py:1186
  598.1 17.8 %collective-permute-start.48 = (bf16[416,896]{1,0:T(8,128)(2,1)}, bf16[416,896]{1,0:T(8,128)(2,1)S(1)}, u32[]{:S(2)}, u32[]{:S(2)}) collective-permute-start(bf16[416,896]{1,0:T(8,128)(2,1)} %get-tuple-element.241), channel_id=1, source_target_pairs={{0,8},{4,12},{8,0},{12,4},{16,24},{20,28},{24,16},{28,20},{1,9},{5... | collective-permute-start | bytes 2236424 | tf_op jit(solution)/shard_map/ppermute | solution.py:1186
  618.7 21.6 %collective-permute-start.50 = (bf16[208,896]{1,0:T(8,128)(2,1)S(1)}, bf16[208,896]{1,0:T(8,128)(2,1)S(1)}, u32[]{:S(2)}, u32[]{:S(2)}) collective-permute-start(bf16[208,896]{1,0:T(8,128)(2,1)S(1)} %get-tuple-element.280), channel_id=1, source_target_pairs={{1,0},{2,1},{3,2},{5,4},{6,5},{7,6},{9,8},{10,9},{11,10},{13,12},{... | collective-permute-start | bytes 1118216 | tf_op jit(solution)/shard_map/ppermute | solution.py:1177
  620.2 44.3 %collective-permute-start.51 = (bf16[208,896]{1,0:T(8,128)(2,1)S(1)}, bf16[208,896]{1,0:T(8,128)(2,1)S(1)}, u32[]{:S(2)}, u32[]{:S(2)}) collective-permute-start(bf16[208,896]{1,0:T(8,128)(2,1)S(1)} %get-tuple-element.281), channel_id=1, source_target_pairs={{0,2},{1,3},{2,0},{3,1},{4,6},{5,7},{6,4},{7,5},{8,10},{9,11},{10,... | collective-permute-start | bytes 1118216 | tf_op jit(solution)/shard_map/ppermute | solution.py:1150
  633.9 30.6 %collective-permute-start.52 = (bf16[208,896]{1,0:T(8,128)(2,1)S(1)}, bf16[208,896]{1,0:T(8,128)(2,1)S(1)}, u32[]{:S(2)}, u32[]{:S(2)}) collective-permute-start(bf16[208,896]{1,0:T(8,128)(2,1)S(1)} %get-tuple-element.282), channel_id=1, source_target_pairs={{0,3},{3,0},{4,7},{7,4},{8,11},{11,8},{12,15},{15,12},{16,19},{19,... | collective-permute-start | bytes 1118216 | tf_op jit(solution)/shard_map/ppermute | solution.py:1146
  637.4 27.2 %collective-permute-start.49 = (bf16[208,896]{1,0:T(8,128)(2,1)S(1)}, bf16[208,896]{1,0:T(8,128)(2,1)S(1)}, u32[]{:S(2)}, u32[]{:S(2)}) collective-permute-start(bf16[208,896]{1,0:T(8,128)(2,1)S(1)} %broadcast_select_fusion), channel_id=1, source_target_pairs={{0,1},{1,2},{2,3},{4,5},{5,6},{6,7},{8,9},{9,10},{10,11},{12,13},{... | collective-permute-start | bytes 1118216 | tf_op jit(solution)/shard_map/ppermute | solution.py:1176
  (72 other events, 490.6 us)
Sparse Core Ops, SparseCore 0:
  206.2 125.5 all-gather.2
  334.0 121.7 reduce-scatter.2
  491.2 130.6 reduce-scatter.4

commit v13 on v12

--- a/solution.py
+++ b/solution.py
@@ -63,16 +63,17 @@
     return values * cosine - pltpu.roll(values, HEAD_DIM // 2, 1) * sine
 
 
-SLOTS = range(4)
 PIECES = (
-    tuple((0, slot) for slot in SLOTS),
-    tuple((1, slot) for slot in SLOTS),
-    tuple((2, slot) for slot in SLOTS),
-    tuple((4, slot) for slot in SLOTS),
-    ((6, 0), (6, 1)),
+    ((0, 0), (2, 0), (4, 0), (6, 0)),
+    ((1, 0), (3, 0), (5, 0), (7, 0)),
+    ((0, 1), (0, 2), (0, 3)),
+    ((2, 1), (2, 2), (2, 3)),
+    ((4, 1), (4, 2), (4, 3)),
+    ((6, 1),),
     ((6, 2), (6, 3)),
-    tuple((flip_bits, slot) for flip_bits in (3, 5) for slot in SLOTS),
-    ((7, 0), (7, 1)),
+    ((1, 1), (1, 2), (1, 3)),
+    ((3, 1), (3, 2), (3, 3), (5, 1), (5, 2), (5, 3)),
+    ((7, 1),),
     ((7, 2), (7, 3)),
 )
 EXTRA = 16
@@ -1169,7 +1170,7 @@
     ]
 
 
-def reduce_slots(slots):
+def reduce_slots(slots, *earlier):
     place = lax.axis_index("cols")
     own, second, third, fourth = slots
     arrived = (
@@ -1178,6 +1179,7 @@
         send_over(second),
         send_far(fourth),
     )
+    arrived = after(arrived, *earlier)
     return own.astype(WIDE) + sum(block.astype(WIDE) for block in arrived)
 
 
@@ -1193,11 +1195,6 @@
 def chips_second(near_x, near_y, got_x, got_y):
     for_y, for_x = corner_adds(near_x, got_x, near_y, got_y)
     return (near_x, got_x, flip(for_y, 4), near_y, got_y, flip(for_x, 2))
-
-
-def turn_corner(beside, across):
-    half = beside.shape[0] // 2
-    return jnp.concatenate([flip(beside[:half], 4), flip(across[half:], 2)], axis=0)
 
 
 def send_chips(sums):
@@ -1282,22 +1279,26 @@
         first_block = after(shard_blocks[0], *packed_near)
         first_near = send_near(first_block)
         first_second = send_second(first_block, first_near)
-        own = jnp.stack(slot_list(packed, packed_near, packed_second, packed_far))
-        own = after(own, info, cosine, sine)
-        beside, across = flip(own, 2), flip(own, 4)
-        own_in = flip(own, 1)
-        beside, across = after((beside, across), own_in, *first_near)
-        corner = [flip(beside[:2], 4), flip(across[2:], 2)]
+        slots = slot_list(packed, packed_near, packed_second, packed_far)
+        first = packed[None]
+        first_four = jnp.concatenate([first] + [flip(first, bits) for bits in (2, 4, 6)], axis=0)
+        others = after(jnp.stack(slots[1:]), info, cosine, sine, first_four)
+        beside, across = flip(others, 2), flip(others, 4)
+        first_in, others_in = flip(first_four, 1), flip(others, 1)
+        at = depth + router_part + 1
+        routes_all = jnp.stack(
+            [part[:, at : at + TOP, :TOK_DEV] for part in (first_four, first_in)], axis=1
+        )
+        routes_all = routes_all.reshape(row_count, TOP, TOK_DEV).astype(jnp.int32)
+        chosen, place_rows = tables(info, routes_all, capacity, local_experts, expert_total)
+        beside, across = after((beside, across), others_in, chosen, *first_near)
+        corner = [flip(beside[:1], 4), flip(across[1:], 2)]
         pair_in = flip(jnp.concatenate([beside, across], axis=0), 1)
         corner_in = [flip(piece, 1) for piece in corner]
+        pieces = [first_four, first_in, others, beside, across, *corner]
+        pieces += [others_in, pair_in, *corner_in]
         grad_in = after(cotangent, *corner)
-        grad_flips = (flip(grad_in, 2), flip(grad_in, 4))
-        pieces = [own, own_in, beside, across, *corner, pair_in, *corner_in]
-        at = depth + router_part + 1
-        near_slots = [own, own_in, beside, pair_in, across, pair_in[4:], corner[0], corner_in[0]]
-        routes_all = jnp.stack([part[0, at : at + TOP, :TOK_DEV] for part in near_slots])
-        routes_all = routes_all.astype(jnp.int32)
-        chosen, place_rows = tables(info, routes_all, capacity, local_experts, expert_total)
+        grad_flips = [flip(grad_in, 2), flip(grad_in, 4)]
         query_refs = pair_refs = out_refs = pieces
         extra_rows = extras(info, pieces)
         router_all = extra_rows[:, :router_part, :depth]
@@ -1335,7 +1336,7 @@
         router_all.reshape(row_count, col_count, router_part, depth), (1, 2, 0, 3)
     ).reshape(expert_total, D)
     router_cols = router_rows.T
-    tokens_in = after(tokens, first_second, chosen) if fast else tokens
+    tokens_in = after(tokens, first_second) if fast else tokens
     normed, own_pair = key_value(info, tokens_in, attention_scale, cosine, sine, pair_refs)
     pairs = [(i + 1, i) for i in range(0, col_count, 2)]
     partner = lax.ppermute(own_pair, "cols", pairs)
@@ -1343,13 +1344,15 @@
     if fast:
         first_far = send_far(after(first_block, partner, queries))
         expert_refs.append([first_block, first_second, *first_near, first_far])
-        grad_flips = after(grad_flips, queries)
-        grad_corner = turn_corner(*grad_flips)
+    if fast:
+        queries = after(queries, *grad_flips)
+        grad_in = after(cotangent, *grad_flips)
+        grad_flips.append(flip(grad_in, 6))
     heads = attention(info, queries, own_pair, partner)
     if fast:
-        heads = after(heads, grad_corner)
-        grad_near = [cotangent, *grad_flips, grad_corner]
+        grad_near = [grad_in, *grad_flips]
         grad_blocks = [block for one in grad_near for block in (one, flip(one, 1))]
+        heads = after(heads, *grad_blocks[1:6])
     else:
         grad_all = lax.all_gather(cotangent, "rows", axis=0)
         grad_blocks = [grad_all[q] for q in range(row_count)]
@@ -1357,7 +1360,7 @@
 
     if fast:
         beside, across = flip(normed_two, 2), flip(normed_two, 4)
-        beside_in = flip(normed_two, 1)
+        beside_in = flip(after(normed_two, *grad_blocks), 1)
         later_block = after(shard_blocks[1], first_far, normed_two)
         expert_refs.append([lax.all_gather(later_block, "cols", axis=0)])
     else:
@@ -1373,9 +1376,9 @@
     if fast:
         half = TOK_DEV // 2
         picked = place_block(0, normed_two, None)
-        picked = place_block(1, beside_in, picked)
         beside, across = after((beside, across), picked, *grad_rows)
         corner = [flip(beside[:half], 4), flip(across[half:], 2)]
+        picked = place_block(1, beside_in, picked)
         picked = place_block(2, beside, picked)
         picked = place_block(4, across, picked)
         beside_in = flip(beside, 1)
@@ -1447,6 +1450,8 @@
     )
     if fast:
         out_flips = send_chips(after(out_first[:2], back_parts[2], back_parts[5]))
+        slots = after(slots, reduced[0], back_parts[2])
+        reduced.append(lax.psum_scatter(slots, "cols", scatter_dimension=0, tiled=False))
         router_parts = jnp.transpose(
             router_grad.astype(LOW).reshape(col_count, router_part, row_count, depth),
             (2, 0, 1, 3),
@@ -1466,37 +1471,41 @@
     arrived = lax.ppermute(source_grad.astype(LOW), "cols", [(j, i) for i, j in pairs])
     if fast:
         parts = ((0, 2, 0, query_part), (1, 3, query_part + 2 * key_part, query_part))
-        slots = after(slots, reduced[0], grad_query)
-        reduced.append(lax.psum_scatter(slots, "cols", scatter_dimension=0, tiled=False))
-        out_flips = after(out_flips, grad_query)
-        near_x, near_y = out_first[2:]
-        for_y, for_x = corner_adds(near_x, out_flips[0], near_y, out_flips[1])
-        mixture = (near_x, out_flips[0], flip(for_y, 4))
-        mixture += (near_y, out_flips[1], flip(for_x, 2))
-        grad_branch = after(grad_branch, for_y)
         keep_send = weight_grads(
             info, [normed, heads], [grad_query, grad_branch], parts, extra
         )
-        arrived = after(arrived, *keep_send, mixture[2], mixture[5])
+        arrived = after(arrived, *keep_send, *out_flips)
     grad_pair = join_grads(info, own_grad, source_grad, arrived, cosine, sine)
     if fast:
         keep, send = weight_grads(
             info, [normed], [grad_pair], ((0, 1, 0, 2 * key_part),), None, keep_send
         )
+        flat = (4, col_count * (depth + EXTRA), wide)
         sent = flip(send, 1)
-        grad_pair = after(grad_pair, keep)
+        sent_first = chip_adds(keep.reshape(flat), sent.reshape(flat))
+        sent_chips = send_chips(sent_first[:2])
+        grad_pair = after(grad_pair, sent_first[0])
     tokens_grad, attention_gain_grad = token_back(
         info, grad_query, grad_pair, tokens, grad_residual, attention_scale, query_refs, pair_refs
     )
 
     if fast:
-        flat = (4, col_count * (depth + EXTRA), wide)
-        sent_first = chip_adds(keep.reshape(flat), sent.reshape(flat))
-        sent_chips = after(send_chips(sent_first[:2]), tokens_grad)
-        slots = sum_parts(chips_second(*sent_first[2:], *sent_chips))
+        sent_chips = after(sent_chips, tokens_grad)
+        sent_parts = chips_second(*sent_first[2:], *sent_chips)
+        near_x, near_y = out_first[2:]
+        mixture = chips_second(near_x, near_y, *after(out_flips, *sent_chips))
+    layer_output = (residual + sum_parts(mixture)).astype(LOW)
+    part = down_weight.shape[1]
+    expert_sums = [block.astype(WIDE) for block in reduced]
+    gate_grad, upward_grad, down_grad = (
+        jnp.stack([sums_of[which * part : (which + 1) * part] for sums_of in expert_sums])
+        for which in range(3)
+    )
+    if fast:
+        slots = sum_parts(sent_parts)
         slots = slots.reshape(col_count, depth + EXTRA, wide)
         width = query_part + 2 * key_part
-        own_slots = own
+        own_slots = [packed, *others]
         gain_sums = sum(
             jnp.sum(own_slots[i][:depth, :width].astype(WIDE) * slots[i, :depth, :width], axis=1)
             for i in range(4)
@@ -1509,7 +1518,7 @@
         )
         slots = after((slots + gain_sums).astype(LOW), reduced[1])
 
-        sums = reduce_slots(slots)
+        sums = reduce_slots(slots, gate_grad, upward_grad, down_grad, layer_output)
         router_sum = sums[depth : depth + router_part, :depth].T
         experts_gain_sum = sums[depth + router_part, :gain_part]
         attention_gain_sum = sums[depth + router_part + 1, :gain_part]
@@ -1548,16 +1557,9 @@
         experts_gain_sum = small_sums[gain_part : 2 * gain_part]
         router_sum = small_sums[2 * gain_part :].reshape(depth, router_part)
 
-    layer_output = (residual + sum_parts(mixture)).astype(LOW)
     key_at = query_part
     value_at = key_at + key_part
     out_at = value_at + key_part
-    part = down_weight.shape[1]
-    expert_sums = [block.astype(WIDE) for block in reduced]
-    gate_grad, upward_grad, down_grad = (
-        jnp.stack([sums_of[which * part : (which + 1) * part] for sums_of in expert_sums])
-        for which in range(3)
-    )
     return (
         layer_output,
         tokens_grad,

time: 694 us -> 725 us (1.045)
  waiting for transfers between devices: 200 us -> 233 us
    ppermute x39 -> x42, waiting for transfers between devices: 143 us -> 163 us  [flip(): return lax.ppermute(block, 'rows', [(i, i ^ bit) for i in range(count)])]
    ppermute x4, starting transfers between devices: 28.1 us -> 14.7 us  [send_near(): return (lax.ppermute(block, 'cols', DOWN), lax.ppermute(block, 'cols', UP))]
    ppermute x3, waiting for transfers between devices: 6.97 us -> 17 us  [send_far(): return lax.ppermute(block, 'cols', FAR)]
    ppermute x2, waiting for transfers between devices: 24.3 us -> 14.8 us  [send_over(): return lax.ppermute(block, 'cols', [(0, 2), (1, 3), (2, 0), (3, 1)])]
    ppermute x4, waiting for transfers between devices: 0.01 us -> 8.69 us  [send_near(): return (lax.ppermute(block, 'cols', DOWN), lax.ppermute(block, 'cols', UP))]
    ppermute x39 -> x42, starting transfers between devices: 27.9 us -> 32 us  [flip(): return lax.ppermute(block, 'rows', [(i, i ^ bit) for i in range(count)])]
    unnamed x141 -> x113, local copies, waits for them, and re-layouts: 26.2 us -> 23.2 us
  transfers between devices with their start and end apart: 56 -> 59, of which waited for: 31 -> 24; matrix products, arithmetic and copies ran while one was open for 7% -> 7% of each run, Pallas kernels for 43% -> 42%
where the time goes in v13:
time: 725 us; the launch traced here: 714 us
  Pallas kernels  299 us (41%)
  waiting for transfers between devices  233 us (32%)
  starting transfers between devices  83.8 us (12%)
  local copies, waits for them, and re-layouts  48.8 us (7%)
  other arithmetic  34.9 us (5%)
  between operations  14.9 us (2%)
    ppermute x42, waiting for transfers between devices, flip(): return lax.ppermute(block, 'rows', [(i, i ^ bit) for i in range(count)])  163 us
    pallas_call x2, Pallas kernels, expert(): pl.pallas_call(functools.partial(expert_kernel, slots), grid=(height // E...  61.7 us
    ppermute x42, starting transfers between devices, flip(): return lax.ppermute(block, 'rows', [(i, i ^ bit) for i in range(count)])  32 us
    pallas_call x4, Pallas kernels, combine(): pl.pallas_call(functools.partial(combine_kernel, local, first, step), out...  30.9 us
    pallas_call x2, Pallas kernels, expert_grads(): pl.pallas_call(expert_grads_kernel, grid=(D // 256,), out_shape=jax.Shape...  29.2 us
    pallas_call x8, Pallas kernels, dispatch(): pl.pallas_call(functools.partial(dispatch_kernel, local), grid=(D // wide...  28.8 us
    unnamed x113, local copies, waits for them, and re-layouts  23.2 us
    pallas_call x3, Pallas kernels, chip_adds(): pl.pallas_call(chip_adds_kernel, out_shape=(shape,) * 4, in_specs=[ANY, A...  22.6 us
  transfers between devices with their start and end apart: 59, of which 24 were waited for; matrix products, arithmetic and copies ran while one was open for 7% of the time, Pallas kernels for 42%

profile of v13, /device:TPU:0, one launch (start us, length us, event | category | flops | bytes accessed | tf_op | source)
XLA Modules:
  0.0 713.9 jit_solution(2712754661916659517)
XLA Ops:
  13.9 6.3 collective-permute-start.1
  26.3 5.5 collective-permute-done.5
  31.8 3.8 collective-permute-start.10
  35.6 4.0 collective-permute-done.6
  47.4 5.8 collective-permute-start.3
  65.1 5.6 route_tables.1
  70.7 16.5 %collective-permute-done.11.rest_3_.rest_9_.rest_14_ = bf16[3,208,896]{2,1,0:T(8,128)(2,1)} collective-permute-done((bf16[3,208,896]{2,1,0:T(8,128)(2,1)S(1)}, bf16[3,208,896]{2,1,0:T(8,128)(2,1)}, u32[]{:S(2)}, u32[]{:S(2)}) %collective-permute-start.11) | collective-permute-done | bytes 1118240 | tf_op jit(solution)/shard_map/ppermute | solution.py:1188
  88.3 8.7 %collective-permute-done.2.rest_2_ = bf16[576,1536]{1,0:T(8,128)(2,1)} collective-permute-done((bf16[576,1536]{1,0:T(8,128)(2,1)}, bf16[576,1536]{1,0:T(8,128)(2,1)}, u32[]{:S(2)}, u32[]{:S(2)}) %collective-permute-start.2) | collective-permute-done | bytes 1769504 | tf_op jit(solution)/shard_map/ppermute | solution.py:1143
  107.5 14.7 %collective-permute-done.15.rest_6_.rest_12_.rest_17_ = bf16[2,208,896]{2,1,0:T(8,128)(2,1)S(1)} collective-permute-done((bf16[2,208,896]{2,1,0:T(8,128)(2,1)S(1)}, bf16[2,208,896]{2,1,0:T(8,128)(2,1)S(1)}, u32[]{:S(2)}, u32[]{:S(2)}) %collective-permute-start.15) | collective-permute-done | bytes 745504 | tf_op jit(solution)/shard_map/ppermute | solution.py:1188
  125.3 16.5 %collective-permute-done.4.rest_1_ = bf16[576,1536]{1,0:T(8,128)(2,1)S(1)} collective-permute-done((bf16[576,1536]{1,0:T(8,128)(2,1)S(1)}, bf16[576,1536]{1,0:T(8,128)(2,1)S(1)}, u32[]{:S(2)}, u32[]{:S(2)}) %collective-permute-start.4) | collective-permute-done | bytes 1769504 | tf_op jit(solution)/shard_map/ppermute | solution.py:1158
  150.3 5.0 norm_key_value.1
  156.6 8.3 %query_projection.1.queries = bf16[512,1536]{1,0:T(8,128)(2,1)} custom-call(s32[16]{0:T(128)} %concatenate.45.info, bf16[512,1536]{1,0:T(8,128)(2,1)} %get-tuple-element.138.normed.rest_0_, f32[512,128]{1,0:T(8,128)} %get-tuple-element.313.cosine, f32[512,128]{1,0:T(8,128)} %get-tuple-element.314.sine, bf16[4,208,896]{2,1,0:T(8,128)(2,1)} %copy-done.1, ...), custom_call_target="tpu_custom_call" | custom-call | flops 1 | bytes 1 | tf_op jit(solution)/shard_map/query_projection/pallas_call | solution.py:196
  164.9 6.5 collective-permute-done.21.partner
  177.4 10.9 %tree_attention.1.heads.rest_1_ = bf16[512,1536]{1,0:T(8,128)(2,1)} custom-call(s32[16]{0:T(128)} %concatenate.45.info, bf16[512,1536]{1,0:T(8,128)(2,1)} %query_projection.1.queries, bf16[512,512]{1,0:T(8,128)(2,1)} %get-tuple-element.141.own, bf16[512,512]{1,0:T(8,128)(2,1)} %copy-done.32), custom_call_target="tpu_custom_call" | custom-call | flops 1 | bytes 1 | tf_op jit(solution)/shard_map/tree_attention/pallas_call | solution.py:278
  188.4 9.8 %out_projection.1 = (f32[512,1536]{1,0:T(8,128)}, bf16[512,1536]{1,0:T(8,128)(2,1)}) custom-call(s32[16]{0:T(128)} %concatenate.45.info, bf16[512,1536]{1,0:T(8,128)(2,1)} %tree_attention.1.heads.rest_1_, bf16[512,1536]{1,0:T(8,128)(2,1)} %tokens.4, f32[1,1536]{1,0:T(1,128)} %reshape.309.gain, bf16[4,208,896]{2,1,0:T(8,128)(2,1)} %copy-done.1, ...), custom_call_target="tpu_custom_call" | custom-call | flops 1 | bytes 1 | tf_op jit(solution)/shard_map/out_projection/pallas_call | solution.py:390
  198.2 17.0 %collective-permute-done.35.rest_4_ = bf16[576,1536]{1,0:T(8,128)(2,1)} collective-permute-done((bf16[576,1536]{1,0:T(8,128)(2,1)}, bf16[576,1536]{1,0:T(8,128)(2,1)}, u32[]{:S(2)}, u32[]{:S(2)}) %collective-permute-start.35) | collective-permute-done | bytes 1769504 | tf_op jit(solution)/shard_map/ppermute | solution.py:1147
  218.2 33.4 %collective-permute-done.27.rest_6_ = bf16[512,1536]{1,0:T(8,128)(2,1)} collective-permute-done((bf16[512,1536]{1,0:T(8,128)(2,1)S(1)}, bf16[512,1536]{1,0:T(8,128)(2,1)}, u32[]{:S(2)}, u32[]{:S(2)}) %collective-permute-start.27) | collective-permute-done | bytes 1572896 | tf_op jit(solution)/shard_map/ppermute | solution.py:1188
  258.0 3.7 dispatch.8
  261.8 9.2 %pick_rows.1 = (bf16[8,160,1536]{2,1,0:T(8,128)(2,1)}, bf16[8,160,1536]{2,1,0:T(8,128)(2,1)}) custom-call(bf16[8,320,512]{2,1,0:T(8,128)(2,1)} %get-tuple-element.135.chosen, bf16[512,1536]{1,0:T(8,128)(2,1)} %cotangent.1, bf16[512,1536]{1,0:T(8,128)(2,1)} %collective-permute-done.22.rest_1_, bf16[512,1536]{1,0:T(8,128)(2,1)} %collective-permute-done.19.rest_2_, ...), custom_call_target="tpu_custom_call" | custom-call | flops 1 | bytes 1 | tf_op jit(solution)/shard_map/pick_rows/pallas_call | solution.py:481
  271.0 17.4 %collective-permute-done.25.rows = bf16[512,1536]{1,0:T(8,128)(2,1)} collective-permute-done((bf16[512,1536]{1,0:T(8,128)(2,1)S(1)}, bf16[512,1536]{1,0:T(8,128)(2,1)}, u32[]{:S(2)}, u32[]{:S(2)}) %collective-permute-start.25) | collective-permute-done | bytes 1572896 | tf_op jit(solution)/shard_map/ppermute | solution.py:1188
  298.0 3.6 dispatch.10
  301.6 3.6 dispatch.11
  306.4 3.6 dispatch.12
  322.1 3.6 dispatch.15
  325.6 30.7 %expert.2 = (bf16[1280,1536]{1,0:T(8,128)(2,1)}, bf16[1280,1536]{1,0:T(8,128)(2,1)}, bf16[1280,1536]{1,0:T(8,128)(2,1)}, bf16[4,576,1280]{2,1,0:T(8,128)(2,1)}, f32[1280,1]{1,0:T(8,128)}) custom-call(s32[16]{0:T(128)} %concatenate.45.info, bf16[1280,1536]{1,0:T(8,128)(2,1)} %bitcast.152, bf16[1280,1536]{1,0:T(8,128)(2,1)} %bitcast.180, f32[1280,1]{1,0:T(8,128)} %bitcast.156, ...), custom_call_target="tpu_custom_call" | custom-call | flops 1 | bytes 1 | tf_op jit(solution)/shard_map/expert/pallas_call | solution.py:671
  356.3 14.6 %expert_gradients.2 = bf16[4,576,1536]{2,1,0:T(8,128)(2,1)} custom-call(bf16[4,576,1280]{2,1,0:T(8,128)(2,1)} %get-tuple-element.186.acts, bf16[1280,1536]{1,0:T(8,128)(2,1)} %bitcast.153, bf16[1280,1536]{1,0:T(8,128)(2,1)} %get-tuple-element.187.grads), custom_call_target="tpu_custom_call" | custom-call | flops 1 | bytes 1 | tf_op jit(solution)/shard_map/expert_gradients/pallas_call | solution.py:700
  371.0 31.0 %expert.3 = (bf16[1280,1536]{1,0:T(8,128)(2,1)}, bf16[1280,1536]{1,0:T(8,128)(2,1)}, bf16[1280,1536]{1,0:T(8,128)(2,1)}, bf16[4,576,1280]{2,1,0:T(8,128)(2,1)}, f32[1280,1]{1,0:T(8,128)}) custom-call(s32[16]{0:T(128)} %concatenate.45.info, bf16[1280,1536]{1,0:T(8,128)(2,1)} %bitcast.154, bf16[1280,1536]{1,0:T(8,128)(2,1)} %bitcast.181, f32[1280,1]{1,0:T(8,128)} %bitcast.157, ...), custom_call_target="tpu_custom_call" | custom-call | flops 1 | bytes 1 | tf_op jit(solution)/shard_map/expert/pallas_call | solution.py:671
  402.0 8.0 %combine.7 = bf16[4,544,1536]{2,1,0:T(8,128)(2,1)} custom-call(s32[16]{0:T(128)} %concatenate.45.info, bf16[8,320,512]{2,1,0:T(8,128)(2,1)} %get-tuple-element.135.chosen, bf16[8,160,1536]{2,1,0:T(8,128)(2,1)} %bitcast.163, bf16[8,160,1536]{2,1,0:T(8,128)(2,1)} %bitcast.167, f32[8,160,1]{2,1,0:T(8,128)} %bitcast.182, f32[8,160,1]{2,1,0:T(8,128)} %bitcast.184), custom_call_target="tpu_custom_call" | custom-call | flops 1 | bytes 1 | tf_op jit(solution)/shard_map/combine/pallas_call | solution.py:763
  410.1 7.3 %combine.5 = bf16[4,512,1536]{2,1,0:T(8,128)(2,1)} custom-call(s32[16]{0:T(128)} %concatenate.45.info, bf16[8,320,512]{2,1,0:T(8,128)(2,1)} %get-tuple-element.135.chosen, bf16[8,160,1536]{2,1,0:T(8,128)(2,1)} %bitcast.161, bf16[8,160,1536]{2,1,0:T(8,128)(2,1)} %bitcast.165), custom_call_target="tpu_custom_call" | custom-call | flops 1 | bytes 1 | tf_op jit(solution)/shard_map/combine/pallas_call | solution.py:763
  418.0 8.1 %combine.6.keep = bf16[4,544,1536]{2,1,0:T(8,128)(2,1)} custom-call(s32[16]{0:T(128)} %concatenate.45.info, bf16[8,320,512]{2,1,0:T(8,128)(2,1)} %get-tuple-element.135.chosen, bf16[8,160,1536]{2,1,0:T(8,128)(2,1)} %bitcast.164, bf16[8,160,1536]{2,1,0:T(8,128)(2,1)} %bitcast.168, f32[8,160,1]{2,1,0:T(8,128)} %bitcast.183, f32[8,160,1]{2,1,0:T(8,128)} %bitcast.185), custom_call_target="tpu_custom_call" | custom-call | flops 1 | bytes 1 | tf_op jit(solution)/shard_map/combine/pallas_call | solution.py:763
  428.8 7.8 %chip_sums.4 = (bf16[2,272,1536]{2,1,0:T(8,128)(2,1)}, bf16[2,272,1536]{2,1,0:T(8,128)(2,1)}, bf16[2,272,1536]{2,1,0:T(8,128)(2,1)}, bf16[2,272,1536]{2,1,0:T(8,128)(2,1)}) custom-call(bf16[4,544,1536]{2,1,0:T(8,128)(2,1)} %combine.6.keep, bf16[4,544,1536]{2,1,0:T(8,128)(2,1)} %copy-done.10), custom_call_target="tpu_custom_call" | custom-call | flops 1 | bytes 1 | tf_op jit(solution)/shard_map/chip_sums/pallas_call | solution.py:812
  438.1 7.5 %combine.4.keep = bf16[4,512,1536]{2,1,0:T(8,128)(2,1)} custom-call(s32[16]{0:T(128)} %concatenate.45.info, bf16[8,320,512]{2,1,0:T(8,128)(2,1)} %get-tuple-element.135.chosen, bf16[8,160,1536]{2,1,0:T(8,128)(2,1)} %bitcast.162, bf16[8,160,1536]{2,1,0:T(8,128)(2,1)} %bitcast.166), custom_call_target="tpu_custom_call" | custom-call | flops 1 | bytes 1 | tf_op jit(solution)/shard_map/combine/pallas_call | solution.py:763
  445.7 14.6 %expert_gradients.3 = bf16[4,576,1536]{2,1,0:T(8,128)(2,1)} custom-call(bf16[4,576,1280]{2,1,0:T(8,128)(2,1)} %get-tuple-element.203.acts, bf16[1280,1536]{1,0:T(8,128)(2,1)} %bitcast.155, bf16[1280,1536]{1,0:T(8,128)(2,1)} %get-tuple-element.204.grads), custom_call_target="tpu_custom_call" | custom-call | flops 1 | bytes 1 | tf_op jit(solution)/shard_map/expert_gradients/pallas_call | solution.py:700
  460.3 15.0 %collective-permute-done.38.got_x.rest_1_ = bf16[2,272,1536]{2,1,0:T(8,128)(2,1)S(1)} collective-permute-done((bf16[2,272,1536]{2,1,0:T(8,128)(2,1)}, bf16[2,272,1536]{2,1,0:T(8,128)(2,1)S(1)}, u32[]{:S(2)}, u32[]{:S(2)}) %collective-permute-start.38) | collective-permute-done | bytes 1671200 | tf_op jit(solution)/shard_map/ppermute | solution.py:1188
  481.9 7.6 %chip_sums.3 = (bf16[2,256,1536]{2,1,0:T(8,128)(2,1)}, bf16[2,256,1536]{2,1,0:T(8,128)(2,1)}, bf16[2,256,1536]{2,1,0:T(8,128)(2,1)}, bf16[2,256,1536]{2,1,0:T(8,128)(2,1)}) custom-call(bf16[4,512,1536]{2,1,0:T(8,128)(2,1)} %combine.4.keep, bf16[4,512,1536]{2,1,0:T(8,128)(2,1)} %collective-permute-done.36.got), custom_call_target="tpu_custom_call" | custom-call | flops 1 | bytes 1 | tf_op jit(solution)/shard_map/chip_sums/pallas_call | solution.py:812
  489.5 11.2 %collective-permute-done.40.rest_2_ = bf16[272,1536]{1,0:T(8,128)(2,1)S(1)} collective-permute-done((bf16[272,1536]{1,0:T(8,128)(2,1)}, bf16[272,1536]{1,0:T(8,128)(2,1)S(1)}, u32[]{:S(2)}, u32[]{:S(2)}) %collective-permute-start.40) | collective-permute-done | bytes 835616 | tf_op jit(solution)/shard_map/ppermute | solution.py:1188
  503.6 13.3 %experts_norm_back.1 = (f32[512,1536]{1,0:T(8,128)}, bf16[512,1536]{1,0:T(8,128)(2,1)}, bf16[512,1536]{1,0:T(8,128)(2,1)}, f32[1,1536]{1,0:T(1,128)}, f32[16,1536]{1,0:T(8,128)}) custom-call(s32[16]{0:T(128)} %concatenate.45.info, f32[512,1536]{1,0:T(8,128)} %get-tuple-element.144.residual, bf16[512,1536]{1,0:T(8,128)(2,1)} %get-tuple-element.154.rows.normed, ...), custom_call_target="tpu_custom_call" | custom-call | flops 1 | bytes 1 | tf_op jit(solution)/shard_map/experts_norm_back/pallas_call | solution.py:923
  516.9 15.4 %tree_attention_back.1 = (bf16[512,1536]{1,0:T(8,128)(2,1)}, f32[512,512]{1,0:T(8,128)}, f32[512,512]{1,0:T(8,128)}) custom-call(s32[16]{0:T(128)} %concatenate.45.info, bf16[512,1536]{1,0:T(8,128)(2,1)} %query_projection.1.queries, bf16[512,512]{1,0:T(8,128)(2,1)} %get-tuple-element.141.own, bf16[512,512]{1,0:T(8,128)(2,1)} %copy-done.32, ...), custom_call_target="tpu_custom_call" | custom-call | flops 1 | bytes 1 | tf_op jit(solution)/shard_map/tree_attention_back/pallas_call | solution.py:339
  536.5 13.9 %weight_gradients.2 = (bf16[4,4,208,896]{3,2,1,0:T(8,128)(2,1)}, bf16[4,4,208,896]{3,2,1,0:T(8,128)(2,1)}) custom-call(s32[16]{0:T(128)} %concatenate.45.info, bf16[512,1536]{1,0:T(8,128)(2,1)} %get-tuple-element.138.normed.rest_0_, bf16[512,1536]{1,0:T(8,128)(2,1)} %tree_attention.1.heads.rest_1_, bf16[512,1536]{1,0:T(8,128)(2,1)} %get-tuple-element.221.rest_2_.grad_query, ...), custom_call_target="tpu_custom_call" | custom-call | flops 1 | bytes 1 | tf_op jit(solution)/shard_map/weight_gradients/pallas_call | solution.py:1088
  550.3 6.7 collective-permute-done.44.arrived
  561.0 5.7 weight_gradients.3
  566.7 9.9 %collective-permute-done.45 = bf16[4,4,208,896]{3,2,1,0:T(8,128)(2,1)S(1)} collective-permute-done((bf16[4,4,208,896]{3,2,1,0:T(8,128)(2,1)}, bf16[4,4,208,896]{3,2,1,0:T(8,128)(2,1)S(1)}, u32[]{:S(2)}, u32[]{:S(2)}) %collective-permute-start.45) | collective-permute-done | bytes 5963808 | tf_op jit(solution)/shard_map/ppermute | solution.py:1188
  579.2 7.2 %chip_sums.5 = (bf16[2,416,896]{2,1,0:T(8,128)(2,1)}, bf16[2,416,896]{2,1,0:T(8,128)(2,1)}, bf16[2,416,896]{2,1,0:T(8,128)(2,1)}, bf16[2,416,896]{2,1,0:T(8,128)(2,1)}) custom-call(bf16[4,832,896]{2,1,0:T(8,128)(2,1)} %bitcast.158, bf16[4,832,896]{2,1,0:T(8,128)(2,1)} %bitcast.179), custom_call_target="tpu_custom_call" | custom-call | flops 1 | bytes 1 | tf_op jit(solution)/shard_map/chip_sums/pallas_call | solution.py:812
  588.9 12.4 %token_gradient.1 = (bf16[512,1536]{1,0:T(8,128)(2,1)}, f32[1,1536]{1,0:T(1,128)}) custom-call(s32[16]{0:T(128)} %concatenate.45.info, bf16[512,1536]{1,0:T(8,128)(2,1)} %get-tuple-element.221.rest_2_.grad_query, bf16[512,512]{1,0:T(8,128)(2,1)} %join_key_value_gradients.1.rest_1_.grad_pair, bf16[512,1536]{1,0:T(8,128)(2,1)} %tokens.4, ...), custom_call_target="tpu_custom_call" | custom-call | flops 1 | bytes 1 | tf_op jit(solution)/shard_map/token_gradient/pallas_call | solution.py:1014
  601.3 20.2 %collective-permute-done.46.got_x = bf16[2,416,896]{2,1,0:T(8,128)(2,1)} collective-permute-done((bf16[2,416,896]{2,1,0:T(8,128)(2,1)}, bf16[2,416,896]{2,1,0:T(8,128)(2,1)}, u32[]{:S(2)}, u32[]{:S(2)}) %collective-permute-start.46) | collective-permute-done | bytes 1490976 | tf_op jit(solution)/shard_map/ppermute | solution.py:1188
  637.1 8.6 %collective-permute-done.50 = bf16[416,896]{1,0:T(8,128)(2,1)S(1)} collective-permute-done((bf16[416,896]{1,0:T(8,128)(2,1)}, bf16[416,896]{1,0:T(8,128)(2,1)S(1)}, u32[]{:S(2)}, u32[]{:S(2)}) %collective-permute-start.50) | collective-permute-done | bytes 745504 | tf_op jit(solution)/shard_map/ppermute | solution.py:1188
  652.8 15.4 %collective-permute-start.54 = (bf16[208,896]{1,0:T(8,128)(2,1)}, bf16[208,896]{1,0:T(8,128)(2,1)S(1)}, u32[]{:S(2)}, u32[]{:S(2)}) collective-permute-start(bf16[208,896]{1,0:T(8,128)(2,1)} %get-tuple-element.289), channel_id=1, source_target_pairs={{0,2},{1,3},{2,0},{3,1},{4,6},{5,7},{6,4},{7,5},{8,10},{9,11},{10,... | collective-permute-start | bytes 1118216 | tf_op jit(solution)/shard_map/ppermute | solution.py:1151
  685.1 11.6 %collective-permute-done.54 = bf16[208,896]{1,0:T(8,128)(2,1)S(1)} collective-permute-done((bf16[208,896]{1,0:T(8,128)(2,1)}, bf16[208,896]{1,0:T(8,128)(2,1)S(1)}, u32[]{:S(2)}, u32[]{:S(2)}) %collective-permute-start.54) | collective-permute-done | bytes 372768 | tf_op jit(solution)/shard_map/ppermute | solution.py:1151
  (306 shorter events, 172.1 us)
Async XLA Ops:
  7.2 363.8 %all-gather.3.cloned.1.call-start = ((), (), s32[]{:S(2)}) async-start(), calls=%async_computation.4 | async-start | bytes 8847360 | tf_op jit(solution)/shard_map/all_gather | solution.py:1365
  12.6 33.5 %collective-permute-start = (bf16[208,896]{1,0:T(8,128)(2,1)S(1)}, bf16[208,896]{1,0:T(8,128)(2,1)}, u32[]{:S(2)}, u32[]{:S(2)}) collective-permute-start(bf16[208,896]{1,0:T(8,128)(2,1)S(1)} %concatenate.49), channel_id=1, source_target_pairs={{1,0},{2,1},{3,2},{5,4},{6,5},{7,6},{9,8},{10,9},{11,10},{13,12},{... | collective-permute-start | bytes 1118216 | tf_op jit(solution)/shard_map/ppermute | solution.py:1143
  13.9 32.2 %collective-permute-start.1 = (bf16[208,896]{1,0:T(8,128)(2,1)S(1)}, bf16[208,896]{1,0:T(8,128)(2,1)}, u32[]{:S(2)}, u32[]{:S(2)}) collective-permute-start(bf16[208,896]{1,0:T(8,128)(2,1)S(1)} %concatenate.49), channel_id=1, source_target_pairs={{0,1},{1,2},{2,3},{4,5},{5,6},{6,7},{8,9},{9,10},{10,11},{12,13},{... | collective-permute-start | bytes 1118216 | tf_op jit(solution)/shard_map/ppermute | solution.py:1143
  22.1 17.6 %collective-permute-start.6 = (bf16[1,208,896]{2,1,0:T(8,128)(2,1)S(1)}, bf16[1,208,896]{2,1,0:T(8,128)(2,1)S(1)}, u32[]{:S(2)}, u32[]{:S(2)}) collective-permute-start(bf16[1,208,896]{2,1,0:T(8,128)(2,1)S(1)} %bitcast.187), channel_id=1, source_target_pairs={{0,16},{4,20},{8,24},{12,28},{16,0},{20,4},{24,8},{28,12},{1,17},{... | collective-permute-start | bytes 1118216 | tf_op jit(solution)/shard_map/ppermute | solution.py:1188
  23.6 18.7 %collective-permute-start.7 = (bf16[1,208,896]{2,1,0:T(8,128)(2,1)S(1)}, bf16[1,208,896]{2,1,0:T(8,128)(2,1)S(1)}, u32[]{:S(2)}, u32[]{:S(2)}) collective-permute-start(bf16[1,208,896]{2,1,0:T(8,128)(2,1)S(1)} %bitcast.188), channel_id=1, source_target_pairs={{0,24},{4,28},{8,16},{12,20},{16,8},{20,12},{24,0},{28,4},{1,25},{... | collective-permute-start | bytes 1118216 | tf_op jit(solution)/shard_map/ppermute | solution.py:1188
  31.8 23.3 %collective-permute-start.10 = (bf16[208,896]{1,0:T(8,128)(2,1)S(1)}, bf16[208,896]{1,0:T(8,128)(2,1)}, u32[]{:S(2)}, u32[]{:S(2)}) collective-permute-start(bf16[208,896]{1,0:T(8,128)(2,1)S(1)} %concatenate.49), channel_id=1, source_target_pairs={{0,3},{3,0},{4,7},{7,4},{8,11},{11,8},{12,15},{15,12},{16,19},{19,... | collective-permute-start | bytes 1118216 | tf_op jit(solution)/shard_map/ppermute | solution.py:1147
  39.7 19.8 %collective-permute-start.9 = (bf16[208,896]{1,0:T(8,128)(2,1)S(1)}, bf16[208,896]{1,0:T(8,128)(2,1)}, u32[]{:S(2)}, u32[]{:S(2)}) collective-permute-start(bf16[208,896]{1,0:T(8,128)(2,1)S(1)} %concatenate.49), channel_id=1, source_target_pairs={{0,2},{1,3},{2,0},{3,1},{4,6},{5,7},{6,4},{7,5},{8,10},{9,11},{10,... | collective-permute-start | bytes 1118216 | tf_op jit(solution)/shard_map/ppermute | solution.py:1151
  42.6 20.9 %collective-permute-start.8 = (bf16[4,208,896]{2,1,0:T(8,128)(2,1)S(1)}, bf16[4,208,896]{2,1,0:T(8,128)(2,1)}, u32[]{:S(2)}, u32[]{:S(2)}) collective-permute-start(bf16[4,208,896]{2,1,0:T(8,128)(2,1)S(1)} %pad_maximum_fusion.7.rest_0_.rest_6_.rest_11_), channel_id=1, source_target_pairs={{0,4},{4,0},{8,12},{12,8},{16,20},{20,16},{24,28},{28,24},{1,5},{5... | collective-permute-start | bytes 4472840 | tf_op jit(solution)/shard_map/ppermute | solution.py:1188
  46.1 50.9 %collective-permute-start.2 = (bf16[576,1536]{1,0:T(8,128)(2,1)}, bf16[576,1536]{1,0:T(8,128)(2,1)}, u32[]{:S(2)}, u32[]{:S(2)}) collective-permute-start(bf16[576,1536]{1,0:T(8,128)(2,1)} %pad_maximum_fusion.5.rest_0_), channel_id=1, source_target_pairs={{1,0},{2,1},{3,2},{5,4},{6,5},{7,6},{9,8},{10,9},{11,10},{13,12},{... | collective-permute-start | bytes 5308424 | tf_op jit(solution)/shard_map/ppermute | solution.py:1143
  47.4 49.6 %collective-permute-start.3 = (bf16[576,1536]{1,0:T(8,128)(2,1)}, bf16[576,1536]{1,0:T(8,128)(2,1)}, u32[]{:S(2)}, u32[]{:S(2)}) collective-permute-start(bf16[576,1536]{1,0:T(8,128)(2,1)} %pad_maximum_fusion.5.rest_0_), channel_id=1, source_target_pairs={{0,1},{1,2},{2,3},{4,5},{5,6},{6,7},{8,9},{9,10},{10,11},{12,13},{... | collective-permute-start | bytes 5308424 | tf_op jit(solution)/shard_map/ppermute | solution.py:1143
  60.6 26.6 %collective-permute-start.11 = (bf16[3,208,896]{2,1,0:T(8,128)(2,1)S(1)}, bf16[3,208,896]{2,1,0:T(8,128)(2,1)}, u32[]{:S(2)}, u32[]{:S(2)}) collective-permute-start(bf16[3,208,896]{2,1,0:T(8,128)(2,1)S(1)} %pad_maximum_fusion.8.rest_2_.rest_8_.rest_13_), channel_id=1, source_target_pairs={{0,8},{4,12},{8,0},{12,4},{16,24},{20,28},{24,16},{28,20},{1,9},{5... | collective-permute-start | bytes 3354632 | tf_op jit(solution)/shard_map/ppermute | solution.py:1188
  62.0 26.3 %collective-permute-start.12 = (bf16[3,208,896]{2,1,0:T(8,128)(2,1)S(1)}, bf16[3,208,896]{2,1,0:T(8,128)(2,1)}, u32[]{:S(2)}, u32[]{:S(2)}) collective-permute-start(bf16[3,208,896]{2,1,0:T(8,128)(2,1)S(1)} %pad_maximum_fusion.8.rest_2_.rest_8_.rest_13_), channel_id=1, source_target_pairs={{0,16},{4,20},{8,24},{12,28},{16,0},{20,4},{24,8},{28,12},{1,17},{... | collective-permute-start | bytes 3354632 | tf_op jit(solution)/shard_map/ppermute | solution.py:1188
  63.5 24.8 %collective-permute-start.13 = (bf16[3,208,896]{2,1,0:T(8,128)(2,1)S(1)}, bf16[3,208,896]{2,1,0:T(8,128)(2,1)}, u32[]{:S(2)}, u32[]{:S(2)}) collective-permute-start(bf16[3,208,896]{2,1,0:T(8,128)(2,1)S(1)} %pad_maximum_fusion.8.rest_2_.rest_8_.rest_13_), channel_id=1, source_target_pairs={{0,4},{4,0},{8,12},{12,8},{16,20},{20,16},{24,28},{28,24},{1,5},{5... | collective-permute-start | bytes 3354632 | tf_op jit(solution)/shard_map/ppermute | solution.py:1188
  98.8 44.6 %collective-permute-start.16 = (bf16[6,208,896]{2,1,0:T(8,128)(2,1)S(1)}, bf16[6,208,896]{2,1,0:T(8,128)(2,1)S(1)}, u32[]{:S(2)}, u32[]{:S(2)}) collective-permute-start(bf16[6,208,896]{2,1,0:T(8,128)(2,1)S(1)} %pad_maximum_fusion.4), channel_id=1, source_target_pairs={{0,4},{4,0},{8,12},{12,8},{16,20},{20,16},{24,28},{28,24},{1,5},{5... | collective-permute-start | bytes 6709256 | tf_op jit(solution)/shard_map/ppermute | solution.py:1188
  100.7 41.0 %collective-permute-start.4 = (bf16[576,1536]{1,0:T(8,128)(2,1)S(1)}, bf16[576,1536]{1,0:T(8,128)(2,1)S(1)}, u32[]{:S(2)}, u32[]{:S(2)}) collective-permute-start(bf16[576,1536]{1,0:T(8,128)(2,1)S(1)} %select_select_fusion), channel_id=1, source_target_pairs={{3,1},{1,0},{0,2},{2,3},{7,5},{5,4},{4,6},{6,7},{11,9},{9,8},{8,10... | collective-permute-start | bytes 5308424 | tf_op jit(solution)/shard_map/ppermute | solution.py:1158
  103.3 18.8 %collective-permute-start.15 = (bf16[2,208,896]{2,1,0:T(8,128)(2,1)S(1)}, bf16[2,208,896]{2,1,0:T(8,128)(2,1)S(1)}, u32[]{:S(2)}, u32[]{:S(2)}) collective-permute-start(bf16[2,208,896]{2,1,0:T(8,128)(2,1)S(1)} %slice.142), channel_id=1, source_target_pairs={{0,8},{4,12},{8,0},{12,4},{16,24},{20,28},{24,16},{28,20},{1,9},{5... | collective-permute-start | bytes 2236424 | tf_op jit(solution)/shard_map/ppermute | solution.py:1188
  105.9 16.3 %collective-permute-start.14 = (bf16[1,208,896]{2,1,0:T(8,128)(2,1)S(1)}, bf16[1,208,896]{2,1,0:T(8,128)(2,1)S(1)}, u32[]{:S(2)}, u32[]{:S(2)}) collective-permute-start(bf16[1,208,896]{2,1,0:T(8,128)(2,1)S(1)} %slice.141), channel_id=1, source_target_pairs={{0,16},{4,20},{8,24},{12,28},{16,0},{20,4},{24,8},{28,12},{1,17},{... | collective-permute-start | bytes 1118216 | tf_op jit(solution)/shard_map/ppermute | solution.py:1188
  122.1 21.3 %collective-permute-start.18 = (bf16[2,208,896]{2,1,0:T(8,128)(2,1)S(1)}, bf16[2,208,896]{2,1,0:T(8,128)(2,1)S(1)}, u32[]{:S(2)}, u32[]{:S(2)}) collective-permute-start(bf16[2,208,896]{2,1,0:T(8,128)(2,1)S(1)} %collective-permute-done.15.rest_6_.rest_12_.rest_17_), channel_id=1, source_target_pairs={{0,4},{4,0},{8,12},{12,8},{16,20},{20,16},{24,28},{28,24},{1,5},{5... | collective-permute-start | bytes 2236424 | tf_op jit(solution)/shard_map/ppermute | solution.py:1188
  122.2 52.5 %collective-permute-start.19 = (bf16[512,1536]{1,0:T(8,128)(2,1)S(1)}, bf16[512,1536]{1,0:T(8,128)(2,1)}, u32[]{:S(2)}, u32[]{:S(2)}) collective-permute-start(bf16[512,1536]{1,0:T(8,128)(2,1)S(1)} %copy-done.13), channel_id=1, source_target_pairs={{0,8},{4,12},{8,0},{12,4},{16,24},{20,28},{24,16},{28,20},{1,9},{5... | collective-permute-start | bytes 4718600 | tf_op jit(solution)/shard_map/ppermute | solution.py:1188
  123.7 51.0 %collective-permute-start.20 = (bf16[512,1536]{1,0:T(8,128)(2,1)S(1)}, bf16[512,1536]{1,0:T(8,128)(2,1)}, u32[]{:S(2)}, u32[]{:S(2)}) collective-permute-start(bf16[512,1536]{1,0:T(8,128)(2,1)S(1)} %copy-done.13), channel_id=1, source_target_pairs={{0,16},{4,20},{8,24},{12,28},{16,0},{20,4},{24,8},{28,12},{1,17},{... | collective-permute-start | bytes 4718600 | tf_op jit(solution)/shard_map/ppermute | solution.py:1188
  171.4 43.8 %collective-permute-start.35 = (bf16[576,1536]{1,0:T(8,128)(2,1)}, bf16[576,1536]{1,0:T(8,128)(2,1)}, u32[]{:S(2)}, u32[]{:S(2)}) collective-permute-start(bf16[576,1536]{1,0:T(8,128)(2,1)} %pad_maximum_fusion.5.rest_0_), channel_id=1, source_target_pairs={{0,3},{3,0},{4,7},{7,4},{8,11},{11,8},{12,15},{15,12},{16,19},{19,... | collective-permute-start | bytes 5308424 | tf_op jit(solution)/shard_map/ppermute | solution.py:1147
  215.2 410.7 %reduce-scatter.3.cloned.1.call-start = ((), (), s32[]{:S(2)}) async-start(), calls=%async_computation.2 | async-start | bytes 8847360 | tf_op jit(solution)/shard_map/reduce_scatter | solution.py:1424
  215.6 36.0 %collective-permute-start.27 = (bf16[512,1536]{1,0:T(8,128)(2,1)S(1)}, bf16[512,1536]{1,0:T(8,128)(2,1)}, u32[]{:S(2)}, u32[]{:S(2)}) collective-permute-start(bf16[512,1536]{1,0:T(8,128)(2,1)S(1)} %copy-done.13), channel_id=1, source_target_pairs={{0,24},{4,28},{8,16},{12,20},{16,8},{20,12},{24,0},{28,4},{1,25},{... | collective-permute-start | bytes 4718600 | tf_op jit(solution)/shard_map/ppermute | solution.py:1188
  251.6 36.9 %collective-permute-start.25 = (bf16[512,1536]{1,0:T(8,128)(2,1)S(1)}, bf16[512,1536]{1,0:T(8,128)(2,1)}, u32[]{:S(2)}, u32[]{:S(2)}) collective-permute-start(bf16[512,1536]{1,0:T(8,128)(2,1)S(1)} %copy-done.14), channel_id=1, source_target_pairs={{0,8},{4,12},{8,0},{12,4},{16,24},{20,28},{24,16},{28,20},{1,9},{5... | collective-permute-start | bytes 4718600 | tf_op jit(solution)/shard_map/ppermute | solution.py:1188
  253.2 36.5 %collective-permute-start.26 = (bf16[512,1536]{1,0:T(8,128)(2,1)S(1)}, bf16[512,1536]{1,0:T(8,128)(2,1)S(1)}, u32[]{:S(2)}, u32[]{:S(2)}) collective-permute-start(bf16[512,1536]{1,0:T(8,128)(2,1)S(1)} %copy-done.14), channel_id=1, source_target_pairs={{0,16},{4,20},{8,24},{12,28},{16,0},{20,4},{24,8},{28,12},{1,17},{... | collective-permute-start | bytes 4718600 | tf_op jit(solution)/shard_map/ppermute | solution.py:1188
  261.7 32.8 %collective-permute-start.33 = (bf16[512,1536]{1,0:T(8,128)(2,1)S(1)}, bf16[512,1536]{1,0:T(8,128)(2,1)}, u32[]{:S(2)}, u32[]{:S(2)}) collective-permute-start(bf16[512,1536]{1,0:T(8,128)(2,1)S(1)} %copy-done.15), channel_id=1, source_target_pairs={{0,4},{4,0},{8,12},{12,8},{16,20},{20,16},{24,28},{28,24},{1,5},{5... | collective-permute-start | bytes 4718600 | tf_op jit(solution)/shard_map/ppermute | solution.py:1188
  289.8 20.3 %collective-permute-start.31 = (bf16[512,1536]{1,0:T(8,128)(2,1)S(1)}, bf16[512,1536]{1,0:T(8,128)(2,1)S(1)}, u32[]{:S(2)}, u32[]{:S(2)}) collective-permute-start(bf16[512,1536]{1,0:T(8,128)(2,1)S(1)} %collective-permute-done.26.rows), channel_id=1, source_target_pairs={{0,4},{4,0},{8,12},{12,8},{16,20},{20,16},{24,28},{28,24},{1,5},{5... | collective-permute-start | bytes 4718600 | tf_op jit(solution)/shard_map/ppermute | solution.py:1188
  292.5 22.3 %collective-permute-start.29 = (bf16[256,1536]{1,0:T(8,128)(2,1)}, bf16[256,1536]{1,0:T(8,128)(2,1)S(1)}, u32[]{:S(2)}, u32[]{:S(2)}) collective-permute-start(bf16[256,1536]{1,0:T(8,128)(2,1)} %slice.146), channel_id=1, source_target_pairs={{0,16},{4,20},{8,24},{12,28},{16,0},{20,4},{24,8},{28,12},{1,17},{... | collective-permute-start | bytes 2359304 | tf_op jit(solution)/shard_map/ppermute | solution.py:1188
  294.1 20.8 %collective-permute-start.30 = (bf16[256,1536]{1,0:T(8,128)(2,1)S(1)}, bf16[256,1536]{1,0:T(8,128)(2,1)}, u32[]{:S(2)}, u32[]{:S(2)}) collective-permute-start(bf16[256,1536]{1,0:T(8,128)(2,1)S(1)} %slice.147), channel_id=1, source_target_pairs={{0,8},{4,12},{8,0},{12,4},{16,24},{20,28},{24,16},{28,20},{1,9},{5... | collective-permute-start | bytes 2359304 | tf_op jit(solution)/shard_map/ppermute | solution.py:1188
  370.9 309.4 %reduce-scatter.5.cloned.1.call-start = ((), (), s32[]{:S(2)}) async-start(), calls=%async_computation.3 | async-start | bytes 8847360 | tf_op jit(solution)/shard_map/reduce_scatter | solution.py:1454
  417.4 64.4 %collective-permute-start.36 = (bf16[4,512,1536]{2,1,0:T(8,128)(2,1)}, bf16[4,512,1536]{2,1,0:T(8,128)(2,1)}, u32[]{:S(2)}, u32[]{:S(2)}) collective-permute-start(bf16[4,512,1536]{2,1,0:T(8,128)(2,1)} %combine.5), channel_id=1, source_target_pairs={{0,4},{4,0},{8,12},{12,8},{16,20},{20,16},{24,28},{28,24},{1,5},{5... | collective-permute-start | bytes 18874376 | tf_op jit(solution)/shard_map/ppermute | solution.py:1188
  436.6 38.7 %collective-permute-start.38 = (bf16[2,272,1536]{2,1,0:T(8,128)(2,1)}, bf16[2,272,1536]{2,1,0:T(8,128)(2,1)S(1)}, u32[]{:S(2)}, u32[]{:S(2)}) collective-permute-start(bf16[2,272,1536]{2,1,0:T(8,128)(2,1)} %get-tuple-element.200), channel_id=1, source_target_pairs={{0,8},{4,12},{8,0},{12,4},{16,24},{20,28},{24,16},{28,20},{1,9},{5... | collective-permute-start | bytes 5013512 | tf_op jit(solution)/shard_map/ppermute | solution.py:1188
  438.1 38.3 %collective-permute-start.39 = (bf16[2,272,1536]{2,1,0:T(8,128)(2,1)}, bf16[2,272,1536]{2,1,0:T(8,128)(2,1)S(1)}, u32[]{:S(2)}, u32[]{:S(2)}) collective-permute-start(bf16[2,272,1536]{2,1,0:T(8,128)(2,1)} %get-tuple-element.201), channel_id=1, source_target_pairs={{0,16},{4,20},{8,24},{12,28},{16,0},{20,4},{24,8},{28,12},{1,17},{... | collective-permute-start | bytes 5013512 | tf_op jit(solution)/shard_map/ppermute | solution.py:1188
  481.0 19.7 %collective-permute-start.40 = (bf16[272,1536]{1,0:T(8,128)(2,1)}, bf16[272,1536]{1,0:T(8,128)(2,1)S(1)}, u32[]{:S(2)}, u32[]{:S(2)}) collective-permute-start(bf16[272,1536]{1,0:T(8,128)(2,1)} %get-tuple-element.208), channel_id=1, source_target_pairs={{0,16},{4,20},{8,24},{12,28},{16,0},{20,4},{24,8},{28,12},{1,17},{... | collective-permute-start | bytes 2506760 | tf_op jit(solution)/shard_map/ppermute | solution.py:1188
  481.2 19.7 %collective-permute-start.41 = (bf16[272,1536]{1,0:T(8,128)(2,1)}, bf16[272,1536]{1,0:T(8,128)(2,1)S(1)}, u32[]{:S(2)}, u32[]{:S(2)}) collective-permute-start(bf16[272,1536]{1,0:T(8,128)(2,1)} %get-tuple-element.209), channel_id=1, source_target_pairs={{0,8},{4,12},{8,0},{12,4},{16,24},{20,28},{24,16},{28,20},{1,9},{5... | collective-permute-start | bytes 2506760 | tf_op jit(solution)/shard_map/ppermute | solution.py:1188
  500.9 56.1 %collective-permute-start.42 = (bf16[2,256,1536]{2,1,0:T(8,128)(2,1)}, bf16[2,256,1536]{2,1,0:T(8,128)(2,1)}, u32[]{:S(2)}, u32[]{:S(2)}) collective-permute-start(bf16[2,256,1536]{2,1,0:T(8,128)(2,1)} %get-tuple-element.212), channel_id=1, source_target_pairs={{0,8},{4,12},{8,0},{12,4},{16,24},{20,28},{24,16},{28,20},{1,9},{5... | collective-permute-start | bytes 4718600 | tf_op jit(solution)/shard_map/ppermute | solution.py:1188
  501.8 55.2 %collective-permute-start.43 = (bf16[2,256,1536]{2,1,0:T(8,128)(2,1)}, bf16[2,256,1536]{2,1,0:T(8,128)(2,1)S(1)}, u32[]{:S(2)}, u32[]{:S(2)}) collective-permute-start(bf16[2,256,1536]{2,1,0:T(8,128)(2,1)} %get-tuple-element.213), channel_id=1, source_target_pairs={{0,16},{4,20},{8,24},{12,28},{16,0},{20,4},{24,8},{28,12},{1,17},{... | collective-permute-start | bytes 4718600 | tf_op jit(solution)/shard_map/ppermute | solution.py:1188
  533.7 23.4 %collective-permute-start.44 = (bf16[512,512]{1,0:T(8,128)(2,1)S(1)}, bf16[512,512]{1,0:T(8,128)(2,1)S(1)}, u32[]{:S(2)}, u32[]{:S(2)}) collective-permute-start(bf16[512,512]{1,0:T(8,128)(2,1)S(1)} %convert_element_type.141), channel_id=1, source_target_pairs={{0,1},{2,3},{4,5},{6,7},{8,9},{10,11},{12,13},{14,15},{16,17},{18,... | collective-permute-start | bytes 1572872 | tf_op jit(solution)/shard_map/ppermute | solution.py:1471
  586.4 35.1 %collective-permute-start.46 = (bf16[2,416,896]{2,1,0:T(8,128)(2,1)}, bf16[2,416,896]{2,1,0:T(8,128)(2,1)}, u32[]{:S(2)}, u32[]{:S(2)}) collective-permute-start(bf16[2,416,896]{2,1,0:T(8,128)(2,1)} %get-tuple-element.230), channel_id=1, source_target_pairs={{0,8},{4,12},{8,0},{12,4},{16,24},{20,28},{24,16},{28,20},{1,9},{5... | collective-permute-start | bytes 4472840 | tf_op jit(solution)/shard_map/ppermute | solution.py:1188
  586.8 34.7 %collective-permute-start.47 = (bf16[2,416,896]{2,1,0:T(8,128)(2,1)}, bf16[2,416,896]{2,1,0:T(8,128)(2,1)S(1)}, u32[]{:S(2)}, u32[]{:S(2)}) collective-permute-start(bf16[2,416,896]{2,1,0:T(8,128)(2,1)} %get-tuple-element.231), channel_id=1, source_target_pairs={{0,16},{4,20},{8,24},{12,28},{16,0},{20,4},{24,8},{28,12},{1,17},{... | collective-permute-start | bytes 4472840 | tf_op jit(solution)/shard_map/ppermute | solution.py:1188
  625.8 19.8 %collective-permute-start.50 = (bf16[416,896]{1,0:T(8,128)(2,1)}, bf16[416,896]{1,0:T(8,128)(2,1)S(1)}, u32[]{:S(2)}, u32[]{:S(2)}) collective-permute-start(bf16[416,896]{1,0:T(8,128)(2,1)} %get-tuple-element.244), channel_id=1, source_target_pairs={{0,16},{4,20},{8,24},{12,28},{16,0},{20,4},{24,8},{28,12},{1,17},{... | collective-permute-start | bytes 2236424 | tf_op jit(solution)/shard_map/ppermute | solution.py:1188
  627.9 19.7 %collective-permute-start.51 = (bf16[416,896]{1,0:T(8,128)(2,1)S(1)}, bf16[416,896]{1,0:T(8,128)(2,1)S(1)}, u32[]{:S(2)}, u32[]{:S(2)}) collective-permute-start(bf16[416,896]{1,0:T(8,128)(2,1)S(1)} %copy-done.52), channel_id=1, source_target_pairs={{0,8},{4,12},{8,0},{12,4},{16,24},{20,28},{24,16},{28,20},{1,9},{5... | collective-permute-start | bytes 2236424 | tf_op jit(solution)/shard_map/ppermute | solution.py:1188
  634.9 37.6 %collective-permute-start.48 = (bf16[256,1536]{1,0:T(8,128)(2,1)}, bf16[256,1536]{1,0:T(8,128)(2,1)}, u32[]{:S(2)}, u32[]{:S(2)}) collective-permute-start(bf16[256,1536]{1,0:T(8,128)(2,1)} %get-tuple-element.240), channel_id=1, source_target_pairs={{0,16},{4,20},{8,24},{12,28},{16,0},{20,4},{24,8},{28,12},{1,17},{... | collective-permute-start | bytes 2359304 | tf_op jit(solution)/shard_map/ppermute | solution.py:1188
  636.8 39.8 %collective-permute-start.49 = (bf16[256,1536]{1,0:T(8,128)(2,1)}, bf16[256,1536]{1,0:T(8,128)(2,1)}, u32[]{:S(2)}, u32[]{:S(2)}) collective-permute-start(bf16[256,1536]{1,0:T(8,128)(2,1)} %get-tuple-element.241), channel_id=1, source_target_pairs={{0,8},{4,12},{8,0},{12,4},{16,24},{20,28},{24,16},{28,20},{1,9},{5... | collective-permute-start | bytes 2359304 | tf_op jit(solution)/shard_map/ppermute | solution.py:1188
  651.3 33.7 %collective-permute-start.53 = (bf16[208,896]{1,0:T(8,128)(2,1)}, bf16[208,896]{1,0:T(8,128)(2,1)S(1)}, u32[]{:S(2)}, u32[]{:S(2)}) collective-permute-start(bf16[208,896]{1,0:T(8,128)(2,1)} %get-tuple-element.290), channel_id=1, source_target_pairs={{1,0},{2,1},{3,2},{5,4},{6,5},{7,6},{9,8},{10,9},{11,10},{13,12},{... | collective-permute-start | bytes 1118216 | tf_op jit(solution)/shard_map/ppermute | solution.py:1178
  652.8 43.9 %collective-permute-start.54 = (bf16[208,896]{1,0:T(8,128)(2,1)}, bf16[208,896]{1,0:T(8,128)(2,1)S(1)}, u32[]{:S(2)}, u32[]{:S(2)}) collective-permute-start(bf16[208,896]{1,0:T(8,128)(2,1)} %get-tuple-element.289), channel_id=1, source_target_pairs={{0,2},{1,3},{2,0},{3,1},{4,6},{5,7},{6,4},{7,5},{8,10},{9,11},{10,... | collective-permute-start | bytes 1118216 | tf_op jit(solution)/shard_map/ppermute | solution.py:1151
  668.2 28.5 %collective-permute-start.55 = (bf16[208,896]{1,0:T(8,128)(2,1)}, bf16[208,896]{1,0:T(8,128)(2,1)S(1)}, u32[]{:S(2)}, u32[]{:S(2)}) collective-permute-start(bf16[208,896]{1,0:T(8,128)(2,1)} %get-tuple-element.288), channel_id=1, source_target_pairs={{0,3},{3,0},{4,7},{7,4},{8,11},{11,8},{12,15},{15,12},{16,19},{19,... | collective-permute-start | bytes 1118216 | tf_op jit(solution)/shard_map/ppermute | solution.py:1147
  672.6 24.1 %collective-permute-start.52 = (bf16[208,896]{1,0:T(8,128)(2,1)}, bf16[208,896]{1,0:T(8,128)(2,1)}, u32[]{:S(2)}, u32[]{:S(2)}) collective-permute-start(bf16[208,896]{1,0:T(8,128)(2,1)} %broadcast_select_fusion), channel_id=1, source_target_pairs={{0,1},{1,2},{2,3},{4,5},{5,6},{6,7},{8,9},{9,10},{10,11},{12,13},{... | collective-permute-start | bytes 1118216 | tf_op jit(solution)/shard_map/ppermute | solution.py:1177
  (65 other events, 578.2 us)
Sparse Core Ops, SparseCore 0:
  215.4 127.2 all-gather.2
  371.1 121.2 reduce-scatter.2
  503.7 129.6 reduce-scatter.4

commit v14 on v12

--- a/solution.py
+++ b/solution.py
@@ -1169,15 +1169,23 @@
     ]
 
 
-def reduce_slots(slots):
+def reduce_slots(slots, *earlier):
     place = lax.axis_index("cols")
     own, second, third, fourth = slots
+    end = (place == 0) | (place == 3)
+    relay = lax.ppermute(second, "cols", [(1, 3), (0, 1), (2, 0), (3, 2)])
+    relayed = relay.astype(WIDE)
+    upward_load = (
+        jnp.where(place == 0, third, fourth).astype(WIDE) + jnp.where(place == 1, relayed, 0.0)
+    ).astype(LOW)
+    downward_load = (third.astype(WIDE) + jnp.where(place == 2, relayed, 0.0)).astype(LOW)
     arrived = (
-        lax.ppermute(jnp.where(place == 0, third, fourth), "cols", UP),
-        lax.ppermute(third, "cols", DOWN),
-        send_over(second),
-        send_far(fourth),
+        lax.ppermute(upward_load, "cols", UP),
+        lax.ppermute(downward_load, "cols", DOWN),
+        send_far(after(fourth, upward_load, downward_load)),
+        jnp.where(end, relay, jnp.zeros_like(relay)),
     )
+    arrived = after(arrived, *earlier)
     return own.astype(WIDE) + sum(block.astype(WIDE) for block in arrived)
 
 
@@ -1291,7 +1299,7 @@
         pair_in = flip(jnp.concatenate([beside, across], axis=0), 1)
         corner_in = [flip(piece, 1) for piece in corner]
         grad_in = after(cotangent, *corner)
-        grad_flips = (flip(grad_in, 2), flip(grad_in, 4))
+        grad_flips = [flip(grad_in, 2), flip(grad_in, 4)]
         pieces = [own, own_in, beside, across, *corner, pair_in, *corner_in]
         at = depth + router_part + 1
         near_slots = [own, own_in, beside, pair_in, across, pair_in[4:], corner[0], corner_in[0]]
@@ -1339,17 +1347,24 @@
     normed, own_pair = key_value(info, tokens_in, attention_scale, cosine, sine, pair_refs)
     pairs = [(i + 1, i) for i in range(0, col_count, 2)]
     partner = lax.ppermute(own_pair, "cols", pairs)
-    queries = query(info, normed, cosine, sine, query_refs)
+    if fast:
+        own_grad_in = flip(grad_in, 1)
+        normed_in = after(normed, own_grad_in)
+    else:
+        normed_in = normed
+    queries = query(info, normed_in, cosine, sine, query_refs)
     if fast:
         first_far = send_far(after(first_block, partner, queries))
         expert_refs.append([first_block, first_second, *first_near, first_far])
+    if fast:
         grad_flips = after(grad_flips, queries)
         grad_corner = turn_corner(*grad_flips)
     heads = attention(info, queries, own_pair, partner)
     if fast:
-        heads = after(heads, grad_corner)
-        grad_near = [cotangent, *grad_flips, grad_corner]
-        grad_blocks = [block for one in grad_near for block in (one, flip(one, 1))]
+        grad_near = [*grad_flips, grad_corner]
+        grad_blocks = [cotangent, own_grad_in]
+        grad_blocks += [block for one in grad_near for block in (one, flip(one, 1))]
+        heads = after(heads, grad_corner, grad_blocks[3], grad_blocks[5])
     else:
         grad_all = lax.all_gather(cotangent, "rows", axis=0)
         grad_blocks = [grad_all[q] for q in range(row_count)]
@@ -1357,7 +1372,7 @@
 
     if fast:
         beside, across = flip(normed_two, 2), flip(normed_two, 4)
-        beside_in = flip(normed_two, 1)
+        beside_in = flip(after(normed_two, *grad_blocks), 1)
         later_block = after(shard_blocks[1], first_far, normed_two)
         expert_refs.append([lax.all_gather(later_block, "cols", axis=0)])
     else:
@@ -1373,9 +1388,9 @@
     if fast:
         half = TOK_DEV // 2
         picked = place_block(0, normed_two, None)
-        picked = place_block(1, beside_in, picked)
         beside, across = after((beside, across), picked, *grad_rows)
         corner = [flip(beside[:half], 4), flip(across[half:], 2)]
+        picked = place_block(1, beside_in, picked)
         picked = place_block(2, beside, picked)
         picked = place_block(4, across, picked)
         beside_in = flip(beside, 1)
@@ -1447,6 +1462,8 @@
     )
     if fast:
         out_flips = send_chips(after(out_first[:2], back_parts[2], back_parts[5]))
+        slots = after(slots, reduced[0], back_parts[2])
+        reduced.append(lax.psum_scatter(slots, "cols", scatter_dimension=0, tiled=False))
         router_parts = jnp.transpose(
             router_grad.astype(LOW).reshape(col_count, router_part, row_count, depth),
             (2, 0, 1, 3),
@@ -1466,34 +1483,38 @@
     arrived = lax.ppermute(source_grad.astype(LOW), "cols", [(j, i) for i, j in pairs])
     if fast:
         parts = ((0, 2, 0, query_part), (1, 3, query_part + 2 * key_part, query_part))
-        slots = after(slots, reduced[0], grad_query)
-        reduced.append(lax.psum_scatter(slots, "cols", scatter_dimension=0, tiled=False))
-        out_flips = after(out_flips, grad_query)
-        near_x, near_y = out_first[2:]
-        for_y, for_x = corner_adds(near_x, out_flips[0], near_y, out_flips[1])
-        mixture = (near_x, out_flips[0], flip(for_y, 4))
-        mixture += (near_y, out_flips[1], flip(for_x, 2))
-        grad_branch = after(grad_branch, for_y)
         keep_send = weight_grads(
             info, [normed, heads], [grad_query, grad_branch], parts, extra
         )
-        arrived = after(arrived, *keep_send, mixture[2], mixture[5])
+        arrived = after(arrived, *keep_send, *out_flips)
     grad_pair = join_grads(info, own_grad, source_grad, arrived, cosine, sine)
     if fast:
         keep, send = weight_grads(
             info, [normed], [grad_pair], ((0, 1, 0, 2 * key_part),), None, keep_send
         )
+        flat = (4, col_count * (depth + EXTRA), wide)
         sent = flip(send, 1)
-        grad_pair = after(grad_pair, keep)
+        sent_first = chip_adds(keep.reshape(flat), sent.reshape(flat))
+        sent_chips = send_chips(sent_first[:2])
+        grad_pair = after(grad_pair, sent_first[0])
     tokens_grad, attention_gain_grad = token_back(
         info, grad_query, grad_pair, tokens, grad_residual, attention_scale, query_refs, pair_refs
     )
 
     if fast:
-        flat = (4, col_count * (depth + EXTRA), wide)
-        sent_first = chip_adds(keep.reshape(flat), sent.reshape(flat))
-        sent_chips = after(send_chips(sent_first[:2]), tokens_grad)
-        slots = sum_parts(chips_second(*sent_first[2:], *sent_chips))
+        sent_chips = after(sent_chips, tokens_grad)
+        sent_parts = chips_second(*sent_first[2:], *sent_chips)
+        near_x, near_y = out_first[2:]
+        mixture = chips_second(near_x, near_y, *after(out_flips, *sent_chips))
+    layer_output = (residual + sum_parts(mixture)).astype(LOW)
+    part = down_weight.shape[1]
+    expert_sums = [block.astype(WIDE) for block in reduced]
+    gate_grad, upward_grad, down_grad = (
+        jnp.stack([sums_of[which * part : (which + 1) * part] for sums_of in expert_sums])
+        for which in range(3)
+    )
+    if fast:
+        slots = sum_parts(sent_parts)
         slots = slots.reshape(col_count, depth + EXTRA, wide)
         width = query_part + 2 * key_part
         own_slots = own
@@ -1509,7 +1530,7 @@
         )
         slots = after((slots + gain_sums).astype(LOW), reduced[1])
 
-        sums = reduce_slots(slots)
+        sums = reduce_slots(slots, gate_grad, upward_grad, down_grad, layer_output)
         router_sum = sums[depth : depth + router_part, :depth].T
         experts_gain_sum = sums[depth + router_part, :gain_part]
         attention_gain_sum = sums[depth + router_part + 1, :gain_part]
@@ -1548,16 +1569,9 @@
         experts_gain_sum = small_sums[gain_part : 2 * gain_part]
         router_sum = small_sums[2 * gain_part :].reshape(depth, router_part)
 
-    layer_output = (residual + sum_parts(mixture)).astype(LOW)
     key_at = query_part
     value_at = key_at + key_part
     out_at = value_at + key_part
-    part = down_weight.shape[1]
-    expert_sums = [block.astype(WIDE) for block in reduced]
-    gate_grad, upward_grad, down_grad = (
-        jnp.stack([sums_of[which * part : (which + 1) * part] for sums_of in expert_sums])
-        for which in range(3)
-    )
     return (
         layer_output,
         tokens_grad,

time: 694 us -> 693 us (level)
  waiting for transfers between devices: 200 us -> 186 us
  local copies, waits for them, and re-layouts: 49.7 us -> 57.8 us
    ppermute x2 -> x1, waiting for transfers between devices: 24.3 us -> 0.01 us  [send_over(): return lax.ppermute(block, 'cols', [(0, 2), (1, 3), (2, 0), (3, 1)])]
    ppermute x2 -> x1, starting transfers between devices: 14.4 us -> 0.69 us  [send_over(): return lax.ppermute(block, 'cols', [(0, 2), (1, 3), (2, 0), (3, 1)])]
    ppermute x3, starting transfers between devices: 10.5 us -> 20.1 us  [send_far(): return lax.ppermute(block, 'cols', FAR)]
    unnamed x141 -> x125, local copies, waits for them, and re-layouts: 26.2 us -> 30.2 us
  transfers between devices with their start and end apart: 56 -> 56, of which waited for: 31 -> 25; matrix products, arithmetic and copies ran while one was open for 7% -> 8% of each run, Pallas kernels for 43% -> 43%
where the time goes in v14:
time: 693 us; the launch traced here: 683 us
  Pallas kernels  297 us (43%)
  waiting for transfers between devices  186 us (27%)
  starting transfers between devices  91.6 us (13%)
  local copies, waits for them, and re-layouts  57.8 us (8%)
  other arithmetic  36.5 us (5%)
  between operations  14.8 us (2%)
    ppermute x39, waiting for transfers between devices, flip(): return lax.ppermute(block, 'rows', [(i, i ^ bit) for i in range(count)])  137 us
    pallas_call x2, Pallas kernels, expert(): pl.pallas_call(functools.partial(expert_kernel, slots), grid=(height // E...  61 us
    pallas_call x4, Pallas kernels, combine(): pl.pallas_call(functools.partial(combine_kernel, local, first, step), out...  30.9 us
    unnamed x125, local copies, waits for them, and re-layouts  30.2 us
    pallas_call x2, Pallas kernels, expert_grads(): pl.pallas_call(expert_grads_kernel, grid=(D // 256,), out_shape=jax.Shape...  29.2 us
    pallas_call x8, Pallas kernels, dispatch(): pl.pallas_call(functools.partial(dispatch_kernel, local), grid=(D // wide...  29.1 us
    ppermute x4, starting transfers between devices, send_near(): return (lax.ppermute(block, 'cols', DOWN), lax.ppermute(block, 'cols', UP))  28 us
    ppermute x39, starting transfers between devices, flip(): return lax.ppermute(block, 'rows', [(i, i ^ bit) for i in range(count)])  27.8 us
  transfers between devices with their start and end apart: 56, of which 25 were waited for; matrix products, arithmetic and copies ran while one was open for 8% of the time, Pallas kernels for 43%

profile of v14, /device:TPU:0, one launch (start us, length us, event | category | flops | bytes accessed | tf_op | source)
XLA Modules:
  0.0 683.4 jit_solution(9745187180239461705)
XLA Ops:
  14.1 6.3 collective-permute-start.1
  20.4 3.8 collective-permute-start.6
  32.6 19.0 %collective-permute-start.3 = (bf16[576,1536]{1,0:T(8,128)(2,1)S(1)}, bf16[576,1536]{1,0:T(8,128)(2,1)}, u32[]{:S(2)}, u32[]{:S(2)}) collective-permute-start(bf16[576,1536]{1,0:T(8,128)(2,1)S(1)} %pad_maximum_fusion.5.rest_0_), channel_id=1, source_target_pairs={{0,1},{1,2},{2,3},{4,5},{5,6},{6,7},{8,9},{9,10},{10,11},{12,13},{... | collective-permute-start | bytes 5308424 | tf_op jit(solution)/shard_map/ppermute | solution.py:1142
  57.4 31.8 %collective-permute-done.8.rest_2_.rest_8_.rest_11_ = bf16[4,208,896]{2,1,0:T(8,128)(2,1)S(1)} collective-permute-done((bf16[4,208,896]{2,1,0:T(8,128)(2,1)S(1)}, bf16[4,208,896]{2,1,0:T(8,128)(2,1)S(1)}, u32[]{:S(2)}, u32[]{:S(2)}) %collective-permute-start.8) | collective-permute-done | bytes 1490976 | tf_op jit(solution)/shard_map/ppermute | solution.py:1194
  104.0 9.6 %collective-permute-done.11.rest_4_.rest_10_.rest_13_ = bf16[2,208,896]{2,1,0:T(8,128)(2,1)} collective-permute-done((bf16[2,208,896]{2,1,0:T(8,128)(2,1)}, bf16[2,208,896]{2,1,0:T(8,128)(2,1)}, u32[]{:S(2)}, u32[]{:S(2)}) %collective-permute-start.11) | collective-permute-done | bytes 745504 | tf_op jit(solution)/shard_map/ppermute | solution.py:1194
  120.9 5.6 route_tables.1
  131.9 10.5 %collective-permute-done.4.rest_1_ = bf16[576,1536]{1,0:T(8,128)(2,1)} collective-permute-done((bf16[576,1536]{1,0:T(8,128)(2,1)}, bf16[576,1536]{1,0:T(8,128)(2,1)}, u32[]{:S(2)}, u32[]{:S(2)}) %collective-permute-start.4) | collective-permute-done | bytes 1769504 | tf_op jit(solution)/shard_map/ppermute | solution.py:1157
  142.4 5.0 norm_key_value.1
  148.7 8.3 %query_projection.1.queries = bf16[512,1536]{1,0:T(8,128)(2,1)} custom-call(s32[16]{0:T(128)} %concatenate.42.info, bf16[512,1536]{1,0:T(8,128)(2,1)} %get-tuple-element.142.normed.rest_0_, f32[512,128]{1,0:T(8,128)} %get-tuple-element.319.cosine, f32[512,128]{1,0:T(8,128)} %get-tuple-element.320.sine, bf16[4,208,896]{2,1,0:T(8,128)(2,1)} %copy-done.1, ...), custom_call_target="tpu_custom_call" | custom-call | flops 1 | bytes 1 | tf_op jit(solution)/shard_map/query_projection/pallas_call | solution.py:195
  157.0 6.3 collective-permute-done.16.partner
  163.3 3.6 collective-permute-start.32
  175.6 11.0 %tree_attention.1.heads.rest_1_ = bf16[512,1536]{1,0:T(8,128)(2,1)} custom-call(s32[16]{0:T(128)} %concatenate.42.info, bf16[512,1536]{1,0:T(8,128)(2,1)} %query_projection.1.queries, bf16[512,512]{1,0:T(8,128)(2,1)} %get-tuple-element.143.own, bf16[512,512]{1,0:T(8,128)(2,1)} %copy-done.36), custom_call_target="tpu_custom_call" | custom-call | flops 1 | bytes 1 | tf_op jit(solution)/shard_map/tree_attention/pallas_call | solution.py:277
  192.6 9.8 %out_projection.1 = (f32[512,1536]{1,0:T(8,128)}, bf16[512,1536]{1,0:T(8,128)(2,1)}) custom-call(s32[16]{0:T(128)} %concatenate.42.info, bf16[512,1536]{1,0:T(8,128)(2,1)} %tree_attention.1.heads.rest_1_, bf16[512,1536]{1,0:T(8,128)(2,1)} %tokens.4, f32[1,1536]{1,0:T(1,128)} %reshape.305.gain, bf16[4,208,896]{2,1,0:T(8,128)(2,1)} %copy-done.1, ...), custom_call_target="tpu_custom_call" | custom-call | flops 1 | bytes 1 | tf_op jit(solution)/shard_map/out_projection/pallas_call | solution.py:389
  202.5 4.0 collective-permute-done.32.rest_4_
  211.7 4.0 dispatch.8
  215.8 9.3 %pick_rows.1 = (bf16[8,160,1536]{2,1,0:T(8,128)(2,1)}, bf16[8,160,1536]{2,1,0:T(8,128)(2,1)}) custom-call(bf16[8,320,512]{2,1,0:T(8,128)(2,1)} %get-tuple-element.138.chosen, bf16[512,1536]{1,0:T(8,128)(2,1)} %cotangent.1, bf16[512,1536]{1,0:T(8,128)(2,1)} %collective-permute-done.15.rest_1_, bf16[512,1536]{1,0:T(8,128)(2,1)} %collective-permute-done.17.rest_2_, ...), custom_call_target="tpu_custom_call" | custom-call | flops 1 | bytes 1 | tf_op jit(solution)/shard_map/pick_rows/pallas_call | solution.py:480
  225.1 18.4 %collective-permute-done.23.rows = bf16[512,1536]{1,0:T(8,128)(2,1)} collective-permute-done((bf16[512,1536]{1,0:T(8,128)(2,1)S(1)}, bf16[512,1536]{1,0:T(8,128)(2,1)}, u32[]{:S(2)}, u32[]{:S(2)}) %collective-permute-start.23) | collective-permute-done | bytes 1572896 | tf_op jit(solution)/shard_map/ppermute | solution.py:1194
  248.4 3.6 dispatch.9
  260.3 3.6 dispatch.12
  275.7 3.6 dispatch.15
  279.3 30.7 %expert.2 = (bf16[1280,1536]{1,0:T(8,128)(2,1)}, bf16[1280,1536]{1,0:T(8,128)(2,1)}, bf16[1280,1536]{1,0:T(8,128)(2,1)}, bf16[4,576,1280]{2,1,0:T(8,128)(2,1)}, f32[1280,1]{1,0:T(8,128)}) custom-call(s32[16]{0:T(128)} %concatenate.42.info, bf16[1280,1536]{1,0:T(8,128)(2,1)} %bitcast.150, bf16[1280,1536]{1,0:T(8,128)(2,1)} %bitcast.169, f32[1280,1]{1,0:T(8,128)} %bitcast.154, ...), custom_call_target="tpu_custom_call" | custom-call | flops 1 | bytes 1 | tf_op jit(solution)/shard_map/expert/pallas_call | solution.py:670
  310.1 14.6 %expert_gradients.2 = bf16[4,576,1536]{2,1,0:T(8,128)(2,1)} custom-call(bf16[4,576,1280]{2,1,0:T(8,128)(2,1)} %get-tuple-element.189.acts, bf16[1280,1536]{1,0:T(8,128)(2,1)} %bitcast.151, bf16[1280,1536]{1,0:T(8,128)(2,1)} %get-tuple-element.190.grads), custom_call_target="tpu_custom_call" | custom-call | flops 1 | bytes 1 | tf_op jit(solution)/shard_map/expert_gradients/pallas_call | solution.py:699
  324.7 7.5 %all-gather.3.cloned.1.call-done = bf16[2304,1536]{1,0:T(8,128)(2,1)} async-done(((bf16[576,1536]{1,0:T(8,128)(2,1)}), bf16[2304,1536]{1,0:T(8,128)(2,1)}) %all-gather.3.cloned.1.call-update) | async-done | bytes 7077904 | tf_op jit(solution)/shard_map/all_gather | solution.py:1377
  332.2 30.3 %expert.3 = (bf16[1280,1536]{1,0:T(8,128)(2,1)}, bf16[1280,1536]{1,0:T(8,128)(2,1)}, bf16[1280,1536]{1,0:T(8,128)(2,1)}, bf16[4,576,1280]{2,1,0:T(8,128)(2,1)}, f32[1280,1]{1,0:T(8,128)}) custom-call(s32[16]{0:T(128)} %concatenate.42.info, bf16[1280,1536]{1,0:T(8,128)(2,1)} %bitcast.152, bf16[1280,1536]{1,0:T(8,128)(2,1)} %bitcast.170, f32[1280,1]{1,0:T(8,128)} %bitcast.155, ...), custom_call_target="tpu_custom_call" | custom-call | flops 1 | bytes 1 | tf_op jit(solution)/shard_map/expert/pallas_call | solution.py:670
  362.4 8.0 %combine.7 = bf16[4,544,1536]{2,1,0:T(8,128)(2,1)} custom-call(s32[16]{0:T(128)} %concatenate.42.info, bf16[8,320,512]{2,1,0:T(8,128)(2,1)} %get-tuple-element.138.chosen, bf16[8,160,1536]{2,1,0:T(8,128)(2,1)} %bitcast.161, bf16[8,160,1536]{2,1,0:T(8,128)(2,1)} %bitcast.165, f32[8,160,1]{2,1,0:T(8,128)} %bitcast.171, f32[8,160,1]{2,1,0:T(8,128)} %bitcast.173), custom_call_target="tpu_custom_call" | custom-call | flops 1 | bytes 1 | tf_op jit(solution)/shard_map/combine/pallas_call | solution.py:762
  370.6 7.3 %combine.5 = bf16[4,512,1536]{2,1,0:T(8,128)(2,1)} custom-call(s32[16]{0:T(128)} %concatenate.42.info, bf16[8,320,512]{2,1,0:T(8,128)(2,1)} %get-tuple-element.138.chosen, bf16[8,160,1536]{2,1,0:T(8,128)(2,1)} %bitcast.159, bf16[8,160,1536]{2,1,0:T(8,128)(2,1)} %bitcast.163), custom_call_target="tpu_custom_call" | custom-call | flops 1 | bytes 1 | tf_op jit(solution)/shard_map/combine/pallas_call | solution.py:762
  378.4 8.1 %combine.6.keep = bf16[4,544,1536]{2,1,0:T(8,128)(2,1)} custom-call(s32[16]{0:T(128)} %concatenate.42.info, bf16[8,320,512]{2,1,0:T(8,128)(2,1)} %get-tuple-element.138.chosen, bf16[8,160,1536]{2,1,0:T(8,128)(2,1)} %bitcast.162, bf16[8,160,1536]{2,1,0:T(8,128)(2,1)} %bitcast.166, f32[8,160,1]{2,1,0:T(8,128)} %bitcast.172, f32[8,160,1]{2,1,0:T(8,128)} %bitcast.174), custom_call_target="tpu_custom_call" | custom-call | flops 1 | bytes 1 | tf_op jit(solution)/shard_map/combine/pallas_call | solution.py:762
  389.3 7.8 %chip_sums.4 = (bf16[2,272,1536]{2,1,0:T(8,128)(2,1)}, bf16[2,272,1536]{2,1,0:T(8,128)(2,1)}, bf16[2,272,1536]{2,1,0:T(8,128)(2,1)}, bf16[2,272,1536]{2,1,0:T(8,128)(2,1)}) custom-call(bf16[4,544,1536]{2,1,0:T(8,128)(2,1)} %combine.6.keep, bf16[4,544,1536]{2,1,0:T(8,128)(2,1)} %copy-done.14), custom_call_target="tpu_custom_call" | custom-call | flops 1 | bytes 1 | tf_op jit(solution)/shard_map/chip_sums/pallas_call | solution.py:811
  400.0 7.5 %combine.4.keep = bf16[4,512,1536]{2,1,0:T(8,128)(2,1)} custom-call(s32[16]{0:T(128)} %concatenate.42.info, bf16[8,320,512]{2,1,0:T(8,128)(2,1)} %get-tuple-element.138.chosen, bf16[8,160,1536]{2,1,0:T(8,128)(2,1)} %bitcast.160, bf16[8,160,1536]{2,1,0:T(8,128)(2,1)} %bitcast.164), custom_call_target="tpu_custom_call" | custom-call | flops 1 | bytes 1 | tf_op jit(solution)/shard_map/combine/pallas_call | solution.py:762
  407.6 14.6 %expert_gradients.3 = bf16[4,576,1536]{2,1,0:T(8,128)(2,1)} custom-call(bf16[4,576,1280]{2,1,0:T(8,128)(2,1)} %get-tuple-element.206.acts, bf16[1280,1536]{1,0:T(8,128)(2,1)} %bitcast.153, bf16[1280,1536]{1,0:T(8,128)(2,1)} %get-tuple-element.207.grads), custom_call_target="tpu_custom_call" | custom-call | flops 1 | bytes 1 | tf_op jit(solution)/shard_map/expert_gradients/pallas_call | solution.py:699
  422.2 13.6 %collective-permute-done.35.got_x.rest_1_ = bf16[2,272,1536]{2,1,0:T(8,128)(2,1)S(1)} collective-permute-done((bf16[2,272,1536]{2,1,0:T(8,128)(2,1)}, bf16[2,272,1536]{2,1,0:T(8,128)(2,1)S(1)}, u32[]{:S(2)}, u32[]{:S(2)}) %collective-permute-start.35) | collective-permute-done | bytes 1671200 | tf_op jit(solution)/shard_map/ppermute | solution.py:1194
  443.7 7.5 %chip_sums.3 = (bf16[2,256,1536]{2,1,0:T(8,128)(2,1)}, bf16[2,256,1536]{2,1,0:T(8,128)(2,1)}, bf16[2,256,1536]{2,1,0:T(8,128)(2,1)}, bf16[2,256,1536]{2,1,0:T(8,128)(2,1)}) custom-call(bf16[4,512,1536]{2,1,0:T(8,128)(2,1)} %combine.4.keep, bf16[4,512,1536]{2,1,0:T(8,128)(2,1)} %collective-permute-done.33.got), custom_call_target="tpu_custom_call" | custom-call | flops 1 | bytes 1 | tf_op jit(solution)/shard_map/chip_sums/pallas_call | solution.py:811
  451.3 9.9 %collective-permute-done.37.rest_2_ = bf16[272,1536]{1,0:T(8,128)(2,1)S(1)} collective-permute-done((bf16[272,1536]{1,0:T(8,128)(2,1)}, bf16[272,1536]{1,0:T(8,128)(2,1)S(1)}, u32[]{:S(2)}, u32[]{:S(2)}) %collective-permute-start.37) | collective-permute-done | bytes 835616 | tf_op jit(solution)/shard_map/ppermute | solution.py:1194
  465.0 12.7 %experts_norm_back.1 = (f32[512,1536]{1,0:T(8,128)}, bf16[512,1536]{1,0:T(8,128)(2,1)}, bf16[512,1536]{1,0:T(8,128)(2,1)}, f32[1,1536]{1,0:T(1,128)}, f32[16,1536]{1,0:T(8,128)}) custom-call(s32[16]{0:T(128)} %concatenate.42.info, f32[512,1536]{1,0:T(8,128)} %get-tuple-element.147.residual, bf16[512,1536]{1,0:T(8,128)(2,1)} %get-tuple-element.157.rows.normed, ...), custom_call_target="tpu_custom_call" | custom-call | flops 1 | bytes 1 | tf_op jit(solution)/shard_map/experts_norm_back/pallas_call | solution.py:922
  477.8 15.4 %tree_attention_back.1 = (bf16[512,1536]{1,0:T(8,128)(2,1)}, f32[512,512]{1,0:T(8,128)}, f32[512,512]{1,0:T(8,128)}) custom-call(s32[16]{0:T(128)} %concatenate.42.info, bf16[512,1536]{1,0:T(8,128)(2,1)} %query_projection.1.queries, bf16[512,512]{1,0:T(8,128)(2,1)} %get-tuple-element.143.own, bf16[512,512]{1,0:T(8,128)(2,1)} %copy-done.36, ...), custom_call_target="tpu_custom_call" | custom-call | flops 1 | bytes 1 | tf_op jit(solution)/shard_map/tree_attention_back/pallas_call | solution.py:338
  497.3 13.7 %weight_gradients.2 = (bf16[4,4,208,896]{3,2,1,0:T(8,128)(2,1)}, bf16[4,4,208,896]{3,2,1,0:T(8,128)(2,1)}) custom-call(s32[16]{0:T(128)} %concatenate.42.info, bf16[512,1536]{1,0:T(8,128)(2,1)} %get-tuple-element.142.normed.rest_0_, bf16[512,1536]{1,0:T(8,128)(2,1)} %tree_attention.1.heads.rest_1_, bf16[512,1536]{1,0:T(8,128)(2,1)} %get-tuple-element.224.rest_2_.grad_query, ...), custom_call_target="tpu_custom_call" | custom-call | flops 1 | bytes 1 | tf_op jit(solution)/shard_map/weight_gradients/pallas_call | solution.py:1087
  511.0 7.1 %collective-permute-done.41.arrived = bf16[512,512]{1,0:T(8,128)(2,1)S(1)} collective-permute-done((bf16[512,512]{1,0:T(8,128)(2,1)S(1)}, bf16[512,512]{1,0:T(8,128)(2,1)S(1)}, u32[]{:S(2)}, u32[]{:S(2)}) %collective-permute-start.41) | collective-permute-done | bytes 524320 | tf_op jit(solution)/shard_map/ppermute | solution.py:1483
  522.0 5.7 weight_gradients.3
  527.7 9.9 %collective-permute-done.42 = bf16[4,4,208,896]{3,2,1,0:T(8,128)(2,1)S(1)} collective-permute-done((bf16[4,4,208,896]{3,2,1,0:T(8,128)(2,1)}, bf16[4,4,208,896]{3,2,1,0:T(8,128)(2,1)S(1)}, u32[]{:S(2)}, u32[]{:S(2)}) %collective-permute-start.42) | collective-permute-done | bytes 5963808 | tf_op jit(solution)/shard_map/ppermute | solution.py:1194
  540.2 7.2 %chip_sums.5 = (bf16[2,416,896]{2,1,0:T(8,128)(2,1)}, bf16[2,416,896]{2,1,0:T(8,128)(2,1)}, bf16[2,416,896]{2,1,0:T(8,128)(2,1)}, bf16[2,416,896]{2,1,0:T(8,128)(2,1)}) custom-call(bf16[4,832,896]{2,1,0:T(8,128)(2,1)} %bitcast.156, bf16[4,832,896]{2,1,0:T(8,128)(2,1)} %bitcast.168), custom_call_target="tpu_custom_call" | custom-call | flops 1 | bytes 1 | tf_op jit(solution)/shard_map/chip_sums/pallas_call | solution.py:811
  551.1 12.4 %token_gradient.1 = (bf16[512,1536]{1,0:T(8,128)(2,1)}, f32[1,1536]{1,0:T(1,128)}) custom-call(s32[16]{0:T(128)} %concatenate.42.info, bf16[512,1536]{1,0:T(8,128)(2,1)} %get-tuple-element.224.rest_2_.grad_query, bf16[512,512]{1,0:T(8,128)(2,1)} %join_key_value_gradients.1.rest_1_.grad_pair, bf16[512,1536]{1,0:T(8,128)(2,1)} %tokens.4, ...), custom_call_target="tpu_custom_call" | custom-call | flops 1 | bytes 1 | tf_op jit(solution)/shard_map/token_gradient/pallas_call | solution.py:1013
  563.5 19.0 %collective-permute-done.43.got_x = bf16[2,416,896]{2,1,0:T(8,128)(2,1)} collective-permute-done((bf16[2,416,896]{2,1,0:T(8,128)(2,1)}, bf16[2,416,896]{2,1,0:T(8,128)(2,1)}, u32[]{:S(2)}, u32[]{:S(2)}) %collective-permute-start.43) | collective-permute-done | bytes 1490976 | tf_op jit(solution)/shard_map/ppermute | solution.py:1194
  597.9 8.6 %collective-permute-done.47 = bf16[416,896]{1,0:T(8,128)(2,1)S(1)} collective-permute-done((bf16[416,896]{1,0:T(8,128)(2,1)}, bf16[416,896]{1,0:T(8,128)(2,1)S(1)}, u32[]{:S(2)}, u32[]{:S(2)}) %collective-permute-start.47) | collective-permute-done | bytes 745504 | tf_op jit(solution)/shard_map/ppermute | solution.py:1194
  615.7 6.0 collective-permute-done.45
  627.4 6.6 collective-permute-done.49
  635.1 4.9 collective-permute-start.50
  641.4 12.7 %collective-permute-start.52 = (bf16[208,896]{1,0:T(8,128)(2,1)}, bf16[208,896]{1,0:T(8,128)(2,1)}, u32[]{:S(2)}, u32[]{:S(2)}) collective-permute-start(bf16[208,896]{1,0:T(8,128)(2,1)} %get-tuple-element.251), channel_id=1, source_target_pairs={{0,3},{3,0},{4,7},{7,4},{8,11},{11,8},{12,15},{15,12},{16,19},{19,... | collective-permute-start | bytes 1118216 | tf_op jit(solution)/shard_map/ppermute | solution.py:1146
  659.6 6.3 collective-permute-done.52
  (313 shorter events, 176.1 us)
Async XLA Ops:
  7.2 325.0 %all-gather.3.cloned.1.call-start = ((), (), s32[]{:S(2)}) async-start(), calls=%async_computation.4 | async-start | bytes 8847360 | tf_op jit(solution)/shard_map/all_gather | solution.py:1377
  12.7 18.7 %collective-permute-start = (bf16[208,896]{1,0:T(8,128)(2,1)S(1)}, bf16[208,896]{1,0:T(8,128)(2,1)}, u32[]{:S(2)}, u32[]{:S(2)}) collective-permute-start(bf16[208,896]{1,0:T(8,128)(2,1)S(1)} %concatenate.46), channel_id=1, source_target_pairs={{1,0},{2,1},{3,2},{5,4},{6,5},{7,6},{9,8},{10,9},{11,10},{13,12},{... | collective-permute-start | bytes 1118216 | tf_op jit(solution)/shard_map/ppermute | solution.py:1142
  14.1 17.3 %collective-permute-start.1 = (bf16[208,896]{1,0:T(8,128)(2,1)S(1)}, bf16[208,896]{1,0:T(8,128)(2,1)}, u32[]{:S(2)}, u32[]{:S(2)}) collective-permute-start(bf16[208,896]{1,0:T(8,128)(2,1)S(1)} %concatenate.46), channel_id=1, source_target_pairs={{0,1},{1,2},{2,3},{4,5},{5,6},{6,7},{8,9},{9,10},{10,11},{12,13},{... | collective-permute-start | bytes 1118216 | tf_op jit(solution)/shard_map/ppermute | solution.py:1142
  20.4 31.3 %collective-permute-start.6 = (bf16[208,896]{1,0:T(8,128)(2,1)S(1)}, bf16[208,896]{1,0:T(8,128)(2,1)}, u32[]{:S(2)}, u32[]{:S(2)}) collective-permute-start(bf16[208,896]{1,0:T(8,128)(2,1)S(1)} %concatenate.46), channel_id=1, source_target_pairs={{0,3},{3,0},{4,7},{7,4},{8,11},{11,8},{12,15},{15,12},{16,19},{19,... | collective-permute-start | bytes 1118216 | tf_op jit(solution)/shard_map/ppermute | solution.py:1146
  24.2 28.7 %collective-permute-start.5 = (bf16[208,896]{1,0:T(8,128)(2,1)S(1)}, bf16[208,896]{1,0:T(8,128)(2,1)}, u32[]{:S(2)}, u32[]{:S(2)}) collective-permute-start(bf16[208,896]{1,0:T(8,128)(2,1)S(1)} %concatenate.46), channel_id=1, source_target_pairs={{0,2},{1,3},{2,0},{3,1},{4,6},{5,7},{6,4},{7,5},{8,10},{9,11},{10,... | collective-permute-start | bytes 1118216 | tf_op jit(solution)/shard_map/ppermute | solution.py:1150
  31.3 58.8 %collective-permute-start.2 = (bf16[576,1536]{1,0:T(8,128)(2,1)S(1)}, bf16[576,1536]{1,0:T(8,128)(2,1)S(1)}, u32[]{:S(2)}, u32[]{:S(2)}) collective-permute-start(bf16[576,1536]{1,0:T(8,128)(2,1)S(1)} %pad_maximum_fusion.5.rest_0_), channel_id=1, source_target_pairs={{1,0},{2,1},{3,2},{5,4},{6,5},{7,6},{9,8},{10,9},{11,10},{13,12},{... | collective-permute-start | bytes 5308424 | tf_op jit(solution)/shard_map/ppermute | solution.py:1142
  32.6 58.7 %collective-permute-start.3 = (bf16[576,1536]{1,0:T(8,128)(2,1)S(1)}, bf16[576,1536]{1,0:T(8,128)(2,1)}, u32[]{:S(2)}, u32[]{:S(2)}) collective-permute-start(bf16[576,1536]{1,0:T(8,128)(2,1)S(1)} %pad_maximum_fusion.5.rest_0_), channel_id=1, source_target_pairs={{0,1},{1,2},{2,3},{4,5},{5,6},{6,7},{8,9},{9,10},{10,11},{12,13},{... | collective-permute-start | bytes 5308424 | tf_op jit(solution)/shard_map/ppermute | solution.py:1142
  54.1 35.1 %collective-permute-start.8 = (bf16[4,208,896]{2,1,0:T(8,128)(2,1)S(1)}, bf16[4,208,896]{2,1,0:T(8,128)(2,1)S(1)}, u32[]{:S(2)}, u32[]{:S(2)}) collective-permute-start(bf16[4,208,896]{2,1,0:T(8,128)(2,1)S(1)} %pad_maximum_fusion.7.rest_0_.rest_6_.rest_9_), channel_id=1, source_target_pairs={{0,8},{4,12},{8,0},{12,4},{16,24},{20,28},{24,16},{28,20},{1,9},{5... | collective-permute-start | bytes 4472840 | tf_op jit(solution)/shard_map/ppermute | solution.py:1194
  55.4 34.7 %collective-permute-start.9 = (bf16[4,208,896]{2,1,0:T(8,128)(2,1)S(1)}, bf16[4,208,896]{2,1,0:T(8,128)(2,1)S(1)}, u32[]{:S(2)}, u32[]{:S(2)}) collective-permute-start(bf16[4,208,896]{2,1,0:T(8,128)(2,1)S(1)} %pad_maximum_fusion.7.rest_0_.rest_6_.rest_9_), channel_id=1, source_target_pairs={{0,16},{4,20},{8,24},{12,28},{16,0},{20,4},{24,8},{28,12},{1,17},{... | collective-permute-start | bytes 4472840 | tf_op jit(solution)/shard_map/ppermute | solution.py:1194
  93.3 23.9 %collective-permute-start.10 = (bf16[8,208,896]{2,1,0:T(8,128)(2,1)}, bf16[8,208,896]{2,1,0:T(8,128)(2,1)S(1)}, u32[]{:S(2)}, u32[]{:S(2)}) collective-permute-start(bf16[8,208,896]{2,1,0:T(8,128)(2,1)} %pad_maximum_fusion), channel_id=1, source_target_pairs={{0,4},{4,0},{8,12},{12,8},{16,20},{20,16},{24,28},{28,24},{1,5},{5... | collective-permute-start | bytes 8945672 | tf_op jit(solution)/shard_map/ppermute | solution.py:1194
  94.2 19.4 %collective-permute-start.11 = (bf16[2,208,896]{2,1,0:T(8,128)(2,1)}, bf16[2,208,896]{2,1,0:T(8,128)(2,1)}, u32[]{:S(2)}, u32[]{:S(2)}) collective-permute-start(bf16[2,208,896]{2,1,0:T(8,128)(2,1)} %slice.184), channel_id=1, source_target_pairs={{0,16},{4,20},{8,24},{12,28},{16,0},{20,4},{24,8},{28,12},{1,17},{... | collective-permute-start | bytes 2236424 | tf_op jit(solution)/shard_map/ppermute | solution.py:1194
  96.9 18.9 %collective-permute-start.13 = (bf16[2,208,896]{2,1,0:T(8,128)(2,1)S(1)}, bf16[2,208,896]{2,1,0:T(8,128)(2,1)S(1)}, u32[]{:S(2)}, u32[]{:S(2)}) collective-permute-start(bf16[2,208,896]{2,1,0:T(8,128)(2,1)S(1)} %slice.187), channel_id=1, source_target_pairs={{0,8},{4,12},{8,0},{12,4},{16,24},{20,28},{24,16},{28,20},{1,9},{5... | collective-permute-start | bytes 2236424 | tf_op jit(solution)/shard_map/ppermute | solution.py:1194
  100.6 41.8 %collective-permute-start.4 = (bf16[576,1536]{1,0:T(8,128)(2,1)}, bf16[576,1536]{1,0:T(8,128)(2,1)}, u32[]{:S(2)}, u32[]{:S(2)}) collective-permute-start(bf16[576,1536]{1,0:T(8,128)(2,1)} %select_select_fusion), channel_id=1, source_target_pairs={{3,1},{1,0},{0,2},{2,3},{7,5},{5,4},{4,6},{6,7},{11,9},{9,8},{8,10... | collective-permute-start | bytes 5308424 | tf_op jit(solution)/shard_map/ppermute | solution.py:1157
  115.8 32.9 %collective-permute-start.15 = (bf16[512,1536]{1,0:T(8,128)(2,1)}, bf16[512,1536]{1,0:T(8,128)(2,1)}, u32[]{:S(2)}, u32[]{:S(2)}) collective-permute-start(bf16[512,1536]{1,0:T(8,128)(2,1)} %cotangent.1), channel_id=1, source_target_pairs={{0,4},{4,0},{8,12},{12,8},{16,20},{20,16},{24,28},{28,24},{1,5},{5... | collective-permute-start | bytes 4718600 | tf_op jit(solution)/shard_map/ppermute | solution.py:1194
  116.4 50.6 %collective-permute-start.17 = (bf16[512,1536]{1,0:T(8,128)(2,1)}, bf16[512,1536]{1,0:T(8,128)(2,1)}, u32[]{:S(2)}, u32[]{:S(2)}) collective-permute-start(bf16[512,1536]{1,0:T(8,128)(2,1)} %cotangent.1), channel_id=1, source_target_pairs={{0,8},{4,12},{8,0},{12,4},{16,24},{20,28},{24,16},{28,20},{1,9},{5... | collective-permute-start | bytes 4718600 | tf_op jit(solution)/shard_map/ppermute | solution.py:1194
  117.2 49.8 %collective-permute-start.18 = (bf16[512,1536]{1,0:T(8,128)(2,1)}, bf16[512,1536]{1,0:T(8,128)(2,1)}, u32[]{:S(2)}, u32[]{:S(2)}) collective-permute-start(bf16[512,1536]{1,0:T(8,128)(2,1)} %cotangent.1), channel_id=1, source_target_pairs={{0,16},{4,20},{8,24},{12,28},{16,0},{20,4},{24,8},{28,12},{1,17},{... | collective-permute-start | bytes 4718600 | tf_op jit(solution)/shard_map/ppermute | solution.py:1194
  163.3 43.1 %collective-permute-start.32 = (bf16[576,1536]{1,0:T(8,128)(2,1)S(1)}, bf16[576,1536]{1,0:T(8,128)(2,1)}, u32[]{:S(2)}, u32[]{:S(2)}) collective-permute-start(bf16[576,1536]{1,0:T(8,128)(2,1)S(1)} %copy-done.10), channel_id=1, source_target_pairs={{0,3},{3,0},{4,7},{7,4},{8,11},{11,8},{12,15},{15,12},{16,19},{19,... | collective-permute-start | bytes 5308424 | tf_op jit(solution)/shard_map/ppermute | solution.py:1146
  167.0 25.6 %collective-permute-start.21 = (bf16[512,1536]{1,0:T(8,128)(2,1)}, bf16[512,1536]{1,0:T(8,128)(2,1)}, u32[]{:S(2)}, u32[]{:S(2)}) collective-permute-start(bf16[512,1536]{1,0:T(8,128)(2,1)} %collective-permute-done.17.rest_2_), channel_id=1, source_target_pairs={{0,4},{4,0},{8,12},{12,8},{16,20},{20,16},{24,28},{28,24},{1,5},{5... | collective-permute-start | bytes 4718600 | tf_op jit(solution)/shard_map/ppermute | solution.py:1194
  167.1 25.6 %collective-permute-start.22 = (bf16[512,1536]{1,0:T(8,128)(2,1)}, bf16[512,1536]{1,0:T(8,128)(2,1)}, u32[]{:S(2)}, u32[]{:S(2)}) collective-permute-start(bf16[512,1536]{1,0:T(8,128)(2,1)} %collective-permute-done.18.rest_4_), channel_id=1, source_target_pairs={{0,4},{4,0},{8,12},{12,8},{16,20},{20,16},{24,28},{28,24},{1,5},{5... | collective-permute-start | bytes 4718600 | tf_op jit(solution)/shard_map/ppermute | solution.py:1194
  169.7 19.8 %collective-permute-start.19 = (bf16[256,1536]{1,0:T(8,128)(2,1)}, bf16[256,1536]{1,0:T(8,128)(2,1)}, u32[]{:S(2)}, u32[]{:S(2)}) collective-permute-start(bf16[256,1536]{1,0:T(8,128)(2,1)} %slice.189), channel_id=1, source_target_pairs={{0,16},{4,20},{8,24},{12,28},{16,0},{20,4},{24,8},{28,12},{1,17},{... | collective-permute-start | bytes 2359304 | tf_op jit(solution)/shard_map/ppermute | solution.py:1194
  172.2 19.5 %collective-permute-start.20 = (bf16[256,1536]{1,0:T(8,128)(2,1)}, bf16[256,1536]{1,0:T(8,128)(2,1)S(1)}, u32[]{:S(2)}, u32[]{:S(2)}) collective-permute-start(bf16[256,1536]{1,0:T(8,128)(2,1)} %slice.190), channel_id=1, source_target_pairs={{0,8},{4,12},{8,0},{12,4},{16,24},{20,28},{24,16},{28,20},{1,9},{5... | collective-permute-start | bytes 2359304 | tf_op jit(solution)/shard_map/ppermute | solution.py:1194
  206.5 381.5 %reduce-scatter.3.cloned.1.call-start = ((), (), s32[]{:S(2)}) async-start(), calls=%async_computation.2 | async-start | bytes 8847360 | tf_op jit(solution)/shard_map/reduce_scatter | solution.py:1436
  206.6 36.9 %collective-permute-start.23 = (bf16[512,1536]{1,0:T(8,128)(2,1)S(1)}, bf16[512,1536]{1,0:T(8,128)(2,1)}, u32[]{:S(2)}, u32[]{:S(2)}) collective-permute-start(bf16[512,1536]{1,0:T(8,128)(2,1)S(1)} %copy-done.17), channel_id=1, source_target_pairs={{0,8},{4,12},{8,0},{12,4},{16,24},{20,28},{24,16},{28,20},{1,9},{5... | collective-permute-start | bytes 4718600 | tf_op jit(solution)/shard_map/ppermute | solution.py:1194
  208.0 36.5 %collective-permute-start.24 = (bf16[512,1536]{1,0:T(8,128)(2,1)S(1)}, bf16[512,1536]{1,0:T(8,128)(2,1)S(1)}, u32[]{:S(2)}, u32[]{:S(2)}) collective-permute-start(bf16[512,1536]{1,0:T(8,128)(2,1)S(1)} %copy-done.17), channel_id=1, source_target_pairs={{0,16},{4,20},{8,24},{12,28},{16,0},{20,4},{24,8},{28,12},{1,17},{... | collective-permute-start | bytes 4718600 | tf_op jit(solution)/shard_map/ppermute | solution.py:1194
  215.7 32.6 %collective-permute-start.30 = (bf16[512,1536]{1,0:T(8,128)(2,1)S(1)}, bf16[512,1536]{1,0:T(8,128)(2,1)}, u32[]{:S(2)}, u32[]{:S(2)}) collective-permute-start(bf16[512,1536]{1,0:T(8,128)(2,1)S(1)} %copy-done.18), channel_id=1, source_target_pairs={{0,4},{4,0},{8,12},{12,8},{16,20},{20,16},{24,28},{28,24},{1,5},{5... | collective-permute-start | bytes 4718600 | tf_op jit(solution)/shard_map/ppermute | solution.py:1194
  244.4 19.4 %collective-permute-start.28 = (bf16[512,1536]{1,0:T(8,128)(2,1)S(1)}, bf16[512,1536]{1,0:T(8,128)(2,1)S(1)}, u32[]{:S(2)}, u32[]{:S(2)}) collective-permute-start(bf16[512,1536]{1,0:T(8,128)(2,1)S(1)} %collective-permute-done.24.rows), channel_id=1, source_target_pairs={{0,4},{4,0},{8,12},{12,8},{16,20},{20,16},{24,28},{28,24},{1,5},{5... | collective-permute-start | bytes 4718600 | tf_op jit(solution)/shard_map/ppermute | solution.py:1194
  247.1 21.5 %collective-permute-start.26 = (bf16[256,1536]{1,0:T(8,128)(2,1)}, bf16[256,1536]{1,0:T(8,128)(2,1)S(1)}, u32[]{:S(2)}, u32[]{:S(2)}) collective-permute-start(bf16[256,1536]{1,0:T(8,128)(2,1)} %slice.193), channel_id=1, source_target_pairs={{0,16},{4,20},{8,24},{12,28},{16,0},{20,4},{24,8},{28,12},{1,17},{... | collective-permute-start | bytes 2359304 | tf_op jit(solution)/shard_map/ppermute | solution.py:1194
  247.7 20.9 %collective-permute-start.27 = (bf16[256,1536]{1,0:T(8,128)(2,1)S(1)}, bf16[256,1536]{1,0:T(8,128)(2,1)}, u32[]{:S(2)}, u32[]{:S(2)}) collective-permute-start(bf16[256,1536]{1,0:T(8,128)(2,1)S(1)} %slice.194), channel_id=1, source_target_pairs={{0,8},{4,12},{8,0},{12,4},{16,24},{20,28},{24,16},{28,20},{1,9},{5... | collective-permute-start | bytes 2359304 | tf_op jit(solution)/shard_map/ppermute | solution.py:1194
  324.6 330.2 %reduce-scatter.5.cloned.1.call-start = ((), (), s32[]{:S(2)}) async-start(), calls=%async_computation.3 | async-start | bytes 8847360 | tf_op jit(solution)/shard_map/reduce_scatter | solution.py:1466
  370.5 16.0 %collective-permute-start.34 = (bf16[4,544,1536]{2,1,0:T(8,128)(2,1)}, bf16[4,544,1536]{2,1,0:T(8,128)(2,1)S(1)}, u32[]{:S(2)}, u32[]{:S(2)}) collective-permute-start(bf16[4,544,1536]{2,1,0:T(8,128)(2,1)} %combine.7), channel_id=1, source_target_pairs={{0,4},{4,0},{8,12},{12,8},{16,20},{20,16},{24,28},{28,24},{1,5},{5... | collective-permute-start | bytes 20054024 | tf_op jit(solution)/shard_map/ppermute | solution.py:1194
  377.9 65.8 %collective-permute-start.33 = (bf16[4,512,1536]{2,1,0:T(8,128)(2,1)}, bf16[4,512,1536]{2,1,0:T(8,128)(2,1)}, u32[]{:S(2)}, u32[]{:S(2)}) collective-permute-start(bf16[4,512,1536]{2,1,0:T(8,128)(2,1)} %combine.5), channel_id=1, source_target_pairs={{0,4},{4,0},{8,12},{12,8},{16,20},{20,16},{24,28},{28,24},{1,5},{5... | collective-permute-start | bytes 18874376 | tf_op jit(solution)/shard_map/ppermute | solution.py:1194
  397.0 38.7 %collective-permute-start.35 = (bf16[2,272,1536]{2,1,0:T(8,128)(2,1)}, bf16[2,272,1536]{2,1,0:T(8,128)(2,1)S(1)}, u32[]{:S(2)}, u32[]{:S(2)}) collective-permute-start(bf16[2,272,1536]{2,1,0:T(8,128)(2,1)} %get-tuple-element.203), channel_id=1, source_target_pairs={{0,8},{4,12},{8,0},{12,4},{16,24},{20,28},{24,16},{28,20},{1,9},{5... | collective-permute-start | bytes 5013512 | tf_op jit(solution)/shard_map/ppermute | solution.py:1194
  398.5 38.4 %collective-permute-start.36 = (bf16[2,272,1536]{2,1,0:T(8,128)(2,1)}, bf16[2,272,1536]{2,1,0:T(8,128)(2,1)S(1)}, u32[]{:S(2)}, u32[]{:S(2)}) collective-permute-start(bf16[2,272,1536]{2,1,0:T(8,128)(2,1)} %get-tuple-element.204), channel_id=1, source_target_pairs={{0,16},{4,20},{8,24},{12,28},{16,0},{20,4},{24,8},{28,12},{1,17},{... | collective-permute-start | bytes 5013512 | tf_op jit(solution)/shard_map/ppermute | solution.py:1194
  441.4 19.7 %collective-permute-start.37 = (bf16[272,1536]{1,0:T(8,128)(2,1)}, bf16[272,1536]{1,0:T(8,128)(2,1)S(1)}, u32[]{:S(2)}, u32[]{:S(2)}) collective-permute-start(bf16[272,1536]{1,0:T(8,128)(2,1)} %get-tuple-element.211), channel_id=1, source_target_pairs={{0,16},{4,20},{8,24},{12,28},{16,0},{20,4},{24,8},{28,12},{1,17},{... | collective-permute-start | bytes 2506760 | tf_op jit(solution)/shard_map/ppermute | solution.py:1194
  442.9 19.4 %collective-permute-start.38 = (bf16[272,1536]{1,0:T(8,128)(2,1)}, bf16[272,1536]{1,0:T(8,128)(2,1)S(1)}, u32[]{:S(2)}, u32[]{:S(2)}) collective-permute-start(bf16[272,1536]{1,0:T(8,128)(2,1)} %get-tuple-element.212), channel_id=1, source_target_pairs={{0,8},{4,12},{8,0},{12,4},{16,24},{20,28},{24,16},{28,20},{1,9},{5... | collective-permute-start | bytes 2506760 | tf_op jit(solution)/shard_map/ppermute | solution.py:1194
  463.3 54.8 %collective-permute-start.39 = (bf16[2,256,1536]{2,1,0:T(8,128)(2,1)}, bf16[2,256,1536]{2,1,0:T(8,128)(2,1)}, u32[]{:S(2)}, u32[]{:S(2)}) collective-permute-start(bf16[2,256,1536]{2,1,0:T(8,128)(2,1)} %get-tuple-element.215), channel_id=1, source_target_pairs={{0,8},{4,12},{8,0},{12,4},{16,24},{20,28},{24,16},{28,20},{1,9},{5... | collective-permute-start | bytes 4718600 | tf_op jit(solution)/shard_map/ppermute | solution.py:1194
  464.4 53.6 %collective-permute-start.40 = (bf16[2,256,1536]{2,1,0:T(8,128)(2,1)}, bf16[2,256,1536]{2,1,0:T(8,128)(2,1)S(1)}, u32[]{:S(2)}, u32[]{:S(2)}) collective-permute-start(bf16[2,256,1536]{2,1,0:T(8,128)(2,1)} %get-tuple-element.216), channel_id=1, source_target_pairs={{0,16},{4,20},{8,24},{12,28},{16,0},{20,4},{24,8},{28,12},{1,17},{... | collective-permute-start | bytes 4718600 | tf_op jit(solution)/shard_map/ppermute | solution.py:1194
  494.5 23.6 %collective-permute-start.41 = (bf16[512,512]{1,0:T(8,128)(2,1)S(1)}, bf16[512,512]{1,0:T(8,128)(2,1)S(1)}, u32[]{:S(2)}, u32[]{:S(2)}) collective-permute-start(bf16[512,512]{1,0:T(8,128)(2,1)S(1)} %convert_element_type.153), channel_id=1, source_target_pairs={{0,1},{2,3},{4,5},{6,7},{8,9},{10,11},{12,13},{14,15},{16,17},{18,... | collective-permute-start | bytes 1572872 | tf_op jit(solution)/shard_map/ppermute | solution.py:1483
  547.4 35.1 %collective-permute-start.43 = (bf16[2,416,896]{2,1,0:T(8,128)(2,1)}, bf16[2,416,896]{2,1,0:T(8,128)(2,1)}, u32[]{:S(2)}, u32[]{:S(2)}) collective-permute-start(bf16[2,416,896]{2,1,0:T(8,128)(2,1)} %get-tuple-element.233), channel_id=1, source_target_pairs={{0,8},{4,12},{8,0},{12,4},{16,24},{20,28},{24,16},{28,20},{1,9},{5... | collective-permute-start | bytes 4472840 | tf_op jit(solution)/shard_map/ppermute | solution.py:1194
  547.7 34.8 %collective-permute-start.44 = (bf16[2,416,896]{2,1,0:T(8,128)(2,1)}, bf16[2,416,896]{2,1,0:T(8,128)(2,1)S(1)}, u32[]{:S(2)}, u32[]{:S(2)}) collective-permute-start(bf16[2,416,896]{2,1,0:T(8,128)(2,1)} %get-tuple-element.234), channel_id=1, source_target_pairs={{0,16},{4,20},{8,24},{12,28},{16,0},{20,4},{24,8},{28,12},{1,17},{... | collective-permute-start | bytes 4472840 | tf_op jit(solution)/shard_map/ppermute | solution.py:1194
  586.7 19.8 %collective-permute-start.47 = (bf16[416,896]{1,0:T(8,128)(2,1)}, bf16[416,896]{1,0:T(8,128)(2,1)S(1)}, u32[]{:S(2)}, u32[]{:S(2)}) collective-permute-start(bf16[416,896]{1,0:T(8,128)(2,1)} %get-tuple-element.247), channel_id=1, source_target_pairs={{0,16},{4,20},{8,24},{12,28},{16,0},{20,4},{24,8},{28,12},{1,17},{... | collective-permute-start | bytes 2236424 | tf_op jit(solution)/shard_map/ppermute | solution.py:1194
  589.9 19.7 %collective-permute-start.48 = (bf16[416,896]{1,0:T(8,128)(2,1)S(1)}, bf16[416,896]{1,0:T(8,128)(2,1)S(1)}, u32[]{:S(2)}, u32[]{:S(2)}) collective-permute-start(bf16[416,896]{1,0:T(8,128)(2,1)S(1)} %copy-done.54), channel_id=1, source_target_pairs={{0,8},{4,12},{8,0},{12,4},{16,24},{20,28},{24,16},{28,20},{1,9},{5... | collective-permute-start | bytes 2236424 | tf_op jit(solution)/shard_map/ppermute | solution.py:1194
  596.7 25.0 %collective-permute-start.45 = (bf16[256,1536]{1,0:T(8,128)(2,1)}, bf16[256,1536]{1,0:T(8,128)(2,1)}, u32[]{:S(2)}, u32[]{:S(2)}) collective-permute-start(bf16[256,1536]{1,0:T(8,128)(2,1)} %get-tuple-element.243), channel_id=1, source_target_pairs={{0,16},{4,20},{8,24},{12,28},{16,0},{20,4},{24,8},{28,12},{1,17},{... | collective-permute-start | bytes 2359304 | tf_op jit(solution)/shard_map/ppermute | solution.py:1194
  597.5 26.9 %collective-permute-start.46 = (bf16[256,1536]{1,0:T(8,128)(2,1)}, bf16[256,1536]{1,0:T(8,128)(2,1)}, u32[]{:S(2)}, u32[]{:S(2)}) collective-permute-start(bf16[256,1536]{1,0:T(8,128)(2,1)} %get-tuple-element.244), channel_id=1, source_target_pairs={{0,8},{4,12},{8,0},{12,4},{16,24},{20,28},{24,16},{28,20},{1,9},{5... | collective-permute-start | bytes 2359304 | tf_op jit(solution)/shard_map/ppermute | solution.py:1194
  613.1 20.9 %collective-permute-start.49 = (bf16[208,896]{1,0:T(8,128)(2,1)S(1)}, bf16[208,896]{1,0:T(8,128)(2,1)S(1)}, u32[]{:S(2)}, u32[]{:S(2)}) collective-permute-start(bf16[208,896]{1,0:T(8,128)(2,1)S(1)} %get-tuple-element.295), channel_id=1, source_target_pairs={{1,3},{0,1},{2,0},{3,2},{5,7},{4,5},{6,4},{7,6},{9,11},{8,9},{10,8... | collective-permute-start | bytes 1118216 | tf_op jit(solution)/shard_map/ppermute | solution.py:1176
  635.1 30.8 %collective-permute-start.50 = (bf16[208,896]{1,0:T(8,128)(2,1)}, bf16[208,896]{1,0:T(8,128)(2,1)}, u32[]{:S(2)}, u32[]{:S(2)}) collective-permute-start(bf16[208,896]{1,0:T(8,128)(2,1)} %get-tuple-element.293), channel_id=1, source_target_pairs={{0,1},{1,2},{2,3},{4,5},{5,6},{6,7},{8,9},{9,10},{10,11},{12,13},{... | collective-permute-start | bytes 1118216 | tf_op jit(solution)/shard_map/ppermute | solution.py:1183
  640.1 25.9 %collective-permute-start.51 = (bf16[208,896]{1,0:T(8,128)(2,1)}, bf16[208,896]{1,0:T(8,128)(2,1)}, u32[]{:S(2)}, u32[]{:S(2)}) collective-permute-start(bf16[208,896]{1,0:T(8,128)(2,1)} %get-tuple-element.292), channel_id=1, source_target_pairs={{1,0},{2,1},{3,2},{5,4},{6,5},{7,6},{9,8},{10,9},{11,10},{13,12},{... | collective-permute-start | bytes 1118216 | tf_op jit(solution)/shard_map/ppermute | solution.py:1184
  641.4 24.6 %collective-permute-start.52 = (bf16[208,896]{1,0:T(8,128)(2,1)}, bf16[208,896]{1,0:T(8,128)(2,1)}, u32[]{:S(2)}, u32[]{:S(2)}) collective-permute-start(bf16[208,896]{1,0:T(8,128)(2,1)} %get-tuple-element.251), channel_id=1, source_target_pairs={{0,3},{3,0},{4,7},{7,4},{8,11},{11,8},{12,15},{15,12},{16,19},{19,... | collective-permute-start | bytes 1118216 | tf_op jit(solution)/shard_map/ppermute | solution.py:1146
  (64 other events, 476.1 us)
Sparse Core Ops, SparseCore 0:
  206.6 125.5 all-gather.2
  334.5 121.7 reduce-scatter.2
  465.1 130.5 reduce-scatter.4

commit v15 on v14

--- a/solution.py
+++ b/solution.py
@@ -982,58 +982,60 @@
     )(info, own_grad, source_grad, arrived, cosine, sine)
 
 
-def token_back_kernel(info, grad_query, grad_pair, tokens, grad_residual, gain, *rest):
-    count = (len(rest) - 6) // 2
-    query_refs, pair_refs = rest[:count], rest[count : 2 * count]
-    out, grad_gain, query_weight, pair_weight, grad_normed, sem = rest[2 * count :]
+def normed_grad_kernel(info, grad_query, *rest):
+    refs, (out, weight, sem) = rest[:-3], rest[-3:]
 
     @pl.when(pl.program_id(0) == 0)
     def _():
-        copies = weight_copies(info, query_refs, query_weight, sem, 0, D // QUARTERS)
-        copies += weight_copies(info, pair_refs, pair_weight, sem, D // QUARTERS, 128)
+        copies = weight_copies(info, refs, weight, sem, 0, D // QUARTERS)
         run_all(copies)
         wait_all(copies)
 
     at = pl.ds(pl.multiple_of(pl.program_id(0) * STEP, STEP), STEP)
-    grad_normed[:, at] = nt(grad_query[...], query_weight[at, :]) + nt(
-        grad_pair[...], pair_weight[at, :]
-    )
-
-    @pl.when(pl.program_id(0) == pl.num_programs(0) - 1)
-    def _():
-        grad_values, gain_grad = norm_back(
-            tokens[...].astype(WIDE), gain[...], grad_normed[...]
-        )
-        grad_gain[...] = gain_grad
-        out[...] = (grad_residual[...] + grad_values).astype(LOW)
-
-
-def token_back(info, grad_query, grad_pair, tokens, grad_residual, gain, query_refs, pair_refs):
+    out[...] = nt(grad_query[...], weight[at, :])
+
+
+def normed_grad(info, grad_query, refs):
+    return pl.pallas_call(
+        normed_grad_kernel,
+        grid=(D // STEP,),
+        out_shape=jax.ShapeDtypeStruct((TOK_DEV, D), WIDE),
+        in_specs=[SMEM, whole((TOK_DEV, D))] + [ANY] * len(refs),
+        out_specs=pl.BlockSpec((TOK_DEV, STEP), lambda i: (0, i)),
+        scratch_shapes=[pltpu.VMEM((D, D), LOW), pltpu.SemaphoreType.DMA],
+        compiler_params=params(),
+        cost_estimate=LITTLE,
+        name="normed_gradient",
+    )(info, grad_query, *refs)
+
+
+def token_back_kernel(info, query_part, grad_pair, tokens, grad_residual, gain, *rest):
+    refs, (out, grad_gain, weight, sem) = rest[:-4], rest[-4:]
+    copies = weight_copies(info, refs, weight, sem, D // QUARTERS, 128)
+    run_all(copies)
+    wait_all(copies)
+    grad_normed = query_part[...] + nt(grad_pair[...], weight[...])
+    grad_values, gain_grad = norm_back(tokens[...].astype(WIDE), gain[...], grad_normed)
+    grad_gain[...] = gain_grad
+    out[...] = (grad_residual[...] + grad_values).astype(LOW)
+
+
+def token_back(info, query_part, grad_pair, tokens, grad_residual, gain, refs):
     full = (TOK_DEV, D)
+    vmem = pl.BlockSpec(memory_space=pltpu.VMEM)
     return pl.pallas_call(
         token_back_kernel,
-        grid=(D // STEP,),
         out_shape=(jax.ShapeDtypeStruct(full, LOW), jax.ShapeDtypeStruct((1, D), WIDE)),
-        in_specs=[
-            SMEM,
-            whole(full),
-            whole((TOK_DEV, 2 * KEY_WIDTH)),
-            whole(full),
-            whole(full),
-            whole((1, D)),
-        ]
-        + [ANY] * (len(query_refs) + len(pair_refs)),
-        out_specs=(whole(full), whole((1, D))),
+        in_specs=[SMEM] + [vmem] * 5 + [ANY] * len(refs),
+        out_specs=(vmem, vmem),
         scratch_shapes=[
-            pltpu.VMEM((D, D), LOW),
             pltpu.VMEM((D, 2 * KEY_WIDTH), LOW),
-            pltpu.VMEM(full, WIDE),
             pltpu.SemaphoreType.DMA,
         ],
         compiler_params=params(),
         cost_estimate=LITTLE,
         name="token_gradient",
-    )(info, grad_query, grad_pair, tokens, grad_residual, gain, *query_refs, *pair_refs)
+    )(info, query_part, grad_pair, tokens, grad_residual, gain, *refs)
 
 
 def weight_grads_kernel(parts, whole_rows, info, *rest):
@@ -1105,6 +1107,44 @@
     )(info, *inputs, *earlier)
 
 
+def last_sums_kernel(part, info, own, *rest):
+    arrived, (query_out, key_out, value_out, out_out, extra_out) = rest[:-5], rest[-5:]
+    total = own[...].astype(WIDE)
+    for ref in arrived[:-1]:
+        total += ref[...].astype(WIDE)
+    end = jnp.logical_or(info[2] == 0, info[2] == 3)
+    total += jnp.where(end, arrived[-1][...].astype(WIDE), 0.0)
+    depth = query_out.shape[0]
+    quarter = query_out.shape[1]
+    query_out[...] = total[:depth, :quarter]
+    pair = total[:depth, quarter : quarter + 2 * part].T
+    key_out[...] = pair[:part]
+    value_out[...] = pair[part:]
+    out_out[...] = total[:depth, quarter + 2 * part :]
+    extra_out[...] = total[depth:]
+
+
+def last_sums(info, own, arrived, depth, part):
+    height, width = own.shape
+    quarter = D // QUARTERS
+    vmem = pl.BlockSpec(memory_space=pltpu.VMEM)
+    return pl.pallas_call(
+        functools.partial(last_sums_kernel, part),
+        out_shape=(
+            jax.ShapeDtypeStruct((depth, quarter), WIDE),
+            jax.ShapeDtypeStruct((part, depth), WIDE),
+            jax.ShapeDtypeStruct((part, depth), WIDE),
+            jax.ShapeDtypeStruct((depth, quarter), WIDE),
+            jax.ShapeDtypeStruct((height - depth, width), WIDE),
+        ),
+        in_specs=[SMEM] + [vmem] * (1 + len(arrived)),
+        out_specs=(vmem,) * 5,
+        compiler_params=params(),
+        cost_estimate=LITTLE,
+        name="last_sums",
+    )(info, own, *arrived)
+
+
 def position_of(token_index):
     branch_place = TRUNK + (token_index - TRUNK) % BRANCH
     leaf_place = TRUNK + BRANCH + (token_index - TOK_DEV) % BRANCH
@@ -1169,24 +1209,21 @@
     ]
 
 
-def reduce_slots(slots, *earlier):
+def send_slots(slots):
     place = lax.axis_index("cols")
-    own, second, third, fourth = slots
-    end = (place == 0) | (place == 3)
+    _, second, third, fourth = slots
     relay = lax.ppermute(second, "cols", [(1, 3), (0, 1), (2, 0), (3, 2)])
     relayed = relay.astype(WIDE)
     upward_load = (
         jnp.where(place == 0, third, fourth).astype(WIDE) + jnp.where(place == 1, relayed, 0.0)
     ).astype(LOW)
     downward_load = (third.astype(WIDE) + jnp.where(place == 2, relayed, 0.0)).astype(LOW)
-    arrived = (
+    return (
         lax.ppermute(upward_load, "cols", UP),
         lax.ppermute(downward_load, "cols", DOWN),
         send_far(after(fourth, upward_load, downward_load)),
-        jnp.where(end, relay, jnp.zeros_like(relay)),
+        relay,
     )
-    arrived = after(arrived, *earlier)
-    return own.astype(WIDE) + sum(block.astype(WIDE) for block in arrived)
 
 
 def flip(block, bit):
@@ -1388,9 +1425,9 @@
     if fast:
         half = TOK_DEV // 2
         picked = place_block(0, normed_two, None)
-        beside, across = after((beside, across), picked, *grad_rows)
+        picked = place_block(1, beside_in, after(picked, *grad_rows))
+        beside, across = after((beside, across), picked)
         corner = [flip(beside[:half], 4), flip(across[half:], 2)]
-        picked = place_block(1, beside_in, picked)
         picked = place_block(2, beside, picked)
         picked = place_block(4, across, picked)
         beside_in = flip(beside, 1)
@@ -1486,7 +1523,16 @@
         keep_send = weight_grads(
             info, [normed, heads], [grad_query, grad_branch], parts, extra
         )
-        arrived = after(arrived, *keep_send, *out_flips)
+        near_x, near_y = out_first[2:]
+        for_y, for_x = corner_adds(
+            near_x, after(out_flips[0], *keep_send), near_y, out_flips[1]
+        )
+        mixture = (near_x, out_flips[0], flip(for_y, 4))
+        mixture += (near_y, out_flips[1], flip(for_x, 2))
+        query_back = normed_grad(info, after(grad_query, for_y), query_refs)
+        arrived = after(arrived, query_back)
+    else:
+        query_back = normed_grad(info, grad_query, query_refs)
     grad_pair = join_grads(info, own_grad, source_grad, arrived, cosine, sine)
     if fast:
         keep, send = weight_grads(
@@ -1498,14 +1544,12 @@
         sent_chips = send_chips(sent_first[:2])
         grad_pair = after(grad_pair, sent_first[0])
     tokens_grad, attention_gain_grad = token_back(
-        info, grad_query, grad_pair, tokens, grad_residual, attention_scale, query_refs, pair_refs
+        info, query_back, grad_pair, tokens, grad_residual, attention_scale, pair_refs
     )
 
     if fast:
         sent_chips = after(sent_chips, tokens_grad)
         sent_parts = chips_second(*sent_first[2:], *sent_chips)
-        near_x, near_y = out_first[2:]
-        mixture = chips_second(near_x, near_y, *after(out_flips, *sent_chips))
     layer_output = (residual + sum_parts(mixture)).astype(LOW)
     part = down_weight.shape[1]
     expert_sums = [block.astype(WIDE) for block in reduced]
@@ -1513,6 +1557,7 @@
         jnp.stack([sums_of[which * part : (which + 1) * part] for sums_of in expert_sums])
         for which in range(3)
     )
+    gate_grad, upward_grad = jnp.swapaxes(gate_grad, 1, 2), jnp.swapaxes(upward_grad, 1, 2)
     if fast:
         slots = sum_parts(sent_parts)
         slots = slots.reshape(col_count, depth + EXTRA, wide)
@@ -1530,11 +1575,15 @@
         )
         slots = after((slots + gain_sums).astype(LOW), reduced[1])
 
-        sums = reduce_slots(slots, gate_grad, upward_grad, down_grad, layer_output)
-        router_sum = sums[depth : depth + router_part, :depth].T
-        experts_gain_sum = sums[depth + router_part, :gain_part]
-        attention_gain_sum = sums[depth + router_part + 1, :gain_part]
-        sums = sums[:depth]
+        arrived = send_slots(slots)
+        earlier = (gate_grad, upward_grad, down_grad, layer_output)
+        query_sum, key_sum, value_sum, out_sum, extra_sum = last_sums(
+            info, slots[0], after(arrived, *earlier), depth, key_part
+        )
+        key_sum, value_sum = key_sum.T, value_sum.T
+        router_sum = extra_sum[:router_part, :depth].T
+        experts_gain_sum = extra_sum[router_part, :gain_part]
+        attention_gain_sum = extra_sum[router_part + 1, :gain_part]
     else:
         full_grads = [
             tn(normed, grad_query),
@@ -1550,6 +1599,11 @@
         )
         row_sums = lax.psum_scatter(packed_grad, "rows", scatter_dimension=0)
         sums = lax.psum_scatter(row_sums, "cols", scatter_dimension=1).astype(WIDE)
+        key_at = query_part
+        value_at = key_at + key_part
+        out_at = value_at + key_part
+        query_sum, out_sum = sums[:, :key_at], sums[:, out_at:]
+        key_sum, value_sum = sums[:, key_at:value_at], sums[:, value_at:out_at]
         small_grads = jnp.concatenate(
             [
                 attention_gain_grad.reshape(-1, gain_part),
@@ -1569,21 +1623,18 @@
         experts_gain_sum = small_sums[gain_part : 2 * gain_part]
         router_sum = small_sums[2 * gain_part :].reshape(depth, router_part)
 
-    key_at = query_part
-    value_at = key_at + key_part
-    out_at = value_at + key_part
     return (
         layer_output,
         tokens_grad,
-        sums[:, :key_at],
-        sums[:, key_at:value_at],
-        sums[:, value_at:out_at],
-        sums[:, out_at:],
+        query_sum,
+        key_sum,
+        value_sum,
+        out_sum,
         router_sum,
         attention_gain_sum,
         experts_gain_sum,
-        jnp.swapaxes(gate_grad, 1, 2),
-        jnp.swapaxes(upward_grad, 1, 2),
+        gate_grad,
+        upward_grad,
         down_grad,
     )
 

time: 693 us -> 683 us (0.986)
  starting transfers between devices: 91.6 us -> 84.1 us
    ppermute x39, waiting for transfers between devices: 137 us -> 146 us  [flip(): return lax.ppermute(block, 'rows', [(i, i ^ bit) for i in range(count)])]
    ppermute x1, waiting for transfers between devices: 7.07 us -> 0.01 us  [on_device(): lax.ppermute(source_grad.astype(LOW), 'cols', [(j, i) for i, j in pairs])]
    pallas_call x1 -> x3, Pallas kernels: 12.4 us -> 18.6 us  [the longest x1 8.14 us: token_back(): pl.pallas_call(token_back_kernel, out_shape=(jax.ShapeDtypeStruct(full, L...]
    unnamed x125 -> x133, local copies, waits for them, and re-layouts: 30.2 us -> 28.4 us
  transfers between devices with their start and end apart: 56 -> 56, of which waited for: 25 -> 27; matrix products, arithmetic and copies ran while one was open for 8% -> 8% of each run, Pallas kernels for 43% -> 45%
where the time goes in v15:
time: 683 us; the launch traced here: 674 us
  Pallas kernels  303 us (44%)
  waiting for transfers between devices  184 us (27%)
  starting transfers between devices  84.1 us (12%)
  local copies, waits for them, and re-layouts  54 us (8%)
  other arithmetic  33.9 us (5%)
  between operations  14.9 us (2%)
    ppermute x39, waiting for transfers between devices, flip(): return lax.ppermute(block, 'rows', [(i, i ^ bit) for i in range(count)])  146 us
    pallas_call x2, Pallas kernels, expert(): pl.pallas_call(functools.partial(expert_kernel, slots), grid=(height // E...  60.9 us
    pallas_call x4, Pallas kernels, combine(): pl.pallas_call(functools.partial(combine_kernel, local, first, step), out...  30.9 us
    pallas_call x2, Pallas kernels, expert_grads(): pl.pallas_call(expert_grads_kernel, grid=(D // 256,), out_shape=jax.Shape...  29.3 us
    ppermute x39, starting transfers between devices, flip(): return lax.ppermute(block, 'rows', [(i, i ^ bit) for i in range(count)])  28.9 us
    pallas_call x8, Pallas kernels, dispatch(): pl.pallas_call(functools.partial(dispatch_kernel, local), grid=(D // wide...  28.7 us
    unnamed x133, local copies, waits for them, and re-layouts  28.4 us
    ppermute x4, starting transfers between devices, send_near(): return (lax.ppermute(block, 'cols', DOWN), lax.ppermute(block, 'cols', UP))  28.1 us
  transfers between devices with their start and end apart: 56, of which 27 were waited for; matrix products, arithmetic and copies ran while one was open for 8% of the time, Pallas kernels for 45%

profile of v15, /device:TPU:0, one launch (start us, length us, event | category | flops | bytes accessed | tf_op | source)
XLA Modules:
  0.0 673.7 jit_solution(16427938415344910456)
XLA Ops:
  14.1 6.3 collective-permute-start.1
  20.4 3.8 collective-permute-start.6
  32.6 19.1 %collective-permute-start.3 = (bf16[576,1536]{1,0:T(8,128)(2,1)S(1)}, bf16[576,1536]{1,0:T(8,128)(2,1)}, u32[]{:S(2)}, u32[]{:S(2)}) collective-permute-start(bf16[576,1536]{1,0:T(8,128)(2,1)S(1)} %pad_maximum_fusion.3.rest_0_), channel_id=1, source_target_pairs={{0,1},{1,2},{2,3},{4,5},{5,6},{6,7},{8,9},{9,10},{10,11},{12,13},{... | collective-permute-start | bytes 5308424 | tf_op jit(solution)/shard_map/ppermute | solution.py:1182
  57.4 31.8 %collective-permute-done.8.rest_2_.rest_8_ = bf16[4,208,896]{2,1,0:T(8,128)(2,1)S(1)} collective-permute-done((bf16[4,208,896]{2,1,0:T(8,128)(2,1)S(1)}, bf16[4,208,896]{2,1,0:T(8,128)(2,1)S(1)}, u32[]{:S(2)}, u32[]{:S(2)}) %collective-permute-start.8) | collective-permute-done | bytes 1490976 | tf_op jit(solution)/shard_map/ppermute | solution.py:1231
  104.0 9.6 %collective-permute-done.11.rest_4_.rest_10_ = bf16[2,208,896]{2,1,0:T(8,128)(2,1)} collective-permute-done((bf16[2,208,896]{2,1,0:T(8,128)(2,1)}, bf16[2,208,896]{2,1,0:T(8,128)(2,1)}, u32[]{:S(2)}, u32[]{:S(2)}) %collective-permute-start.11) | collective-permute-done | bytes 745504 | tf_op jit(solution)/shard_map/ppermute | solution.py:1231
  120.9 5.6 route_tables.1
  131.9 10.5 %collective-permute-done.4.rest_1_ = bf16[576,1536]{1,0:T(8,128)(2,1)} collective-permute-done((bf16[576,1536]{1,0:T(8,128)(2,1)}, bf16[576,1536]{1,0:T(8,128)(2,1)}, u32[]{:S(2)}, u32[]{:S(2)}) %collective-permute-start.4) | collective-permute-done | bytes 1769504 | tf_op jit(solution)/shard_map/ppermute | solution.py:1197
  142.4 5.0 norm_key_value.1
  148.7 8.3 %query_projection.1.queries = bf16[512,1536]{1,0:T(8,128)(2,1)} custom-call(s32[16]{0:T(128)} %concatenate.42.info, bf16[512,1536]{1,0:T(8,128)(2,1)} %get-tuple-element.151.normed.rest_0_, f32[512,128]{1,0:T(8,128)} %get-tuple-element.310.cosine, f32[512,128]{1,0:T(8,128)} %get-tuple-element.311.sine, bf16[4,208,896]{2,1,0:T(8,128)(2,1)} %copy-done.1, ...), custom_call_target="tpu_custom_call" | custom-call | flops 1 | bytes 1 | tf_op jit(solution)/shard_map/query_projection/pallas_call | solution.py:195
  157.1 6.3 collective-permute-done.16.partner
  175.5 11.0 %tree_attention.1.heads.rest_1_ = bf16[512,1536]{1,0:T(8,128)(2,1)} custom-call(s32[16]{0:T(128)} %concatenate.42.info, bf16[512,1536]{1,0:T(8,128)(2,1)} %query_projection.1.queries, bf16[512,512]{1,0:T(8,128)(2,1)} %get-tuple-element.152.own, bf16[512,512]{1,0:T(8,128)(2,1)} %copy-done.39), custom_call_target="tpu_custom_call" | custom-call | flops 1 | bytes 1 | tf_op jit(solution)/shard_map/tree_attention/pallas_call | solution.py:277
  192.5 9.8 %out_projection.1 = (f32[512,1536]{1,0:T(8,128)}, bf16[512,1536]{1,0:T(8,128)(2,1)}) custom-call(s32[16]{0:T(128)} %concatenate.42.info, bf16[512,1536]{1,0:T(8,128)(2,1)} %tree_attention.1.heads.rest_1_, bf16[512,1536]{1,0:T(8,128)(2,1)} %tokens.4, f32[1,1536]{1,0:T(1,128)} %reshape.303.gain, bf16[4,208,896]{2,1,0:T(8,128)(2,1)} %copy-done.1, ...), custom_call_target="tpu_custom_call" | custom-call | flops 1 | bytes 1 | tf_op jit(solution)/shard_map/out_projection/pallas_call | solution.py:389
  202.4 4.1 collective-permute-done.32.rest_4_
  206.6 3.6 collective-permute-done.25.rest_7_
  220.0 9.3 %pick_rows.1 = (bf16[8,160,1536]{2,1,0:T(8,128)(2,1)}, bf16[8,160,1536]{2,1,0:T(8,128)(2,1)}) custom-call(bf16[8,320,512]{2,1,0:T(8,128)(2,1)} %get-tuple-element.147.chosen, bf16[512,1536]{1,0:T(8,128)(2,1)} %cotangent.1, bf16[512,1536]{1,0:T(8,128)(2,1)} %collective-permute-done.15.rest_1_, bf16[512,1536]{1,0:T(8,128)(2,1)} %collective-permute-done.17.rest_2_, ...), custom_call_target="tpu_custom_call" | custom-call | flops 1 | bytes 1 | tf_op jit(solution)/shard_map/pick_rows/pallas_call | solution.py:480
  229.3 3.6 dispatch.9
  232.9 15.0 %collective-permute-done.23.rows = bf16[512,1536]{1,0:T(8,128)(2,1)} collective-permute-done((bf16[512,1536]{1,0:T(8,128)(2,1)S(1)}, bf16[512,1536]{1,0:T(8,128)(2,1)}, u32[]{:S(2)}, u32[]{:S(2)}) %collective-permute-start.23) | collective-permute-done | bytes 1572896 | tf_op jit(solution)/shard_map/ppermute | solution.py:1231
  255.5 3.6 dispatch.11
  260.2 3.6 dispatch.12
  276.3 3.6 dispatch.15
  279.9 30.4 %expert.2 = (bf16[1280,1536]{1,0:T(8,128)(2,1)}, bf16[1280,1536]{1,0:T(8,128)(2,1)}, bf16[1280,1536]{1,0:T(8,128)(2,1)}, bf16[4,576,1280]{2,1,0:T(8,128)(2,1)}, f32[1280,1]{1,0:T(8,128)}) custom-call(s32[16]{0:T(128)} %concatenate.42.info, bf16[1280,1536]{1,0:T(8,128)(2,1)} %bitcast.151, bf16[1280,1536]{1,0:T(8,128)(2,1)} %bitcast.169, f32[1280,1]{1,0:T(8,128)} %bitcast.155, ...), custom_call_target="tpu_custom_call" | custom-call | flops 1 | bytes 1 | tf_op jit(solution)/shard_map/expert/pallas_call | solution.py:670
  310.3 14.6 %expert_gradients.2 = bf16[4,576,1536]{2,1,0:T(8,128)(2,1)} custom-call(bf16[4,576,1280]{2,1,0:T(8,128)(2,1)} %get-tuple-element.202.acts, bf16[1280,1536]{1,0:T(8,128)(2,1)} %bitcast.152, bf16[1280,1536]{1,0:T(8,128)(2,1)} %get-tuple-element.203.grads), custom_call_target="tpu_custom_call" | custom-call | flops 1 | bytes 1 | tf_op jit(solution)/shard_map/expert_gradients/pallas_call | solution.py:699
  325.0 7.2 %all-gather.3.cloned.1.call-done = bf16[2304,1536]{1,0:T(8,128)(2,1)} async-done(((bf16[576,1536]{1,0:T(8,128)(2,1)}), bf16[2304,1536]{1,0:T(8,128)(2,1)}) %all-gather.3.cloned.1.call-update) | async-done | bytes 7077904 | tf_op jit(solution)/shard_map/all_gather | solution.py:1414
  332.2 30.5 %expert.3 = (bf16[1280,1536]{1,0:T(8,128)(2,1)}, bf16[1280,1536]{1,0:T(8,128)(2,1)}, bf16[1280,1536]{1,0:T(8,128)(2,1)}, bf16[4,576,1280]{2,1,0:T(8,128)(2,1)}, f32[1280,1]{1,0:T(8,128)}) custom-call(s32[16]{0:T(128)} %concatenate.42.info, bf16[1280,1536]{1,0:T(8,128)(2,1)} %bitcast.153, bf16[1280,1536]{1,0:T(8,128)(2,1)} %bitcast.170, f32[1280,1]{1,0:T(8,128)} %bitcast.156, ...), custom_call_target="tpu_custom_call" | custom-call | flops 1 | bytes 1 | tf_op jit(solution)/shard_map/expert/pallas_call | solution.py:670
  362.6 8.0 %combine.7 = bf16[4,544,1536]{2,1,0:T(8,128)(2,1)} custom-call(s32[16]{0:T(128)} %concatenate.42.info, bf16[8,320,512]{2,1,0:T(8,128)(2,1)} %get-tuple-element.147.chosen, bf16[8,160,1536]{2,1,0:T(8,128)(2,1)} %bitcast.162, bf16[8,160,1536]{2,1,0:T(8,128)(2,1)} %bitcast.166, f32[8,160,1]{2,1,0:T(8,128)} %bitcast.171, f32[8,160,1]{2,1,0:T(8,128)} %bitcast.173), custom_call_target="tpu_custom_call" | custom-call | flops 1 | bytes 1 | tf_op jit(solution)/shard_map/combine/pallas_call | solution.py:762
  370.8 7.3 %combine.5 = bf16[4,512,1536]{2,1,0:T(8,128)(2,1)} custom-call(s32[16]{0:T(128)} %concatenate.42.info, bf16[8,320,512]{2,1,0:T(8,128)(2,1)} %get-tuple-element.147.chosen, bf16[8,160,1536]{2,1,0:T(8,128)(2,1)} %bitcast.160, bf16[8,160,1536]{2,1,0:T(8,128)(2,1)} %bitcast.164), custom_call_target="tpu_custom_call" | custom-call | flops 1 | bytes 1 | tf_op jit(solution)/shard_map/combine/pallas_call | solution.py:762
  378.6 8.1 %combine.6.keep = bf16[4,544,1536]{2,1,0:T(8,128)(2,1)} custom-call(s32[16]{0:T(128)} %concatenate.42.info, bf16[8,320,512]{2,1,0:T(8,128)(2,1)} %get-tuple-element.147.chosen, bf16[8,160,1536]{2,1,0:T(8,128)(2,1)} %bitcast.163, bf16[8,160,1536]{2,1,0:T(8,128)(2,1)} %bitcast.167, f32[8,160,1]{2,1,0:T(8,128)} %bitcast.172, f32[8,160,1]{2,1,0:T(8,128)} %bitcast.174), custom_call_target="tpu_custom_call" | custom-call | flops 1 | bytes 1 | tf_op jit(solution)/shard_map/combine/pallas_call | solution.py:762
  389.4 7.8 %chip_sums.4 = (bf16[2,272,1536]{2,1,0:T(8,128)(2,1)}, bf16[2,272,1536]{2,1,0:T(8,128)(2,1)}, bf16[2,272,1536]{2,1,0:T(8,128)(2,1)}, bf16[2,272,1536]{2,1,0:T(8,128)(2,1)}) custom-call(bf16[4,544,1536]{2,1,0:T(8,128)(2,1)} %combine.6.keep, bf16[4,544,1536]{2,1,0:T(8,128)(2,1)} %copy-done.13), custom_call_target="tpu_custom_call" | custom-call | flops 1 | bytes 1 | tf_op jit(solution)/shard_map/chip_sums/pallas_call | solution.py:811
  400.2 7.5 %combine.4.keep = bf16[4,512,1536]{2,1,0:T(8,128)(2,1)} custom-call(s32[16]{0:T(128)} %concatenate.42.info, bf16[8,320,512]{2,1,0:T(8,128)(2,1)} %get-tuple-element.147.chosen, bf16[8,160,1536]{2,1,0:T(8,128)(2,1)} %bitcast.161, bf16[8,160,1536]{2,1,0:T(8,128)(2,1)} %bitcast.165), custom_call_target="tpu_custom_call" | custom-call | flops 1 | bytes 1 | tf_op jit(solution)/shard_map/combine/pallas_call | solution.py:762
  407.7 14.7 %expert_gradients.3 = bf16[4,576,1536]{2,1,0:T(8,128)(2,1)} custom-call(bf16[4,576,1280]{2,1,0:T(8,128)(2,1)} %get-tuple-element.219.acts, bf16[1280,1536]{1,0:T(8,128)(2,1)} %bitcast.154, bf16[1280,1536]{1,0:T(8,128)(2,1)} %get-tuple-element.220.grads), custom_call_target="tpu_custom_call" | custom-call | flops 1 | bytes 1 | tf_op jit(solution)/shard_map/expert_gradients/pallas_call | solution.py:699
  422.4 13.6 %collective-permute-done.35.got_x.rest_1_ = bf16[2,272,1536]{2,1,0:T(8,128)(2,1)S(1)} collective-permute-done((bf16[2,272,1536]{2,1,0:T(8,128)(2,1)}, bf16[2,272,1536]{2,1,0:T(8,128)(2,1)S(1)}, u32[]{:S(2)}, u32[]{:S(2)}) %collective-permute-start.35) | collective-permute-done | bytes 1671200 | tf_op jit(solution)/shard_map/ppermute | solution.py:1231
  443.9 7.5 %chip_sums.3 = (bf16[2,256,1536]{2,1,0:T(8,128)(2,1)}, bf16[2,256,1536]{2,1,0:T(8,128)(2,1)}, bf16[2,256,1536]{2,1,0:T(8,128)(2,1)}, bf16[2,256,1536]{2,1,0:T(8,128)(2,1)}) custom-call(bf16[4,512,1536]{2,1,0:T(8,128)(2,1)} %combine.4.keep, bf16[4,512,1536]{2,1,0:T(8,128)(2,1)} %collective-permute-done.33.got), custom_call_target="tpu_custom_call" | custom-call | flops 1 | bytes 1 | tf_op jit(solution)/shard_map/chip_sums/pallas_call | solution.py:811
  451.4 10.0 %collective-permute-done.37.rest_2_ = bf16[272,1536]{1,0:T(8,128)(2,1)} collective-permute-done((bf16[272,1536]{1,0:T(8,128)(2,1)}, bf16[272,1536]{1,0:T(8,128)(2,1)}, u32[]{:S(2)}, u32[]{:S(2)}) %collective-permute-start.37) | collective-permute-done | bytes 835616 | tf_op jit(solution)/shard_map/ppermute | solution.py:1231
  464.4 13.3 %experts_norm_back.1 = (f32[512,1536]{1,0:T(8,128)}, bf16[512,1536]{1,0:T(8,128)(2,1)}, bf16[512,1536]{1,0:T(8,128)(2,1)}, f32[1,1536]{1,0:T(1,128)}, f32[16,1536]{1,0:T(8,128)}) custom-call(s32[16]{0:T(128)} %concatenate.42.info, f32[512,1536]{1,0:T(8,128)} %get-tuple-element.156.residual, bf16[512,1536]{1,0:T(8,128)(2,1)} %get-tuple-element.158.rows.normed, ...), custom_call_target="tpu_custom_call" | custom-call | flops 1 | bytes 1 | tf_op jit(solution)/shard_map/experts_norm_back/pallas_call | solution.py:922
  477.7 15.4 %tree_attention_back.1 = (bf16[512,1536]{1,0:T(8,128)(2,1)}, f32[512,512]{1,0:T(8,128)}, f32[512,512]{1,0:T(8,128)}) custom-call(s32[16]{0:T(128)} %concatenate.42.info, bf16[512,1536]{1,0:T(8,128)(2,1)} %query_projection.1.queries, bf16[512,512]{1,0:T(8,128)(2,1)} %get-tuple-element.152.own, bf16[512,512]{1,0:T(8,128)(2,1)} %copy-done.39, ...), custom_call_target="tpu_custom_call" | custom-call | flops 1 | bytes 1 | tf_op jit(solution)/shard_map/tree_attention_back/pallas_call | solution.py:338
  498.8 13.5 %weight_gradients.2 = (bf16[4,4,208,896]{3,2,1,0:T(8,128)(2,1)}, bf16[4,4,208,896]{3,2,1,0:T(8,128)(2,1)}) custom-call(s32[16]{0:T(128)} %concatenate.42.info, bf16[512,1536]{1,0:T(8,128)(2,1)} %get-tuple-element.151.normed.rest_0_, bf16[512,1536]{1,0:T(8,128)(2,1)} %tree_attention.1.heads.rest_1_, bf16[512,1536]{1,0:T(8,128)(2,1)} %get-tuple-element.245.rest_2_.grad_query, ...), custom_call_target="tpu_custom_call" | custom-call | flops 1 | bytes 1 | tf_op jit(solution)/shard_map/weight_gradients/pallas_call | solution.py:1089
  517.2 8.0 %normed_gradient.1.query_part = f32[512,1536]{1,0:T(8,128)} custom-call(s32[16]{0:T(128)} %concatenate.42.info, bf16[512,1536]{1,0:T(8,128)(2,1)} %get-tuple-element.245.rest_2_.grad_query, bf16[4,208,896]{2,1,0:T(8,128)(2,1)} %copy-done.1, bf16[4,208,896]{2,1,0:T(8,128)(2,1)} %copy-done.5, bf16[4,208,896]{2,1,0:T(8,128)(2,1)} %copy-done.3, ...), custom_call_target="tpu_custom_call" | custom-call | flops 1 | bytes 1 | tf_op jit(solution)/shard_map/normed_gradient/pallas_call | solution.py:999
  528.3 5.7 weight_gradients.3
  534.1 10.0 %collective-permute-done.44 = bf16[4,4,208,896]{3,2,1,0:T(8,128)(2,1)} collective-permute-done((bf16[4,4,208,896]{3,2,1,0:T(8,128)(2,1)}, bf16[4,4,208,896]{3,2,1,0:T(8,128)(2,1)}, u32[]{:S(2)}, u32[]{:S(2)}) %collective-permute-start.44) | collective-permute-done | bytes 5963808 | tf_op jit(solution)/shard_map/ppermute | solution.py:1231
  544.1 7.3 %chip_sums.5 = (bf16[2,416,896]{2,1,0:T(8,128)(2,1)}, bf16[2,416,896]{2,1,0:T(8,128)(2,1)}, bf16[2,416,896]{2,1,0:T(8,128)(2,1)}, bf16[2,416,896]{2,1,0:T(8,128)(2,1)}) custom-call(bf16[4,832,896]{2,1,0:T(8,128)(2,1)} %bitcast.157, bf16[4,832,896]{2,1,0:T(8,128)(2,1)} %bitcast.41.got), custom_call_target="tpu_custom_call" | custom-call | flops 1 | bytes 1 | tf_op jit(solution)/shard_map/chip_sums/pallas_call | solution.py:811
  561.4 8.1 %token_gradient.1 = (bf16[512,1536]{1,0:T(8,128)(2,1)}, f32[1,1536]{1,0:T(1,128)}) custom-call(s32[16]{0:T(128)} %concatenate.42.info, f32[512,1536]{1,0:T(8,128)} %normed_gradient.1.query_part, bf16[512,512]{1,0:T(8,128)(2,1)} %join_key_value_gradients.1.rest_1_.grad_pair, bf16[512,1536]{1,0:T(8,128)(2,1)} %tokens.4, ...), custom_call_target="tpu_custom_call" | custom-call | flops 1 | bytes 1 | tf_op jit(solution)/shard_map/token_gradient/pallas_call | solution.py:1026
  569.5 17.6 %collective-permute-done.45.got_x = bf16[2,416,896]{2,1,0:T(8,128)(2,1)S(1)} collective-permute-done((bf16[2,416,896]{2,1,0:T(8,128)(2,1)}, bf16[2,416,896]{2,1,0:T(8,128)(2,1)S(1)}, u32[]{:S(2)}, u32[]{:S(2)}) %collective-permute-start.45) | collective-permute-done | bytes 1490976 | tf_op jit(solution)/shard_map/ppermute | solution.py:1231
  594.1 11.0 %collective-permute-done.41 = bf16[256,1536]{1,0:T(8,128)(2,1)} collective-permute-done((bf16[256,1536]{1,0:T(8,128)(2,1)}, bf16[256,1536]{1,0:T(8,128)(2,1)}, u32[]{:S(2)}, u32[]{:S(2)}) %collective-permute-start.41) | collective-permute-done | bytes 786464 | tf_op jit(solution)/shard_map/ppermute | solution.py:1231
  610.2 9.6 %collective-permute-done.47 = bf16[416,896]{1,0:T(8,128)(2,1)S(1)} collective-permute-done((bf16[416,896]{1,0:T(8,128)(2,1)}, bf16[416,896]{1,0:T(8,128)(2,1)S(1)}, u32[]{:S(2)}, u32[]{:S(2)}) %collective-permute-start.47) | collective-permute-done | bytes 745504 | tf_op jit(solution)/shard_map/ppermute | solution.py:1231
  620.0 4.0 collective-permute-done.48
  631.1 7.2 %collective-permute-done.49.rest_3_ = bf16[208,896]{1,0:T(8,128)(2,1)S(1)} collective-permute-done((bf16[208,896]{1,0:T(8,128)(2,1)S(1)}, bf16[208,896]{1,0:T(8,128)(2,1)S(1)}, u32[]{:S(2)}, u32[]{:S(2)}) %collective-permute-start.49) | collective-permute-done | bytes 372768 | tf_op jit(solution)/shard_map/ppermute | solution.py:1215
  638.5 3.7 collective-permute-start.50
  643.5 7.4 %collective-permute-start.52 = (bf16[208,896]{1,0:T(8,128)(2,1)S(1)}, bf16[208,896]{1,0:T(8,128)(2,1)S(1)}, u32[]{:S(2)}, u32[]{:S(2)}) collective-permute-start(bf16[208,896]{1,0:T(8,128)(2,1)S(1)} %get-tuple-element.264), channel_id=1, source_target_pairs={{0,3},{3,0},{4,7},{7,4},{8,11},{11,8},{12,15},{15,12},{16,19},{19,... | collective-permute-start | bytes 1118216 | tf_op jit(solution)/shard_map/ppermute | solution.py:1186
  (319 shorter events, 176.7 us)
Async XLA Ops:
  7.2 325.0 %all-gather.3.cloned.1.call-start = ((), (), s32[]{:S(2)}) async-start(), calls=%async_computation.4 | async-start | bytes 8847360 | tf_op jit(solution)/shard_map/all_gather | solution.py:1414
  12.7 18.7 %collective-permute-start = (bf16[208,896]{1,0:T(8,128)(2,1)S(1)}, bf16[208,896]{1,0:T(8,128)(2,1)}, u32[]{:S(2)}, u32[]{:S(2)}) collective-permute-start(bf16[208,896]{1,0:T(8,128)(2,1)S(1)} %concatenate.46), channel_id=1, source_target_pairs={{1,0},{2,1},{3,2},{5,4},{6,5},{7,6},{9,8},{10,9},{11,10},{13,12},{... | collective-permute-start | bytes 1118216 | tf_op jit(solution)/shard_map/ppermute | solution.py:1182
  14.1 17.2 %collective-permute-start.1 = (bf16[208,896]{1,0:T(8,128)(2,1)S(1)}, bf16[208,896]{1,0:T(8,128)(2,1)}, u32[]{:S(2)}, u32[]{:S(2)}) collective-permute-start(bf16[208,896]{1,0:T(8,128)(2,1)S(1)} %concatenate.46), channel_id=1, source_target_pairs={{0,1},{1,2},{2,3},{4,5},{5,6},{6,7},{8,9},{9,10},{10,11},{12,13},{... | collective-permute-start | bytes 1118216 | tf_op jit(solution)/shard_map/ppermute | solution.py:1182
  20.4 31.3 %collective-permute-start.6 = (bf16[208,896]{1,0:T(8,128)(2,1)S(1)}, bf16[208,896]{1,0:T(8,128)(2,1)}, u32[]{:S(2)}, u32[]{:S(2)}) collective-permute-start(bf16[208,896]{1,0:T(8,128)(2,1)S(1)} %concatenate.46), channel_id=1, source_target_pairs={{0,3},{3,0},{4,7},{7,4},{8,11},{11,8},{12,15},{15,12},{16,19},{19,... | collective-permute-start | bytes 1118216 | tf_op jit(solution)/shard_map/ppermute | solution.py:1186
  24.2 28.7 %collective-permute-start.5 = (bf16[208,896]{1,0:T(8,128)(2,1)S(1)}, bf16[208,896]{1,0:T(8,128)(2,1)}, u32[]{:S(2)}, u32[]{:S(2)}) collective-permute-start(bf16[208,896]{1,0:T(8,128)(2,1)S(1)} %concatenate.46), channel_id=1, source_target_pairs={{0,2},{1,3},{2,0},{3,1},{4,6},{5,7},{6,4},{7,5},{8,10},{9,11},{10,... | collective-permute-start | bytes 1118216 | tf_op jit(solution)/shard_map/ppermute | solution.py:1190
  31.3 58.8 %collective-permute-start.2 = (bf16[576,1536]{1,0:T(8,128)(2,1)S(1)}, bf16[576,1536]{1,0:T(8,128)(2,1)S(1)}, u32[]{:S(2)}, u32[]{:S(2)}) collective-permute-start(bf16[576,1536]{1,0:T(8,128)(2,1)S(1)} %pad_maximum_fusion.3.rest_0_), channel_id=1, source_target_pairs={{1,0},{2,1},{3,2},{5,4},{6,5},{7,6},{9,8},{10,9},{11,10},{13,12},{... | collective-permute-start | bytes 5308424 | tf_op jit(solution)/shard_map/ppermute | solution.py:1182
  32.6 58.8 %collective-permute-start.3 = (bf16[576,1536]{1,0:T(8,128)(2,1)S(1)}, bf16[576,1536]{1,0:T(8,128)(2,1)}, u32[]{:S(2)}, u32[]{:S(2)}) collective-permute-start(bf16[576,1536]{1,0:T(8,128)(2,1)S(1)} %pad_maximum_fusion.3.rest_0_), channel_id=1, source_target_pairs={{0,1},{1,2},{2,3},{4,5},{5,6},{6,7},{8,9},{9,10},{10,11},{12,13},{... | collective-permute-start | bytes 5308424 | tf_op jit(solution)/shard_map/ppermute | solution.py:1182
  54.2 35.1 %collective-permute-start.8 = (bf16[4,208,896]{2,1,0:T(8,128)(2,1)S(1)}, bf16[4,208,896]{2,1,0:T(8,128)(2,1)S(1)}, u32[]{:S(2)}, u32[]{:S(2)}) collective-permute-start(bf16[4,208,896]{2,1,0:T(8,128)(2,1)S(1)} %pad_maximum_fusion.5.rest_0_.rest_6_), channel_id=1, source_target_pairs={{0,8},{4,12},{8,0},{12,4},{16,24},{20,28},{24,16},{28,20},{1,9},{5... | collective-permute-start | bytes 4472840 | tf_op jit(solution)/shard_map/ppermute | solution.py:1231
  55.4 34.7 %collective-permute-start.9 = (bf16[4,208,896]{2,1,0:T(8,128)(2,1)S(1)}, bf16[4,208,896]{2,1,0:T(8,128)(2,1)S(1)}, u32[]{:S(2)}, u32[]{:S(2)}) collective-permute-start(bf16[4,208,896]{2,1,0:T(8,128)(2,1)S(1)} %pad_maximum_fusion.5.rest_0_.rest_6_), channel_id=1, source_target_pairs={{0,16},{4,20},{8,24},{12,28},{16,0},{20,4},{24,8},{28,12},{1,17},{... | collective-permute-start | bytes 4472840 | tf_op jit(solution)/shard_map/ppermute | solution.py:1231
  93.3 23.9 %collective-permute-start.10 = (bf16[8,208,896]{2,1,0:T(8,128)(2,1)}, bf16[8,208,896]{2,1,0:T(8,128)(2,1)S(1)}, u32[]{:S(2)}, u32[]{:S(2)}) collective-permute-start(bf16[8,208,896]{2,1,0:T(8,128)(2,1)} %pad_maximum_fusion), channel_id=1, source_target_pairs={{0,4},{4,0},{8,12},{12,8},{16,20},{20,16},{24,28},{28,24},{1,5},{5... | collective-permute-start | bytes 8945672 | tf_op jit(solution)/shard_map/ppermute | solution.py:1231
  94.2 19.4 %collective-permute-start.11 = (bf16[2,208,896]{2,1,0:T(8,128)(2,1)}, bf16[2,208,896]{2,1,0:T(8,128)(2,1)}, u32[]{:S(2)}, u32[]{:S(2)}) collective-permute-start(bf16[2,208,896]{2,1,0:T(8,128)(2,1)} %slice.170), channel_id=1, source_target_pairs={{0,16},{4,20},{8,24},{12,28},{16,0},{20,4},{24,8},{28,12},{1,17},{... | collective-permute-start | bytes 2236424 | tf_op jit(solution)/shard_map/ppermute | solution.py:1231
  96.9 18.9 %collective-permute-start.13 = (bf16[2,208,896]{2,1,0:T(8,128)(2,1)S(1)}, bf16[2,208,896]{2,1,0:T(8,128)(2,1)S(1)}, u32[]{:S(2)}, u32[]{:S(2)}) collective-permute-start(bf16[2,208,896]{2,1,0:T(8,128)(2,1)S(1)} %slice.173), channel_id=1, source_target_pairs={{0,8},{4,12},{8,0},{12,4},{16,24},{20,28},{24,16},{28,20},{1,9},{5... | collective-permute-start | bytes 2236424 | tf_op jit(solution)/shard_map/ppermute | solution.py:1231
  100.6 41.8 %collective-permute-start.4 = (bf16[576,1536]{1,0:T(8,128)(2,1)}, bf16[576,1536]{1,0:T(8,128)(2,1)}, u32[]{:S(2)}, u32[]{:S(2)}) collective-permute-start(bf16[576,1536]{1,0:T(8,128)(2,1)} %select_select_fusion), channel_id=1, source_target_pairs={{3,1},{1,0},{0,2},{2,3},{7,5},{5,4},{4,6},{6,7},{11,9},{9,8},{8,10... | collective-permute-start | bytes 5308424 | tf_op jit(solution)/shard_map/ppermute | solution.py:1197
  115.8 32.9 %collective-permute-start.15 = (bf16[512,1536]{1,0:T(8,128)(2,1)}, bf16[512,1536]{1,0:T(8,128)(2,1)}, u32[]{:S(2)}, u32[]{:S(2)}) collective-permute-start(bf16[512,1536]{1,0:T(8,128)(2,1)} %cotangent.1), channel_id=1, source_target_pairs={{0,4},{4,0},{8,12},{12,8},{16,20},{20,16},{24,28},{28,24},{1,5},{5... | collective-permute-start | bytes 4718600 | tf_op jit(solution)/shard_map/ppermute | solution.py:1231
  116.4 50.5 %collective-permute-start.17 = (bf16[512,1536]{1,0:T(8,128)(2,1)}, bf16[512,1536]{1,0:T(8,128)(2,1)}, u32[]{:S(2)}, u32[]{:S(2)}) collective-permute-start(bf16[512,1536]{1,0:T(8,128)(2,1)} %cotangent.1), channel_id=1, source_target_pairs={{0,8},{4,12},{8,0},{12,4},{16,24},{20,28},{24,16},{28,20},{1,9},{5... | collective-permute-start | bytes 4718600 | tf_op jit(solution)/shard_map/ppermute | solution.py:1231
  117.2 49.7 %collective-permute-start.18 = (bf16[512,1536]{1,0:T(8,128)(2,1)}, bf16[512,1536]{1,0:T(8,128)(2,1)}, u32[]{:S(2)}, u32[]{:S(2)}) collective-permute-start(bf16[512,1536]{1,0:T(8,128)(2,1)} %cotangent.1), channel_id=1, source_target_pairs={{0,16},{4,20},{8,24},{12,28},{16,0},{20,4},{24,8},{28,12},{1,17},{... | collective-permute-start | bytes 4718600 | tf_op jit(solution)/shard_map/ppermute | solution.py:1231
  147.4 15.9 %collective-permute-start.16 = (bf16[512,512]{1,0:T(8,128)(2,1)}, bf16[512,512]{1,0:T(8,128)(2,1)S(1)}, u32[]{:S(2)}, u32[]{:S(2)}) collective-permute-start(bf16[512,512]{1,0:T(8,128)(2,1)} %get-tuple-element.152.own), channel_id=1, source_target_pairs={{1,0},{3,2},{5,4},{7,6},{9,8},{11,10},{13,12},{15,14},{17,16},{19,... | collective-permute-start | bytes 1572872 | tf_op jit(solution)/shard_map/ppermute | solution.py:1386
  163.3 43.1 %collective-permute-start.32 = (bf16[576,1536]{1,0:T(8,128)(2,1)S(1)}, bf16[576,1536]{1,0:T(8,128)(2,1)}, u32[]{:S(2)}, u32[]{:S(2)}) collective-permute-start(bf16[576,1536]{1,0:T(8,128)(2,1)S(1)} %copy-done.10), channel_id=1, source_target_pairs={{0,3},{3,0},{4,7},{7,4},{8,11},{11,8},{12,15},{15,12},{16,19},{19,... | collective-permute-start | bytes 5308424 | tf_op jit(solution)/shard_map/ppermute | solution.py:1186
  166.9 25.6 %collective-permute-start.21 = (bf16[512,1536]{1,0:T(8,128)(2,1)}, bf16[512,1536]{1,0:T(8,128)(2,1)}, u32[]{:S(2)}, u32[]{:S(2)}) collective-permute-start(bf16[512,1536]{1,0:T(8,128)(2,1)} %collective-permute-done.17.rest_2_), channel_id=1, source_target_pairs={{0,4},{4,0},{8,12},{12,8},{16,20},{20,16},{24,28},{28,24},{1,5},{5... | collective-permute-start | bytes 4718600 | tf_op jit(solution)/shard_map/ppermute | solution.py:1231
  167.0 25.6 %collective-permute-start.22 = (bf16[512,1536]{1,0:T(8,128)(2,1)}, bf16[512,1536]{1,0:T(8,128)(2,1)}, u32[]{:S(2)}, u32[]{:S(2)}) collective-permute-start(bf16[512,1536]{1,0:T(8,128)(2,1)} %collective-permute-done.18.rest_4_), channel_id=1, source_target_pairs={{0,4},{4,0},{8,12},{12,8},{16,20},{20,16},{24,28},{28,24},{1,5},{5... | collective-permute-start | bytes 4718600 | tf_op jit(solution)/shard_map/ppermute | solution.py:1231
  169.5 19.8 %collective-permute-start.19 = (bf16[256,1536]{1,0:T(8,128)(2,1)}, bf16[256,1536]{1,0:T(8,128)(2,1)}, u32[]{:S(2)}, u32[]{:S(2)}) collective-permute-start(bf16[256,1536]{1,0:T(8,128)(2,1)} %slice.175), channel_id=1, source_target_pairs={{0,16},{4,20},{8,24},{12,28},{16,0},{20,4},{24,8},{28,12},{1,17},{... | collective-permute-start | bytes 2359304 | tf_op jit(solution)/shard_map/ppermute | solution.py:1231
  172.1 19.5 %collective-permute-start.20 = (bf16[256,1536]{1,0:T(8,128)(2,1)}, bf16[256,1536]{1,0:T(8,128)(2,1)S(1)}, u32[]{:S(2)}, u32[]{:S(2)}) collective-permute-start(bf16[256,1536]{1,0:T(8,128)(2,1)} %slice.176), channel_id=1, source_target_pairs={{0,8},{4,12},{8,0},{12,4},{16,24},{20,28},{24,16},{28,20},{1,9},{5... | collective-permute-start | bytes 2359304 | tf_op jit(solution)/shard_map/ppermute | solution.py:1231
  206.5 349.8 %reduce-scatter.3.cloned.1.call-start = ((), (), s32[]{:S(2)}) async-start(), calls=%async_computation.2 | async-start | bytes 8847360 | tf_op jit(solution)/shard_map/reduce_scatter | solution.py:1473
  210.2 19.1 %collective-permute-start.26 = (bf16[512,1536]{1,0:T(8,128)(2,1)S(1)}, bf16[512,1536]{1,0:T(8,128)(2,1)}, u32[]{:S(2)}, u32[]{:S(2)}) collective-permute-start(bf16[512,1536]{1,0:T(8,128)(2,1)S(1)} %copy-done.16), channel_id=1, source_target_pairs={{0,4},{4,0},{8,12},{12,8},{16,20},{20,16},{24,28},{28,24},{1,5},{5... | collective-permute-start | bytes 4718600 | tf_op jit(solution)/shard_map/ppermute | solution.py:1231
  211.4 36.5 %collective-permute-start.23 = (bf16[512,1536]{1,0:T(8,128)(2,1)S(1)}, bf16[512,1536]{1,0:T(8,128)(2,1)}, u32[]{:S(2)}, u32[]{:S(2)}) collective-permute-start(bf16[512,1536]{1,0:T(8,128)(2,1)S(1)} %copy-done.16), channel_id=1, source_target_pairs={{0,8},{4,12},{8,0},{12,4},{16,24},{20,28},{24,16},{28,20},{1,9},{5... | collective-permute-start | bytes 4718600 | tf_op jit(solution)/shard_map/ppermute | solution.py:1231
  212.7 36.2 %collective-permute-start.24 = (bf16[512,1536]{1,0:T(8,128)(2,1)S(1)}, bf16[512,1536]{1,0:T(8,128)(2,1)S(1)}, u32[]{:S(2)}, u32[]{:S(2)}) collective-permute-start(bf16[512,1536]{1,0:T(8,128)(2,1)S(1)} %copy-done.16), channel_id=1, source_target_pairs={{0,16},{4,20},{8,24},{12,28},{16,0},{20,4},{24,8},{28,12},{1,17},{... | collective-permute-start | bytes 4718600 | tf_op jit(solution)/shard_map/ppermute | solution.py:1231
  248.8 15.0 %collective-permute-start.29 = (bf16[512,1536]{1,0:T(8,128)(2,1)S(1)}, bf16[512,1536]{1,0:T(8,128)(2,1)S(1)}, u32[]{:S(2)}, u32[]{:S(2)}) collective-permute-start(bf16[512,1536]{1,0:T(8,128)(2,1)S(1)} %collective-permute-done.24.rows), channel_id=1, source_target_pairs={{0,4},{4,0},{8,12},{12,8},{16,20},{20,16},{24,28},{28,24},{1,5},{5... | collective-permute-start | bytes 4718600 | tf_op jit(solution)/shard_map/ppermute | solution.py:1231
  250.6 19.5 %collective-permute-start.27 = (bf16[256,1536]{1,0:T(8,128)(2,1)S(1)}, bf16[256,1536]{1,0:T(8,128)(2,1)S(1)}, u32[]{:S(2)}, u32[]{:S(2)}) collective-permute-start(bf16[256,1536]{1,0:T(8,128)(2,1)S(1)} %slice.179), channel_id=1, source_target_pairs={{0,16},{4,20},{8,24},{12,28},{16,0},{20,4},{24,8},{28,12},{1,17},{... | collective-permute-start | bytes 2359304 | tf_op jit(solution)/shard_map/ppermute | solution.py:1231
  251.2 19.1 %collective-permute-start.28 = (bf16[256,1536]{1,0:T(8,128)(2,1)S(1)}, bf16[256,1536]{1,0:T(8,128)(2,1)S(1)}, u32[]{:S(2)}, u32[]{:S(2)}) collective-permute-start(bf16[256,1536]{1,0:T(8,128)(2,1)S(1)} %slice.180), channel_id=1, source_target_pairs={{0,8},{4,12},{8,0},{12,4},{16,24},{20,28},{24,16},{28,20},{1,9},{5... | collective-permute-start | bytes 2359304 | tf_op jit(solution)/shard_map/ppermute | solution.py:1231
  324.9 326.0 %reduce-scatter.5.cloned.1.call-start = ((), (), s32[]{:S(2)}) async-start(), calls=%async_computation.3 | async-start | bytes 8847360 | tf_op jit(solution)/shard_map/reduce_scatter | solution.py:1503
  370.7 16.0 %collective-permute-start.34 = (bf16[4,544,1536]{2,1,0:T(8,128)(2,1)}, bf16[4,544,1536]{2,1,0:T(8,128)(2,1)S(1)}, u32[]{:S(2)}, u32[]{:S(2)}) collective-permute-start(bf16[4,544,1536]{2,1,0:T(8,128)(2,1)} %combine.7), channel_id=1, source_target_pairs={{0,4},{4,0},{8,12},{12,8},{16,20},{20,16},{24,28},{28,24},{1,5},{5... | collective-permute-start | bytes 20054024 | tf_op jit(solution)/shard_map/ppermute | solution.py:1231
  378.1 65.8 %collective-permute-start.33 = (bf16[4,512,1536]{2,1,0:T(8,128)(2,1)}, bf16[4,512,1536]{2,1,0:T(8,128)(2,1)}, u32[]{:S(2)}, u32[]{:S(2)}) collective-permute-start(bf16[4,512,1536]{2,1,0:T(8,128)(2,1)} %combine.5), channel_id=1, source_target_pairs={{0,4},{4,0},{8,12},{12,8},{16,20},{20,16},{24,28},{28,24},{1,5},{5... | collective-permute-start | bytes 18874376 | tf_op jit(solution)/shard_map/ppermute | solution.py:1231
  397.2 38.7 %collective-permute-start.35 = (bf16[2,272,1536]{2,1,0:T(8,128)(2,1)}, bf16[2,272,1536]{2,1,0:T(8,128)(2,1)S(1)}, u32[]{:S(2)}, u32[]{:S(2)}) collective-permute-start(bf16[2,272,1536]{2,1,0:T(8,128)(2,1)} %get-tuple-element.216), channel_id=1, source_target_pairs={{0,8},{4,12},{8,0},{12,4},{16,24},{20,28},{24,16},{28,20},{1,9},{5... | collective-permute-start | bytes 5013512 | tf_op jit(solution)/shard_map/ppermute | solution.py:1231
  398.7 38.4 %collective-permute-start.36 = (bf16[2,272,1536]{2,1,0:T(8,128)(2,1)}, bf16[2,272,1536]{2,1,0:T(8,128)(2,1)S(1)}, u32[]{:S(2)}, u32[]{:S(2)}) collective-permute-start(bf16[2,272,1536]{2,1,0:T(8,128)(2,1)} %get-tuple-element.217), channel_id=1, source_target_pairs={{0,16},{4,20},{8,24},{12,28},{16,0},{20,4},{24,8},{28,12},{1,17},{... | collective-permute-start | bytes 5013512 | tf_op jit(solution)/shard_map/ppermute | solution.py:1231
  441.6 19.8 %collective-permute-start.37 = (bf16[272,1536]{1,0:T(8,128)(2,1)}, bf16[272,1536]{1,0:T(8,128)(2,1)}, u32[]{:S(2)}, u32[]{:S(2)}) collective-permute-start(bf16[272,1536]{1,0:T(8,128)(2,1)} %get-tuple-element.224), channel_id=1, source_target_pairs={{0,16},{4,20},{8,24},{12,28},{16,0},{20,4},{24,8},{28,12},{1,17},{... | collective-permute-start | bytes 2506760 | tf_op jit(solution)/shard_map/ppermute | solution.py:1231
  443.1 19.5 %collective-permute-start.38 = (bf16[272,1536]{1,0:T(8,128)(2,1)}, bf16[272,1536]{1,0:T(8,128)(2,1)}, u32[]{:S(2)}, u32[]{:S(2)}) collective-permute-start(bf16[272,1536]{1,0:T(8,128)(2,1)} %get-tuple-element.225), channel_id=1, source_target_pairs={{0,8},{4,12},{8,0},{12,4},{16,24},{20,28},{24,16},{28,20},{1,9},{5... | collective-permute-start | bytes 2506760 | tf_op jit(solution)/shard_map/ppermute | solution.py:1231
  462.7 49.7 %collective-permute-start.39 = (bf16[2,256,1536]{2,1,0:T(8,128)(2,1)}, bf16[2,256,1536]{2,1,0:T(8,128)(2,1)S(1)}, u32[]{:S(2)}, u32[]{:S(2)}) collective-permute-start(bf16[2,256,1536]{2,1,0:T(8,128)(2,1)} %get-tuple-element.228), channel_id=1, source_target_pairs={{0,8},{4,12},{8,0},{12,4},{16,24},{20,28},{24,16},{28,20},{1,9},{5... | collective-permute-start | bytes 4718600 | tf_op jit(solution)/shard_map/ppermute | solution.py:1231
  463.9 48.5 %collective-permute-start.40 = (bf16[2,256,1536]{2,1,0:T(8,128)(2,1)}, bf16[2,256,1536]{2,1,0:T(8,128)(2,1)S(1)}, u32[]{:S(2)}, u32[]{:S(2)}) collective-permute-start(bf16[2,256,1536]{2,1,0:T(8,128)(2,1)} %get-tuple-element.242), channel_id=1, source_target_pairs={{0,16},{4,20},{8,24},{12,28},{16,0},{20,4},{24,8},{28,12},{1,17},{... | collective-permute-start | bytes 4718600 | tf_op jit(solution)/shard_map/ppermute | solution.py:1231
  495.3 29.9 %collective-permute-start.43 = (bf16[512,512]{1,0:T(8,128)(2,1)}, bf16[512,512]{1,0:T(8,128)(2,1)}, u32[]{:S(2)}, u32[]{:S(2)}) collective-permute-start(bf16[512,512]{1,0:T(8,128)(2,1)} %convert_element_type.143), channel_id=1, source_target_pairs={{0,1},{2,3},{4,5},{6,7},{8,9},{10,11},{12,13},{14,15},{16,17},{18,... | collective-permute-start | bytes 1572872 | tf_op jit(solution)/shard_map/ppermute | solution.py:1520
  551.4 35.8 %collective-permute-start.45 = (bf16[2,416,896]{2,1,0:T(8,128)(2,1)}, bf16[2,416,896]{2,1,0:T(8,128)(2,1)S(1)}, u32[]{:S(2)}, u32[]{:S(2)}) collective-permute-start(bf16[2,416,896]{2,1,0:T(8,128)(2,1)} %get-tuple-element.251), channel_id=1, source_target_pairs={{0,8},{4,12},{8,0},{12,4},{16,24},{20,28},{24,16},{28,20},{1,9},{5... | collective-permute-start | bytes 4472840 | tf_op jit(solution)/shard_map/ppermute | solution.py:1231
  552.4 35.7 %collective-permute-start.46 = (bf16[2,416,896]{2,1,0:T(8,128)(2,1)}, bf16[2,416,896]{2,1,0:T(8,128)(2,1)S(1)}, u32[]{:S(2)}, u32[]{:S(2)}) collective-permute-start(bf16[2,416,896]{2,1,0:T(8,128)(2,1)} %get-tuple-element.256), channel_id=1, source_target_pairs={{0,16},{4,20},{8,24},{12,28},{16,0},{20,4},{24,8},{28,12},{1,17},{... | collective-permute-start | bytes 4472840 | tf_op jit(solution)/shard_map/ppermute | solution.py:1231
  555.8 49.3 %collective-permute-start.41 = (bf16[256,1536]{1,0:T(8,128)(2,1)}, bf16[256,1536]{1,0:T(8,128)(2,1)}, u32[]{:S(2)}, u32[]{:S(2)}) collective-permute-start(bf16[256,1536]{1,0:T(8,128)(2,1)} %get-tuple-element.243), channel_id=1, source_target_pairs={{0,16},{4,20},{8,24},{12,28},{16,0},{20,4},{24,8},{28,12},{1,17},{... | collective-permute-start | bytes 2359304 | tf_op jit(solution)/shard_map/ppermute | solution.py:1231
  558.3 50.4 %collective-permute-start.42 = (bf16[256,1536]{1,0:T(8,128)(2,1)S(1)}, bf16[256,1536]{1,0:T(8,128)(2,1)S(1)}, u32[]{:S(2)}, u32[]{:S(2)}) collective-permute-start(bf16[256,1536]{1,0:T(8,128)(2,1)S(1)} %copy-done.58), channel_id=1, source_target_pairs={{0,8},{4,12},{8,0},{12,4},{16,24},{20,28},{24,16},{28,20},{1,9},{5... | collective-permute-start | bytes 2359304 | tf_op jit(solution)/shard_map/ppermute | solution.py:1231
  592.5 27.3 %collective-permute-start.47 = (bf16[416,896]{1,0:T(8,128)(2,1)}, bf16[416,896]{1,0:T(8,128)(2,1)S(1)}, u32[]{:S(2)}, u32[]{:S(2)}) collective-permute-start(bf16[416,896]{1,0:T(8,128)(2,1)} %get-tuple-element.260), channel_id=1, source_target_pairs={{0,16},{4,20},{8,24},{12,28},{16,0},{20,4},{24,8},{28,12},{1,17},{... | collective-permute-start | bytes 2236424 | tf_op jit(solution)/shard_map/ppermute | solution.py:1231
  607.6 16.4 %collective-permute-start.48 = (bf16[416,896]{1,0:T(8,128)(2,1)S(1)}, bf16[416,896]{1,0:T(8,128)(2,1)S(1)}, u32[]{:S(2)}, u32[]{:S(2)}) collective-permute-start(bf16[416,896]{1,0:T(8,128)(2,1)S(1)} %copy-done.59), channel_id=1, source_target_pairs={{0,8},{4,12},{8,0},{12,4},{16,24},{20,28},{24,16},{28,20},{1,9},{5... | collective-permute-start | bytes 2236424 | tf_op jit(solution)/shard_map/ppermute | solution.py:1231
  638.5 22.3 %collective-permute-start.50 = (bf16[208,896]{1,0:T(8,128)(2,1)S(1)}, bf16[208,896]{1,0:T(8,128)(2,1)S(1)}, u32[]{:S(2)}, u32[]{:S(2)}) collective-permute-start(bf16[208,896]{1,0:T(8,128)(2,1)S(1)} %get-tuple-element.287), channel_id=1, source_target_pairs={{0,1},{1,2},{2,3},{4,5},{5,6},{6,7},{8,9},{9,10},{10,11},{12,13},{... | collective-permute-start | bytes 1118216 | tf_op jit(solution)/shard_map/ppermute | solution.py:1222
  642.2 18.7 %collective-permute-start.51 = (bf16[208,896]{1,0:T(8,128)(2,1)S(1)}, bf16[208,896]{1,0:T(8,128)(2,1)S(1)}, u32[]{:S(2)}, u32[]{:S(2)}) collective-permute-start(bf16[208,896]{1,0:T(8,128)(2,1)S(1)} %get-tuple-element.286), channel_id=1, source_target_pairs={{1,0},{2,1},{3,2},{5,4},{6,5},{7,6},{9,8},{10,9},{11,10},{13,12},{... | collective-permute-start | bytes 1118216 | tf_op jit(solution)/shard_map/ppermute | solution.py:1223
  643.5 17.4 %collective-permute-start.52 = (bf16[208,896]{1,0:T(8,128)(2,1)S(1)}, bf16[208,896]{1,0:T(8,128)(2,1)S(1)}, u32[]{:S(2)}, u32[]{:S(2)}) collective-permute-start(bf16[208,896]{1,0:T(8,128)(2,1)S(1)} %get-tuple-element.264), channel_id=1, source_target_pairs={{0,3},{3,0},{4,7},{7,4},{8,11},{11,8},{12,15},{15,12},{16,19},{19,... | collective-permute-start | bytes 1118216 | tf_op jit(solution)/shard_map/ppermute | solution.py:1186
  (69 other events, 497.1 us)
Sparse Core Ops, SparseCore 0:
  206.6 125.5 all-gather.2
  334.5 121.7 reduce-scatter.2
  462.8 130.0 reduce-scatter.4

commit v16 on v15

--- a/solution.py
+++ b/solution.py
@@ -1326,7 +1326,7 @@
         packed_second = send_over(packed)
         first_block = after(shard_blocks[0], *packed_near)
         first_near = send_near(first_block)
-        first_second = send_second(first_block, first_near)
+        first_far = send_far(first_block)
         own = jnp.stack(slot_list(packed, packed_near, packed_second, packed_far))
         own = after(own, info, cosine, sine)
         beside, across = flip(own, 2), flip(own, 4)
@@ -1380,7 +1380,7 @@
         router_all.reshape(row_count, col_count, router_part, depth), (1, 2, 0, 3)
     ).reshape(expert_total, D)
     router_cols = router_rows.T
-    tokens_in = after(tokens, first_second, chosen) if fast else tokens
+    tokens_in = after(tokens, first_far, chosen) if fast else tokens
     normed, own_pair = key_value(info, tokens_in, attention_scale, cosine, sine, pair_refs)
     pairs = [(i + 1, i) for i in range(0, col_count, 2)]
     partner = lax.ppermute(own_pair, "cols", pairs)
@@ -1391,7 +1391,7 @@
         normed_in = normed
     queries = query(info, normed_in, cosine, sine, query_refs)
     if fast:
-        first_far = send_far(after(first_block, partner, queries))
+        first_second = send_second(after(first_block, partner, queries), first_near)
         expert_refs.append([first_block, first_second, *first_near, first_far])
     if fast:
         grad_flips = after(grad_flips, queries)
@@ -1409,8 +1409,8 @@
 
     if fast:
         beside, across = flip(normed_two, 2), flip(normed_two, 4)
-        beside_in = flip(after(normed_two, *grad_blocks), 1)
-        later_block = after(shard_blocks[1], first_far, normed_two)
+        beside_in = flip(normed_two, 1)
+        later_block = after(shard_blocks[1], first_second, normed_two)
         expert_refs.append([lax.all_gather(later_block, "cols", axis=0)])
     else:
         rows_all = lax.all_gather(normed_two, "rows", axis=0)
@@ -1523,14 +1523,8 @@
         keep_send = weight_grads(
             info, [normed, heads], [grad_query, grad_branch], parts, extra
         )
-        near_x, near_y = out_first[2:]
-        for_y, for_x = corner_adds(
-            near_x, after(out_flips[0], *keep_send), near_y, out_flips[1]
-        )
-        mixture = (near_x, out_flips[0], flip(for_y, 4))
-        mixture += (near_y, out_flips[1], flip(for_x, 2))
-        query_back = normed_grad(info, after(grad_query, for_y), query_refs)
-        arrived = after(arrived, query_back)
+        query_back = normed_grad(info, after(grad_query, *keep_send), query_refs)
+        arrived = after(arrived, query_back, *out_flips)
     else:
         query_back = normed_grad(info, grad_query, query_refs)
     grad_pair = join_grads(info, own_grad, source_grad, arrived, cosine, sine)
@@ -1550,6 +1544,8 @@
     if fast:
         sent_chips = after(sent_chips, tokens_grad)
         sent_parts = chips_second(*sent_first[2:], *sent_chips)
+        near_x, near_y = out_first[2:]
+        mixture = chips_second(near_x, near_y, *after(out_flips, *sent_chips))
     layer_output = (residual + sum_parts(mixture)).astype(LOW)
     part = down_weight.shape[1]
     expert_sums = [block.astype(WIDE) for block in reduced]

time: 683 us -> 685 us (level)
  starting transfers between devices: 84.1 us -> 91.9 us
    ppermute x1, waiting for transfers between devices: 10.5 us -> 0.8 us  [send_second(): return lax.ppermute(payload, 'cols', [(3, 1), (1, 0), (0, 2), (2, 3)])]
    ppermute x3, waiting for transfers between devices: 5.81 us -> 13.7 us  [send_far(): return lax.ppermute(block, 'cols', FAR)]
    ppermute x3, starting transfers between devices: 14.6 us -> 22.5 us  [send_far(): return lax.ppermute(block, 'cols', FAR)]
    unnamed x133 -> x125, local copies, waits for them, and re-layouts: 28.4 us -> 24.3 us
  transfers between devices with their start and end apart: 56 -> 56, of which waited for: 27 -> 28; matrix products, arithmetic and copies ran while one was open for 8% -> 8% of each run, Pallas kernels for 45% -> 45%
where the time goes in v16:
time: 685 us; the launch traced here: 674 us
  Pallas kernels  303 us (44%)
  waiting for transfers between devices  183 us (27%)
  starting transfers between devices  91.9 us (13%)
  local copies, waits for them, and re-layouts  47.7 us (7%)
  other arithmetic  32.9 us (5%)
  between operations  14.9 us (2%)
    ppermute x39, waiting for transfers between devices, flip(): return lax.ppermute(block, 'rows', [(i, i ^ bit) for i in range(count)])  147 us
    pallas_call x2, Pallas kernels, expert(): pl.pallas_call(functools.partial(expert_kernel, slots), grid=(height // E...  61 us
    pallas_call x4, Pallas kernels, combine(): pl.pallas_call(functools.partial(combine_kernel, local, first, step), out...  30.9 us
    pallas_call x2, Pallas kernels, expert_grads(): pl.pallas_call(expert_grads_kernel, grid=(D // 256,), out_shape=jax.Shape...  29.2 us
    pallas_call x8, Pallas kernels, dispatch(): pl.pallas_call(functools.partial(dispatch_kernel, local), grid=(D // wide...  29 us
    ppermute x39, starting transfers between devices, flip(): return lax.ppermute(block, 'rows', [(i, i ^ bit) for i in range(count)])  28.6 us
    ppermute x4, starting transfers between devices, send_near(): return (lax.ppermute(block, 'cols', DOWN), lax.ppermute(block, 'cols', UP))  28.4 us
    unnamed x125, local copies, waits for them, and re-layouts  24.3 us
  transfers between devices with their start and end apart: 56, of which 28 were waited for; matrix products, arithmetic and copies ran while one was open for 8% of the time, Pallas kernels for 45%

profile of v16, /device:TPU:0, one launch (start us, length us, event | category | flops | bytes accessed | tf_op | source)
XLA Modules:
  0.0 674.2 jit_solution(4155468002304223327)
XLA Ops:
  14.1 6.3 collective-permute-start.1
  32.3 19.4 %collective-permute-start.9 = (bf16[576,1536]{1,0:T(8,128)(2,1)}, bf16[576,1536]{1,0:T(8,128)(2,1)}, u32[]{:S(2)}, u32[]{:S(2)}) collective-permute-start(bf16[576,1536]{1,0:T(8,128)(2,1)} %pad_maximum_fusion.3.rest_0_), channel_id=1, source_target_pairs={{0,1},{1,2},{2,3},{4,5},{5,6},{6,7},{8,9},{9,10},{10,11},{12,13},{... | collective-permute-start | bytes 5308424 | tf_op jit(solution)/shard_map/ppermute | solution.py:1182
  57.4 31.8 %collective-permute-done.6.rest_2_.rest_8_ = bf16[4,208,896]{2,1,0:T(8,128)(2,1)S(1)} collective-permute-done((bf16[4,208,896]{2,1,0:T(8,128)(2,1)S(1)}, bf16[4,208,896]{2,1,0:T(8,128)(2,1)S(1)}, u32[]{:S(2)}, u32[]{:S(2)}) %collective-permute-start.6) | collective-permute-done | bytes 1490976 | tf_op jit(solution)/shard_map/ppermute | solution.py:1231
  93.1 6.8 %collective-permute-start.2 = (bf16[576,1536]{1,0:T(8,128)(2,1)}, bf16[576,1536]{1,0:T(8,128)(2,1)}, u32[]{:S(2)}, u32[]{:S(2)}) collective-permute-start(bf16[576,1536]{1,0:T(8,128)(2,1)} %pad_maximum_fusion.3.rest_0_), channel_id=1, source_target_pairs={{0,3},{3,0},{4,7},{7,4},{8,11},{11,8},{12,15},{15,12},{16,19},{19,... | collective-permute-start | bytes 5308424 | tf_op jit(solution)/shard_map/ppermute | solution.py:1186
  99.9 10.1 %collective-permute-done.11.rest_4_.rest_10_ = bf16[2,208,896]{2,1,0:T(8,128)(2,1)S(1)} collective-permute-done((bf16[2,208,896]{2,1,0:T(8,128)(2,1)S(1)}, bf16[2,208,896]{2,1,0:T(8,128)(2,1)S(1)}, u32[]{:S(2)}, u32[]{:S(2)}) %collective-permute-start.11) | collective-permute-done | bytes 745504 | tf_op jit(solution)/shard_map/ppermute | solution.py:1231
  112.5 4.4 collective-permute-done.12.rest_7_.rest_13_
  118.1 5.6 route_tables.1
  129.1 9.7 %collective-permute-done.2.rest_4_ = bf16[576,1536]{1,0:T(8,128)(2,1)} collective-permute-done((bf16[576,1536]{1,0:T(8,128)(2,1)}, bf16[576,1536]{1,0:T(8,128)(2,1)}, u32[]{:S(2)}, u32[]{:S(2)}) %collective-permute-start.2) | collective-permute-done | bytes 1769504 | tf_op jit(solution)/shard_map/ppermute | solution.py:1186
  138.8 5.0 norm_key_value.1
  145.2 8.2 %query_projection.1.queries = bf16[512,1536]{1,0:T(8,128)(2,1)} custom-call(s32[16]{0:T(128)} %concatenate.42.info, bf16[512,1536]{1,0:T(8,128)(2,1)} %get-tuple-element.151.normed.rest_0_, f32[512,128]{1,0:T(8,128)} %get-tuple-element.310.cosine, f32[512,128]{1,0:T(8,128)} %get-tuple-element.311.sine, bf16[4,208,896]{2,1,0:T(8,128)(2,1)} %copy-done.1, ...), custom_call_target="tpu_custom_call" | custom-call | flops 1 | bytes 1 | tf_op jit(solution)/shard_map/query_projection/pallas_call | solution.py:195
  153.4 5.9 collective-permute-done.16.partner
  171.2 11.0 %tree_attention.1.heads.rest_1_ = bf16[512,1536]{1,0:T(8,128)(2,1)} custom-call(s32[16]{0:T(128)} %concatenate.42.info, bf16[512,1536]{1,0:T(8,128)(2,1)} %query_projection.1.queries, bf16[512,512]{1,0:T(8,128)(2,1)} %get-tuple-element.152.own, bf16[512,512]{1,0:T(8,128)(2,1)} %collective-permute-done.16.partner), custom_call_target="tpu_custom_call" | custom-call | flops 1 | bytes 1 | tf_op jit(solution)/shard_map/tree_attention/pallas_call | solution.py:277
  190.8 9.9 %out_projection.1 = (f32[512,1536]{1,0:T(8,128)}, bf16[512,1536]{1,0:T(8,128)(2,1)}) custom-call(s32[16]{0:T(128)} %concatenate.42.info, bf16[512,1536]{1,0:T(8,128)(2,1)} %tree_attention.1.heads.rest_1_, bf16[512,1536]{1,0:T(8,128)(2,1)} %tokens.4, f32[1,1536]{1,0:T(1,128)} %reshape.303.gain, bf16[4,208,896]{2,1,0:T(8,128)(2,1)} %copy-done.1, ...), custom_call_target="tpu_custom_call" | custom-call | flops 1 | bytes 1 | tf_op jit(solution)/shard_map/out_projection/pallas_call | solution.py:389
  208.3 3.9 dispatch.8
  212.3 9.4 %pick_rows.1 = (bf16[8,160,1536]{2,1,0:T(8,128)(2,1)}, bf16[8,160,1536]{2,1,0:T(8,128)(2,1)}) custom-call(bf16[8,320,512]{2,1,0:T(8,128)(2,1)} %get-tuple-element.147.chosen, bf16[512,1536]{1,0:T(8,128)(2,1)} %cotangent.1, bf16[512,1536]{1,0:T(8,128)(2,1)} %collective-permute-done.15.rest_1_, bf16[512,1536]{1,0:T(8,128)(2,1)} %copy-done.19, ...), custom_call_target="tpu_custom_call" | custom-call | flops 1 | bytes 1 | tf_op jit(solution)/shard_map/pick_rows/pallas_call | solution.py:480
  221.7 3.6 dispatch.9
  225.2 13.8 %collective-permute-done.23.rows = bf16[512,1536]{1,0:T(8,128)(2,1)} collective-permute-done((bf16[512,1536]{1,0:T(8,128)(2,1)S(1)}, bf16[512,1536]{1,0:T(8,128)(2,1)}, u32[]{:S(2)}, u32[]{:S(2)}) %collective-permute-start.23) | collective-permute-done | bytes 1572896 | tf_op jit(solution)/shard_map/ppermute | solution.py:1231
  245.2 3.6 dispatch.10
  248.9 3.6 dispatch.11
  253.6 3.6 dispatch.12
  273.4 30.8 %expert.2 = (bf16[1280,1536]{1,0:T(8,128)(2,1)}, bf16[1280,1536]{1,0:T(8,128)(2,1)}, bf16[1280,1536]{1,0:T(8,128)(2,1)}, bf16[4,576,1280]{2,1,0:T(8,128)(2,1)}, f32[1280,1]{1,0:T(8,128)}) custom-call(s32[16]{0:T(128)} %concatenate.42.info, bf16[1280,1536]{1,0:T(8,128)(2,1)} %bitcast.151, bf16[1280,1536]{1,0:T(8,128)(2,1)} %bitcast.170, f32[1280,1]{1,0:T(8,128)} %bitcast.155, ...), custom_call_target="tpu_custom_call" | custom-call | flops 1 | bytes 1 | tf_op jit(solution)/shard_map/expert/pallas_call | solution.py:670
  304.2 14.6 %expert_gradients.2 = bf16[4,576,1536]{2,1,0:T(8,128)(2,1)} custom-call(bf16[4,576,1280]{2,1,0:T(8,128)(2,1)} %get-tuple-element.201.acts, bf16[1280,1536]{1,0:T(8,128)(2,1)} %bitcast.152, bf16[1280,1536]{1,0:T(8,128)(2,1)} %get-tuple-element.202.grads), custom_call_target="tpu_custom_call" | custom-call | flops 1 | bytes 1 | tf_op jit(solution)/shard_map/expert_gradients/pallas_call | solution.py:699
  318.9 10.0 %all-gather.3.cloned.1.call-done = bf16[2304,1536]{1,0:T(8,128)(2,1)} async-done(((bf16[576,1536]{1,0:T(8,128)(2,1)}), bf16[2304,1536]{1,0:T(8,128)(2,1)}) %all-gather.3.cloned.1.call-update) | async-done | bytes 7077904 | tf_op jit(solution)/shard_map/all_gather | solution.py:1414
  328.9 30.2 %expert.3 = (bf16[1280,1536]{1,0:T(8,128)(2,1)}, bf16[1280,1536]{1,0:T(8,128)(2,1)}, bf16[1280,1536]{1,0:T(8,128)(2,1)}, bf16[4,576,1280]{2,1,0:T(8,128)(2,1)}, f32[1280,1]{1,0:T(8,128)}) custom-call(s32[16]{0:T(128)} %concatenate.42.info, bf16[1280,1536]{1,0:T(8,128)(2,1)} %bitcast.153, bf16[1280,1536]{1,0:T(8,128)(2,1)} %bitcast.171, f32[1280,1]{1,0:T(8,128)} %bitcast.156, ...), custom_call_target="tpu_custom_call" | custom-call | flops 1 | bytes 1 | tf_op jit(solution)/shard_map/expert/pallas_call | solution.py:670
  359.1 8.0 %combine.7 = bf16[4,544,1536]{2,1,0:T(8,128)(2,1)} custom-call(s32[16]{0:T(128)} %concatenate.42.info, bf16[8,320,512]{2,1,0:T(8,128)(2,1)} %get-tuple-element.147.chosen, bf16[8,160,1536]{2,1,0:T(8,128)(2,1)} %bitcast.162, bf16[8,160,1536]{2,1,0:T(8,128)(2,1)} %bitcast.166, f32[8,160,1]{2,1,0:T(8,128)} %bitcast.172, f32[8,160,1]{2,1,0:T(8,128)} %bitcast.174), custom_call_target="tpu_custom_call" | custom-call | flops 1 | bytes 1 | tf_op jit(solution)/shard_map/combine/pallas_call | solution.py:762
  367.3 7.3 %combine.5 = bf16[4,512,1536]{2,1,0:T(8,128)(2,1)} custom-call(s32[16]{0:T(128)} %concatenate.42.info, bf16[8,320,512]{2,1,0:T(8,128)(2,1)} %get-tuple-element.147.chosen, bf16[8,160,1536]{2,1,0:T(8,128)(2,1)} %bitcast.160, bf16[8,160,1536]{2,1,0:T(8,128)(2,1)} %bitcast.164), custom_call_target="tpu_custom_call" | custom-call | flops 1 | bytes 1 | tf_op jit(solution)/shard_map/combine/pallas_call | solution.py:762
  375.1 8.1 %combine.6.keep = bf16[4,544,1536]{2,1,0:T(8,128)(2,1)} custom-call(s32[16]{0:T(128)} %concatenate.42.info, bf16[8,320,512]{2,1,0:T(8,128)(2,1)} %get-tuple-element.147.chosen, bf16[8,160,1536]{2,1,0:T(8,128)(2,1)} %bitcast.163, bf16[8,160,1536]{2,1,0:T(8,128)(2,1)} %bitcast.167, f32[8,160,1]{2,1,0:T(8,128)} %bitcast.173, f32[8,160,1]{2,1,0:T(8,128)} %bitcast.175), custom_call_target="tpu_custom_call" | custom-call | flops 1 | bytes 1 | tf_op jit(solution)/shard_map/combine/pallas_call | solution.py:762
  386.0 7.8 %chip_sums.4 = (bf16[2,272,1536]{2,1,0:T(8,128)(2,1)}, bf16[2,272,1536]{2,1,0:T(8,128)(2,1)}, bf16[2,272,1536]{2,1,0:T(8,128)(2,1)}, bf16[2,272,1536]{2,1,0:T(8,128)(2,1)}) custom-call(bf16[4,544,1536]{2,1,0:T(8,128)(2,1)} %combine.6.keep, bf16[4,544,1536]{2,1,0:T(8,128)(2,1)} %copy-done.10), custom_call_target="tpu_custom_call" | custom-call | flops 1 | bytes 1 | tf_op jit(solution)/shard_map/chip_sums/pallas_call | solution.py:811
  396.7 7.5 %combine.4.keep = bf16[4,512,1536]{2,1,0:T(8,128)(2,1)} custom-call(s32[16]{0:T(128)} %concatenate.42.info, bf16[8,320,512]{2,1,0:T(8,128)(2,1)} %get-tuple-element.147.chosen, bf16[8,160,1536]{2,1,0:T(8,128)(2,1)} %bitcast.161, bf16[8,160,1536]{2,1,0:T(8,128)(2,1)} %bitcast.165), custom_call_target="tpu_custom_call" | custom-call | flops 1 | bytes 1 | tf_op jit(solution)/shard_map/combine/pallas_call | solution.py:762
  404.2 14.6 %expert_gradients.3 = bf16[4,576,1536]{2,1,0:T(8,128)(2,1)} custom-call(bf16[4,576,1280]{2,1,0:T(8,128)(2,1)} %get-tuple-element.218.acts, bf16[1280,1536]{1,0:T(8,128)(2,1)} %bitcast.154, bf16[1280,1536]{1,0:T(8,128)(2,1)} %get-tuple-element.219.grads), custom_call_target="tpu_custom_call" | custom-call | flops 1 | bytes 1 | tf_op jit(solution)/shard_map/expert_gradients/pallas_call | solution.py:699
  418.9 13.6 %collective-permute-done.35.got_x.rest_1_ = bf16[2,272,1536]{2,1,0:T(8,128)(2,1)S(1)} collective-permute-done((bf16[2,272,1536]{2,1,0:T(8,128)(2,1)}, bf16[2,272,1536]{2,1,0:T(8,128)(2,1)S(1)}, u32[]{:S(2)}, u32[]{:S(2)}) %collective-permute-start.35) | collective-permute-done | bytes 1671200 | tf_op jit(solution)/shard_map/ppermute | solution.py:1231
  440.4 7.5 %chip_sums.3 = (bf16[2,256,1536]{2,1,0:T(8,128)(2,1)}, bf16[2,256,1536]{2,1,0:T(8,128)(2,1)}, bf16[2,256,1536]{2,1,0:T(8,128)(2,1)}, bf16[2,256,1536]{2,1,0:T(8,128)(2,1)}) custom-call(bf16[4,512,1536]{2,1,0:T(8,128)(2,1)} %combine.4.keep, bf16[4,512,1536]{2,1,0:T(8,128)(2,1)} %collective-permute-done.33.got), custom_call_target="tpu_custom_call" | custom-call | flops 1 | bytes 1 | tf_op jit(solution)/shard_map/chip_sums/pallas_call | solution.py:811
  447.9 9.9 %collective-permute-done.37.rest_2_ = bf16[272,1536]{1,0:T(8,128)(2,1)S(1)} collective-permute-done((bf16[272,1536]{1,0:T(8,128)(2,1)}, bf16[272,1536]{1,0:T(8,128)(2,1)S(1)}, u32[]{:S(2)}, u32[]{:S(2)}) %collective-permute-start.37) | collective-permute-done | bytes 835616 | tf_op jit(solution)/shard_map/ppermute | solution.py:1231
  461.7 12.8 %experts_norm_back.1 = (f32[512,1536]{1,0:T(8,128)}, bf16[512,1536]{1,0:T(8,128)(2,1)}, bf16[512,1536]{1,0:T(8,128)(2,1)}, f32[1,1536]{1,0:T(1,128)}, f32[16,1536]{1,0:T(8,128)}) custom-call(s32[16]{0:T(128)} %concatenate.42.info, f32[512,1536]{1,0:T(8,128)} %get-tuple-element.156.residual, bf16[512,1536]{1,0:T(8,128)(2,1)} %get-tuple-element.157.rows.normed, ...), custom_call_target="tpu_custom_call" | custom-call | flops 1 | bytes 1 | tf_op jit(solution)/shard_map/experts_norm_back/pallas_call | solution.py:922
  474.5 15.4 %tree_attention_back.1 = (bf16[512,1536]{1,0:T(8,128)(2,1)}, f32[512,512]{1,0:T(8,128)}, f32[512,512]{1,0:T(8,128)}) custom-call(s32[16]{0:T(128)} %concatenate.42.info, bf16[512,1536]{1,0:T(8,128)(2,1)} %query_projection.1.queries, bf16[512,512]{1,0:T(8,128)(2,1)} %get-tuple-element.152.own, bf16[512,512]{1,0:T(8,128)(2,1)} %collective-permute-done.16.partner, ...), custom_call_target="tpu_custom_call" | custom-call | flops 1 | bytes 1 | tf_op jit(solution)/shard_map/tree_attention_back/pallas_call | solution.py:338
  494.0 13.7 %weight_gradients.2 = (bf16[4,4,208,896]{3,2,1,0:T(8,128)(2,1)}, bf16[4,4,208,896]{3,2,1,0:T(8,128)(2,1)}) custom-call(s32[16]{0:T(128)} %concatenate.42.info, bf16[512,1536]{1,0:T(8,128)(2,1)} %get-tuple-element.151.normed.rest_0_, bf16[512,1536]{1,0:T(8,128)(2,1)} %tree_attention.1.heads.rest_1_, bf16[512,1536]{1,0:T(8,128)(2,1)} %get-tuple-element.242.rest_2_.grad_query, ...), custom_call_target="tpu_custom_call" | custom-call | flops 1 | bytes 1 | tf_op jit(solution)/shard_map/weight_gradients/pallas_call | solution.py:1089
  507.7 7.9 %normed_gradient.1.query_part = f32[512,1536]{1,0:T(8,128)} custom-call(s32[16]{0:T(128)} %concatenate.42.info, bf16[512,1536]{1,0:T(8,128)(2,1)} %get-tuple-element.242.rest_2_.grad_query, bf16[4,208,896]{2,1,0:T(8,128)(2,1)} %copy-done.1, bf16[4,208,896]{2,1,0:T(8,128)(2,1)} %copy-done.5, bf16[4,208,896]{2,1,0:T(8,128)(2,1)} %copy-done.3, ...), custom_call_target="tpu_custom_call" | custom-call | flops 1 | bytes 1 | tf_op jit(solution)/shard_map/normed_gradient/pallas_call | solution.py:999
  519.5 5.7 weight_gradients.3
  525.2 9.9 %collective-permute-done.42 = bf16[4,4,208,896]{3,2,1,0:T(8,128)(2,1)S(1)} collective-permute-done((bf16[4,4,208,896]{3,2,1,0:T(8,128)(2,1)}, bf16[4,4,208,896]{3,2,1,0:T(8,128)(2,1)S(1)}, u32[]{:S(2)}, u32[]{:S(2)}) %collective-permute-start.42) | collective-permute-done | bytes 5963808 | tf_op jit(solution)/shard_map/ppermute | solution.py:1231
  537.7 7.2 %chip_sums.5 = (bf16[2,416,896]{2,1,0:T(8,128)(2,1)}, bf16[2,416,896]{2,1,0:T(8,128)(2,1)}, bf16[2,416,896]{2,1,0:T(8,128)(2,1)}, bf16[2,416,896]{2,1,0:T(8,128)(2,1)}) custom-call(bf16[4,832,896]{2,1,0:T(8,128)(2,1)} %bitcast.157, bf16[4,832,896]{2,1,0:T(8,128)(2,1)} %bitcast.169), custom_call_target="tpu_custom_call" | custom-call | flops 1 | bytes 1 | tf_op jit(solution)/shard_map/chip_sums/pallas_call | solution.py:811
  548.5 8.0 %token_gradient.1 = (bf16[512,1536]{1,0:T(8,128)(2,1)}, f32[1,1536]{1,0:T(1,128)}) custom-call(s32[16]{0:T(128)} %concatenate.42.info, f32[512,1536]{1,0:T(8,128)} %normed_gradient.1.query_part, bf16[512,512]{1,0:T(8,128)(2,1)} %join_key_value_gradients.1.rest_1_.grad_pair, bf16[512,1536]{1,0:T(8,128)(2,1)} %tokens.4, ...), custom_call_target="tpu_custom_call" | custom-call | flops 1 | bytes 1 | tf_op jit(solution)/shard_map/token_gradient/pallas_call | solution.py:1026
  556.5 23.5 %collective-permute-done.43.got_x = bf16[2,416,896]{2,1,0:T(8,128)(2,1)} collective-permute-done((bf16[2,416,896]{2,1,0:T(8,128)(2,1)}, bf16[2,416,896]{2,1,0:T(8,128)(2,1)}, u32[]{:S(2)}, u32[]{:S(2)}) %collective-permute-start.43) | collective-permute-done | bytes 1490976 | tf_op jit(solution)/shard_map/ppermute | solution.py:1231
  595.5 8.5 %collective-permute-done.47 = bf16[416,896]{1,0:T(8,128)(2,1)S(1)} collective-permute-done((bf16[416,896]{1,0:T(8,128)(2,1)}, bf16[416,896]{1,0:T(8,128)(2,1)S(1)}, u32[]{:S(2)}, u32[]{:S(2)}) %collective-permute-start.47) | collective-permute-done | bytes 745504 | tf_op jit(solution)/shard_map/ppermute | solution.py:1231
  612.5 6.8 %collective-permute-done.45 = bf16[256,1536]{1,0:T(8,128)(2,1)} collective-permute-done((bf16[256,1536]{1,0:T(8,128)(2,1)}, bf16[256,1536]{1,0:T(8,128)(2,1)}, u32[]{:S(2)}, u32[]{:S(2)}) %collective-permute-start.45) | collective-permute-done | bytes 786464 | tf_op jit(solution)/shard_map/ppermute | solution.py:1231
  624.9 5.8 collective-permute-done.49.rest_3_
  630.9 4.2 collective-permute-start.50
  636.4 12.7 %collective-permute-start.52 = (bf16[208,896]{1,0:T(8,128)(2,1)S(1)}, bf16[208,896]{1,0:T(8,128)(2,1)S(1)}, u32[]{:S(2)}, u32[]{:S(2)}) collective-permute-start(bf16[208,896]{1,0:T(8,128)(2,1)S(1)} %get-tuple-element.264), channel_id=1, source_target_pairs={{0,3},{3,0},{4,7},{7,4},{8,11},{11,8},{12,15},{15,12},{16,19},{19,... | collective-permute-start | bytes 1118216 | tf_op jit(solution)/shard_map/ppermute | solution.py:1186
  657.4 4.0 collective-permute-done.52.rest_2_
  (311 shorter events, 167.7 us)
Async XLA Ops:
  7.2 321.7 %all-gather.3.cloned.1.call-start = ((), (), s32[]{:S(2)}) async-start(), calls=%async_computation.4 | async-start | bytes 8847360 | tf_op jit(solution)/shard_map/all_gather | solution.py:1414
  12.7 18.4 %collective-permute-start = (bf16[208,896]{1,0:T(8,128)(2,1)S(1)}, bf16[208,896]{1,0:T(8,128)(2,1)S(1)}, u32[]{:S(2)}, u32[]{:S(2)}) collective-permute-start(bf16[208,896]{1,0:T(8,128)(2,1)S(1)} %concatenate.46), channel_id=1, source_target_pairs={{1,0},{2,1},{3,2},{5,4},{6,5},{7,6},{9,8},{10,9},{11,10},{13,12},{... | collective-permute-start | bytes 1118216 | tf_op jit(solution)/shard_map/ppermute | solution.py:1182
  14.1 17.0 %collective-permute-start.1 = (bf16[208,896]{1,0:T(8,128)(2,1)S(1)}, bf16[208,896]{1,0:T(8,128)(2,1)}, u32[]{:S(2)}, u32[]{:S(2)}) collective-permute-start(bf16[208,896]{1,0:T(8,128)(2,1)S(1)} %concatenate.46), channel_id=1, source_target_pairs={{0,1},{1,2},{2,3},{4,5},{5,6},{6,7},{8,9},{9,10},{10,11},{12,13},{... | collective-permute-start | bytes 1118216 | tf_op jit(solution)/shard_map/ppermute | solution.py:1182
  20.4 31.3 %collective-permute-start.4 = (bf16[208,896]{1,0:T(8,128)(2,1)S(1)}, bf16[208,896]{1,0:T(8,128)(2,1)}, u32[]{:S(2)}, u32[]{:S(2)}) collective-permute-start(bf16[208,896]{1,0:T(8,128)(2,1)S(1)} %concatenate.46), channel_id=1, source_target_pairs={{0,3},{3,0},{4,7},{7,4},{8,11},{11,8},{12,15},{15,12},{16,19},{19,... | collective-permute-start | bytes 1118216 | tf_op jit(solution)/shard_map/ppermute | solution.py:1186
  23.4 29.4 %collective-permute-start.3 = (bf16[208,896]{1,0:T(8,128)(2,1)S(1)}, bf16[208,896]{1,0:T(8,128)(2,1)}, u32[]{:S(2)}, u32[]{:S(2)}) collective-permute-start(bf16[208,896]{1,0:T(8,128)(2,1)S(1)} %concatenate.46), channel_id=1, source_target_pairs={{0,2},{1,3},{2,0},{3,1},{4,6},{5,7},{6,4},{7,5},{8,10},{9,11},{10,... | collective-permute-start | bytes 1118216 | tf_op jit(solution)/shard_map/ppermute | solution.py:1190
  31.0 59.3 %collective-permute-start.8 = (bf16[576,1536]{1,0:T(8,128)(2,1)}, bf16[576,1536]{1,0:T(8,128)(2,1)}, u32[]{:S(2)}, u32[]{:S(2)}) collective-permute-start(bf16[576,1536]{1,0:T(8,128)(2,1)} %pad_maximum_fusion.3.rest_0_), channel_id=1, source_target_pairs={{1,0},{2,1},{3,2},{5,4},{6,5},{7,6},{9,8},{10,9},{11,10},{13,12},{... | collective-permute-start | bytes 5308424 | tf_op jit(solution)/shard_map/ppermute | solution.py:1182
  32.3 58.1 %collective-permute-start.9 = (bf16[576,1536]{1,0:T(8,128)(2,1)}, bf16[576,1536]{1,0:T(8,128)(2,1)}, u32[]{:S(2)}, u32[]{:S(2)}) collective-permute-start(bf16[576,1536]{1,0:T(8,128)(2,1)} %pad_maximum_fusion.3.rest_0_), channel_id=1, source_target_pairs={{0,1},{1,2},{2,3},{4,5},{5,6},{6,7},{8,9},{9,10},{10,11},{12,13},{... | collective-permute-start | bytes 5308424 | tf_op jit(solution)/shard_map/ppermute | solution.py:1182
  54.1 35.1 %collective-permute-start.6 = (bf16[4,208,896]{2,1,0:T(8,128)(2,1)S(1)}, bf16[4,208,896]{2,1,0:T(8,128)(2,1)S(1)}, u32[]{:S(2)}, u32[]{:S(2)}) collective-permute-start(bf16[4,208,896]{2,1,0:T(8,128)(2,1)S(1)} %pad_maximum_fusion.5.rest_0_.rest_6_), channel_id=1, source_target_pairs={{0,8},{4,12},{8,0},{12,4},{16,24},{20,28},{24,16},{28,20},{1,9},{5... | collective-permute-start | bytes 4472840 | tf_op jit(solution)/shard_map/ppermute | solution.py:1231
  55.7 34.7 %collective-permute-start.7 = (bf16[4,208,896]{2,1,0:T(8,128)(2,1)S(1)}, bf16[4,208,896]{2,1,0:T(8,128)(2,1)S(1)}, u32[]{:S(2)}, u32[]{:S(2)}) collective-permute-start(bf16[4,208,896]{2,1,0:T(8,128)(2,1)S(1)} %pad_maximum_fusion.5.rest_0_.rest_6_), channel_id=1, source_target_pairs={{0,16},{4,20},{8,24},{12,28},{16,0},{20,4},{24,8},{28,12},{1,17},{... | collective-permute-start | bytes 4472840 | tf_op jit(solution)/shard_map/ppermute | solution.py:1231
  90.7 21.5 %collective-permute-start.10 = (bf16[8,208,896]{2,1,0:T(8,128)(2,1)S(1)}, bf16[8,208,896]{2,1,0:T(8,128)(2,1)S(1)}, u32[]{:S(2)}, u32[]{:S(2)}) collective-permute-start(bf16[8,208,896]{2,1,0:T(8,128)(2,1)S(1)} %pad_maximum_fusion), channel_id=1, source_target_pairs={{0,4},{4,0},{8,12},{12,8},{16,20},{20,16},{24,28},{28,24},{1,5},{5... | collective-permute-start | bytes 8945672 | tf_op jit(solution)/shard_map/ppermute | solution.py:1231
  90.9 19.1 %collective-permute-start.11 = (bf16[2,208,896]{2,1,0:T(8,128)(2,1)S(1)}, bf16[2,208,896]{2,1,0:T(8,128)(2,1)S(1)}, u32[]{:S(2)}, u32[]{:S(2)}) collective-permute-start(bf16[2,208,896]{2,1,0:T(8,128)(2,1)S(1)} %slice.170), channel_id=1, source_target_pairs={{0,16},{4,20},{8,24},{12,28},{16,0},{20,4},{24,8},{28,12},{1,17},{... | collective-permute-start | bytes 2236424 | tf_op jit(solution)/shard_map/ppermute | solution.py:1231
  92.5 18.9 %collective-permute-start.13 = (bf16[2,208,896]{2,1,0:T(8,128)(2,1)S(1)}, bf16[2,208,896]{2,1,0:T(8,128)(2,1)}, u32[]{:S(2)}, u32[]{:S(2)}) collective-permute-start(bf16[2,208,896]{2,1,0:T(8,128)(2,1)S(1)} %slice.173), channel_id=1, source_target_pairs={{0,8},{4,12},{8,0},{12,4},{16,24},{20,28},{24,16},{28,20},{1,9},{5... | collective-permute-start | bytes 2236424 | tf_op jit(solution)/shard_map/ppermute | solution.py:1231
  93.1 45.8 %collective-permute-start.2 = (bf16[576,1536]{1,0:T(8,128)(2,1)}, bf16[576,1536]{1,0:T(8,128)(2,1)}, u32[]{:S(2)}, u32[]{:S(2)}) collective-permute-start(bf16[576,1536]{1,0:T(8,128)(2,1)} %pad_maximum_fusion.3.rest_0_), channel_id=1, source_target_pairs={{0,3},{3,0},{4,7},{7,4},{8,11},{11,8},{12,15},{15,12},{16,19},{19,... | collective-permute-start | bytes 5308424 | tf_op jit(solution)/shard_map/ppermute | solution.py:1186
  111.4 33.8 %collective-permute-start.15 = (bf16[512,1536]{1,0:T(8,128)(2,1)S(1)}, bf16[512,1536]{1,0:T(8,128)(2,1)}, u32[]{:S(2)}, u32[]{:S(2)}) collective-permute-start(bf16[512,1536]{1,0:T(8,128)(2,1)S(1)} %copy-done.13), channel_id=1, source_target_pairs={{0,4},{4,0},{8,12},{12,8},{16,20},{20,16},{24,28},{28,24},{1,5},{5... | collective-permute-start | bytes 4718600 | tf_op jit(solution)/shard_map/ppermute | solution.py:1231
  111.4 52.2 %collective-permute-start.17 = (bf16[512,1536]{1,0:T(8,128)(2,1)S(1)}, bf16[512,1536]{1,0:T(8,128)(2,1)S(1)}, u32[]{:S(2)}, u32[]{:S(2)}) collective-permute-start(bf16[512,1536]{1,0:T(8,128)(2,1)S(1)} %copy-done.13), channel_id=1, source_target_pairs={{0,8},{4,12},{8,0},{12,4},{16,24},{20,28},{24,16},{28,20},{1,9},{5... | collective-permute-start | bytes 4718600 | tf_op jit(solution)/shard_map/ppermute | solution.py:1231
  117.0 46.7 %collective-permute-start.18 = (bf16[512,1536]{1,0:T(8,128)(2,1)S(1)}, bf16[512,1536]{1,0:T(8,128)(2,1)}, u32[]{:S(2)}, u32[]{:S(2)}) collective-permute-start(bf16[512,1536]{1,0:T(8,128)(2,1)S(1)} %copy-done.13), channel_id=1, source_target_pairs={{0,16},{4,20},{8,24},{12,28},{16,0},{20,4},{24,8},{28,12},{1,17},{... | collective-permute-start | bytes 4718600 | tf_op jit(solution)/shard_map/ppermute | solution.py:1231
  162.2 39.3 %collective-permute-start.32 = (bf16[576,1536]{1,0:T(8,128)(2,1)}, bf16[576,1536]{1,0:T(8,128)(2,1)}, u32[]{:S(2)}, u32[]{:S(2)}) collective-permute-start(bf16[576,1536]{1,0:T(8,128)(2,1)} %select_select_fusion), channel_id=1, source_target_pairs={{3,1},{1,0},{0,2},{2,3},{7,5},{5,4},{4,6},{6,7},{11,9},{9,8},{8,10... | collective-permute-start | bytes 5308424 | tf_op jit(solution)/shard_map/ppermute | solution.py:1197
  163.6 24.8 %collective-permute-start.21 = (bf16[512,1536]{1,0:T(8,128)(2,1)S(1)}, bf16[512,1536]{1,0:T(8,128)(2,1)S(1)}, u32[]{:S(2)}, u32[]{:S(2)}) collective-permute-start(bf16[512,1536]{1,0:T(8,128)(2,1)S(1)} %collective-permute-done.17.rest_2_), channel_id=1, source_target_pairs={{0,4},{4,0},{8,12},{12,8},{16,20},{20,16},{24,28},{28,24},{1,5},{5... | collective-permute-start | bytes 4718600 | tf_op jit(solution)/shard_map/ppermute | solution.py:1231
  163.7 25.9 %collective-permute-start.22 = (bf16[512,1536]{1,0:T(8,128)(2,1)}, bf16[512,1536]{1,0:T(8,128)(2,1)}, u32[]{:S(2)}, u32[]{:S(2)}) collective-permute-start(bf16[512,1536]{1,0:T(8,128)(2,1)} %collective-permute-done.18.rest_4_), channel_id=1, source_target_pairs={{0,4},{4,0},{8,12},{12,8},{16,20},{20,16},{24,28},{28,24},{1,5},{5... | collective-permute-start | bytes 4718600 | tf_op jit(solution)/shard_map/ppermute | solution.py:1231
  165.1 19.8 %collective-permute-start.19 = (bf16[256,1536]{1,0:T(8,128)(2,1)}, bf16[256,1536]{1,0:T(8,128)(2,1)}, u32[]{:S(2)}, u32[]{:S(2)}) collective-permute-start(bf16[256,1536]{1,0:T(8,128)(2,1)} %slice.175), channel_id=1, source_target_pairs={{0,16},{4,20},{8,24},{12,28},{16,0},{20,4},{24,8},{28,12},{1,17},{... | collective-permute-start | bytes 2359304 | tf_op jit(solution)/shard_map/ppermute | solution.py:1231
  167.7 19.6 %collective-permute-start.20 = (bf16[256,1536]{1,0:T(8,128)(2,1)}, bf16[256,1536]{1,0:T(8,128)(2,1)}, u32[]{:S(2)}, u32[]{:S(2)}) collective-permute-start(bf16[256,1536]{1,0:T(8,128)(2,1)} %slice.176), channel_id=1, source_target_pairs={{0,8},{4,12},{8,0},{12,4},{16,24},{20,28},{24,16},{28,20},{1,9},{5... | collective-permute-start | bytes 2359304 | tf_op jit(solution)/shard_map/ppermute | solution.py:1231
  201.5 383.9 %reduce-scatter.3.cloned.1.call-start = ((), (), s32[]{:S(2)}) async-start(), calls=%async_computation.2 | async-start | bytes 8847360 | tf_op jit(solution)/shard_map/reduce_scatter | solution.py:1473
  202.1 19.5 %collective-permute-start.25 = (bf16[512,1536]{1,0:T(8,128)(2,1)S(1)}, bf16[512,1536]{1,0:T(8,128)(2,1)}, u32[]{:S(2)}, u32[]{:S(2)}) collective-permute-start(bf16[512,1536]{1,0:T(8,128)(2,1)S(1)} %copy-done.14), channel_id=1, source_target_pairs={{0,4},{4,0},{8,12},{12,8},{16,20},{20,16},{24,28},{28,24},{1,5},{5... | collective-permute-start | bytes 4718600 | tf_op jit(solution)/shard_map/ppermute | solution.py:1231
  202.5 36.6 %collective-permute-start.23 = (bf16[512,1536]{1,0:T(8,128)(2,1)S(1)}, bf16[512,1536]{1,0:T(8,128)(2,1)}, u32[]{:S(2)}, u32[]{:S(2)}) collective-permute-start(bf16[512,1536]{1,0:T(8,128)(2,1)S(1)} %copy-done.14), channel_id=1, source_target_pairs={{0,8},{4,12},{8,0},{12,4},{16,24},{20,28},{24,16},{28,20},{1,9},{5... | collective-permute-start | bytes 4718600 | tf_op jit(solution)/shard_map/ppermute | solution.py:1231
  204.0 36.3 %collective-permute-start.24 = (bf16[512,1536]{1,0:T(8,128)(2,1)S(1)}, bf16[512,1536]{1,0:T(8,128)(2,1)}, u32[]{:S(2)}, u32[]{:S(2)}) collective-permute-start(bf16[512,1536]{1,0:T(8,128)(2,1)S(1)} %copy-done.14), channel_id=1, source_target_pairs={{0,16},{4,20},{8,24},{12,28},{16,0},{20,4},{24,8},{28,12},{1,17},{... | collective-permute-start | bytes 4718600 | tf_op jit(solution)/shard_map/ppermute | solution.py:1231
  240.2 16.9 %collective-permute-start.29 = (bf16[512,1536]{1,0:T(8,128)(2,1)}, bf16[512,1536]{1,0:T(8,128)(2,1)S(1)}, u32[]{:S(2)}, u32[]{:S(2)}) collective-permute-start(bf16[512,1536]{1,0:T(8,128)(2,1)} %collective-permute-done.24.rows), channel_id=1, source_target_pairs={{0,4},{4,0},{8,12},{12,8},{16,20},{20,16},{24,28},{28,24},{1,5},{5... | collective-permute-start | bytes 4718600 | tf_op jit(solution)/shard_map/ppermute | solution.py:1231
  243.1 19.5 %collective-permute-start.27 = (bf16[256,1536]{1,0:T(8,128)(2,1)S(1)}, bf16[256,1536]{1,0:T(8,128)(2,1)S(1)}, u32[]{:S(2)}, u32[]{:S(2)}) collective-permute-start(bf16[256,1536]{1,0:T(8,128)(2,1)S(1)} %slice.179), channel_id=1, source_target_pairs={{0,16},{4,20},{8,24},{12,28},{16,0},{20,4},{24,8},{28,12},{1,17},{... | collective-permute-start | bytes 2359304 | tf_op jit(solution)/shard_map/ppermute | solution.py:1231
  244.7 19.2 %collective-permute-start.28 = (bf16[256,1536]{1,0:T(8,128)(2,1)S(1)}, bf16[256,1536]{1,0:T(8,128)(2,1)S(1)}, u32[]{:S(2)}, u32[]{:S(2)}) collective-permute-start(bf16[256,1536]{1,0:T(8,128)(2,1)S(1)} %slice.180), channel_id=1, source_target_pairs={{0,8},{4,12},{8,0},{12,4},{16,24},{20,28},{24,16},{28,20},{1,9},{5... | collective-permute-start | bytes 2359304 | tf_op jit(solution)/shard_map/ppermute | solution.py:1231
  318.8 330.3 %reduce-scatter.5.cloned.1.call-start = ((), (), s32[]{:S(2)}) async-start(), calls=%async_computation.3 | async-start | bytes 8847360 | tf_op jit(solution)/shard_map/reduce_scatter | solution.py:1503
  367.2 16.0 %collective-permute-start.34 = (bf16[4,544,1536]{2,1,0:T(8,128)(2,1)}, bf16[4,544,1536]{2,1,0:T(8,128)(2,1)S(1)}, u32[]{:S(2)}, u32[]{:S(2)}) collective-permute-start(bf16[4,544,1536]{2,1,0:T(8,128)(2,1)} %combine.7), channel_id=1, source_target_pairs={{0,4},{4,0},{8,12},{12,8},{16,20},{20,16},{24,28},{28,24},{1,5},{5... | collective-permute-start | bytes 20054024 | tf_op jit(solution)/shard_map/ppermute | solution.py:1231
  374.6 65.8 %collective-permute-start.33 = (bf16[4,512,1536]{2,1,0:T(8,128)(2,1)}, bf16[4,512,1536]{2,1,0:T(8,128)(2,1)}, u32[]{:S(2)}, u32[]{:S(2)}) collective-permute-start(bf16[4,512,1536]{2,1,0:T(8,128)(2,1)} %combine.5), channel_id=1, source_target_pairs={{0,4},{4,0},{8,12},{12,8},{16,20},{20,16},{24,28},{28,24},{1,5},{5... | collective-permute-start | bytes 18874376 | tf_op jit(solution)/shard_map/ppermute | solution.py:1231
  393.7 38.7 %collective-permute-start.35 = (bf16[2,272,1536]{2,1,0:T(8,128)(2,1)}, bf16[2,272,1536]{2,1,0:T(8,128)(2,1)S(1)}, u32[]{:S(2)}, u32[]{:S(2)}) collective-permute-start(bf16[2,272,1536]{2,1,0:T(8,128)(2,1)} %get-tuple-element.215), channel_id=1, source_target_pairs={{0,8},{4,12},{8,0},{12,4},{16,24},{20,28},{24,16},{28,20},{1,9},{5... | collective-permute-start | bytes 5013512 | tf_op jit(solution)/shard_map/ppermute | solution.py:1231
  395.2 38.4 %collective-permute-start.36 = (bf16[2,272,1536]{2,1,0:T(8,128)(2,1)}, bf16[2,272,1536]{2,1,0:T(8,128)(2,1)S(1)}, u32[]{:S(2)}, u32[]{:S(2)}) collective-permute-start(bf16[2,272,1536]{2,1,0:T(8,128)(2,1)} %get-tuple-element.216), channel_id=1, source_target_pairs={{0,16},{4,20},{8,24},{12,28},{16,0},{20,4},{24,8},{28,12},{1,17},{... | collective-permute-start | bytes 5013512 | tf_op jit(solution)/shard_map/ppermute | solution.py:1231
  438.1 19.7 %collective-permute-start.37 = (bf16[272,1536]{1,0:T(8,128)(2,1)}, bf16[272,1536]{1,0:T(8,128)(2,1)S(1)}, u32[]{:S(2)}, u32[]{:S(2)}) collective-permute-start(bf16[272,1536]{1,0:T(8,128)(2,1)} %get-tuple-element.223), channel_id=1, source_target_pairs={{0,16},{4,20},{8,24},{12,28},{16,0},{20,4},{24,8},{28,12},{1,17},{... | collective-permute-start | bytes 2506760 | tf_op jit(solution)/shard_map/ppermute | solution.py:1231
  439.6 19.4 %collective-permute-start.38 = (bf16[272,1536]{1,0:T(8,128)(2,1)}, bf16[272,1536]{1,0:T(8,128)(2,1)S(1)}, u32[]{:S(2)}, u32[]{:S(2)}) collective-permute-start(bf16[272,1536]{1,0:T(8,128)(2,1)} %get-tuple-element.224), channel_id=1, source_target_pairs={{0,8},{4,12},{8,0},{12,4},{16,24},{20,28},{24,16},{28,20},{1,9},{5... | collective-permute-start | bytes 2506760 | tf_op jit(solution)/shard_map/ppermute | solution.py:1231
  459.9 55.7 %collective-permute-start.39 = (bf16[2,256,1536]{2,1,0:T(8,128)(2,1)}, bf16[2,256,1536]{2,1,0:T(8,128)(2,1)}, u32[]{:S(2)}, u32[]{:S(2)}) collective-permute-start(bf16[2,256,1536]{2,1,0:T(8,128)(2,1)} %get-tuple-element.227), channel_id=1, source_target_pairs={{0,8},{4,12},{8,0},{12,4},{16,24},{20,28},{24,16},{28,20},{1,9},{5... | collective-permute-start | bytes 4718600 | tf_op jit(solution)/shard_map/ppermute | solution.py:1231
  461.1 54.6 %collective-permute-start.40 = (bf16[2,256,1536]{2,1,0:T(8,128)(2,1)}, bf16[2,256,1536]{2,1,0:T(8,128)(2,1)S(1)}, u32[]{:S(2)}, u32[]{:S(2)}) collective-permute-start(bf16[2,256,1536]{2,1,0:T(8,128)(2,1)} %get-tuple-element.228), channel_id=1, source_target_pairs={{0,16},{4,20},{8,24},{12,28},{16,0},{20,4},{24,8},{28,12},{1,17},{... | collective-permute-start | bytes 4718600 | tf_op jit(solution)/shard_map/ppermute | solution.py:1231
  491.2 24.4 %collective-permute-start.41 = (bf16[512,512]{1,0:T(8,128)(2,1)S(1)}, bf16[512,512]{1,0:T(8,128)(2,1)S(1)}, u32[]{:S(2)}, u32[]{:S(2)}) collective-permute-start(bf16[512,512]{1,0:T(8,128)(2,1)S(1)} %convert_element_type.135), channel_id=1, source_target_pairs={{0,1},{2,3},{4,5},{6,7},{8,9},{10,11},{12,13},{14,15},{16,17},{18,... | collective-permute-start | bytes 1572872 | tf_op jit(solution)/shard_map/ppermute | solution.py:1520
  545.0 35.1 %collective-permute-start.43 = (bf16[2,416,896]{2,1,0:T(8,128)(2,1)}, bf16[2,416,896]{2,1,0:T(8,128)(2,1)}, u32[]{:S(2)}, u32[]{:S(2)}) collective-permute-start(bf16[2,416,896]{2,1,0:T(8,128)(2,1)} %get-tuple-element.246), channel_id=1, source_target_pairs={{0,8},{4,12},{8,0},{12,4},{16,24},{20,28},{24,16},{28,20},{1,9},{5... | collective-permute-start | bytes 4472840 | tf_op jit(solution)/shard_map/ppermute | solution.py:1231
  545.2 34.8 %collective-permute-start.44 = (bf16[2,416,896]{2,1,0:T(8,128)(2,1)}, bf16[2,416,896]{2,1,0:T(8,128)(2,1)S(1)}, u32[]{:S(2)}, u32[]{:S(2)}) collective-permute-start(bf16[2,416,896]{2,1,0:T(8,128)(2,1)} %get-tuple-element.247), channel_id=1, source_target_pairs={{0,16},{4,20},{8,24},{12,28},{16,0},{20,4},{24,8},{28,12},{1,17},{... | collective-permute-start | bytes 4472840 | tf_op jit(solution)/shard_map/ppermute | solution.py:1231
  584.3 19.8 %collective-permute-start.47 = (bf16[416,896]{1,0:T(8,128)(2,1)}, bf16[416,896]{1,0:T(8,128)(2,1)S(1)}, u32[]{:S(2)}, u32[]{:S(2)}) collective-permute-start(bf16[416,896]{1,0:T(8,128)(2,1)} %get-tuple-element.260), channel_id=1, source_target_pairs={{0,16},{4,20},{8,24},{12,28},{16,0},{20,4},{24,8},{28,12},{1,17},{... | collective-permute-start | bytes 2236424 | tf_op jit(solution)/shard_map/ppermute | solution.py:1231
  587.4 19.7 %collective-permute-start.48 = (bf16[416,896]{1,0:T(8,128)(2,1)S(1)}, bf16[416,896]{1,0:T(8,128)(2,1)S(1)}, u32[]{:S(2)}, u32[]{:S(2)}) collective-permute-start(bf16[416,896]{1,0:T(8,128)(2,1)S(1)} %copy-done.55), channel_id=1, source_target_pairs={{0,8},{4,12},{8,0},{12,4},{16,24},{20,28},{24,16},{28,20},{1,9},{5... | collective-permute-start | bytes 2236424 | tf_op jit(solution)/shard_map/ppermute | solution.py:1231
  594.3 25.0 %collective-permute-start.45 = (bf16[256,1536]{1,0:T(8,128)(2,1)}, bf16[256,1536]{1,0:T(8,128)(2,1)}, u32[]{:S(2)}, u32[]{:S(2)}) collective-permute-start(bf16[256,1536]{1,0:T(8,128)(2,1)} %get-tuple-element.256), channel_id=1, source_target_pairs={{0,16},{4,20},{8,24},{12,28},{16,0},{20,4},{24,8},{28,12},{1,17},{... | collective-permute-start | bytes 2359304 | tf_op jit(solution)/shard_map/ppermute | solution.py:1231
  595.1 26.7 %collective-permute-start.46 = (bf16[256,1536]{1,0:T(8,128)(2,1)}, bf16[256,1536]{1,0:T(8,128)(2,1)}, u32[]{:S(2)}, u32[]{:S(2)}) collective-permute-start(bf16[256,1536]{1,0:T(8,128)(2,1)} %get-tuple-element.257), channel_id=1, source_target_pairs={{0,8},{4,12},{8,0},{12,4},{16,24},{20,28},{24,16},{28,20},{1,9},{5... | collective-permute-start | bytes 2359304 | tf_op jit(solution)/shard_map/ppermute | solution.py:1231
  610.6 20.1 %collective-permute-start.49 = (bf16[208,896]{1,0:T(8,128)(2,1)S(1)}, bf16[208,896]{1,0:T(8,128)(2,1)S(1)}, u32[]{:S(2)}, u32[]{:S(2)}) collective-permute-start(bf16[208,896]{1,0:T(8,128)(2,1)S(1)} %get-tuple-element.289), channel_id=1, source_target_pairs={{1,3},{0,1},{2,0},{3,2},{5,7},{4,5},{6,4},{7,6},{9,11},{8,9},{10,8... | collective-permute-start | bytes 1118216 | tf_op jit(solution)/shard_map/ppermute | solution.py:1215
  630.9 30.5 %collective-permute-start.50 = (bf16[208,896]{1,0:T(8,128)(2,1)S(1)}, bf16[208,896]{1,0:T(8,128)(2,1)S(1)}, u32[]{:S(2)}, u32[]{:S(2)}) collective-permute-start(bf16[208,896]{1,0:T(8,128)(2,1)S(1)} %get-tuple-element.287), channel_id=1, source_target_pairs={{0,1},{1,2},{2,3},{4,5},{5,6},{6,7},{8,9},{9,10},{10,11},{12,13},{... | collective-permute-start | bytes 1118216 | tf_op jit(solution)/shard_map/ppermute | solution.py:1222
  635.1 26.3 %collective-permute-start.51 = (bf16[208,896]{1,0:T(8,128)(2,1)S(1)}, bf16[208,896]{1,0:T(8,128)(2,1)S(1)}, u32[]{:S(2)}, u32[]{:S(2)}) collective-permute-start(bf16[208,896]{1,0:T(8,128)(2,1)S(1)} %get-tuple-element.286), channel_id=1, source_target_pairs={{1,0},{2,1},{3,2},{5,4},{6,5},{7,6},{9,8},{10,9},{11,10},{13,12},{... | collective-permute-start | bytes 1118216 | tf_op jit(solution)/shard_map/ppermute | solution.py:1223
  636.4 25.0 %collective-permute-start.52 = (bf16[208,896]{1,0:T(8,128)(2,1)S(1)}, bf16[208,896]{1,0:T(8,128)(2,1)S(1)}, u32[]{:S(2)}, u32[]{:S(2)}) collective-permute-start(bf16[208,896]{1,0:T(8,128)(2,1)S(1)} %get-tuple-element.264), channel_id=1, source_target_pairs={{0,3},{3,0},{4,7},{7,4},{8,11},{11,8},{12,15},{15,12},{16,19},{19,... | collective-permute-start | bytes 1118216 | tf_op jit(solution)/shard_map/ppermute | solution.py:1186
  (65 other events, 477.2 us)
Sparse Core Ops, SparseCore 0:
  201.7 127.1 all-gather.2
  331.2 121.7 reduce-scatter.2
  461.8 130.5 reduce-scatter.4

commit v17 on v16

--- a/solution.py
+++ b/solution.py
@@ -1038,7 +1038,7 @@
     )(info, query_part, grad_pair, tokens, grad_residual, gain, *refs)
 
 
-def weight_grads_kernel(parts, whole_rows, info, *rest):
+def weight_grads_kernel(parts, info, *rest):
     ins, (keep, send) = rest[:-2], rest[-2:]
     depth = D // 8
     core = info[0] & 1
@@ -1055,12 +1055,8 @@
                     upper, lower = piece[:depth], piece[depth:]
                     keep[0, slot, :depth, columns] = jnp.where(core == 0, upper, lower)
                     send[0, slot, :depth, columns] = jnp.where(core == 0, lower, upper)
-                    if not whole_rows:
-                        blank = jnp.zeros((EXTRA, width), LOW)
-                        keep[0, slot, depth:, columns] = blank
-                        send[0, slot, depth:, columns] = blank
-
-    if whole_rows:
+
+    if keep.shape[2] > depth:
         extra = ins[-1]
         for slot in range(QUARTERS):
             to = info[2 + slot]
@@ -1068,26 +1064,15 @@
             send[0, slot, depth:] = extra[(chip * 2 + 1 - core) * QUARTERS + to]
 
 
-def weight_grads(info, strips, grads, parts, extra, earlier=()):
+def weight_grads(info, strips, grads, parts, extra=None):
     depth = D // 8
     strip = pl.BlockSpec((TOK_DEV, 2 * depth), lambda i, info: (0, i ^ (info[0] >> 1)))
     more = [] if extra is None else [extra]
-    width = 2 * D // QUARTERS + 128
-    shape = (4, QUARTERS, depth + EXTRA, width)
-    if earlier:
-        out = pl.BlockSpec((1, QUARTERS, depth + EXTRA, 128), lambda i, info: (i, 0, 0, 3))
-    else:
-        out = pl.BlockSpec((1,) + shape[1:], lambda i, info: (i, 0, 0, 0))
-    inputs = [*strips, *grads, *more]
-
-    def kernel(info, *rest):
-        count = len(inputs)
-        weight_grads_kernel(
-            parts, extra is not None, info, *rest[:count], *rest[count + len(earlier) :]
-        )
-
-    return pl.pallas_call(
-        kernel,
+    width = sum(part[3] for part in parts)
+    shape = (4, QUARTERS, depth + EXTRA * len(more), width)
+    out = pl.BlockSpec((1,) + shape[1:], lambda i, info: (i, 0, 0, 0))
+    return pl.pallas_call(
+        functools.partial(weight_grads_kernel, parts),
         grid_spec=pltpu.PrefetchScalarGridSpec(
             num_scalar_prefetch=1,
             grid=(4,),
@@ -1095,16 +1080,14 @@
             + [
                 pl.BlockSpec(a.shape, lambda i, info, n=a.ndim: (0,) * n)
                 for a in (*grads, *more)
-            ]
-            + [ANY] * len(earlier),
+            ],
             out_specs=(out, out),
         ),
         out_shape=(jax.ShapeDtypeStruct(shape, LOW),) * 2,
-        input_output_aliases={1 + len(inputs) + i: i for i in range(len(earlier))},
         compiler_params=params(),
         cost_estimate=LITTLE,
         name="weight_gradients",
-    )(info, *inputs, *earlier)
+    )(info, *strips, *grads, *more)
 
 
 def last_sums_kernel(part, info, own, *rest):
@@ -1117,10 +1100,10 @@
     depth = query_out.shape[0]
     quarter = query_out.shape[1]
     query_out[...] = total[:depth, :quarter]
-    pair = total[:depth, quarter : quarter + 2 * part].T
+    pair = total[:depth, 2 * quarter :].T
     key_out[...] = pair[:part]
     value_out[...] = pair[part:]
-    out_out[...] = total[:depth, quarter + 2 * part :]
+    out_out[...] = total[:depth, quarter : 2 * quarter]
     extra_out[...] = total[depth:]
 
 
@@ -1501,6 +1484,7 @@
         out_flips = send_chips(after(out_first[:2], back_parts[2], back_parts[5]))
         slots = after(slots, reduced[0], back_parts[2])
         reduced.append(lax.psum_scatter(slots, "cols", scatter_dimension=0, tiled=False))
+        main_width = 2 * query_part
         router_parts = jnp.transpose(
             router_grad.astype(LOW).reshape(col_count, router_part, row_count, depth),
             (2, 0, 1, 3),
@@ -1508,9 +1492,9 @@
         gain_rows = experts_gain_grad.astype(LOW).reshape(row_count * col_count, 1, gain_part)
         extra = jnp.concatenate(
             [
-                jnp.pad(router_parts, ((0, 0), (0, 0), (0, wide - depth))),
-                jnp.pad(gain_rows, ((0, 0), (0, 0), (0, wide - gain_part))),
-                jnp.zeros((row_count * col_count, EXTRA - router_part - 1, wide), LOW),
+                jnp.pad(router_parts, ((0, 0), (0, 0), (0, main_width - depth))),
+                jnp.pad(gain_rows, ((0, 0), (0, 0), (0, main_width - gain_part))),
+                jnp.zeros((row_count * col_count, EXTRA - router_part - 1, main_width), LOW),
             ],
             axis=1,
         )
@@ -1519,33 +1503,39 @@
     )
     arrived = lax.ppermute(source_grad.astype(LOW), "cols", [(j, i) for i, j in pairs])
     if fast:
-        parts = ((0, 2, 0, query_part), (1, 3, query_part + 2 * key_part, query_part))
-        keep_send = weight_grads(
+        parts = ((0, 2, 0, query_part), (1, 3, query_part, query_part))
+        grad_branch = after(grad_branch, *out_flips)
+        keep, send = weight_grads(
             info, [normed, heads], [grad_query, grad_branch], parts, extra
         )
-        query_back = normed_grad(info, after(grad_query, *keep_send), query_refs)
-        arrived = after(arrived, query_back, *out_flips)
+        flat = (4, col_count * (depth + EXTRA), main_width)
+        sent = flip(send, 1)
+        main_first = chip_adds(keep.reshape(flat), sent.reshape(flat))
+        main_chips = send_chips(main_first[:2])
+        query_back = normed_grad(info, after(grad_query, main_first[0]), query_refs)
+        main_chips = after(main_chips, query_back)
+        main_x, main_y = main_first[2:]
+        for_y, for_x = corner_adds(main_x, main_chips[0], main_y, main_chips[1])
+        main_parts = (main_x, main_chips[0], flip(for_y, 4), main_y, main_chips[1])
+        main_parts += (flip(for_x, 2),)
+        arrived = after(arrived, for_y)
     else:
         query_back = normed_grad(info, grad_query, query_refs)
     grad_pair = join_grads(info, own_grad, source_grad, arrived, cosine, sine)
     if fast:
-        keep, send = weight_grads(
-            info, [normed], [grad_pair], ((0, 1, 0, 2 * key_part),), None, keep_send
-        )
-        flat = (4, col_count * (depth + EXTRA), wide)
-        sent = flip(send, 1)
-        sent_first = chip_adds(keep.reshape(flat), sent.reshape(flat))
-        sent_chips = send_chips(sent_first[:2])
-        grad_pair = after(grad_pair, sent_first[0])
+        keep, send = weight_grads(info, [normed], [grad_pair], ((0, 1, 0, 2 * key_part),))
+        flat = (4, col_count * depth, 2 * key_part)
+        pair_first = chip_adds(keep.reshape(flat), flip(send, 1).reshape(flat))
+        pair_chips = send_chips(pair_first[:2])
+        grad_pair = after(grad_pair, pair_first[0])
     tokens_grad, attention_gain_grad = token_back(
         info, query_back, grad_pair, tokens, grad_residual, attention_scale, pair_refs
     )
 
     if fast:
-        sent_chips = after(sent_chips, tokens_grad)
-        sent_parts = chips_second(*sent_first[2:], *sent_chips)
+        pair_parts = chips_second(*pair_first[2:], *after(pair_chips, tokens_grad))
         near_x, near_y = out_first[2:]
-        mixture = chips_second(near_x, near_y, *after(out_flips, *sent_chips))
+        mixture = chips_second(near_x, near_y, *after(out_flips, pair_parts[2], pair_parts[5]))
     layer_output = (residual + sum_parts(mixture)).astype(LOW)
     part = down_weight.shape[1]
     expert_sums = [block.astype(WIDE) for block in reduced]
@@ -1555,21 +1545,26 @@
     )
     gate_grad, upward_grad = jnp.swapaxes(gate_grad, 1, 2), jnp.swapaxes(upward_grad, 1, 2)
     if fast:
-        slots = sum_parts(sent_parts)
-        slots = slots.reshape(col_count, depth + EXTRA, wide)
+        slots = sum_parts(main_parts).reshape(col_count, depth + EXTRA, main_width)
+        pairs_sum = sum_parts(pair_parts).reshape(col_count, depth, 2 * key_part)
         width = query_part + 2 * key_part
-        own_slots = own
-        gain_sums = sum(
-            jnp.sum(own_slots[i][:depth, :width].astype(WIDE) * slots[i, :depth, :width], axis=1)
-            for i in range(4)
-        )
+        weights_own = jnp.stack([own[i, :depth, :width].astype(WIDE) for i in range(4)])
+        gain_sums = jnp.sum(
+            weights_own[..., :query_part] * slots[:, :depth, :query_part], axis=(0, 2)
+        ) + jnp.sum(weights_own[..., query_part:] * pairs_sum, axis=(0, 2))
         own_gains = lax.dynamic_slice_in_dim(attention_scale[0], row_place * depth, depth, 0)
         gain_sums = (gain_sums / own_gains).reshape(col_count, 1, gain_part)
         gain_sums = jnp.pad(
             jnp.take(gain_sums, shards, axis=0),
-            ((0, 0), (depth + router_part + 1, EXTRA - router_part - 2), (0, wide - gain_part)),
+            (
+                (0, 0),
+                (depth + router_part + 1, EXTRA - router_part - 2),
+                (0, main_width - gain_part),
+            ),
         )
-        slots = after((slots + gain_sums).astype(LOW), reduced[1])
+        pairs_sum = jnp.pad(pairs_sum, ((0, 0), (0, EXTRA), (0, 0)))
+        slots = jnp.concatenate([slots + gain_sums, pairs_sum], axis=2).astype(LOW)
+        slots = after(slots, reduced[1])
 
         arrived = send_slots(slots)
         earlier = (gate_grad, upward_grad, down_grad, layer_output)

time: 685 us -> 671 us (0.980)
  waiting for transfers between devices: 183 us -> 165 us
    ppermute x39 -> x44, waiting for transfers between devices: 147 us -> 136 us  [flip(): return lax.ppermute(block, 'rows', [(i, i ^ bit) for i in range(count)])]
    ppermute x39 -> x44, starting transfers between devices: 28.6 us -> 34.1 us  [flip(): return lax.ppermute(block, 'rows', [(i, i ^ bit) for i in range(count)])]
    pallas_call x3 -> x4, Pallas kernels: 22.5 us -> 24.2 us  [chip_adds(): pl.pallas_call(chip_adds_kernel, out_shape=(shape,) * 4, in_specs=[ANY, A...]
    unnamed x125 -> x137, local copies, waits for them, and re-layouts: 24.3 us -> 24.8 us
  transfers between devices with their start and end apart: 56 -> 61, of which waited for: 28 -> 29; matrix products, arithmetic and copies ran while one was open for 8% -> 8% of each run, Pallas kernels for 45% -> 46%
where the time goes in v17:
time: 671 us; the launch traced here: 660 us
  Pallas kernels  307 us (46%)
  waiting for transfers between devices  165 us (25%)
  starting transfers between devices  90.2 us (13%)
  local copies, waits for them, and re-layouts  46.8 us (7%)
  other arithmetic  35.1 us (5%)
  between operations  15.3 us (2%)
    ppermute x44, waiting for transfers between devices, flip(): return lax.ppermute(block, 'rows', [(i, i ^ bit) for i in range(count)])  136 us
    pallas_call x2, Pallas kernels, expert(): pl.pallas_call(functools.partial(expert_kernel, slots), grid=(height // E...  60.9 us
    ppermute x44, starting transfers between devices, flip(): return lax.ppermute(block, 'rows', [(i, i ^ bit) for i in range(count)])  34.1 us
    pallas_call x4, Pallas kernels, combine(): pl.pallas_call(functools.partial(combine_kernel, local, first, step), out...  30.9 us
    pallas_call x2, Pallas kernels, expert_grads(): pl.pallas_call(expert_grads_kernel, grid=(D // 256,), out_shape=jax.Shape...  29.2 us
    pallas_call x8, Pallas kernels, dispatch(): pl.pallas_call(functools.partial(dispatch_kernel, local), grid=(D // wide...  29 us
    ppermute x4, starting transfers between devices, send_near(): return (lax.ppermute(block, 'cols', DOWN), lax.ppermute(block, 'cols', UP))  28.3 us
    unnamed x137, local copies, waits for them, and re-layouts  24.8 us
  transfers between devices with their start and end apart: 61, of which 29 were waited for; matrix products, arithmetic and copies ran while one was open for 8% of the time, Pallas kernels for 46%

profile of v17, /device:TPU:0, one launch (start us, length us, event | category | flops | bytes accessed | tf_op | source)
XLA Modules:
  0.0 659.9 jit_solution(423533392829621292)
XLA Ops:
  14.1 6.3 collective-permute-start.1
  32.3 19.3 %collective-permute-start.9 = (bf16[576,1536]{1,0:T(8,128)(2,1)}, bf16[576,1536]{1,0:T(8,128)(2,1)}, u32[]{:S(2)}, u32[]{:S(2)}) collective-permute-start(bf16[576,1536]{1,0:T(8,128)(2,1)} %pad_maximum_fusion.3.rest_0_), channel_id=1, source_target_pairs={{0,1},{1,2},{2,3},{4,5},{5,6},{6,7},{8,9},{9,10},{10,11},{12,13},{... | collective-permute-start | bytes 5308424 | tf_op jit(solution)/shard_map/ppermute | solution.py:1165
  57.4 31.8 %collective-permute-done.6.rest_2_.rest_8_ = bf16[4,208,896]{2,1,0:T(8,128)(2,1)S(1)} collective-permute-done((bf16[4,208,896]{2,1,0:T(8,128)(2,1)S(1)}, bf16[4,208,896]{2,1,0:T(8,128)(2,1)S(1)}, u32[]{:S(2)}, u32[]{:S(2)}) %collective-permute-start.6) | collective-permute-done | bytes 1490976 | tf_op jit(solution)/shard_map/ppermute | solution.py:1214
  93.1 6.8 %collective-permute-start.2 = (bf16[576,1536]{1,0:T(8,128)(2,1)}, bf16[576,1536]{1,0:T(8,128)(2,1)}, u32[]{:S(2)}, u32[]{:S(2)}) collective-permute-start(bf16[576,1536]{1,0:T(8,128)(2,1)} %pad_maximum_fusion.3.rest_0_), channel_id=1, source_target_pairs={{0,3},{3,0},{4,7},{7,4},{8,11},{11,8},{12,15},{15,12},{16,19},{19,... | collective-permute-start | bytes 5308424 | tf_op jit(solution)/shard_map/ppermute | solution.py:1169
  99.9 10.1 %collective-permute-done.11.rest_4_.rest_10_ = bf16[2,208,896]{2,1,0:T(8,128)(2,1)S(1)} collective-permute-done((bf16[2,208,896]{2,1,0:T(8,128)(2,1)S(1)}, bf16[2,208,896]{2,1,0:T(8,128)(2,1)S(1)}, u32[]{:S(2)}, u32[]{:S(2)}) %collective-permute-start.11) | collective-permute-done | bytes 745504 | tf_op jit(solution)/shard_map/ppermute | solution.py:1214
  112.5 4.4 collective-permute-done.12.rest_7_.rest_13_
  118.1 5.6 route_tables.1
  129.1 9.8 %collective-permute-done.2.rest_4_ = bf16[576,1536]{1,0:T(8,128)(2,1)} collective-permute-done((bf16[576,1536]{1,0:T(8,128)(2,1)}, bf16[576,1536]{1,0:T(8,128)(2,1)}, u32[]{:S(2)}, u32[]{:S(2)}) %collective-permute-start.2) | collective-permute-done | bytes 1769504 | tf_op jit(solution)/shard_map/ppermute | solution.py:1169
  138.9 5.0 norm_key_value.1
  145.2 8.2 %query_projection.1.queries = bf16[512,1536]{1,0:T(8,128)(2,1)} custom-call(s32[16]{0:T(128)} %concatenate.49.info, bf16[512,1536]{1,0:T(8,128)(2,1)} %get-tuple-element.160.normed.rest_0_, f32[512,128]{1,0:T(8,128)} %get-tuple-element.320.cosine, f32[512,128]{1,0:T(8,128)} %get-tuple-element.321.sine, bf16[4,208,896]{2,1,0:T(8,128)(2,1)} %copy-done.1, ...), custom_call_target="tpu_custom_call" | custom-call | flops 1 | bytes 1 | tf_op jit(solution)/shard_map/query_projection/pallas_call | solution.py:195
  153.4 5.9 collective-permute-done.16.partner
  171.3 11.0 %tree_attention.1.heads.rest_1_ = bf16[512,1536]{1,0:T(8,128)(2,1)} custom-call(s32[16]{0:T(128)} %concatenate.49.info, bf16[512,1536]{1,0:T(8,128)(2,1)} %query_projection.1.queries, bf16[512,512]{1,0:T(8,128)(2,1)} %get-tuple-element.161.own, bf16[512,512]{1,0:T(8,128)(2,1)} %collective-permute-done.16.partner), custom_call_target="tpu_custom_call" | custom-call | flops 1 | bytes 1 | tf_op jit(solution)/shard_map/tree_attention/pallas_call | solution.py:277
  190.8 9.9 %out_projection.1 = (f32[512,1536]{1,0:T(8,128)}, bf16[512,1536]{1,0:T(8,128)(2,1)}) custom-call(s32[16]{0:T(128)} %concatenate.49.info, bf16[512,1536]{1,0:T(8,128)(2,1)} %tree_attention.1.heads.rest_1_, bf16[512,1536]{1,0:T(8,128)(2,1)} %tokens.4, f32[1,1536]{1,0:T(1,128)} %reshape.299.gain, bf16[4,208,896]{2,1,0:T(8,128)(2,1)} %copy-done.1, ...), custom_call_target="tpu_custom_call" | custom-call | flops 1 | bytes 1 | tf_op jit(solution)/shard_map/out_projection/pallas_call | solution.py:389
  208.4 3.9 dispatch.8
  212.3 9.3 %pick_rows.1 = (bf16[8,160,1536]{2,1,0:T(8,128)(2,1)}, bf16[8,160,1536]{2,1,0:T(8,128)(2,1)}) custom-call(bf16[8,320,512]{2,1,0:T(8,128)(2,1)} %get-tuple-element.156.chosen, bf16[512,1536]{1,0:T(8,128)(2,1)} %cotangent.1, bf16[512,1536]{1,0:T(8,128)(2,1)} %collective-permute-done.15.rest_1_, bf16[512,1536]{1,0:T(8,128)(2,1)} %copy-done.20, ...), custom_call_target="tpu_custom_call" | custom-call | flops 1 | bytes 1 | tf_op jit(solution)/shard_map/pick_rows/pallas_call | solution.py:480
  221.7 3.6 dispatch.9
  225.3 13.8 %collective-permute-done.23.rows = bf16[512,1536]{1,0:T(8,128)(2,1)} collective-permute-done((bf16[512,1536]{1,0:T(8,128)(2,1)S(1)}, bf16[512,1536]{1,0:T(8,128)(2,1)}, u32[]{:S(2)}, u32[]{:S(2)}) %collective-permute-start.23) | collective-permute-done | bytes 1572896 | tf_op jit(solution)/shard_map/ppermute | solution.py:1214
  245.3 3.6 dispatch.10
  248.9 3.6 dispatch.11
  253.6 3.6 dispatch.12
  265.2 3.6 dispatch.14
  270.0 3.6 dispatch.15
  273.6 30.5 %expert.2 = (bf16[1280,1536]{1,0:T(8,128)(2,1)}, bf16[1280,1536]{1,0:T(8,128)(2,1)}, bf16[1280,1536]{1,0:T(8,128)(2,1)}, bf16[4,576,1280]{2,1,0:T(8,128)(2,1)}, f32[1280,1]{1,0:T(8,128)}) custom-call(s32[16]{0:T(128)} %concatenate.49.info, bf16[1280,1536]{1,0:T(8,128)(2,1)} %bitcast.126, bf16[1280,1536]{1,0:T(8,128)(2,1)} %bitcast.145, f32[1280,1]{1,0:T(8,128)} %bitcast.130, ...), custom_call_target="tpu_custom_call" | custom-call | flops 1 | bytes 1 | tf_op jit(solution)/shard_map/expert/pallas_call | solution.py:670
  304.0 14.6 %expert_gradients.2 = bf16[4,576,1536]{2,1,0:T(8,128)(2,1)} custom-call(bf16[4,576,1280]{2,1,0:T(8,128)(2,1)} %get-tuple-element.210.acts, bf16[1280,1536]{1,0:T(8,128)(2,1)} %bitcast.127, bf16[1280,1536]{1,0:T(8,128)(2,1)} %get-tuple-element.211.grads), custom_call_target="tpu_custom_call" | custom-call | flops 1 | bytes 1 | tf_op jit(solution)/shard_map/expert_gradients/pallas_call | solution.py:699
  318.7 10.1 %all-gather.3.cloned.1.call-done = bf16[2304,1536]{1,0:T(8,128)(2,1)} async-done(((bf16[576,1536]{1,0:T(8,128)(2,1)}), bf16[2304,1536]{1,0:T(8,128)(2,1)}) %all-gather.3.cloned.1.call-update) | async-done | bytes 7077904 | tf_op jit(solution)/shard_map/all_gather | solution.py:1397
  328.9 30.5 %expert.3 = (bf16[1280,1536]{1,0:T(8,128)(2,1)}, bf16[1280,1536]{1,0:T(8,128)(2,1)}, bf16[1280,1536]{1,0:T(8,128)(2,1)}, bf16[4,576,1280]{2,1,0:T(8,128)(2,1)}, f32[1280,1]{1,0:T(8,128)}) custom-call(s32[16]{0:T(128)} %concatenate.49.info, bf16[1280,1536]{1,0:T(8,128)(2,1)} %bitcast.128, bf16[1280,1536]{1,0:T(8,128)(2,1)} %bitcast.146, f32[1280,1]{1,0:T(8,128)} %bitcast.131, ...), custom_call_target="tpu_custom_call" | custom-call | flops 1 | bytes 1 | tf_op jit(solution)/shard_map/expert/pallas_call | solution.py:670
  359.4 8.0 %combine.7 = bf16[4,544,1536]{2,1,0:T(8,128)(2,1)} custom-call(s32[16]{0:T(128)} %concatenate.49.info, bf16[8,320,512]{2,1,0:T(8,128)(2,1)} %get-tuple-element.156.chosen, bf16[8,160,1536]{2,1,0:T(8,128)(2,1)} %bitcast.134, bf16[8,160,1536]{2,1,0:T(8,128)(2,1)} %bitcast.138, f32[8,160,1]{2,1,0:T(8,128)} %bitcast.149, f32[8,160,1]{2,1,0:T(8,128)} %bitcast.151), custom_call_target="tpu_custom_call" | custom-call | flops 1 | bytes 1 | tf_op jit(solution)/shard_map/combine/pallas_call | solution.py:762
  367.5 7.3 %combine.5 = bf16[4,512,1536]{2,1,0:T(8,128)(2,1)} custom-call(s32[16]{0:T(128)} %concatenate.49.info, bf16[8,320,512]{2,1,0:T(8,128)(2,1)} %get-tuple-element.156.chosen, bf16[8,160,1536]{2,1,0:T(8,128)(2,1)} %bitcast.132, bf16[8,160,1536]{2,1,0:T(8,128)(2,1)} %bitcast.136), custom_call_target="tpu_custom_call" | custom-call | flops 1 | bytes 1 | tf_op jit(solution)/shard_map/combine/pallas_call | solution.py:762
  375.3 8.1 %combine.6.keep = bf16[4,544,1536]{2,1,0:T(8,128)(2,1)} custom-call(s32[16]{0:T(128)} %concatenate.49.info, bf16[8,320,512]{2,1,0:T(8,128)(2,1)} %get-tuple-element.156.chosen, bf16[8,160,1536]{2,1,0:T(8,128)(2,1)} %bitcast.135, bf16[8,160,1536]{2,1,0:T(8,128)(2,1)} %bitcast.139, f32[8,160,1]{2,1,0:T(8,128)} %bitcast.150, f32[8,160,1]{2,1,0:T(8,128)} %bitcast.152), custom_call_target="tpu_custom_call" | custom-call | flops 1 | bytes 1 | tf_op jit(solution)/shard_map/combine/pallas_call | solution.py:762
  386.2 7.8 %chip_sums.5 = (bf16[2,272,1536]{2,1,0:T(8,128)(2,1)}, bf16[2,272,1536]{2,1,0:T(8,128)(2,1)}, bf16[2,272,1536]{2,1,0:T(8,128)(2,1)}, bf16[2,272,1536]{2,1,0:T(8,128)(2,1)}) custom-call(bf16[4,544,1536]{2,1,0:T(8,128)(2,1)} %combine.6.keep, bf16[4,544,1536]{2,1,0:T(8,128)(2,1)} %copy-done.11), custom_call_target="tpu_custom_call" | custom-call | flops 1 | bytes 1 | tf_op jit(solution)/shard_map/chip_sums/pallas_call | solution.py:811
  397.0 7.5 %combine.4.keep = bf16[4,512,1536]{2,1,0:T(8,128)(2,1)} custom-call(s32[16]{0:T(128)} %concatenate.49.info, bf16[8,320,512]{2,1,0:T(8,128)(2,1)} %get-tuple-element.156.chosen, bf16[8,160,1536]{2,1,0:T(8,128)(2,1)} %bitcast.133, bf16[8,160,1536]{2,1,0:T(8,128)(2,1)} %bitcast.137), custom_call_target="tpu_custom_call" | custom-call | flops 1 | bytes 1 | tf_op jit(solution)/shard_map/combine/pallas_call | solution.py:762
  404.5 14.6 %expert_gradients.3 = bf16[4,576,1536]{2,1,0:T(8,128)(2,1)} custom-call(bf16[4,576,1280]{2,1,0:T(8,128)(2,1)} %get-tuple-element.227.acts, bf16[1280,1536]{1,0:T(8,128)(2,1)} %bitcast.129, bf16[1280,1536]{1,0:T(8,128)(2,1)} %get-tuple-element.228.grads), custom_call_target="tpu_custom_call" | custom-call | flops 1 | bytes 1 | tf_op jit(solution)/shard_map/expert_gradients/pallas_call | solution.py:699
  419.1 13.6 %collective-permute-done.35.got_x.rest_1_ = bf16[2,272,1536]{2,1,0:T(8,128)(2,1)S(1)} collective-permute-done((bf16[2,272,1536]{2,1,0:T(8,128)(2,1)}, bf16[2,272,1536]{2,1,0:T(8,128)(2,1)S(1)}, u32[]{:S(2)}, u32[]{:S(2)}) %collective-permute-start.35) | collective-permute-done | bytes 1671200 | tf_op jit(solution)/shard_map/ppermute | solution.py:1214
  440.7 7.5 %chip_sums.4 = (bf16[2,256,1536]{2,1,0:T(8,128)(2,1)}, bf16[2,256,1536]{2,1,0:T(8,128)(2,1)}, bf16[2,256,1536]{2,1,0:T(8,128)(2,1)}, bf16[2,256,1536]{2,1,0:T(8,128)(2,1)}) custom-call(bf16[4,512,1536]{2,1,0:T(8,128)(2,1)} %combine.4.keep, bf16[4,512,1536]{2,1,0:T(8,128)(2,1)} %collective-permute-done.33.got), custom_call_target="tpu_custom_call" | custom-call | flops 1 | bytes 1 | tf_op jit(solution)/shard_map/chip_sums/pallas_call | solution.py:811
  448.2 9.8 %collective-permute-done.37.rest_2_ = bf16[272,1536]{1,0:T(8,128)(2,1)S(1)} collective-permute-done((bf16[272,1536]{1,0:T(8,128)(2,1)}, bf16[272,1536]{1,0:T(8,128)(2,1)S(1)}, u32[]{:S(2)}, u32[]{:S(2)}) %collective-permute-start.37) | collective-permute-done | bytes 835616 | tf_op jit(solution)/shard_map/ppermute | solution.py:1214
  461.7 13.2 %experts_norm_back.1 = (f32[512,1536]{1,0:T(8,128)}, bf16[512,1536]{1,0:T(8,128)(2,1)}, bf16[512,1536]{1,0:T(8,128)(2,1)}, f32[1,1536]{1,0:T(1,128)}, f32[16,1536]{1,0:T(8,128)}) custom-call(s32[16]{0:T(128)} %concatenate.49.info, f32[512,1536]{1,0:T(8,128)} %get-tuple-element.165.residual, bf16[512,1536]{1,0:T(8,128)(2,1)} %get-tuple-element.166.rows.normed, ...), custom_call_target="tpu_custom_call" | custom-call | flops 1 | bytes 1 | tf_op jit(solution)/shard_map/experts_norm_back/pallas_call | solution.py:922
  474.9 15.4 %tree_attention_back.1 = (bf16[512,1536]{1,0:T(8,128)(2,1)}, f32[512,512]{1,0:T(8,128)}, f32[512,512]{1,0:T(8,128)}) custom-call(s32[16]{0:T(128)} %concatenate.49.info, bf16[512,1536]{1,0:T(8,128)(2,1)} %query_projection.1.queries, bf16[512,512]{1,0:T(8,128)(2,1)} %get-tuple-element.161.own, bf16[512,512]{1,0:T(8,128)(2,1)} %collective-permute-done.16.partner, ...), custom_call_target="tpu_custom_call" | custom-call | flops 1 | bytes 1 | tf_op jit(solution)/shard_map/tree_attention_back/pallas_call | solution.py:338
  494.8 13.6 %weight_gradients.2 = (bf16[4,4,208,768]{3,2,1,0:T(8,128)(2,1)}, bf16[4,4,208,768]{3,2,1,0:T(8,128)(2,1)}) custom-call(s32[16]{0:T(128)} %concatenate.49.info, bf16[512,1536]{1,0:T(8,128)(2,1)} %get-tuple-element.160.normed.rest_0_, bf16[512,1536]{1,0:T(8,128)(2,1)} %tree_attention.1.heads.rest_1_, bf16[512,1536]{1,0:T(8,128)(2,1)} %get-tuple-element.255.rest_2_.grad_query, ...), custom_call_target="tpu_custom_call" | custom-call | flops 1 | bytes 1 | tf_op jit(solution)/shard_map/weight_gradients/pallas_call | solution.py:1074
  508.4 8.7 %collective-permute-done.42 = bf16[4,4,208,768]{3,2,1,0:T(8,128)(2,1)S(1)} collective-permute-done((bf16[4,4,208,768]{3,2,1,0:T(8,128)(2,1)}, bf16[4,4,208,768]{3,2,1,0:T(8,128)(2,1)S(1)}, u32[]{:S(2)}, u32[]{:S(2)}) %collective-permute-start.42) | collective-permute-done | bytes 5111840 | tf_op jit(solution)/shard_map/ppermute | solution.py:1214
  519.4 6.5 chip_sums.6
  530.0 8.1 %normed_gradient.1.query_part = f32[512,1536]{1,0:T(8,128)} custom-call(s32[16]{0:T(128)} %concatenate.49.info, bf16[512,1536]{1,0:T(8,128)(2,1)} %get-tuple-element.255.rest_2_.grad_query, bf16[4,208,896]{2,1,0:T(8,128)(2,1)} %copy-done.1, bf16[4,208,896]{2,1,0:T(8,128)(2,1)} %copy-done.5, bf16[4,208,896]{2,1,0:T(8,128)(2,1)} %copy-done.3, ...), custom_call_target="tpu_custom_call" | custom-call | flops 1 | bytes 1 | tf_op jit(solution)/shard_map/normed_gradient/pallas_call | solution.py:999
  538.1 18.2 %collective-permute-done.43.got_x = bf16[2,416,768]{2,1,0:T(8,128)(2,1)} collective-permute-done((bf16[2,416,768]{2,1,0:T(8,128)(2,1)}, bf16[2,416,768]{2,1,0:T(8,128)(2,1)}, u32[]{:S(2)}, u32[]{:S(2)}) %collective-permute-start.43) | collective-permute-done | bytes 1277984 | tf_op jit(solution)/shard_map/ppermute | solution.py:1214
  568.1 5.6 weight_gradients.3
  575.3 3.7 bitcast_convert_fusion.1
  585.4 5.8 collective-permute-done.53
  592.7 8.1 %token_gradient.1 = (bf16[512,1536]{1,0:T(8,128)(2,1)}, f32[1,1536]{1,0:T(1,128)}) custom-call(s32[16]{0:T(128)} %concatenate.49.info, f32[512,1536]{1,0:T(8,128)} %normed_gradient.1.query_part, bf16[512,512]{1,0:T(8,128)(2,1)} %join_key_value_gradients.1.rest_1_.grad_pair, bf16[512,1536]{1,0:T(8,128)(2,1)} %tokens.4, ...), custom_call_target="tpu_custom_call" | custom-call | flops 1 | bytes 1 | tf_op jit(solution)/shard_map/token_gradient/pallas_call | solution.py:1026
  622.7 4.0 collective-permute-start.55
  628.0 7.5 %collective-permute-start.57 = (bf16[208,896]{1,0:T(8,128)(2,1)}, bf16[208,896]{1,0:T(8,128)(2,1)}, u32[]{:S(2)}, u32[]{:S(2)}) collective-permute-start(bf16[208,896]{1,0:T(8,128)(2,1)} %get-tuple-element.282), channel_id=1, source_target_pairs={{0,3},{3,0},{4,7},{7,4},{8,11},{11,8},{12,15},{15,12},{16,19},{19,... | collective-permute-start | bytes 1118216 | tf_op jit(solution)/shard_map/ppermute | solution.py:1169
  (341 shorter events, 173.6 us)
Async XLA Ops:
  7.2 321.7 %all-gather.3.cloned.1.call-start = ((), (), s32[]{:S(2)}) async-start(), calls=%async_computation.4 | async-start | bytes 8847360 | tf_op jit(solution)/shard_map/all_gather | solution.py:1397
  12.7 18.4 %collective-permute-start = (bf16[208,896]{1,0:T(8,128)(2,1)S(1)}, bf16[208,896]{1,0:T(8,128)(2,1)S(1)}, u32[]{:S(2)}, u32[]{:S(2)}) collective-permute-start(bf16[208,896]{1,0:T(8,128)(2,1)S(1)} %concatenate.53), channel_id=1, source_target_pairs={{1,0},{2,1},{3,2},{5,4},{6,5},{7,6},{9,8},{10,9},{11,10},{13,12},{... | collective-permute-start | bytes 1118216 | tf_op jit(solution)/shard_map/ppermute | solution.py:1165
  14.1 17.0 %collective-permute-start.1 = (bf16[208,896]{1,0:T(8,128)(2,1)S(1)}, bf16[208,896]{1,0:T(8,128)(2,1)}, u32[]{:S(2)}, u32[]{:S(2)}) collective-permute-start(bf16[208,896]{1,0:T(8,128)(2,1)S(1)} %concatenate.53), channel_id=1, source_target_pairs={{0,1},{1,2},{2,3},{4,5},{5,6},{6,7},{8,9},{9,10},{10,11},{12,13},{... | collective-permute-start | bytes 1118216 | tf_op jit(solution)/shard_map/ppermute | solution.py:1165
  20.4 31.3 %collective-permute-start.4 = (bf16[208,896]{1,0:T(8,128)(2,1)S(1)}, bf16[208,896]{1,0:T(8,128)(2,1)}, u32[]{:S(2)}, u32[]{:S(2)}) collective-permute-start(bf16[208,896]{1,0:T(8,128)(2,1)S(1)} %concatenate.53), channel_id=1, source_target_pairs={{0,3},{3,0},{4,7},{7,4},{8,11},{11,8},{12,15},{15,12},{16,19},{19,... | collective-permute-start | bytes 1118216 | tf_op jit(solution)/shard_map/ppermute | solution.py:1169
  23.4 29.4 %collective-permute-start.3 = (bf16[208,896]{1,0:T(8,128)(2,1)S(1)}, bf16[208,896]{1,0:T(8,128)(2,1)}, u32[]{:S(2)}, u32[]{:S(2)}) collective-permute-start(bf16[208,896]{1,0:T(8,128)(2,1)S(1)} %concatenate.53), channel_id=1, source_target_pairs={{0,2},{1,3},{2,0},{3,1},{4,6},{5,7},{6,4},{7,5},{8,10},{9,11},{10,... | collective-permute-start | bytes 1118216 | tf_op jit(solution)/shard_map/ppermute | solution.py:1173
  31.1 59.3 %collective-permute-start.8 = (bf16[576,1536]{1,0:T(8,128)(2,1)}, bf16[576,1536]{1,0:T(8,128)(2,1)}, u32[]{:S(2)}, u32[]{:S(2)}) collective-permute-start(bf16[576,1536]{1,0:T(8,128)(2,1)} %pad_maximum_fusion.3.rest_0_), channel_id=1, source_target_pairs={{1,0},{2,1},{3,2},{5,4},{6,5},{7,6},{9,8},{10,9},{11,10},{13,12},{... | collective-permute-start | bytes 5308424 | tf_op jit(solution)/shard_map/ppermute | solution.py:1165
  32.3 58.1 %collective-permute-start.9 = (bf16[576,1536]{1,0:T(8,128)(2,1)}, bf16[576,1536]{1,0:T(8,128)(2,1)}, u32[]{:S(2)}, u32[]{:S(2)}) collective-permute-start(bf16[576,1536]{1,0:T(8,128)(2,1)} %pad_maximum_fusion.3.rest_0_), channel_id=1, source_target_pairs={{0,1},{1,2},{2,3},{4,5},{5,6},{6,7},{8,9},{9,10},{10,11},{12,13},{... | collective-permute-start | bytes 5308424 | tf_op jit(solution)/shard_map/ppermute | solution.py:1165
  54.1 35.1 %collective-permute-start.6 = (bf16[4,208,896]{2,1,0:T(8,128)(2,1)S(1)}, bf16[4,208,896]{2,1,0:T(8,128)(2,1)S(1)}, u32[]{:S(2)}, u32[]{:S(2)}) collective-permute-start(bf16[4,208,896]{2,1,0:T(8,128)(2,1)S(1)} %pad_maximum_fusion.5.rest_0_.rest_6_), channel_id=1, source_target_pairs={{0,8},{4,12},{8,0},{12,4},{16,24},{20,28},{24,16},{28,20},{1,9},{5... | collective-permute-start | bytes 4472840 | tf_op jit(solution)/shard_map/ppermute | solution.py:1214
  55.7 34.7 %collective-permute-start.7 = (bf16[4,208,896]{2,1,0:T(8,128)(2,1)S(1)}, bf16[4,208,896]{2,1,0:T(8,128)(2,1)S(1)}, u32[]{:S(2)}, u32[]{:S(2)}) collective-permute-start(bf16[4,208,896]{2,1,0:T(8,128)(2,1)S(1)} %pad_maximum_fusion.5.rest_0_.rest_6_), channel_id=1, source_target_pairs={{0,16},{4,20},{8,24},{12,28},{16,0},{20,4},{24,8},{28,12},{1,17},{... | collective-permute-start | bytes 4472840 | tf_op jit(solution)/shard_map/ppermute | solution.py:1214
  90.7 21.5 %collective-permute-start.10 = (bf16[8,208,896]{2,1,0:T(8,128)(2,1)S(1)}, bf16[8,208,896]{2,1,0:T(8,128)(2,1)S(1)}, u32[]{:S(2)}, u32[]{:S(2)}) collective-permute-start(bf16[8,208,896]{2,1,0:T(8,128)(2,1)S(1)} %pad_maximum_fusion), channel_id=1, source_target_pairs={{0,4},{4,0},{8,12},{12,8},{16,20},{20,16},{24,28},{28,24},{1,5},{5... | collective-permute-start | bytes 8945672 | tf_op jit(solution)/shard_map/ppermute | solution.py:1214
  90.9 19.1 %collective-permute-start.11 = (bf16[2,208,896]{2,1,0:T(8,128)(2,1)S(1)}, bf16[2,208,896]{2,1,0:T(8,128)(2,1)S(1)}, u32[]{:S(2)}, u32[]{:S(2)}) collective-permute-start(bf16[2,208,896]{2,1,0:T(8,128)(2,1)S(1)} %slice.162), channel_id=1, source_target_pairs={{0,16},{4,20},{8,24},{12,28},{16,0},{20,4},{24,8},{28,12},{1,17},{... | collective-permute-start | bytes 2236424 | tf_op jit(solution)/shard_map/ppermute | solution.py:1214
  92.5 18.9 %collective-permute-start.13 = (bf16[2,208,896]{2,1,0:T(8,128)(2,1)S(1)}, bf16[2,208,896]{2,1,0:T(8,128)(2,1)}, u32[]{:S(2)}, u32[]{:S(2)}) collective-permute-start(bf16[2,208,896]{2,1,0:T(8,128)(2,1)S(1)} %slice.165), channel_id=1, source_target_pairs={{0,8},{4,12},{8,0},{12,4},{16,24},{20,28},{24,16},{28,20},{1,9},{5... | collective-permute-start | bytes 2236424 | tf_op jit(solution)/shard_map/ppermute | solution.py:1214
  93.1 45.8 %collective-permute-start.2 = (bf16[576,1536]{1,0:T(8,128)(2,1)}, bf16[576,1536]{1,0:T(8,128)(2,1)}, u32[]{:S(2)}, u32[]{:S(2)}) collective-permute-start(bf16[576,1536]{1,0:T(8,128)(2,1)} %pad_maximum_fusion.3.rest_0_), channel_id=1, source_target_pairs={{0,3},{3,0},{4,7},{7,4},{8,11},{11,8},{12,15},{15,12},{16,19},{19,... | collective-permute-start | bytes 5308424 | tf_op jit(solution)/shard_map/ppermute | solution.py:1169
  111.4 33.8 %collective-permute-start.15 = (bf16[512,1536]{1,0:T(8,128)(2,1)S(1)}, bf16[512,1536]{1,0:T(8,128)(2,1)}, u32[]{:S(2)}, u32[]{:S(2)}) collective-permute-start(bf16[512,1536]{1,0:T(8,128)(2,1)S(1)} %copy-done.14), channel_id=1, source_target_pairs={{0,4},{4,0},{8,12},{12,8},{16,20},{20,16},{24,28},{28,24},{1,5},{5... | collective-permute-start | bytes 4718600 | tf_op jit(solution)/shard_map/ppermute | solution.py:1214
  111.4 52.2 %collective-permute-start.17 = (bf16[512,1536]{1,0:T(8,128)(2,1)S(1)}, bf16[512,1536]{1,0:T(8,128)(2,1)S(1)}, u32[]{:S(2)}, u32[]{:S(2)}) collective-permute-start(bf16[512,1536]{1,0:T(8,128)(2,1)S(1)} %copy-done.14), channel_id=1, source_target_pairs={{0,8},{4,12},{8,0},{12,4},{16,24},{20,28},{24,16},{28,20},{1,9},{5... | collective-permute-start | bytes 4718600 | tf_op jit(solution)/shard_map/ppermute | solution.py:1214
  117.0 46.7 %collective-permute-start.18 = (bf16[512,1536]{1,0:T(8,128)(2,1)S(1)}, bf16[512,1536]{1,0:T(8,128)(2,1)}, u32[]{:S(2)}, u32[]{:S(2)}) collective-permute-start(bf16[512,1536]{1,0:T(8,128)(2,1)S(1)} %copy-done.14), channel_id=1, source_target_pairs={{0,16},{4,20},{8,24},{12,28},{16,0},{20,4},{24,8},{28,12},{1,17},{... | collective-permute-start | bytes 4718600 | tf_op jit(solution)/shard_map/ppermute | solution.py:1214
  162.2 39.3 %collective-permute-start.32 = (bf16[576,1536]{1,0:T(8,128)(2,1)}, bf16[576,1536]{1,0:T(8,128)(2,1)}, u32[]{:S(2)}, u32[]{:S(2)}) collective-permute-start(bf16[576,1536]{1,0:T(8,128)(2,1)} %select_select_fusion), channel_id=1, source_target_pairs={{3,1},{1,0},{0,2},{2,3},{7,5},{5,4},{4,6},{6,7},{11,9},{9,8},{8,10... | collective-permute-start | bytes 5308424 | tf_op jit(solution)/shard_map/ppermute | solution.py:1180
  163.7 24.9 %collective-permute-start.21 = (bf16[512,1536]{1,0:T(8,128)(2,1)S(1)}, bf16[512,1536]{1,0:T(8,128)(2,1)S(1)}, u32[]{:S(2)}, u32[]{:S(2)}) collective-permute-start(bf16[512,1536]{1,0:T(8,128)(2,1)S(1)} %collective-permute-done.17.rest_2_), channel_id=1, source_target_pairs={{0,4},{4,0},{8,12},{12,8},{16,20},{20,16},{24,28},{28,24},{1,5},{5... | collective-permute-start | bytes 4718600 | tf_op jit(solution)/shard_map/ppermute | solution.py:1214
  163.7 26.0 %collective-permute-start.22 = (bf16[512,1536]{1,0:T(8,128)(2,1)}, bf16[512,1536]{1,0:T(8,128)(2,1)}, u32[]{:S(2)}, u32[]{:S(2)}) collective-permute-start(bf16[512,1536]{1,0:T(8,128)(2,1)} %collective-permute-done.18.rest_4_), channel_id=1, source_target_pairs={{0,4},{4,0},{8,12},{12,8},{16,20},{20,16},{24,28},{28,24},{1,5},{5... | collective-permute-start | bytes 4718600 | tf_op jit(solution)/shard_map/ppermute | solution.py:1214
  165.2 19.8 %collective-permute-start.19 = (bf16[256,1536]{1,0:T(8,128)(2,1)}, bf16[256,1536]{1,0:T(8,128)(2,1)}, u32[]{:S(2)}, u32[]{:S(2)}) collective-permute-start(bf16[256,1536]{1,0:T(8,128)(2,1)} %slice.167), channel_id=1, source_target_pairs={{0,16},{4,20},{8,24},{12,28},{16,0},{20,4},{24,8},{28,12},{1,17},{... | collective-permute-start | bytes 2359304 | tf_op jit(solution)/shard_map/ppermute | solution.py:1214
  167.8 19.6 %collective-permute-start.20 = (bf16[256,1536]{1,0:T(8,128)(2,1)}, bf16[256,1536]{1,0:T(8,128)(2,1)}, u32[]{:S(2)}, u32[]{:S(2)}) collective-permute-start(bf16[256,1536]{1,0:T(8,128)(2,1)} %slice.168), channel_id=1, source_target_pairs={{0,8},{4,12},{8,0},{12,4},{16,24},{20,28},{24,16},{28,20},{1,9},{5... | collective-permute-start | bytes 2359304 | tf_op jit(solution)/shard_map/ppermute | solution.py:1214
  201.6 373.7 %reduce-scatter.3.cloned.1.call-start = ((), (), s32[]{:S(2)}) async-start(), calls=%async_computation.2 | async-start | bytes 8847360 | tf_op jit(solution)/shard_map/reduce_scatter | solution.py:1456
  202.2 19.5 %collective-permute-start.25 = (bf16[512,1536]{1,0:T(8,128)(2,1)S(1)}, bf16[512,1536]{1,0:T(8,128)(2,1)}, u32[]{:S(2)}, u32[]{:S(2)}) collective-permute-start(bf16[512,1536]{1,0:T(8,128)(2,1)S(1)} %copy-done.15), channel_id=1, source_target_pairs={{0,4},{4,0},{8,12},{12,8},{16,20},{20,16},{24,28},{28,24},{1,5},{5... | collective-permute-start | bytes 4718600 | tf_op jit(solution)/shard_map/ppermute | solution.py:1214
  202.4 36.7 %collective-permute-start.23 = (bf16[512,1536]{1,0:T(8,128)(2,1)S(1)}, bf16[512,1536]{1,0:T(8,128)(2,1)}, u32[]{:S(2)}, u32[]{:S(2)}) collective-permute-start(bf16[512,1536]{1,0:T(8,128)(2,1)S(1)} %copy-done.15), channel_id=1, source_target_pairs={{0,8},{4,12},{8,0},{12,4},{16,24},{20,28},{24,16},{28,20},{1,9},{5... | collective-permute-start | bytes 4718600 | tf_op jit(solution)/shard_map/ppermute | solution.py:1214
  203.9 36.4 %collective-permute-start.24 = (bf16[512,1536]{1,0:T(8,128)(2,1)S(1)}, bf16[512,1536]{1,0:T(8,128)(2,1)}, u32[]{:S(2)}, u32[]{:S(2)}) collective-permute-start(bf16[512,1536]{1,0:T(8,128)(2,1)S(1)} %copy-done.15), channel_id=1, source_target_pairs={{0,16},{4,20},{8,24},{12,28},{16,0},{20,4},{24,8},{28,12},{1,17},{... | collective-permute-start | bytes 4718600 | tf_op jit(solution)/shard_map/ppermute | solution.py:1214
  240.3 16.9 %collective-permute-start.29 = (bf16[512,1536]{1,0:T(8,128)(2,1)}, bf16[512,1536]{1,0:T(8,128)(2,1)S(1)}, u32[]{:S(2)}, u32[]{:S(2)}) collective-permute-start(bf16[512,1536]{1,0:T(8,128)(2,1)} %collective-permute-done.24.rows), channel_id=1, source_target_pairs={{0,4},{4,0},{8,12},{12,8},{16,20},{20,16},{24,28},{28,24},{1,5},{5... | collective-permute-start | bytes 4718600 | tf_op jit(solution)/shard_map/ppermute | solution.py:1214
  243.2 19.5 %collective-permute-start.27 = (bf16[256,1536]{1,0:T(8,128)(2,1)S(1)}, bf16[256,1536]{1,0:T(8,128)(2,1)S(1)}, u32[]{:S(2)}, u32[]{:S(2)}) collective-permute-start(bf16[256,1536]{1,0:T(8,128)(2,1)S(1)} %slice.171), channel_id=1, source_target_pairs={{0,16},{4,20},{8,24},{12,28},{16,0},{20,4},{24,8},{28,12},{1,17},{... | collective-permute-start | bytes 2359304 | tf_op jit(solution)/shard_map/ppermute | solution.py:1214
  244.8 19.2 %collective-permute-start.28 = (bf16[256,1536]{1,0:T(8,128)(2,1)S(1)}, bf16[256,1536]{1,0:T(8,128)(2,1)S(1)}, u32[]{:S(2)}, u32[]{:S(2)}) collective-permute-start(bf16[256,1536]{1,0:T(8,128)(2,1)S(1)} %slice.172), channel_id=1, source_target_pairs={{0,8},{4,12},{8,0},{12,4},{16,24},{20,28},{24,16},{28,20},{1,9},{5... | collective-permute-start | bytes 2359304 | tf_op jit(solution)/shard_map/ppermute | solution.py:1214
  318.7 320.6 %reduce-scatter.5.cloned.1.call-start = ((), (), s32[]{:S(2)}) async-start(), calls=%async_computation.3 | async-start | bytes 8847360 | tf_op jit(solution)/shard_map/reduce_scatter | solution.py:1486
  374.8 65.8 %collective-permute-start.33 = (bf16[4,512,1536]{2,1,0:T(8,128)(2,1)}, bf16[4,512,1536]{2,1,0:T(8,128)(2,1)}, u32[]{:S(2)}, u32[]{:S(2)}) collective-permute-start(bf16[4,512,1536]{2,1,0:T(8,128)(2,1)} %combine.5), channel_id=1, source_target_pairs={{0,4},{4,0},{8,12},{12,8},{16,20},{20,16},{24,28},{28,24},{1,5},{5... | collective-permute-start | bytes 18874376 | tf_op jit(solution)/shard_map/ppermute | solution.py:1214
  394.0 38.7 %collective-permute-start.35 = (bf16[2,272,1536]{2,1,0:T(8,128)(2,1)}, bf16[2,272,1536]{2,1,0:T(8,128)(2,1)S(1)}, u32[]{:S(2)}, u32[]{:S(2)}) collective-permute-start(bf16[2,272,1536]{2,1,0:T(8,128)(2,1)} %get-tuple-element.224), channel_id=1, source_target_pairs={{0,8},{4,12},{8,0},{12,4},{16,24},{20,28},{24,16},{28,20},{1,9},{5... | collective-permute-start | bytes 5013512 | tf_op jit(solution)/shard_map/ppermute | solution.py:1214
  395.5 38.4 %collective-permute-start.36 = (bf16[2,272,1536]{2,1,0:T(8,128)(2,1)}, bf16[2,272,1536]{2,1,0:T(8,128)(2,1)S(1)}, u32[]{:S(2)}, u32[]{:S(2)}) collective-permute-start(bf16[2,272,1536]{2,1,0:T(8,128)(2,1)} %get-tuple-element.225), channel_id=1, source_target_pairs={{0,16},{4,20},{8,24},{12,28},{16,0},{20,4},{24,8},{28,12},{1,17},{... | collective-permute-start | bytes 5013512 | tf_op jit(solution)/shard_map/ppermute | solution.py:1214
  438.3 19.7 %collective-permute-start.37 = (bf16[272,1536]{1,0:T(8,128)(2,1)}, bf16[272,1536]{1,0:T(8,128)(2,1)S(1)}, u32[]{:S(2)}, u32[]{:S(2)}) collective-permute-start(bf16[272,1536]{1,0:T(8,128)(2,1)} %get-tuple-element.232), channel_id=1, source_target_pairs={{0,16},{4,20},{8,24},{12,28},{16,0},{20,4},{24,8},{28,12},{1,17},{... | collective-permute-start | bytes 2506760 | tf_op jit(solution)/shard_map/ppermute | solution.py:1214
  439.8 19.4 %collective-permute-start.38 = (bf16[272,1536]{1,0:T(8,128)(2,1)}, bf16[272,1536]{1,0:T(8,128)(2,1)S(1)}, u32[]{:S(2)}, u32[]{:S(2)}) collective-permute-start(bf16[272,1536]{1,0:T(8,128)(2,1)} %get-tuple-element.233), channel_id=1, source_target_pairs={{0,8},{4,12},{8,0},{12,4},{16,24},{20,28},{24,16},{28,20},{1,9},{5... | collective-permute-start | bytes 2506760 | tf_op jit(solution)/shard_map/ppermute | solution.py:1214
  459.2 34.3 %collective-permute-start.39 = (bf16[2,256,1536]{2,1,0:T(8,128)(2,1)}, bf16[2,256,1536]{2,1,0:T(8,128)(2,1)S(1)}, u32[]{:S(2)}, u32[]{:S(2)}) collective-permute-start(bf16[2,256,1536]{2,1,0:T(8,128)(2,1)} %get-tuple-element.236), channel_id=1, source_target_pairs={{0,8},{4,12},{8,0},{12,4},{16,24},{20,28},{24,16},{28,20},{1,9},{5... | collective-permute-start | bytes 4718600 | tf_op jit(solution)/shard_map/ppermute | solution.py:1214
  460.4 34.3 %collective-permute-start.40 = (bf16[2,256,1536]{2,1,0:T(8,128)(2,1)}, bf16[2,256,1536]{2,1,0:T(8,128)(2,1)S(1)}, u32[]{:S(2)}, u32[]{:S(2)}) collective-permute-start(bf16[2,256,1536]{2,1,0:T(8,128)(2,1)} %get-tuple-element.237), channel_id=1, source_target_pairs={{0,16},{4,20},{8,24},{12,28},{16,0},{20,4},{24,8},{28,12},{1,17},{... | collective-permute-start | bytes 4718600 | tf_op jit(solution)/shard_map/ppermute | solution.py:1214
  525.8 30.5 %collective-permute-start.43 = (bf16[2,416,768]{2,1,0:T(8,128)(2,1)}, bf16[2,416,768]{2,1,0:T(8,128)(2,1)}, u32[]{:S(2)}, u32[]{:S(2)}) collective-permute-start(bf16[2,416,768]{2,1,0:T(8,128)(2,1)} %get-tuple-element.253), channel_id=1, source_target_pairs={{0,8},{4,12},{8,0},{12,4},{16,24},{20,28},{24,16},{28,20},{1,9},{5... | collective-permute-start | bytes 3833864 | tf_op jit(solution)/shard_map/ppermute | solution.py:1214
  527.2 30.0 %collective-permute-start.44 = (bf16[2,416,768]{2,1,0:T(8,128)(2,1)}, bf16[2,416,768]{2,1,0:T(8,128)(2,1)S(1)}, u32[]{:S(2)}, u32[]{:S(2)}) collective-permute-start(bf16[2,416,768]{2,1,0:T(8,128)(2,1)} %get-tuple-element.254), channel_id=1, source_target_pairs={{0,16},{4,20},{8,24},{12,28},{16,0},{20,4},{24,8},{28,12},{1,17},{... | collective-permute-start | bytes 3833864 | tf_op jit(solution)/shard_map/ppermute | solution.py:1214
  528.6 35.4 %collective-permute-start.41 = (bf16[512,512]{1,0:T(8,128)(2,1)}, bf16[512,512]{1,0:T(8,128)(2,1)S(1)}, u32[]{:S(2)}, u32[]{:S(2)}) collective-permute-start(bf16[512,512]{1,0:T(8,128)(2,1)} %convert_element_type.153), channel_id=1, source_target_pairs={{0,1},{2,3},{4,5},{6,7},{8,9},{10,11},{12,13},{14,15},{16,17},{18,... | collective-permute-start | bytes 1572872 | tf_op jit(solution)/shard_map/ppermute | solution.py:1504
  561.2 17.8 %collective-permute-start.52 = (bf16[416,768]{1,0:T(8,128)(2,1)}, bf16[416,768]{1,0:T(8,128)(2,1)S(1)}, u32[]{:S(2)}, u32[]{:S(2)}) collective-permute-start(bf16[416,768]{1,0:T(8,128)(2,1)} %get-tuple-element.259), channel_id=1, source_target_pairs={{0,16},{4,20},{8,24},{12,28},{16,0},{20,4},{24,8},{28,12},{1,17},{... | collective-permute-start | bytes 1916936 | tf_op jit(solution)/shard_map/ppermute | solution.py:1214
  573.6 17.6 %collective-permute-start.53 = (bf16[416,768]{1,0:T(8,128)(2,1)}, bf16[416,768]{1,0:T(8,128)(2,1)}, u32[]{:S(2)}, u32[]{:S(2)}) collective-permute-start(bf16[416,768]{1,0:T(8,128)(2,1)} %get-tuple-element.279), channel_id=1, source_target_pairs={{0,8},{4,12},{8,0},{12,4},{16,24},{20,28},{24,16},{28,20},{1,9},{5... | collective-permute-start | bytes 1916936 | tf_op jit(solution)/shard_map/ppermute | solution.py:1214
  583.7 17.1 %collective-permute-start.46 = (bf16[2,384,128]{2,1,0:T(8,128)(2,1)}, bf16[2,384,128]{2,1,0:T(8,128)(2,1)S(1)}, u32[]{:S(2)}, u32[]{:S(2)}) collective-permute-start(bf16[2,384,128]{2,1,0:T(8,128)(2,1)} %get-tuple-element.264), channel_id=1, source_target_pairs={{0,8},{4,12},{8,0},{12,4},{16,24},{20,28},{24,16},{28,20},{1,9},{5... | collective-permute-start | bytes 589832 | tf_op jit(solution)/shard_map/ppermute | solution.py:1214
  584.2 16.7 %collective-permute-start.47 = (bf16[2,384,128]{2,1,0:T(8,128)(2,1)}, bf16[2,384,128]{2,1,0:T(8,128)(2,1)S(1)}, u32[]{:S(2)}, u32[]{:S(2)}) collective-permute-start(bf16[2,384,128]{2,1,0:T(8,128)(2,1)} %get-tuple-element.265), channel_id=1, source_target_pairs={{0,16},{4,20},{8,24},{12,28},{16,0},{20,4},{24,8},{28,12},{1,17},{... | collective-permute-start | bytes 589832 | tf_op jit(solution)/shard_map/ppermute | solution.py:1214
  615.5 20.0 %collective-permute-start.50 = (bf16[256,1536]{1,0:T(8,128)(2,1)}, bf16[256,1536]{1,0:T(8,128)(2,1)S(1)}, u32[]{:S(2)}, u32[]{:S(2)}) collective-permute-start(bf16[256,1536]{1,0:T(8,128)(2,1)} %get-tuple-element.277), channel_id=1, source_target_pairs={{0,16},{4,20},{8,24},{12,28},{16,0},{20,4},{24,8},{28,12},{1,17},{... | collective-permute-start | bytes 2359304 | tf_op jit(solution)/shard_map/ppermute | solution.py:1214
  617.5 18.3 %collective-permute-start.51 = (bf16[256,1536]{1,0:T(8,128)(2,1)S(1)}, bf16[256,1536]{1,0:T(8,128)(2,1)S(1)}, u32[]{:S(2)}, u32[]{:S(2)}) collective-permute-start(bf16[256,1536]{1,0:T(8,128)(2,1)S(1)} %copy-done.60), channel_id=1, source_target_pairs={{0,8},{4,12},{8,0},{12,4},{16,24},{20,28},{24,16},{28,20},{1,9},{5... | collective-permute-start | bytes 2359304 | tf_op jit(solution)/shard_map/ppermute | solution.py:1214
  622.7 24.5 %collective-permute-start.55 = (bf16[208,896]{1,0:T(8,128)(2,1)}, bf16[208,896]{1,0:T(8,128)(2,1)S(1)}, u32[]{:S(2)}, u32[]{:S(2)}) collective-permute-start(bf16[208,896]{1,0:T(8,128)(2,1)} %get-tuple-element.301), channel_id=1, source_target_pairs={{0,1},{1,2},{2,3},{4,5},{5,6},{6,7},{8,9},{9,10},{10,11},{12,13},{... | collective-permute-start | bytes 1118216 | tf_op jit(solution)/shard_map/ppermute | solution.py:1205
  626.7 20.5 %collective-permute-start.56 = (bf16[208,896]{1,0:T(8,128)(2,1)}, bf16[208,896]{1,0:T(8,128)(2,1)}, u32[]{:S(2)}, u32[]{:S(2)}) collective-permute-start(bf16[208,896]{1,0:T(8,128)(2,1)} %get-tuple-element.300), channel_id=1, source_target_pairs={{1,0},{2,1},{3,2},{5,4},{6,5},{7,6},{9,8},{10,9},{11,10},{13,12},{... | collective-permute-start | bytes 1118216 | tf_op jit(solution)/shard_map/ppermute | solution.py:1206
  628.0 19.2 %collective-permute-start.57 = (bf16[208,896]{1,0:T(8,128)(2,1)}, bf16[208,896]{1,0:T(8,128)(2,1)}, u32[]{:S(2)}, u32[]{:S(2)}) collective-permute-start(bf16[208,896]{1,0:T(8,128)(2,1)} %get-tuple-element.282), channel_id=1, source_target_pairs={{0,3},{3,0},{4,7},{7,4},{8,11},{11,8},{12,15},{15,12},{16,19},{19,... | collective-permute-start | bytes 1118216 | tf_op jit(solution)/shard_map/ppermute | solution.py:1169
  (76 other events, 590.3 us)
Sparse Core Ops, SparseCore 0:
  201.7 127.1 all-gather.2
  331.2 121.7 reduce-scatter.2
  461.7 130.0 reduce-scatter.4

commit v18 on v17

--- a/solution.py
+++ b/solution.py
@@ -1126,6 +1126,28 @@
         cost_estimate=LITTLE,
         name="last_sums",
     )(info, own, *arrived)
+
+
+def expert_sums_kernel(count, *rest):
+    blocks, outs = rest[:count], rest[count:]
+    part = outs[0].shape[1]
+    for e in range(count):
+        for which, out in enumerate(outs):
+            out[e] = blocks[e][which * part : (which + 1) * part].astype(WIDE)
+
+
+def expert_sums(blocks):
+    count, part = len(blocks), blocks[0].shape[0] // 3
+    vmem = pl.BlockSpec(memory_space=pltpu.VMEM)
+    return pl.pallas_call(
+        functools.partial(expert_sums_kernel, count),
+        out_shape=(jax.ShapeDtypeStruct((count, part, D), WIDE),) * 3,
+        in_specs=[vmem] * count,
+        out_specs=(vmem,) * 3,
+        compiler_params=params(),
+        cost_estimate=LITTLE,
+        name="expert_sums",
+    )(*blocks)
 
 
 def position_of(token_index):
@@ -1537,14 +1559,10 @@
         near_x, near_y = out_first[2:]
         mixture = chips_second(near_x, near_y, *after(out_flips, pair_parts[2], pair_parts[5]))
     layer_output = (residual + sum_parts(mixture)).astype(LOW)
-    part = down_weight.shape[1]
-    expert_sums = [block.astype(WIDE) for block in reduced]
-    gate_grad, upward_grad, down_grad = (
-        jnp.stack([sums_of[which * part : (which + 1) * part] for sums_of in expert_sums])
-        for which in range(3)
-    )
+    gate_grad, upward_grad, down_grad = expert_sums(reduced)
     gate_grad, upward_grad = jnp.swapaxes(gate_grad, 1, 2), jnp.swapaxes(upward_grad, 1, 2)
     if fast:
+        main_parts = after(main_parts, tokens_grad)
         slots = sum_parts(main_parts).reshape(col_count, depth + EXTRA, main_width)
         pairs_sum = sum_parts(pair_parts).reshape(col_count, depth, 2 * key_part)
         width = query_part + 2 * key_part

time: 671 us -> 682 us (1.016)
  waiting for transfers between devices: 165 us -> 184 us
  other arithmetic: 35.1 us -> 26 us
    ppermute x44, waiting for transfers between devices: 136 us -> 145 us  [flip(): return lax.ppermute(block, 'rows', [(i, i ^ bit) for i in range(count)])]
    unnamed x137 -> x133, local copies, waits for them, and re-layouts: 24.8 us -> 24.6 us
  transfers between devices with their start and end apart: 61 -> 61, of which waited for: 29 -> 30; matrix products, arithmetic and copies ran while one was open for 8% -> 6% of each run, Pallas kernels for 46% -> 46%
where the time goes in v18:
time: 682 us; the launch traced here: 671 us
  Pallas kernels  312 us (46%)
  waiting for transfers between devices  184 us (27%)
  starting transfers between devices  87.8 us (13%)
  local copies, waits for them, and re-layouts  46.2 us (7%)
  other arithmetic  26 us (4%)
  between operations  14.9 us (2%)
    ppermute x44, waiting for transfers between devices, flip(): return lax.ppermute(block, 'rows', [(i, i ^ bit) for i in range(count)])  145 us
    pallas_call x2, Pallas kernels, expert(): pl.pallas_call(functools.partial(expert_kernel, slots), grid=(height // E...  60.9 us
    ppermute x44, starting transfers between devices, flip(): return lax.ppermute(block, 'rows', [(i, i ^ bit) for i in range(count)])  33 us
    pallas_call x4, Pallas kernels, combine(): pl.pallas_call(functools.partial(combine_kernel, local, first, step), out...  31.1 us
    pallas_call x2, Pallas kernels, expert_grads(): pl.pallas_call(expert_grads_kernel, grid=(D // 256,), out_shape=jax.Shape...  29.2 us
    pallas_call x8, Pallas kernels, dispatch(): pl.pallas_call(functools.partial(dispatch_kernel, local), grid=(D // wide...  29 us
    ppermute x4, starting transfers between devices, send_near(): return (lax.ppermute(block, 'cols', DOWN), lax.ppermute(block, 'cols', UP))  27.8 us
    unnamed x133, local copies, waits for them, and re-layouts  24.6 us
  transfers between devices with their start and end apart: 61, of which 30 were waited for; matrix products, arithmetic and copies ran while one was open for 6% of the time, Pallas kernels for 46%

profile of v18, /device:TPU:0, one launch (start us, length us, event | category | flops | bytes accessed | tf_op | source)
XLA Modules:
  0.0 670.8 jit_solution(10050109815962661769)
XLA Ops:
  14.1 6.3 collective-permute-start.1
  32.9 18.7 %collective-permute-start.9 = (bf16[576,1536]{1,0:T(8,128)(2,1)}, bf16[576,1536]{1,0:T(8,128)(2,1)}, u32[]{:S(2)}, u32[]{:S(2)}) collective-permute-start(bf16[576,1536]{1,0:T(8,128)(2,1)} %pad_maximum_fusion.2.rest_0_), channel_id=1, source_target_pairs={{0,1},{1,2},{2,3},{4,5},{5,6},{6,7},{8,9},{9,10},{10,11},{12,13},{... | collective-permute-start | bytes 5308424 | tf_op jit(solution)/shard_map/ppermute | solution.py:1187
  57.4 31.8 %collective-permute-done.6.rest_2_.rest_8_ = bf16[4,208,896]{2,1,0:T(8,128)(2,1)S(1)} collective-permute-done((bf16[4,208,896]{2,1,0:T(8,128)(2,1)S(1)}, bf16[4,208,896]{2,1,0:T(8,128)(2,1)S(1)}, u32[]{:S(2)}, u32[]{:S(2)}) %collective-permute-start.6) | collective-permute-done | bytes 1490976 | tf_op jit(solution)/shard_map/ppermute | solution.py:1236
  93.1 6.8 %collective-permute-start.2 = (bf16[576,1536]{1,0:T(8,128)(2,1)}, bf16[576,1536]{1,0:T(8,128)(2,1)}, u32[]{:S(2)}, u32[]{:S(2)}) collective-permute-start(bf16[576,1536]{1,0:T(8,128)(2,1)} %pad_maximum_fusion.2.rest_0_), channel_id=1, source_target_pairs={{0,3},{3,0},{4,7},{7,4},{8,11},{11,8},{12,15},{15,12},{16,19},{19,... | collective-permute-start | bytes 5308424 | tf_op jit(solution)/shard_map/ppermute | solution.py:1191
  99.9 10.1 %collective-permute-done.11.rest_4_.rest_10_ = bf16[2,208,896]{2,1,0:T(8,128)(2,1)S(1)} collective-permute-done((bf16[2,208,896]{2,1,0:T(8,128)(2,1)S(1)}, bf16[2,208,896]{2,1,0:T(8,128)(2,1)S(1)}, u32[]{:S(2)}, u32[]{:S(2)}) %collective-permute-start.11) | collective-permute-done | bytes 745504 | tf_op jit(solution)/shard_map/ppermute | solution.py:1236
  112.5 4.4 collective-permute-done.12.rest_7_.rest_13_
  118.1 5.6 route_tables.1
  129.1 9.7 %collective-permute-done.2.rest_4_ = bf16[576,1536]{1,0:T(8,128)(2,1)} collective-permute-done((bf16[576,1536]{1,0:T(8,128)(2,1)}, bf16[576,1536]{1,0:T(8,128)(2,1)}, u32[]{:S(2)}, u32[]{:S(2)}) %collective-permute-start.2) | collective-permute-done | bytes 1769504 | tf_op jit(solution)/shard_map/ppermute | solution.py:1191
  138.8 5.0 norm_key_value.1
  145.2 8.2 %query_projection.1.queries = bf16[512,1536]{1,0:T(8,128)(2,1)} custom-call(s32[16]{0:T(128)} %concatenate.49.info, bf16[512,1536]{1,0:T(8,128)(2,1)} %get-tuple-element.169.normed.rest_0_, f32[512,128]{1,0:T(8,128)} %get-tuple-element.332.cosine, f32[512,128]{1,0:T(8,128)} %get-tuple-element.333.sine, bf16[4,208,896]{2,1,0:T(8,128)(2,1)} %copy-done.1, ...), custom_call_target="tpu_custom_call" | custom-call | flops 1 | bytes 1 | tf_op jit(solution)/shard_map/query_projection/pallas_call | solution.py:195
  153.4 5.9 collective-permute-done.16.partner
  171.2 11.0 %tree_attention.1.heads.rest_1_ = bf16[512,1536]{1,0:T(8,128)(2,1)} custom-call(s32[16]{0:T(128)} %concatenate.49.info, bf16[512,1536]{1,0:T(8,128)(2,1)} %query_projection.1.queries, bf16[512,512]{1,0:T(8,128)(2,1)} %get-tuple-element.170.own, bf16[512,512]{1,0:T(8,128)(2,1)} %collective-permute-done.16.partner), custom_call_target="tpu_custom_call" | custom-call | flops 1 | bytes 1 | tf_op jit(solution)/shard_map/tree_attention/pallas_call | solution.py:277
  190.8 9.9 %out_projection.1 = (f32[512,1536]{1,0:T(8,128)}, bf16[512,1536]{1,0:T(8,128)(2,1)}) custom-call(s32[16]{0:T(128)} %concatenate.49.info, bf16[512,1536]{1,0:T(8,128)(2,1)} %tree_attention.1.heads.rest_1_, bf16[512,1536]{1,0:T(8,128)(2,1)} %tokens.4, f32[1,1536]{1,0:T(1,128)} %reshape.299.gain, bf16[4,208,896]{2,1,0:T(8,128)(2,1)} %copy-done.1, ...), custom_call_target="tpu_custom_call" | custom-call | flops 1 | bytes 1 | tf_op jit(solution)/shard_map/out_projection/pallas_call | solution.py:389
  208.3 3.9 dispatch.8
  212.3 9.4 %pick_rows.1 = (bf16[8,160,1536]{2,1,0:T(8,128)(2,1)}, bf16[8,160,1536]{2,1,0:T(8,128)(2,1)}) custom-call(bf16[8,320,512]{2,1,0:T(8,128)(2,1)} %get-tuple-element.165.chosen, bf16[512,1536]{1,0:T(8,128)(2,1)} %cotangent.1, bf16[512,1536]{1,0:T(8,128)(2,1)} %collective-permute-done.15.rest_1_, bf16[512,1536]{1,0:T(8,128)(2,1)} %copy-done.18, ...), custom_call_target="tpu_custom_call" | custom-call | flops 1 | bytes 1 | tf_op jit(solution)/shard_map/pick_rows/pallas_call | solution.py:480
  221.6 3.6 dispatch.9
  225.2 13.8 %collective-permute-done.23.rows = bf16[512,1536]{1,0:T(8,128)(2,1)} collective-permute-done((bf16[512,1536]{1,0:T(8,128)(2,1)S(1)}, bf16[512,1536]{1,0:T(8,128)(2,1)}, u32[]{:S(2)}, u32[]{:S(2)}) %collective-permute-start.23) | collective-permute-done | bytes 1572896 | tf_op jit(solution)/shard_map/ppermute | solution.py:1236
  245.3 3.6 dispatch.10
  253.6 3.6 dispatch.12
  258.3 3.6 dispatch.13
  265.2 3.6 dispatch.14
  273.5 30.6 %expert.2 = (bf16[1280,1536]{1,0:T(8,128)(2,1)}, bf16[1280,1536]{1,0:T(8,128)(2,1)}, bf16[1280,1536]{1,0:T(8,128)(2,1)}, bf16[4,576,1280]{2,1,0:T(8,128)(2,1)}, f32[1280,1]{1,0:T(8,128)}) custom-call(s32[16]{0:T(128)} %concatenate.49.info, bf16[1280,1536]{1,0:T(8,128)(2,1)} %bitcast.110, bf16[1280,1536]{1,0:T(8,128)(2,1)} %bitcast.129, f32[1280,1]{1,0:T(8,128)} %bitcast.114, ...), custom_call_target="tpu_custom_call" | custom-call | flops 1 | bytes 1 | tf_op jit(solution)/shard_map/expert/pallas_call | solution.py:670
  304.1 14.6 %expert_gradients.2 = bf16[4,576,1536]{2,1,0:T(8,128)(2,1)} custom-call(bf16[4,576,1280]{2,1,0:T(8,128)(2,1)} %get-tuple-element.219.acts, bf16[1280,1536]{1,0:T(8,128)(2,1)} %bitcast.111, bf16[1280,1536]{1,0:T(8,128)(2,1)} %get-tuple-element.220.grads), custom_call_target="tpu_custom_call" | custom-call | flops 1 | bytes 1 | tf_op jit(solution)/shard_map/expert_gradients/pallas_call | solution.py:699
  318.8 10.0 %all-gather.3.cloned.1.call-done = bf16[2304,1536]{1,0:T(8,128)(2,1)} async-done(((bf16[576,1536]{1,0:T(8,128)(2,1)}), bf16[2304,1536]{1,0:T(8,128)(2,1)}) %all-gather.3.cloned.1.call-update) | async-done | bytes 7077904 | tf_op jit(solution)/shard_map/all_gather | solution.py:1419
  328.9 30.2 %expert.3 = (bf16[1280,1536]{1,0:T(8,128)(2,1)}, bf16[1280,1536]{1,0:T(8,128)(2,1)}, bf16[1280,1536]{1,0:T(8,128)(2,1)}, bf16[4,576,1280]{2,1,0:T(8,128)(2,1)}, f32[1280,1]{1,0:T(8,128)}) custom-call(s32[16]{0:T(128)} %concatenate.49.info, bf16[1280,1536]{1,0:T(8,128)(2,1)} %bitcast.112, bf16[1280,1536]{1,0:T(8,128)(2,1)} %bitcast.130, f32[1280,1]{1,0:T(8,128)} %bitcast.115, ...), custom_call_target="tpu_custom_call" | custom-call | flops 1 | bytes 1 | tf_op jit(solution)/shard_map/expert/pallas_call | solution.py:670
  359.1 8.0 %combine.7 = bf16[4,544,1536]{2,1,0:T(8,128)(2,1)} custom-call(s32[16]{0:T(128)} %concatenate.49.info, bf16[8,320,512]{2,1,0:T(8,128)(2,1)} %get-tuple-element.165.chosen, bf16[8,160,1536]{2,1,0:T(8,128)(2,1)} %bitcast.118, bf16[8,160,1536]{2,1,0:T(8,128)(2,1)} %bitcast.122, f32[8,160,1]{2,1,0:T(8,128)} %bitcast.133, f32[8,160,1]{2,1,0:T(8,128)} %bitcast.135), custom_call_target="tpu_custom_call" | custom-call | flops 1 | bytes 1 | tf_op jit(solution)/shard_map/combine/pallas_call | solution.py:762
  367.2 7.3 %combine.5 = bf16[4,512,1536]{2,1,0:T(8,128)(2,1)} custom-call(s32[16]{0:T(128)} %concatenate.49.info, bf16[8,320,512]{2,1,0:T(8,128)(2,1)} %get-tuple-element.165.chosen, bf16[8,160,1536]{2,1,0:T(8,128)(2,1)} %bitcast.116, bf16[8,160,1536]{2,1,0:T(8,128)(2,1)} %bitcast.120), custom_call_target="tpu_custom_call" | custom-call | flops 1 | bytes 1 | tf_op jit(solution)/shard_map/combine/pallas_call | solution.py:762
  375.1 8.1 %combine.6.keep = bf16[4,544,1536]{2,1,0:T(8,128)(2,1)} custom-call(s32[16]{0:T(128)} %concatenate.49.info, bf16[8,320,512]{2,1,0:T(8,128)(2,1)} %get-tuple-element.165.chosen, bf16[8,160,1536]{2,1,0:T(8,128)(2,1)} %bitcast.119, bf16[8,160,1536]{2,1,0:T(8,128)(2,1)} %bitcast.123, f32[8,160,1]{2,1,0:T(8,128)} %bitcast.134, f32[8,160,1]{2,1,0:T(8,128)} %bitcast.136), custom_call_target="tpu_custom_call" | custom-call | flops 1 | bytes 1 | tf_op jit(solution)/shard_map/combine/pallas_call | solution.py:762
  385.9 7.8 %chip_sums.5 = (bf16[2,272,1536]{2,1,0:T(8,128)(2,1)}, bf16[2,272,1536]{2,1,0:T(8,128)(2,1)}, bf16[2,272,1536]{2,1,0:T(8,128)(2,1)}, bf16[2,272,1536]{2,1,0:T(8,128)(2,1)}) custom-call(bf16[4,544,1536]{2,1,0:T(8,128)(2,1)} %combine.6.keep, bf16[4,544,1536]{2,1,0:T(8,128)(2,1)} %copy-done.10), custom_call_target="tpu_custom_call" | custom-call | flops 1 | bytes 1 | tf_op jit(solution)/shard_map/chip_sums/pallas_call | solution.py:811
  396.7 7.7 %combine.4.keep = bf16[4,512,1536]{2,1,0:T(8,128)(2,1)} custom-call(s32[16]{0:T(128)} %concatenate.49.info, bf16[8,320,512]{2,1,0:T(8,128)(2,1)} %get-tuple-element.165.chosen, bf16[8,160,1536]{2,1,0:T(8,128)(2,1)} %bitcast.117, bf16[8,160,1536]{2,1,0:T(8,128)(2,1)} %bitcast.121), custom_call_target="tpu_custom_call" | custom-call | flops 1 | bytes 1 | tf_op jit(solution)/shard_map/combine/pallas_call | solution.py:762
  404.4 14.6 %expert_gradients.3 = bf16[4,576,1536]{2,1,0:T(8,128)(2,1)} custom-call(bf16[4,576,1280]{2,1,0:T(8,128)(2,1)} %get-tuple-element.236.acts, bf16[1280,1536]{1,0:T(8,128)(2,1)} %bitcast.113, bf16[1280,1536]{1,0:T(8,128)(2,1)} %get-tuple-element.237.grads), custom_call_target="tpu_custom_call" | custom-call | flops 1 | bytes 1 | tf_op jit(solution)/shard_map/expert_gradients/pallas_call | solution.py:699
  419.0 13.4 %collective-permute-done.35.got_x.rest_1_ = bf16[2,272,1536]{2,1,0:T(8,128)(2,1)S(1)} collective-permute-done((bf16[2,272,1536]{2,1,0:T(8,128)(2,1)}, bf16[2,272,1536]{2,1,0:T(8,128)(2,1)S(1)}, u32[]{:S(2)}, u32[]{:S(2)}) %collective-permute-start.35) | collective-permute-done | bytes 1671200 | tf_op jit(solution)/shard_map/ppermute | solution.py:1236
  440.4 7.5 %chip_sums.4 = (bf16[2,256,1536]{2,1,0:T(8,128)(2,1)}, bf16[2,256,1536]{2,1,0:T(8,128)(2,1)}, bf16[2,256,1536]{2,1,0:T(8,128)(2,1)}, bf16[2,256,1536]{2,1,0:T(8,128)(2,1)}) custom-call(bf16[4,512,1536]{2,1,0:T(8,128)(2,1)} %combine.4.keep, bf16[4,512,1536]{2,1,0:T(8,128)(2,1)} %collective-permute-done.33.got), custom_call_target="tpu_custom_call" | custom-call | flops 1 | bytes 1 | tf_op jit(solution)/shard_map/chip_sums/pallas_call | solution.py:811
  447.9 10.0 %collective-permute-done.37.rest_2_ = bf16[272,1536]{1,0:T(8,128)(2,1)} collective-permute-done((bf16[272,1536]{1,0:T(8,128)(2,1)}, bf16[272,1536]{1,0:T(8,128)(2,1)}, u32[]{:S(2)}, u32[]{:S(2)}) %collective-permute-start.37) | collective-permute-done | bytes 835616 | tf_op jit(solution)/shard_map/ppermute | solution.py:1236
  461.0 13.3 %experts_norm_back.1 = (f32[512,1536]{1,0:T(8,128)}, bf16[512,1536]{1,0:T(8,128)(2,1)}, bf16[512,1536]{1,0:T(8,128)(2,1)}, f32[1,1536]{1,0:T(1,128)}, f32[16,1536]{1,0:T(8,128)}) custom-call(s32[16]{0:T(128)} %concatenate.49.info, f32[512,1536]{1,0:T(8,128)} %get-tuple-element.174.residual, bf16[512,1536]{1,0:T(8,128)(2,1)} %get-tuple-element.175.rows.normed, ...), custom_call_target="tpu_custom_call" | custom-call | flops 1 | bytes 1 | tf_op jit(solution)/shard_map/experts_norm_back/pallas_call | solution.py:922
  474.3 15.4 %tree_attention_back.1 = (bf16[512,1536]{1,0:T(8,128)(2,1)}, f32[512,512]{1,0:T(8,128)}, f32[512,512]{1,0:T(8,128)}) custom-call(s32[16]{0:T(128)} %concatenate.49.info, bf16[512,1536]{1,0:T(8,128)(2,1)} %query_projection.1.queries, bf16[512,512]{1,0:T(8,128)(2,1)} %get-tuple-element.170.own, bf16[512,512]{1,0:T(8,128)(2,1)} %collective-permute-done.16.partner, ...), custom_call_target="tpu_custom_call" | custom-call | flops 1 | bytes 1 | tf_op jit(solution)/shard_map/tree_attention_back/pallas_call | solution.py:338
  494.7 13.3 %weight_gradients.2 = (bf16[4,4,208,768]{3,2,1,0:T(8,128)(2,1)}, bf16[4,4,208,768]{3,2,1,0:T(8,128)(2,1)}) custom-call(s32[16]{0:T(128)} %concatenate.49.info, bf16[512,1536]{1,0:T(8,128)(2,1)} %get-tuple-element.169.normed.rest_0_, bf16[512,1536]{1,0:T(8,128)(2,1)} %tree_attention.1.heads.rest_1_, bf16[512,1536]{1,0:T(8,128)(2,1)} %get-tuple-element.264.rest_2_.grad_query, ...), custom_call_target="tpu_custom_call" | custom-call | flops 1 | bytes 1 | tf_op jit(solution)/shard_map/weight_gradients/pallas_call | solution.py:1074
  508.0 8.7 %collective-permute-done.42 = bf16[4,4,208,768]{3,2,1,0:T(8,128)(2,1)S(1)} collective-permute-done((bf16[4,4,208,768]{3,2,1,0:T(8,128)(2,1)}, bf16[4,4,208,768]{3,2,1,0:T(8,128)(2,1)S(1)}, u32[]{:S(2)}, u32[]{:S(2)}) %collective-permute-start.42) | collective-permute-done | bytes 5111840 | tf_op jit(solution)/shard_map/ppermute | solution.py:1236
  519.0 6.6 chip_sums.6
  528.1 8.1 %normed_gradient.1.query_part = f32[512,1536]{1,0:T(8,128)} custom-call(s32[16]{0:T(128)} %concatenate.49.info, bf16[512,1536]{1,0:T(8,128)(2,1)} %get-tuple-element.264.rest_2_.grad_query, bf16[4,208,896]{2,1,0:T(8,128)(2,1)} %copy-done.1, bf16[4,208,896]{2,1,0:T(8,128)(2,1)} %copy-done.5, bf16[4,208,896]{2,1,0:T(8,128)(2,1)} %copy-done.3, ...), custom_call_target="tpu_custom_call" | custom-call | flops 1 | bytes 1 | tf_op jit(solution)/shard_map/normed_gradient/pallas_call | solution.py:999
  536.3 19.7 %collective-permute-done.43.got_x = bf16[2,416,768]{2,1,0:T(8,128)(2,1)S(1)} collective-permute-done((bf16[2,416,768]{2,1,0:T(8,128)(2,1)}, bf16[2,416,768]{2,1,0:T(8,128)(2,1)S(1)}, u32[]{:S(2)}, u32[]{:S(2)}) %collective-permute-start.43) | collective-permute-done | bytes 1277984 | tf_op jit(solution)/shard_map/ppermute | solution.py:1236
  564.2 5.7 weight_gradients.3
  582.5 8.2 %token_gradient.1 = (bf16[512,1536]{1,0:T(8,128)(2,1)}, f32[1,1536]{1,0:T(1,128)}) custom-call(s32[16]{0:T(128)} %concatenate.49.info, f32[512,1536]{1,0:T(8,128)} %normed_gradient.1.query_part, bf16[512,512]{1,0:T(8,128)(2,1)} %join_key_value_gradients.1.rest_1_.grad_pair, bf16[512,1536]{1,0:T(8,128)(2,1)} %tokens.4, ...), custom_call_target="tpu_custom_call" | custom-call | flops 1 | bytes 1 | tf_op jit(solution)/shard_map/token_gradient/pallas_call | solution.py:1026
  608.3 14.0 %collective-permute-done.50 = bf16[256,1536]{1,0:T(8,128)(2,1)} collective-permute-done((bf16[256,1536]{1,0:T(8,128)(2,1)}, bf16[256,1536]{1,0:T(8,128)(2,1)}, u32[]{:S(2)}, u32[]{:S(2)}) %collective-permute-start.50) | collective-permute-done | bytes 786464 | tf_op jit(solution)/shard_map/ppermute | solution.py:1236
  627.1 8.1 %collective-permute-done.54.rest_3_ = bf16[208,896]{1,0:T(8,128)(2,1)S(1)} collective-permute-done((bf16[208,896]{1,0:T(8,128)(2,1)S(1)}, bf16[208,896]{1,0:T(8,128)(2,1)S(1)}, u32[]{:S(2)}, u32[]{:S(2)}) %collective-permute-start.54) | collective-permute-done | bytes 372768 | tf_op jit(solution)/shard_map/ppermute | solution.py:1220
  640.1 7.4 %collective-permute-start.57 = (bf16[208,896]{1,0:T(8,128)(2,1)S(1)}, bf16[208,896]{1,0:T(8,128)(2,1)S(1)}, u32[]{:S(2)}, u32[]{:S(2)}) collective-permute-start(bf16[208,896]{1,0:T(8,128)(2,1)S(1)} %get-tuple-element.297), channel_id=1, source_target_pairs={{0,3},{3,0},{4,7},{7,4},{8,11},{11,8},{12,15},{15,12},{16,19},{19,... | collective-permute-start | bytes 1118216 | tf_op jit(solution)/shard_map/ppermute | solution.py:1191
  649.1 5.1 expert_sums.1
  654.2 3.8 collective-permute-done.57.rest_2_
  (331 shorter events, 170.1 us)
Async XLA Ops:
  7.2 321.7 %all-gather.3.cloned.1.call-start = ((), (), s32[]{:S(2)}) async-start(), calls=%async_computation.4 | async-start | bytes 8847360 | tf_op jit(solution)/shard_map/all_gather | solution.py:1419
  12.7 19.0 %collective-permute-start = (bf16[208,896]{1,0:T(8,128)(2,1)S(1)}, bf16[208,896]{1,0:T(8,128)(2,1)S(1)}, u32[]{:S(2)}, u32[]{:S(2)}) collective-permute-start(bf16[208,896]{1,0:T(8,128)(2,1)S(1)} %concatenate.53), channel_id=1, source_target_pairs={{1,0},{2,1},{3,2},{5,4},{6,5},{7,6},{9,8},{10,9},{11,10},{13,12},{... | collective-permute-start | bytes 1118216 | tf_op jit(solution)/shard_map/ppermute | solution.py:1187
  14.1 17.5 %collective-permute-start.1 = (bf16[208,896]{1,0:T(8,128)(2,1)S(1)}, bf16[208,896]{1,0:T(8,128)(2,1)}, u32[]{:S(2)}, u32[]{:S(2)}) collective-permute-start(bf16[208,896]{1,0:T(8,128)(2,1)S(1)} %concatenate.53), channel_id=1, source_target_pairs={{0,1},{1,2},{2,3},{4,5},{5,6},{6,7},{8,9},{9,10},{10,11},{12,13},{... | collective-permute-start | bytes 1118216 | tf_op jit(solution)/shard_map/ppermute | solution.py:1187
  20.4 31.3 %collective-permute-start.4 = (bf16[208,896]{1,0:T(8,128)(2,1)S(1)}, bf16[208,896]{1,0:T(8,128)(2,1)}, u32[]{:S(2)}, u32[]{:S(2)}) collective-permute-start(bf16[208,896]{1,0:T(8,128)(2,1)S(1)} %concatenate.53), channel_id=1, source_target_pairs={{0,3},{3,0},{4,7},{7,4},{8,11},{11,8},{12,15},{15,12},{16,19},{19,... | collective-permute-start | bytes 1118216 | tf_op jit(solution)/shard_map/ppermute | solution.py:1191
  23.4 29.4 %collective-permute-start.3 = (bf16[208,896]{1,0:T(8,128)(2,1)S(1)}, bf16[208,896]{1,0:T(8,128)(2,1)}, u32[]{:S(2)}, u32[]{:S(2)}) collective-permute-start(bf16[208,896]{1,0:T(8,128)(2,1)S(1)} %concatenate.53), channel_id=1, source_target_pairs={{0,2},{1,3},{2,0},{3,1},{4,6},{5,7},{6,4},{7,5},{8,10},{9,11},{10,... | collective-permute-start | bytes 1118216 | tf_op jit(solution)/shard_map/ppermute | solution.py:1195
  31.6 58.8 %collective-permute-start.8 = (bf16[576,1536]{1,0:T(8,128)(2,1)}, bf16[576,1536]{1,0:T(8,128)(2,1)}, u32[]{:S(2)}, u32[]{:S(2)}) collective-permute-start(bf16[576,1536]{1,0:T(8,128)(2,1)} %pad_maximum_fusion.2.rest_0_), channel_id=1, source_target_pairs={{1,0},{2,1},{3,2},{5,4},{6,5},{7,6},{9,8},{10,9},{11,10},{13,12},{... | collective-permute-start | bytes 5308424 | tf_op jit(solution)/shard_map/ppermute | solution.py:1187
  32.9 57.5 %collective-permute-start.9 = (bf16[576,1536]{1,0:T(8,128)(2,1)}, bf16[576,1536]{1,0:T(8,128)(2,1)}, u32[]{:S(2)}, u32[]{:S(2)}) collective-permute-start(bf16[576,1536]{1,0:T(8,128)(2,1)} %pad_maximum_fusion.2.rest_0_), channel_id=1, source_target_pairs={{0,1},{1,2},{2,3},{4,5},{5,6},{6,7},{8,9},{9,10},{10,11},{12,13},{... | collective-permute-start | bytes 5308424 | tf_op jit(solution)/shard_map/ppermute | solution.py:1187
  54.1 35.1 %collective-permute-start.6 = (bf16[4,208,896]{2,1,0:T(8,128)(2,1)S(1)}, bf16[4,208,896]{2,1,0:T(8,128)(2,1)S(1)}, u32[]{:S(2)}, u32[]{:S(2)}) collective-permute-start(bf16[4,208,896]{2,1,0:T(8,128)(2,1)S(1)} %pad_maximum_fusion.4.rest_0_.rest_6_), channel_id=1, source_target_pairs={{0,8},{4,12},{8,0},{12,4},{16,24},{20,28},{24,16},{28,20},{1,9},{5... | collective-permute-start | bytes 4472840 | tf_op jit(solution)/shard_map/ppermute | solution.py:1236
  55.7 34.7 %collective-permute-start.7 = (bf16[4,208,896]{2,1,0:T(8,128)(2,1)S(1)}, bf16[4,208,896]{2,1,0:T(8,128)(2,1)S(1)}, u32[]{:S(2)}, u32[]{:S(2)}) collective-permute-start(bf16[4,208,896]{2,1,0:T(8,128)(2,1)S(1)} %pad_maximum_fusion.4.rest_0_.rest_6_), channel_id=1, source_target_pairs={{0,16},{4,20},{8,24},{12,28},{16,0},{20,4},{24,8},{28,12},{1,17},{... | collective-permute-start | bytes 4472840 | tf_op jit(solution)/shard_map/ppermute | solution.py:1236
  90.7 21.5 %collective-permute-start.10 = (bf16[8,208,896]{2,1,0:T(8,128)(2,1)S(1)}, bf16[8,208,896]{2,1,0:T(8,128)(2,1)S(1)}, u32[]{:S(2)}, u32[]{:S(2)}) collective-permute-start(bf16[8,208,896]{2,1,0:T(8,128)(2,1)S(1)} %pad_maximum_fusion), channel_id=1, source_target_pairs={{0,4},{4,0},{8,12},{12,8},{16,20},{20,16},{24,28},{28,24},{1,5},{5... | collective-permute-start | bytes 8945672 | tf_op jit(solution)/shard_map/ppermute | solution.py:1236
  90.9 19.1 %collective-permute-start.11 = (bf16[2,208,896]{2,1,0:T(8,128)(2,1)S(1)}, bf16[2,208,896]{2,1,0:T(8,128)(2,1)S(1)}, u32[]{:S(2)}, u32[]{:S(2)}) collective-permute-start(bf16[2,208,896]{2,1,0:T(8,128)(2,1)S(1)} %slice.144), channel_id=1, source_target_pairs={{0,16},{4,20},{8,24},{12,28},{16,0},{20,4},{24,8},{28,12},{1,17},{... | collective-permute-start | bytes 2236424 | tf_op jit(solution)/shard_map/ppermute | solution.py:1236
  92.5 18.9 %collective-permute-start.13 = (bf16[2,208,896]{2,1,0:T(8,128)(2,1)S(1)}, bf16[2,208,896]{2,1,0:T(8,128)(2,1)}, u32[]{:S(2)}, u32[]{:S(2)}) collective-permute-start(bf16[2,208,896]{2,1,0:T(8,128)(2,1)S(1)} %slice.147), channel_id=1, source_target_pairs={{0,8},{4,12},{8,0},{12,4},{16,24},{20,28},{24,16},{28,20},{1,9},{5... | collective-permute-start | bytes 2236424 | tf_op jit(solution)/shard_map/ppermute | solution.py:1236
  93.1 45.8 %collective-permute-start.2 = (bf16[576,1536]{1,0:T(8,128)(2,1)}, bf16[576,1536]{1,0:T(8,128)(2,1)}, u32[]{:S(2)}, u32[]{:S(2)}) collective-permute-start(bf16[576,1536]{1,0:T(8,128)(2,1)} %pad_maximum_fusion.2.rest_0_), channel_id=1, source_target_pairs={{0,3},{3,0},{4,7},{7,4},{8,11},{11,8},{12,15},{15,12},{16,19},{19,... | collective-permute-start | bytes 5308424 | tf_op jit(solution)/shard_map/ppermute | solution.py:1191
  111.4 33.8 %collective-permute-start.15 = (bf16[512,1536]{1,0:T(8,128)(2,1)S(1)}, bf16[512,1536]{1,0:T(8,128)(2,1)}, u32[]{:S(2)}, u32[]{:S(2)}) collective-permute-start(bf16[512,1536]{1,0:T(8,128)(2,1)S(1)} %copy-done.13), channel_id=1, source_target_pairs={{0,4},{4,0},{8,12},{12,8},{16,20},{20,16},{24,28},{28,24},{1,5},{5... | collective-permute-start | bytes 4718600 | tf_op jit(solution)/shard_map/ppermute | solution.py:1236
  111.4 52.2 %collective-permute-start.17 = (bf16[512,1536]{1,0:T(8,128)(2,1)S(1)}, bf16[512,1536]{1,0:T(8,128)(2,1)S(1)}, u32[]{:S(2)}, u32[]{:S(2)}) collective-permute-start(bf16[512,1536]{1,0:T(8,128)(2,1)S(1)} %copy-done.13), channel_id=1, source_target_pairs={{0,8},{4,12},{8,0},{12,4},{16,24},{20,28},{24,16},{28,20},{1,9},{5... | collective-permute-start | bytes 4718600 | tf_op jit(solution)/shard_map/ppermute | solution.py:1236
  117.0 46.7 %collective-permute-start.18 = (bf16[512,1536]{1,0:T(8,128)(2,1)S(1)}, bf16[512,1536]{1,0:T(8,128)(2,1)}, u32[]{:S(2)}, u32[]{:S(2)}) collective-permute-start(bf16[512,1536]{1,0:T(8,128)(2,1)S(1)} %copy-done.13), channel_id=1, source_target_pairs={{0,16},{4,20},{8,24},{12,28},{16,0},{20,4},{24,8},{28,12},{1,17},{... | collective-permute-start | bytes 4718600 | tf_op jit(solution)/shard_map/ppermute | solution.py:1236
  143.9 15.4 %collective-permute-start.16 = (bf16[512,512]{1,0:T(8,128)(2,1)}, bf16[512,512]{1,0:T(8,128)(2,1)}, u32[]{:S(2)}, u32[]{:S(2)}) collective-permute-start(bf16[512,512]{1,0:T(8,128)(2,1)} %get-tuple-element.170.own), channel_id=1, source_target_pairs={{1,0},{3,2},{5,4},{7,6},{9,8},{11,10},{13,12},{15,14},{17,16},{19,... | collective-permute-start | bytes 1572872 | tf_op jit(solution)/shard_map/ppermute | solution.py:1391
  162.2 39.3 %collective-permute-start.32 = (bf16[576,1536]{1,0:T(8,128)(2,1)}, bf16[576,1536]{1,0:T(8,128)(2,1)}, u32[]{:S(2)}, u32[]{:S(2)}) collective-permute-start(bf16[576,1536]{1,0:T(8,128)(2,1)} %select_select_fusion), channel_id=1, source_target_pairs={{3,1},{1,0},{0,2},{2,3},{7,5},{5,4},{4,6},{6,7},{11,9},{9,8},{8,10... | collective-permute-start | bytes 5308424 | tf_op jit(solution)/shard_map/ppermute | solution.py:1202
  163.6 24.9 %collective-permute-start.21 = (bf16[512,1536]{1,0:T(8,128)(2,1)S(1)}, bf16[512,1536]{1,0:T(8,128)(2,1)S(1)}, u32[]{:S(2)}, u32[]{:S(2)}) collective-permute-start(bf16[512,1536]{1,0:T(8,128)(2,1)S(1)} %collective-permute-done.17.rest_2_), channel_id=1, source_target_pairs={{0,4},{4,0},{8,12},{12,8},{16,20},{20,16},{24,28},{28,24},{1,5},{5... | collective-permute-start | bytes 4718600 | tf_op jit(solution)/shard_map/ppermute | solution.py:1236
  163.7 25.9 %collective-permute-start.22 = (bf16[512,1536]{1,0:T(8,128)(2,1)}, bf16[512,1536]{1,0:T(8,128)(2,1)}, u32[]{:S(2)}, u32[]{:S(2)}) collective-permute-start(bf16[512,1536]{1,0:T(8,128)(2,1)} %collective-permute-done.18.rest_4_), channel_id=1, source_target_pairs={{0,4},{4,0},{8,12},{12,8},{16,20},{20,16},{24,28},{28,24},{1,5},{5... | collective-permute-start | bytes 4718600 | tf_op jit(solution)/shard_map/ppermute | solution.py:1236
  165.2 19.8 %collective-permute-start.19 = (bf16[256,1536]{1,0:T(8,128)(2,1)}, bf16[256,1536]{1,0:T(8,128)(2,1)}, u32[]{:S(2)}, u32[]{:S(2)}) collective-permute-start(bf16[256,1536]{1,0:T(8,128)(2,1)} %slice.149), channel_id=1, source_target_pairs={{0,16},{4,20},{8,24},{12,28},{16,0},{20,4},{24,8},{28,12},{1,17},{... | collective-permute-start | bytes 2359304 | tf_op jit(solution)/shard_map/ppermute | solution.py:1236
  167.7 19.6 %collective-permute-start.20 = (bf16[256,1536]{1,0:T(8,128)(2,1)}, bf16[256,1536]{1,0:T(8,128)(2,1)}, u32[]{:S(2)}, u32[]{:S(2)}) collective-permute-start(bf16[256,1536]{1,0:T(8,128)(2,1)} %slice.150), channel_id=1, source_target_pairs={{0,8},{4,12},{8,0},{12,4},{16,24},{20,28},{24,16},{28,20},{1,9},{5... | collective-permute-start | bytes 2359304 | tf_op jit(solution)/shard_map/ppermute | solution.py:1236
  201.5 257.5 %reduce-scatter.3.cloned.1.call-start = ((), (), s32[]{:S(2)}) async-start(), calls=%async_computation.2 | async-start | bytes 8847360 | tf_op jit(solution)/shard_map/reduce_scatter | solution.py:1478
  202.1 19.5 %collective-permute-start.25 = (bf16[512,1536]{1,0:T(8,128)(2,1)S(1)}, bf16[512,1536]{1,0:T(8,128)(2,1)}, u32[]{:S(2)}, u32[]{:S(2)}) collective-permute-start(bf16[512,1536]{1,0:T(8,128)(2,1)S(1)} %copy-done.14), channel_id=1, source_target_pairs={{0,4},{4,0},{8,12},{12,8},{16,20},{20,16},{24,28},{28,24},{1,5},{5... | collective-permute-start | bytes 4718600 | tf_op jit(solution)/shard_map/ppermute | solution.py:1236
  202.4 36.7 %collective-permute-start.23 = (bf16[512,1536]{1,0:T(8,128)(2,1)S(1)}, bf16[512,1536]{1,0:T(8,128)(2,1)}, u32[]{:S(2)}, u32[]{:S(2)}) collective-permute-start(bf16[512,1536]{1,0:T(8,128)(2,1)S(1)} %copy-done.14), channel_id=1, source_target_pairs={{0,8},{4,12},{8,0},{12,4},{16,24},{20,28},{24,16},{28,20},{1,9},{5... | collective-permute-start | bytes 4718600 | tf_op jit(solution)/shard_map/ppermute | solution.py:1236
  203.9 36.4 %collective-permute-start.24 = (bf16[512,1536]{1,0:T(8,128)(2,1)S(1)}, bf16[512,1536]{1,0:T(8,128)(2,1)}, u32[]{:S(2)}, u32[]{:S(2)}) collective-permute-start(bf16[512,1536]{1,0:T(8,128)(2,1)S(1)} %copy-done.14), channel_id=1, source_target_pairs={{0,16},{4,20},{8,24},{12,28},{16,0},{20,4},{24,8},{28,12},{1,17},{... | collective-permute-start | bytes 4718600 | tf_op jit(solution)/shard_map/ppermute | solution.py:1236
  240.3 16.9 %collective-permute-start.29 = (bf16[512,1536]{1,0:T(8,128)(2,1)}, bf16[512,1536]{1,0:T(8,128)(2,1)S(1)}, u32[]{:S(2)}, u32[]{:S(2)}) collective-permute-start(bf16[512,1536]{1,0:T(8,128)(2,1)} %collective-permute-done.24.rows), channel_id=1, source_target_pairs={{0,4},{4,0},{8,12},{12,8},{16,20},{20,16},{24,28},{28,24},{1,5},{5... | collective-permute-start | bytes 4718600 | tf_op jit(solution)/shard_map/ppermute | solution.py:1236
  243.1 19.5 %collective-permute-start.27 = (bf16[256,1536]{1,0:T(8,128)(2,1)S(1)}, bf16[256,1536]{1,0:T(8,128)(2,1)S(1)}, u32[]{:S(2)}, u32[]{:S(2)}) collective-permute-start(bf16[256,1536]{1,0:T(8,128)(2,1)S(1)} %slice.153), channel_id=1, source_target_pairs={{0,16},{4,20},{8,24},{12,28},{16,0},{20,4},{24,8},{28,12},{1,17},{... | collective-permute-start | bytes 2359304 | tf_op jit(solution)/shard_map/ppermute | solution.py:1236
  244.7 19.2 %collective-permute-start.28 = (bf16[256,1536]{1,0:T(8,128)(2,1)S(1)}, bf16[256,1536]{1,0:T(8,128)(2,1)S(1)}, u32[]{:S(2)}, u32[]{:S(2)}) collective-permute-start(bf16[256,1536]{1,0:T(8,128)(2,1)S(1)} %slice.154), channel_id=1, source_target_pairs={{0,8},{4,12},{8,0},{12,4},{16,24},{20,28},{24,16},{28,20},{1,9},{5... | collective-permute-start | bytes 2359304 | tf_op jit(solution)/shard_map/ppermute | solution.py:1236
  318.8 304.9 %reduce-scatter.5.cloned.1.call-start = ((), (), s32[]{:S(2)}) async-start(), calls=%async_computation.3 | async-start | bytes 8847360 | tf_op jit(solution)/shard_map/reduce_scatter | solution.py:1508
  367.1 16.0 %collective-permute-start.34 = (bf16[4,544,1536]{2,1,0:T(8,128)(2,1)}, bf16[4,544,1536]{2,1,0:T(8,128)(2,1)S(1)}, u32[]{:S(2)}, u32[]{:S(2)}) collective-permute-start(bf16[4,544,1536]{2,1,0:T(8,128)(2,1)} %combine.7), channel_id=1, source_target_pairs={{0,4},{4,0},{8,12},{12,8},{16,20},{20,16},{24,28},{28,24},{1,5},{5... | collective-permute-start | bytes 20054024 | tf_op jit(solution)/shard_map/ppermute | solution.py:1236
  374.6 65.8 %collective-permute-start.33 = (bf16[4,512,1536]{2,1,0:T(8,128)(2,1)}, bf16[4,512,1536]{2,1,0:T(8,128)(2,1)}, u32[]{:S(2)}, u32[]{:S(2)}) collective-permute-start(bf16[4,512,1536]{2,1,0:T(8,128)(2,1)} %combine.5), channel_id=1, source_target_pairs={{0,4},{4,0},{8,12},{12,8},{16,20},{20,16},{24,28},{28,24},{1,5},{5... | collective-permute-start | bytes 18874376 | tf_op jit(solution)/shard_map/ppermute | solution.py:1236
  393.7 38.7 %collective-permute-start.35 = (bf16[2,272,1536]{2,1,0:T(8,128)(2,1)}, bf16[2,272,1536]{2,1,0:T(8,128)(2,1)S(1)}, u32[]{:S(2)}, u32[]{:S(2)}) collective-permute-start(bf16[2,272,1536]{2,1,0:T(8,128)(2,1)} %get-tuple-element.233), channel_id=1, source_target_pairs={{0,8},{4,12},{8,0},{12,4},{16,24},{20,28},{24,16},{28,20},{1,9},{5... | collective-permute-start | bytes 5013512 | tf_op jit(solution)/shard_map/ppermute | solution.py:1236
  395.2 38.4 %collective-permute-start.36 = (bf16[2,272,1536]{2,1,0:T(8,128)(2,1)}, bf16[2,272,1536]{2,1,0:T(8,128)(2,1)S(1)}, u32[]{:S(2)}, u32[]{:S(2)}) collective-permute-start(bf16[2,272,1536]{2,1,0:T(8,128)(2,1)} %get-tuple-element.234), channel_id=1, source_target_pairs={{0,16},{4,20},{8,24},{12,28},{16,0},{20,4},{24,8},{28,12},{1,17},{... | collective-permute-start | bytes 5013512 | tf_op jit(solution)/shard_map/ppermute | solution.py:1236
  438.1 19.8 %collective-permute-start.37 = (bf16[272,1536]{1,0:T(8,128)(2,1)}, bf16[272,1536]{1,0:T(8,128)(2,1)}, u32[]{:S(2)}, u32[]{:S(2)}) collective-permute-start(bf16[272,1536]{1,0:T(8,128)(2,1)} %get-tuple-element.241), channel_id=1, source_target_pairs={{0,16},{4,20},{8,24},{12,28},{16,0},{20,4},{24,8},{28,12},{1,17},{... | collective-permute-start | bytes 2506760 | tf_op jit(solution)/shard_map/ppermute | solution.py:1236
  439.5 19.5 %collective-permute-start.38 = (bf16[272,1536]{1,0:T(8,128)(2,1)}, bf16[272,1536]{1,0:T(8,128)(2,1)}, u32[]{:S(2)}, u32[]{:S(2)}) collective-permute-start(bf16[272,1536]{1,0:T(8,128)(2,1)} %get-tuple-element.242), channel_id=1, source_target_pairs={{0,8},{4,12},{8,0},{12,4},{16,24},{20,28},{24,16},{28,20},{1,9},{5... | collective-permute-start | bytes 2506760 | tf_op jit(solution)/shard_map/ppermute | solution.py:1236
  459.1 34.4 %collective-permute-start.39 = (bf16[2,256,1536]{2,1,0:T(8,128)(2,1)}, bf16[2,256,1536]{2,1,0:T(8,128)(2,1)S(1)}, u32[]{:S(2)}, u32[]{:S(2)}) collective-permute-start(bf16[2,256,1536]{2,1,0:T(8,128)(2,1)} %get-tuple-element.245), channel_id=1, source_target_pairs={{0,8},{4,12},{8,0},{12,4},{16,24},{20,28},{24,16},{28,20},{1,9},{5... | collective-permute-start | bytes 4718600 | tf_op jit(solution)/shard_map/ppermute | solution.py:1236
  460.3 34.4 %collective-permute-start.40 = (bf16[2,256,1536]{2,1,0:T(8,128)(2,1)}, bf16[2,256,1536]{2,1,0:T(8,128)(2,1)S(1)}, u32[]{:S(2)}, u32[]{:S(2)}) collective-permute-start(bf16[2,256,1536]{2,1,0:T(8,128)(2,1)} %get-tuple-element.246), channel_id=1, source_target_pairs={{0,16},{4,20},{8,24},{12,28},{16,0},{20,4},{24,8},{28,12},{1,17},{... | collective-permute-start | bytes 4718600 | tf_op jit(solution)/shard_map/ppermute | solution.py:1236
  525.6 30.4 %collective-permute-start.43 = (bf16[2,416,768]{2,1,0:T(8,128)(2,1)}, bf16[2,416,768]{2,1,0:T(8,128)(2,1)S(1)}, u32[]{:S(2)}, u32[]{:S(2)}) collective-permute-start(bf16[2,416,768]{2,1,0:T(8,128)(2,1)} %get-tuple-element.262), channel_id=1, source_target_pairs={{0,8},{4,12},{8,0},{12,4},{16,24},{20,28},{24,16},{28,20},{1,9},{5... | collective-permute-start | bytes 3833864 | tf_op jit(solution)/shard_map/ppermute | solution.py:1236
  526.2 30.1 %collective-permute-start.44 = (bf16[2,416,768]{2,1,0:T(8,128)(2,1)}, bf16[2,416,768]{2,1,0:T(8,128)(2,1)S(1)}, u32[]{:S(2)}, u32[]{:S(2)}) collective-permute-start(bf16[2,416,768]{2,1,0:T(8,128)(2,1)} %get-tuple-element.263), channel_id=1, source_target_pairs={{0,16},{4,20},{8,24},{12,28},{16,0},{20,4},{24,8},{28,12},{1,17},{... | collective-permute-start | bytes 3833864 | tf_op jit(solution)/shard_map/ppermute | solution.py:1236
  526.8 33.5 %collective-permute-start.41 = (bf16[512,512]{1,0:T(8,128)(2,1)S(1)}, bf16[512,512]{1,0:T(8,128)(2,1)S(1)}, u32[]{:S(2)}, u32[]{:S(2)}) collective-permute-start(bf16[512,512]{1,0:T(8,128)(2,1)S(1)} %convert_element_type.147), channel_id=1, source_target_pairs={{0,1},{2,3},{4,5},{6,7},{8,9},{10,11},{12,13},{14,15},{16,17},{18,... | collective-permute-start | bytes 1572872 | tf_op jit(solution)/shard_map/ppermute | solution.py:1526
  569.9 20.8 %collective-permute-start.52 = (bf16[416,768]{1,0:T(8,128)(2,1)}, bf16[416,768]{1,0:T(8,128)(2,1)S(1)}, u32[]{:S(2)}, u32[]{:S(2)}) collective-permute-start(bf16[416,768]{1,0:T(8,128)(2,1)} %get-tuple-element.268), channel_id=1, source_target_pairs={{0,16},{4,20},{8,24},{12,28},{16,0},{20,4},{24,8},{28,12},{1,17},{... | collective-permute-start | bytes 1916936 | tf_op jit(solution)/shard_map/ppermute | solution.py:1236
  570.6 20.1 %collective-permute-start.53 = (bf16[416,768]{1,0:T(8,128)(2,1)}, bf16[416,768]{1,0:T(8,128)(2,1)S(1)}, u32[]{:S(2)}, u32[]{:S(2)}) collective-permute-start(bf16[416,768]{1,0:T(8,128)(2,1)} %get-tuple-element.288), channel_id=1, source_target_pairs={{0,8},{4,12},{8,0},{12,4},{16,24},{20,28},{24,16},{28,20},{1,9},{5... | collective-permute-start | bytes 1916936 | tf_op jit(solution)/shard_map/ppermute | solution.py:1236
  604.6 17.7 %collective-permute-start.50 = (bf16[256,1536]{1,0:T(8,128)(2,1)}, bf16[256,1536]{1,0:T(8,128)(2,1)}, u32[]{:S(2)}, u32[]{:S(2)}) collective-permute-start(bf16[256,1536]{1,0:T(8,128)(2,1)} %get-tuple-element.286), channel_id=1, source_target_pairs={{0,16},{4,20},{8,24},{12,28},{16,0},{20,4},{24,8},{28,12},{1,17},{... | collective-permute-start | bytes 2359304 | tf_op jit(solution)/shard_map/ppermute | solution.py:1236
  605.9 18.7 %collective-permute-start.51 = (bf16[256,1536]{1,0:T(8,128)(2,1)}, bf16[256,1536]{1,0:T(8,128)(2,1)}, u32[]{:S(2)}, u32[]{:S(2)}) collective-permute-start(bf16[256,1536]{1,0:T(8,128)(2,1)} %get-tuple-element.287), channel_id=1, source_target_pairs={{0,8},{4,12},{8,0},{12,4},{16,24},{20,28},{24,16},{28,20},{1,9},{5... | collective-permute-start | bytes 2359304 | tf_op jit(solution)/shard_map/ppermute | solution.py:1236
  635.4 22.7 %collective-permute-start.55 = (bf16[208,896]{1,0:T(8,128)(2,1)S(1)}, bf16[208,896]{1,0:T(8,128)(2,1)S(1)}, u32[]{:S(2)}, u32[]{:S(2)}) collective-permute-start(bf16[208,896]{1,0:T(8,128)(2,1)S(1)} %get-tuple-element.313), channel_id=1, source_target_pairs={{0,1},{1,2},{2,3},{4,5},{5,6},{6,7},{8,9},{9,10},{10,11},{12,13},{... | collective-permute-start | bytes 1118216 | tf_op jit(solution)/shard_map/ppermute | solution.py:1227
  638.8 19.2 %collective-permute-start.56 = (bf16[208,896]{1,0:T(8,128)(2,1)S(1)}, bf16[208,896]{1,0:T(8,128)(2,1)S(1)}, u32[]{:S(2)}, u32[]{:S(2)}) collective-permute-start(bf16[208,896]{1,0:T(8,128)(2,1)S(1)} %get-tuple-element.312), channel_id=1, source_target_pairs={{1,0},{2,1},{3,2},{5,4},{6,5},{7,6},{9,8},{10,9},{11,10},{13,12},{... | collective-permute-start | bytes 1118216 | tf_op jit(solution)/shard_map/ppermute | solution.py:1228
  640.1 17.9 %collective-permute-start.57 = (bf16[208,896]{1,0:T(8,128)(2,1)S(1)}, bf16[208,896]{1,0:T(8,128)(2,1)S(1)}, u32[]{:S(2)}, u32[]{:S(2)}) collective-permute-start(bf16[208,896]{1,0:T(8,128)(2,1)S(1)} %get-tuple-element.297), channel_id=1, source_target_pairs={{0,3},{3,0},{4,7},{7,4},{8,11},{11,8},{12,15},{15,12},{16,19},{19,... | collective-permute-start | bytes 1118216 | tf_op jit(solution)/shard_map/ppermute | solution.py:1191
  (74 other events, 557.4 us)
Sparse Core Ops, SparseCore 0:
  201.7 127.1 all-gather.2
  331.2 121.7 reduce-scatter.2
  459.2 130.0 reduce-scatter.4

commit v19 on v18

--- a/solution.py
+++ b/solution.py
@@ -1223,12 +1223,13 @@
         jnp.where(place == 0, third, fourth).astype(WIDE) + jnp.where(place == 1, relayed, 0.0)
     ).astype(LOW)
     downward_load = (third.astype(WIDE) + jnp.where(place == 2, relayed, 0.0)).astype(LOW)
-    return (
+    arrived = (
         lax.ppermute(upward_load, "cols", UP),
         lax.ppermute(downward_load, "cols", DOWN),
         send_far(after(fourth, upward_load, downward_load)),
         relay,
     )
+    return arrived, upward_load
 
 
 def flip(block, bit):
@@ -1556,9 +1557,6 @@
 
     if fast:
         pair_parts = chips_second(*pair_first[2:], *after(pair_chips, tokens_grad))
-        near_x, near_y = out_first[2:]
-        mixture = chips_second(near_x, near_y, *after(out_flips, pair_parts[2], pair_parts[5]))
-    layer_output = (residual + sum_parts(mixture)).astype(LOW)
     gate_grad, upward_grad, down_grad = expert_sums(reduced)
     gate_grad, upward_grad = jnp.swapaxes(gate_grad, 1, 2), jnp.swapaxes(upward_grad, 1, 2)
     if fast:
@@ -1584,7 +1582,10 @@
         slots = jnp.concatenate([slots + gain_sums, pairs_sum], axis=2).astype(LOW)
         slots = after(slots, reduced[1])
 
-        arrived = send_slots(slots)
+        arrived, sent_load = send_slots(slots)
+        near_x, near_y = out_first[2:]
+        mixture = chips_second(near_x, near_y, *after(out_flips, sent_load))
+        layer_output = (residual + sum_parts(mixture)).astype(LOW)
         earlier = (gate_grad, upward_grad, down_grad, layer_output)
         query_sum, key_sum, value_sum, out_sum, extra_sum = last_sums(
             info, slots[0], after(arrived, *earlier), depth, key_part
@@ -1594,6 +1595,7 @@
         experts_gain_sum = extra_sum[router_part, :gain_part]
         attention_gain_sum = extra_sum[router_part + 1, :gain_part]
     else:
+        layer_output = (residual + sum_parts(mixture)).astype(LOW)
         full_grads = [
             tn(normed, grad_query),
             *jnp.moveaxis(tn(normed, grad_pair).reshape(D, QUARTERS, 2, -1), 2, 0),

time: 682 us -> 672 us (0.985)
  waiting for transfers between devices: 184 us -> 176 us
    ppermute x44, waiting for transfers between devices: 145 us -> 131 us  [flip(): return lax.ppermute(block, 'rows', [(i, i ^ bit) for i in range(count)])]
    unnamed x133 -> x137, local copies, waits for them, and re-layouts: 24.6 us -> 25.5 us
  transfers between devices with their start and end apart: 61 -> 61, of which waited for: 30 -> 29; matrix products, arithmetic and copies ran while one was open for 6% -> 6% of each run, Pallas kernels for 46% -> 46%
where the time goes in v19:
time: 672 us; the launch traced here: 661 us
  Pallas kernels  312 us (46%)
  waiting for transfers between devices  176 us (26%)
  starting transfers between devices  87.7 us (13%)
  local copies, waits for them, and re-layouts  47.2 us (7%)
  other arithmetic  23.4 us (3%)
  between operations  15 us (2%)
    ppermute x44, waiting for transfers between devices, flip(): return lax.ppermute(block, 'rows', [(i, i ^ bit) for i in range(count)])  131 us
    pallas_call x2, Pallas kernels, expert(): pl.pallas_call(functools.partial(expert_kernel, slots), grid=(height // E...  61 us
    ppermute x44, starting transfers between devices, flip(): return lax.ppermute(block, 'rows', [(i, i ^ bit) for i in range(count)])  32.8 us
    pallas_call x4, Pallas kernels, combine(): pl.pallas_call(functools.partial(combine_kernel, local, first, step), out...  30.9 us
    pallas_call x2, Pallas kernels, expert_grads(): pl.pallas_call(expert_grads_kernel, grid=(D // 256,), out_shape=jax.Shape...  29.3 us
    pallas_call x8, Pallas kernels, dispatch(): pl.pallas_call(functools.partial(dispatch_kernel, local), grid=(D // wide...  29 us
    ppermute x4, starting transfers between devices, send_near(): return (lax.ppermute(block, 'cols', DOWN), lax.ppermute(block, 'cols', UP))  27.7 us
    unnamed x137, local copies, waits for them, and re-layouts  25.5 us
  transfers between devices with their start and end apart: 61, of which 29 were waited for; matrix products, arithmetic and copies ran while one was open for 6% of the time, Pallas kernels for 46%

profile of v19, /device:TPU:0, one launch (start us, length us, event | category | flops | bytes accessed | tf_op | source)
XLA Modules:
  0.0 661.0 jit_solution(8487013950126577821)
XLA Ops:
  14.1 6.3 collective-permute-start.1
  33.0 18.7 %collective-permute-start.9 = (bf16[576,1536]{1,0:T(8,128)(2,1)}, bf16[576,1536]{1,0:T(8,128)(2,1)}, u32[]{:S(2)}, u32[]{:S(2)}) collective-permute-start(bf16[576,1536]{1,0:T(8,128)(2,1)} %pad_maximum_fusion.2.rest_0_), channel_id=1, source_target_pairs={{0,1},{1,2},{2,3},{4,5},{5,6},{6,7},{8,9},{9,10},{10,11},{12,13},{... | collective-permute-start | bytes 5308424 | tf_op jit(solution)/shard_map/ppermute | solution.py:1187
  57.4 31.8 %collective-permute-done.6.rest_2_.rest_8_ = bf16[4,208,896]{2,1,0:T(8,128)(2,1)S(1)} collective-permute-done((bf16[4,208,896]{2,1,0:T(8,128)(2,1)S(1)}, bf16[4,208,896]{2,1,0:T(8,128)(2,1)S(1)}, u32[]{:S(2)}, u32[]{:S(2)}) %collective-permute-start.6) | collective-permute-done | bytes 1490976 | tf_op jit(solution)/shard_map/ppermute | solution.py:1237
  93.1 6.8 %collective-permute-start.2 = (bf16[576,1536]{1,0:T(8,128)(2,1)}, bf16[576,1536]{1,0:T(8,128)(2,1)}, u32[]{:S(2)}, u32[]{:S(2)}) collective-permute-start(bf16[576,1536]{1,0:T(8,128)(2,1)} %pad_maximum_fusion.2.rest_0_), channel_id=1, source_target_pairs={{0,3},{3,0},{4,7},{7,4},{8,11},{11,8},{12,15},{15,12},{16,19},{19,... | collective-permute-start | bytes 5308424 | tf_op jit(solution)/shard_map/ppermute | solution.py:1191
  99.9 10.1 %collective-permute-done.11.rest_4_.rest_10_ = bf16[2,208,896]{2,1,0:T(8,128)(2,1)S(1)} collective-permute-done((bf16[2,208,896]{2,1,0:T(8,128)(2,1)S(1)}, bf16[2,208,896]{2,1,0:T(8,128)(2,1)S(1)}, u32[]{:S(2)}, u32[]{:S(2)}) %collective-permute-start.11) | collective-permute-done | bytes 745504 | tf_op jit(solution)/shard_map/ppermute | solution.py:1237
  112.5 4.4 collective-permute-done.12.rest_7_.rest_13_
  118.1 5.6 route_tables.1
  129.1 9.8 %collective-permute-done.2.rest_4_ = bf16[576,1536]{1,0:T(8,128)(2,1)} collective-permute-done((bf16[576,1536]{1,0:T(8,128)(2,1)}, bf16[576,1536]{1,0:T(8,128)(2,1)}, u32[]{:S(2)}, u32[]{:S(2)}) %collective-permute-start.2) | collective-permute-done | bytes 1769504 | tf_op jit(solution)/shard_map/ppermute | solution.py:1191
  138.8 5.0 norm_key_value.1
  145.2 8.2 %query_projection.1.queries = bf16[512,1536]{1,0:T(8,128)(2,1)} custom-call(s32[16]{0:T(128)} %concatenate.49.info, bf16[512,1536]{1,0:T(8,128)(2,1)} %get-tuple-element.169.normed.rest_0_, f32[512,128]{1,0:T(8,128)} %get-tuple-element.332.cosine, f32[512,128]{1,0:T(8,128)} %get-tuple-element.333.sine, bf16[4,208,896]{2,1,0:T(8,128)(2,1)} %copy-done.1, ...), custom_call_target="tpu_custom_call" | custom-call | flops 1 | bytes 1 | tf_op jit(solution)/shard_map/query_projection/pallas_call | solution.py:195
  153.4 5.9 collective-permute-done.16.partner
  171.3 11.0 %tree_attention.1.heads.rest_1_ = bf16[512,1536]{1,0:T(8,128)(2,1)} custom-call(s32[16]{0:T(128)} %concatenate.49.info, bf16[512,1536]{1,0:T(8,128)(2,1)} %query_projection.1.queries, bf16[512,512]{1,0:T(8,128)(2,1)} %get-tuple-element.170.own, bf16[512,512]{1,0:T(8,128)(2,1)} %collective-permute-done.16.partner), custom_call_target="tpu_custom_call" | custom-call | flops 1 | bytes 1 | tf_op jit(solution)/shard_map/tree_attention/pallas_call | solution.py:277
  190.8 9.9 %out_projection.1 = (f32[512,1536]{1,0:T(8,128)}, bf16[512,1536]{1,0:T(8,128)(2,1)}) custom-call(s32[16]{0:T(128)} %concatenate.49.info, bf16[512,1536]{1,0:T(8,128)(2,1)} %tree_attention.1.heads.rest_1_, bf16[512,1536]{1,0:T(8,128)(2,1)} %tokens.4, f32[1,1536]{1,0:T(1,128)} %reshape.299.gain, bf16[4,208,896]{2,1,0:T(8,128)(2,1)} %copy-done.1, ...), custom_call_target="tpu_custom_call" | custom-call | flops 1 | bytes 1 | tf_op jit(solution)/shard_map/out_projection/pallas_call | solution.py:389
  208.4 3.9 dispatch.8
  212.3 9.4 %pick_rows.1 = (bf16[8,160,1536]{2,1,0:T(8,128)(2,1)}, bf16[8,160,1536]{2,1,0:T(8,128)(2,1)}) custom-call(bf16[8,320,512]{2,1,0:T(8,128)(2,1)} %get-tuple-element.165.chosen, bf16[512,1536]{1,0:T(8,128)(2,1)} %cotangent.1, bf16[512,1536]{1,0:T(8,128)(2,1)} %collective-permute-done.15.rest_1_, bf16[512,1536]{1,0:T(8,128)(2,1)} %copy-done.18, ...), custom_call_target="tpu_custom_call" | custom-call | flops 1 | bytes 1 | tf_op jit(solution)/shard_map/pick_rows/pallas_call | solution.py:480
  221.7 3.6 dispatch.9
  225.3 13.8 %collective-permute-done.23.rows = bf16[512,1536]{1,0:T(8,128)(2,1)} collective-permute-done((bf16[512,1536]{1,0:T(8,128)(2,1)S(1)}, bf16[512,1536]{1,0:T(8,128)(2,1)}, u32[]{:S(2)}, u32[]{:S(2)}) %collective-permute-start.23) | collective-permute-done | bytes 1572896 | tf_op jit(solution)/shard_map/ppermute | solution.py:1237
  245.3 3.6 dispatch.10
  248.9 3.6 dispatch.11
  253.6 3.6 dispatch.12
  258.3 3.6 dispatch.13
  265.2 3.6 dispatch.14
  273.5 30.7 %expert.2 = (bf16[1280,1536]{1,0:T(8,128)(2,1)}, bf16[1280,1536]{1,0:T(8,128)(2,1)}, bf16[1280,1536]{1,0:T(8,128)(2,1)}, bf16[4,576,1280]{2,1,0:T(8,128)(2,1)}, f32[1280,1]{1,0:T(8,128)}) custom-call(s32[16]{0:T(128)} %concatenate.49.info, bf16[1280,1536]{1,0:T(8,128)(2,1)} %bitcast.110, bf16[1280,1536]{1,0:T(8,128)(2,1)} %bitcast.129, f32[1280,1]{1,0:T(8,128)} %bitcast.114, ...), custom_call_target="tpu_custom_call" | custom-call | flops 1 | bytes 1 | tf_op jit(solution)/shard_map/expert/pallas_call | solution.py:670
  304.3 14.6 %expert_gradients.2 = bf16[4,576,1536]{2,1,0:T(8,128)(2,1)} custom-call(bf16[4,576,1280]{2,1,0:T(8,128)(2,1)} %get-tuple-element.219.acts, bf16[1280,1536]{1,0:T(8,128)(2,1)} %bitcast.111, bf16[1280,1536]{1,0:T(8,128)(2,1)} %get-tuple-element.220.grads), custom_call_target="tpu_custom_call" | custom-call | flops 1 | bytes 1 | tf_op jit(solution)/shard_map/expert_gradients/pallas_call | solution.py:699
  319.0 9.9 %all-gather.3.cloned.1.call-done = bf16[2304,1536]{1,0:T(8,128)(2,1)} async-done(((bf16[576,1536]{1,0:T(8,128)(2,1)}), bf16[2304,1536]{1,0:T(8,128)(2,1)}) %all-gather.3.cloned.1.call-update) | async-done | bytes 7077904 | tf_op jit(solution)/shard_map/all_gather | solution.py:1420
  328.9 30.2 %expert.3 = (bf16[1280,1536]{1,0:T(8,128)(2,1)}, bf16[1280,1536]{1,0:T(8,128)(2,1)}, bf16[1280,1536]{1,0:T(8,128)(2,1)}, bf16[4,576,1280]{2,1,0:T(8,128)(2,1)}, f32[1280,1]{1,0:T(8,128)}) custom-call(s32[16]{0:T(128)} %concatenate.49.info, bf16[1280,1536]{1,0:T(8,128)(2,1)} %bitcast.112, bf16[1280,1536]{1,0:T(8,128)(2,1)} %bitcast.130, f32[1280,1]{1,0:T(8,128)} %bitcast.115, ...), custom_call_target="tpu_custom_call" | custom-call | flops 1 | bytes 1 | tf_op jit(solution)/shard_map/expert/pallas_call | solution.py:670
  359.1 8.0 %combine.7 = bf16[4,544,1536]{2,1,0:T(8,128)(2,1)} custom-call(s32[16]{0:T(128)} %concatenate.49.info, bf16[8,320,512]{2,1,0:T(8,128)(2,1)} %get-tuple-element.165.chosen, bf16[8,160,1536]{2,1,0:T(8,128)(2,1)} %bitcast.118, bf16[8,160,1536]{2,1,0:T(8,128)(2,1)} %bitcast.122, f32[8,160,1]{2,1,0:T(8,128)} %bitcast.133, f32[8,160,1]{2,1,0:T(8,128)} %bitcast.135), custom_call_target="tpu_custom_call" | custom-call | flops 1 | bytes 1 | tf_op jit(solution)/shard_map/combine/pallas_call | solution.py:762
  367.3 7.3 %combine.5 = bf16[4,512,1536]{2,1,0:T(8,128)(2,1)} custom-call(s32[16]{0:T(128)} %concatenate.49.info, bf16[8,320,512]{2,1,0:T(8,128)(2,1)} %get-tuple-element.165.chosen, bf16[8,160,1536]{2,1,0:T(8,128)(2,1)} %bitcast.116, bf16[8,160,1536]{2,1,0:T(8,128)(2,1)} %bitcast.120), custom_call_target="tpu_custom_call" | custom-call | flops 1 | bytes 1 | tf_op jit(solution)/shard_map/combine/pallas_call | solution.py:762
  375.1 8.1 %combine.6.keep = bf16[4,544,1536]{2,1,0:T(8,128)(2,1)} custom-call(s32[16]{0:T(128)} %concatenate.49.info, bf16[8,320,512]{2,1,0:T(8,128)(2,1)} %get-tuple-element.165.chosen, bf16[8,160,1536]{2,1,0:T(8,128)(2,1)} %bitcast.119, bf16[8,160,1536]{2,1,0:T(8,128)(2,1)} %bitcast.123, f32[8,160,1]{2,1,0:T(8,128)} %bitcast.134, f32[8,160,1]{2,1,0:T(8,128)} %bitcast.136), custom_call_target="tpu_custom_call" | custom-call | flops 1 | bytes 1 | tf_op jit(solution)/shard_map/combine/pallas_call | solution.py:762
  385.9 7.8 %chip_sums.5 = (bf16[2,272,1536]{2,1,0:T(8,128)(2,1)}, bf16[2,272,1536]{2,1,0:T(8,128)(2,1)}, bf16[2,272,1536]{2,1,0:T(8,128)(2,1)}, bf16[2,272,1536]{2,1,0:T(8,128)(2,1)}) custom-call(bf16[4,544,1536]{2,1,0:T(8,128)(2,1)} %combine.6.keep, bf16[4,544,1536]{2,1,0:T(8,128)(2,1)} %copy-done.10), custom_call_target="tpu_custom_call" | custom-call | flops 1 | bytes 1 | tf_op jit(solution)/shard_map/chip_sums/pallas_call | solution.py:811
  396.7 7.5 %combine.4.keep = bf16[4,512,1536]{2,1,0:T(8,128)(2,1)} custom-call(s32[16]{0:T(128)} %concatenate.49.info, bf16[8,320,512]{2,1,0:T(8,128)(2,1)} %get-tuple-element.165.chosen, bf16[8,160,1536]{2,1,0:T(8,128)(2,1)} %bitcast.117, bf16[8,160,1536]{2,1,0:T(8,128)(2,1)} %bitcast.121), custom_call_target="tpu_custom_call" | custom-call | flops 1 | bytes 1 | tf_op jit(solution)/shard_map/combine/pallas_call | solution.py:762
  404.3 14.7 %expert_gradients.3 = bf16[4,576,1536]{2,1,0:T(8,128)(2,1)} custom-call(bf16[4,576,1280]{2,1,0:T(8,128)(2,1)} %get-tuple-element.236.acts, bf16[1280,1536]{1,0:T(8,128)(2,1)} %bitcast.113, bf16[1280,1536]{1,0:T(8,128)(2,1)} %get-tuple-element.237.grads), custom_call_target="tpu_custom_call" | custom-call | flops 1 | bytes 1 | tf_op jit(solution)/shard_map/expert_gradients/pallas_call | solution.py:699
  419.0 13.5 %collective-permute-done.35.got_x.rest_1_ = bf16[2,272,1536]{2,1,0:T(8,128)(2,1)S(1)} collective-permute-done((bf16[2,272,1536]{2,1,0:T(8,128)(2,1)}, bf16[2,272,1536]{2,1,0:T(8,128)(2,1)S(1)}, u32[]{:S(2)}, u32[]{:S(2)}) %collective-permute-start.35) | collective-permute-done | bytes 1671200 | tf_op jit(solution)/shard_map/ppermute | solution.py:1237
  440.4 7.5 %chip_sums.4 = (bf16[2,256,1536]{2,1,0:T(8,128)(2,1)}, bf16[2,256,1536]{2,1,0:T(8,128)(2,1)}, bf16[2,256,1536]{2,1,0:T(8,128)(2,1)}, bf16[2,256,1536]{2,1,0:T(8,128)(2,1)}) custom-call(bf16[4,512,1536]{2,1,0:T(8,128)(2,1)} %combine.4.keep, bf16[4,512,1536]{2,1,0:T(8,128)(2,1)} %collective-permute-done.33.got), custom_call_target="tpu_custom_call" | custom-call | flops 1 | bytes 1 | tf_op jit(solution)/shard_map/chip_sums/pallas_call | solution.py:811
  447.9 10.0 %collective-permute-done.37.rest_2_ = bf16[272,1536]{1,0:T(8,128)(2,1)} collective-permute-done((bf16[272,1536]{1,0:T(8,128)(2,1)}, bf16[272,1536]{1,0:T(8,128)(2,1)}, u32[]{:S(2)}, u32[]{:S(2)}) %collective-permute-start.37) | collective-permute-done | bytes 835616 | tf_op jit(solution)/shard_map/ppermute | solution.py:1237
  461.0 13.3 %experts_norm_back.1 = (f32[512,1536]{1,0:T(8,128)}, bf16[512,1536]{1,0:T(8,128)(2,1)}, bf16[512,1536]{1,0:T(8,128)(2,1)}, f32[1,1536]{1,0:T(1,128)}, f32[16,1536]{1,0:T(8,128)}) custom-call(s32[16]{0:T(128)} %concatenate.49.info, f32[512,1536]{1,0:T(8,128)} %get-tuple-element.174.residual, bf16[512,1536]{1,0:T(8,128)(2,1)} %get-tuple-element.175.rows.normed, ...), custom_call_target="tpu_custom_call" | custom-call | flops 1 | bytes 1 | tf_op jit(solution)/shard_map/experts_norm_back/pallas_call | solution.py:922
  474.3 15.5 %tree_attention_back.1 = (bf16[512,1536]{1,0:T(8,128)(2,1)}, f32[512,512]{1,0:T(8,128)}, f32[512,512]{1,0:T(8,128)}) custom-call(s32[16]{0:T(128)} %concatenate.49.info, bf16[512,1536]{1,0:T(8,128)(2,1)} %query_projection.1.queries, bf16[512,512]{1,0:T(8,128)(2,1)} %get-tuple-element.170.own, bf16[512,512]{1,0:T(8,128)(2,1)} %collective-permute-done.16.partner, ...), custom_call_target="tpu_custom_call" | custom-call | flops 1 | bytes 1 | tf_op jit(solution)/shard_map/tree_attention_back/pallas_call | solution.py:338
  494.8 13.5 %weight_gradients.2 = (bf16[4,4,208,768]{3,2,1,0:T(8,128)(2,1)}, bf16[4,4,208,768]{3,2,1,0:T(8,128)(2,1)}) custom-call(s32[16]{0:T(128)} %concatenate.49.info, bf16[512,1536]{1,0:T(8,128)(2,1)} %get-tuple-element.169.normed.rest_0_, bf16[512,1536]{1,0:T(8,128)(2,1)} %tree_attention.1.heads.rest_1_, bf16[512,1536]{1,0:T(8,128)(2,1)} %get-tuple-element.262.rest_2_.grad_query, ...), custom_call_target="tpu_custom_call" | custom-call | flops 1 | bytes 1 | tf_op jit(solution)/shard_map/weight_gradients/pallas_call | solution.py:1074
  508.3 8.7 %collective-permute-done.41 = bf16[4,4,208,768]{3,2,1,0:T(8,128)(2,1)S(1)} collective-permute-done((bf16[4,4,208,768]{3,2,1,0:T(8,128)(2,1)}, bf16[4,4,208,768]{3,2,1,0:T(8,128)(2,1)S(1)}, u32[]{:S(2)}, u32[]{:S(2)}) %collective-permute-start.41) | collective-permute-done | bytes 5111840 | tf_op jit(solution)/shard_map/ppermute | solution.py:1237
  519.2 6.6 chip_sums.6
  528.4 8.0 %normed_gradient.1.query_part = f32[512,1536]{1,0:T(8,128)} custom-call(s32[16]{0:T(128)} %concatenate.49.info, bf16[512,1536]{1,0:T(8,128)(2,1)} %get-tuple-element.262.rest_2_.grad_query, bf16[4,208,896]{2,1,0:T(8,128)(2,1)} %copy-done.1, bf16[4,208,896]{2,1,0:T(8,128)(2,1)} %copy-done.5, bf16[4,208,896]{2,1,0:T(8,128)(2,1)} %copy-done.3, ...), custom_call_target="tpu_custom_call" | custom-call | flops 1 | bytes 1 | tf_op jit(solution)/shard_map/normed_gradient/pallas_call | solution.py:999
  536.4 19.8 %collective-permute-done.42.got_x = bf16[2,416,768]{2,1,0:T(8,128)(2,1)S(1)} collective-permute-done((bf16[2,416,768]{2,1,0:T(8,128)(2,1)}, bf16[2,416,768]{2,1,0:T(8,128)(2,1)S(1)}, u32[]{:S(2)}, u32[]{:S(2)}) %collective-permute-start.42) | collective-permute-done | bytes 1277984 | tf_op jit(solution)/shard_map/ppermute | solution.py:1237
  564.4 5.7 weight_gradients.3
  582.7 8.2 %token_gradient.1 = (bf16[512,1536]{1,0:T(8,128)(2,1)}, f32[1,1536]{1,0:T(1,128)}) custom-call(s32[16]{0:T(128)} %concatenate.49.info, f32[512,1536]{1,0:T(8,128)} %normed_gradient.1.query_part, bf16[512,512]{1,0:T(8,128)(2,1)} %join_key_value_gradients.1.rest_1_.grad_pair, bf16[512,1536]{1,0:T(8,128)(2,1)} %tokens.4, ...), custom_call_target="tpu_custom_call" | custom-call | flops 1 | bytes 1 | tf_op jit(solution)/shard_map/token_gradient/pallas_call | solution.py:1026
  603.7 11.1 %collective-permute-done.52.rest_3_ = bf16[208,896]{1,0:T(8,128)(2,1)S(1)} collective-permute-done((bf16[208,896]{1,0:T(8,128)(2,1)S(1)}, bf16[208,896]{1,0:T(8,128)(2,1)S(1)}, u32[]{:S(2)}, u32[]{:S(2)}) %collective-permute-start.52) | collective-permute-done | bytes 372768 | tf_op jit(solution)/shard_map/ppermute | solution.py:1220
  620.6 5.1 expert_sums.1
  630.2 7.6 %collective-permute-start.57 = (bf16[208,896]{1,0:T(8,128)(2,1)S(1)}, bf16[208,896]{1,0:T(8,128)(2,1)S(1)}, u32[]{:S(2)}, u32[]{:S(2)}) collective-permute-start(bf16[208,896]{1,0:T(8,128)(2,1)S(1)} %get-tuple-element.297), channel_id=1, source_target_pairs={{0,3},{3,0},{4,7},{7,4},{8,11},{11,8},{12,15},{15,12},{16,19},{19,... | collective-permute-start | bytes 1118216 | tf_op jit(solution)/shard_map/ppermute | solution.py:1191
  641.6 6.6 %collective-permute-done.57.rest_2_ = bf16[208,896]{1,0:T(8,128)(2,1)S(1)} collective-permute-done((bf16[208,896]{1,0:T(8,128)(2,1)S(1)}, bf16[208,896]{1,0:T(8,128)(2,1)S(1)}, u32[]{:S(2)}, u32[]{:S(2)}) %collective-permute-start.57) | collective-permute-done | bytes 372768 | tf_op jit(solution)/shard_map/ppermute | solution.py:1191
  (335 shorter events, 164.4 us)
Async XLA Ops:
  7.2 321.7 %all-gather.3.cloned.1.call-start = ((), (), s32[]{:S(2)}) async-start(), calls=%async_computation.4 | async-start | bytes 8847360 | tf_op jit(solution)/shard_map/all_gather | solution.py:1420
  12.7 19.0 %collective-permute-start = (bf16[208,896]{1,0:T(8,128)(2,1)S(1)}, bf16[208,896]{1,0:T(8,128)(2,1)S(1)}, u32[]{:S(2)}, u32[]{:S(2)}) collective-permute-start(bf16[208,896]{1,0:T(8,128)(2,1)S(1)} %concatenate.53), channel_id=1, source_target_pairs={{1,0},{2,1},{3,2},{5,4},{6,5},{7,6},{9,8},{10,9},{11,10},{13,12},{... | collective-permute-start | bytes 1118216 | tf_op jit(solution)/shard_map/ppermute | solution.py:1187
  14.1 17.6 %collective-permute-start.1 = (bf16[208,896]{1,0:T(8,128)(2,1)S(1)}, bf16[208,896]{1,0:T(8,128)(2,1)}, u32[]{:S(2)}, u32[]{:S(2)}) collective-permute-start(bf16[208,896]{1,0:T(8,128)(2,1)S(1)} %concatenate.53), channel_id=1, source_target_pairs={{0,1},{1,2},{2,3},{4,5},{5,6},{6,7},{8,9},{9,10},{10,11},{12,13},{... | collective-permute-start | bytes 1118216 | tf_op jit(solution)/shard_map/ppermute | solution.py:1187
  20.4 31.3 %collective-permute-start.4 = (bf16[208,896]{1,0:T(8,128)(2,1)S(1)}, bf16[208,896]{1,0:T(8,128)(2,1)}, u32[]{:S(2)}, u32[]{:S(2)}) collective-permute-start(bf16[208,896]{1,0:T(8,128)(2,1)S(1)} %concatenate.53), channel_id=1, source_target_pairs={{0,3},{3,0},{4,7},{7,4},{8,11},{11,8},{12,15},{15,12},{16,19},{19,... | collective-permute-start | bytes 1118216 | tf_op jit(solution)/shard_map/ppermute | solution.py:1191
  23.4 29.4 %collective-permute-start.3 = (bf16[208,896]{1,0:T(8,128)(2,1)S(1)}, bf16[208,896]{1,0:T(8,128)(2,1)}, u32[]{:S(2)}, u32[]{:S(2)}) collective-permute-start(bf16[208,896]{1,0:T(8,128)(2,1)S(1)} %concatenate.53), channel_id=1, source_target_pairs={{0,2},{1,3},{2,0},{3,1},{4,6},{5,7},{6,4},{7,5},{8,10},{9,11},{10,... | collective-permute-start | bytes 1118216 | tf_op jit(solution)/shard_map/ppermute | solution.py:1195
  31.7 58.7 %collective-permute-start.8 = (bf16[576,1536]{1,0:T(8,128)(2,1)}, bf16[576,1536]{1,0:T(8,128)(2,1)}, u32[]{:S(2)}, u32[]{:S(2)}) collective-permute-start(bf16[576,1536]{1,0:T(8,128)(2,1)} %pad_maximum_fusion.2.rest_0_), channel_id=1, source_target_pairs={{1,0},{2,1},{3,2},{5,4},{6,5},{7,6},{9,8},{10,9},{11,10},{13,12},{... | collective-permute-start | bytes 5308424 | tf_op jit(solution)/shard_map/ppermute | solution.py:1187
  33.0 57.4 %collective-permute-start.9 = (bf16[576,1536]{1,0:T(8,128)(2,1)}, bf16[576,1536]{1,0:T(8,128)(2,1)}, u32[]{:S(2)}, u32[]{:S(2)}) collective-permute-start(bf16[576,1536]{1,0:T(8,128)(2,1)} %pad_maximum_fusion.2.rest_0_), channel_id=1, source_target_pairs={{0,1},{1,2},{2,3},{4,5},{5,6},{6,7},{8,9},{9,10},{10,11},{12,13},{... | collective-permute-start | bytes 5308424 | tf_op jit(solution)/shard_map/ppermute | solution.py:1187
  54.1 35.1 %collective-permute-start.6 = (bf16[4,208,896]{2,1,0:T(8,128)(2,1)S(1)}, bf16[4,208,896]{2,1,0:T(8,128)(2,1)S(1)}, u32[]{:S(2)}, u32[]{:S(2)}) collective-permute-start(bf16[4,208,896]{2,1,0:T(8,128)(2,1)S(1)} %pad_maximum_fusion.4.rest_0_.rest_6_), channel_id=1, source_target_pairs={{0,8},{4,12},{8,0},{12,4},{16,24},{20,28},{24,16},{28,20},{1,9},{5... | collective-permute-start | bytes 4472840 | tf_op jit(solution)/shard_map/ppermute | solution.py:1237
  55.7 34.7 %collective-permute-start.7 = (bf16[4,208,896]{2,1,0:T(8,128)(2,1)S(1)}, bf16[4,208,896]{2,1,0:T(8,128)(2,1)S(1)}, u32[]{:S(2)}, u32[]{:S(2)}) collective-permute-start(bf16[4,208,896]{2,1,0:T(8,128)(2,1)S(1)} %pad_maximum_fusion.4.rest_0_.rest_6_), channel_id=1, source_target_pairs={{0,16},{4,20},{8,24},{12,28},{16,0},{20,4},{24,8},{28,12},{1,17},{... | collective-permute-start | bytes 4472840 | tf_op jit(solution)/shard_map/ppermute | solution.py:1237
  90.7 21.5 %collective-permute-start.10 = (bf16[8,208,896]{2,1,0:T(8,128)(2,1)S(1)}, bf16[8,208,896]{2,1,0:T(8,128)(2,1)S(1)}, u32[]{:S(2)}, u32[]{:S(2)}) collective-permute-start(bf16[8,208,896]{2,1,0:T(8,128)(2,1)S(1)} %pad_maximum_fusion), channel_id=1, source_target_pairs={{0,4},{4,0},{8,12},{12,8},{16,20},{20,16},{24,28},{28,24},{1,5},{5... | collective-permute-start | bytes 8945672 | tf_op jit(solution)/shard_map/ppermute | solution.py:1237
  90.9 19.1 %collective-permute-start.11 = (bf16[2,208,896]{2,1,0:T(8,128)(2,1)S(1)}, bf16[2,208,896]{2,1,0:T(8,128)(2,1)S(1)}, u32[]{:S(2)}, u32[]{:S(2)}) collective-permute-start(bf16[2,208,896]{2,1,0:T(8,128)(2,1)S(1)} %slice.144), channel_id=1, source_target_pairs={{0,16},{4,20},{8,24},{12,28},{16,0},{20,4},{24,8},{28,12},{1,17},{... | collective-permute-start | bytes 2236424 | tf_op jit(solution)/shard_map/ppermute | solution.py:1237
  92.5 18.9 %collective-permute-start.13 = (bf16[2,208,896]{2,1,0:T(8,128)(2,1)S(1)}, bf16[2,208,896]{2,1,0:T(8,128)(2,1)}, u32[]{:S(2)}, u32[]{:S(2)}) collective-permute-start(bf16[2,208,896]{2,1,0:T(8,128)(2,1)S(1)} %slice.147), channel_id=1, source_target_pairs={{0,8},{4,12},{8,0},{12,4},{16,24},{20,28},{24,16},{28,20},{1,9},{5... | collective-permute-start | bytes 2236424 | tf_op jit(solution)/shard_map/ppermute | solution.py:1237
  93.1 45.8 %collective-permute-start.2 = (bf16[576,1536]{1,0:T(8,128)(2,1)}, bf16[576,1536]{1,0:T(8,128)(2,1)}, u32[]{:S(2)}, u32[]{:S(2)}) collective-permute-start(bf16[576,1536]{1,0:T(8,128)(2,1)} %pad_maximum_fusion.2.rest_0_), channel_id=1, source_target_pairs={{0,3},{3,0},{4,7},{7,4},{8,11},{11,8},{12,15},{15,12},{16,19},{19,... | collective-permute-start | bytes 5308424 | tf_op jit(solution)/shard_map/ppermute | solution.py:1191
  111.4 33.8 %collective-permute-start.15 = (bf16[512,1536]{1,0:T(8,128)(2,1)S(1)}, bf16[512,1536]{1,0:T(8,128)(2,1)}, u32[]{:S(2)}, u32[]{:S(2)}) collective-permute-start(bf16[512,1536]{1,0:T(8,128)(2,1)S(1)} %copy-done.13), channel_id=1, source_target_pairs={{0,4},{4,0},{8,12},{12,8},{16,20},{20,16},{24,28},{28,24},{1,5},{5... | collective-permute-start | bytes 4718600 | tf_op jit(solution)/shard_map/ppermute | solution.py:1237
  111.4 52.2 %collective-permute-start.17 = (bf16[512,1536]{1,0:T(8,128)(2,1)S(1)}, bf16[512,1536]{1,0:T(8,128)(2,1)S(1)}, u32[]{:S(2)}, u32[]{:S(2)}) collective-permute-start(bf16[512,1536]{1,0:T(8,128)(2,1)S(1)} %copy-done.13), channel_id=1, source_target_pairs={{0,8},{4,12},{8,0},{12,4},{16,24},{20,28},{24,16},{28,20},{1,9},{5... | collective-permute-start | bytes 4718600 | tf_op jit(solution)/shard_map/ppermute | solution.py:1237
  117.0 46.7 %collective-permute-start.18 = (bf16[512,1536]{1,0:T(8,128)(2,1)S(1)}, bf16[512,1536]{1,0:T(8,128)(2,1)}, u32[]{:S(2)}, u32[]{:S(2)}) collective-permute-start(bf16[512,1536]{1,0:T(8,128)(2,1)S(1)} %copy-done.13), channel_id=1, source_target_pairs={{0,16},{4,20},{8,24},{12,28},{16,0},{20,4},{24,8},{28,12},{1,17},{... | collective-permute-start | bytes 4718600 | tf_op jit(solution)/shard_map/ppermute | solution.py:1237
  143.9 15.4 %collective-permute-start.16 = (bf16[512,512]{1,0:T(8,128)(2,1)}, bf16[512,512]{1,0:T(8,128)(2,1)}, u32[]{:S(2)}, u32[]{:S(2)}) collective-permute-start(bf16[512,512]{1,0:T(8,128)(2,1)} %get-tuple-element.170.own), channel_id=1, source_target_pairs={{1,0},{3,2},{5,4},{7,6},{9,8},{11,10},{13,12},{15,14},{17,16},{19,... | collective-permute-start | bytes 1572872 | tf_op jit(solution)/shard_map/ppermute | solution.py:1392
  162.2 39.3 %collective-permute-start.32 = (bf16[576,1536]{1,0:T(8,128)(2,1)}, bf16[576,1536]{1,0:T(8,128)(2,1)}, u32[]{:S(2)}, u32[]{:S(2)}) collective-permute-start(bf16[576,1536]{1,0:T(8,128)(2,1)} %select_select_fusion), channel_id=1, source_target_pairs={{3,1},{1,0},{0,2},{2,3},{7,5},{5,4},{4,6},{6,7},{11,9},{9,8},{8,10... | collective-permute-start | bytes 5308424 | tf_op jit(solution)/shard_map/ppermute | solution.py:1202
  163.7 24.9 %collective-permute-start.21 = (bf16[512,1536]{1,0:T(8,128)(2,1)S(1)}, bf16[512,1536]{1,0:T(8,128)(2,1)S(1)}, u32[]{:S(2)}, u32[]{:S(2)}) collective-permute-start(bf16[512,1536]{1,0:T(8,128)(2,1)S(1)} %collective-permute-done.17.rest_2_), channel_id=1, source_target_pairs={{0,4},{4,0},{8,12},{12,8},{16,20},{20,16},{24,28},{28,24},{1,5},{5... | collective-permute-start | bytes 4718600 | tf_op jit(solution)/shard_map/ppermute | solution.py:1237
  163.7 25.9 %collective-permute-start.22 = (bf16[512,1536]{1,0:T(8,128)(2,1)}, bf16[512,1536]{1,0:T(8,128)(2,1)}, u32[]{:S(2)}, u32[]{:S(2)}) collective-permute-start(bf16[512,1536]{1,0:T(8,128)(2,1)} %collective-permute-done.18.rest_4_), channel_id=1, source_target_pairs={{0,4},{4,0},{8,12},{12,8},{16,20},{20,16},{24,28},{28,24},{1,5},{5... | collective-permute-start | bytes 4718600 | tf_op jit(solution)/shard_map/ppermute | solution.py:1237
  165.2 19.8 %collective-permute-start.19 = (bf16[256,1536]{1,0:T(8,128)(2,1)}, bf16[256,1536]{1,0:T(8,128)(2,1)}, u32[]{:S(2)}, u32[]{:S(2)}) collective-permute-start(bf16[256,1536]{1,0:T(8,128)(2,1)} %slice.149), channel_id=1, source_target_pairs={{0,16},{4,20},{8,24},{12,28},{16,0},{20,4},{24,8},{28,12},{1,17},{... | collective-permute-start | bytes 2359304 | tf_op jit(solution)/shard_map/ppermute | solution.py:1237
  167.8 19.6 %collective-permute-start.20 = (bf16[256,1536]{1,0:T(8,128)(2,1)}, bf16[256,1536]{1,0:T(8,128)(2,1)}, u32[]{:S(2)}, u32[]{:S(2)}) collective-permute-start(bf16[256,1536]{1,0:T(8,128)(2,1)} %slice.150), channel_id=1, source_target_pairs={{0,8},{4,12},{8,0},{12,4},{16,24},{20,28},{24,16},{28,20},{1,9},{5... | collective-permute-start | bytes 2359304 | tf_op jit(solution)/shard_map/ppermute | solution.py:1237
  201.6 257.5 %reduce-scatter.3.cloned.1.call-start = ((), (), s32[]{:S(2)}) async-start(), calls=%async_computation.2 | async-start | bytes 8847360 | tf_op jit(solution)/shard_map/reduce_scatter | solution.py:1479
  202.2 19.5 %collective-permute-start.25 = (bf16[512,1536]{1,0:T(8,128)(2,1)S(1)}, bf16[512,1536]{1,0:T(8,128)(2,1)}, u32[]{:S(2)}, u32[]{:S(2)}) collective-permute-start(bf16[512,1536]{1,0:T(8,128)(2,1)S(1)} %copy-done.14), channel_id=1, source_target_pairs={{0,4},{4,0},{8,12},{12,8},{16,20},{20,16},{24,28},{28,24},{1,5},{5... | collective-permute-start | bytes 4718600 | tf_op jit(solution)/shard_map/ppermute | solution.py:1237
  202.5 36.6 %collective-permute-start.23 = (bf16[512,1536]{1,0:T(8,128)(2,1)S(1)}, bf16[512,1536]{1,0:T(8,128)(2,1)}, u32[]{:S(2)}, u32[]{:S(2)}) collective-permute-start(bf16[512,1536]{1,0:T(8,128)(2,1)S(1)} %copy-done.14), channel_id=1, source_target_pairs={{0,8},{4,12},{8,0},{12,4},{16,24},{20,28},{24,16},{28,20},{1,9},{5... | collective-permute-start | bytes 4718600 | tf_op jit(solution)/shard_map/ppermute | solution.py:1237
  204.0 36.3 %collective-permute-start.24 = (bf16[512,1536]{1,0:T(8,128)(2,1)S(1)}, bf16[512,1536]{1,0:T(8,128)(2,1)}, u32[]{:S(2)}, u32[]{:S(2)}) collective-permute-start(bf16[512,1536]{1,0:T(8,128)(2,1)S(1)} %copy-done.14), channel_id=1, source_target_pairs={{0,16},{4,20},{8,24},{12,28},{16,0},{20,4},{24,8},{28,12},{1,17},{... | collective-permute-start | bytes 4718600 | tf_op jit(solution)/shard_map/ppermute | solution.py:1237
  240.3 16.9 %collective-permute-start.29 = (bf16[512,1536]{1,0:T(8,128)(2,1)}, bf16[512,1536]{1,0:T(8,128)(2,1)S(1)}, u32[]{:S(2)}, u32[]{:S(2)}) collective-permute-start(bf16[512,1536]{1,0:T(8,128)(2,1)} %collective-permute-done.24.rows), channel_id=1, source_target_pairs={{0,4},{4,0},{8,12},{12,8},{16,20},{20,16},{24,28},{28,24},{1,5},{5... | collective-permute-start | bytes 4718600 | tf_op jit(solution)/shard_map/ppermute | solution.py:1237
  243.2 19.5 %collective-permute-start.27 = (bf16[256,1536]{1,0:T(8,128)(2,1)S(1)}, bf16[256,1536]{1,0:T(8,128)(2,1)S(1)}, u32[]{:S(2)}, u32[]{:S(2)}) collective-permute-start(bf16[256,1536]{1,0:T(8,128)(2,1)S(1)} %slice.153), channel_id=1, source_target_pairs={{0,16},{4,20},{8,24},{12,28},{16,0},{20,4},{24,8},{28,12},{1,17},{... | collective-permute-start | bytes 2359304 | tf_op jit(solution)/shard_map/ppermute | solution.py:1237
  244.8 19.2 %collective-permute-start.28 = (bf16[256,1536]{1,0:T(8,128)(2,1)S(1)}, bf16[256,1536]{1,0:T(8,128)(2,1)S(1)}, u32[]{:S(2)}, u32[]{:S(2)}) collective-permute-start(bf16[256,1536]{1,0:T(8,128)(2,1)S(1)} %slice.154), channel_id=1, source_target_pairs={{0,8},{4,12},{8,0},{12,4},{16,24},{20,28},{24,16},{28,20},{1,9},{5... | collective-permute-start | bytes 2359304 | tf_op jit(solution)/shard_map/ppermute | solution.py:1237
  318.9 283.8 %reduce-scatter.5.cloned.1.call-start = ((), (), s32[]{:S(2)}) async-start(), calls=%async_computation.3 | async-start | bytes 8847360 | tf_op jit(solution)/shard_map/reduce_scatter | solution.py:1509
  367.1 16.1 %collective-permute-start.34 = (bf16[4,544,1536]{2,1,0:T(8,128)(2,1)}, bf16[4,544,1536]{2,1,0:T(8,128)(2,1)S(1)}, u32[]{:S(2)}, u32[]{:S(2)}) collective-permute-start(bf16[4,544,1536]{2,1,0:T(8,128)(2,1)} %combine.7), channel_id=1, source_target_pairs={{0,4},{4,0},{8,12},{12,8},{16,20},{20,16},{24,28},{28,24},{1,5},{5... | collective-permute-start | bytes 20054024 | tf_op jit(solution)/shard_map/ppermute | solution.py:1237
  374.6 65.8 %collective-permute-start.33 = (bf16[4,512,1536]{2,1,0:T(8,128)(2,1)}, bf16[4,512,1536]{2,1,0:T(8,128)(2,1)}, u32[]{:S(2)}, u32[]{:S(2)}) collective-permute-start(bf16[4,512,1536]{2,1,0:T(8,128)(2,1)} %combine.5), channel_id=1, source_target_pairs={{0,4},{4,0},{8,12},{12,8},{16,20},{20,16},{24,28},{28,24},{1,5},{5... | collective-permute-start | bytes 18874376 | tf_op jit(solution)/shard_map/ppermute | solution.py:1237
  393.7 38.8 %collective-permute-start.35 = (bf16[2,272,1536]{2,1,0:T(8,128)(2,1)}, bf16[2,272,1536]{2,1,0:T(8,128)(2,1)S(1)}, u32[]{:S(2)}, u32[]{:S(2)}) collective-permute-start(bf16[2,272,1536]{2,1,0:T(8,128)(2,1)} %get-tuple-element.233), channel_id=1, source_target_pairs={{0,8},{4,12},{8,0},{12,4},{16,24},{20,28},{24,16},{28,20},{1,9},{5... | collective-permute-start | bytes 5013512 | tf_op jit(solution)/shard_map/ppermute | solution.py:1237
  395.2 38.4 %collective-permute-start.36 = (bf16[2,272,1536]{2,1,0:T(8,128)(2,1)}, bf16[2,272,1536]{2,1,0:T(8,128)(2,1)S(1)}, u32[]{:S(2)}, u32[]{:S(2)}) collective-permute-start(bf16[2,272,1536]{2,1,0:T(8,128)(2,1)} %get-tuple-element.234), channel_id=1, source_target_pairs={{0,16},{4,20},{8,24},{12,28},{16,0},{20,4},{24,8},{28,12},{1,17},{... | collective-permute-start | bytes 5013512 | tf_op jit(solution)/shard_map/ppermute | solution.py:1237
  438.1 19.8 %collective-permute-start.37 = (bf16[272,1536]{1,0:T(8,128)(2,1)}, bf16[272,1536]{1,0:T(8,128)(2,1)}, u32[]{:S(2)}, u32[]{:S(2)}) collective-permute-start(bf16[272,1536]{1,0:T(8,128)(2,1)} %get-tuple-element.241), channel_id=1, source_target_pairs={{0,16},{4,20},{8,24},{12,28},{16,0},{20,4},{24,8},{28,12},{1,17},{... | collective-permute-start | bytes 2506760 | tf_op jit(solution)/shard_map/ppermute | solution.py:1237
  439.6 19.5 %collective-permute-start.38 = (bf16[272,1536]{1,0:T(8,128)(2,1)}, bf16[272,1536]{1,0:T(8,128)(2,1)}, u32[]{:S(2)}, u32[]{:S(2)}) collective-permute-start(bf16[272,1536]{1,0:T(8,128)(2,1)} %get-tuple-element.242), channel_id=1, source_target_pairs={{0,8},{4,12},{8,0},{12,4},{16,24},{20,28},{24,16},{28,20},{1,9},{5... | collective-permute-start | bytes 2506760 | tf_op jit(solution)/shard_map/ppermute | solution.py:1237
  459.1 34.4 %collective-permute-start.39 = (bf16[2,256,1536]{2,1,0:T(8,128)(2,1)}, bf16[2,256,1536]{2,1,0:T(8,128)(2,1)S(1)}, u32[]{:S(2)}, u32[]{:S(2)}) collective-permute-start(bf16[2,256,1536]{2,1,0:T(8,128)(2,1)} %get-tuple-element.245), channel_id=1, source_target_pairs={{0,8},{4,12},{8,0},{12,4},{16,24},{20,28},{24,16},{28,20},{1,9},{5... | collective-permute-start | bytes 4718600 | tf_op jit(solution)/shard_map/ppermute | solution.py:1237
  460.4 34.4 %collective-permute-start.40 = (bf16[2,256,1536]{2,1,0:T(8,128)(2,1)}, bf16[2,256,1536]{2,1,0:T(8,128)(2,1)S(1)}, u32[]{:S(2)}, u32[]{:S(2)}) collective-permute-start(bf16[2,256,1536]{2,1,0:T(8,128)(2,1)} %get-tuple-element.246), channel_id=1, source_target_pairs={{0,16},{4,20},{8,24},{12,28},{16,0},{20,4},{24,8},{28,12},{1,17},{... | collective-permute-start | bytes 4718600 | tf_op jit(solution)/shard_map/ppermute | solution.py:1237
  525.8 30.4 %collective-permute-start.42 = (bf16[2,416,768]{2,1,0:T(8,128)(2,1)}, bf16[2,416,768]{2,1,0:T(8,128)(2,1)S(1)}, u32[]{:S(2)}, u32[]{:S(2)}) collective-permute-start(bf16[2,416,768]{2,1,0:T(8,128)(2,1)} %get-tuple-element.260), channel_id=1, source_target_pairs={{0,8},{4,12},{8,0},{12,4},{16,24},{20,28},{24,16},{28,20},{1,9},{5... | collective-permute-start | bytes 3833864 | tf_op jit(solution)/shard_map/ppermute | solution.py:1237
  526.3 30.1 %collective-permute-start.43 = (bf16[2,416,768]{2,1,0:T(8,128)(2,1)}, bf16[2,416,768]{2,1,0:T(8,128)(2,1)S(1)}, u32[]{:S(2)}, u32[]{:S(2)}) collective-permute-start(bf16[2,416,768]{2,1,0:T(8,128)(2,1)} %get-tuple-element.261), channel_id=1, source_target_pairs={{0,16},{4,20},{8,24},{12,28},{16,0},{20,4},{24,8},{28,12},{1,17},{... | collective-permute-start | bytes 3833864 | tf_op jit(solution)/shard_map/ppermute | solution.py:1237
  527.0 33.5 %collective-permute-start.46 = (bf16[512,512]{1,0:T(8,128)(2,1)S(1)}, bf16[512,512]{1,0:T(8,128)(2,1)S(1)}, u32[]{:S(2)}, u32[]{:S(2)}) collective-permute-start(bf16[512,512]{1,0:T(8,128)(2,1)S(1)} %convert_element_type.149), channel_id=1, source_target_pairs={{0,1},{2,3},{4,5},{6,7},{8,9},{10,11},{12,13},{14,15},{16,17},{18,... | collective-permute-start | bytes 1572872 | tf_op jit(solution)/shard_map/ppermute | solution.py:1527
  570.1 20.8 %collective-permute-start.44 = (bf16[416,768]{1,0:T(8,128)(2,1)}, bf16[416,768]{1,0:T(8,128)(2,1)S(1)}, u32[]{:S(2)}, u32[]{:S(2)}) collective-permute-start(bf16[416,768]{1,0:T(8,128)(2,1)} %get-tuple-element.266), channel_id=1, source_target_pairs={{0,16},{4,20},{8,24},{12,28},{16,0},{20,4},{24,8},{28,12},{1,17},{... | collective-permute-start | bytes 1916936 | tf_op jit(solution)/shard_map/ppermute | solution.py:1237
  570.8 20.1 %collective-permute-start.45 = (bf16[416,768]{1,0:T(8,128)(2,1)}, bf16[416,768]{1,0:T(8,128)(2,1)S(1)}, u32[]{:S(2)}, u32[]{:S(2)}) collective-permute-start(bf16[416,768]{1,0:T(8,128)(2,1)} %get-tuple-element.267), channel_id=1, source_target_pairs={{0,8},{4,12},{8,0},{12,4},{16,24},{20,28},{24,16},{28,20},{1,9},{5... | collective-permute-start | bytes 1916936 | tf_op jit(solution)/shard_map/ppermute | solution.py:1237
  618.2 19.6 %collective-permute-start.53 = (bf16[256,1536]{1,0:T(8,128)(2,1)}, bf16[256,1536]{1,0:T(8,128)(2,1)S(1)}, u32[]{:S(2)}, u32[]{:S(2)}) collective-permute-start(bf16[256,1536]{1,0:T(8,128)(2,1)} %get-tuple-element.295), channel_id=1, source_target_pairs={{0,16},{4,20},{8,24},{12,28},{16,0},{20,4},{24,8},{28,12},{1,17},{... | collective-permute-start | bytes 2359304 | tf_op jit(solution)/shard_map/ppermute | solution.py:1237
  618.7 19.4 %collective-permute-start.54 = (bf16[256,1536]{1,0:T(8,128)(2,1)}, bf16[256,1536]{1,0:T(8,128)(2,1)S(1)}, u32[]{:S(2)}, u32[]{:S(2)}) collective-permute-start(bf16[256,1536]{1,0:T(8,128)(2,1)} %get-tuple-element.296), channel_id=1, source_target_pairs={{0,8},{4,12},{8,0},{12,4},{16,24},{20,28},{24,16},{28,20},{1,9},{5... | collective-permute-start | bytes 2359304 | tf_op jit(solution)/shard_map/ppermute | solution.py:1237
  625.7 22.5 %collective-permute-start.55 = (bf16[208,896]{1,0:T(8,128)(2,1)S(1)}, bf16[208,896]{1,0:T(8,128)(2,1)S(1)}, u32[]{:S(2)}, u32[]{:S(2)}) collective-permute-start(bf16[208,896]{1,0:T(8,128)(2,1)S(1)} %get-tuple-element.313), channel_id=1, source_target_pairs={{0,1},{1,2},{2,3},{4,5},{5,6},{6,7},{8,9},{9,10},{10,11},{12,13},{... | collective-permute-start | bytes 1118216 | tf_op jit(solution)/shard_map/ppermute | solution.py:1227
  628.8 19.4 %collective-permute-start.56 = (bf16[208,896]{1,0:T(8,128)(2,1)S(1)}, bf16[208,896]{1,0:T(8,128)(2,1)S(1)}, u32[]{:S(2)}, u32[]{:S(2)}) collective-permute-start(bf16[208,896]{1,0:T(8,128)(2,1)S(1)} %get-tuple-element.312), channel_id=1, source_target_pairs={{1,0},{2,1},{3,2},{5,4},{6,5},{7,6},{9,8},{10,9},{11,10},{13,12},{... | collective-permute-start | bytes 1118216 | tf_op jit(solution)/shard_map/ppermute | solution.py:1228
  630.2 18.1 %collective-permute-start.57 = (bf16[208,896]{1,0:T(8,128)(2,1)S(1)}, bf16[208,896]{1,0:T(8,128)(2,1)S(1)}, u32[]{:S(2)}, u32[]{:S(2)}) collective-permute-start(bf16[208,896]{1,0:T(8,128)(2,1)S(1)} %get-tuple-element.297), channel_id=1, source_target_pairs={{0,3},{3,0},{4,7},{7,4},{8,11},{11,8},{12,15},{15,12},{16,19},{19,... | collective-permute-start | bytes 1118216 | tf_op jit(solution)/shard_map/ppermute | solution.py:1191
  (76 other events, 565.3 us)
Sparse Core Ops, SparseCore 0:
  201.7 127.1 all-gather.2
  331.2 121.7 reduce-scatter.2
  459.2 130.0 reduce-scatter.4

commit v20 on v19

--- a/solution.py
+++ b/solution.py
@@ -1557,8 +1557,6 @@
 
     if fast:
         pair_parts = chips_second(*pair_first[2:], *after(pair_chips, tokens_grad))
-    gate_grad, upward_grad, down_grad = expert_sums(reduced)
-    gate_grad, upward_grad = jnp.swapaxes(gate_grad, 1, 2), jnp.swapaxes(upward_grad, 1, 2)
     if fast:
         main_parts = after(main_parts, tokens_grad)
         slots = sum_parts(main_parts).reshape(col_count, depth + EXTRA, main_width)
@@ -1586,6 +1584,7 @@
         near_x, near_y = out_first[2:]
         mixture = chips_second(near_x, near_y, *after(out_flips, sent_load))
         layer_output = (residual + sum_parts(mixture)).astype(LOW)
+        gate_grad, upward_grad, down_grad = expert_sums(after(reduced, mixture[2], mixture[5]))
         earlier = (gate_grad, upward_grad, down_grad, layer_output)
         query_sum, key_sum, value_sum, out_sum, extra_sum = last_sums(
             info, slots[0], after(arrived, *earlier), depth, key_part
@@ -1596,6 +1595,7 @@
         attention_gain_sum = extra_sum[router_part + 1, :gain_part]
     else:
         layer_output = (residual + sum_parts(mixture)).astype(LOW)
+        gate_grad, upward_grad, down_grad = expert_sums(reduced)
         full_grads = [
             tn(normed, grad_query),
             *jnp.moveaxis(tn(normed, grad_pair).reshape(D, QUARTERS, 2, -1), 2, 0),
@@ -1644,8 +1644,8 @@
         router_sum,
         attention_gain_sum,
         experts_gain_sum,
-        gate_grad,
-        upward_grad,
+        jnp.swapaxes(gate_grad, 1, 2),
+        jnp.swapaxes(upward_grad, 1, 2),
         down_grad,
     )
 

time: 672 us -> 670 us (level)
  transfers between devices with their start and end apart: 61 -> 61, of which waited for: 29 -> 30; matrix products, arithmetic and copies ran while one was open for 6% -> 6% of each run, Pallas kernels for 46% -> 46%
where the time goes in v20:
time: 670 us; the launch traced here: 659 us
  Pallas kernels  312 us (47%)
  waiting for transfers between devices  172 us (26%)
  starting transfers between devices  87.7 us (13%)
  local copies, waits for them, and re-layouts  48.8 us (7%)
  other arithmetic  23.4 us (3%)
  between operations  14.9 us (2%)
    ppermute x44, waiting for transfers between devices, flip(): return lax.ppermute(block, 'rows', [(i, i ^ bit) for i in range(count)])  135 us
    pallas_call x2, Pallas kernels, expert(): pl.pallas_call(functools.partial(expert_kernel, slots), grid=(height // E...  61 us
    ppermute x44, starting transfers between devices, flip(): return lax.ppermute(block, 'rows', [(i, i ^ bit) for i in range(count)])  32.8 us
    pallas_call x4, Pallas kernels, combine(): pl.pallas_call(functools.partial(combine_kernel, local, first, step), out...  30.9 us
    pallas_call x2, Pallas kernels, expert_grads(): pl.pallas_call(expert_grads_kernel, grid=(D // 256,), out_shape=jax.Shape...  29.3 us
    pallas_call x8, Pallas kernels, dispatch(): pl.pallas_call(functools.partial(dispatch_kernel, local), grid=(D // wide...  29 us
    ppermute x4, starting transfers between devices, send_near(): return (lax.ppermute(block, 'cols', DOWN), lax.ppermute(block, 'cols', UP))  27.7 us
    unnamed x137, local copies, waits for them, and re-layouts  27.1 us
  transfers between devices with their start and end apart: 61, of which 30 were waited for; matrix products, arithmetic and copies ran while one was open for 6% of the time, Pallas kernels for 46%

profile of v20, /device:TPU:0, one launch (start us, length us, event | category | flops | bytes accessed | tf_op | source)
XLA Modules:
  0.0 659.2 jit_solution(5423064843960387395)
XLA Ops:
  14.1 6.3 collective-permute-start.1
  33.0 18.7 %collective-permute-start.9 = (bf16[576,1536]{1,0:T(8,128)(2,1)}, bf16[576,1536]{1,0:T(8,128)(2,1)}, u32[]{:S(2)}, u32[]{:S(2)}) collective-permute-start(bf16[576,1536]{1,0:T(8,128)(2,1)} %pad_maximum_fusion.2.rest_0_), channel_id=1, source_target_pairs={{0,1},{1,2},{2,3},{4,5},{5,6},{6,7},{8,9},{9,10},{10,11},{12,13},{... | collective-permute-start | bytes 5308424 | tf_op jit(solution)/shard_map/ppermute | solution.py:1187
  57.4 31.8 %collective-permute-done.6.rest_2_.rest_8_ = bf16[4,208,896]{2,1,0:T(8,128)(2,1)S(1)} collective-permute-done((bf16[4,208,896]{2,1,0:T(8,128)(2,1)S(1)}, bf16[4,208,896]{2,1,0:T(8,128)(2,1)S(1)}, u32[]{:S(2)}, u32[]{:S(2)}) %collective-permute-start.6) | collective-permute-done | bytes 1490976 | tf_op jit(solution)/shard_map/ppermute | solution.py:1237
  93.1 6.8 %collective-permute-start.2 = (bf16[576,1536]{1,0:T(8,128)(2,1)}, bf16[576,1536]{1,0:T(8,128)(2,1)}, u32[]{:S(2)}, u32[]{:S(2)}) collective-permute-start(bf16[576,1536]{1,0:T(8,128)(2,1)} %pad_maximum_fusion.2.rest_0_), channel_id=1, source_target_pairs={{0,3},{3,0},{4,7},{7,4},{8,11},{11,8},{12,15},{15,12},{16,19},{19,... | collective-permute-start | bytes 5308424 | tf_op jit(solution)/shard_map/ppermute | solution.py:1191
  99.9 10.1 %collective-permute-done.11.rest_4_.rest_10_ = bf16[2,208,896]{2,1,0:T(8,128)(2,1)S(1)} collective-permute-done((bf16[2,208,896]{2,1,0:T(8,128)(2,1)S(1)}, bf16[2,208,896]{2,1,0:T(8,128)(2,1)S(1)}, u32[]{:S(2)}, u32[]{:S(2)}) %collective-permute-start.11) | collective-permute-done | bytes 745504 | tf_op jit(solution)/shard_map/ppermute | solution.py:1237
  112.5 4.4 collective-permute-done.12.rest_7_.rest_13_
  118.1 5.6 route_tables.1
  129.1 9.8 %collective-permute-done.2.rest_4_ = bf16[576,1536]{1,0:T(8,128)(2,1)} collective-permute-done((bf16[576,1536]{1,0:T(8,128)(2,1)}, bf16[576,1536]{1,0:T(8,128)(2,1)}, u32[]{:S(2)}, u32[]{:S(2)}) %collective-permute-start.2) | collective-permute-done | bytes 1769504 | tf_op jit(solution)/shard_map/ppermute | solution.py:1191
  138.8 5.0 norm_key_value.1
  145.2 8.2 %query_projection.1.queries = bf16[512,1536]{1,0:T(8,128)(2,1)} custom-call(s32[16]{0:T(128)} %concatenate.49.info, bf16[512,1536]{1,0:T(8,128)(2,1)} %get-tuple-element.171.normed.rest_0_, f32[512,128]{1,0:T(8,128)} %get-tuple-element.336.cosine, f32[512,128]{1,0:T(8,128)} %get-tuple-element.337.sine, bf16[4,208,896]{2,1,0:T(8,128)(2,1)} %copy-done.1, ...), custom_call_target="tpu_custom_call" | custom-call | flops 1 | bytes 1 | tf_op jit(solution)/shard_map/query_projection/pallas_call | solution.py:195
  153.4 5.9 collective-permute-done.16.partner
  171.3 11.0 %tree_attention.1.heads.rest_1_ = bf16[512,1536]{1,0:T(8,128)(2,1)} custom-call(s32[16]{0:T(128)} %concatenate.49.info, bf16[512,1536]{1,0:T(8,128)(2,1)} %query_projection.1.queries, bf16[512,512]{1,0:T(8,128)(2,1)} %get-tuple-element.172.own, bf16[512,512]{1,0:T(8,128)(2,1)} %collective-permute-done.16.partner), custom_call_target="tpu_custom_call" | custom-call | flops 1 | bytes 1 | tf_op jit(solution)/shard_map/tree_attention/pallas_call | solution.py:277
  190.8 9.9 %out_projection.1 = (f32[512,1536]{1,0:T(8,128)}, bf16[512,1536]{1,0:T(8,128)(2,1)}) custom-call(s32[16]{0:T(128)} %concatenate.49.info, bf16[512,1536]{1,0:T(8,128)(2,1)} %tree_attention.1.heads.rest_1_, bf16[512,1536]{1,0:T(8,128)(2,1)} %tokens.4, f32[1,1536]{1,0:T(1,128)} %reshape.299.gain, bf16[4,208,896]{2,1,0:T(8,128)(2,1)} %copy-done.1, ...), custom_call_target="tpu_custom_call" | custom-call | flops 1 | bytes 1 | tf_op jit(solution)/shard_map/out_projection/pallas_call | solution.py:389
  208.4 3.9 dispatch.8
  212.3 9.4 %pick_rows.1 = (bf16[8,160,1536]{2,1,0:T(8,128)(2,1)}, bf16[8,160,1536]{2,1,0:T(8,128)(2,1)}) custom-call(bf16[8,320,512]{2,1,0:T(8,128)(2,1)} %get-tuple-element.167.chosen, bf16[512,1536]{1,0:T(8,128)(2,1)} %cotangent.1, bf16[512,1536]{1,0:T(8,128)(2,1)} %collective-permute-done.15.rest_1_, bf16[512,1536]{1,0:T(8,128)(2,1)} %copy-done.18, ...), custom_call_target="tpu_custom_call" | custom-call | flops 1 | bytes 1 | tf_op jit(solution)/shard_map/pick_rows/pallas_call | solution.py:480
  221.7 3.6 dispatch.9
  225.3 13.8 %collective-permute-done.23.rows = bf16[512,1536]{1,0:T(8,128)(2,1)} collective-permute-done((bf16[512,1536]{1,0:T(8,128)(2,1)S(1)}, bf16[512,1536]{1,0:T(8,128)(2,1)}, u32[]{:S(2)}, u32[]{:S(2)}) %collective-permute-start.23) | collective-permute-done | bytes 1572896 | tf_op jit(solution)/shard_map/ppermute | solution.py:1237
  245.3 3.6 dispatch.10
  248.9 3.6 dispatch.11
  253.6 3.6 dispatch.12
  258.3 3.6 dispatch.13
  265.2 3.6 dispatch.14
  269.9 3.6 dispatch.15
  273.5 30.7 %expert.2 = (bf16[1280,1536]{1,0:T(8,128)(2,1)}, bf16[1280,1536]{1,0:T(8,128)(2,1)}, bf16[1280,1536]{1,0:T(8,128)(2,1)}, bf16[4,576,1280]{2,1,0:T(8,128)(2,1)}, f32[1280,1]{1,0:T(8,128)}) custom-call(s32[16]{0:T(128)} %concatenate.49.info, bf16[1280,1536]{1,0:T(8,128)(2,1)} %bitcast.110, bf16[1280,1536]{1,0:T(8,128)(2,1)} %bitcast.129, f32[1280,1]{1,0:T(8,128)} %bitcast.114, ...), custom_call_target="tpu_custom_call" | custom-call | flops 1 | bytes 1 | tf_op jit(solution)/shard_map/expert/pallas_call | solution.py:670
  304.3 14.6 %expert_gradients.2 = bf16[4,576,1536]{2,1,0:T(8,128)(2,1)} custom-call(bf16[4,576,1280]{2,1,0:T(8,128)(2,1)} %get-tuple-element.221.acts, bf16[1280,1536]{1,0:T(8,128)(2,1)} %bitcast.111, bf16[1280,1536]{1,0:T(8,128)(2,1)} %get-tuple-element.222.grads), custom_call_target="tpu_custom_call" | custom-call | flops 1 | bytes 1 | tf_op jit(solution)/shard_map/expert_gradients/pallas_call | solution.py:699
  319.0 9.9 %all-gather.3.cloned.1.call-done = bf16[2304,1536]{1,0:T(8,128)(2,1)} async-done(((bf16[576,1536]{1,0:T(8,128)(2,1)}), bf16[2304,1536]{1,0:T(8,128)(2,1)}) %all-gather.3.cloned.1.call-update) | async-done | bytes 7077904 | tf_op jit(solution)/shard_map/all_gather | solution.py:1420
  328.9 30.2 %expert.3 = (bf16[1280,1536]{1,0:T(8,128)(2,1)}, bf16[1280,1536]{1,0:T(8,128)(2,1)}, bf16[1280,1536]{1,0:T(8,128)(2,1)}, bf16[4,576,1280]{2,1,0:T(8,128)(2,1)}, f32[1280,1]{1,0:T(8,128)}) custom-call(s32[16]{0:T(128)} %concatenate.49.info, bf16[1280,1536]{1,0:T(8,128)(2,1)} %bitcast.112, bf16[1280,1536]{1,0:T(8,128)(2,1)} %bitcast.130, f32[1280,1]{1,0:T(8,128)} %bitcast.115, ...), custom_call_target="tpu_custom_call" | custom-call | flops 1 | bytes 1 | tf_op jit(solution)/shard_map/expert/pallas_call | solution.py:670
  359.1 8.0 %combine.7 = bf16[4,544,1536]{2,1,0:T(8,128)(2,1)} custom-call(s32[16]{0:T(128)} %concatenate.49.info, bf16[8,320,512]{2,1,0:T(8,128)(2,1)} %get-tuple-element.167.chosen, bf16[8,160,1536]{2,1,0:T(8,128)(2,1)} %bitcast.118, bf16[8,160,1536]{2,1,0:T(8,128)(2,1)} %bitcast.122, f32[8,160,1]{2,1,0:T(8,128)} %bitcast.133, f32[8,160,1]{2,1,0:T(8,128)} %bitcast.135), custom_call_target="tpu_custom_call" | custom-call | flops 1 | bytes 1 | tf_op jit(solution)/shard_map/combine/pallas_call | solution.py:762
  367.3 7.3 %combine.5 = bf16[4,512,1536]{2,1,0:T(8,128)(2,1)} custom-call(s32[16]{0:T(128)} %concatenate.49.info, bf16[8,320,512]{2,1,0:T(8,128)(2,1)} %get-tuple-element.167.chosen, bf16[8,160,1536]{2,1,0:T(8,128)(2,1)} %bitcast.116, bf16[8,160,1536]{2,1,0:T(8,128)(2,1)} %bitcast.120), custom_call_target="tpu_custom_call" | custom-call | flops 1 | bytes 1 | tf_op jit(solution)/shard_map/combine/pallas_call | solution.py:762
  375.1 8.1 %combine.6.keep = bf16[4,544,1536]{2,1,0:T(8,128)(2,1)} custom-call(s32[16]{0:T(128)} %concatenate.49.info, bf16[8,320,512]{2,1,0:T(8,128)(2,1)} %get-tuple-element.167.chosen, bf16[8,160,1536]{2,1,0:T(8,128)(2,1)} %bitcast.119, bf16[8,160,1536]{2,1,0:T(8,128)(2,1)} %bitcast.123, f32[8,160,1]{2,1,0:T(8,128)} %bitcast.134, f32[8,160,1]{2,1,0:T(8,128)} %bitcast.136), custom_call_target="tpu_custom_call" | custom-call | flops 1 | bytes 1 | tf_op jit(solution)/shard_map/combine/pallas_call | solution.py:762
  385.9 7.8 %chip_sums.5 = (bf16[2,272,1536]{2,1,0:T(8,128)(2,1)}, bf16[2,272,1536]{2,1,0:T(8,128)(2,1)}, bf16[2,272,1536]{2,1,0:T(8,128)(2,1)}, bf16[2,272,1536]{2,1,0:T(8,128)(2,1)}) custom-call(bf16[4,544,1536]{2,1,0:T(8,128)(2,1)} %combine.6.keep, bf16[4,544,1536]{2,1,0:T(8,128)(2,1)} %copy-done.10), custom_call_target="tpu_custom_call" | custom-call | flops 1 | bytes 1 | tf_op jit(solution)/shard_map/chip_sums/pallas_call | solution.py:811
  396.7 7.5 %combine.4.keep = bf16[4,512,1536]{2,1,0:T(8,128)(2,1)} custom-call(s32[16]{0:T(128)} %concatenate.49.info, bf16[8,320,512]{2,1,0:T(8,128)(2,1)} %get-tuple-element.167.chosen, bf16[8,160,1536]{2,1,0:T(8,128)(2,1)} %bitcast.117, bf16[8,160,1536]{2,1,0:T(8,128)(2,1)} %bitcast.121), custom_call_target="tpu_custom_call" | custom-call | flops 1 | bytes 1 | tf_op jit(solution)/shard_map/combine/pallas_call | solution.py:762
  404.3 14.7 %expert_gradients.3 = bf16[4,576,1536]{2,1,0:T(8,128)(2,1)} custom-call(bf16[4,576,1280]{2,1,0:T(8,128)(2,1)} %get-tuple-element.238.acts, bf16[1280,1536]{1,0:T(8,128)(2,1)} %bitcast.113, bf16[1280,1536]{1,0:T(8,128)(2,1)} %get-tuple-element.239.grads), custom_call_target="tpu_custom_call" | custom-call | flops 1 | bytes 1 | tf_op jit(solution)/shard_map/expert_gradients/pallas_call | solution.py:699
  419.0 13.5 %collective-permute-done.35.got_x.rest_1_ = bf16[2,272,1536]{2,1,0:T(8,128)(2,1)S(1)} collective-permute-done((bf16[2,272,1536]{2,1,0:T(8,128)(2,1)}, bf16[2,272,1536]{2,1,0:T(8,128)(2,1)S(1)}, u32[]{:S(2)}, u32[]{:S(2)}) %collective-permute-start.35) | collective-permute-done | bytes 1671200 | tf_op jit(solution)/shard_map/ppermute | solution.py:1237
  440.4 7.5 %chip_sums.4 = (bf16[2,256,1536]{2,1,0:T(8,128)(2,1)}, bf16[2,256,1536]{2,1,0:T(8,128)(2,1)}, bf16[2,256,1536]{2,1,0:T(8,128)(2,1)}, bf16[2,256,1536]{2,1,0:T(8,128)(2,1)}) custom-call(bf16[4,512,1536]{2,1,0:T(8,128)(2,1)} %combine.4.keep, bf16[4,512,1536]{2,1,0:T(8,128)(2,1)} %collective-permute-done.33.got), custom_call_target="tpu_custom_call" | custom-call | flops 1 | bytes 1 | tf_op jit(solution)/shard_map/chip_sums/pallas_call | solution.py:811
  447.9 10.0 %collective-permute-done.37.rest_2_ = bf16[272,1536]{1,0:T(8,128)(2,1)} collective-permute-done((bf16[272,1536]{1,0:T(8,128)(2,1)}, bf16[272,1536]{1,0:T(8,128)(2,1)}, u32[]{:S(2)}, u32[]{:S(2)}) %collective-permute-start.37) | collective-permute-done | bytes 835616 | tf_op jit(solution)/shard_map/ppermute | solution.py:1237
  461.0 13.3 %experts_norm_back.1 = (f32[512,1536]{1,0:T(8,128)}, bf16[512,1536]{1,0:T(8,128)(2,1)}, bf16[512,1536]{1,0:T(8,128)(2,1)}, f32[1,1536]{1,0:T(1,128)}, f32[16,1536]{1,0:T(8,128)}) custom-call(s32[16]{0:T(128)} %concatenate.49.info, f32[512,1536]{1,0:T(8,128)} %get-tuple-element.176.residual, bf16[512,1536]{1,0:T(8,128)(2,1)} %get-tuple-element.177.rows.normed, ...), custom_call_target="tpu_custom_call" | custom-call | flops 1 | bytes 1 | tf_op jit(solution)/shard_map/experts_norm_back/pallas_call | solution.py:922
  474.3 15.5 %tree_attention_back.1 = (bf16[512,1536]{1,0:T(8,128)(2,1)}, f32[512,512]{1,0:T(8,128)}, f32[512,512]{1,0:T(8,128)}) custom-call(s32[16]{0:T(128)} %concatenate.49.info, bf16[512,1536]{1,0:T(8,128)(2,1)} %query_projection.1.queries, bf16[512,512]{1,0:T(8,128)(2,1)} %get-tuple-element.172.own, bf16[512,512]{1,0:T(8,128)(2,1)} %collective-permute-done.16.partner, ...), custom_call_target="tpu_custom_call" | custom-call | flops 1 | bytes 1 | tf_op jit(solution)/shard_map/tree_attention_back/pallas_call | solution.py:338
  494.8 13.5 %weight_gradients.2 = (bf16[4,4,208,768]{3,2,1,0:T(8,128)(2,1)}, bf16[4,4,208,768]{3,2,1,0:T(8,128)(2,1)}) custom-call(s32[16]{0:T(128)} %concatenate.49.info, bf16[512,1536]{1,0:T(8,128)(2,1)} %get-tuple-element.171.normed.rest_0_, bf16[512,1536]{1,0:T(8,128)(2,1)} %tree_attention.1.heads.rest_1_, bf16[512,1536]{1,0:T(8,128)(2,1)} %get-tuple-element.264.rest_2_.grad_query, ...), custom_call_target="tpu_custom_call" | custom-call | flops 1 | bytes 1 | tf_op jit(solution)/shard_map/weight_gradients/pallas_call | solution.py:1074
  508.3 8.7 %collective-permute-done.41 = bf16[4,4,208,768]{3,2,1,0:T(8,128)(2,1)S(1)} collective-permute-done((bf16[4,4,208,768]{3,2,1,0:T(8,128)(2,1)}, bf16[4,4,208,768]{3,2,1,0:T(8,128)(2,1)S(1)}, u32[]{:S(2)}, u32[]{:S(2)}) %collective-permute-start.41) | collective-permute-done | bytes 5111840 | tf_op jit(solution)/shard_map/ppermute | solution.py:1237
  519.2 6.6 chip_sums.6
  528.4 8.0 %normed_gradient.1.query_part = f32[512,1536]{1,0:T(8,128)} custom-call(s32[16]{0:T(128)} %concatenate.49.info, bf16[512,1536]{1,0:T(8,128)(2,1)} %get-tuple-element.264.rest_2_.grad_query, bf16[4,208,896]{2,1,0:T(8,128)(2,1)} %copy-done.1, bf16[4,208,896]{2,1,0:T(8,128)(2,1)} %copy-done.5, bf16[4,208,896]{2,1,0:T(8,128)(2,1)} %copy-done.3, ...), custom_call_target="tpu_custom_call" | custom-call | flops 1 | bytes 1 | tf_op jit(solution)/shard_map/normed_gradient/pallas_call | solution.py:999
  536.4 19.8 %collective-permute-done.42.got_x = bf16[2,416,768]{2,1,0:T(8,128)(2,1)S(1)} collective-permute-done((bf16[2,416,768]{2,1,0:T(8,128)(2,1)}, bf16[2,416,768]{2,1,0:T(8,128)(2,1)S(1)}, u32[]{:S(2)}, u32[]{:S(2)}) %collective-permute-start.42) | collective-permute-done | bytes 1277984 | tf_op jit(solution)/shard_map/ppermute | solution.py:1237
  564.4 5.7 weight_gradients.3
  582.7 8.2 %token_gradient.1 = (bf16[512,1536]{1,0:T(8,128)(2,1)}, f32[1,1536]{1,0:T(1,128)}) custom-call(s32[16]{0:T(128)} %concatenate.49.info, f32[512,1536]{1,0:T(8,128)} %normed_gradient.1.query_part, bf16[512,512]{1,0:T(8,128)(2,1)} %join_key_value_gradients.1.rest_1_.grad_pair, bf16[512,1536]{1,0:T(8,128)(2,1)} %tokens.4, ...), custom_call_target="tpu_custom_call" | custom-call | flops 1 | bytes 1 | tf_op jit(solution)/shard_map/token_gradient/pallas_call | solution.py:1026
  603.7 11.1 %collective-permute-done.52.rest_3_ = bf16[208,896]{1,0:T(8,128)(2,1)S(1)} collective-permute-done((bf16[208,896]{1,0:T(8,128)(2,1)S(1)}, bf16[208,896]{1,0:T(8,128)(2,1)S(1)}, u32[]{:S(2)}, u32[]{:S(2)}) %collective-permute-start.52) | collective-permute-done | bytes 372768 | tf_op jit(solution)/shard_map/ppermute | solution.py:1220
  625.0 7.6 %collective-permute-start.57 = (bf16[208,896]{1,0:T(8,128)(2,1)S(1)}, bf16[208,896]{1,0:T(8,128)(2,1)S(1)}, u32[]{:S(2)}, u32[]{:S(2)}) collective-permute-start(bf16[208,896]{1,0:T(8,128)(2,1)S(1)} %get-tuple-element.299), channel_id=1, source_target_pairs={{0,3},{3,0},{4,7},{7,4},{8,11},{11,8},{12,15},{15,12},{16,19},{19,... | collective-permute-start | bytes 1118216 | tf_op jit(solution)/shard_map/ppermute | solution.py:1191
  636.0 5.1 expert_sums.1
  (335 shorter events, 165.8 us)
Async XLA Ops:
  7.2 321.7 %all-gather.3.cloned.1.call-start = ((), (), s32[]{:S(2)}) async-start(), calls=%async_computation.4 | async-start | bytes 8847360 | tf_op jit(solution)/shard_map/all_gather | solution.py:1420
  12.7 19.0 %collective-permute-start = (bf16[208,896]{1,0:T(8,128)(2,1)S(1)}, bf16[208,896]{1,0:T(8,128)(2,1)S(1)}, u32[]{:S(2)}, u32[]{:S(2)}) collective-permute-start(bf16[208,896]{1,0:T(8,128)(2,1)S(1)} %concatenate.53), channel_id=1, source_target_pairs={{1,0},{2,1},{3,2},{5,4},{6,5},{7,6},{9,8},{10,9},{11,10},{13,12},{... | collective-permute-start | bytes 1118216 | tf_op jit(solution)/shard_map/ppermute | solution.py:1187
  14.1 17.6 %collective-permute-start.1 = (bf16[208,896]{1,0:T(8,128)(2,1)S(1)}, bf16[208,896]{1,0:T(8,128)(2,1)}, u32[]{:S(2)}, u32[]{:S(2)}) collective-permute-start(bf16[208,896]{1,0:T(8,128)(2,1)S(1)} %concatenate.53), channel_id=1, source_target_pairs={{0,1},{1,2},{2,3},{4,5},{5,6},{6,7},{8,9},{9,10},{10,11},{12,13},{... | collective-permute-start | bytes 1118216 | tf_op jit(solution)/shard_map/ppermute | solution.py:1187
  20.4 31.3 %collective-permute-start.4 = (bf16[208,896]{1,0:T(8,128)(2,1)S(1)}, bf16[208,896]{1,0:T(8,128)(2,1)}, u32[]{:S(2)}, u32[]{:S(2)}) collective-permute-start(bf16[208,896]{1,0:T(8,128)(2,1)S(1)} %concatenate.53), channel_id=1, source_target_pairs={{0,3},{3,0},{4,7},{7,4},{8,11},{11,8},{12,15},{15,12},{16,19},{19,... | collective-permute-start | bytes 1118216 | tf_op jit(solution)/shard_map/ppermute | solution.py:1191
  23.4 29.4 %collective-permute-start.3 = (bf16[208,896]{1,0:T(8,128)(2,1)S(1)}, bf16[208,896]{1,0:T(8,128)(2,1)}, u32[]{:S(2)}, u32[]{:S(2)}) collective-permute-start(bf16[208,896]{1,0:T(8,128)(2,1)S(1)} %concatenate.53), channel_id=1, source_target_pairs={{0,2},{1,3},{2,0},{3,1},{4,6},{5,7},{6,4},{7,5},{8,10},{9,11},{10,... | collective-permute-start | bytes 1118216 | tf_op jit(solution)/shard_map/ppermute | solution.py:1195
  31.7 58.7 %collective-permute-start.8 = (bf16[576,1536]{1,0:T(8,128)(2,1)}, bf16[576,1536]{1,0:T(8,128)(2,1)}, u32[]{:S(2)}, u32[]{:S(2)}) collective-permute-start(bf16[576,1536]{1,0:T(8,128)(2,1)} %pad_maximum_fusion.2.rest_0_), channel_id=1, source_target_pairs={{1,0},{2,1},{3,2},{5,4},{6,5},{7,6},{9,8},{10,9},{11,10},{13,12},{... | collective-permute-start | bytes 5308424 | tf_op jit(solution)/shard_map/ppermute | solution.py:1187
  33.0 57.4 %collective-permute-start.9 = (bf16[576,1536]{1,0:T(8,128)(2,1)}, bf16[576,1536]{1,0:T(8,128)(2,1)}, u32[]{:S(2)}, u32[]{:S(2)}) collective-permute-start(bf16[576,1536]{1,0:T(8,128)(2,1)} %pad_maximum_fusion.2.rest_0_), channel_id=1, source_target_pairs={{0,1},{1,2},{2,3},{4,5},{5,6},{6,7},{8,9},{9,10},{10,11},{12,13},{... | collective-permute-start | bytes 5308424 | tf_op jit(solution)/shard_map/ppermute | solution.py:1187
  54.1 35.1 %collective-permute-start.6 = (bf16[4,208,896]{2,1,0:T(8,128)(2,1)S(1)}, bf16[4,208,896]{2,1,0:T(8,128)(2,1)S(1)}, u32[]{:S(2)}, u32[]{:S(2)}) collective-permute-start(bf16[4,208,896]{2,1,0:T(8,128)(2,1)S(1)} %pad_maximum_fusion.4.rest_0_.rest_6_), channel_id=1, source_target_pairs={{0,8},{4,12},{8,0},{12,4},{16,24},{20,28},{24,16},{28,20},{1,9},{5... | collective-permute-start | bytes 4472840 | tf_op jit(solution)/shard_map/ppermute | solution.py:1237
  55.7 34.7 %collective-permute-start.7 = (bf16[4,208,896]{2,1,0:T(8,128)(2,1)S(1)}, bf16[4,208,896]{2,1,0:T(8,128)(2,1)S(1)}, u32[]{:S(2)}, u32[]{:S(2)}) collective-permute-start(bf16[4,208,896]{2,1,0:T(8,128)(2,1)S(1)} %pad_maximum_fusion.4.rest_0_.rest_6_), channel_id=1, source_target_pairs={{0,16},{4,20},{8,24},{12,28},{16,0},{20,4},{24,8},{28,12},{1,17},{... | collective-permute-start | bytes 4472840 | tf_op jit(solution)/shard_map/ppermute | solution.py:1237
  90.7 21.5 %collective-permute-start.10 = (bf16[8,208,896]{2,1,0:T(8,128)(2,1)S(1)}, bf16[8,208,896]{2,1,0:T(8,128)(2,1)S(1)}, u32[]{:S(2)}, u32[]{:S(2)}) collective-permute-start(bf16[8,208,896]{2,1,0:T(8,128)(2,1)S(1)} %pad_maximum_fusion), channel_id=1, source_target_pairs={{0,4},{4,0},{8,12},{12,8},{16,20},{20,16},{24,28},{28,24},{1,5},{5... | collective-permute-start | bytes 8945672 | tf_op jit(solution)/shard_map/ppermute | solution.py:1237
  90.9 19.1 %collective-permute-start.11 = (bf16[2,208,896]{2,1,0:T(8,128)(2,1)S(1)}, bf16[2,208,896]{2,1,0:T(8,128)(2,1)S(1)}, u32[]{:S(2)}, u32[]{:S(2)}) collective-permute-start(bf16[2,208,896]{2,1,0:T(8,128)(2,1)S(1)} %slice.144), channel_id=1, source_target_pairs={{0,16},{4,20},{8,24},{12,28},{16,0},{20,4},{24,8},{28,12},{1,17},{... | collective-permute-start | bytes 2236424 | tf_op jit(solution)/shard_map/ppermute | solution.py:1237
  92.5 18.9 %collective-permute-start.13 = (bf16[2,208,896]{2,1,0:T(8,128)(2,1)S(1)}, bf16[2,208,896]{2,1,0:T(8,128)(2,1)}, u32[]{:S(2)}, u32[]{:S(2)}) collective-permute-start(bf16[2,208,896]{2,1,0:T(8,128)(2,1)S(1)} %slice.147), channel_id=1, source_target_pairs={{0,8},{4,12},{8,0},{12,4},{16,24},{20,28},{24,16},{28,20},{1,9},{5... | collective-permute-start | bytes 2236424 | tf_op jit(solution)/shard_map/ppermute | solution.py:1237
  93.1 45.8 %collective-permute-start.2 = (bf16[576,1536]{1,0:T(8,128)(2,1)}, bf16[576,1536]{1,0:T(8,128)(2,1)}, u32[]{:S(2)}, u32[]{:S(2)}) collective-permute-start(bf16[576,1536]{1,0:T(8,128)(2,1)} %pad_maximum_fusion.2.rest_0_), channel_id=1, source_target_pairs={{0,3},{3,0},{4,7},{7,4},{8,11},{11,8},{12,15},{15,12},{16,19},{19,... | collective-permute-start | bytes 5308424 | tf_op jit(solution)/shard_map/ppermute | solution.py:1191
  111.4 33.8 %collective-permute-start.15 = (bf16[512,1536]{1,0:T(8,128)(2,1)S(1)}, bf16[512,1536]{1,0:T(8,128)(2,1)}, u32[]{:S(2)}, u32[]{:S(2)}) collective-permute-start(bf16[512,1536]{1,0:T(8,128)(2,1)S(1)} %copy-done.13), channel_id=1, source_target_pairs={{0,4},{4,0},{8,12},{12,8},{16,20},{20,16},{24,28},{28,24},{1,5},{5... | collective-permute-start | bytes 4718600 | tf_op jit(solution)/shard_map/ppermute | solution.py:1237
  111.4 52.2 %collective-permute-start.17 = (bf16[512,1536]{1,0:T(8,128)(2,1)S(1)}, bf16[512,1536]{1,0:T(8,128)(2,1)S(1)}, u32[]{:S(2)}, u32[]{:S(2)}) collective-permute-start(bf16[512,1536]{1,0:T(8,128)(2,1)S(1)} %copy-done.13), channel_id=1, source_target_pairs={{0,8},{4,12},{8,0},{12,4},{16,24},{20,28},{24,16},{28,20},{1,9},{5... | collective-permute-start | bytes 4718600 | tf_op jit(solution)/shard_map/ppermute | solution.py:1237
  117.0 46.7 %collective-permute-start.18 = (bf16[512,1536]{1,0:T(8,128)(2,1)S(1)}, bf16[512,1536]{1,0:T(8,128)(2,1)}, u32[]{:S(2)}, u32[]{:S(2)}) collective-permute-start(bf16[512,1536]{1,0:T(8,128)(2,1)S(1)} %copy-done.13), channel_id=1, source_target_pairs={{0,16},{4,20},{8,24},{12,28},{16,0},{20,4},{24,8},{28,12},{1,17},{... | collective-permute-start | bytes 4718600 | tf_op jit(solution)/shard_map/ppermute | solution.py:1237
  143.9 15.4 %collective-permute-start.16 = (bf16[512,512]{1,0:T(8,128)(2,1)}, bf16[512,512]{1,0:T(8,128)(2,1)}, u32[]{:S(2)}, u32[]{:S(2)}) collective-permute-start(bf16[512,512]{1,0:T(8,128)(2,1)} %get-tuple-element.172.own), channel_id=1, source_target_pairs={{1,0},{3,2},{5,4},{7,6},{9,8},{11,10},{13,12},{15,14},{17,16},{19,... | collective-permute-start | bytes 1572872 | tf_op jit(solution)/shard_map/ppermute | solution.py:1392
  162.2 39.3 %collective-permute-start.32 = (bf16[576,1536]{1,0:T(8,128)(2,1)}, bf16[576,1536]{1,0:T(8,128)(2,1)}, u32[]{:S(2)}, u32[]{:S(2)}) collective-permute-start(bf16[576,1536]{1,0:T(8,128)(2,1)} %select_select_fusion), channel_id=1, source_target_pairs={{3,1},{1,0},{0,2},{2,3},{7,5},{5,4},{4,6},{6,7},{11,9},{9,8},{8,10... | collective-permute-start | bytes 5308424 | tf_op jit(solution)/shard_map/ppermute | solution.py:1202
  163.7 24.9 %collective-permute-start.21 = (bf16[512,1536]{1,0:T(8,128)(2,1)S(1)}, bf16[512,1536]{1,0:T(8,128)(2,1)S(1)}, u32[]{:S(2)}, u32[]{:S(2)}) collective-permute-start(bf16[512,1536]{1,0:T(8,128)(2,1)S(1)} %collective-permute-done.17.rest_2_), channel_id=1, source_target_pairs={{0,4},{4,0},{8,12},{12,8},{16,20},{20,16},{24,28},{28,24},{1,5},{5... | collective-permute-start | bytes 4718600 | tf_op jit(solution)/shard_map/ppermute | solution.py:1237
  163.7 25.9 %collective-permute-start.22 = (bf16[512,1536]{1,0:T(8,128)(2,1)}, bf16[512,1536]{1,0:T(8,128)(2,1)}, u32[]{:S(2)}, u32[]{:S(2)}) collective-permute-start(bf16[512,1536]{1,0:T(8,128)(2,1)} %collective-permute-done.18.rest_4_), channel_id=1, source_target_pairs={{0,4},{4,0},{8,12},{12,8},{16,20},{20,16},{24,28},{28,24},{1,5},{5... | collective-permute-start | bytes 4718600 | tf_op jit(solution)/shard_map/ppermute | solution.py:1237
  165.2 19.8 %collective-permute-start.19 = (bf16[256,1536]{1,0:T(8,128)(2,1)}, bf16[256,1536]{1,0:T(8,128)(2,1)}, u32[]{:S(2)}, u32[]{:S(2)}) collective-permute-start(bf16[256,1536]{1,0:T(8,128)(2,1)} %slice.149), channel_id=1, source_target_pairs={{0,16},{4,20},{8,24},{12,28},{16,0},{20,4},{24,8},{28,12},{1,17},{... | collective-permute-start | bytes 2359304 | tf_op jit(solution)/shard_map/ppermute | solution.py:1237
  167.8 19.6 %collective-permute-start.20 = (bf16[256,1536]{1,0:T(8,128)(2,1)}, bf16[256,1536]{1,0:T(8,128)(2,1)}, u32[]{:S(2)}, u32[]{:S(2)}) collective-permute-start(bf16[256,1536]{1,0:T(8,128)(2,1)} %slice.150), channel_id=1, source_target_pairs={{0,8},{4,12},{8,0},{12,4},{16,24},{20,28},{24,16},{28,20},{1,9},{5... | collective-permute-start | bytes 2359304 | tf_op jit(solution)/shard_map/ppermute | solution.py:1237
  201.6 257.5 %reduce-scatter.3.cloned.1.call-start = ((), (), s32[]{:S(2)}) async-start(), calls=%async_computation.2 | async-start | bytes 8847360 | tf_op jit(solution)/shard_map/reduce_scatter | solution.py:1479
  202.2 19.5 %collective-permute-start.25 = (bf16[512,1536]{1,0:T(8,128)(2,1)S(1)}, bf16[512,1536]{1,0:T(8,128)(2,1)}, u32[]{:S(2)}, u32[]{:S(2)}) collective-permute-start(bf16[512,1536]{1,0:T(8,128)(2,1)S(1)} %copy-done.14), channel_id=1, source_target_pairs={{0,4},{4,0},{8,12},{12,8},{16,20},{20,16},{24,28},{28,24},{1,5},{5... | collective-permute-start | bytes 4718600 | tf_op jit(solution)/shard_map/ppermute | solution.py:1237
  202.5 36.6 %collective-permute-start.23 = (bf16[512,1536]{1,0:T(8,128)(2,1)S(1)}, bf16[512,1536]{1,0:T(8,128)(2,1)}, u32[]{:S(2)}, u32[]{:S(2)}) collective-permute-start(bf16[512,1536]{1,0:T(8,128)(2,1)S(1)} %copy-done.14), channel_id=1, source_target_pairs={{0,8},{4,12},{8,0},{12,4},{16,24},{20,28},{24,16},{28,20},{1,9},{5... | collective-permute-start | bytes 4718600 | tf_op jit(solution)/shard_map/ppermute | solution.py:1237
  204.0 36.3 %collective-permute-start.24 = (bf16[512,1536]{1,0:T(8,128)(2,1)S(1)}, bf16[512,1536]{1,0:T(8,128)(2,1)}, u32[]{:S(2)}, u32[]{:S(2)}) collective-permute-start(bf16[512,1536]{1,0:T(8,128)(2,1)S(1)} %copy-done.14), channel_id=1, source_target_pairs={{0,16},{4,20},{8,24},{12,28},{16,0},{20,4},{24,8},{28,12},{1,17},{... | collective-permute-start | bytes 4718600 | tf_op jit(solution)/shard_map/ppermute | solution.py:1237
  240.3 16.9 %collective-permute-start.29 = (bf16[512,1536]{1,0:T(8,128)(2,1)}, bf16[512,1536]{1,0:T(8,128)(2,1)S(1)}, u32[]{:S(2)}, u32[]{:S(2)}) collective-permute-start(bf16[512,1536]{1,0:T(8,128)(2,1)} %collective-permute-done.24.rows), channel_id=1, source_target_pairs={{0,4},{4,0},{8,12},{12,8},{16,20},{20,16},{24,28},{28,24},{1,5},{5... | collective-permute-start | bytes 4718600 | tf_op jit(solution)/shard_map/ppermute | solution.py:1237
  243.2 19.5 %collective-permute-start.27 = (bf16[256,1536]{1,0:T(8,128)(2,1)S(1)}, bf16[256,1536]{1,0:T(8,128)(2,1)S(1)}, u32[]{:S(2)}, u32[]{:S(2)}) collective-permute-start(bf16[256,1536]{1,0:T(8,128)(2,1)S(1)} %slice.153), channel_id=1, source_target_pairs={{0,16},{4,20},{8,24},{12,28},{16,0},{20,4},{24,8},{28,12},{1,17},{... | collective-permute-start | bytes 2359304 | tf_op jit(solution)/shard_map/ppermute | solution.py:1237
  244.8 19.2 %collective-permute-start.28 = (bf16[256,1536]{1,0:T(8,128)(2,1)S(1)}, bf16[256,1536]{1,0:T(8,128)(2,1)S(1)}, u32[]{:S(2)}, u32[]{:S(2)}) collective-permute-start(bf16[256,1536]{1,0:T(8,128)(2,1)S(1)} %slice.154), channel_id=1, source_target_pairs={{0,8},{4,12},{8,0},{12,4},{16,24},{20,28},{24,16},{28,20},{1,9},{5... | collective-permute-start | bytes 2359304 | tf_op jit(solution)/shard_map/ppermute | solution.py:1237
  318.9 283.8 %reduce-scatter.5.cloned.1.call-start = ((), (), s32[]{:S(2)}) async-start(), calls=%async_computation.3 | async-start | bytes 8847360 | tf_op jit(solution)/shard_map/reduce_scatter | solution.py:1509
  367.1 16.1 %collective-permute-start.34 = (bf16[4,544,1536]{2,1,0:T(8,128)(2,1)}, bf16[4,544,1536]{2,1,0:T(8,128)(2,1)S(1)}, u32[]{:S(2)}, u32[]{:S(2)}) collective-permute-start(bf16[4,544,1536]{2,1,0:T(8,128)(2,1)} %combine.7), channel_id=1, source_target_pairs={{0,4},{4,0},{8,12},{12,8},{16,20},{20,16},{24,28},{28,24},{1,5},{5... | collective-permute-start | bytes 20054024 | tf_op jit(solution)/shard_map/ppermute | solution.py:1237
  374.6 65.8 %collective-permute-start.33 = (bf16[4,512,1536]{2,1,0:T(8,128)(2,1)}, bf16[4,512,1536]{2,1,0:T(8,128)(2,1)}, u32[]{:S(2)}, u32[]{:S(2)}) collective-permute-start(bf16[4,512,1536]{2,1,0:T(8,128)(2,1)} %combine.5), channel_id=1, source_target_pairs={{0,4},{4,0},{8,12},{12,8},{16,20},{20,16},{24,28},{28,24},{1,5},{5... | collective-permute-start | bytes 18874376 | tf_op jit(solution)/shard_map/ppermute | solution.py:1237
  393.7 38.8 %collective-permute-start.35 = (bf16[2,272,1536]{2,1,0:T(8,128)(2,1)}, bf16[2,272,1536]{2,1,0:T(8,128)(2,1)S(1)}, u32[]{:S(2)}, u32[]{:S(2)}) collective-permute-start(bf16[2,272,1536]{2,1,0:T(8,128)(2,1)} %get-tuple-element.235), channel_id=1, source_target_pairs={{0,8},{4,12},{8,0},{12,4},{16,24},{20,28},{24,16},{28,20},{1,9},{5... | collective-permute-start | bytes 5013512 | tf_op jit(solution)/shard_map/ppermute | solution.py:1237
  395.2 38.4 %collective-permute-start.36 = (bf16[2,272,1536]{2,1,0:T(8,128)(2,1)}, bf16[2,272,1536]{2,1,0:T(8,128)(2,1)S(1)}, u32[]{:S(2)}, u32[]{:S(2)}) collective-permute-start(bf16[2,272,1536]{2,1,0:T(8,128)(2,1)} %get-tuple-element.236), channel_id=1, source_target_pairs={{0,16},{4,20},{8,24},{12,28},{16,0},{20,4},{24,8},{28,12},{1,17},{... | collective-permute-start | bytes 5013512 | tf_op jit(solution)/shard_map/ppermute | solution.py:1237
  438.1 19.8 %collective-permute-start.37 = (bf16[272,1536]{1,0:T(8,128)(2,1)}, bf16[272,1536]{1,0:T(8,128)(2,1)}, u32[]{:S(2)}, u32[]{:S(2)}) collective-permute-start(bf16[272,1536]{1,0:T(8,128)(2,1)} %get-tuple-element.243), channel_id=1, source_target_pairs={{0,16},{4,20},{8,24},{12,28},{16,0},{20,4},{24,8},{28,12},{1,17},{... | collective-permute-start | bytes 2506760 | tf_op jit(solution)/shard_map/ppermute | solution.py:1237
  439.6 19.5 %collective-permute-start.38 = (bf16[272,1536]{1,0:T(8,128)(2,1)}, bf16[272,1536]{1,0:T(8,128)(2,1)}, u32[]{:S(2)}, u32[]{:S(2)}) collective-permute-start(bf16[272,1536]{1,0:T(8,128)(2,1)} %get-tuple-element.244), channel_id=1, source_target_pairs={{0,8},{4,12},{8,0},{12,4},{16,24},{20,28},{24,16},{28,20},{1,9},{5... | collective-permute-start | bytes 2506760 | tf_op jit(solution)/shard_map/ppermute | solution.py:1237
  459.1 34.4 %collective-permute-start.39 = (bf16[2,256,1536]{2,1,0:T(8,128)(2,1)}, bf16[2,256,1536]{2,1,0:T(8,128)(2,1)S(1)}, u32[]{:S(2)}, u32[]{:S(2)}) collective-permute-start(bf16[2,256,1536]{2,1,0:T(8,128)(2,1)} %get-tuple-element.247), channel_id=1, source_target_pairs={{0,8},{4,12},{8,0},{12,4},{16,24},{20,28},{24,16},{28,20},{1,9},{5... | collective-permute-start | bytes 4718600 | tf_op jit(solution)/shard_map/ppermute | solution.py:1237
  460.4 34.4 %collective-permute-start.40 = (bf16[2,256,1536]{2,1,0:T(8,128)(2,1)}, bf16[2,256,1536]{2,1,0:T(8,128)(2,1)S(1)}, u32[]{:S(2)}, u32[]{:S(2)}) collective-permute-start(bf16[2,256,1536]{2,1,0:T(8,128)(2,1)} %get-tuple-element.248), channel_id=1, source_target_pairs={{0,16},{4,20},{8,24},{12,28},{16,0},{20,4},{24,8},{28,12},{1,17},{... | collective-permute-start | bytes 4718600 | tf_op jit(solution)/shard_map/ppermute | solution.py:1237
  525.8 30.4 %collective-permute-start.42 = (bf16[2,416,768]{2,1,0:T(8,128)(2,1)}, bf16[2,416,768]{2,1,0:T(8,128)(2,1)S(1)}, u32[]{:S(2)}, u32[]{:S(2)}) collective-permute-start(bf16[2,416,768]{2,1,0:T(8,128)(2,1)} %get-tuple-element.262), channel_id=1, source_target_pairs={{0,8},{4,12},{8,0},{12,4},{16,24},{20,28},{24,16},{28,20},{1,9},{5... | collective-permute-start | bytes 3833864 | tf_op jit(solution)/shard_map/ppermute | solution.py:1237
  526.3 30.1 %collective-permute-start.43 = (bf16[2,416,768]{2,1,0:T(8,128)(2,1)}, bf16[2,416,768]{2,1,0:T(8,128)(2,1)S(1)}, u32[]{:S(2)}, u32[]{:S(2)}) collective-permute-start(bf16[2,416,768]{2,1,0:T(8,128)(2,1)} %get-tuple-element.263), channel_id=1, source_target_pairs={{0,16},{4,20},{8,24},{12,28},{16,0},{20,4},{24,8},{28,12},{1,17},{... | collective-permute-start | bytes 3833864 | tf_op jit(solution)/shard_map/ppermute | solution.py:1237
  527.0 33.5 %collective-permute-start.46 = (bf16[512,512]{1,0:T(8,128)(2,1)S(1)}, bf16[512,512]{1,0:T(8,128)(2,1)S(1)}, u32[]{:S(2)}, u32[]{:S(2)}) collective-permute-start(bf16[512,512]{1,0:T(8,128)(2,1)S(1)} %convert_element_type.149), channel_id=1, source_target_pairs={{0,1},{2,3},{4,5},{6,7},{8,9},{10,11},{12,13},{14,15},{16,17},{18,... | collective-permute-start | bytes 1572872 | tf_op jit(solution)/shard_map/ppermute | solution.py:1527
  570.1 20.8 %collective-permute-start.44 = (bf16[416,768]{1,0:T(8,128)(2,1)}, bf16[416,768]{1,0:T(8,128)(2,1)S(1)}, u32[]{:S(2)}, u32[]{:S(2)}) collective-permute-start(bf16[416,768]{1,0:T(8,128)(2,1)} %get-tuple-element.268), channel_id=1, source_target_pairs={{0,16},{4,20},{8,24},{12,28},{16,0},{20,4},{24,8},{28,12},{1,17},{... | collective-permute-start | bytes 1916936 | tf_op jit(solution)/shard_map/ppermute | solution.py:1237
  570.8 20.1 %collective-permute-start.45 = (bf16[416,768]{1,0:T(8,128)(2,1)}, bf16[416,768]{1,0:T(8,128)(2,1)S(1)}, u32[]{:S(2)}, u32[]{:S(2)}) collective-permute-start(bf16[416,768]{1,0:T(8,128)(2,1)} %get-tuple-element.269), channel_id=1, source_target_pairs={{0,8},{4,12},{8,0},{12,4},{16,24},{20,28},{24,16},{28,20},{1,9},{5... | collective-permute-start | bytes 1916936 | tf_op jit(solution)/shard_map/ppermute | solution.py:1237
  618.2 17.2 %collective-permute-start.53 = (bf16[256,1536]{1,0:T(8,128)(2,1)}, bf16[256,1536]{1,0:T(8,128)(2,1)S(1)}, u32[]{:S(2)}, u32[]{:S(2)}) collective-permute-start(bf16[256,1536]{1,0:T(8,128)(2,1)} %get-tuple-element.297), channel_id=1, source_target_pairs={{0,16},{4,20},{8,24},{12,28},{16,0},{20,4},{24,8},{28,12},{1,17},{... | collective-permute-start | bytes 2359304 | tf_op jit(solution)/shard_map/ppermute | solution.py:1237
  618.7 17.3 %collective-permute-start.54 = (bf16[256,1536]{1,0:T(8,128)(2,1)}, bf16[256,1536]{1,0:T(8,128)(2,1)S(1)}, u32[]{:S(2)}, u32[]{:S(2)}) collective-permute-start(bf16[256,1536]{1,0:T(8,128)(2,1)} %get-tuple-element.298), channel_id=1, source_target_pairs={{0,8},{4,12},{8,0},{12,4},{16,24},{20,28},{24,16},{28,20},{1,9},{5... | collective-permute-start | bytes 2359304 | tf_op jit(solution)/shard_map/ppermute | solution.py:1237
  620.5 26.0 %collective-permute-start.55 = (bf16[208,896]{1,0:T(8,128)(2,1)S(1)}, bf16[208,896]{1,0:T(8,128)(2,1)S(1)}, u32[]{:S(2)}, u32[]{:S(2)}) collective-permute-start(bf16[208,896]{1,0:T(8,128)(2,1)S(1)} %get-tuple-element.317), channel_id=1, source_target_pairs={{0,1},{1,2},{2,3},{4,5},{5,6},{6,7},{8,9},{9,10},{10,11},{12,13},{... | collective-permute-start | bytes 1118216 | tf_op jit(solution)/shard_map/ppermute | solution.py:1227
  623.7 22.8 %collective-permute-start.56 = (bf16[208,896]{1,0:T(8,128)(2,1)S(1)}, bf16[208,896]{1,0:T(8,128)(2,1)S(1)}, u32[]{:S(2)}, u32[]{:S(2)}) collective-permute-start(bf16[208,896]{1,0:T(8,128)(2,1)S(1)} %get-tuple-element.316), channel_id=1, source_target_pairs={{1,0},{2,1},{3,2},{5,4},{6,5},{7,6},{9,8},{10,9},{11,10},{13,12},{... | collective-permute-start | bytes 1118216 | tf_op jit(solution)/shard_map/ppermute | solution.py:1228
  625.0 21.5 %collective-permute-start.57 = (bf16[208,896]{1,0:T(8,128)(2,1)S(1)}, bf16[208,896]{1,0:T(8,128)(2,1)S(1)}, u32[]{:S(2)}, u32[]{:S(2)}) collective-permute-start(bf16[208,896]{1,0:T(8,128)(2,1)S(1)} %get-tuple-element.299), channel_id=1, source_target_pairs={{0,3},{3,0},{4,7},{7,4},{8,11},{11,8},{12,15},{15,12},{16,19},{19,... | collective-permute-start | bytes 1118216 | tf_op jit(solution)/shard_map/ppermute | solution.py:1191
  (76 other events, 546.7 us)
Sparse Core Ops, SparseCore 0:
  201.7 127.1 all-gather.2
  331.2 121.7 reduce-scatter.2
  459.2 130.0 reduce-scatter.4
